TPU v7x, 32 devices: a whole 2x2x4 slice. The times are simulated.
32 devices in a mesh: section: 2 (over core), dp: 16 (over z, y, x).
Axes of the slice: x: 2, y: 2, z: 4, core: 2. Of those that a mesh axis runs over, the one named last changes fastest.
Arguments:
- inputs: bfloat16 [2, 1024, 4096], P(None, 'dp'), may hold values from -6 to 6
- cotangent: bfloat16 [2, 1024, 4096], P(None, 'dp'), may hold values from -6 to 6
- doc_lengths: int32 [2, 16, 2], P(None, 'dp'), may hold values from 1 to 48, 64 in all within a row
- norm_gain: bfloat16 [2, 4096], P('section'), may hold values from 0.25 to 1.75
- w_qkv: bfloat16 [2, 4096, 192], P('section', 'dp'), may hold values from -0.09375 to 0.09375
- w_out: bfloat16 [2, 64, 4096], P('section', None, 'dp'), may hold values from -0.75 to 0.75
Outputs:
- grad_qkv: float32 [2, 4096, 192], P('section', 'dp')
- grad_out: float32 [2, 64, 4096], P('section', None, 'dp')
Inputs may be any that keep to these rules, and one draw needn't show every extreme that they name: `doc_lengths`: each row's 2 lengths add up to 64.
All inputs are finite; a program needn't handle non-finite values.
Results may differ from a plain program's by a relative error of at most 0.025.
Values may be sent and summed in bfloat16 or wider, within the bound.
No kernel may reach another device: no remote copies, remote signals or barrier semaphores. Data moves between devices by JAX's collectives and lax.ppermute only.
A program may use at most 64 MiB of HBM per device.

v0:
```python
import jax
import jax.numpy as jnp
from jax import lax
from jax.sharding import PartitionSpec as P


def passed_along(block, axis, distance):
    devices = range(lax.axis_size(axis))
    route = [(i - distance, i) for i in devices if i - distance in devices]
    return lax.ppermute(block, axis, route)


def segments_of(lengths, count):
    ends = jnp.cumsum(lengths)
    position = jnp.arange(count, dtype=jnp.int32)
    return jnp.sum((position[:, None] >= ends[None, :]).astype(jnp.int32), axis=1)


def layer(x, gain, w_qkv, w_out, seg):
    head = w_out.shape[0]
    x_wide = x.astype(jnp.float32)
    scale = lax.rsqrt(jnp.mean(x_wide * x_wide, axis=-1, keepdims=True) + 1e-05)
    normed = (x_wide * scale * gain.astype(jnp.float32)).astype(jnp.bfloat16)
    qkv = jnp.dot(normed, w_qkv, preferred_element_type=jnp.float32).astype(jnp.bfloat16)
    query = qkv[:, :head]
    keys = qkv[:, head : 2 * head]
    values = qkv[:, 2 * head :]
    scores = jnp.dot(query, keys.T, preferred_element_type=jnp.float32) * head ** (-0.5)
    rows = jnp.arange(x.shape[0], dtype=jnp.int32)
    allowed = (seg[:, None] == seg[None, :]) & (rows[:, None] >= rows[None, :])
    scores = jnp.where(allowed, scores, -1e30)
    probs = jax.nn.softmax(scores, axis=-1).astype(jnp.bfloat16)
    attended = jnp.dot(probs, values, preferred_element_type=jnp.float32).astype(jnp.bfloat16)
    return (x_wide + jnp.dot(attended, w_out, preferred_element_type=jnp.float32)).astype(
        jnp.bfloat16
    )


def body(inputs, cotangent, doc_lengths, norm_gain, w_qkv, w_out):
    sections = lax.axis_size("section")
    section = lax.axis_index("section")
    micro = inputs.shape[0]
    count = inputs.shape[1]
    segs = jax.vmap(lambda lens: segments_of(lens, count))(doc_lengths[:, 0, :])
    gain = norm_gain[0]
    full_qkv, full_out = (
        lax.all_gather(w_qkv[0], "dp", axis=0, tiled=True),
        lax.all_gather(w_out[0], "dp", axis=1, tiled=True),
    )
    total_steps = micro + sections - 1
    empty = jnp.zeros(inputs.shape[1:], inputs.dtype)

    def forward_at(step, incoming, saved):
        index = step - section
        live = (index >= 0) & (index < micro)
        slot = jnp.clip(index, 0, micro - 1)
        first = lax.dynamic_index_in_dim(inputs, slot, 0, keepdims=False)
        x = jnp.where(section == 0, first, incoming)
        seg = lax.dynamic_index_in_dim(segs, slot, 0, keepdims=False)
        out = layer(x, gain, full_qkv, full_out, seg)
        old = lax.dynamic_index_in_dim(saved, slot, 0, keepdims=False)
        saved = lax.dynamic_update_index_in_dim(saved, jnp.where(live, x, old), slot, 0)
        return (out, saved)

    def forward_step(carry, step):
        incoming, saved = carry
        out, saved = forward_at(step, incoming, saved)
        incoming = passed_along(out, "section", 1)
        return ((incoming, saved), None)

    start_saved = jnp.zeros(inputs.shape, inputs.dtype)
    (incoming, saved), _ = lax.scan(
        forward_step, (empty, start_saved), jnp.arange(total_steps - 1, dtype=jnp.int32)
    )
    _, saved = forward_at(jnp.int32(total_steps - 1), incoming, saved)
    back_qkv, back_out = (
        lax.all_gather(w_qkv[0], "dp", axis=0, tiled=True),
        lax.all_gather(w_out[0], "dp", axis=1, tiled=True),
    )

    def backward_at(step, incoming, sum_qkv, sum_out):
        index = step - (sections - 1 - section)
        live = (index >= 0) & (index < micro)
        slot = jnp.clip(index, 0, micro - 1)
        last = lax.dynamic_index_in_dim(cotangent, slot, 0, keepdims=False)
        grad_y = jnp.where(section == sections - 1, last, incoming)
        x = lax.dynamic_index_in_dim(saved, slot, 0, keepdims=False)
        seg = lax.dynamic_index_in_dim(segs, slot, 0, keepdims=False)
        _, pull = jax.vjp(lambda a, b, c: layer(a, gain, b, c, seg), x, back_qkv, back_out)
        grad_x, grad_q, grad_o = pull(grad_y)
        sum_qkv = sum_qkv + jnp.where(live, grad_q.astype(jnp.float32), 0.0)
        sum_out = sum_out + jnp.where(live, grad_o.astype(jnp.float32), 0.0)
        return (grad_x, sum_qkv, sum_out)

    def backward_step(carry, step):
        incoming, sum_qkv, sum_out = carry
        grad_x, sum_qkv, sum_out = backward_at(step, incoming, sum_qkv, sum_out)
        incoming = passed_along(grad_x, "section", -1)
        return ((incoming, sum_qkv, sum_out), None)

    zero_qkv = jnp.zeros(back_qkv.shape, jnp.float32)
    zero_out = jnp.zeros(back_out.shape, jnp.float32)
    (incoming, sum_qkv, sum_out), _ = lax.scan(
        backward_step, (empty, zero_qkv, zero_out), jnp.arange(total_steps - 1, dtype=jnp.int32)
    )
    _, sum_qkv, sum_out = backward_at(jnp.int32(total_steps - 1), incoming, sum_qkv, sum_out)
    share_qkv, share_out = (
        lax.psum_scatter(sum_qkv, "dp", scatter_dimension=0, tiled=True),
        lax.psum_scatter(sum_out, "dp", scatter_dimension=1, tiled=True),
    )
    return (share_qkv[None], share_out[None])


def solution(mesh):
    return jax.shard_map(
        body,
        mesh=mesh,
        in_specs=(
            P(None, "dp", None),
            P(None, "dp", None),
            P(None, "dp", None),
            P("section", None),
            P("section", "dp", None),
            P("section", None, "dp"),
        ),
        out_specs=(P("section", "dp", None), P("section", None, "dp")),
        check_vma=False,
    )
```

profile of v0, /device:TPU:0, one launch (start us, length us, event | category | flops | bytes accessed | tf_op | source)
XLA Modules:
  0.0 351.4 jit_solution(767960133056842057)
XLA Ops:
  7.2 1.7 copy.9
  9.0 0.8 reduce_window_sum.14
  9.8 0.8 reduce
  10.7 48.8 %all-gather.1 = bf16[1,64,4096]{2,1,0:T(8,128)(2,1)} all-gather(bf16[1,64,256]{2,1,0:T(8,128)(2,1)} %param.15), channel_id=3, replica_groups=mesh['section'=2,'dp'=16] {'dp'}, dimensions={2}, use_global_device_ids=true | all-gather | bytes 557056 | tf_op jit(solution)/shard_map/all_gather | solution.py:48
  59.5 16.5 %all-gather.4.cloned.1.call-done = bf16[1,4096,192]{2,1,0:T(8,128)(2,1)} async-done(((bf16[1,256,192]{2,1,0:T(8,128)(2,1)}), bf16[1,4096,192]{2,1,0:T(8,128)(2,1)}) %all-gather.4.cloned.1.call-update) | async-done | bytes 1572880 | tf_op jit(solution)/shard_map/all_gather | solution.py:47
  76.0 0.8 broadcast_in_dim.102.clone
  77.0 21.2 %while.30 = (s32[]{:T(128)}, bf16[64,4096]{1,0:T(8,128)(2,1)}, bf16[2,64,4096]{2,1,0:T(8,128)(2,1)S(1)}, pred[]{:T(512)}, s32[2]{0:T(128)S(1)}, /*index=5*/s32[]...) while((s32[]{:T(128)}, bf16[64,4096]{1,0:T(8,128)(2,1)}, ...), condition=%wide.region_6.7_spmd, body=%wide.region_2.6_spmd.sunk | while | flops 138477504 | bytes 20632148 | solution.py:72
  77.0 0.6 dynamic_slice.104
  78.3 0.9 constant_dynamic-slice_fusion.6
  79.2 1.4 bitcast_dynamic-update-slice_fusion.3
  80.6 0.2 fusion.141
  80.9 0.5 convolution_convert_fusion.27
  81.4 0.2 fusion.143
  81.7 1.7 fusion.145
  83.3 1.5 collective-permute-start
  84.8 1.5 collective-permute-done
  86.3 0.8 copy-done.6
  87.1 0.6 dynamic_slice.104
  88.4 0.9 constant_dynamic-slice_fusion.6
  89.3 1.4 bitcast_dynamic-update-slice_fusion.3
  90.7 0.2 fusion.141
  91.0 0.5 convolution_convert_fusion.27
  91.5 0.2 fusion.143
  91.8 1.7 fusion.145
  93.4 2.5 collective-permute-start
  95.9 1.5 collective-permute-done
  97.4 0.8 copy-done.6
  98.3 1.4 bitcast_dynamic-update-slice_fusion.1
  99.7 0.2 fusion.59
  100.0 0.5 convolution_convert_fusion.14
  100.5 0.2 fusion.89
  100.7 0.8 broadcast_in_dim.102
  101.6 28.0 %while.31 = (s32[]{:T(128)}, bf16[64,4096]{1,0:T(8,128)(2,1)}, f32[4096,192]{0,1:T(8,128)}, f32[64,4096]{1,0:T(8,128)}, pred[]{:T(512)}, /*index=5*/s32[2]{0:T(1...) while((s32[]{:T(128)}, bf16[64,4096]{1,0:T(8,128)(2,1)}, ...), condition=%wide.region_13.14_spmd.clone, body=%wide.region_7.13_spmd.clone.sunk | while | flops 384602496 | bytes 32000636 | solution.py:103
  101.6 0.6 dynamic_slice.112
  102.8 0.2 fusion.160
  103.1 0.5 convolution_convert_fusion.28
  103.6 0.2 fusion.163
  103.9 0.2 copy-done.7
  104.0 1.1 bitcast_select_fusion.10
  105.2 0.3 convolution_convert_fusion.29
  105.7 0.2 convolution_convert_fusion.30
  106.2 0.9 fusion.165
  107.0 1.2 fusion.166
  108.2 1.3 collective-permute-start.1
  109.5 2.6 fusion.168
  112.1 2.4 fusion.167
  114.4 0.6 dynamic_slice.112
  115.7 0.2 fusion.160
  115.9 0.5 convolution_convert_fusion.28
  116.5 0.2 fusion.163
  116.9 1.1 bitcast_select_fusion.10
  118.0 0.3 convolution_convert_fusion.29
  118.6 0.2 convolution_convert_fusion.30
  119.0 0.9 fusion.165
  119.9 1.2 fusion.166
  121.1 1.3 collective-permute-start.1
  122.4 2.9 fusion.168
  125.3 4.2 %fusion.167 = f32[4096,192]{0,1:T(8,128)} fusion(f32[4096,192]{0,1:T(8,128)} %get-tuple-element.580, pred[]{:T(512)S(6)} %compare.9, pred[]{:T(512)S(6)} %and.51, f32[4096]{0:T(1024)S(1)} %convert_element_type.404, f32[64]{0:T(128)S(1)} %fusion.161, bf16[2,64,4096]{2,1,0:T(8,128)(2,1)S(1)} %get-tuple-element.603, s32[]{:T(128)S(6)} %min.22, ...), kind=kOutput, calls=%fused_computation.33.clone.1 | convolution fusion | flops 105717760 | bytes 6881798 | tf_op jit(solution)/shard_map/while/body/eval_jaxpr/transpose(jvp())/dot_general | solution.py:24
  129.6 3.2 fusion.56
  132.9 1.3 convolution_convert_fusion.20
  134.5 0.2 convolution_convert_fusion.16
  134.9 4.3 %fusion.53 = f32[4096,192]{0,1:T(8,128)} fusion(f32[4096,192]{0,1:T(8,128)} %get-tuple-element.247, pred[]{:T(512)S(6)} %and.29, f32[4096]{0:T(1024)S(1)} %mul.200, f32[64]{0:T(128)S(1)} %add_rsqrt_fusion.1, bf16[2,64,4096]{2,1,0:T(8,128)(2,1)S(1)} %get-tuple-element.615, s32[]{:T(128)S(6)} %min.17, bf16[64,64]{1,0:T(8,128)(2,1)S(1)} %convolution_convert_fusion.16, ...), kind=kOutput, calls=%fused_computation.89 | convolution fusion | flops 104931328 | bytes 6881797 | tf_op jit(solution)/shard_map/transpose(jvp())/dot_general | solution.py:24
  139.2 71.3 %reduce-scatter.5.cloned.1.call-done = f32[64,256]{1,0:T(8,128)} async-done(((f32[64,4096]{1,0:T(8,128)}), f32[64,256]{1,0:T(8,128)}) %reduce-scatter.5.cloned.1.call-update) | async-done | bytes 65552 | tf_op jit(solution)/shard_map/reduce_scatter | solution.py:109
  210.5 134.3 %reduce-scatter.3.cloned.1.call-done = f32[256,192]{0,1:T(8,128)} async-done(((f32[4096,192]{0,1:T(8,128)}), f32[256,192]{0,1:T(8,128)}) %reduce-scatter.3.cloned.1.call-update) | async-done | bytes 196624 | tf_op jit(solution)/shard_map/reduce_scatter | solution.py:108
  (82 shorter events, 2.6 us)
Async XLA Ops:
  7.2 68.9 %all-gather.4.cloned.1.call-start = ((), (), s32[]{:S(2)}) async-start(), calls=%async_computation.4 | async-start | bytes 2228224 | tf_op jit(solution)/shard_map/all_gather | solution.py:47
  8.9 201.6 %reduce-scatter.5.cloned.1.call-start = ((), (), s32[]{:S(2)}) async-start(), calls=%async_computation.3 | async-start | bytes 1114112 | tf_op jit(solution)/shard_map/reduce_scatter | solution.py:109
  77.0 3.9 %copy-start = (bf16[4096,192]{1,0:T(8,128)(2,1)S(1)}, bf16[4096,192]{1,0:T(8,128)(2,1)}, u32[]{:S(2)}) copy-start(bf16[4096,192]{1,0:T(8,128)(2,1)} %get-tuple-element.557) | copy-start | bytes 4718596 | tf_op jit(solution)/shard_map/while
  80.6 0.8 copy-start.3
  83.3 3.0 collective-permute-start
  86.3 0.8 copy-start.6
  87.1 3.9 %copy-start = (bf16[4096,192]{1,0:T(8,128)(2,1)S(1)}, bf16[4096,192]{1,0:T(8,128)(2,1)}, u32[]{:S(2)}) copy-start(bf16[4096,192]{1,0:T(8,128)(2,1)} %get-tuple-element.557) | copy-start | bytes 4718596 | tf_op jit(solution)/shard_map/while
  90.7 0.8 copy-start.3
  93.4 4.0 %collective-permute-start = (bf16[64,4096]{1,0:T(8,128)(2,1)S(1)}, bf16[64,4096]{1,0:T(8,128)(2,1)S(1)}, u32[]{:S(2)}, u32[]{:S(2)}) collective-permute-start(bf16[64,4096]{1,0:T(8,128)(2,1)S(1)} %fusion.145), channel_id=1, source_target_pairs={{0,16},{1,17},{2,18},{3,19},{4,20},{5,21},{6,22},{7,23},{8,24},{9,... | collective-permute-start | bytes 1572872 | tf_op jit(solution)/shard_map/while/body/eval_jaxpr/ppermute | solution.py:10
  97.4 0.8 copy-start.6
  98.2 1.7 copy-start.1
  102.8 1.2 copy-start.7
  102.8 2.3 copy-start.4
  105.1 3.1 copy-start.2
  108.2 6.2 %collective-permute-start.1 = (bf16[64,4096]{1,0:T(8,128)(2,1)}, bf16[64,4096]{1,0:T(8,128)(2,1)}, u32[]{:S(2)}, u32[]{:S(2)}) collective-permute-start(bf16[64,4096]{1,0:T(8,128)(2,1)} %fusion.166), channel_id=1, source_target_pairs={{16,0},{17,1},{18,2},{19,3},{20,4},{21,5},{22,6},{23,7},{24,8},{25... | collective-permute-start | bytes 1572872 | tf_op jit(solution)/shard_map/while/body/eval_jaxpr/ppermute | solution.py:10
  115.7 1.2 copy-start.7
  115.7 2.3 copy-start.4
  118.0 3.1 copy-start.2
  121.1 8.5 %collective-permute-start.1 = (bf16[64,4096]{1,0:T(8,128)(2,1)}, bf16[64,4096]{1,0:T(8,128)(2,1)}, u32[]{:S(2)}, u32[]{:S(2)}) collective-permute-start(bf16[64,4096]{1,0:T(8,128)(2,1)} %fusion.166), channel_id=1, source_target_pairs={{16,0},{17,1},{18,2},{19,3},{20,4},{21,5},{22,6},{23,7},{24,8},{25... | collective-permute-start | bytes 1572872 | tf_op jit(solution)/shard_map/while/body/eval_jaxpr/ppermute | solution.py:10
  129.6 3.3 copy-start.5
  129.6 3.3 copy-start.8
  132.8 212.1 %reduce-scatter.3.cloned.1.call-start = ((), (), s32[]{:S(2)}) async-start(), calls=%async_computation.2 | async-start | bytes 3342336 | tf_op jit(solution)/shard_map/reduce_scatter | solution.py:108
Sparse Core Ops, SparseCore 0:
  11.3 64.6 all-gather.3
  132.9 77.5 reduce-scatter.4
  216.8 127.9 reduce-scatter.2
where the time goes:
time: 352 us; the launch traced here: 351 us
  waiting for transfers between devices  225 us (64%)
  blocking collectives  48.8 us (14%)
  matrix products  32 us (9%)
  between operations  13.9 us (4%)
  other arithmetic  12.1 us (3%)
  local copies, waits for them, and re-layouts  9.69 us (3%)
  starting transfers between devices  6.65 us (2%)
    reduce_scatter x1, waiting for transfers between devices, body(): lax.psum_scatter(sum_qkv, 'dp', scatter_dimension=0, tiled=True)  134 us
    reduce_scatter x1, waiting for transfers between devices, body(): lax.psum_scatter(sum_out, 'dp', scatter_dimension=1, tiled=True)  71.3 us
    all_gather x1, blocking collectives, body(): lax.all_gather(w_out[0], 'dp', axis=1, tiled=True)  48.8 us
    all_gather x1, waiting for transfers between devices, body(): lax.all_gather(w_qkv[0], 'dp', axis=0, tiled=True)  16.5 us
    dot_general x10, matrix products, layer(): jnp.dot(normed, w_qkv, preferred_element_type=jnp.float32)  15.2 us
    dot_general x8, matrix products, layer(): jnp.dot(attended, w_out, preferred_element_type=jnp.float32)  13.9 us
  transfers between devices with their start and end apart: 7, of which 5 were waited for; matrix products, arithmetic and copies ran while one was open for 6% of the time, Pallas kernels for 0%

commit v1 on v0

--- a/solution.py
+++ b/solution.py
@@ -1,7 +1,17 @@
+import functools
+
 import jax
 import jax.numpy as jnp
 from jax import lax
+from jax.experimental import pallas as pl
+from jax.experimental.pallas import tpu as pltpu
 from jax.sharding import PartitionSpec as P
+
+F32 = jnp.float32
+BF16 = jnp.bfloat16
+PLANE = 4
+STATS = 16
+VMEM_LIMIT = 32 * 1024 * 1024
 
 
 def passed_along(block, axis, distance):
@@ -36,7 +46,7 @@
     )
 
 
-def body(inputs, cotangent, doc_lengths, norm_gain, w_qkv, w_out):
+def pipelined(inputs, cotangent, doc_lengths, norm_gain, w_qkv, w_out):
     sections = lax.axis_size("section")
     section = lax.axis_index("section")
     micro = inputs.shape[0]
@@ -73,10 +83,6 @@
         forward_step, (empty, start_saved), jnp.arange(total_steps - 1, dtype=jnp.int32)
     )
     _, saved = forward_at(jnp.int32(total_steps - 1), incoming, saved)
-    back_qkv, back_out = (
-        lax.all_gather(w_qkv[0], "dp", axis=0, tiled=True),
-        lax.all_gather(w_out[0], "dp", axis=1, tiled=True),
-    )
 
     def backward_at(step, incoming, sum_qkv, sum_out):
         index = step - (sections - 1 - section)
@@ -86,7 +92,7 @@
         grad_y = jnp.where(section == sections - 1, last, incoming)
         x = lax.dynamic_index_in_dim(saved, slot, 0, keepdims=False)
         seg = lax.dynamic_index_in_dim(segs, slot, 0, keepdims=False)
-        _, pull = jax.vjp(lambda a, b, c: layer(a, gain, b, c, seg), x, back_qkv, back_out)
+        _, pull = jax.vjp(lambda a, b, c: layer(a, gain, b, c, seg), x, full_qkv, full_out)
         grad_x, grad_q, grad_o = pull(grad_y)
         sum_qkv = sum_qkv + jnp.where(live, grad_q.astype(jnp.float32), 0.0)
         sum_out = sum_out + jnp.where(live, grad_o.astype(jnp.float32), 0.0)
@@ -98,8 +104,8 @@
         incoming = passed_along(grad_x, "section", -1)
         return ((incoming, sum_qkv, sum_out), None)
 
-    zero_qkv = jnp.zeros(back_qkv.shape, jnp.float32)
-    zero_out = jnp.zeros(back_out.shape, jnp.float32)
+    zero_qkv = jnp.zeros(full_qkv.shape, jnp.float32)
+    zero_out = jnp.zeros(full_out.shape, jnp.float32)
     (incoming, sum_qkv, sum_out), _ = lax.scan(
         backward_step, (empty, zero_qkv, zero_out), jnp.arange(total_steps - 1, dtype=jnp.int32)
     )
@@ -111,7 +117,359 @@
     return (share_qkv[None], share_out[None])
 
 
+def nn(a, b):
+    return lax.dot_general(a, b, (((1,), (0,)), ((), ())), preferred_element_type=F32)
+
+
+def nt(a, b):
+    return lax.dot_general(a, b, (((1,), (1,)), ((), ())), preferred_element_type=F32)
+
+
+def prepare_kernel(planes, index, x_ref, c_ref, xs_ref, cs_ref):
+    width = xs_ref.shape[-1] // planes
+    for z in range(planes):
+        for p in range(PLANE):
+            here = slice((z * PLANE + p) * width, (z * PLANE + p + 1) * width)
+            there = slice(z * width, (z + 1) * width)
+            xs_ref[p, :, there] = x_ref[0, :, here]
+            cs_ref[p, :, there] = c_ref[0, :, here]
+
+
+def gain_of(w_ref, z, wide):
+    return w_ref[z, wide : wide + STATS, :].astype(F32)[0:1, :]
+
+
+def partial_qkv(x_of, w_ref, qkv_rows, out_rows):
+    total = None
+    squares = None
+    for z in range(w_ref.shape[0]):
+        x = x_of(z)
+        gained = (x * gain_of(w_ref, z, qkv_rows + out_rows)).astype(BF16)
+        part = nt(w_ref[z, :qkv_rows, :], gained)
+        square = jnp.sum(x * x, axis=1, keepdims=True)
+        total = part if total is None else total + part
+        squares = square if squares is None else squares + square
+    return total, squares
+
+
+def stat_rows(squares, extra):
+    rows = squares.shape[0]
+    row = jnp.transpose(jnp.broadcast_to(squares, (rows, 128)))[0:STATS, :]
+    at = lax.broadcasted_iota(jnp.int32, (STATS, rows), 0)
+    high = row.astype(BF16).astype(F32)
+    low = row - high
+    out = jnp.where(at == 0, high, jnp.where(at == 1, low, 0.0))
+    if extra is not None:
+        out = jnp.where(at == 2, extra, out)
+    return out.astype(BF16)
+
+
+def spread(out_ref, at, value):
+    for p in range(PLANE):
+        out_ref[p, at : at + value.shape[0], :] = value
+
+
+def first_kernel(planes, heads, index, docs, x_ref, *refs):
+    own, other = refs[:planes], refs[planes : 2 * planes]
+    w0_ref, w1_ref, out_ref = refs[2 * planes :]
+    qkv_rows, out_rows = 3 * heads, heads
+    section, z, p = index[0], index[1], index[2]
+    for k in range(planes):
+        mine, theirs = own[k][...], other[k][...]
+        w0_ref[z ^ k] = jnp.where(section == 0, mine, theirs)
+        w1_ref[z ^ k] = jnp.where(section == 0, theirs, mine)
+    width = x_ref.shape[-1] // planes
+    rows = x_ref.shape[0] * x_ref.shape[1]
+
+    def x_of(z):
+        x = x_ref[:, :, z * width : (z + 1) * width]
+        return x.reshape(rows, width).astype(F32)
+
+    total, squares = partial_qkv(x_of, w0_ref, qkv_rows, out_rows)
+    spread(out_ref, 0, total.astype(BF16))
+    position = lax.broadcasted_iota(jnp.int32, (STATS, rows), 1)
+    block = rows // PLANE
+    local = position - p * block
+    ends = docs[0]
+    seg = (local >= ends).astype(F32)
+    for i in range(1, docs.shape[0]):
+        ends = ends + docs[i]
+        seg = seg + (local >= ends).astype(F32)
+    seg = jnp.where((local >= 0) & (local < block), seg, 0.0)
+    spread(out_ref, qkv_rows, stat_rows(squares, seg))
+
+
+def attention(qkv_t, codes_row, codes_col, heads):
+    rows = qkv_t.shape[1]
+    narrow = qkv_t.astype(BF16)
+    keys = jnp.transpose(qkv_t[heads : 2 * heads]).astype(BF16)
+    scores = nn(keys, narrow[:heads]) * heads ** (-0.5)
+    key_at = lax.broadcasted_iota(jnp.int32, (rows, rows), 0)
+    query_at = lax.broadcasted_iota(jnp.int32, (rows, rows), 1)
+    allowed = (codes_row == codes_col) & (query_at >= key_at)
+    scores = jnp.where(allowed, scores, -1e30)
+    top = jnp.max(scores, axis=0, keepdims=True)
+    raised = jnp.exp(scores - top)
+    probs = raised / jnp.sum(raised, axis=0, keepdims=True)
+    attended = nn(narrow[2 * heads :], probs.astype(BF16)).astype(BF16)
+    return probs, attended
+
+
+def attention_grad(qkv_t, probs, d_att_t, heads):
+    narrow = qkv_t.astype(BF16)
+    values = jnp.transpose(qkv_t[2 * heads :]).astype(BF16)
+    d_values = nt(d_att_t, probs.astype(BF16))
+    d_probs = nn(values, d_att_t).astype(BF16).astype(F32)
+    inner = jnp.sum(probs * d_probs, axis=0, keepdims=True)
+    d_scores = (probs * (d_probs - inner) * heads ** (-0.5)).astype(BF16)
+    d_query = nn(narrow[heads : 2 * heads], d_scores)
+    d_keys = nt(narrow[:heads], d_scores)
+    return jnp.concatenate([d_query, d_keys, d_values], axis=0).astype(BF16)
+
+
+def summed(parts_ref, start, stop):
+    total = parts_ref[0, start:stop, :].astype(F32)
+    for p in range(1, PLANE):
+        total = total + parts_ref[p, start:stop, :].astype(F32)
+    return total
+
+
+def scaled(parts_ref, qkv_rows, features):
+    stats = summed(parts_ref, qkv_rows, qkv_rows + STATS)
+    scale = lax.rsqrt((stats[0:1, :] + stats[1:2, :]) / features + 1e-05)
+    qkv_t = (summed(parts_ref, 0, qkv_rows) * scale).astype(BF16).astype(F32)
+    return qkv_t, scale, stats
+
+
+def column(row):
+    count = row.shape[1]
+    return jnp.transpose(jnp.broadcast_to(row, (128, count)))[:, 0:1]
+
+
+def second_kernel(
+    features, heads, parts_ref, x_ref, c_ref, w0_ref, w1_ref, out_ref, y_ref, qkv_ref, probs_ref, att_ref, stat_ref
+):
+    planes = w0_ref.shape[0]
+    qkv_rows, out_rows = 3 * heads, heads
+    width = x_ref.shape[-1] // planes
+    rows = x_ref.shape[0] * x_ref.shape[1]
+    qkv_t, scale, stats = scaled(parts_ref, qkv_rows, features)
+    block = lax.broadcasted_iota(jnp.int32, (1, rows), 1) // (rows // PLANE)
+    codes = stats[2:3, :] + (block * rows).astype(F32)
+    probs, att_t = attention(qkv_t, codes, column(codes), heads)
+    qkv_ref[...] = qkv_t
+    probs_ref[...] = probs
+    att_ref[...] = att_t
+    at = lax.broadcasted_iota(jnp.int32, stat_ref.shape, 0)
+    stat_ref[...] = jnp.where(at == 0, scale, codes)
+    att = jnp.transpose(att_t.astype(F32)).astype(BF16)
+    d_att = None
+    for z in range(planes):
+        cols = slice(z * width, (z + 1) * width)
+        x = x_ref[:, :, cols].reshape(rows, width).astype(F32)
+        y_ref[:, cols] = (x + nn(att, w0_ref[z, qkv_rows : qkv_rows + out_rows, :])).astype(BF16)
+        c = c_ref[:, :, cols].reshape(rows, width)
+        part = nt(w1_ref[z, qkv_rows : qkv_rows + out_rows, :], c)
+        d_att = part if d_att is None else d_att + part
+    total, squares = partial_qkv(
+        lambda z: y_ref[:, z * width : (z + 1) * width].astype(F32), w1_ref, qkv_rows, out_rows
+    )
+    spread(out_ref, 0, total.astype(BF16))
+    spread(out_ref, qkv_rows, stat_rows(squares, None))
+    spread(out_ref, qkv_rows + STATS, d_att.astype(BF16))
+
+
+def third_kernel(
+    features, heads, parts_ref, c_ref, y_ref, att_ref, stat_ref, w0_ref, w1_ref, out_ref, g0_ref, g1_ref
+):
+    planes = w0_ref.shape[0]
+    qkv_rows, out_rows = 3 * heads, heads
+    width = y_ref.shape[-1] // planes
+    rows = y_ref.shape[0]
+    qkv_t, scale, _ = scaled(parts_ref, qkv_rows, features)
+    d_att_t = summed(parts_ref, qkv_rows + STATS, qkv_rows + STATS + heads).astype(BF16)
+    codes = stat_ref[1:2, :]
+    probs, att_t = attention(qkv_t, codes, column(codes), heads)
+    d_qkv_t = attention_grad(qkv_t, probs, d_att_t, heads)
+    wide = d_qkv_t.astype(F32)
+    inner = jnp.sum(wide * qkv_t, axis=0, keepdims=True) * scale * scale / features
+    d_qkv = jnp.transpose(wide).astype(BF16)
+    scale_col, inner_col = column(scale), column(inner)
+    att0_t = att_ref[...]
+    d_att = None
+    for z in range(planes):
+        cols = slice(z * width, (z + 1) * width)
+        gain = gain_of(w1_ref, z, qkv_rows + out_rows)
+        c = c_ref[:, :, cols].reshape(rows, width)
+        y = y_ref[:, cols].astype(F32)
+        normed = (y * scale_col * gain).astype(BF16)
+        g1_ref[z, :qkv_rows, :] = nn(d_qkv_t, normed).astype(g1_ref.dtype)
+        g1_ref[z, qkv_rows:, :] = nn(att_t, c).astype(g1_ref.dtype)
+        d_normed = nn(d_qkv, w1_ref[z, :qkv_rows, :])
+        d_y = (c.astype(F32) + scale_col * gain * d_normed - y * inner_col).astype(BF16)
+        g0_ref[z] = nn(att0_t, d_y).astype(g0_ref.dtype)
+        part = nt(w0_ref[z, qkv_rows : qkv_rows + out_rows, :], d_y)
+        d_att = part if d_att is None else d_att + part
+    spread(out_ref, 0, d_att.astype(BF16))
+
+
+def fourth_kernel(
+    heads, index, parts_ref, x_ref, qkv_ref, probs_ref, stat_ref, w0_ref, g0_ref, g1_ref, keep_ref, send_ref
+):
+    planes = w0_ref.shape[0]
+    qkv_rows, out_rows = 3 * heads, heads
+    width = x_ref.shape[-1] // planes
+    rows = x_ref.shape[0] * x_ref.shape[1]
+    section, place = index[0], index[1]
+    d_att_t = summed(parts_ref, 0, heads).astype(BF16)
+    d_qkv_t = attention_grad(qkv_ref[...], probs_ref[...], d_att_t, heads)
+    scale_col = column(stat_ref[0:1, :])
+    for z in range(planes):
+        cols = slice(z * width, (z + 1) * width)
+        x = x_ref[:, :, cols].reshape(rows, width).astype(F32)
+        normed = (x * scale_col * gain_of(w0_ref, z, qkv_rows + out_rows)).astype(BF16)
+        zero = nn(d_qkv_t, normed)
+        one = g1_ref[z, :qkv_rows, :]
+        keep_ref[z, :qkv_rows, :] = jnp.where(section == 0, zero, one)
+        send_ref[z, :qkv_rows, :] = jnp.where(section == 0, one, zero).astype(BF16)
+        zero, one = g0_ref[z], g1_ref[z, qkv_rows:, :]
+        keep_ref[z, qkv_rows:, :] = jnp.where(section == 0, zero, one)
+        send_ref[z, qkv_rows:, :] = jnp.where(section == 0, one, zero).astype(BF16)
+
+
+def merge_kernel(index, keep_ref, come_ref, *out_refs):
+    place = index[1]
+    out_refs[0][...] = keep_ref[place] + come_ref[place].astype(F32)
+    for k in range(1, len(out_refs)):
+        out_refs[k][...] = (keep_ref[place ^ k] + come_ref[place ^ k].astype(F32)).astype(BF16)
+
+
+def last_kernel(qkv_rows, keep_ref, *refs):
+    parts, (qkv_ref, out_ref) = refs[:-2], refs[-2:]
+    total = keep_ref[...]
+    for part in parts:
+        total = total + part[...].astype(F32)
+    qkv_ref[...] = total[:qkv_rows]
+    out_ref[...] = total[qkv_rows:]
+
+
+def call(kernel, outs, *args, scalars=0):
+    smem = pl.BlockSpec(memory_space=pltpu.SMEM)
+    vmem = pl.BlockSpec(memory_space=pltpu.VMEM)
+    return pl.pallas_call(
+        kernel,
+        out_shape=[jax.ShapeDtypeStruct(shape, dtype) for shape, dtype in outs],
+        in_specs=[smem] * scalars + [vmem] * (len(args) - scalars),
+        out_specs=[vmem] * len(outs),
+        compiler_params=pltpu.CompilerParams(vmem_limit_bytes=VMEM_LIMIT),
+    )(*args)
+
+
+def planar(inputs, cotangent, doc_lengths, norm_gain, w_qkv, w_out):
+    shards = lax.axis_size("dp")
+    planes = shards // PLANE
+    section, place = lax.axis_index("section"), lax.axis_index("dp")
+    z, p = place // PLANE, place % PLANE
+    index = jnp.stack([section, z, p]).astype(jnp.int32)
+    block, features = inputs.shape[1:]
+    rows = PLANE * block
+    heads, width = w_out.shape[1:]
+    qkv_rows = w_qkv.shape[2]
+    cols = planes * width
+    in_plane = [[a * PLANE + b for b in range(PLANE)] for a in range(planes)]
+
+    def along_z(value, k):
+        route = [(a * PLANE + b, (a ^ k) * PLANE + b) for a in range(planes) for b in range(PLANE)]
+        return lax.ppermute(value, "dp", route)
+
+    def to_sibling(value):
+        return lax.ppermute(value, "section", [(0, 1), (1, 0)])
+
+    def exchange(value):
+        return lax.all_to_all(value, "dp", 0, 0, axis_index_groups=in_plane, tiled=True)
+
+    gain = lax.dynamic_slice(norm_gain, (0, place * width), (1, width))
+    pack = jnp.concatenate(
+        [w_qkv[0].T, w_out[0], jnp.pad(gain, ((0, STATS - 1), (0, 0)))], axis=0
+    )
+    own = [pack] + [along_z(pack, k) for k in range(1, planes)]
+
+    one_batch = pl.BlockSpec((1, block, features), lambda i, index: (index[0], 0, 0))
+    split = pl.BlockSpec((PLANE, block, cols), lambda i, index: (0, 0, 0))
+    xs, cs = pl.pallas_call(
+        functools.partial(prepare_kernel, planes),
+        grid_spec=pltpu.PrefetchScalarGridSpec(
+            num_scalar_prefetch=1,
+            grid=(1,),
+            in_specs=[one_batch, one_batch],
+            out_specs=[split, split],
+        ),
+        out_shape=[jax.ShapeDtypeStruct((PLANE, block, cols), BF16)] * 2,
+        compiler_params=pltpu.CompilerParams(vmem_limit_bytes=VMEM_LIMIT),
+    )(index, inputs, cotangent)
+    x = exchange(xs)
+    c = exchange(cs)
+    other = [to_sibling(piece) for piece in own]
+
+    docs = lax.dynamic_index_in_dim(doc_lengths, section, 0, keepdims=False)[0]
+    weights = ((planes,) + pack.shape, BF16)
+    w0, w1, sent = call(
+        functools.partial(first_kernel, planes, heads),
+        [weights, weights, ((PLANE, qkv_rows + STATS, rows), BF16)],
+        index, docs, x, *own, *other, scalars=2,
+    )
+    y, qkv, probs, att, stats = None, None, None, None, None
+    sent, y, qkv, probs, att, stats = call(
+        functools.partial(second_kernel, features, heads),
+        [
+            ((PLANE, qkv_rows + STATS + heads, rows), BF16),
+            ((rows, cols), BF16),
+            ((qkv_rows, rows), F32),
+            ((rows, rows), F32),
+            ((heads, rows), BF16),
+            ((8, rows), F32),
+        ],
+        exchange(sent), x, c, w0, w1,
+    )
+    sent, g0, g1 = call(
+        functools.partial(third_kernel, features, heads),
+        [
+            ((PLANE, heads, rows), BF16),
+            ((planes, heads, width), F32),
+            ((planes, qkv_rows + heads, width), F32),
+        ],
+        exchange(sent), c, y, att, stats, w0, w1,
+    )
+    grads = (planes, qkv_rows + heads, width)
+    keep, send = call(
+        functools.partial(fourth_kernel, heads),
+        [(grads, F32), (grads, BF16)],
+        index, exchange(sent), x, qkv, probs, stats, w0, g0, g1, scalars=1,
+    )
+    merged = call(
+        merge_kernel,
+        [(grads[1:], F32)] + [(grads[1:], BF16)] * (planes - 1),
+        index, keep, to_sibling(send), scalars=1,
+    )
+    parts = [along_z(merged[k], k) for k in range(1, planes)]
+    grad_qkv, grad_out = call(
+        functools.partial(last_kernel, qkv_rows),
+        [((qkv_rows, width), F32), ((heads, width), F32)],
+        merged[0], *parts,
+    )
+    return (grad_qkv.T[None], grad_out[None])
+
+
 def solution(mesh):
+    sections, shards = mesh.shape["section"], mesh.shape["dp"]
+    planes = shards // PLANE
+
+    def body(inputs, *rest):
+        fits = shards % PLANE == 0 and planes & (planes - 1) == 0
+        if sections == 2 and inputs.shape[0] == 2 and fits:
+            return planar(inputs, *rest)
+        return pipelined(inputs, *rest)
+
     return jax.shard_map(
         body,
         mesh=mesh,

time: 352 us -> 92.8 us (0.26)
  waiting for transfers between devices: 225 us -> 28.6 us
  matrix products: 32 us -> 0 us
  blocking collectives: 48.8 us -> 29.9 us
  between operations: 13.9 us -> 0.77 us
  other arithmetic: 12.1 us -> 0.09 us
  starting transfers between devices: 6.65 us -> 18.2 us
  Pallas kernels: 0 us -> 8.49 us
    reduce_scatter x2 -> x0, waiting for transfers between devices: 206 us -> none  [the longest x1 134 us: body(): lax.psum_scatter(sum_qkv, 'dp', scatter_dimension=0, tiled=True)]
    all_gather x1 -> x0, blocking collectives: 48.8 us -> none  [body(): lax.all_gather(w_out[0], 'dp', axis=1, tiled=True)]
    dot_general x35 -> x0, matrix products: 32 us -> none  [the longest x10 15.2 us: layer(): jnp.dot(normed, w_qkv, preferred_element_type=jnp.float32)]
    all_to_all x0 -> x3, blocking collectives: none -> 29.9 us  [exchange(): lax.all_to_all(value, 'dp', 0, 0, axis_index_groups=in_plane, tiled=True)]
    ppermute x4 -> x11, waiting for transfers between devices: 2.97 us -> 20.5 us  [the longest x6 18.5 us: along_z(): return lax.ppermute(value, 'dp', route)]
    all_gather x1 -> x0, waiting for transfers between devices: 16.5 us -> none  [body(): lax.all_gather(w_qkv[0], 'dp', axis=0, tiled=True)]
    all_to_all x0 -> x2, starting transfers between devices: none -> 8.76 us  [exchange(): lax.all_to_all(value, 'dp', 0, 0, axis_index_groups=in_plane, tiled=True)]
    pallas_call x0 -> x7, Pallas kernels: none -> 8.49 us  [the longest x6 6.8 us: call(): pl.pallas_call(kernel, out_shape=[jax.ShapeDtypeStruct(shape, dtype) for...]
  transfers between devices with their start and end apart: 7 -> 13, of which waited for: 5 -> 7; matrix products, arithmetic and copies ran while one was open for 6% -> 0% of each run, Pallas kernels for 0% -> 1%
where the time goes in v1:
time: 92.8 us; the launch traced here: 92.4 us
  blocking collectives  29.9 us (32%)
  waiting for transfers between devices  28.6 us (31%)
  starting transfers between devices  18.2 us (20%)
  Pallas kernels  8.49 us (9%)
  local copies, waits for them, and re-layouts  6.29 us (7%)
    all_to_all x3, blocking collectives, exchange(): lax.all_to_all(value, 'dp', 0, 0, axis_index_groups=in_plane, tiled=True)  29.9 us
    ppermute x6, waiting for transfers between devices, along_z(): return lax.ppermute(value, 'dp', route)  18.5 us
    ppermute x6, starting transfers between devices, along_z(): return lax.ppermute(value, 'dp', route)  8.9 us
    all_to_all x2, starting transfers between devices, exchange(): lax.all_to_all(value, 'dp', 0, 0, axis_index_groups=in_plane, tiled=True)  8.76 us
    all_to_all x2, waiting for transfers between devices, exchange(): lax.all_to_all(value, 'dp', 0, 0, axis_index_groups=in_plane, tiled=True)  8.01 us
    pallas_call x6, Pallas kernels, call(): pl.pallas_call(kernel, out_shape=[jax.ShapeDtypeStruct(shape, dtype) for...  6.8 us
    unnamed x20, local copies, waits for them, and re-layouts  6.28 us
    ppermute x5, waiting for transfers between devices, to_sibling(): return lax.ppermute(value, 'section', [(0, 1), (1, 0)])  2.06 us
  transfers between devices with their start and end apart: 13, of which 7 were waited for; matrix products, arithmetic and copies ran while one was open for 0% of the time, Pallas kernels for 1%

profile of v1, /device:TPU:0, one launch (start us, length us, event | category | flops | bytes accessed | tf_op | source)
XLA Modules:
  0.0 92.4 jit_solution(5156863409997188368)
XLA Ops:
  0.6 0.0 copy-start
  0.7 0.1 pad_add_fusion.index
  0.7 0.0 copy-start.1
  0.7 1.2 %copy-done.1 = bf16[2,64,4096]{2,1,0:T(8,128)(2,1)S(1)} copy-done((bf16[2,64,4096]{2,1,0:T(8,128)(2,1)S(1)}, bf16[2,64,4096]{2,1,0:T(8,128)(2,1)}, u32[]{:S(2)}) %copy-start.1) | copy-done | bytes 1048600
  2.0 0.0 copy-start.2
  2.0 1.2 %copy-done.2 = bf16[2,64,4096]{2,1,0:T(8,128)(2,1)S(1)} copy-done((bf16[2,64,4096]{2,1,0:T(8,128)(2,1)S(1)}, bf16[2,64,4096]{2,1,0:T(8,128)(2,1)}, u32[]{:S(2)}) %copy-start.2) | copy-done | bytes 1048600
  3.2 1.7 %shard_map.77 = (bf16[4,64,1024]{2,1,0:T(8,128)(2,1)}, bf16[4,64,1024]{2,1,0:T(8,128)(2,1)}) custom-call(s32[3]{0:T(128)S(1)} %pad_add_fusion.index, bf16[2,64,4096]{2,1,0:T(8,128)(2,1)S(1)} %copy-done.1, bf16[2,64,4096]{2,1,0:T(8,128)(2,1)S(1)} %copy-done.2), custom_call_target="tpu_custom_call" | custom-call | tf_op jit(solution)/shard_map/pallas_call | solution.py:399
  4.9 5.2 %all-to-all-start = ((bf16[4,64,1024]{2,1,0:T(8,128)(2,1)}), bf16[4,64,1024]{2,1,0:T(8,128)(2,1)S(1)}, u32[]{:S(2)}, u32[]{:S(2)}) async-start(bf16[4,64,1024]{2,1,0:T(8,128)(2,1)} %get-tuple-element.24), calls=%async_computation | async-start | bytes 1048576 | tf_op jit(solution)/shard_map/all_to_all | solution.py:389
  10.0 0.0 copy-done
  10.1 8.0 %all-to-all-done.x_ref = bf16[4,64,1024]{2,1,0:T(8,128)(2,1)S(1)} async-done(((bf16[4,64,1024]{2,1,0:T(8,128)(2,1)}), bf16[4,64,1024]{2,1,0:T(8,128)(2,1)S(1)}, u32[]{:S(2)}, u32[]{:S(2)}) %all-to-all-start) | async-done | bytes 524320 | tf_op jit(solution)/shard_map/all_to_all | solution.py:389
  18.1 0.0 copy-start.7
  18.1 0.0 copy-start.8
  18.1 3.6 %all-to-all-start.2 = ((bf16[4,64,1024]{2,1,0:T(8,128)(2,1)}), bf16[4,64,1024]{2,1,0:T(8,128)(2,1)S(1)}, u32[]{:S(2)}, u32[]{:S(2)}) async-start(bf16[4,64,1024]{2,1,0:T(8,128)(2,1)} %get-tuple-element.26), calls=%async_computation.2 | async-start | bytes 1048576 | tf_op jit(solution)/shard_map/all_to_all | solution.py:389
  21.7 0.0 copy-done.7
  21.7 0.0 copy-done.8
  21.7 3.7 %collective-permute-start.2 = (bf16[272,256]{1,0:T(8,128)(2,1)S(1)}, bf16[272,256]{1,0:T(8,128)(2,1)S(1)}, u32[]{:S(2)}, u32[]{:S(2)}) collective-permute-start(bf16[272,256]{1,0:T(8,128)(2,1)S(1)} %fusion.1.refs_0_), channel_id=1, source_target_pairs={{0,12},{1,13},{2,14},{3,15},{4,8},{5,9},{6,10},{7,11},{8,4},{9,5},... | collective-permute-start | bytes 417800 | tf_op jit(solution)/shard_map/ppermute | solution.py:383
  25.4 0.0 collective-permute-start.1
  25.4 0.8 collective-permute-start
  26.2 0.0 collective-permute-start.3
  26.2 4.0 %collective-permute-done.2.refs_3_ = bf16[272,256]{1,0:T(8,128)(2,1)S(1)} collective-permute-done((bf16[272,256]{1,0:T(8,128)(2,1)S(1)}, bf16[272,256]{1,0:T(8,128)(2,1)S(1)}, u32[]{:S(2)}, u32[]{:S(2)}) %collective-permute-start.2) | collective-permute-done | bytes 139296 | tf_op jit(solution)/shard_map/ppermute | solution.py:383
  30.2 0.0 collective-permute-start.6
  30.2 5.8 %collective-permute-done.1.refs_2_ = bf16[272,256]{1,0:T(8,128)(2,1)S(1)} collective-permute-done((bf16[272,256]{1,0:T(8,128)(2,1)S(1)}, bf16[272,256]{1,0:T(8,128)(2,1)S(1)}, u32[]{:S(2)}, u32[]{:S(2)}) %collective-permute-start.1) | collective-permute-done | bytes 139296 | tf_op jit(solution)/shard_map/ppermute | solution.py:383
  36.0 0.0 collective-permute-start.5
  36.0 0.0 collective-permute-done.refs_1_
  36.0 0.5 collective-permute-start.4
  36.5 0.0 copy-start.9
  36.5 0.7 copy-done.9
  37.2 0.0 collective-permute-done.3.refs_4_
  37.2 0.0 collective-permute-done.6.refs_7_
  37.2 0.2 collective-permute-done.5.refs_6_
  37.4 0.0 copy-start.3
  37.4 0.7 copy-done.3
  38.1 0.0 collective-permute-done.4.refs_5_
  38.1 0.0 copy-start.5
  38.1 0.7 copy-done.5
  38.7 0.0 copy-start.4
  38.7 0.9 copy-done.4
  39.6 0.0 copy-start.6
  39.6 0.9 copy-done.6
  40.5 1.0 %shard_map.78 = (bf16[4,272,256]{2,1,0:T(8,128)(2,1)S(1)}, bf16[4,272,256]{2,1,0:T(8,128)(2,1)S(1)}, bf16[4,208,256]{2,1,0:T(8,128)(2,1)S(1)}) custom-call(s32[3]{0:T(128)S(1)} %pad_add_fusion.index, s32[2]{0:T(128)S(1)} %dynamic-slice_bitcast_fusion.docs, bf16[4,64,1024]{2,1,0:T(8,128)(2,1)S(1)} %all-to-all-done.x_ref, bf16[272,256]{1,0:T(8,128)(2,1)S(1)} %fusion.1.refs_0_, ...), custom_call_target="tpu_custom_call" | custom-call | tf_op jit(solution)/shard_map/pallas_call | solution.py:359
  41.5 0.0 all-to-all-done.2.c_ref
  41.5 11.7 %all_to_all.25.parts_ref = bf16[4,208,256]{2,1,0:T(8,128)(2,1)S(1)} all-to-all(bf16[4,208,256]{2,1,0:T(8,128)(2,1)S(1)} %get-tuple-element.25), channel_id=1, replica_groups={{0,1,2,3},{4,5,6,7},{8,9,10,11},{12,13,14,15},{16,17,18,19},{20,21,22,2..., dimensions={0} | all-to-all | bytes 851968 | tf_op jit(solution)/shard_map/all_to_all | solution.py:389
  53.2 1.2 %shard_map.79 = (bf16[4,272,256]{2,1,0:T(8,128)(2,1)S(1)}, bf16[256,1024]{1,0:T(8,128)(2,1)S(1)}, f32[192,256]{1,0:T(8,128)S(1)}, f32[256,256]{1,0:T(8,128)S(1)}...) custom-call(bf16[4,208,256]{2,1,0:T(8,128)(2,1)S(1)} %all_to_all.25.parts_ref, ...), custom_call_target="tpu_custom_call" | custom-call | tf_op jit(solution)/shard_map/pallas_call | solution.py:359
  54.4 10.8 %all_to_all.26.parts_ref = bf16[4,272,256]{2,1,0:T(8,128)(2,1)S(1)} all-to-all(bf16[4,272,256]{2,1,0:T(8,128)(2,1)S(1)} %get-tuple-element.29), channel_id=1, replica_groups={{0,1,2,3},{4,5,6,7},{8,9,10,11},{12,13,14,15},{16,17,18,19},{20,21,22,2..., dimensions={0} | all-to-all | bytes 1114112 | tf_op jit(solution)/shard_map/all_to_all | solution.py:389
  65.3 1.9 %shard_map.80 = (bf16[4,64,256]{2,1,0:T(8,128)(2,1)S(1)}, f32[4,64,256]{2,1,0:T(8,128)S(1)}, f32[4,256,256]{2,1,0:T(8,128)S(1)}) custom-call(bf16[4,272,256]{2,1,0:T(8,128)(2,1)S(1)} %all_to_all.26.parts_ref, bf16[4,64,1024]{2,1,0:T(8,128)(2,1)S(1)} %all-to-all-done.2.c_ref, bf16[256,1024]{1,0:T(8,128)(2,1)S(1)} %get-tuple-element.30.y_ref, ...), custom_call_target="tpu_custom_call" | custom-call | tf_op jit(solution)/shard_map/pallas_call | solution.py:359
  67.2 7.4 %all_to_all.27.parts_ref = bf16[4,64,256]{2,1,0:T(8,128)(2,1)S(1)} all-to-all(bf16[4,64,256]{2,1,0:T(8,128)(2,1)S(1)} %get-tuple-element.33), channel_id=1, replica_groups={{0,1,2,3},{4,5,6,7},{8,9,10,11},{12,13,14,15},{16,17,18,19},{20,21,22,2..., dimensions={0} | all-to-all | bytes 262144 | tf_op jit(solution)/shard_map/all_to_all | solution.py:389
  74.6 1.3 %shard_map.81 = (f32[4,256,256]{2,1,0:T(8,128)S(1)}, bf16[4,256,256]{2,1,0:T(8,128)(2,1)S(1)}) custom-call(s32[3]{0:T(128)S(1)} %pad_add_fusion.index, bf16[4,64,256]{2,1,0:T(8,128)(2,1)S(1)} %all_to_all.27.parts_ref, bf16[4,64,1024]{2,1,0:T(8,128)(2,1)S(1)} %all-to-all-done.x_ref, f32[192,256]{1,0:T(8,128)S(1)} %get-tuple-element.34.qkv_ref, ...), custom_call_target="tpu_custom_call" | custom-call | tf_op jit(solution)/shard_map/pallas_call | solution.py:359
  75.9 0.1 collective-permute-start.7
  76.0 1.9 %collective-permute-done.7.come_ref = bf16[4,256,256]{2,1,0:T(8,128)(2,1)S(1)} collective-permute-done((bf16[4,256,256]{2,1,0:T(8,128)(2,1)S(1)}, bf16[4,256,256]{2,1,0:T(8,128)(2,1)S(1)}, u32[]{:S(2)}, u32[]{:S(2)}) %collective-permute-start.7) | collective-permute-done | bytes 524320 | tf_op jit(solution)/shard_map/ppermute | solution.py:386
  77.9 0.7 shard_map.82
  78.5 0.1 collective-permute-start.8
  78.6 3.0 %collective-permute-start.9 = (bf16[256,256]{1,0:T(8,128)(2,1)S(1)}, bf16[256,256]{1,0:T(8,128)(2,1)S(1)}, u32[]{:S(2)}, u32[]{:S(2)}) collective-permute-start(bf16[256,256]{1,0:T(8,128)(2,1)S(1)} %get-tuple-element.42), channel_id=1, source_target_pairs={{0,8},{1,9},{2,10},{3,11},{4,12},{5,13},{6,14},{7,15},{8,0},{9,1},... | collective-permute-start | bytes 393224 | tf_op jit(solution)/shard_map/ppermute | solution.py:383
  81.6 1.3 %collective-permute-start.10 = (bf16[256,256]{1,0:T(8,128)(2,1)S(1)}, bf16[256,256]{1,0:T(8,128)(2,1)S(1)}, u32[]{:S(2)}, u32[]{:S(2)}) collective-permute-start(bf16[256,256]{1,0:T(8,128)(2,1)S(1)} %get-tuple-element.43), channel_id=1, source_target_pairs={{0,12},{1,13},{2,14},{3,15},{4,8},{5,9},{6,10},{7,11},{8,4},{9,5},... | collective-permute-start | bytes 393224 | tf_op jit(solution)/shard_map/ppermute | solution.py:383
  83.0 3.4 %collective-permute-done.8.refs_0_ = bf16[256,256]{1,0:T(8,128)(2,1)S(1)} collective-permute-done((bf16[256,256]{1,0:T(8,128)(2,1)S(1)}, bf16[256,256]{1,0:T(8,128)(2,1)S(1)}, u32[]{:S(2)}, u32[]{:S(2)}) %collective-permute-start.8) | collective-permute-done | bytes 131104 | tf_op jit(solution)/shard_map/ppermute | solution.py:383
  86.4 5.2 %collective-permute-done.9.refs_1_ = bf16[256,256]{1,0:T(8,128)(2,1)S(1)} collective-permute-done((bf16[256,256]{1,0:T(8,128)(2,1)S(1)}, bf16[256,256]{1,0:T(8,128)(2,1)S(1)}, u32[]{:S(2)}, u32[]{:S(2)}) %collective-permute-start.9) | collective-permute-done | bytes 131104 | tf_op jit(solution)/shard_map/ppermute | solution.py:383
  91.6 0.0 collective-permute-done.10.refs_2_
  91.6 0.7 shard_map.83
  (3 shorter events, 0.0 us)
Async XLA Ops:
  0.6 9.4 %copy-start = (bf16[1,4096]{1,0:T(2,128)(2,1)S(1)}, bf16[1,4096]{1,0:T(2,128)(2,1)}, u32[]{:S(2)}) copy-start(bf16[1,4096]{1,0:T(2,128)(2,1)} %param.9) | copy-start | bytes 24580
  0.7 1.2 %copy-start.1 = (bf16[2,64,4096]{2,1,0:T(8,128)(2,1)S(1)}, bf16[2,64,4096]{2,1,0:T(8,128)(2,1)}, u32[]{:S(2)}) copy-start(bf16[2,64,4096]{2,1,0:T(8,128)(2,1)} %x_ref.1) | copy-start | bytes 3145732
  2.0 1.2 %copy-start.2 = (bf16[2,64,4096]{2,1,0:T(8,128)(2,1)S(1)}, bf16[2,64,4096]{2,1,0:T(8,128)(2,1)}, u32[]{:S(2)}) copy-start(bf16[2,64,4096]{2,1,0:T(8,128)(2,1)} %c_ref.1) | copy-start | bytes 3145732
  4.9 13.2 %all-to-all-start = ((bf16[4,64,1024]{2,1,0:T(8,128)(2,1)}), bf16[4,64,1024]{2,1,0:T(8,128)(2,1)S(1)}, u32[]{:S(2)}, u32[]{:S(2)}) async-start(bf16[4,64,1024]{2,1,0:T(8,128)(2,1)} %get-tuple-element.24), calls=%async_computation | async-start | bytes 1048576 | tf_op jit(solution)/shard_map/all_to_all | solution.py:389
  18.1 3.6 %copy-start.7 = (bf16[1,256,192]{1,2,0:T(8,128)(2,1)S(1)}, bf16[1,256,192]{1,2,0:T(8,128)(2,1)}, u32[]{:S(2)}) copy-start(bf16[1,256,192]{1,2,0:T(8,128)(2,1)} %param.10) | copy-start | bytes 294916
  18.1 3.6 %copy-start.8 = (bf16[1,64,256]{2,1,0:T(8,128)(2,1)S(1)}, bf16[1,64,256]{2,1,0:T(8,128)(2,1)}, u32[]{:S(2)}) copy-start(bf16[1,64,256]{2,1,0:T(8,128)(2,1)} %param.11) | copy-start | bytes 98308
  18.1 23.4 %all-to-all-start.2 = ((bf16[4,64,1024]{2,1,0:T(8,128)(2,1)}), bf16[4,64,1024]{2,1,0:T(8,128)(2,1)S(1)}, u32[]{:S(2)}, u32[]{:S(2)}) async-start(bf16[4,64,1024]{2,1,0:T(8,128)(2,1)} %get-tuple-element.26), calls=%async_computation.2 | async-start | bytes 1048576 | tf_op jit(solution)/shard_map/all_to_all | solution.py:389
  21.7 8.5 %collective-permute-start.2 = (bf16[272,256]{1,0:T(8,128)(2,1)S(1)}, bf16[272,256]{1,0:T(8,128)(2,1)S(1)}, u32[]{:S(2)}, u32[]{:S(2)}) collective-permute-start(bf16[272,256]{1,0:T(8,128)(2,1)S(1)} %fusion.1.refs_0_), channel_id=1, source_target_pairs={{0,12},{1,13},{2,14},{3,15},{4,8},{5,9},{6,10},{7,11},{8,4},{9,5},... | collective-permute-start | bytes 417800 | tf_op jit(solution)/shard_map/ppermute | solution.py:383
  25.4 10.6 %collective-permute-start.1 = (bf16[272,256]{1,0:T(8,128)(2,1)S(1)}, bf16[272,256]{1,0:T(8,128)(2,1)S(1)}, u32[]{:S(2)}, u32[]{:S(2)}) collective-permute-start(bf16[272,256]{1,0:T(8,128)(2,1)S(1)} %fusion.1.refs_0_), channel_id=1, source_target_pairs={{0,8},{1,9},{2,10},{3,11},{4,12},{5,13},{6,14},{7,15},{8,0},{9,1},... | collective-permute-start | bytes 417800 | tf_op jit(solution)/shard_map/ppermute | solution.py:383
  25.4 10.6 %collective-permute-start = (bf16[272,256]{1,0:T(8,128)(2,1)S(1)}, bf16[272,256]{1,0:T(8,128)(2,1)S(1)}, u32[]{:S(2)}, u32[]{:S(2)}) collective-permute-start(bf16[272,256]{1,0:T(8,128)(2,1)S(1)} %fusion.1.refs_0_), channel_id=1, source_target_pairs={{0,4},{1,5},{2,6},{3,7},{4,0},{5,1},{6,2},{7,3},{8,12},{9,13},{10,... | collective-permute-start | bytes 417800 | tf_op jit(solution)/shard_map/ppermute | solution.py:383
  26.2 11.1 %collective-permute-start.3 = (bf16[272,256]{1,0:T(8,128)(2,1)S(1)}, bf16[272,256]{1,0:T(8,128)(2,1)S(1)}, u32[]{:S(2)}, u32[]{:S(2)}) collective-permute-start(bf16[272,256]{1,0:T(8,128)(2,1)S(1)} %fusion.1.refs_0_), channel_id=1, source_target_pairs={{0,16},{16,0},{1,17},{17,1},{2,18},{18,2},{3,19},{19,3},{4,20},{20... | collective-permute-start | bytes 417800 | tf_op jit(solution)/shard_map/ppermute | solution.py:386
  30.2 7.0 %collective-permute-start.6 = (bf16[272,256]{1,0:T(8,128)(2,1)S(1)}, bf16[272,256]{1,0:T(8,128)(2,1)S(1)}, u32[]{:S(2)}, u32[]{:S(2)}) collective-permute-start(bf16[272,256]{1,0:T(8,128)(2,1)S(1)} %collective-permute-done.2.refs_3_), channel_id=1, source_target_pairs={{0,16},{16,0},{1,17},{17,1},{2,18},{18,2},{3,19},{19,3},{4,20},{20... | collective-permute-start | bytes 417800 | tf_op jit(solution)/shard_map/ppermute | solution.py:386
  36.0 1.4 %collective-permute-start.5 = (bf16[272,256]{1,0:T(8,128)(2,1)S(1)}, bf16[272,256]{1,0:T(8,128)(2,1)S(1)}, u32[]{:S(2)}, u32[]{:S(2)}) collective-permute-start(bf16[272,256]{1,0:T(8,128)(2,1)S(1)} %collective-permute-done.1.refs_2_), channel_id=1, source_target_pairs={{0,16},{16,0},{1,17},{17,1},{2,18},{18,2},{3,19},{19,3},{4,20},{20... | collective-permute-start | bytes 417800 | tf_op jit(solution)/shard_map/ppermute | solution.py:386
  36.0 2.0 %collective-permute-start.4 = (bf16[272,256]{1,0:T(8,128)(2,1)S(1)}, bf16[272,256]{1,0:T(8,128)(2,1)S(1)}, u32[]{:S(2)}, u32[]{:S(2)}) collective-permute-start(bf16[272,256]{1,0:T(8,128)(2,1)S(1)} %collective-permute-done.refs_1_), channel_id=1, source_target_pairs={{0,16},{16,0},{1,17},{17,1},{2,18},{18,2},{3,19},{19,3},{4,20},{20... | collective-permute-start | bytes 417800 | tf_op jit(solution)/shard_map/ppermute | solution.py:386
  36.5 0.7 copy-start.9
  37.4 0.7 copy-start.3
  38.1 0.7 copy-start.5
  38.7 0.9 copy-start.4
  39.6 0.9 copy-start.6
  75.9 2.0 %collective-permute-start.7 = (bf16[4,256,256]{2,1,0:T(8,128)(2,1)S(1)}, bf16[4,256,256]{2,1,0:T(8,128)(2,1)S(1)}, u32[]{:S(2)}, u32[]{:S(2)}) collective-permute-start(bf16[4,256,256]{2,1,0:T(8,128)(2,1)S(1)} %get-tuple-element.39), channel_id=1, source_target_pairs={{0,16},{16,0},{1,17},{17,1},{2,18},{18,2},{3,19},{19,3},{4,20},{20... | collective-permute-start | bytes 1572872 | tf_op jit(solution)/shard_map/ppermute | solution.py:386
  78.5 7.9 %collective-permute-start.8 = (bf16[256,256]{1,0:T(8,128)(2,1)S(1)}, bf16[256,256]{1,0:T(8,128)(2,1)S(1)}, u32[]{:S(2)}, u32[]{:S(2)}) collective-permute-start(bf16[256,256]{1,0:T(8,128)(2,1)S(1)} %get-tuple-element.41), channel_id=1, source_target_pairs={{0,4},{1,5},{2,6},{3,7},{4,0},{5,1},{6,2},{7,3},{8,12},{9,13},{10,... | collective-permute-start | bytes 393224 | tf_op jit(solution)/shard_map/ppermute | solution.py:383
  78.6 13.0 %collective-permute-start.9 = (bf16[256,256]{1,0:T(8,128)(2,1)S(1)}, bf16[256,256]{1,0:T(8,128)(2,1)S(1)}, u32[]{:S(2)}, u32[]{:S(2)}) collective-permute-start(bf16[256,256]{1,0:T(8,128)(2,1)S(1)} %get-tuple-element.42), channel_id=1, source_target_pairs={{0,8},{1,9},{2,10},{3,11},{4,12},{5,13},{6,14},{7,15},{8,0},{9,1},... | collective-permute-start | bytes 393224 | tf_op jit(solution)/shard_map/ppermute | solution.py:383
  81.6 10.0 %collective-permute-start.10 = (bf16[256,256]{1,0:T(8,128)(2,1)S(1)}, bf16[256,256]{1,0:T(8,128)(2,1)S(1)}, u32[]{:S(2)}, u32[]{:S(2)}) collective-permute-start(bf16[256,256]{1,0:T(8,128)(2,1)S(1)} %get-tuple-element.43), channel_id=1, source_target_pairs={{0,12},{1,13},{2,14},{3,15},{4,8},{5,9},{6,10},{7,11},{8,4},{9,5},... | collective-permute-start | bytes 393224 | tf_op jit(solution)/shard_map/ppermute | solution.py:383

commit v2 on v1

--- a/solution.py
+++ b/solution.py
@@ -11,7 +11,7 @@
 BF16 = jnp.bfloat16
 PLANE = 4
 STATS = 16
-VMEM_LIMIT = 32 * 1024 * 1024
+VMEM_LIMIT = 16 * 1024 * 1024
 
 
 def passed_along(block, axis, distance):
@@ -125,14 +125,26 @@
     return lax.dot_general(a, b, (((1,), (1,)), ((), ())), preferred_element_type=F32)
 
 
-def prepare_kernel(planes, index, x_ref, c_ref, xs_ref, cs_ref):
-    width = xs_ref.shape[-1] // planes
-    for z in range(planes):
-        for p in range(PLANE):
-            here = slice((z * PLANE + p) * width, (z * PLANE + p + 1) * width)
-            there = slice(z * width, (z + 1) * width)
-            xs_ref[p, :, there] = x_ref[0, :, here]
-            cs_ref[p, :, there] = c_ref[0, :, here]
+def blocks_kernel(planes, index, x_ref, c_ref, *refs):
+    out_refs, sems = refs[:PLANE], refs[PLANE]
+    width = x_ref.shape[-1] // (planes * PLANE)
+    section, p = index[0], index[2]
+    copies = []
+    for k in range(PLANE):
+        for z in range(planes):
+            at = pl.multiple_of((z * PLANE + (p ^ k)) * width, width)
+            for half, ref in enumerate((x_ref, c_ref)):
+                copies.append(
+                    pltpu.make_async_copy(
+                        ref.at[section, :, pl.ds(at, width)],
+                        out_refs[k].at[half, :, pl.ds(z * width, width)],
+                        sems.at[len(copies)],
+                    )
+                )
+    for copy in copies:
+        copy.start()
+    for copy in copies:
+        copy.wait()
 
 
 def gain_of(w_ref, z, wide):
@@ -164,20 +176,18 @@
     return out.astype(BF16)
 
 
-def spread(out_ref, at, value):
-    for p in range(PLANE):
-        out_ref[p, at : at + value.shape[0], :] = value
-
-
-def first_kernel(planes, heads, index, docs, x_ref, *refs):
-    own, other = refs[:planes], refs[planes : 2 * planes]
-    w0_ref, w1_ref, out_ref = refs[2 * planes :]
+def first_kernel(planes, heads, index, docs, *refs):
+    blocks, own, other = refs[:PLANE], refs[PLANE : PLANE + planes], refs[PLANE + planes : PLANE + 2 * planes]
+    x_ref, c_ref, w0_ref, w1_ref, out_ref = refs[PLANE + 2 * planes :]
     qkv_rows, out_rows = 3 * heads, heads
     section, z, p = index[0], index[1], index[2]
     for k in range(planes):
         mine, theirs = own[k][...], other[k][...]
         w0_ref[z ^ k] = jnp.where(section == 0, mine, theirs)
         w1_ref[z ^ k] = jnp.where(section == 0, theirs, mine)
+    for k in range(PLANE):
+        x_ref[p ^ k] = blocks[k][0]
+        c_ref[p ^ k] = blocks[k][1]
     width = x_ref.shape[-1] // planes
     rows = x_ref.shape[0] * x_ref.shape[1]
 
@@ -186,17 +196,17 @@
         return x.reshape(rows, width).astype(F32)
 
     total, squares = partial_qkv(x_of, w0_ref, qkv_rows, out_rows)
-    spread(out_ref, 0, total.astype(BF16))
+    out_ref[:qkv_rows, :] = total.astype(BF16)
     position = lax.broadcasted_iota(jnp.int32, (STATS, rows), 1)
     block = rows // PLANE
     local = position - p * block
-    ends = docs[0]
+    ends = docs[section, 0, 0]
     seg = (local >= ends).astype(F32)
-    for i in range(1, docs.shape[0]):
-        ends = ends + docs[i]
+    for i in range(1, docs.shape[2]):
+        ends = ends + docs[section, 0, i]
         seg = seg + (local >= ends).astype(F32)
     seg = jnp.where((local >= 0) & (local < block), seg, 0.0)
-    spread(out_ref, qkv_rows, stat_rows(squares, seg))
+    out_ref[qkv_rows:, :] = stat_rows(squares, seg)
 
 
 def attention(qkv_t, codes_row, codes_col, heads):
@@ -227,17 +237,17 @@
     return jnp.concatenate([d_query, d_keys, d_values], axis=0).astype(BF16)
 
 
-def summed(parts_ref, start, stop):
-    total = parts_ref[0, start:stop, :].astype(F32)
-    for p in range(1, PLANE):
-        total = total + parts_ref[p, start:stop, :].astype(F32)
+def summed(parts, start, stop):
+    total = parts[0][start:stop, :].astype(F32)
+    for part in parts[1:]:
+        total = total + part[start:stop, :].astype(F32)
     return total
 
 
-def scaled(parts_ref, qkv_rows, features):
-    stats = summed(parts_ref, qkv_rows, qkv_rows + STATS)
+def scaled(parts, qkv_rows, features):
+    stats = summed(parts, qkv_rows, qkv_rows + STATS)
     scale = lax.rsqrt((stats[0:1, :] + stats[1:2, :]) / features + 1e-05)
-    qkv_t = (summed(parts_ref, 0, qkv_rows) * scale).astype(BF16).astype(F32)
+    qkv_t = (summed(parts, 0, qkv_rows) * scale).astype(BF16).astype(F32)
     return qkv_t, scale, stats
 
 
@@ -246,14 +256,14 @@
     return jnp.transpose(jnp.broadcast_to(row, (128, count)))[:, 0:1]
 
 
-def second_kernel(
-    features, heads, parts_ref, x_ref, c_ref, w0_ref, w1_ref, out_ref, y_ref, qkv_ref, probs_ref, att_ref, stat_ref
-):
+def second_kernel(features, heads, *refs):
+    parts, (x_ref, c_ref, w0_ref, w1_ref) = refs[:PLANE], refs[PLANE : PLANE + 4]
+    out_ref, y_ref, qkv_ref, probs_ref, att_ref, stat_ref = refs[PLANE + 4 :]
     planes = w0_ref.shape[0]
     qkv_rows, out_rows = 3 * heads, heads
     width = x_ref.shape[-1] // planes
     rows = x_ref.shape[0] * x_ref.shape[1]
-    qkv_t, scale, stats = scaled(parts_ref, qkv_rows, features)
+    qkv_t, scale, stats = scaled(parts, qkv_rows, features)
     block = lax.broadcasted_iota(jnp.int32, (1, rows), 1) // (rows // PLANE)
     codes = stats[2:3, :] + (block * rows).astype(F32)
     probs, att_t = attention(qkv_t, codes, column(codes), heads)
@@ -274,20 +284,20 @@
     total, squares = partial_qkv(
         lambda z: y_ref[:, z * width : (z + 1) * width].astype(F32), w1_ref, qkv_rows, out_rows
     )
-    spread(out_ref, 0, total.astype(BF16))
-    spread(out_ref, qkv_rows, stat_rows(squares, None))
-    spread(out_ref, qkv_rows + STATS, d_att.astype(BF16))
-
-
-def third_kernel(
-    features, heads, parts_ref, c_ref, y_ref, att_ref, stat_ref, w0_ref, w1_ref, out_ref, g0_ref, g1_ref
-):
+    out_ref[:qkv_rows, :] = total.astype(BF16)
+    out_ref[qkv_rows : qkv_rows + STATS, :] = stat_rows(squares, None)
+    out_ref[qkv_rows + STATS :, :] = d_att.astype(BF16)
+
+
+def third_kernel(features, heads, *refs):
+    parts, (c_ref, y_ref, att_ref, stat_ref, w0_ref, w1_ref) = refs[:PLANE], refs[PLANE : PLANE + 6]
+    out_ref, g0_ref, g1_ref = refs[PLANE + 6 :]
     planes = w0_ref.shape[0]
     qkv_rows, out_rows = 3 * heads, heads
     width = y_ref.shape[-1] // planes
     rows = y_ref.shape[0]
-    qkv_t, scale, _ = scaled(parts_ref, qkv_rows, features)
-    d_att_t = summed(parts_ref, qkv_rows + STATS, qkv_rows + STATS + heads).astype(BF16)
+    qkv_t, scale, _ = scaled(parts, qkv_rows, features)
+    d_att_t = summed(parts, qkv_rows + STATS, qkv_rows + STATS + heads).astype(BF16)
     codes = stat_ref[1:2, :]
     probs, att_t = attention(qkv_t, codes, column(codes), heads)
     d_qkv_t = attention_grad(qkv_t, probs, d_att_t, heads)
@@ -310,18 +320,18 @@
         g0_ref[z] = nn(att0_t, d_y).astype(g0_ref.dtype)
         part = nt(w0_ref[z, qkv_rows : qkv_rows + out_rows, :], d_y)
         d_att = part if d_att is None else d_att + part
-    spread(out_ref, 0, d_att.astype(BF16))
-
-
-def fourth_kernel(
-    heads, index, parts_ref, x_ref, qkv_ref, probs_ref, stat_ref, w0_ref, g0_ref, g1_ref, keep_ref, send_ref
-):
+    out_ref[...] = d_att.astype(BF16)
+
+
+def fourth_kernel(heads, index, *refs):
+    parts, (x_ref, qkv_ref, probs_ref, stat_ref, w0_ref, g0_ref, g1_ref) = refs[:PLANE], refs[PLANE : PLANE + 7]
+    keep_ref, send_ref = refs[PLANE + 7 :]
     planes = w0_ref.shape[0]
     qkv_rows, out_rows = 3 * heads, heads
     width = x_ref.shape[-1] // planes
     rows = x_ref.shape[0] * x_ref.shape[1]
-    section, place = index[0], index[1]
-    d_att_t = summed(parts_ref, 0, heads).astype(BF16)
+    section = index[0]
+    d_att_t = summed(parts, 0, heads).astype(BF16)
     d_qkv_t = attention_grad(qkv_ref[...], probs_ref[...], d_att_t, heads)
     scale_col = column(stat_ref[0:1, :])
     for z in range(planes):
@@ -376,8 +386,6 @@
     heads, width = w_out.shape[1:]
     qkv_rows = w_qkv.shape[2]
     cols = planes * width
-    in_plane = [[a * PLANE + b for b in range(PLANE)] for a in range(planes)]
-
     def along_z(value, k):
         route = [(a * PLANE + b, (a ^ k) * PLANE + b) for a in range(planes) for b in range(PLANE)]
         return lax.ppermute(value, "dp", route)
@@ -385,8 +393,12 @@
     def to_sibling(value):
         return lax.ppermute(value, "section", [(0, 1), (1, 0)])
 
+    def along_plane(value, k):
+        route = [(a * PLANE + b, a * PLANE + (b ^ k)) for a in range(planes) for b in range(PLANE)]
+        return lax.ppermute(value, "dp", route)
+
     def exchange(value):
-        return lax.all_to_all(value, "dp", 0, 0, axis_index_groups=in_plane, tiled=True)
+        return [value] + [along_plane(value, k) for k in range(1, PLANE)]
 
     gain = lax.dynamic_slice(norm_gain, (0, place * width), (1, width))
     pack = jnp.concatenate(
@@ -394,57 +406,50 @@
     )
     own = [pack] + [along_z(pack, k) for k in range(1, planes)]
 
-    one_batch = pl.BlockSpec((1, block, features), lambda i, index: (index[0], 0, 0))
-    split = pl.BlockSpec((PLANE, block, cols), lambda i, index: (0, 0, 0))
-    xs, cs = pl.pallas_call(
-        functools.partial(prepare_kernel, planes),
-        grid_spec=pltpu.PrefetchScalarGridSpec(
-            num_scalar_prefetch=1,
-            grid=(1,),
-            in_specs=[one_batch, one_batch],
-            out_specs=[split, split],
-        ),
-        out_shape=[jax.ShapeDtypeStruct((PLANE, block, cols), BF16)] * 2,
+    blocks = pl.pallas_call(
+        functools.partial(blocks_kernel, planes),
+        out_shape=[jax.ShapeDtypeStruct((2, block, cols), BF16)] * PLANE,
+        in_specs=[pl.BlockSpec(memory_space=pltpu.SMEM)] + [pl.BlockSpec(memory_space=pltpu.HBM)] * 2,
+        out_specs=[pl.BlockSpec(memory_space=pltpu.VMEM)] * PLANE,
+        scratch_shapes=[pltpu.SemaphoreType.DMA((2 * PLANE * planes,))],
         compiler_params=pltpu.CompilerParams(vmem_limit_bytes=VMEM_LIMIT),
     )(index, inputs, cotangent)
-    x = exchange(xs)
-    c = exchange(cs)
+    blocks = [blocks[0]] + [along_plane(blocks[k], k) for k in range(1, PLANE)]
     other = [to_sibling(piece) for piece in own]
 
-    docs = lax.dynamic_index_in_dim(doc_lengths, section, 0, keepdims=False)[0]
     weights = ((planes,) + pack.shape, BF16)
-    w0, w1, sent = call(
+    split = ((PLANE, block, cols), BF16)
+    x, c, w0, w1, sent = call(
         functools.partial(first_kernel, planes, heads),
-        [weights, weights, ((PLANE, qkv_rows + STATS, rows), BF16)],
-        index, docs, x, *own, *other, scalars=2,
-    )
-    y, qkv, probs, att, stats = None, None, None, None, None
+        [split, split, weights, weights, ((qkv_rows + STATS, rows), BF16)],
+        index, doc_lengths, *blocks, *own, *other, scalars=2,
+    )
     sent, y, qkv, probs, att, stats = call(
         functools.partial(second_kernel, features, heads),
         [
-            ((PLANE, qkv_rows + STATS + heads, rows), BF16),
+            ((qkv_rows + STATS + heads, rows), BF16),
             ((rows, cols), BF16),
             ((qkv_rows, rows), F32),
             ((rows, rows), F32),
             ((heads, rows), BF16),
             ((8, rows), F32),
         ],
-        exchange(sent), x, c, w0, w1,
+        *exchange(sent), x, c, w0, w1,
     )
     sent, g0, g1 = call(
         functools.partial(third_kernel, features, heads),
         [
-            ((PLANE, heads, rows), BF16),
+            ((heads, rows), BF16),
             ((planes, heads, width), F32),
             ((planes, qkv_rows + heads, width), F32),
         ],
-        exchange(sent), c, y, att, stats, w0, w1,
+        *exchange(sent), c, y, att, stats, w0, w1,
     )
     grads = (planes, qkv_rows + heads, width)
     keep, send = call(
         functools.partial(fourth_kernel, heads),
         [(grads, F32), (grads, BF16)],
-        index, exchange(sent), x, qkv, probs, stats, w0, g0, g1, scalars=1,
+        index, *exchange(sent), x, qkv, probs, stats, w0, g0, g1, scalars=1,
     )
     merged = call(
         merge_kernel,

time: 92.8 us -> 72 us (0.78)
  blocking collectives: 29.9 us -> 0 us
  starting transfers between devices: 18.2 us -> 25.1 us
  waiting for transfers between devices: 28.6 us -> 33.6 us
  local copies, waits for them, and re-layouts: 6.29 us -> 3.17 us
    all_to_all x3 -> x0, blocking collectives: 29.9 us -> none  [exchange(): lax.all_to_all(value, 'dp', 0, 0, axis_index_groups=in_plane, tiled=True)]
    ppermute x0 -> x12, waiting for transfers between devices: none -> 15.6 us  [along_plane(): return lax.ppermute(value, 'dp', route)]
    ppermute x0 -> x12, starting transfers between devices: none -> 14 us  [along_plane(): return lax.ppermute(value, 'dp', route)]
    all_to_all x2 -> x0, starting transfers between devices: 8.76 us -> none  [exchange(): lax.all_to_all(value, 'dp', 0, 0, axis_index_groups=in_plane, tiled=True)]
    all_to_all x2 -> x0, waiting for transfers between devices: 8.01 us -> none  [exchange(): lax.all_to_all(value, 'dp', 0, 0, axis_index_groups=in_plane, tiled=True)]
    unnamed x20 -> x8, local copies, waits for them, and re-layouts: 6.28 us -> 3.16 us
    ppermute x6, waiting for transfers between devices: 18.5 us -> 16.1 us  [along_z(): return lax.ppermute(value, 'dp', route)]
    ppermute x6, starting transfers between devices: 8.9 us -> 9.94 us  [along_z(): return lax.ppermute(value, 'dp', route)]
  transfers between devices with their start and end apart: 13 -> 23, of which waited for: 7 -> 13; matrix products, arithmetic and copies ran while one was open for 0% -> 0% of each run, Pallas kernels for 1% -> 2%
where the time goes in v2:
time: 72 us; the launch traced here: 71.7 us
  waiting for transfers between devices  33.6 us (47%)
  starting transfers between devices  25.1 us (35%)
  Pallas kernels  8.1 us (11%)
  local copies, waits for them, and re-layouts  3.17 us (4%)
  other arithmetic  1 us (1%)
  between operations  0.73 us (1%)
    ppermute x6, waiting for transfers between devices, along_z(): return lax.ppermute(value, 'dp', route)  16.1 us
    ppermute x12, waiting for transfers between devices, along_plane(): return lax.ppermute(value, 'dp', route)  15.6 us
    ppermute x12, starting transfers between devices, along_plane(): return lax.ppermute(value, 'dp', route)  14 us
    ppermute x6, starting transfers between devices, along_z(): return lax.ppermute(value, 'dp', route)  9.94 us
    pallas_call x6, Pallas kernels, call(): pl.pallas_call(kernel, out_shape=[jax.ShapeDtypeStruct(shape, dtype) for...  6.98 us
    unnamed x8, local copies, waits for them, and re-layouts  3.16 us
    ppermute x5, waiting for transfers between devices, to_sibling(): return lax.ppermute(value, 'section', [(0, 1), (1, 0)])  1.91 us
  transfers between devices with their start and end apart: 23, of which 13 were waited for; matrix products, arithmetic and copies ran while one was open for 0% of the time, Pallas kernels for 2%

profile of v2, /device:TPU:0, one launch (start us, length us, event | category | flops | bytes accessed | tf_op | source)
XLA Modules:
  0.0 71.7 jit_solution(14122769359556057798)
XLA Ops:
  0.6 0.0 copy-start
  0.7 0.7 copy-done
  1.4 0.9 %fusion.1.refs_4_ = bf16[272,256]{1,0:T(8,128)(2,1)S(1)} fusion(bf16[1,256]{1,0:T(2,128)(2,1)S(1)} %constant_dynamic-slice_fusion, bf16[64,256]{1,0:T(8,128)(2,1)} %bitcast.12, bf16[192,256]{1,0:T(8,128)(2,1)} %bitcast.11), kind=kLoop, calls=%fused_computation.2 | loop fusion | flops 557056 | bytes 270848 | tf_op jit(solution)/shard_map/concatenate | solution.py:404
  2.3 0.5 collective-permute-start.6
  2.8 4.7 %collective-permute-start.5 = (bf16[272,256]{1,0:T(8,128)(2,1)S(1)}, bf16[272,256]{1,0:T(8,128)(2,1)S(1)}, u32[]{:S(2)}, u32[]{:S(2)}) collective-permute-start(bf16[272,256]{1,0:T(8,128)(2,1)S(1)} %fusion.1.refs_4_), channel_id=1, source_target_pairs={{0,12},{1,13},{2,14},{3,15},{4,8},{5,9},{6,10},{7,11},{8,4},{9,5},... | collective-permute-start | bytes 417800 | tf_op jit(solution)/shard_map/ppermute | solution.py:391
  7.5 0.1 pad_add_fusion.index
  7.6 0.0 copy-start.1
  7.6 1.2 %copy-done.1 = bf16[2,64,4096]{2,1,0:T(8,128)(2,1)S(1)} copy-done((bf16[2,64,4096]{2,1,0:T(8,128)(2,1)S(1)}, bf16[2,64,4096]{2,1,0:T(8,128)(2,1)}, u32[]{:S(2)}) %copy-start.1) | copy-done | bytes 1048600
  8.8 0.0 copy-start.2
  8.8 1.2 %copy-done.2 = bf16[2,64,4096]{2,1,0:T(8,128)(2,1)S(1)} copy-done((bf16[2,64,4096]{2,1,0:T(8,128)(2,1)S(1)}, bf16[2,64,4096]{2,1,0:T(8,128)(2,1)}, u32[]{:S(2)}) %copy-start.2) | copy-done | bytes 1048600
  10.0 1.1 %shard_map.77 = (bf16[2,64,1024]{2,1,0:T(8,128)(2,1)S(1)}, bf16[2,64,1024]{2,1,0:T(8,128)(2,1)S(1)}, bf16[2,64,1024]{2,1,0:T(8,128)(2,1)S(1)}, bf16[2,64,1024]{2,1,0:T(8,128)(2,1)S(1)}) custom-call(s32[3]{0:T(128)S(1)} %pad_add_fusion.index, bf16[2,64,4096]{2,1,0:T(8,128)(2,1)S(1)} %copy-done.1, bf16[2,64,4096]{2,1,0:T(8,128)(2,1)S(1)} %copy-done.2), custom_call_target="tpu_custom_call" | custom-call | tf_op jit(solution)/shard_map/pallas_call | solution.py:409
  11.1 1.6 %collective-permute-start = (bf16[2,64,1024]{2,1,0:T(8,128)(2,1)S(1)}, bf16[2,64,1024]{2,1,0:T(8,128)(2,1)S(1)}, u32[]{:S(2)}, u32[]{:S(2)}) collective-permute-start(bf16[2,64,1024]{2,1,0:T(8,128)(2,1)S(1)} %get-tuple-element.29), channel_id=1, source_target_pairs={{0,1},{1,0},{2,3},{3,2},{4,5},{5,4},{6,7},{7,6},{8,9},{9,8},{10,11... | collective-permute-start | bytes 786440 | tf_op jit(solution)/shard_map/ppermute | solution.py:398
  12.7 0.0 collective-permute-start.4
  12.7 0.8 %collective-permute-start.3 = (bf16[272,256]{1,0:T(8,128)(2,1)S(1)}, bf16[272,256]{1,0:T(8,128)(2,1)S(1)}, u32[]{:S(2)}, u32[]{:S(2)}) collective-permute-start(bf16[272,256]{1,0:T(8,128)(2,1)S(1)} %fusion.1.refs_4_), channel_id=1, source_target_pairs={{0,4},{1,5},{2,6},{3,7},{4,0},{5,1},{6,2},{7,3},{8,12},{9,13},{10,... | collective-permute-start | bytes 417800 | tf_op jit(solution)/shard_map/ppermute | solution.py:391
  13.5 0.0 collective-permute-done.6.refs_8_
  13.5 1.5 %collective-permute-start.1 = (bf16[2,64,1024]{2,1,0:T(8,128)(2,1)S(1)}, bf16[2,64,1024]{2,1,0:T(8,128)(2,1)S(1)}, u32[]{:S(2)}, u32[]{:S(2)}) collective-permute-start(bf16[2,64,1024]{2,1,0:T(8,128)(2,1)S(1)} %get-tuple-element.30), channel_id=1, source_target_pairs={{0,2},{1,3},{2,0},{3,1},{4,6},{5,7},{6,4},{7,5},{8,10},{9,11},{10,... | collective-permute-start | bytes 786440 | tf_op jit(solution)/shard_map/ppermute | solution.py:398
  15.0 0.0 collective-permute-done.5.refs_7_
  15.0 0.0 copy-start.3
  15.0 0.3 collective-permute-start.2
  15.3 5.8 %collective-permute-done.4.refs_6_ = bf16[272,256]{1,0:T(8,128)(2,1)S(1)} collective-permute-done((bf16[272,256]{1,0:T(8,128)(2,1)S(1)}, bf16[272,256]{1,0:T(8,128)(2,1)S(1)}, u32[]{:S(2)}, u32[]{:S(2)}) %collective-permute-start.4) | collective-permute-done | bytes 139296 | tf_op jit(solution)/shard_map/ppermute | solution.py:391
  21.1 0.0 collective-permute-start.9
  21.1 0.0 collective-permute-done.3.refs_5_
  21.1 0.5 collective-permute-start.8
  21.6 0.0 collective-permute-done.refs_1_
  21.7 0.1 collective-permute-start.7
  21.7 5.0 %collective-permute-done.1.refs_2_ = bf16[2,64,1024]{2,1,0:T(8,128)(2,1)S(1)} collective-permute-done((bf16[2,64,1024]{2,1,0:T(8,128)(2,1)S(1)}, bf16[2,64,1024]{2,1,0:T(8,128)(2,1)S(1)}, u32[]{:S(2)}, u32[]{:S(2)}) %collective-permute-start.1) | collective-permute-done | bytes 262176 | tf_op jit(solution)/shard_map/ppermute | solution.py:398
  26.7 0.0 collective-permute-done.2.refs_3_
  26.7 0.0 collective-permute-done.9.refs_11_
  26.7 0.0 collective-permute-done.8.refs_10_
  26.7 0.0 collective-permute-done.7.refs_9_
  26.7 0.0 copy-done.3
  26.7 1.1 %shard_map.78 = (bf16[4,64,1024]{2,1,0:T(8,128)(2,1)S(1)}, bf16[4,64,1024]{2,1,0:T(8,128)(2,1)S(1)}, bf16[4,272,256]{2,1,0:T(8,128)(2,1)S(1)}, bf16[4,272,256]{2,1,0:T(8,128)(2,1)S(1)}, bf16[208,256]{1,0:T(8,128)(2,1)S(1)}) custom-call(s32[3]{0:T(128)S(1)} %pad_add_fusion.index, s32[2,1,2]{2,1,0:T(1,128)S(1)} %copy-done.3, ...), custom_call_target="tpu_custom_call" | custom-call | tf_op jit(solution)/shard_map/pallas_call | solution.py:369
  27.8 1.6 %collective-permute-start.12 = (bf16[208,256]{1,0:T(8,128)(2,1)S(1)}, bf16[208,256]{1,0:T(8,128)(2,1)S(1)}, u32[]{:S(2)}, u32[]{:S(2)}) collective-permute-start(bf16[208,256]{1,0:T(8,128)(2,1)S(1)} %get-tuple-element.32.refs_0_), channel_id=1, source_target_pairs={{0,3},{1,2},{2,1},{3,0},{4,7},{5,6},{6,5},{7,4},{8,11},{9,10},{10,... | collective-permute-start | bytes 319496 | tf_op jit(solution)/shard_map/ppermute | solution.py:398
  29.4 0.9 %collective-permute-start.11 = (bf16[208,256]{1,0:T(8,128)(2,1)S(1)}, bf16[208,256]{1,0:T(8,128)(2,1)S(1)}, u32[]{:S(2)}, u32[]{:S(2)}) collective-permute-start(bf16[208,256]{1,0:T(8,128)(2,1)S(1)} %get-tuple-element.32.refs_0_), channel_id=1, source_target_pairs={{0,2},{1,3},{2,0},{3,1},{4,6},{5,7},{6,4},{7,5},{8,10},{9,11},{10,... | collective-permute-start | bytes 319496 | tf_op jit(solution)/shard_map/ppermute | solution.py:398
  30.3 1.1 %collective-permute-start.10 = (bf16[208,256]{1,0:T(8,128)(2,1)S(1)}, bf16[208,256]{1,0:T(8,128)(2,1)S(1)}, u32[]{:S(2)}, u32[]{:S(2)}) collective-permute-start(bf16[208,256]{1,0:T(8,128)(2,1)S(1)} %get-tuple-element.32.refs_0_), channel_id=1, source_target_pairs={{0,1},{1,0},{2,3},{3,2},{4,5},{5,4},{6,7},{7,6},{8,9},{9,8},{10,11... | collective-permute-start | bytes 319496 | tf_op jit(solution)/shard_map/ppermute | solution.py:398
  31.4 2.6 %collective-permute-done.12.refs_3_ = bf16[208,256]{1,0:T(8,128)(2,1)S(1)} collective-permute-done((bf16[208,256]{1,0:T(8,128)(2,1)S(1)}, bf16[208,256]{1,0:T(8,128)(2,1)S(1)}, u32[]{:S(2)}, u32[]{:S(2)}) %collective-permute-start.12) | collective-permute-done | bytes 106528 | tf_op jit(solution)/shard_map/ppermute | solution.py:398
  34.0 0.9 %collective-permute-done.11.refs_2_ = bf16[208,256]{1,0:T(8,128)(2,1)S(1)} collective-permute-done((bf16[208,256]{1,0:T(8,128)(2,1)S(1)}, bf16[208,256]{1,0:T(8,128)(2,1)S(1)}, u32[]{:S(2)}, u32[]{:S(2)}) %collective-permute-start.11) | collective-permute-done | bytes 106528 | tf_op jit(solution)/shard_map/ppermute | solution.py:398
  34.9 0.2 collective-permute-done.10.refs_1_
  35.1 1.2 %shard_map.79 = (bf16[272,256]{1,0:T(8,128)(2,1)S(1)}, bf16[256,1024]{1,0:T(8,128)(2,1)S(1)}, f32[192,256]{1,0:T(8,128)S(1)}, f32[256,256]{1,0:T(8,128)S(1)}, bf...) custom-call(bf16[208,256]{1,0:T(8,128)(2,1)S(1)} %get-tuple-element.32.refs_0_, ...), custom_call_target="tpu_custom_call" | custom-call | tf_op jit(solution)/shard_map/pallas_call | solution.py:369
  36.3 2.0 %collective-permute-start.15 = (bf16[272,256]{1,0:T(8,128)(2,1)S(1)}, bf16[272,256]{1,0:T(8,128)(2,1)S(1)}, u32[]{:S(2)}, u32[]{:S(2)}) collective-permute-start(bf16[272,256]{1,0:T(8,128)(2,1)S(1)} %get-tuple-element.37.refs_0_), channel_id=1, source_target_pairs={{0,3},{1,2},{2,1},{3,0},{4,7},{5,6},{6,5},{7,4},{8,11},{9,10},{10,... | collective-permute-start | bytes 417800 | tf_op jit(solution)/shard_map/ppermute | solution.py:398
  38.4 0.6 collective-permute-start.14
  39.0 0.9 %collective-permute-start.13 = (bf16[272,256]{1,0:T(8,128)(2,1)S(1)}, bf16[272,256]{1,0:T(8,128)(2,1)S(1)}, u32[]{:S(2)}, u32[]{:S(2)}) collective-permute-start(bf16[272,256]{1,0:T(8,128)(2,1)S(1)} %get-tuple-element.37.refs_0_), channel_id=1, source_target_pairs={{0,1},{1,0},{2,3},{3,2},{4,5},{5,4},{6,7},{7,6},{8,9},{9,8},{10,11... | collective-permute-start | bytes 417800 | tf_op jit(solution)/shard_map/ppermute | solution.py:398
  39.9 2.8 %collective-permute-done.15.refs_3_ = bf16[272,256]{1,0:T(8,128)(2,1)S(1)} collective-permute-done((bf16[272,256]{1,0:T(8,128)(2,1)S(1)}, bf16[272,256]{1,0:T(8,128)(2,1)S(1)}, u32[]{:S(2)}, u32[]{:S(2)}) %collective-permute-start.15) | collective-permute-done | bytes 139296 | tf_op jit(solution)/shard_map/ppermute | solution.py:398
  42.7 1.4 %collective-permute-done.14.refs_2_ = bf16[272,256]{1,0:T(8,128)(2,1)S(1)} collective-permute-done((bf16[272,256]{1,0:T(8,128)(2,1)S(1)}, bf16[272,256]{1,0:T(8,128)(2,1)S(1)}, u32[]{:S(2)}, u32[]{:S(2)}) %collective-permute-start.14) | collective-permute-done | bytes 139296 | tf_op jit(solution)/shard_map/ppermute | solution.py:398
  44.1 0.0 collective-permute-done.13.refs_1_
  44.1 1.9 %shard_map.80 = (bf16[64,256]{1,0:T(8,128)(2,1)S(1)}, f32[4,64,256]{2,1,0:T(8,128)S(1)}, f32[4,256,256]{2,1,0:T(8,128)S(1)}) custom-call(bf16[272,256]{1,0:T(8,128)(2,1)S(1)} %get-tuple-element.37.refs_0_, bf16[272,256]{1,0:T(8,128)(2,1)S(1)} %collective-permute-done.13.refs_1_, bf16[272,256]{1,0:T(8,128)(2,1)S(1)} %collective-permute-done.14.refs_2_, ...), custom_call_target="tpu_custom_call" | custom-call | tf_op jit(solution)/shard_map/pallas_call | solution.py:369
  46.1 1.7 %collective-permute-start.18 = (bf16[64,256]{1,0:T(8,128)(2,1)S(1)}, bf16[64,256]{1,0:T(8,128)(2,1)S(1)}, u32[]{:S(2)}, u32[]{:S(2)}) collective-permute-start(bf16[64,256]{1,0:T(8,128)(2,1)S(1)} %get-tuple-element.41.refs_0_), channel_id=1, source_target_pairs={{0,3},{1,2},{2,1},{3,0},{4,7},{5,6},{6,5},{7,4},{8,11},{9,10},{10,... | collective-permute-start | bytes 98312 | tf_op jit(solution)/shard_map/ppermute | solution.py:398
  47.7 0.6 collective-permute-start.17
  48.3 1.2 %collective-permute-start.16 = (bf16[64,256]{1,0:T(8,128)(2,1)S(1)}, bf16[64,256]{1,0:T(8,128)(2,1)S(1)}, u32[]{:S(2)}, u32[]{:S(2)}) collective-permute-start(bf16[64,256]{1,0:T(8,128)(2,1)S(1)} %get-tuple-element.41.refs_0_), channel_id=1, source_target_pairs={{0,1},{1,0},{2,3},{3,2},{4,5},{5,4},{6,7},{7,6},{8,9},{9,8},{10,11... | collective-permute-start | bytes 98312 | tf_op jit(solution)/shard_map/ppermute | solution.py:398
  49.6 1.3 %collective-permute-done.18.refs_3_ = bf16[64,256]{1,0:T(8,128)(2,1)S(1)} collective-permute-done((bf16[64,256]{1,0:T(8,128)(2,1)S(1)}, bf16[64,256]{1,0:T(8,128)(2,1)S(1)}, u32[]{:S(2)}, u32[]{:S(2)}) %collective-permute-start.18) | collective-permute-done | bytes 32800 | tf_op jit(solution)/shard_map/ppermute | solution.py:398
  50.9 0.8 %collective-permute-done.17.refs_2_ = bf16[64,256]{1,0:T(8,128)(2,1)S(1)} collective-permute-done((bf16[64,256]{1,0:T(8,128)(2,1)S(1)}, bf16[64,256]{1,0:T(8,128)(2,1)S(1)}, u32[]{:S(2)}, u32[]{:S(2)}) %collective-permute-start.17) | collective-permute-done | bytes 32800 | tf_op jit(solution)/shard_map/ppermute | solution.py:398
  51.7 0.6 collective-permute-done.16.refs_1_
  52.3 1.3 %shard_map.81 = (f32[4,256,256]{2,1,0:T(8,128)S(1)}, bf16[4,256,256]{2,1,0:T(8,128)(2,1)S(1)}) custom-call(s32[3]{0:T(128)S(1)} %pad_add_fusion.index, bf16[64,256]{1,0:T(8,128)(2,1)S(1)} %get-tuple-element.41.refs_0_, bf16[64,256]{1,0:T(8,128)(2,1)S(1)} %collective-permute-done.16.refs_1_, bf16[64,256]{1,0:T(8,128)(2,1)S(1)} %collective-permute-done.17.refs_2_, ...), custom_call_target="tpu_custom_call" | custom-call | tf_op jit(solution)/shard_map/pallas_call | solution.py:369
  53.6 0.1 collective-permute-start.19
  53.7 1.9 %collective-permute-done.19.come_ref = bf16[4,256,256]{2,1,0:T(8,128)(2,1)S(1)} collective-permute-done((bf16[4,256,256]{2,1,0:T(8,128)(2,1)S(1)}, bf16[4,256,256]{2,1,0:T(8,128)(2,1)S(1)}, u32[]{:S(2)}, u32[]{:S(2)}) %collective-permute-start.19) | collective-permute-done | bytes 524320 | tf_op jit(solution)/shard_map/ppermute | solution.py:394
  55.6 0.7 shard_map.82
  56.2 1.8 %collective-permute-start.20 = (bf16[256,256]{1,0:T(8,128)(2,1)S(1)}, bf16[256,256]{1,0:T(8,128)(2,1)S(1)}, u32[]{:S(2)}, u32[]{:S(2)}) collective-permute-start(bf16[256,256]{1,0:T(8,128)(2,1)S(1)} %get-tuple-element.49), channel_id=1, source_target_pairs={{0,4},{1,5},{2,6},{3,7},{4,0},{5,1},{6,2},{7,3},{8,12},{9,13},{10,... | collective-permute-start | bytes 393224 | tf_op jit(solution)/shard_map/ppermute | solution.py:391
  58.1 2.6 %collective-permute-start.21 = (bf16[256,256]{1,0:T(8,128)(2,1)S(1)}, bf16[256,256]{1,0:T(8,128)(2,1)S(1)}, u32[]{:S(2)}, u32[]{:S(2)}) collective-permute-start(bf16[256,256]{1,0:T(8,128)(2,1)S(1)} %get-tuple-element.50), channel_id=1, source_target_pairs={{0,8},{1,9},{2,10},{3,11},{4,12},{5,13},{6,14},{7,15},{8,0},{9,1},... | collective-permute-start | bytes 393224 | tf_op jit(solution)/shard_map/ppermute | solution.py:391
  60.7 0.0 collective-permute-start.22
  60.7 3.0 %collective-permute-done.20.refs_0_ = bf16[256,256]{1,0:T(8,128)(2,1)S(1)} collective-permute-done((bf16[256,256]{1,0:T(8,128)(2,1)S(1)}, bf16[256,256]{1,0:T(8,128)(2,1)S(1)}, u32[]{:S(2)}, u32[]{:S(2)}) %collective-permute-start.20) | collective-permute-done | bytes 131104 | tf_op jit(solution)/shard_map/ppermute | solution.py:391
  63.7 7.3 %collective-permute-done.21.refs_1_ = bf16[256,256]{1,0:T(8,128)(2,1)S(1)} collective-permute-done((bf16[256,256]{1,0:T(8,128)(2,1)S(1)}, bf16[256,256]{1,0:T(8,128)(2,1)S(1)}, u32[]{:S(2)}, u32[]{:S(2)}) %collective-permute-start.21) | collective-permute-done | bytes 131104 | tf_op jit(solution)/shard_map/ppermute | solution.py:391
  71.0 0.0 collective-permute-done.22.refs_2_
  71.0 0.7 %shard_map.83 = (f32[192,256]{1,0:T(8,128)}, f32[64,256]{1,0:T(8,128)}) custom-call(f32[256,256]{1,0:T(8,128)S(1)} %get-tuple-element.48.keep_ref, bf16[256,256]{1,0:T(8,128)(2,1)S(1)} %collective-permute-done.20.refs_0_, bf16[256,256]{1,0:T(8,128)(2,1)S(1)} %collective-permute-done.21.refs_1_, bf16[256,256]{1,0:T(8,128)(2,1)S(1)} %collective-permute-done.22.refs_2_), custom_call_target="tpu_custom_call" | custom-call | tf_op jit(solution)/shard_map/pallas_call | solution.py:369
  (1 shorter events, 0.0 us)
Async XLA Ops:
  0.6 0.7 %copy-start = (bf16[1,4096]{1,0:T(2,128)(2,1)S(1)}, bf16[1,4096]{1,0:T(2,128)(2,1)}, u32[]{:S(2)}) copy-start(bf16[1,4096]{1,0:T(2,128)(2,1)} %param.9) | copy-start | bytes 24580
  2.3 11.2 %collective-permute-start.6 = (bf16[272,256]{1,0:T(8,128)(2,1)S(1)}, bf16[272,256]{1,0:T(8,128)(2,1)S(1)}, u32[]{:S(2)}, u32[]{:S(2)}) collective-permute-start(bf16[272,256]{1,0:T(8,128)(2,1)S(1)} %fusion.1.refs_4_), channel_id=1, source_target_pairs={{0,16},{16,0},{1,17},{17,1},{2,18},{18,2},{3,19},{19,3},{4,20},{20... | collective-permute-start | bytes 417800 | tf_op jit(solution)/shard_map/ppermute | solution.py:394
  2.8 12.2 %collective-permute-start.5 = (bf16[272,256]{1,0:T(8,128)(2,1)S(1)}, bf16[272,256]{1,0:T(8,128)(2,1)S(1)}, u32[]{:S(2)}, u32[]{:S(2)}) collective-permute-start(bf16[272,256]{1,0:T(8,128)(2,1)S(1)} %fusion.1.refs_4_), channel_id=1, source_target_pairs={{0,12},{1,13},{2,14},{3,15},{4,8},{5,9},{6,10},{7,11},{8,4},{9,5},... | collective-permute-start | bytes 417800 | tf_op jit(solution)/shard_map/ppermute | solution.py:391
  7.6 1.2 %copy-start.1 = (bf16[2,64,4096]{2,1,0:T(8,128)(2,1)S(1)}, bf16[2,64,4096]{2,1,0:T(8,128)(2,1)}, u32[]{:S(2)}) copy-start(bf16[2,64,4096]{2,1,0:T(8,128)(2,1)} %x_ref.1) | copy-start | bytes 3145732
  8.8 1.2 %copy-start.2 = (bf16[2,64,4096]{2,1,0:T(8,128)(2,1)S(1)}, bf16[2,64,4096]{2,1,0:T(8,128)(2,1)}, u32[]{:S(2)}) copy-start(bf16[2,64,4096]{2,1,0:T(8,128)(2,1)} %c_ref.1) | copy-start | bytes 3145732
  11.1 10.5 %collective-permute-start = (bf16[2,64,1024]{2,1,0:T(8,128)(2,1)S(1)}, bf16[2,64,1024]{2,1,0:T(8,128)(2,1)S(1)}, u32[]{:S(2)}, u32[]{:S(2)}) collective-permute-start(bf16[2,64,1024]{2,1,0:T(8,128)(2,1)S(1)} %get-tuple-element.29), channel_id=1, source_target_pairs={{0,1},{1,0},{2,3},{3,2},{4,5},{5,4},{6,7},{7,6},{8,9},{9,8},{10,11... | collective-permute-start | bytes 786440 | tf_op jit(solution)/shard_map/ppermute | solution.py:398
  12.7 8.4 %collective-permute-start.4 = (bf16[272,256]{1,0:T(8,128)(2,1)S(1)}, bf16[272,256]{1,0:T(8,128)(2,1)S(1)}, u32[]{:S(2)}, u32[]{:S(2)}) collective-permute-start(bf16[272,256]{1,0:T(8,128)(2,1)S(1)} %fusion.1.refs_4_), channel_id=1, source_target_pairs={{0,8},{1,9},{2,10},{3,11},{4,12},{5,13},{6,14},{7,15},{8,0},{9,1},... | collective-permute-start | bytes 417800 | tf_op jit(solution)/shard_map/ppermute | solution.py:391
  12.7 8.4 %collective-permute-start.3 = (bf16[272,256]{1,0:T(8,128)(2,1)S(1)}, bf16[272,256]{1,0:T(8,128)(2,1)S(1)}, u32[]{:S(2)}, u32[]{:S(2)}) collective-permute-start(bf16[272,256]{1,0:T(8,128)(2,1)S(1)} %fusion.1.refs_4_), channel_id=1, source_target_pairs={{0,4},{1,5},{2,6},{3,7},{4,0},{5,1},{6,2},{7,3},{8,12},{9,13},{10,... | collective-permute-start | bytes 417800 | tf_op jit(solution)/shard_map/ppermute | solution.py:391
  13.5 13.2 %collective-permute-start.1 = (bf16[2,64,1024]{2,1,0:T(8,128)(2,1)S(1)}, bf16[2,64,1024]{2,1,0:T(8,128)(2,1)S(1)}, u32[]{:S(2)}, u32[]{:S(2)}) collective-permute-start(bf16[2,64,1024]{2,1,0:T(8,128)(2,1)S(1)} %get-tuple-element.30), channel_id=1, source_target_pairs={{0,2},{1,3},{2,0},{3,1},{4,6},{5,7},{6,4},{7,5},{8,10},{9,11},{10,... | collective-permute-start | bytes 786440 | tf_op jit(solution)/shard_map/ppermute | solution.py:398
  15.0 11.7 %copy-start.3 = (s32[2,1,2]{2,1,0:T(1,128)S(1)}, s32[2,1,2]{2,1,0:T(1,128)}, u32[]{:S(2)}) copy-start(s32[2,1,2]{2,1,0:T(1,128)} %docs.1) | copy-start | bytes 52
  15.0 11.7 %collective-permute-start.2 = (bf16[2,64,1024]{2,1,0:T(8,128)(2,1)S(1)}, bf16[2,64,1024]{2,1,0:T(8,128)(2,1)S(1)}, u32[]{:S(2)}, u32[]{:S(2)}) collective-permute-start(bf16[2,64,1024]{2,1,0:T(8,128)(2,1)S(1)} %get-tuple-element.31), channel_id=1, source_target_pairs={{0,3},{1,2},{2,1},{3,0},{4,7},{5,6},{6,5},{7,4},{8,11},{9,10},{10,... | collective-permute-start | bytes 786440 | tf_op jit(solution)/shard_map/ppermute | solution.py:398
  21.1 5.6 %collective-permute-start.9 = (bf16[272,256]{1,0:T(8,128)(2,1)S(1)}, bf16[272,256]{1,0:T(8,128)(2,1)S(1)}, u32[]{:S(2)}, u32[]{:S(2)}) collective-permute-start(bf16[272,256]{1,0:T(8,128)(2,1)S(1)} %collective-permute-done.5.refs_7_), channel_id=1, source_target_pairs={{0,16},{16,0},{1,17},{17,1},{2,18},{18,2},{3,19},{19,3},{4,20},{20... | collective-permute-start | bytes 417800 | tf_op jit(solution)/shard_map/ppermute | solution.py:394
  21.1 5.5 %collective-permute-start.8 = (bf16[272,256]{1,0:T(8,128)(2,1)S(1)}, bf16[272,256]{1,0:T(8,128)(2,1)S(1)}, u32[]{:S(2)}, u32[]{:S(2)}) collective-permute-start(bf16[272,256]{1,0:T(8,128)(2,1)S(1)} %collective-permute-done.4.refs_6_), channel_id=1, source_target_pairs={{0,16},{16,0},{1,17},{17,1},{2,18},{18,2},{3,19},{19,3},{4,20},{20... | collective-permute-start | bytes 417800 | tf_op jit(solution)/shard_map/ppermute | solution.py:394
  21.7 5.0 %collective-permute-start.7 = (bf16[272,256]{1,0:T(8,128)(2,1)S(1)}, bf16[272,256]{1,0:T(8,128)(2,1)S(1)}, u32[]{:S(2)}, u32[]{:S(2)}) collective-permute-start(bf16[272,256]{1,0:T(8,128)(2,1)S(1)} %collective-permute-done.3.refs_5_), channel_id=1, source_target_pairs={{0,16},{16,0},{1,17},{17,1},{2,18},{18,2},{3,19},{19,3},{4,20},{20... | collective-permute-start | bytes 417800 | tf_op jit(solution)/shard_map/ppermute | solution.py:394
  27.8 6.2 %collective-permute-start.12 = (bf16[208,256]{1,0:T(8,128)(2,1)S(1)}, bf16[208,256]{1,0:T(8,128)(2,1)S(1)}, u32[]{:S(2)}, u32[]{:S(2)}) collective-permute-start(bf16[208,256]{1,0:T(8,128)(2,1)S(1)} %get-tuple-element.32.refs_0_), channel_id=1, source_target_pairs={{0,3},{1,2},{2,1},{3,0},{4,7},{5,6},{6,5},{7,4},{8,11},{9,10},{10,... | collective-permute-start | bytes 319496 | tf_op jit(solution)/shard_map/ppermute | solution.py:398
  29.4 5.5 %collective-permute-start.11 = (bf16[208,256]{1,0:T(8,128)(2,1)S(1)}, bf16[208,256]{1,0:T(8,128)(2,1)S(1)}, u32[]{:S(2)}, u32[]{:S(2)}) collective-permute-start(bf16[208,256]{1,0:T(8,128)(2,1)S(1)} %get-tuple-element.32.refs_0_), channel_id=1, source_target_pairs={{0,2},{1,3},{2,0},{3,1},{4,6},{5,7},{6,4},{7,5},{8,10},{9,11},{10,... | collective-permute-start | bytes 319496 | tf_op jit(solution)/shard_map/ppermute | solution.py:398
  30.3 4.8 %collective-permute-start.10 = (bf16[208,256]{1,0:T(8,128)(2,1)S(1)}, bf16[208,256]{1,0:T(8,128)(2,1)S(1)}, u32[]{:S(2)}, u32[]{:S(2)}) collective-permute-start(bf16[208,256]{1,0:T(8,128)(2,1)S(1)} %get-tuple-element.32.refs_0_), channel_id=1, source_target_pairs={{0,1},{1,0},{2,3},{3,2},{4,5},{5,4},{6,7},{7,6},{8,9},{9,8},{10,11... | collective-permute-start | bytes 319496 | tf_op jit(solution)/shard_map/ppermute | solution.py:398
  36.3 6.4 %collective-permute-start.15 = (bf16[272,256]{1,0:T(8,128)(2,1)S(1)}, bf16[272,256]{1,0:T(8,128)(2,1)S(1)}, u32[]{:S(2)}, u32[]{:S(2)}) collective-permute-start(bf16[272,256]{1,0:T(8,128)(2,1)S(1)} %get-tuple-element.37.refs_0_), channel_id=1, source_target_pairs={{0,3},{1,2},{2,1},{3,0},{4,7},{5,6},{6,5},{7,4},{8,11},{9,10},{10,... | collective-permute-start | bytes 417800 | tf_op jit(solution)/shard_map/ppermute | solution.py:398
  38.4 5.8 %collective-permute-start.14 = (bf16[272,256]{1,0:T(8,128)(2,1)S(1)}, bf16[272,256]{1,0:T(8,128)(2,1)S(1)}, u32[]{:S(2)}, u32[]{:S(2)}) collective-permute-start(bf16[272,256]{1,0:T(8,128)(2,1)S(1)} %get-tuple-element.37.refs_0_), channel_id=1, source_target_pairs={{0,2},{1,3},{2,0},{3,1},{4,6},{5,7},{6,4},{7,5},{8,10},{9,11},{10,... | collective-permute-start | bytes 417800 | tf_op jit(solution)/shard_map/ppermute | solution.py:398
  39.0 5.2 %collective-permute-start.13 = (bf16[272,256]{1,0:T(8,128)(2,1)S(1)}, bf16[272,256]{1,0:T(8,128)(2,1)S(1)}, u32[]{:S(2)}, u32[]{:S(2)}) collective-permute-start(bf16[272,256]{1,0:T(8,128)(2,1)S(1)} %get-tuple-element.37.refs_0_), channel_id=1, source_target_pairs={{0,1},{1,0},{2,3},{3,2},{4,5},{5,4},{6,7},{7,6},{8,9},{9,8},{10,11... | collective-permute-start | bytes 417800 | tf_op jit(solution)/shard_map/ppermute | solution.py:398
  46.1 4.8 %collective-permute-start.18 = (bf16[64,256]{1,0:T(8,128)(2,1)S(1)}, bf16[64,256]{1,0:T(8,128)(2,1)S(1)}, u32[]{:S(2)}, u32[]{:S(2)}) collective-permute-start(bf16[64,256]{1,0:T(8,128)(2,1)S(1)} %get-tuple-element.41.refs_0_), channel_id=1, source_target_pairs={{0,3},{1,2},{2,1},{3,0},{4,7},{5,6},{6,5},{7,4},{8,11},{9,10},{10,... | collective-permute-start | bytes 98312 | tf_op jit(solution)/shard_map/ppermute | solution.py:398
  47.7 3.9 %collective-permute-start.17 = (bf16[64,256]{1,0:T(8,128)(2,1)S(1)}, bf16[64,256]{1,0:T(8,128)(2,1)S(1)}, u32[]{:S(2)}, u32[]{:S(2)}) collective-permute-start(bf16[64,256]{1,0:T(8,128)(2,1)S(1)} %get-tuple-element.41.refs_0_), channel_id=1, source_target_pairs={{0,2},{1,3},{2,0},{3,1},{4,6},{5,7},{6,4},{7,5},{8,10},{9,11},{10,... | collective-permute-start | bytes 98312 | tf_op jit(solution)/shard_map/ppermute | solution.py:398
  48.3 3.9 %collective-permute-start.16 = (bf16[64,256]{1,0:T(8,128)(2,1)S(1)}, bf16[64,256]{1,0:T(8,128)(2,1)S(1)}, u32[]{:S(2)}, u32[]{:S(2)}) collective-permute-start(bf16[64,256]{1,0:T(8,128)(2,1)S(1)} %get-tuple-element.41.refs_0_), channel_id=1, source_target_pairs={{0,1},{1,0},{2,3},{3,2},{4,5},{5,4},{6,7},{7,6},{8,9},{9,8},{10,11... | collective-permute-start | bytes 98312 | tf_op jit(solution)/shard_map/ppermute | solution.py:398
  53.6 2.0 %collective-permute-start.19 = (bf16[4,256,256]{2,1,0:T(8,128)(2,1)S(1)}, bf16[4,256,256]{2,1,0:T(8,128)(2,1)S(1)}, u32[]{:S(2)}, u32[]{:S(2)}) collective-permute-start(bf16[4,256,256]{2,1,0:T(8,128)(2,1)S(1)} %get-tuple-element.47), channel_id=1, source_target_pairs={{0,16},{16,0},{1,17},{17,1},{2,18},{18,2},{3,19},{19,3},{4,20},{20... | collective-permute-start | bytes 1572872 | tf_op jit(solution)/shard_map/ppermute | solution.py:394
  56.2 7.5 %collective-permute-start.20 = (bf16[256,256]{1,0:T(8,128)(2,1)S(1)}, bf16[256,256]{1,0:T(8,128)(2,1)S(1)}, u32[]{:S(2)}, u32[]{:S(2)}) collective-permute-start(bf16[256,256]{1,0:T(8,128)(2,1)S(1)} %get-tuple-element.49), channel_id=1, source_target_pairs={{0,4},{1,5},{2,6},{3,7},{4,0},{5,1},{6,2},{7,3},{8,12},{9,13},{10,... | collective-permute-start | bytes 393224 | tf_op jit(solution)/shard_map/ppermute | solution.py:391
  58.1 12.9 %collective-permute-start.21 = (bf16[256,256]{1,0:T(8,128)(2,1)S(1)}, bf16[256,256]{1,0:T(8,128)(2,1)S(1)}, u32[]{:S(2)}, u32[]{:S(2)}) collective-permute-start(bf16[256,256]{1,0:T(8,128)(2,1)S(1)} %get-tuple-element.50), channel_id=1, source_target_pairs={{0,8},{1,9},{2,10},{3,11},{4,12},{5,13},{6,14},{7,15},{8,0},{9,1},... | collective-permute-start | bytes 393224 | tf_op jit(solution)/shard_map/ppermute | solution.py:391
  60.7 10.3 %collective-permute-start.22 = (bf16[256,256]{1,0:T(8,128)(2,1)S(1)}, bf16[256,256]{1,0:T(8,128)(2,1)S(1)}, u32[]{:S(2)}, u32[]{:S(2)}) collective-permute-start(bf16[256,256]{1,0:T(8,128)(2,1)S(1)} %get-tuple-element.51), channel_id=1, source_target_pairs={{0,12},{1,13},{2,14},{3,15},{4,8},{5,9},{6,10},{7,11},{8,4},{9,5},... | collective-permute-start | bytes 393224 | tf_op jit(solution)/shard_map/ppermute | solution.py:391

commit v3 on v2

--- a/solution.py
+++ b/solution.py
@@ -125,11 +125,15 @@
     return lax.dot_general(a, b, (((1,), (1,)), ((), ())), preferred_element_type=F32)
 
 
-def blocks_kernel(planes, index, x_ref, c_ref, *refs):
+def blocks_kernel(planes, index, gain_ref, qkv_ref, wout_ref, x_ref, c_ref, pack_ref, *refs):
     out_refs, sems = refs[:PLANE], refs[PLANE]
+    qkv_rows, heads = qkv_ref.shape[0], wout_ref.shape[0]
     width = x_ref.shape[-1] // (planes * PLANE)
     section, p = index[0], index[2]
-    copies = []
+    copies = [
+        pltpu.make_async_copy(qkv_ref, pack_ref.at[:qkv_rows], sems.at[0]),
+        pltpu.make_async_copy(wout_ref, pack_ref.at[qkv_rows : qkv_rows + heads], sems.at[1]),
+    ]
     for k in range(PLANE):
         for z in range(planes):
             at = pl.multiple_of((z * PLANE + (p ^ k)) * width, width)
@@ -143,6 +147,7 @@
                 )
     for copy in copies:
         copy.start()
+    pack_ref[qkv_rows + heads :, :] = jnp.broadcast_to(gain_ref[...].astype(F32), (STATS, width)).astype(BF16)
     for copy in copies:
         copy.wait()
 
@@ -363,6 +368,12 @@
     out_ref[...] = total[qkv_rows:]
 
 
+def far_first(value, count, send):
+    of = lambda k: value[k] if isinstance(value, (list, tuple)) else value
+    got = {k: send(of(k), k) for k in reversed(range(1, count))}
+    return [of(0)] + [got[k] for k in range(1, count)]
+
+
 def call(kernel, outs, *args, scalars=0):
     smem = pl.BlockSpec(memory_space=pltpu.SMEM)
     vmem = pl.BlockSpec(memory_space=pltpu.VMEM)
@@ -398,23 +409,26 @@
         return lax.ppermute(value, "dp", route)
 
     def exchange(value):
-        return [value] + [along_plane(value, k) for k in range(1, PLANE)]
+        return far_first(value, PLANE, along_plane)
 
     gain = lax.dynamic_slice(norm_gain, (0, place * width), (1, width))
-    pack = jnp.concatenate(
-        [w_qkv[0].T, w_out[0], jnp.pad(gain, ((0, STATS - 1), (0, 0)))], axis=0
-    )
-    own = [pack] + [along_z(pack, k) for k in range(1, planes)]
-
-    blocks = pl.pallas_call(
+    smem, vmem = pl.BlockSpec(memory_space=pltpu.SMEM), pl.BlockSpec(memory_space=pltpu.VMEM)
+    hbm = pl.BlockSpec(memory_space=pltpu.HBM)
+    in_hbm = [
+        pltpu.with_memory_space_constraint(value, pltpu.HBM)
+        for value in (w_qkv[0].T, w_out[0], inputs, cotangent)
+    ]
+    pack, *blocks = pl.pallas_call(
         functools.partial(blocks_kernel, planes),
-        out_shape=[jax.ShapeDtypeStruct((2, block, cols), BF16)] * PLANE,
-        in_specs=[pl.BlockSpec(memory_space=pltpu.SMEM)] + [pl.BlockSpec(memory_space=pltpu.HBM)] * 2,
-        out_specs=[pl.BlockSpec(memory_space=pltpu.VMEM)] * PLANE,
-        scratch_shapes=[pltpu.SemaphoreType.DMA((2 * PLANE * planes,))],
+        out_shape=[jax.ShapeDtypeStruct((qkv_rows + heads + STATS, width), BF16)]
+        + [jax.ShapeDtypeStruct((2, block, cols), BF16)] * PLANE,
+        in_specs=[smem, vmem] + [hbm] * 4,
+        out_specs=[vmem] * (1 + PLANE),
+        scratch_shapes=[pltpu.SemaphoreType.DMA((2 + 2 * PLANE * planes,))],
         compiler_params=pltpu.CompilerParams(vmem_limit_bytes=VMEM_LIMIT),
-    )(index, inputs, cotangent)
-    blocks = [blocks[0]] + [along_plane(blocks[k], k) for k in range(1, PLANE)]
+    )(index, gain, *in_hbm)
+    own = far_first(pack, planes, along_z)
+    blocks = [blocks[0]] + far_first(blocks, PLANE, along_plane)[1:]
     other = [to_sibling(piece) for piece in own]
 
     weights = ((planes,) + pack.shape, BF16)
@@ -456,7 +470,7 @@
         [(grads[1:], F32)] + [(grads[1:], BF16)] * (planes - 1),
         index, keep, to_sibling(send), scalars=1,
     )
-    parts = [along_z(merged[k], k) for k in range(1, planes)]
+    parts = far_first(merged, planes, along_z)[1:]
     grad_qkv, grad_out = call(
         functools.partial(last_kernel, qkv_rows),
         [((qkv_rows, width), F32), ((heads, width), F32)],

time: 72 us -> 71.6 us (level)
  starting transfers between devices: 25.1 us -> 27.9 us
  local copies, waits for them, and re-layouts: 3.17 us -> 0.7 us
  Pallas kernels: 8.1 us -> 9.03 us
  other arithmetic: 1 us -> 0.08 us
    unnamed x8 -> x4, local copies, waits for them, and re-layouts: 3.16 us -> 0.7 us
    ppermute x12, starting transfers between devices: 14 us -> 16.2 us  [along_plane(): return lax.ppermute(value, 'dp', route)]
    ppermute x12, waiting for transfers between devices: 15.6 us -> 14.6 us  [along_plane(): return lax.ppermute(value, 'dp', route)]
    pallas_call x1, Pallas kernels: 1.12 us -> 2.05 us  [planar(): pl.pallas_call(functools.partial(blocks_kernel, planes), out_shape=[jax.S...]
    concatenate x1 -> x0, other arithmetic: 0.92 us -> none  [planar(): jnp.concatenate([w_qkv[0].T, w_out[0], jnp.pad(gain, ((0, STATS - 1), (0,...]
  transfers between devices with their start and end apart: 23 -> 23, of which waited for: 13 -> 15; matrix products, arithmetic and copies ran while one was open for 0% -> 0% of each run, Pallas kernels for 2% -> 0%
where the time goes in v3:
time: 71.6 us; the launch traced here: 71.3 us
  waiting for transfers between devices  32.9 us (46%)
  starting transfers between devices  27.9 us (39%)
  Pallas kernels  9.03 us (13%)
  between operations  0.74 us (1%)
    ppermute x6, waiting for transfers between devices, along_z(): return lax.ppermute(value, 'dp', route)  16.4 us
    ppermute x12, starting transfers between devices, along_plane(): return lax.ppermute(value, 'dp', route)  16.2 us
    ppermute x12, waiting for transfers between devices, along_plane(): return lax.ppermute(value, 'dp', route)  14.6 us
    ppermute x6, starting transfers between devices, along_z(): return lax.ppermute(value, 'dp', route)  10.5 us
    pallas_call x6, Pallas kernels, call(): pl.pallas_call(kernel, out_shape=[jax.ShapeDtypeStruct(shape, dtype) for...  6.98 us
    pallas_call x1, Pallas kernels, planar(): pl.pallas_call(functools.partial(blocks_kernel, planes), out_shape=[jax.S...  2.05 us
    ppermute x5, waiting for transfers between devices, to_sibling(): return lax.ppermute(value, 'section', [(0, 1), (1, 0)])  1.91 us
  transfers between devices with their start and end apart: 23, of which 15 were waited for; matrix products, arithmetic and copies ran while one was open for 0% of the time, Pallas kernels for 0%

profile of v3, /device:TPU:0, one launch (start us, length us, event | category | flops | bytes accessed | tf_op | source)
XLA Modules:
  0.0 71.3 jit_solution(12178233482038389391)
XLA Ops:
  0.6 0.0 copy-start
  0.7 0.7 copy-done
  1.4 0.1 pad_add_fusion.index
  1.4 2.0 %shard_map.77 = (bf16[272,256]{1,0:T(8,128)(2,1)S(1)}, bf16[2,64,1024]{2,1,0:T(8,128)(2,1)S(1)}, bf16[2,64,1024]{2,1,0:T(8,128)(2,1)S(1)}, bf16[2,64,1024]{2,1,0:T(8,128)(2,1)S(1)}, bf16[2,64,1024]{2,1,0:T(8,128)(2,1)S(1)}) custom-call(s32[3]{0:T(128)S(1)} %pad_add_fusion.index, bf16[1,256]{1,0:T(2,128)(2,1)S(1)} %constant_dynamic-slice_fusion.gain_ref, ...), custom_call_target="tpu_custom_call" | custom-call | tf_op jit(solution)/shard_map/pallas_call | solution.py:421
  3.5 0.5 collective-permute-start.6
  4.0 4.7 %collective-permute-start.5 = (bf16[272,256]{1,0:T(8,128)(2,1)S(1)}, bf16[272,256]{1,0:T(8,128)(2,1)S(1)}, u32[]{:S(2)}, u32[]{:S(2)}) collective-permute-start(bf16[272,256]{1,0:T(8,128)(2,1)S(1)} %get-tuple-element.33.refs_4_), channel_id=1, source_target_pairs={{0,12},{1,13},{2,14},{3,15},{4,8},{5,9},{6,10},{7,11},{8,4},{9,5},... | collective-permute-start | bytes 417800 | tf_op jit(solution)/shard_map/ppermute | solution.py:402
  8.7 1.5 %collective-permute-start = (bf16[2,64,1024]{2,1,0:T(8,128)(2,1)S(1)}, bf16[2,64,1024]{2,1,0:T(8,128)(2,1)S(1)}, u32[]{:S(2)}, u32[]{:S(2)}) collective-permute-start(bf16[2,64,1024]{2,1,0:T(8,128)(2,1)S(1)} %get-tuple-element.30), channel_id=1, source_target_pairs={{0,1},{1,0},{2,3},{3,2},{4,5},{5,4},{6,7},{7,6},{8,9},{9,8},{10,11... | collective-permute-start | bytes 786440 | tf_op jit(solution)/shard_map/ppermute | solution.py:409
  10.2 0.0 collective-permute-start.4
  10.2 0.8 %collective-permute-start.3 = (bf16[272,256]{1,0:T(8,128)(2,1)S(1)}, bf16[272,256]{1,0:T(8,128)(2,1)S(1)}, u32[]{:S(2)}, u32[]{:S(2)}) collective-permute-start(bf16[272,256]{1,0:T(8,128)(2,1)S(1)} %get-tuple-element.33.refs_4_), channel_id=1, source_target_pairs={{0,4},{1,5},{2,6},{3,7},{4,0},{5,1},{6,2},{7,3},{8,12},{9,13},{10,... | collective-permute-start | bytes 417800 | tf_op jit(solution)/shard_map/ppermute | solution.py:402
  11.0 0.0 collective-permute-done.6.refs_8_
  11.0 1.5 %collective-permute-start.1 = (bf16[2,64,1024]{2,1,0:T(8,128)(2,1)S(1)}, bf16[2,64,1024]{2,1,0:T(8,128)(2,1)S(1)}, u32[]{:S(2)}, u32[]{:S(2)}) collective-permute-start(bf16[2,64,1024]{2,1,0:T(8,128)(2,1)S(1)} %get-tuple-element.31), channel_id=1, source_target_pairs={{0,2},{1,3},{2,0},{3,1},{4,6},{5,7},{6,4},{7,5},{8,10},{9,11},{10,... | collective-permute-start | bytes 786440 | tf_op jit(solution)/shard_map/ppermute | solution.py:409
  12.5 0.8 %collective-permute-done.5.refs_7_ = bf16[272,256]{1,0:T(8,128)(2,1)S(1)} collective-permute-done((bf16[272,256]{1,0:T(8,128)(2,1)S(1)}, bf16[272,256]{1,0:T(8,128)(2,1)S(1)}, u32[]{:S(2)}, u32[]{:S(2)}) %collective-permute-start.5) | collective-permute-done | bytes 139296 | tf_op jit(solution)/shard_map/ppermute | solution.py:402
  13.3 0.0 copy-start.1
  13.3 2.6 %collective-permute-start.2 = (bf16[2,64,1024]{2,1,0:T(8,128)(2,1)S(1)}, bf16[2,64,1024]{2,1,0:T(8,128)(2,1)S(1)}, u32[]{:S(2)}, u32[]{:S(2)}) collective-permute-start(bf16[2,64,1024]{2,1,0:T(8,128)(2,1)S(1)} %get-tuple-element.32), channel_id=1, source_target_pairs={{0,3},{1,2},{2,1},{3,0},{4,7},{5,6},{6,5},{7,4},{8,11},{9,10},{10,... | collective-permute-start | bytes 786440 | tf_op jit(solution)/shard_map/ppermute | solution.py:409
  15.9 5.2 %collective-permute-done.4.refs_6_ = bf16[272,256]{1,0:T(8,128)(2,1)S(1)} collective-permute-done((bf16[272,256]{1,0:T(8,128)(2,1)S(1)}, bf16[272,256]{1,0:T(8,128)(2,1)S(1)}, u32[]{:S(2)}, u32[]{:S(2)}) %collective-permute-start.4) | collective-permute-done | bytes 139296 | tf_op jit(solution)/shard_map/ppermute | solution.py:402
  21.1 0.0 collective-permute-start.9
  21.1 0.0 collective-permute-done.3.refs_5_
  21.1 0.5 collective-permute-start.8
  21.6 0.0 collective-permute-done.refs_1_
  21.6 0.1 collective-permute-start.7
  21.7 2.5 %collective-permute-done.1.refs_2_ = bf16[2,64,1024]{2,1,0:T(8,128)(2,1)S(1)} collective-permute-done((bf16[2,64,1024]{2,1,0:T(8,128)(2,1)S(1)}, bf16[2,64,1024]{2,1,0:T(8,128)(2,1)S(1)}, u32[]{:S(2)}, u32[]{:S(2)}) %collective-permute-start.1) | collective-permute-done | bytes 262176 | tf_op jit(solution)/shard_map/ppermute | solution.py:409
  24.2 0.0 collective-permute-done.2.refs_3_
  24.2 0.0 collective-permute-done.9.refs_11_
  24.2 0.0 collective-permute-done.8.refs_10_
  24.2 0.0 collective-permute-done.7.refs_9_
  24.2 0.0 copy-done.1
  24.2 1.1 %shard_map.78 = (bf16[4,64,1024]{2,1,0:T(8,128)(2,1)S(1)}, bf16[4,64,1024]{2,1,0:T(8,128)(2,1)S(1)}, bf16[4,272,256]{2,1,0:T(8,128)(2,1)S(1)}, bf16[4,272,256]{2,1,0:T(8,128)(2,1)S(1)}, bf16[208,256]{1,0:T(8,128)(2,1)S(1)}) custom-call(s32[3]{0:T(128)S(1)} %pad_add_fusion.index, s32[2,1,2]{2,1,0:T(1,128)S(1)} %copy-done.1, ...), custom_call_target="tpu_custom_call" | custom-call | tf_op jit(solution)/shard_map/pallas_call | solution.py:380
  25.3 1.6 %collective-permute-start.12 = (bf16[208,256]{1,0:T(8,128)(2,1)S(1)}, bf16[208,256]{1,0:T(8,128)(2,1)S(1)}, u32[]{:S(2)}, u32[]{:S(2)}) collective-permute-start(bf16[208,256]{1,0:T(8,128)(2,1)S(1)} %get-tuple-element.34.refs_0_), channel_id=1, source_target_pairs={{0,3},{1,2},{2,1},{3,0},{4,7},{5,6},{6,5},{7,4},{8,11},{9,10},{10,... | collective-permute-start | bytes 319496 | tf_op jit(solution)/shard_map/ppermute | solution.py:409
  26.9 0.9 %collective-permute-start.11 = (bf16[208,256]{1,0:T(8,128)(2,1)S(1)}, bf16[208,256]{1,0:T(8,128)(2,1)S(1)}, u32[]{:S(2)}, u32[]{:S(2)}) collective-permute-start(bf16[208,256]{1,0:T(8,128)(2,1)S(1)} %get-tuple-element.34.refs_0_), channel_id=1, source_target_pairs={{0,2},{1,3},{2,0},{3,1},{4,6},{5,7},{6,4},{7,5},{8,10},{9,11},{10,... | collective-permute-start | bytes 319496 | tf_op jit(solution)/shard_map/ppermute | solution.py:409
  27.8 1.1 %collective-permute-start.10 = (bf16[208,256]{1,0:T(8,128)(2,1)S(1)}, bf16[208,256]{1,0:T(8,128)(2,1)S(1)}, u32[]{:S(2)}, u32[]{:S(2)}) collective-permute-start(bf16[208,256]{1,0:T(8,128)(2,1)S(1)} %get-tuple-element.34.refs_0_), channel_id=1, source_target_pairs={{0,1},{1,0},{2,3},{3,2},{4,5},{5,4},{6,7},{7,6},{8,9},{9,8},{10,11... | collective-permute-start | bytes 319496 | tf_op jit(solution)/shard_map/ppermute | solution.py:409
  28.9 2.9 %collective-permute-done.12.refs_3_ = bf16[208,256]{1,0:T(8,128)(2,1)S(1)} collective-permute-done((bf16[208,256]{1,0:T(8,128)(2,1)S(1)}, bf16[208,256]{1,0:T(8,128)(2,1)S(1)}, u32[]{:S(2)}, u32[]{:S(2)}) %collective-permute-start.12) | collective-permute-done | bytes 106528 | tf_op jit(solution)/shard_map/ppermute | solution.py:409
  31.8 0.7 %collective-permute-done.11.refs_2_ = bf16[208,256]{1,0:T(8,128)(2,1)S(1)} collective-permute-done((bf16[208,256]{1,0:T(8,128)(2,1)S(1)}, bf16[208,256]{1,0:T(8,128)(2,1)S(1)}, u32[]{:S(2)}, u32[]{:S(2)}) %collective-permute-start.11) | collective-permute-done | bytes 106528 | tf_op jit(solution)/shard_map/ppermute | solution.py:409
  32.5 0.2 collective-permute-done.10.refs_1_
  32.7 1.2 %shard_map.79 = (bf16[272,256]{1,0:T(8,128)(2,1)S(1)}, bf16[256,1024]{1,0:T(8,128)(2,1)S(1)}, f32[192,256]{1,0:T(8,128)S(1)}, f32[256,256]{1,0:T(8,128)S(1)}, bf...) custom-call(bf16[208,256]{1,0:T(8,128)(2,1)S(1)} %get-tuple-element.34.refs_0_, ...), custom_call_target="tpu_custom_call" | custom-call | tf_op jit(solution)/shard_map/pallas_call | solution.py:380
  34.0 1.9 %collective-permute-start.15 = (bf16[272,256]{1,0:T(8,128)(2,1)S(1)}, bf16[272,256]{1,0:T(8,128)(2,1)S(1)}, u32[]{:S(2)}, u32[]{:S(2)}) collective-permute-start(bf16[272,256]{1,0:T(8,128)(2,1)S(1)} %get-tuple-element.39.refs_0_), channel_id=1, source_target_pairs={{0,3},{1,2},{2,1},{3,0},{4,7},{5,6},{6,5},{7,4},{8,11},{9,10},{10,... | collective-permute-start | bytes 417800 | tf_op jit(solution)/shard_map/ppermute | solution.py:409
  35.8 0.9 %collective-permute-start.14 = (bf16[272,256]{1,0:T(8,128)(2,1)S(1)}, bf16[272,256]{1,0:T(8,128)(2,1)S(1)}, u32[]{:S(2)}, u32[]{:S(2)}) collective-permute-start(bf16[272,256]{1,0:T(8,128)(2,1)S(1)} %get-tuple-element.39.refs_0_), channel_id=1, source_target_pairs={{0,2},{1,3},{2,0},{3,1},{4,6},{5,7},{6,4},{7,5},{8,10},{9,11},{10,... | collective-permute-start | bytes 417800 | tf_op jit(solution)/shard_map/ppermute | solution.py:409
  36.7 0.8 %collective-permute-start.13 = (bf16[272,256]{1,0:T(8,128)(2,1)S(1)}, bf16[272,256]{1,0:T(8,128)(2,1)S(1)}, u32[]{:S(2)}, u32[]{:S(2)}) collective-permute-start(bf16[272,256]{1,0:T(8,128)(2,1)S(1)} %get-tuple-element.39.refs_0_), channel_id=1, source_target_pairs={{0,1},{1,0},{2,3},{3,2},{4,5},{5,4},{6,7},{7,6},{8,9},{9,8},{10,11... | collective-permute-start | bytes 417800 | tf_op jit(solution)/shard_map/ppermute | solution.py:409
  37.5 3.5 %collective-permute-done.15.refs_3_ = bf16[272,256]{1,0:T(8,128)(2,1)S(1)} collective-permute-done((bf16[272,256]{1,0:T(8,128)(2,1)S(1)}, bf16[272,256]{1,0:T(8,128)(2,1)S(1)}, u32[]{:S(2)}, u32[]{:S(2)}) %collective-permute-start.15) | collective-permute-done | bytes 139296 | tf_op jit(solution)/shard_map/ppermute | solution.py:409
  41.0 1.2 %collective-permute-done.14.refs_2_ = bf16[272,256]{1,0:T(8,128)(2,1)S(1)} collective-permute-done((bf16[272,256]{1,0:T(8,128)(2,1)S(1)}, bf16[272,256]{1,0:T(8,128)(2,1)S(1)}, u32[]{:S(2)}, u32[]{:S(2)}) %collective-permute-start.14) | collective-permute-done | bytes 139296 | tf_op jit(solution)/shard_map/ppermute | solution.py:409
  42.2 0.1 collective-permute-done.13.refs_1_
  42.3 1.9 %shard_map.80 = (bf16[64,256]{1,0:T(8,128)(2,1)S(1)}, f32[4,64,256]{2,1,0:T(8,128)S(1)}, f32[4,256,256]{2,1,0:T(8,128)S(1)}) custom-call(bf16[272,256]{1,0:T(8,128)(2,1)S(1)} %get-tuple-element.39.refs_0_, bf16[272,256]{1,0:T(8,128)(2,1)S(1)} %collective-permute-done.13.refs_1_, bf16[272,256]{1,0:T(8,128)(2,1)S(1)} %collective-permute-done.14.refs_2_, ...), custom_call_target="tpu_custom_call" | custom-call | tf_op jit(solution)/shard_map/pallas_call | solution.py:380
  44.2 1.6 %collective-permute-start.18 = (bf16[64,256]{1,0:T(8,128)(2,1)S(1)}, bf16[64,256]{1,0:T(8,128)(2,1)S(1)}, u32[]{:S(2)}, u32[]{:S(2)}) collective-permute-start(bf16[64,256]{1,0:T(8,128)(2,1)S(1)} %get-tuple-element.43.refs_0_), channel_id=1, source_target_pairs={{0,3},{1,2},{2,1},{3,0},{4,7},{5,6},{6,5},{7,4},{8,11},{9,10},{10,... | collective-permute-start | bytes 98312 | tf_op jit(solution)/shard_map/ppermute | solution.py:409
  45.9 1.3 %collective-permute-start.17 = (bf16[64,256]{1,0:T(8,128)(2,1)S(1)}, bf16[64,256]{1,0:T(8,128)(2,1)S(1)}, u32[]{:S(2)}, u32[]{:S(2)}) collective-permute-start(bf16[64,256]{1,0:T(8,128)(2,1)S(1)} %get-tuple-element.43.refs_0_), channel_id=1, source_target_pairs={{0,2},{1,3},{2,0},{3,1},{4,6},{5,7},{6,4},{7,5},{8,10},{9,11},{10,... | collective-permute-start | bytes 98312 | tf_op jit(solution)/shard_map/ppermute | solution.py:409
  47.2 0.5 collective-permute-start.16
  47.7 1.4 %collective-permute-done.18.refs_3_ = bf16[64,256]{1,0:T(8,128)(2,1)S(1)} collective-permute-done((bf16[64,256]{1,0:T(8,128)(2,1)S(1)}, bf16[64,256]{1,0:T(8,128)(2,1)S(1)}, u32[]{:S(2)}, u32[]{:S(2)}) %collective-permute-start.18) | collective-permute-done | bytes 32800 | tf_op jit(solution)/shard_map/ppermute | solution.py:409
  49.2 0.6 collective-permute-done.17.refs_2_
  49.8 1.3 %collective-permute-done.16.refs_1_ = bf16[64,256]{1,0:T(8,128)(2,1)S(1)} collective-permute-done((bf16[64,256]{1,0:T(8,128)(2,1)S(1)}, bf16[64,256]{1,0:T(8,128)(2,1)S(1)}, u32[]{:S(2)}, u32[]{:S(2)}) %collective-permute-start.16) | collective-permute-done | bytes 32800 | tf_op jit(solution)/shard_map/ppermute | solution.py:409
  51.1 1.3 %shard_map.81 = (f32[4,256,256]{2,1,0:T(8,128)S(1)}, bf16[4,256,256]{2,1,0:T(8,128)(2,1)S(1)}) custom-call(s32[3]{0:T(128)S(1)} %pad_add_fusion.index, bf16[64,256]{1,0:T(8,128)(2,1)S(1)} %get-tuple-element.43.refs_0_, bf16[64,256]{1,0:T(8,128)(2,1)S(1)} %collective-permute-done.16.refs_1_, bf16[64,256]{1,0:T(8,128)(2,1)S(1)} %collective-permute-done.17.refs_2_, ...), custom_call_target="tpu_custom_call" | custom-call | tf_op jit(solution)/shard_map/pallas_call | solution.py:380
  52.4 0.1 collective-permute-start.19
  52.5 1.9 %collective-permute-done.19.come_ref = bf16[4,256,256]{2,1,0:T(8,128)(2,1)S(1)} collective-permute-done((bf16[4,256,256]{2,1,0:T(8,128)(2,1)S(1)}, bf16[4,256,256]{2,1,0:T(8,128)(2,1)S(1)}, u32[]{:S(2)}, u32[]{:S(2)}) %collective-permute-start.19) | collective-permute-done | bytes 524320 | tf_op jit(solution)/shard_map/ppermute | solution.py:405
  54.4 0.7 shard_map.82
  55.1 2.6 %collective-permute-start.20 = (bf16[256,256]{1,0:T(8,128)(2,1)S(1)}, bf16[256,256]{1,0:T(8,128)(2,1)S(1)}, u32[]{:S(2)}, u32[]{:S(2)}) collective-permute-start(bf16[256,256]{1,0:T(8,128)(2,1)S(1)} %get-tuple-element.51), channel_id=1, source_target_pairs={{0,4},{1,5},{2,6},{3,7},{4,0},{5,1},{6,2},{7,3},{8,12},{9,13},{10,... | collective-permute-start | bytes 393224 | tf_op jit(solution)/shard_map/ppermute | solution.py:402
  57.7 1.1 %collective-permute-start.21 = (bf16[256,256]{1,0:T(8,128)(2,1)S(1)}, bf16[256,256]{1,0:T(8,128)(2,1)S(1)}, u32[]{:S(2)}, u32[]{:S(2)}) collective-permute-start(bf16[256,256]{1,0:T(8,128)(2,1)S(1)} %get-tuple-element.52), channel_id=1, source_target_pairs={{0,8},{1,9},{2,10},{3,11},{4,12},{5,13},{6,14},{7,15},{8,0},{9,1},... | collective-permute-start | bytes 393224 | tf_op jit(solution)/shard_map/ppermute | solution.py:402
  58.8 1.4 %collective-permute-start.22 = (bf16[256,256]{1,0:T(8,128)(2,1)S(1)}, bf16[256,256]{1,0:T(8,128)(2,1)S(1)}, u32[]{:S(2)}, u32[]{:S(2)}) collective-permute-start(bf16[256,256]{1,0:T(8,128)(2,1)S(1)} %get-tuple-element.53), channel_id=1, source_target_pairs={{0,12},{1,13},{2,14},{3,15},{4,8},{5,9},{6,10},{7,11},{8,4},{9,5},... | collective-permute-start | bytes 393224 | tf_op jit(solution)/shard_map/ppermute | solution.py:402
  60.2 3.2 %collective-permute-done.20.refs_0_ = bf16[256,256]{1,0:T(8,128)(2,1)S(1)} collective-permute-done((bf16[256,256]{1,0:T(8,128)(2,1)S(1)}, bf16[256,256]{1,0:T(8,128)(2,1)S(1)}, u32[]{:S(2)}, u32[]{:S(2)}) %collective-permute-start.20) | collective-permute-done | bytes 131104 | tf_op jit(solution)/shard_map/ppermute | solution.py:402
  63.4 7.2 %collective-permute-done.21.refs_1_ = bf16[256,256]{1,0:T(8,128)(2,1)S(1)} collective-permute-done((bf16[256,256]{1,0:T(8,128)(2,1)S(1)}, bf16[256,256]{1,0:T(8,128)(2,1)S(1)}, u32[]{:S(2)}, u32[]{:S(2)}) %collective-permute-start.21) | collective-permute-done | bytes 131104 | tf_op jit(solution)/shard_map/ppermute | solution.py:402
  70.6 0.0 collective-permute-done.22.refs_2_
  70.6 0.7 %shard_map.83 = (f32[192,256]{1,0:T(8,128)}, f32[64,256]{1,0:T(8,128)}) custom-call(f32[256,256]{1,0:T(8,128)S(1)} %get-tuple-element.50.keep_ref, bf16[256,256]{1,0:T(8,128)(2,1)S(1)} %collective-permute-done.20.refs_0_, bf16[256,256]{1,0:T(8,128)(2,1)S(1)} %collective-permute-done.21.refs_1_, bf16[256,256]{1,0:T(8,128)(2,1)S(1)} %collective-permute-done.22.refs_2_), custom_call_target="tpu_custom_call" | custom-call | tf_op jit(solution)/shard_map/pallas_call | solution.py:380
  (1 shorter events, 0.0 us)
Async XLA Ops:
  0.6 0.7 %copy-start = (bf16[1,4096]{1,0:T(2,128)(2,1)S(1)}, bf16[1,4096]{1,0:T(2,128)(2,1)}, u32[]{:S(2)}) copy-start(bf16[1,4096]{1,0:T(2,128)(2,1)} %param.9) | copy-start | bytes 24580
  3.5 7.5 %collective-permute-start.6 = (bf16[272,256]{1,0:T(8,128)(2,1)S(1)}, bf16[272,256]{1,0:T(8,128)(2,1)S(1)}, u32[]{:S(2)}, u32[]{:S(2)}) collective-permute-start(bf16[272,256]{1,0:T(8,128)(2,1)S(1)} %get-tuple-element.33.refs_4_), channel_id=1, source_target_pairs={{0,16},{16,0},{1,17},{17,1},{2,18},{18,2},{3,19},{19,3},{4,20},{20... | collective-permute-start | bytes 417800 | tf_op jit(solution)/shard_map/ppermute | solution.py:405
  4.0 9.3 %collective-permute-start.5 = (bf16[272,256]{1,0:T(8,128)(2,1)S(1)}, bf16[272,256]{1,0:T(8,128)(2,1)S(1)}, u32[]{:S(2)}, u32[]{:S(2)}) collective-permute-start(bf16[272,256]{1,0:T(8,128)(2,1)S(1)} %get-tuple-element.33.refs_4_), channel_id=1, source_target_pairs={{0,12},{1,13},{2,14},{3,15},{4,8},{5,9},{6,10},{7,11},{8,4},{9,5},... | collective-permute-start | bytes 417800 | tf_op jit(solution)/shard_map/ppermute | solution.py:402
  8.7 12.9 %collective-permute-start = (bf16[2,64,1024]{2,1,0:T(8,128)(2,1)S(1)}, bf16[2,64,1024]{2,1,0:T(8,128)(2,1)S(1)}, u32[]{:S(2)}, u32[]{:S(2)}) collective-permute-start(bf16[2,64,1024]{2,1,0:T(8,128)(2,1)S(1)} %get-tuple-element.30), channel_id=1, source_target_pairs={{0,1},{1,0},{2,3},{3,2},{4,5},{5,4},{6,7},{7,6},{8,9},{9,8},{10,11... | collective-permute-start | bytes 786440 | tf_op jit(solution)/shard_map/ppermute | solution.py:409
  10.2 10.9 %collective-permute-start.4 = (bf16[272,256]{1,0:T(8,128)(2,1)S(1)}, bf16[272,256]{1,0:T(8,128)(2,1)S(1)}, u32[]{:S(2)}, u32[]{:S(2)}) collective-permute-start(bf16[272,256]{1,0:T(8,128)(2,1)S(1)} %get-tuple-element.33.refs_4_), channel_id=1, source_target_pairs={{0,8},{1,9},{2,10},{3,11},{4,12},{5,13},{6,14},{7,15},{8,0},{9,1},... | collective-permute-start | bytes 417800 | tf_op jit(solution)/shard_map/ppermute | solution.py:402
  10.2 10.9 %collective-permute-start.3 = (bf16[272,256]{1,0:T(8,128)(2,1)S(1)}, bf16[272,256]{1,0:T(8,128)(2,1)S(1)}, u32[]{:S(2)}, u32[]{:S(2)}) collective-permute-start(bf16[272,256]{1,0:T(8,128)(2,1)S(1)} %get-tuple-element.33.refs_4_), channel_id=1, source_target_pairs={{0,4},{1,5},{2,6},{3,7},{4,0},{5,1},{6,2},{7,3},{8,12},{9,13},{10,... | collective-permute-start | bytes 417800 | tf_op jit(solution)/shard_map/ppermute | solution.py:402
  11.0 13.2 %collective-permute-start.1 = (bf16[2,64,1024]{2,1,0:T(8,128)(2,1)S(1)}, bf16[2,64,1024]{2,1,0:T(8,128)(2,1)S(1)}, u32[]{:S(2)}, u32[]{:S(2)}) collective-permute-start(bf16[2,64,1024]{2,1,0:T(8,128)(2,1)S(1)} %get-tuple-element.31), channel_id=1, source_target_pairs={{0,2},{1,3},{2,0},{3,1},{4,6},{5,7},{6,4},{7,5},{8,10},{9,11},{10,... | collective-permute-start | bytes 786440 | tf_op jit(solution)/shard_map/ppermute | solution.py:409
  13.3 10.9 %copy-start.1 = (s32[2,1,2]{2,1,0:T(1,128)S(1)}, s32[2,1,2]{2,1,0:T(1,128)}, u32[]{:S(2)}) copy-start(s32[2,1,2]{2,1,0:T(1,128)} %docs.1) | copy-start | bytes 52
  13.3 10.9 %collective-permute-start.2 = (bf16[2,64,1024]{2,1,0:T(8,128)(2,1)S(1)}, bf16[2,64,1024]{2,1,0:T(8,128)(2,1)S(1)}, u32[]{:S(2)}, u32[]{:S(2)}) collective-permute-start(bf16[2,64,1024]{2,1,0:T(8,128)(2,1)S(1)} %get-tuple-element.32), channel_id=1, source_target_pairs={{0,3},{1,2},{2,1},{3,0},{4,7},{5,6},{6,5},{7,4},{8,11},{9,10},{10,... | collective-permute-start | bytes 786440 | tf_op jit(solution)/shard_map/ppermute | solution.py:409
  21.1 3.1 %collective-permute-start.9 = (bf16[272,256]{1,0:T(8,128)(2,1)S(1)}, bf16[272,256]{1,0:T(8,128)(2,1)S(1)}, u32[]{:S(2)}, u32[]{:S(2)}) collective-permute-start(bf16[272,256]{1,0:T(8,128)(2,1)S(1)} %collective-permute-done.5.refs_7_), channel_id=1, source_target_pairs={{0,16},{16,0},{1,17},{17,1},{2,18},{18,2},{3,19},{19,3},{4,20},{20... | collective-permute-start | bytes 417800 | tf_op jit(solution)/shard_map/ppermute | solution.py:405
  21.1 3.1 %collective-permute-start.8 = (bf16[272,256]{1,0:T(8,128)(2,1)S(1)}, bf16[272,256]{1,0:T(8,128)(2,1)S(1)}, u32[]{:S(2)}, u32[]{:S(2)}) collective-permute-start(bf16[272,256]{1,0:T(8,128)(2,1)S(1)} %collective-permute-done.4.refs_6_), channel_id=1, source_target_pairs={{0,16},{16,0},{1,17},{17,1},{2,18},{18,2},{3,19},{19,3},{4,20},{20... | collective-permute-start | bytes 417800 | tf_op jit(solution)/shard_map/ppermute | solution.py:405
  21.6 2.6 %collective-permute-start.7 = (bf16[272,256]{1,0:T(8,128)(2,1)S(1)}, bf16[272,256]{1,0:T(8,128)(2,1)S(1)}, u32[]{:S(2)}, u32[]{:S(2)}) collective-permute-start(bf16[272,256]{1,0:T(8,128)(2,1)S(1)} %collective-permute-done.3.refs_5_), channel_id=1, source_target_pairs={{0,16},{16,0},{1,17},{17,1},{2,18},{18,2},{3,19},{19,3},{4,20},{20... | collective-permute-start | bytes 417800 | tf_op jit(solution)/shard_map/ppermute | solution.py:405
  25.3 6.5 %collective-permute-start.12 = (bf16[208,256]{1,0:T(8,128)(2,1)S(1)}, bf16[208,256]{1,0:T(8,128)(2,1)S(1)}, u32[]{:S(2)}, u32[]{:S(2)}) collective-permute-start(bf16[208,256]{1,0:T(8,128)(2,1)S(1)} %get-tuple-element.34.refs_0_), channel_id=1, source_target_pairs={{0,3},{1,2},{2,1},{3,0},{4,7},{5,6},{6,5},{7,4},{8,11},{9,10},{10,... | collective-permute-start | bytes 319496 | tf_op jit(solution)/shard_map/ppermute | solution.py:409
  26.9 5.6 %collective-permute-start.11 = (bf16[208,256]{1,0:T(8,128)(2,1)S(1)}, bf16[208,256]{1,0:T(8,128)(2,1)S(1)}, u32[]{:S(2)}, u32[]{:S(2)}) collective-permute-start(bf16[208,256]{1,0:T(8,128)(2,1)S(1)} %get-tuple-element.34.refs_0_), channel_id=1, source_target_pairs={{0,2},{1,3},{2,0},{3,1},{4,6},{5,7},{6,4},{7,5},{8,10},{9,11},{10,... | collective-permute-start | bytes 319496 | tf_op jit(solution)/shard_map/ppermute | solution.py:409
  27.8 4.9 %collective-permute-start.10 = (bf16[208,256]{1,0:T(8,128)(2,1)S(1)}, bf16[208,256]{1,0:T(8,128)(2,1)S(1)}, u32[]{:S(2)}, u32[]{:S(2)}) collective-permute-start(bf16[208,256]{1,0:T(8,128)(2,1)S(1)} %get-tuple-element.34.refs_0_), channel_id=1, source_target_pairs={{0,1},{1,0},{2,3},{3,2},{4,5},{5,4},{6,7},{7,6},{8,9},{9,8},{10,11... | collective-permute-start | bytes 319496 | tf_op jit(solution)/shard_map/ppermute | solution.py:409
  34.0 7.1 %collective-permute-start.15 = (bf16[272,256]{1,0:T(8,128)(2,1)S(1)}, bf16[272,256]{1,0:T(8,128)(2,1)S(1)}, u32[]{:S(2)}, u32[]{:S(2)}) collective-permute-start(bf16[272,256]{1,0:T(8,128)(2,1)S(1)} %get-tuple-element.39.refs_0_), channel_id=1, source_target_pairs={{0,3},{1,2},{2,1},{3,0},{4,7},{5,6},{6,5},{7,4},{8,11},{9,10},{10,... | collective-permute-start | bytes 417800 | tf_op jit(solution)/shard_map/ppermute | solution.py:409
  35.8 6.4 %collective-permute-start.14 = (bf16[272,256]{1,0:T(8,128)(2,1)S(1)}, bf16[272,256]{1,0:T(8,128)(2,1)S(1)}, u32[]{:S(2)}, u32[]{:S(2)}) collective-permute-start(bf16[272,256]{1,0:T(8,128)(2,1)S(1)} %get-tuple-element.39.refs_0_), channel_id=1, source_target_pairs={{0,2},{1,3},{2,0},{3,1},{4,6},{5,7},{6,4},{7,5},{8,10},{9,11},{10,... | collective-permute-start | bytes 417800 | tf_op jit(solution)/shard_map/ppermute | solution.py:409
  36.7 5.6 %collective-permute-start.13 = (bf16[272,256]{1,0:T(8,128)(2,1)S(1)}, bf16[272,256]{1,0:T(8,128)(2,1)S(1)}, u32[]{:S(2)}, u32[]{:S(2)}) collective-permute-start(bf16[272,256]{1,0:T(8,128)(2,1)S(1)} %get-tuple-element.39.refs_0_), channel_id=1, source_target_pairs={{0,1},{1,0},{2,3},{3,2},{4,5},{5,4},{6,7},{7,6},{8,9},{9,8},{10,11... | collective-permute-start | bytes 417800 | tf_op jit(solution)/shard_map/ppermute | solution.py:409
  44.2 4.9 %collective-permute-start.18 = (bf16[64,256]{1,0:T(8,128)(2,1)S(1)}, bf16[64,256]{1,0:T(8,128)(2,1)S(1)}, u32[]{:S(2)}, u32[]{:S(2)}) collective-permute-start(bf16[64,256]{1,0:T(8,128)(2,1)S(1)} %get-tuple-element.43.refs_0_), channel_id=1, source_target_pairs={{0,3},{1,2},{2,1},{3,0},{4,7},{5,6},{6,5},{7,4},{8,11},{9,10},{10,... | collective-permute-start | bytes 98312 | tf_op jit(solution)/shard_map/ppermute | solution.py:409
  45.9 3.9 %collective-permute-start.17 = (bf16[64,256]{1,0:T(8,128)(2,1)S(1)}, bf16[64,256]{1,0:T(8,128)(2,1)S(1)}, u32[]{:S(2)}, u32[]{:S(2)}) collective-permute-start(bf16[64,256]{1,0:T(8,128)(2,1)S(1)} %get-tuple-element.43.refs_0_), channel_id=1, source_target_pairs={{0,2},{1,3},{2,0},{3,1},{4,6},{5,7},{6,4},{7,5},{8,10},{9,11},{10,... | collective-permute-start | bytes 98312 | tf_op jit(solution)/shard_map/ppermute | solution.py:409
  47.2 3.9 %collective-permute-start.16 = (bf16[64,256]{1,0:T(8,128)(2,1)S(1)}, bf16[64,256]{1,0:T(8,128)(2,1)S(1)}, u32[]{:S(2)}, u32[]{:S(2)}) collective-permute-start(bf16[64,256]{1,0:T(8,128)(2,1)S(1)} %get-tuple-element.43.refs_0_), channel_id=1, source_target_pairs={{0,1},{1,0},{2,3},{3,2},{4,5},{5,4},{6,7},{7,6},{8,9},{9,8},{10,11... | collective-permute-start | bytes 98312 | tf_op jit(solution)/shard_map/ppermute | solution.py:409
  52.4 2.0 %collective-permute-start.19 = (bf16[4,256,256]{2,1,0:T(8,128)(2,1)S(1)}, bf16[4,256,256]{2,1,0:T(8,128)(2,1)S(1)}, u32[]{:S(2)}, u32[]{:S(2)}) collective-permute-start(bf16[4,256,256]{2,1,0:T(8,128)(2,1)S(1)} %get-tuple-element.49), channel_id=1, source_target_pairs={{0,16},{16,0},{1,17},{17,1},{2,18},{18,2},{3,19},{19,3},{4,20},{20... | collective-permute-start | bytes 1572872 | tf_op jit(solution)/shard_map/ppermute | solution.py:405
  55.1 8.3 %collective-permute-start.20 = (bf16[256,256]{1,0:T(8,128)(2,1)S(1)}, bf16[256,256]{1,0:T(8,128)(2,1)S(1)}, u32[]{:S(2)}, u32[]{:S(2)}) collective-permute-start(bf16[256,256]{1,0:T(8,128)(2,1)S(1)} %get-tuple-element.51), channel_id=1, source_target_pairs={{0,4},{1,5},{2,6},{3,7},{4,0},{5,1},{6,2},{7,3},{8,12},{9,13},{10,... | collective-permute-start | bytes 393224 | tf_op jit(solution)/shard_map/ppermute | solution.py:402
  57.7 12.9 %collective-permute-start.21 = (bf16[256,256]{1,0:T(8,128)(2,1)S(1)}, bf16[256,256]{1,0:T(8,128)(2,1)S(1)}, u32[]{:S(2)}, u32[]{:S(2)}) collective-permute-start(bf16[256,256]{1,0:T(8,128)(2,1)S(1)} %get-tuple-element.52), channel_id=1, source_target_pairs={{0,8},{1,9},{2,10},{3,11},{4,12},{5,13},{6,14},{7,15},{8,0},{9,1},... | collective-permute-start | bytes 393224 | tf_op jit(solution)/shard_map/ppermute | solution.py:402
  58.8 11.8 %collective-permute-start.22 = (bf16[256,256]{1,0:T(8,128)(2,1)S(1)}, bf16[256,256]{1,0:T(8,128)(2,1)S(1)}, u32[]{:S(2)}, u32[]{:S(2)}) collective-permute-start(bf16[256,256]{1,0:T(8,128)(2,1)S(1)} %get-tuple-element.53), channel_id=1, source_target_pairs={{0,12},{1,13},{2,14},{3,15},{4,8},{5,9},{6,10},{7,11},{8,4},{9,5},... | collective-permute-start | bytes 393224 | tf_op jit(solution)/shard_map/ppermute | solution.py:402

commit v4 on v0

--- a/solution.py
+++ b/solution.py
@@ -1,7 +1,17 @@
+import functools
+
 import jax
 import jax.numpy as jnp
 from jax import lax
+from jax.experimental import pallas as pl
+from jax.experimental.pallas import tpu as pltpu
 from jax.sharding import PartitionSpec as P
+
+F32 = jnp.float32
+BF16 = jnp.bfloat16
+PLANE = 4
+STATS = 16
+VMEM_LIMIT = 16 * 1024 * 1024
 
 
 def passed_along(block, axis, distance):
@@ -36,7 +46,7 @@
     )
 
 
-def body(inputs, cotangent, doc_lengths, norm_gain, w_qkv, w_out):
+def pipelined(inputs, cotangent, doc_lengths, norm_gain, w_qkv, w_out):
     sections = lax.axis_size("section")
     section = lax.axis_index("section")
     micro = inputs.shape[0]
@@ -73,10 +83,6 @@
         forward_step, (empty, start_saved), jnp.arange(total_steps - 1, dtype=jnp.int32)
     )
     _, saved = forward_at(jnp.int32(total_steps - 1), incoming, saved)
-    back_qkv, back_out = (
-        lax.all_gather(w_qkv[0], "dp", axis=0, tiled=True),
-        lax.all_gather(w_out[0], "dp", axis=1, tiled=True),
-    )
 
     def backward_at(step, incoming, sum_qkv, sum_out):
         index = step - (sections - 1 - section)
@@ -86,7 +92,7 @@
         grad_y = jnp.where(section == sections - 1, last, incoming)
         x = lax.dynamic_index_in_dim(saved, slot, 0, keepdims=False)
         seg = lax.dynamic_index_in_dim(segs, slot, 0, keepdims=False)
-        _, pull = jax.vjp(lambda a, b, c: layer(a, gain, b, c, seg), x, back_qkv, back_out)
+        _, pull = jax.vjp(lambda a, b, c: layer(a, gain, b, c, seg), x, full_qkv, full_out)
         grad_x, grad_q, grad_o = pull(grad_y)
         sum_qkv = sum_qkv + jnp.where(live, grad_q.astype(jnp.float32), 0.0)
         sum_out = sum_out + jnp.where(live, grad_o.astype(jnp.float32), 0.0)
@@ -98,8 +104,8 @@
         incoming = passed_along(grad_x, "section", -1)
         return ((incoming, sum_qkv, sum_out), None)
 
-    zero_qkv = jnp.zeros(back_qkv.shape, jnp.float32)
-    zero_out = jnp.zeros(back_out.shape, jnp.float32)
+    zero_qkv = jnp.zeros(full_qkv.shape, jnp.float32)
+    zero_out = jnp.zeros(full_out.shape, jnp.float32)
     (incoming, sum_qkv, sum_out), _ = lax.scan(
         backward_step, (empty, zero_qkv, zero_out), jnp.arange(total_steps - 1, dtype=jnp.int32)
     )
@@ -111,7 +117,319 @@
     return (share_qkv[None], share_out[None])
 
 
+def nn(a, b):
+    return lax.dot_general(a, b, (((1,), (0,)), ((), ())), preferred_element_type=F32)
+
+
+def nt(a, b):
+    return lax.dot_general(a, b, (((1,), (1,)), ((), ())), preferred_element_type=F32)
+
+
+def blocks_kernel(planes, index, gain_ref, qkv_ref, wout_ref, x_ref, c_ref, pack_ref, *refs):
+    out_refs, sems = refs[:PLANE], refs[PLANE]
+    qkv_rows, heads = qkv_ref.shape[0], wout_ref.shape[0]
+    width = x_ref.shape[-1] // (planes * PLANE)
+    section, p = index[0], index[2]
+    copies = [
+        pltpu.make_async_copy(qkv_ref, pack_ref.at[:qkv_rows], sems.at[0]),
+        pltpu.make_async_copy(wout_ref, pack_ref.at[qkv_rows : qkv_rows + heads], sems.at[1]),
+    ]
+    for k in range(PLANE):
+        for z in range(planes):
+            at = pl.multiple_of((z * PLANE + (p ^ k)) * width, width)
+            for half, ref in enumerate((x_ref, c_ref)):
+                copies.append(
+                    pltpu.make_async_copy(
+                        ref.at[section, :, pl.ds(at, width)],
+                        out_refs[k].at[half, :, pl.ds(z * width, width)],
+                        sems.at[len(copies)],
+                    )
+                )
+    for copy in copies:
+        copy.start()
+    pack_ref[qkv_rows + heads :, :] = jnp.broadcast_to(gain_ref[...].astype(F32), (STATS, width)).astype(BF16)
+    for copy in copies:
+        copy.wait()
+
+
+def project_kernel(planes, heads, index, *refs):
+    blocks, own, other = refs[:PLANE], refs[PLANE : PLANE + planes], refs[PLANE + planes : PLANE + 2 * planes]
+    x_ref, c_ref, vx_ref, gain_ref = refs[PLANE + 2 * planes : PLANE + 2 * planes + 4]
+    out_refs = refs[PLANE + 2 * planes + 4 : -2]
+    vc_ref, sum_ref = refs[-2:]
+    qkv, width = 3 * heads, vx_ref.shape[-1]
+    section, z, p = index[0], index[1], index[2]
+    for k in range(planes):
+        at = z ^ k
+        zero = jnp.where(section == 0, own[k][...], other[k][...])
+        one = jnp.where(section == 0, other[k][...], own[k][...])
+        gains = [w[qkv + heads :].astype(F32)[0:1] for w in (zero, one)]
+        gain_ref[at, 0:1, :] = gains[0]
+        gain_ref[at, 1:2, :] = gains[1]
+        empty = jnp.zeros((heads, width), BF16)
+        vx_ref[at, :qkv, :] = (zero[:qkv].astype(F32) * gains[0]).astype(BF16)
+        vx_ref[at, qkv : qkv + heads, :] = zero[qkv : qkv + heads]
+        vx_ref[at, qkv + heads : 2 * qkv + heads, :] = (one[:qkv].astype(F32) * gains[1]).astype(BF16)
+        vx_ref[at, 2 * qkv + heads :, :] = empty
+        vc_ref[at, :heads, :] = empty
+        vc_ref[at, heads : 2 * heads, :] = one[qkv : qkv + heads]
+        vc_ref[at, 2 * heads : 3 * heads, :] = zero[qkv : qkv + heads]
+        vc_ref[at, 3 * heads :, :] = empty
+    for k in range(PLANE):
+        x_ref[p ^ k] = blocks[k][0]
+        c_ref[p ^ k] = blocks[k][1]
+    rows = x_ref.shape[0] * x_ref.shape[1]
+    with_x = with_c = squares = products = None
+    for z in range(planes):
+        cols = slice(z * width, (z + 1) * width)
+        x = x_ref[:, :, cols].reshape(rows, width)
+        c = c_ref[:, :, cols].reshape(rows, width)
+        wide = x.astype(F32)
+        out = vx_ref[z, qkv : qkv + heads, :]
+        right = jnp.concatenate([vx_ref[z, qkv + heads : 2 * qkv + heads, :], out], axis=0)
+        new = nt(x, vx_ref[z]), nt(c, vc_ref[z]), jnp.sum(wide * wide, axis=1, keepdims=True), nt(out, right)
+        if with_x is None:
+            with_x, with_c, squares, products = new
+        else:
+            with_x, with_c = with_x + new[0], with_c + new[1]
+            squares, products = squares + new[2], products + new[3]
+    half = 2 * heads
+    lane = lax.broadcasted_iota(jnp.int32, (rows, half), 1)
+    high = squares.astype(BF16).astype(F32)
+    last = jnp.where(lane == heads, high, jnp.where(lane == heads + 1, squares - high, with_c[:, half:]))
+    sum_ref[:, : 3 * half] = with_x[:, : 3 * half].astype(BF16)
+    sum_ref[:, 3 * half : 4 * half] = (with_x[:, 3 * half :] + with_c[:, :half]).astype(BF16)
+    sum_ref[:, 4 * half :] = last.astype(BF16)
+    block = rows // PLANE
+    for k in range(PLANE):
+        start = pl.multiple_of((p ^ k) * block, block)
+        out_refs[k][:, : 5 * half] = sum_ref[pl.ds(start, block), :]
+        out_refs[k][:, 5 * half :] = products.astype(BF16)
+
+
+def exact(a, b, dims):
+    return lax.dot_general(
+        a, b, (dims, ((), ())), precision=lax.Precision.HIGHEST, preferred_element_type=F32
+    )
+
+
+def attention(qkv, allowed, heads):
+    query, keys, values = (qkv[:, i * heads : (i + 1) * heads].astype(BF16) for i in range(3))
+    scores = jnp.where(allowed, nt(query, keys) * heads ** (-0.5), -1e30)
+    raised = jnp.exp(scores - jnp.max(scores, axis=1, keepdims=True))
+    probs = raised / jnp.sum(raised, axis=1, keepdims=True)
+    return probs, nn(probs.astype(BF16), values).astype(BF16)
+
+
+def attention_grad(qkv, probs, d_att, heads):
+    query, keys, values = (qkv[:, i * heads : (i + 1) * heads].astype(BF16) for i in range(3))
+    d_values = nn(jnp.transpose(probs).astype(BF16), d_att)
+    d_probs = nt(d_att, values).astype(BF16).astype(F32)
+    inner = jnp.sum(probs * d_probs, axis=1, keepdims=True)
+    d_scores = probs * (d_probs - inner) * heads ** (-0.5)
+    d_query = nn(d_scores.astype(BF16), keys)
+    d_keys = nn(jnp.transpose(d_scores).astype(BF16), query)
+    return jnp.concatenate([d_query, d_keys, d_values], axis=1).astype(BF16).astype(F32)
+
+
+def chain_kernel(features, heads, index, docs, *refs):
+    parts, out_ref = refs[:-1], refs[-1]
+    qkv, half = 3 * heads, 2 * heads
+    total = parts[0][...].astype(F32)
+    for part in parts[1:]:
+        total = total + part[...].astype(F32)
+    rows = total.shape[0]
+    section = index[0]
+    query_at = lax.broadcasted_iota(jnp.int32, (rows, rows), 0)
+    key_at = lax.broadcasted_iota(jnp.int32, (rows, rows), 1)
+    allowed = query_at >= key_at
+    end = 0
+    for i in range(docs.shape[2]):
+        end = end + docs[section, 0, i]
+        allowed = allowed & ((query_at >= end) == (key_at >= end))
+    x_out = total[:, qkv : 2 * half]
+    x_one = total[:, 2 * half : 2 * half + qkv]
+    c_one = total[:, 4 * half - heads : 4 * half].astype(BF16)
+    tail = total[:, 4 * half : 5 * half]
+    c_zero = tail[:, :heads]
+    lane = lax.broadcasted_iota(jnp.int32, tail.shape, 1)
+    squares = jnp.sum(jnp.where((lane == heads) | (lane == heads + 1), tail, 0.0), axis=1, keepdims=True)
+    mixed = total[:, 5 * half : 5 * half + qkv]
+    gram = total[:, 5 * half + qkv :]
+
+    scale0 = lax.rsqrt(squares / features + 1e-05)
+    qkv0 = (total[:, :qkv] * scale0).astype(BF16).astype(F32)
+    probs0, att0 = attention(qkv0, allowed, heads)
+    wide0 = att0.astype(F32)
+    y_out = x_out + exact(wide0, gram, ((1,), (0,)))
+    squares = squares + jnp.sum(wide0 * (x_out + y_out), axis=1, keepdims=True)
+    scale1 = lax.rsqrt(jnp.maximum(squares, 0.0) / features + 1e-05)
+    qkv1 = ((x_one + exact(wide0, mixed, ((1,), (0,)))) * scale1).astype(BF16).astype(F32)
+    probs1, att1 = attention(qkv1, allowed, heads)
+    d_qkv1 = attention_grad(qkv1, probs1, c_one, heads)
+    inner = jnp.sum(d_qkv1 * qkv1, axis=1, keepdims=True) * scale1 * scale1 / features
+    e1 = d_qkv1 * scale1
+    d_att0 = c_zero + exact(e1, mixed, ((1,), (1,))) - inner * y_out
+    e0 = attention_grad(qkv0, probs0, d_att0.astype(BF16), heads) * scale0
+    factors = [e0, wide0, e1, wide0 * inner, att1.astype(F32), jnp.zeros((rows, heads), F32)]
+    out_ref[...] = jnp.concatenate(factors, axis=1).astype(BF16)
+
+
+def grads_kernel(planes, heads, index, *refs):
+    factors, (x_ref, c_ref, vx_ref, gain_ref) = refs[:PLANE], refs[PLANE : PLANE + 4]
+    keep_ref, send_ref, all_ref = refs[PLANE + 4 :]
+    qkv, half, width = 3 * heads, 2 * heads, vx_ref.shape[-1]
+    section, p = index[0], index[2]
+    for k in range(PLANE):
+        all_ref[p ^ k] = factors[k][...]
+    rows = x_ref.shape[0] * x_ref.shape[1]
+    turned = jnp.transpose(all_ref[...].astype(F32).reshape(rows, 5 * half)).astype(BF16)
+    att0, att1 = turned[qkv : qkv + heads], turned[4 * half : 4 * half + heads]
+    right = turned[2 * half : 4 * half]
+    small = nt(right, att0).astype(BF16)
+    small_t = nt(att0, right[:qkv]).astype(BF16)
+    for z in range(planes):
+        cols = slice(z * width, (z + 1) * width)
+        x = x_ref[:, :, cols].reshape(rows, width)
+        c = c_ref[:, :, cols].reshape(rows, width)
+        out = vx_ref[z, qkv : qkv + heads, :]
+        with_x = nn(turned[: 4 * half], x)
+        left = with_x[2 * half :] + nn(small, out)
+        zero = with_x[:qkv] * gain_ref[z, 0:1, :]
+        one = left[:qkv] * gain_ref[z, 1:2, :]
+        keep_ref[z, :qkv, :] = jnp.where(section == 0, zero, one)
+        send_ref[z, :qkv, :] = jnp.where(section == 0, one, zero).astype(BF16)
+        zero = nn(att0, c) + nn(small_t, vx_ref[z, qkv + heads : 2 * qkv + heads, :]) - left[qkv:]
+        one = nn(att1, c)
+        keep_ref[z, qkv:, :] = jnp.where(section == 0, zero, one)
+        send_ref[z, qkv:, :] = jnp.where(section == 0, one, zero).astype(BF16)
+
+
+def merge_kernel(index, keep_ref, come_ref, *out_refs):
+    place = index[1]
+    out_refs[0][...] = keep_ref[place] + come_ref[place].astype(F32)
+    for k in range(1, len(out_refs)):
+        out_refs[k][...] = (keep_ref[place ^ k] + come_ref[place ^ k].astype(F32)).astype(BF16)
+
+
+def last_kernel(qkv_rows, keep_ref, *refs):
+    parts, (qkv_ref, out_ref) = refs[:-2], refs[-2:]
+    total = keep_ref[...]
+    for part in parts:
+        total = total + part[...].astype(F32)
+    qkv_ref[...] = total[:qkv_rows]
+    out_ref[...] = total[qkv_rows:]
+
+
+def far_first(value, count, send):
+    of = lambda k: value[k] if isinstance(value, (list, tuple)) else value
+    got = {k: send(of(k), k) for k in reversed(range(1, count))}
+    return [of(0)] + [got[k] for k in range(1, count)]
+
+
+def call(kernel, outs, *args, scalars=0, scratch=()):
+    smem = pl.BlockSpec(memory_space=pltpu.SMEM)
+    vmem = pl.BlockSpec(memory_space=pltpu.VMEM)
+    return pl.pallas_call(
+        kernel,
+        out_shape=[jax.ShapeDtypeStruct(shape, dtype) for shape, dtype in outs],
+        in_specs=[smem] * scalars + [vmem] * (len(args) - scalars),
+        out_specs=[vmem] * len(outs),
+        scratch_shapes=[pltpu.VMEM(shape, dtype) for shape, dtype in scratch],
+        compiler_params=pltpu.CompilerParams(vmem_limit_bytes=VMEM_LIMIT),
+    )(*args)
+
+
+def planar(inputs, cotangent, doc_lengths, norm_gain, w_qkv, w_out):
+    shards = lax.axis_size("dp")
+    planes = shards // PLANE
+    section, place = lax.axis_index("section"), lax.axis_index("dp")
+    z, p = place // PLANE, place % PLANE
+    index = jnp.stack([section, z, p]).astype(jnp.int32)
+    block, features = inputs.shape[1:]
+    rows = PLANE * block
+    heads, width = w_out.shape[1:]
+    qkv_rows = w_qkv.shape[2]
+    cols = planes * width
+    def along_z(value, k):
+        route = [(a * PLANE + b, (a ^ k) * PLANE + b) for a in range(planes) for b in range(PLANE)]
+        return lax.ppermute(value, "dp", route)
+
+    def to_sibling(value):
+        return lax.ppermute(value, "section", [(0, 1), (1, 0)])
+
+    def along_plane(value, k):
+        route = [(a * PLANE + b, a * PLANE + (b ^ k)) for a in range(planes) for b in range(PLANE)]
+        return lax.ppermute(value, "dp", route)
+
+    def exchange(value):
+        return far_first(value, PLANE, along_plane)
+
+    gain = lax.dynamic_slice(norm_gain, (0, place * width), (1, width))
+    smem, vmem = pl.BlockSpec(memory_space=pltpu.SMEM), pl.BlockSpec(memory_space=pltpu.VMEM)
+    hbm = pl.BlockSpec(memory_space=pltpu.HBM)
+    in_hbm = [
+        pltpu.with_memory_space_constraint(value, pltpu.HBM)
+        for value in (w_qkv[0].T, w_out[0], inputs, cotangent)
+    ]
+    pack, *blocks = pl.pallas_call(
+        functools.partial(blocks_kernel, planes),
+        out_shape=[jax.ShapeDtypeStruct((qkv_rows + heads + STATS, width), BF16)]
+        + [jax.ShapeDtypeStruct((2, block, cols), BF16)] * PLANE,
+        in_specs=[smem, vmem] + [hbm] * 4,
+        out_specs=[vmem] * (1 + PLANE),
+        scratch_shapes=[pltpu.SemaphoreType.DMA((2 + 2 * PLANE * planes,))],
+        compiler_params=pltpu.CompilerParams(vmem_limit_bytes=VMEM_LIMIT),
+    )(index, gain, *in_hbm)
+    own = far_first(pack, planes, along_z)
+    blocks = [blocks[0]] + far_first(blocks, PLANE, along_plane)[1:]
+    other = [to_sibling(piece) for piece in own]
+
+    split = ((PLANE, block, cols), BF16)
+    half = 2 * heads
+    x, c, vx, gains, *sent = call(
+        functools.partial(project_kernel, planes, heads),
+        [split, split, ((planes, 4 * half, width), BF16), ((planes, 8, width), F32)]
+        + [((block, 7 * half), BF16)] * PLANE,
+        index, *blocks, *own, *other, scalars=1,
+        scratch=[((planes, 2 * half, width), BF16), ((rows, 5 * half), BF16)],
+    )
+    (factors,) = call(
+        functools.partial(chain_kernel, features, heads),
+        [((block, 5 * half), BF16)],
+        index, doc_lengths, *exchange(sent), scalars=2,
+    )
+    grads = (planes, qkv_rows + heads, width)
+    keep, send = call(
+        functools.partial(grads_kernel, planes, heads),
+        [(grads, F32), (grads, BF16)],
+        index, *exchange(factors), x, c, vx, gains, scalars=1,
+        scratch=[((PLANE, block, 5 * half), BF16)],
+    )
+    merged = call(
+        merge_kernel,
+        [(grads[1:], F32)] + [(grads[1:], BF16)] * (planes - 1),
+        index, keep, to_sibling(send), scalars=1,
+    )
+    parts = far_first(merged, planes, along_z)[1:]
+    grad_qkv, grad_out = call(
+        functools.partial(last_kernel, qkv_rows),
+        [((qkv_rows, width), F32), ((heads, width), F32)],
+        merged[0], *parts,
+    )
+    return (grad_qkv.T[None], grad_out[None])
+
+
 def solution(mesh):
+    sections, shards = mesh.shape["section"], mesh.shape["dp"]
+    planes = shards // PLANE
+
+    def body(inputs, *rest):
+        fits = shards % PLANE == 0 and planes & (planes - 1) == 0
+        if sections == 2 and inputs.shape[0] == 2 and fits:
+            return planar(inputs, *rest)
+        return pipelined(inputs, *rest)
+
     return jax.shard_map(
         body,
         mesh=mesh,

time: 352 us -> 65.6 us (0.19)
  waiting for transfers between devices: 225 us -> 29 us
  blocking collectives: 48.8 us -> 0 us
  matrix products: 32 us -> 0 us
  starting transfers between devices: 6.65 us -> 25.1 us
  between operations: 13.9 us -> 0.74 us
  other arithmetic: 12.1 us -> 0.08 us
  Pallas kernels: 0 us -> 9.72 us
  local copies, waits for them, and re-layouts: 9.69 us -> 0.7 us
    reduce_scatter x2 -> x0, waiting for transfers between devices: 206 us -> none  [the longest x1 134 us: body(): lax.psum_scatter(sum_qkv, 'dp', scatter_dimension=0, tiled=True)]
    all_gather x1 -> x0, blocking collectives: 48.8 us -> none  [body(): lax.all_gather(w_out[0], 'dp', axis=1, tiled=True)]
    dot_general x35 -> x0, matrix products: 32 us -> none  [the longest x10 15.2 us: layer(): jnp.dot(normed, w_qkv, preferred_element_type=jnp.float32)]
    ppermute x4 -> x20, waiting for transfers between devices: 2.97 us -> 29 us  [the longest x6 16.4 us: along_z(): return lax.ppermute(value, 'dp', route)]
    ppermute x4 -> x20, starting transfers between devices: 6.52 us -> 25.1 us  [the longest x9 12.7 us: along_plane(): return lax.ppermute(value, 'dp', route)]
    all_gather x1 -> x0, waiting for transfers between devices: 16.5 us -> none  [body(): lax.all_gather(w_qkv[0], 'dp', axis=0, tiled=True)]
    pallas_call x0 -> x6, Pallas kernels: none -> 9.72 us  [the longest x5 7.67 us: call(): pl.pallas_call(kernel, out_shape=[jax.ShapeDtypeStruct(shape, dtype) for...]
    dynamic_update_slice x3 -> x0, other arithmetic: 4.28 us -> none  [forward_at(): lax.dynamic_update_index_in_dim(saved, jnp.where(live, x, old), slot, 0)]
  transfers between devices with their start and end apart: 7 -> 20, of which waited for: 5 -> 12; matrix products, arithmetic and copies ran while one was open for 6% -> 0% of each run, Pallas kernels for 0% -> 0%
where the time goes in v4:
time: 65.6 us; the launch traced here: 65.4 us
  waiting for transfers between devices  29 us (44%)
  starting transfers between devices  25.1 us (38%)
  Pallas kernels  9.72 us (15%)
  between operations  0.74 us (1%)
  local copies, waits for them, and re-layouts  0.7 us (1%)
    ppermute x6, waiting for transfers between devices, along_z(): return lax.ppermute(value, 'dp', route)  16.4 us
    ppermute x9, starting transfers between devices, along_plane(): return lax.ppermute(value, 'dp', route)  12.7 us
    ppermute x6, starting transfers between devices, along_z(): return lax.ppermute(value, 'dp', route)  11.2 us
    ppermute x9, waiting for transfers between devices, along_plane(): return lax.ppermute(value, 'dp', route)  10.7 us
    pallas_call x5, Pallas kernels, call(): pl.pallas_call(kernel, out_shape=[jax.ShapeDtypeStruct(shape, dtype) for...  7.67 us
    pallas_call x1, Pallas kernels, planar(): pl.pallas_call(functools.partial(blocks_kernel, planes), out_shape=[jax.S...  2.05 us
    ppermute x5, waiting for transfers between devices, to_sibling(): return lax.ppermute(value, 'section', [(0, 1), (1, 0)])  1.91 us
  transfers between devices with their start and end apart: 20, of which 12 were waited for; matrix products, arithmetic and copies ran while one was open for 0% of the time, Pallas kernels for 0%

profile of v4, /device:TPU:0, one launch (start us, length us, event | category | flops | bytes accessed | tf_op | source)
XLA Modules:
  0.0 65.4 jit_solution(10964198722233226902)
XLA Ops:
  0.6 0.0 copy-start
  0.7 0.7 %copy-done = bf16[1,4096]{1,0:T(2,128)(2,1)S(1)} copy-done((bf16[1,4096]{1,0:T(2,128)(2,1)S(1)}, bf16[1,4096]{1,0:T(2,128)(2,1)}, u32[]{:S(2)}) %copy-start) | copy-done | bytes 8216
  1.4 0.1 pad_add_fusion.index
  1.4 2.0 %shard_map.77 = (bf16[272,256]{1,0:T(8,128)(2,1)S(1)}, bf16[2,64,1024]{2,1,0:T(8,128)(2,1)S(1)}, bf16[2,64,1024]{2,1,0:T(8,128)(2,1)S(1)}, bf16[2,64,1024]{2,1,0:T(8,128)(2,1)S(1)}, bf16[2,64,1024]{2,1,0:T(8,128)(2,1)S(1)}) custom-call(s32[3]{0:T(128)S(1)} %pad_add_fusion.index, bf16[1,256]{1,0:T(2,128)(2,1)S(1)} %constant_dynamic-slice_fusion.gain_ref, ...), custom_call_target="tpu_custom_call" | custom-call | tf_op jit(solution)/shard_map/pallas_call | solution.py:375
  3.5 0.5 collective-permute-start.6
  4.0 4.7 %collective-permute-start.5 = (bf16[272,256]{1,0:T(8,128)(2,1)S(1)}, bf16[272,256]{1,0:T(8,128)(2,1)S(1)}, u32[]{:S(2)}, u32[]{:S(2)}) collective-permute-start(bf16[272,256]{1,0:T(8,128)(2,1)S(1)} %get-tuple-element.27.refs_4_), channel_id=1, source_target_pairs={{0,12},{1,13},{2,14},{3,15},{4,8},{5,9},{6,10},{7,11},{8,4},{9,5},... | collective-permute-start | bytes 417800 | tf_op jit(solution)/shard_map/ppermute | solution.py:356
  8.7 1.5 %collective-permute-start = (bf16[2,64,1024]{2,1,0:T(8,128)(2,1)S(1)}, bf16[2,64,1024]{2,1,0:T(8,128)(2,1)S(1)}, u32[]{:S(2)}, u32[]{:S(2)}) collective-permute-start(bf16[2,64,1024]{2,1,0:T(8,128)(2,1)S(1)} %get-tuple-element.24), channel_id=1, source_target_pairs={{0,1},{1,0},{2,3},{3,2},{4,5},{5,4},{6,7},{7,6},{8,9},{9,8},{10,11... | collective-permute-start | bytes 786440 | tf_op jit(solution)/shard_map/ppermute | solution.py:363
  10.2 0.0 collective-permute-start.4
  10.2 0.8 %collective-permute-start.3 = (bf16[272,256]{1,0:T(8,128)(2,1)S(1)}, bf16[272,256]{1,0:T(8,128)(2,1)S(1)}, u32[]{:S(2)}, u32[]{:S(2)}) collective-permute-start(bf16[272,256]{1,0:T(8,128)(2,1)S(1)} %get-tuple-element.27.refs_4_), channel_id=1, source_target_pairs={{0,4},{1,5},{2,6},{3,7},{4,0},{5,1},{6,2},{7,3},{8,12},{9,13},{10,... | collective-permute-start | bytes 417800 | tf_op jit(solution)/shard_map/ppermute | solution.py:356
  11.0 0.0 collective-permute-done.6.refs_8_
  11.0 1.5 %collective-permute-start.1 = (bf16[2,64,1024]{2,1,0:T(8,128)(2,1)S(1)}, bf16[2,64,1024]{2,1,0:T(8,128)(2,1)S(1)}, u32[]{:S(2)}, u32[]{:S(2)}) collective-permute-start(bf16[2,64,1024]{2,1,0:T(8,128)(2,1)S(1)} %get-tuple-element.25), channel_id=1, source_target_pairs={{0,2},{1,3},{2,0},{3,1},{4,6},{5,7},{6,4},{7,5},{8,10},{9,11},{10,... | collective-permute-start | bytes 786440 | tf_op jit(solution)/shard_map/ppermute | solution.py:363
  12.5 0.8 %collective-permute-done.5.refs_7_ = bf16[272,256]{1,0:T(8,128)(2,1)S(1)} collective-permute-done((bf16[272,256]{1,0:T(8,128)(2,1)S(1)}, bf16[272,256]{1,0:T(8,128)(2,1)S(1)}, u32[]{:S(2)}, u32[]{:S(2)}) %collective-permute-start.5) | collective-permute-done | bytes 139296 | tf_op jit(solution)/shard_map/ppermute | solution.py:356
  13.3 2.6 %collective-permute-start.2 = (bf16[2,64,1024]{2,1,0:T(8,128)(2,1)S(1)}, bf16[2,64,1024]{2,1,0:T(8,128)(2,1)S(1)}, u32[]{:S(2)}, u32[]{:S(2)}) collective-permute-start(bf16[2,64,1024]{2,1,0:T(8,128)(2,1)S(1)} %get-tuple-element.26), channel_id=1, source_target_pairs={{0,3},{1,2},{2,1},{3,0},{4,7},{5,6},{6,5},{7,4},{8,11},{9,10},{10,... | collective-permute-start | bytes 786440 | tf_op jit(solution)/shard_map/ppermute | solution.py:363
  15.9 5.2 %collective-permute-done.4.refs_6_ = bf16[272,256]{1,0:T(8,128)(2,1)S(1)} collective-permute-done((bf16[272,256]{1,0:T(8,128)(2,1)S(1)}, bf16[272,256]{1,0:T(8,128)(2,1)S(1)}, u32[]{:S(2)}, u32[]{:S(2)}) %collective-permute-start.4) | collective-permute-done | bytes 139296 | tf_op jit(solution)/shard_map/ppermute | solution.py:356
  21.1 0.0 collective-permute-start.9
  21.1 0.0 collective-permute-done.3.refs_5_
  21.1 0.5 collective-permute-start.8
  21.6 0.0 collective-permute-done.refs_1_
  21.6 0.1 collective-permute-start.7
  21.7 2.5 %collective-permute-done.1.refs_2_ = bf16[2,64,1024]{2,1,0:T(8,128)(2,1)S(1)} collective-permute-done((bf16[2,64,1024]{2,1,0:T(8,128)(2,1)S(1)}, bf16[2,64,1024]{2,1,0:T(8,128)(2,1)S(1)}, u32[]{:S(2)}, u32[]{:S(2)}) %collective-permute-start.1) | collective-permute-done | bytes 262176 | tf_op jit(solution)/shard_map/ppermute | solution.py:363
  24.2 0.0 collective-permute-done.2.refs_3_
  24.2 0.0 collective-permute-done.9.refs_11_
  24.2 0.0 collective-permute-done.8.refs_10_
  24.2 0.0 collective-permute-done.7.refs_9_
  24.2 1.6 %shard_map.78 = (bf16[4,64,1024]{2,1,0:T(8,128)(2,1)S(1)}, bf16[4,64,1024]{2,1,0:T(8,128)(2,1)S(1)}, bf16[4,512,256]{2,1,0:T(8,128)(2,1)S(1)}, f32[4,8,256]{2,1,...) custom-call(s32[3]{0:T(128)S(1)} %pad_add_fusion.index, ...), custom_call_target="tpu_custom_call" | custom-call | tf_op jit(solution)/shard_map/pallas_call | solution.py:333
  25.8 1.0 %collective-permute-start.10 = (bf16[64,896]{1,0:T(8,128)(2,1)S(1)}, bf16[64,896]{1,0:T(8,128)(2,1)S(1)}, u32[]{:S(2)}, u32[]{:S(2)}) collective-permute-start(bf16[64,896]{1,0:T(8,128)(2,1)S(1)} %get-tuple-element.29), channel_id=1, source_target_pairs={{0,1},{1,0},{2,3},{3,2},{4,5},{5,4},{6,7},{7,6},{8,9},{9,8},{10,11... | collective-permute-start | bytes 344072 | tf_op jit(solution)/shard_map/ppermute | solution.py:363
  26.8 1.1 %collective-permute-start.11 = (bf16[64,896]{1,0:T(8,128)(2,1)S(1)}, bf16[64,896]{1,0:T(8,128)(2,1)S(1)}, u32[]{:S(2)}, u32[]{:S(2)}) collective-permute-start(bf16[64,896]{1,0:T(8,128)(2,1)S(1)} %get-tuple-element.30), channel_id=1, source_target_pairs={{0,2},{1,3},{2,0},{3,1},{4,6},{5,7},{6,4},{7,5},{8,10},{9,11},{10,... | collective-permute-start | bytes 344072 | tf_op jit(solution)/shard_map/ppermute | solution.py:363
  27.9 0.0 copy-start.1
  27.9 1.4 %collective-permute-start.12 = (bf16[64,896]{1,0:T(8,128)(2,1)S(1)}, bf16[64,896]{1,0:T(8,128)(2,1)S(1)}, u32[]{:S(2)}, u32[]{:S(2)}) collective-permute-start(bf16[64,896]{1,0:T(8,128)(2,1)S(1)} %get-tuple-element.31), channel_id=1, source_target_pairs={{0,3},{1,2},{2,1},{3,0},{4,7},{5,6},{6,5},{7,4},{8,11},{9,10},{10,... | collective-permute-start | bytes 344072 | tf_op jit(solution)/shard_map/ppermute | solution.py:363
  29.4 2.2 %collective-permute-done.10.refs_1_ = bf16[64,896]{1,0:T(8,128)(2,1)S(1)} collective-permute-done((bf16[64,896]{1,0:T(8,128)(2,1)S(1)}, bf16[64,896]{1,0:T(8,128)(2,1)S(1)}, u32[]{:S(2)}, u32[]{:S(2)}) %collective-permute-start.10) | collective-permute-done | bytes 114720 | tf_op jit(solution)/shard_map/ppermute | solution.py:363
  31.6 1.0 %collective-permute-done.11.refs_2_ = bf16[64,896]{1,0:T(8,128)(2,1)S(1)} collective-permute-done((bf16[64,896]{1,0:T(8,128)(2,1)S(1)}, bf16[64,896]{1,0:T(8,128)(2,1)S(1)}, u32[]{:S(2)}, u32[]{:S(2)}) %collective-permute-start.11) | collective-permute-done | bytes 114720 | tf_op jit(solution)/shard_map/ppermute | solution.py:363
  32.6 1.5 %collective-permute-done.12.refs_3_ = bf16[64,896]{1,0:T(8,128)(2,1)S(1)} collective-permute-done((bf16[64,896]{1,0:T(8,128)(2,1)S(1)}, bf16[64,896]{1,0:T(8,128)(2,1)S(1)}, u32[]{:S(2)}, u32[]{:S(2)}) %collective-permute-start.12) | collective-permute-done | bytes 114720 | tf_op jit(solution)/shard_map/ppermute | solution.py:363
  34.1 0.0 copy-done.1
  34.1 3.1 %shard_map.79.refs_0_ = bf16[64,640]{1,0:T(8,128)(2,1)S(1)} custom-call(s32[3]{0:T(128)S(1)} %pad_add_fusion.index, s32[2,1,2]{2,1,0:T(1,128)S(1)} %copy-done.1, bf16[64,896]{1,0:T(8,128)(2,1)S(1)} %get-tuple-element.28.refs_0_, bf16[64,896]{1,0:T(8,128)(2,1)S(1)} %collective-permute-done.10.refs_1_, bf16[64,896]{1,0:T(8,128)(2,1)S(1)} %collective-permute-done.11.refs_2_, ...), custom_call_target="tpu_custom_call" | custom-call | tf_op jit(solution)/shard_map/pallas_call | solution.py:333
  37.2 1.5 %collective-permute-start.15 = (bf16[64,640]{1,0:T(8,128)(2,1)S(1)}, bf16[64,640]{1,0:T(8,128)(2,1)S(1)}, u32[]{:S(2)}, u32[]{:S(2)}) collective-permute-start(bf16[64,640]{1,0:T(8,128)(2,1)S(1)} %shard_map.79.refs_0_), channel_id=1, source_target_pairs={{0,3},{1,2},{2,1},{3,0},{4,7},{5,6},{6,5},{7,4},{8,11},{9,10},{10,... | collective-permute-start | bytes 245768 | tf_op jit(solution)/shard_map/ppermute | solution.py:363
  38.7 1.1 %collective-permute-start.14 = (bf16[64,640]{1,0:T(8,128)(2,1)S(1)}, bf16[64,640]{1,0:T(8,128)(2,1)S(1)}, u32[]{:S(2)}, u32[]{:S(2)}) collective-permute-start(bf16[64,640]{1,0:T(8,128)(2,1)S(1)} %shard_map.79.refs_0_), channel_id=1, source_target_pairs={{0,2},{1,3},{2,0},{3,1},{4,6},{5,7},{6,4},{7,5},{8,10},{9,11},{10,... | collective-permute-start | bytes 245768 | tf_op jit(solution)/shard_map/ppermute | solution.py:363
  39.8 1.0 %collective-permute-start.13 = (bf16[64,640]{1,0:T(8,128)(2,1)S(1)}, bf16[64,640]{1,0:T(8,128)(2,1)S(1)}, u32[]{:S(2)}, u32[]{:S(2)}) collective-permute-start(bf16[64,640]{1,0:T(8,128)(2,1)S(1)} %shard_map.79.refs_0_), channel_id=1, source_target_pairs={{0,1},{1,0},{2,3},{3,2},{4,5},{5,4},{6,7},{7,6},{8,9},{9,8},{10,11... | collective-permute-start | bytes 245768 | tf_op jit(solution)/shard_map/ppermute | solution.py:363
  40.7 1.9 %collective-permute-done.15.refs_3_ = bf16[64,640]{1,0:T(8,128)(2,1)S(1)} collective-permute-done((bf16[64,640]{1,0:T(8,128)(2,1)S(1)}, bf16[64,640]{1,0:T(8,128)(2,1)S(1)}, u32[]{:S(2)}, u32[]{:S(2)}) %collective-permute-start.15) | collective-permute-done | bytes 81952 | tf_op jit(solution)/shard_map/ppermute | solution.py:363
  42.6 0.8 %collective-permute-done.14.refs_2_ = bf16[64,640]{1,0:T(8,128)(2,1)S(1)} collective-permute-done((bf16[64,640]{1,0:T(8,128)(2,1)S(1)}, bf16[64,640]{1,0:T(8,128)(2,1)S(1)}, u32[]{:S(2)}, u32[]{:S(2)}) %collective-permute-start.14) | collective-permute-done | bytes 81952 | tf_op jit(solution)/shard_map/ppermute | solution.py:363
  43.5 0.7 %collective-permute-done.13.refs_1_ = bf16[64,640]{1,0:T(8,128)(2,1)S(1)} collective-permute-done((bf16[64,640]{1,0:T(8,128)(2,1)S(1)}, bf16[64,640]{1,0:T(8,128)(2,1)S(1)}, u32[]{:S(2)}, u32[]{:S(2)}) %collective-permute-start.13) | collective-permute-done | bytes 81952 | tf_op jit(solution)/shard_map/ppermute | solution.py:363
  44.2 1.6 %shard_map.80 = (f32[4,256,256]{2,1,0:T(8,128)S(1)}, bf16[4,256,256]{2,1,0:T(8,128)(2,1)S(1)}) custom-call(s32[3]{0:T(128)S(1)} %pad_add_fusion.index, bf16[64,640]{1,0:T(8,128)(2,1)S(1)} %shard_map.79.refs_0_, bf16[64,640]{1,0:T(8,128)(2,1)S(1)} %collective-permute-done.13.refs_1_, bf16[64,640]{1,0:T(8,128)(2,1)S(1)} %collective-permute-done.14.refs_2_, ...), custom_call_target="tpu_custom_call" | custom-call | tf_op jit(solution)/shard_map/pallas_call | solution.py:333
  45.8 0.1 collective-permute-start.16
  45.9 1.9 %collective-permute-done.16.come_ref = bf16[4,256,256]{2,1,0:T(8,128)(2,1)S(1)} collective-permute-done((bf16[4,256,256]{2,1,0:T(8,128)(2,1)S(1)}, bf16[4,256,256]{2,1,0:T(8,128)(2,1)S(1)}, u32[]{:S(2)}, u32[]{:S(2)}) %collective-permute-start.16) | collective-permute-done | bytes 524320 | tf_op jit(solution)/shard_map/ppermute | solution.py:359
  47.8 0.6 shard_map.81
  48.4 3.3 %collective-permute-start.17 = (bf16[256,256]{1,0:T(8,128)(2,1)S(1)}, bf16[256,256]{1,0:T(8,128)(2,1)S(1)}, u32[]{:S(2)}, u32[]{:S(2)}) collective-permute-start(bf16[256,256]{1,0:T(8,128)(2,1)S(1)} %get-tuple-element.39), channel_id=1, source_target_pairs={{0,4},{1,5},{2,6},{3,7},{4,0},{5,1},{6,2},{7,3},{8,12},{9,13},{10,... | collective-permute-start | bytes 393224 | tf_op jit(solution)/shard_map/ppermute | solution.py:356
  51.7 1.1 %collective-permute-start.18 = (bf16[256,256]{1,0:T(8,128)(2,1)S(1)}, bf16[256,256]{1,0:T(8,128)(2,1)S(1)}, u32[]{:S(2)}, u32[]{:S(2)}) collective-permute-start(bf16[256,256]{1,0:T(8,128)(2,1)S(1)} %get-tuple-element.40), channel_id=1, source_target_pairs={{0,8},{1,9},{2,10},{3,11},{4,12},{5,13},{6,14},{7,15},{8,0},{9,1},... | collective-permute-start | bytes 393224 | tf_op jit(solution)/shard_map/ppermute | solution.py:356
  52.8 1.4 %collective-permute-start.19 = (bf16[256,256]{1,0:T(8,128)(2,1)S(1)}, bf16[256,256]{1,0:T(8,128)(2,1)S(1)}, u32[]{:S(2)}, u32[]{:S(2)}) collective-permute-start(bf16[256,256]{1,0:T(8,128)(2,1)S(1)} %get-tuple-element.41), channel_id=1, source_target_pairs={{0,12},{1,13},{2,14},{3,15},{4,8},{5,9},{6,10},{7,11},{8,4},{9,5},... | collective-permute-start | bytes 393224 | tf_op jit(solution)/shard_map/ppermute | solution.py:356
  54.2 3.2 %collective-permute-done.17.refs_0_ = bf16[256,256]{1,0:T(8,128)(2,1)S(1)} collective-permute-done((bf16[256,256]{1,0:T(8,128)(2,1)S(1)}, bf16[256,256]{1,0:T(8,128)(2,1)S(1)}, u32[]{:S(2)}, u32[]{:S(2)}) %collective-permute-start.17) | collective-permute-done | bytes 131104 | tf_op jit(solution)/shard_map/ppermute | solution.py:356
  57.4 7.2 %collective-permute-done.18.refs_1_ = bf16[256,256]{1,0:T(8,128)(2,1)S(1)} collective-permute-done((bf16[256,256]{1,0:T(8,128)(2,1)S(1)}, bf16[256,256]{1,0:T(8,128)(2,1)S(1)}, u32[]{:S(2)}, u32[]{:S(2)}) %collective-permute-start.18) | collective-permute-done | bytes 131104 | tf_op jit(solution)/shard_map/ppermute | solution.py:356
  64.6 0.0 collective-permute-done.19.refs_2_
  64.6 0.7 %shard_map.82 = (f32[192,256]{1,0:T(8,128)}, f32[64,256]{1,0:T(8,128)}) custom-call(f32[256,256]{1,0:T(8,128)S(1)} %get-tuple-element.38.keep_ref, bf16[256,256]{1,0:T(8,128)(2,1)S(1)} %collective-permute-done.17.refs_0_, bf16[256,256]{1,0:T(8,128)(2,1)S(1)} %collective-permute-done.18.refs_1_, bf16[256,256]{1,0:T(8,128)(2,1)S(1)} %collective-permute-done.19.refs_2_), custom_call_target="tpu_custom_call" | custom-call | tf_op jit(solution)/shard_map/pallas_call | solution.py:333
  (1 shorter events, 0.0 us)
Async XLA Ops:
  0.6 0.7 %copy-start = (bf16[1,4096]{1,0:T(2,128)(2,1)S(1)}, bf16[1,4096]{1,0:T(2,128)(2,1)}, u32[]{:S(2)}) copy-start(bf16[1,4096]{1,0:T(2,128)(2,1)} %param.9) | copy-start | bytes 24580
  3.5 7.5 %collective-permute-start.6 = (bf16[272,256]{1,0:T(8,128)(2,1)S(1)}, bf16[272,256]{1,0:T(8,128)(2,1)S(1)}, u32[]{:S(2)}, u32[]{:S(2)}) collective-permute-start(bf16[272,256]{1,0:T(8,128)(2,1)S(1)} %get-tuple-element.27.refs_4_), channel_id=1, source_target_pairs={{0,16},{16,0},{1,17},{17,1},{2,18},{18,2},{3,19},{19,3},{4,20},{20... | collective-permute-start | bytes 417800 | tf_op jit(solution)/shard_map/ppermute | solution.py:359
  4.0 9.3 %collective-permute-start.5 = (bf16[272,256]{1,0:T(8,128)(2,1)S(1)}, bf16[272,256]{1,0:T(8,128)(2,1)S(1)}, u32[]{:S(2)}, u32[]{:S(2)}) collective-permute-start(bf16[272,256]{1,0:T(8,128)(2,1)S(1)} %get-tuple-element.27.refs_4_), channel_id=1, source_target_pairs={{0,12},{1,13},{2,14},{3,15},{4,8},{5,9},{6,10},{7,11},{8,4},{9,5},... | collective-permute-start | bytes 417800 | tf_op jit(solution)/shard_map/ppermute | solution.py:356
  8.7 12.9 %collective-permute-start = (bf16[2,64,1024]{2,1,0:T(8,128)(2,1)S(1)}, bf16[2,64,1024]{2,1,0:T(8,128)(2,1)S(1)}, u32[]{:S(2)}, u32[]{:S(2)}) collective-permute-start(bf16[2,64,1024]{2,1,0:T(8,128)(2,1)S(1)} %get-tuple-element.24), channel_id=1, source_target_pairs={{0,1},{1,0},{2,3},{3,2},{4,5},{5,4},{6,7},{7,6},{8,9},{9,8},{10,11... | collective-permute-start | bytes 786440 | tf_op jit(solution)/shard_map/ppermute | solution.py:363
  10.2 10.9 %collective-permute-start.4 = (bf16[272,256]{1,0:T(8,128)(2,1)S(1)}, bf16[272,256]{1,0:T(8,128)(2,1)S(1)}, u32[]{:S(2)}, u32[]{:S(2)}) collective-permute-start(bf16[272,256]{1,0:T(8,128)(2,1)S(1)} %get-tuple-element.27.refs_4_), channel_id=1, source_target_pairs={{0,8},{1,9},{2,10},{3,11},{4,12},{5,13},{6,14},{7,15},{8,0},{9,1},... | collective-permute-start | bytes 417800 | tf_op jit(solution)/shard_map/ppermute | solution.py:356
  10.2 10.9 %collective-permute-start.3 = (bf16[272,256]{1,0:T(8,128)(2,1)S(1)}, bf16[272,256]{1,0:T(8,128)(2,1)S(1)}, u32[]{:S(2)}, u32[]{:S(2)}) collective-permute-start(bf16[272,256]{1,0:T(8,128)(2,1)S(1)} %get-tuple-element.27.refs_4_), channel_id=1, source_target_pairs={{0,4},{1,5},{2,6},{3,7},{4,0},{5,1},{6,2},{7,3},{8,12},{9,13},{10,... | collective-permute-start | bytes 417800 | tf_op jit(solution)/shard_map/ppermute | solution.py:356
  11.0 13.2 %collective-permute-start.1 = (bf16[2,64,1024]{2,1,0:T(8,128)(2,1)S(1)}, bf16[2,64,1024]{2,1,0:T(8,128)(2,1)S(1)}, u32[]{:S(2)}, u32[]{:S(2)}) collective-permute-start(bf16[2,64,1024]{2,1,0:T(8,128)(2,1)S(1)} %get-tuple-element.25), channel_id=1, source_target_pairs={{0,2},{1,3},{2,0},{3,1},{4,6},{5,7},{6,4},{7,5},{8,10},{9,11},{10,... | collective-permute-start | bytes 786440 | tf_op jit(solution)/shard_map/ppermute | solution.py:363
  13.3 10.9 %collective-permute-start.2 = (bf16[2,64,1024]{2,1,0:T(8,128)(2,1)S(1)}, bf16[2,64,1024]{2,1,0:T(8,128)(2,1)S(1)}, u32[]{:S(2)}, u32[]{:S(2)}) collective-permute-start(bf16[2,64,1024]{2,1,0:T(8,128)(2,1)S(1)} %get-tuple-element.26), channel_id=1, source_target_pairs={{0,3},{1,2},{2,1},{3,0},{4,7},{5,6},{6,5},{7,4},{8,11},{9,10},{10,... | collective-permute-start | bytes 786440 | tf_op jit(solution)/shard_map/ppermute | solution.py:363
  21.1 3.1 %collective-permute-start.9 = (bf16[272,256]{1,0:T(8,128)(2,1)S(1)}, bf16[272,256]{1,0:T(8,128)(2,1)S(1)}, u32[]{:S(2)}, u32[]{:S(2)}) collective-permute-start(bf16[272,256]{1,0:T(8,128)(2,1)S(1)} %collective-permute-done.5.refs_7_), channel_id=1, source_target_pairs={{0,16},{16,0},{1,17},{17,1},{2,18},{18,2},{3,19},{19,3},{4,20},{20... | collective-permute-start | bytes 417800 | tf_op jit(solution)/shard_map/ppermute | solution.py:359
  21.1 3.1 %collective-permute-start.8 = (bf16[272,256]{1,0:T(8,128)(2,1)S(1)}, bf16[272,256]{1,0:T(8,128)(2,1)S(1)}, u32[]{:S(2)}, u32[]{:S(2)}) collective-permute-start(bf16[272,256]{1,0:T(8,128)(2,1)S(1)} %collective-permute-done.4.refs_6_), channel_id=1, source_target_pairs={{0,16},{16,0},{1,17},{17,1},{2,18},{18,2},{3,19},{19,3},{4,20},{20... | collective-permute-start | bytes 417800 | tf_op jit(solution)/shard_map/ppermute | solution.py:359
  21.6 2.6 %collective-permute-start.7 = (bf16[272,256]{1,0:T(8,128)(2,1)S(1)}, bf16[272,256]{1,0:T(8,128)(2,1)S(1)}, u32[]{:S(2)}, u32[]{:S(2)}) collective-permute-start(bf16[272,256]{1,0:T(8,128)(2,1)S(1)} %collective-permute-done.3.refs_5_), channel_id=1, source_target_pairs={{0,16},{16,0},{1,17},{17,1},{2,18},{18,2},{3,19},{19,3},{4,20},{20... | collective-permute-start | bytes 417800 | tf_op jit(solution)/shard_map/ppermute | solution.py:359
  25.8 5.8 %collective-permute-start.10 = (bf16[64,896]{1,0:T(8,128)(2,1)S(1)}, bf16[64,896]{1,0:T(8,128)(2,1)S(1)}, u32[]{:S(2)}, u32[]{:S(2)}) collective-permute-start(bf16[64,896]{1,0:T(8,128)(2,1)S(1)} %get-tuple-element.29), channel_id=1, source_target_pairs={{0,1},{1,0},{2,3},{3,2},{4,5},{5,4},{6,7},{7,6},{8,9},{9,8},{10,11... | collective-permute-start | bytes 344072 | tf_op jit(solution)/shard_map/ppermute | solution.py:363
  26.8 5.8 %collective-permute-start.11 = (bf16[64,896]{1,0:T(8,128)(2,1)S(1)}, bf16[64,896]{1,0:T(8,128)(2,1)S(1)}, u32[]{:S(2)}, u32[]{:S(2)}) collective-permute-start(bf16[64,896]{1,0:T(8,128)(2,1)S(1)} %get-tuple-element.30), channel_id=1, source_target_pairs={{0,2},{1,3},{2,0},{3,1},{4,6},{5,7},{6,4},{7,5},{8,10},{9,11},{10,... | collective-permute-start | bytes 344072 | tf_op jit(solution)/shard_map/ppermute | solution.py:363
  27.9 6.2 %copy-start.1 = (s32[2,1,2]{2,1,0:T(1,128)S(1)}, s32[2,1,2]{2,1,0:T(1,128)}, u32[]{:S(2)}) copy-start(s32[2,1,2]{2,1,0:T(1,128)} %docs.1) | copy-start | bytes 52
  27.9 6.2 %collective-permute-start.12 = (bf16[64,896]{1,0:T(8,128)(2,1)S(1)}, bf16[64,896]{1,0:T(8,128)(2,1)S(1)}, u32[]{:S(2)}, u32[]{:S(2)}) collective-permute-start(bf16[64,896]{1,0:T(8,128)(2,1)S(1)} %get-tuple-element.31), channel_id=1, source_target_pairs={{0,3},{1,2},{2,1},{3,0},{4,7},{5,6},{6,5},{7,4},{8,11},{9,10},{10,... | collective-permute-start | bytes 344072 | tf_op jit(solution)/shard_map/ppermute | solution.py:363
  37.2 5.4 %collective-permute-start.15 = (bf16[64,640]{1,0:T(8,128)(2,1)S(1)}, bf16[64,640]{1,0:T(8,128)(2,1)S(1)}, u32[]{:S(2)}, u32[]{:S(2)}) collective-permute-start(bf16[64,640]{1,0:T(8,128)(2,1)S(1)} %shard_map.79.refs_0_), channel_id=1, source_target_pairs={{0,3},{1,2},{2,1},{3,0},{4,7},{5,6},{6,5},{7,4},{8,11},{9,10},{10,... | collective-permute-start | bytes 245768 | tf_op jit(solution)/shard_map/ppermute | solution.py:363
  38.7 4.8 %collective-permute-start.14 = (bf16[64,640]{1,0:T(8,128)(2,1)S(1)}, bf16[64,640]{1,0:T(8,128)(2,1)S(1)}, u32[]{:S(2)}, u32[]{:S(2)}) collective-permute-start(bf16[64,640]{1,0:T(8,128)(2,1)S(1)} %shard_map.79.refs_0_), channel_id=1, source_target_pairs={{0,2},{1,3},{2,0},{3,1},{4,6},{5,7},{6,4},{7,5},{8,10},{9,11},{10,... | collective-permute-start | bytes 245768 | tf_op jit(solution)/shard_map/ppermute | solution.py:363
  39.8 4.4 %collective-permute-start.13 = (bf16[64,640]{1,0:T(8,128)(2,1)S(1)}, bf16[64,640]{1,0:T(8,128)(2,1)S(1)}, u32[]{:S(2)}, u32[]{:S(2)}) collective-permute-start(bf16[64,640]{1,0:T(8,128)(2,1)S(1)} %shard_map.79.refs_0_), channel_id=1, source_target_pairs={{0,1},{1,0},{2,3},{3,2},{4,5},{5,4},{6,7},{7,6},{8,9},{9,8},{10,11... | collective-permute-start | bytes 245768 | tf_op jit(solution)/shard_map/ppermute | solution.py:363
  45.8 2.0 %collective-permute-start.16 = (bf16[4,256,256]{2,1,0:T(8,128)(2,1)S(1)}, bf16[4,256,256]{2,1,0:T(8,128)(2,1)S(1)}, u32[]{:S(2)}, u32[]{:S(2)}) collective-permute-start(bf16[4,256,256]{2,1,0:T(8,128)(2,1)S(1)} %get-tuple-element.37), channel_id=1, source_target_pairs={{0,16},{16,0},{1,17},{17,1},{2,18},{18,2},{3,19},{19,3},{4,20},{20... | collective-permute-start | bytes 1572872 | tf_op jit(solution)/shard_map/ppermute | solution.py:359
  48.4 9.0 %collective-permute-start.17 = (bf16[256,256]{1,0:T(8,128)(2,1)S(1)}, bf16[256,256]{1,0:T(8,128)(2,1)S(1)}, u32[]{:S(2)}, u32[]{:S(2)}) collective-permute-start(bf16[256,256]{1,0:T(8,128)(2,1)S(1)} %get-tuple-element.39), channel_id=1, source_target_pairs={{0,4},{1,5},{2,6},{3,7},{4,0},{5,1},{6,2},{7,3},{8,12},{9,13},{10,... | collective-permute-start | bytes 393224 | tf_op jit(solution)/shard_map/ppermute | solution.py:356
  51.7 12.9 %collective-permute-start.18 = (bf16[256,256]{1,0:T(8,128)(2,1)S(1)}, bf16[256,256]{1,0:T(8,128)(2,1)S(1)}, u32[]{:S(2)}, u32[]{:S(2)}) collective-permute-start(bf16[256,256]{1,0:T(8,128)(2,1)S(1)} %get-tuple-element.40), channel_id=1, source_target_pairs={{0,8},{1,9},{2,10},{3,11},{4,12},{5,13},{6,14},{7,15},{8,0},{9,1},... | collective-permute-start | bytes 393224 | tf_op jit(solution)/shard_map/ppermute | solution.py:356
  52.8 11.8 %collective-permute-start.19 = (bf16[256,256]{1,0:T(8,128)(2,1)S(1)}, bf16[256,256]{1,0:T(8,128)(2,1)S(1)}, u32[]{:S(2)}, u32[]{:S(2)}) collective-permute-start(bf16[256,256]{1,0:T(8,128)(2,1)S(1)} %get-tuple-element.41), channel_id=1, source_target_pairs={{0,12},{1,13},{2,14},{3,15},{4,8},{5,9},{6,10},{7,11},{8,4},{9,5},... | collective-permute-start | bytes 393224 | tf_op jit(solution)/shard_map/ppermute | solution.py:356

commit v5 on v4

--- a/solution.py
+++ b/solution.py
@@ -153,16 +153,15 @@
 
 
 def project_kernel(planes, heads, index, *refs):
-    blocks, own, other = refs[:PLANE], refs[PLANE : PLANE + planes], refs[PLANE + planes : PLANE + 2 * planes]
-    x_ref, c_ref, vx_ref, gain_ref = refs[PLANE + 2 * planes : PLANE + 2 * planes + 4]
-    out_refs = refs[PLANE + 2 * planes + 4 : -2]
+    blocks, (own, other) = refs[:PLANE], refs[PLANE : PLANE + 2]
+    x_ref, c_ref, vx_ref, gain_ref = refs[PLANE + 2 : PLANE + 6]
+    out_refs = refs[PLANE + 6 : -2]
     vc_ref, sum_ref = refs[-2:]
     qkv, width = 3 * heads, vx_ref.shape[-1]
-    section, z, p = index[0], index[1], index[2]
-    for k in range(planes):
-        at = z ^ k
-        zero = jnp.where(section == 0, own[k][...], other[k][...])
-        one = jnp.where(section == 0, other[k][...], own[k][...])
+    section, p = index[0], index[2]
+    for at in range(planes):
+        zero = jnp.where(section == 0, own[at], other[at])
+        one = jnp.where(section == 0, other[at], own[at])
         gains = [w[qkv + heads :].astype(F32)[0:1] for w in (zero, one)]
         gain_ref[at, 0:1, :] = gains[0]
         gain_ref[at, 1:2, :] = gains[1]
@@ -381,9 +380,10 @@
         scratch_shapes=[pltpu.SemaphoreType.DMA((2 + 2 * PLANE * planes,))],
         compiler_params=pltpu.CompilerParams(vmem_limit_bytes=VMEM_LIMIT),
     )(index, gain, *in_hbm)
-    own = far_first(pack, planes, along_z)
+    in_column = [[a * PLANE + b for a in range(planes)] for b in range(PLANE)]
+    own = lax.all_gather(pack, "dp", axis=0, axis_index_groups=in_column)
     blocks = [blocks[0]] + far_first(blocks, PLANE, along_plane)[1:]
-    other = [to_sibling(piece) for piece in own]
+    other = to_sibling(own)
 
     split = ((PLANE, block, cols), BF16)
     half = 2 * heads
@@ -391,7 +391,7 @@
         functools.partial(project_kernel, planes, heads),
         [split, split, ((planes, 4 * half, width), BF16), ((planes, 8, width), F32)]
         + [((block, 7 * half), BF16)] * PLANE,
-        index, *blocks, *own, *other, scalars=1,
+        index, *blocks, own, other, scalars=1,
         scratch=[((planes, 2 * half, width), BF16), ((rows, 5 * half), BF16)],
     )
     (factors,) = call(

time: 65.6 us -> 76.8 us (1.17)
  blocking collectives: 0 us -> 17.7 us
  starting transfers between devices: 25.1 us -> 15.3 us
  waiting for transfers between devices: 29 us -> 32.5 us
    all_gather x0 -> x1, blocking collectives: none -> 17.7 us  [planar(): own = lax.all_gather(pack, 'dp', axis=0, axis_index_groups=in_column)]
    ppermute x9, waiting for transfers between devices: 10.7 us -> 20.3 us  [along_plane(): return lax.ppermute(value, 'dp', route)]
    ppermute x6 -> x3, starting transfers between devices: 11.2 us -> 4.62 us  [along_z(): return lax.ppermute(value, 'dp', route)]
    ppermute x6 -> x3, waiting for transfers between devices: 16.4 us -> 10.3 us  [along_z(): return lax.ppermute(value, 'dp', route)]
    ppermute x9, starting transfers between devices: 12.7 us -> 10.6 us  [along_plane(): return lax.ppermute(value, 'dp', route)]
    ppermute x5 -> x2, starting transfers between devices: 1.17 us -> 0.07 us  [to_sibling(): return lax.ppermute(value, 'section', [(0, 1), (1, 0)])]
    ppermute x5 -> x2, waiting for transfers between devices: 1.91 us -> 1.9 us  [to_sibling(): return lax.ppermute(value, 'section', [(0, 1), (1, 0)])]
  transfers between devices with their start and end apart: 20 -> 14, of which waited for: 12 -> 10; matrix products, arithmetic and copies ran while one was open for 0% -> 0% of each run, Pallas kernels for 0% -> 0%
where the time goes in v5:
time: 76.8 us; the launch traced here: 76.5 us
  waiting for transfers between devices  32.5 us (42%)
  blocking collectives  17.7 us (23%)
  starting transfers between devices  15.3 us (20%)
  Pallas kernels  9.48 us (12%)
    ppermute x9, waiting for transfers between devices, along_plane(): return lax.ppermute(value, 'dp', route)  20.3 us
    all_gather x1, blocking collectives, planar(): own = lax.all_gather(pack, 'dp', axis=0, axis_index_groups=in_column)  17.7 us
    ppermute x9, starting transfers between devices, along_plane(): return lax.ppermute(value, 'dp', route)  10.6 us
    ppermute x3, waiting for transfers between devices, along_z(): return lax.ppermute(value, 'dp', route)  10.3 us
    pallas_call x5, Pallas kernels, call(): pl.pallas_call(kernel, out_shape=[jax.ShapeDtypeStruct(shape, dtype) for...  7.43 us
    ppermute x3, starting transfers between devices, along_z(): return lax.ppermute(value, 'dp', route)  4.62 us
    pallas_call x1, Pallas kernels, planar(): pl.pallas_call(functools.partial(blocks_kernel, planes), out_shape=[jax.S...  2.05 us
    ppermute x2, waiting for transfers between devices, to_sibling(): return lax.ppermute(value, 'section', [(0, 1), (1, 0)])  1.9 us
  transfers between devices with their start and end apart: 14, of which 10 were waited for; matrix products, arithmetic and copies ran while one was open for 0% of the time, Pallas kernels for 0%

profile of v5, /device:TPU:0, one launch (start us, length us, event | category | flops | bytes accessed | tf_op | source)
XLA Modules:
  0.0 76.5 jit_solution(9172908193562025427)
XLA Ops:
  0.6 0.0 copy-start
  0.7 0.7 copy-done
  1.4 0.1 pad_add_fusion.index
  1.4 2.0 %shard_map.77 = (bf16[272,256]{1,0:T(8,128)(2,1)S(1)}, bf16[2,64,1024]{2,1,0:T(8,128)(2,1)S(1)}, bf16[2,64,1024]{2,1,0:T(8,128)(2,1)S(1)}, bf16[2,64,1024]{2,1,0:T(8,128)(2,1)S(1)}, bf16[2,64,1024]{2,1,0:T(8,128)(2,1)S(1)}) custom-call(s32[3]{0:T(128)S(1)} %pad_add_fusion.index, bf16[1,256]{1,0:T(2,128)(2,1)S(1)} %constant_dynamic-slice_fusion.gain_ref, ...), custom_call_target="tpu_custom_call" | custom-call | tf_op jit(solution)/shard_map/pallas_call | solution.py:374
  3.5 17.7 %all-gather = bf16[1088,256]{1,0:T(8,128)(2,1)S(1)} all-gather(bf16[272,256]{1,0:T(8,128)(2,1)S(1)} %get-tuple-element.27), channel_id=2, replica_groups={{0,4,8,12},{1,5,9,13},{2,6,10,14},{3,7,11,15},{16,20,24,28},{17,21,25,2..., dimensions={0}, use_global_device_ids=true | all-gather | bytes 696320 | tf_op jit(solution)/shard_map/all_gather | solution.py:384
  21.2 0.0 collective-permute-start.3
  21.2 1.5 %collective-permute-start = (bf16[2,64,1024]{2,1,0:T(8,128)(2,1)S(1)}, bf16[2,64,1024]{2,1,0:T(8,128)(2,1)S(1)}, u32[]{:S(2)}, u32[]{:S(2)}) collective-permute-start(bf16[2,64,1024]{2,1,0:T(8,128)(2,1)S(1)} %get-tuple-element.24), channel_id=1, source_target_pairs={{0,1},{1,0},{2,3},{3,2},{4,5},{5,4},{6,7},{7,6},{8,9},{9,8},{10,11... | collective-permute-start | bytes 786440 | tf_op jit(solution)/shard_map/ppermute | solution.py:362
  22.7 1.5 %collective-permute-start.1 = (bf16[2,64,1024]{2,1,0:T(8,128)(2,1)S(1)}, bf16[2,64,1024]{2,1,0:T(8,128)(2,1)S(1)}, u32[]{:S(2)}, u32[]{:S(2)}) collective-permute-start(bf16[2,64,1024]{2,1,0:T(8,128)(2,1)S(1)} %get-tuple-element.25), channel_id=1, source_target_pairs={{0,2},{1,3},{2,0},{3,1},{4,6},{5,7},{6,4},{7,5},{8,10},{9,11},{10,... | collective-permute-start | bytes 786440 | tf_op jit(solution)/shard_map/ppermute | solution.py:362
  24.3 0.5 collective-permute-start.2
  24.7 5.6 %collective-permute-done.refs_1_ = bf16[2,64,1024]{2,1,0:T(8,128)(2,1)S(1)} collective-permute-done((bf16[2,64,1024]{2,1,0:T(8,128)(2,1)S(1)}, bf16[2,64,1024]{2,1,0:T(8,128)(2,1)S(1)}, u32[]{:S(2)}, u32[]{:S(2)}) %collective-permute-start) | collective-permute-done | bytes 262176 | tf_op jit(solution)/shard_map/ppermute | solution.py:362
  30.3 6.4 %collective-permute-done.1.refs_2_ = bf16[2,64,1024]{2,1,0:T(8,128)(2,1)S(1)} collective-permute-done((bf16[2,64,1024]{2,1,0:T(8,128)(2,1)S(1)}, bf16[2,64,1024]{2,1,0:T(8,128)(2,1)S(1)}, u32[]{:S(2)}, u32[]{:S(2)}) %collective-permute-start.1) | collective-permute-done | bytes 262176 | tf_op jit(solution)/shard_map/ppermute | solution.py:362
  36.8 0.0 collective-permute-done.2.refs_3_
  36.8 0.0 collective-permute-done.3.refs_5_
  36.8 1.4 %shard_map.78 = (bf16[4,64,1024]{2,1,0:T(8,128)(2,1)S(1)}, bf16[4,64,1024]{2,1,0:T(8,128)(2,1)S(1)}, bf16[4,512,256]{2,1,0:T(8,128)(2,1)S(1)}, f32[4,8,256]{2,1,...) custom-call(s32[3]{0:T(128)S(1)} %pad_add_fusion.index, ...), custom_call_target="tpu_custom_call" | custom-call | tf_op jit(solution)/shard_map/pallas_call | solution.py:332
  38.2 1.3 %collective-permute-start.4 = (bf16[64,896]{1,0:T(8,128)(2,1)S(1)}, bf16[64,896]{1,0:T(8,128)(2,1)S(1)}, u32[]{:S(2)}, u32[]{:S(2)}) collective-permute-start(bf16[64,896]{1,0:T(8,128)(2,1)S(1)} %get-tuple-element.29), channel_id=1, source_target_pairs={{0,1},{1,0},{2,3},{3,2},{4,5},{5,4},{6,7},{7,6},{8,9},{9,8},{10,11... | collective-permute-start | bytes 344072 | tf_op jit(solution)/shard_map/ppermute | solution.py:362
  39.5 0.8 %collective-permute-start.5 = (bf16[64,896]{1,0:T(8,128)(2,1)S(1)}, bf16[64,896]{1,0:T(8,128)(2,1)S(1)}, u32[]{:S(2)}, u32[]{:S(2)}) collective-permute-start(bf16[64,896]{1,0:T(8,128)(2,1)S(1)} %get-tuple-element.30), channel_id=1, source_target_pairs={{0,2},{1,3},{2,0},{3,1},{4,6},{5,7},{6,4},{7,5},{8,10},{9,11},{10,... | collective-permute-start | bytes 344072 | tf_op jit(solution)/shard_map/ppermute | solution.py:362
  40.3 0.0 copy-start.1
  40.3 1.4 %collective-permute-start.6 = (bf16[64,896]{1,0:T(8,128)(2,1)S(1)}, bf16[64,896]{1,0:T(8,128)(2,1)S(1)}, u32[]{:S(2)}, u32[]{:S(2)}) collective-permute-start(bf16[64,896]{1,0:T(8,128)(2,1)S(1)} %get-tuple-element.31), channel_id=1, source_target_pairs={{0,3},{1,2},{2,1},{3,0},{4,7},{5,6},{6,5},{7,4},{8,11},{9,10},{10,... | collective-permute-start | bytes 344072 | tf_op jit(solution)/shard_map/ppermute | solution.py:362
  41.7 1.6 %collective-permute-done.4.refs_1_ = bf16[64,896]{1,0:T(8,128)(2,1)S(1)} collective-permute-done((bf16[64,896]{1,0:T(8,128)(2,1)S(1)}, bf16[64,896]{1,0:T(8,128)(2,1)S(1)}, u32[]{:S(2)}, u32[]{:S(2)}) %collective-permute-start.4) | collective-permute-done | bytes 114720 | tf_op jit(solution)/shard_map/ppermute | solution.py:362
  43.4 3.1 %collective-permute-done.5.refs_2_ = bf16[64,896]{1,0:T(8,128)(2,1)S(1)} collective-permute-done((bf16[64,896]{1,0:T(8,128)(2,1)S(1)}, bf16[64,896]{1,0:T(8,128)(2,1)S(1)}, u32[]{:S(2)}, u32[]{:S(2)}) %collective-permute-start.5) | collective-permute-done | bytes 114720 | tf_op jit(solution)/shard_map/ppermute | solution.py:362
  46.5 0.0 collective-permute-done.6.refs_3_
  46.5 0.0 copy-done.1
  46.5 3.1 %shard_map.79.refs_0_ = bf16[64,640]{1,0:T(8,128)(2,1)S(1)} custom-call(s32[3]{0:T(128)S(1)} %pad_add_fusion.index, s32[2,1,2]{2,1,0:T(1,128)S(1)} %copy-done.1, bf16[64,896]{1,0:T(8,128)(2,1)S(1)} %get-tuple-element.28.refs_0_, bf16[64,896]{1,0:T(8,128)(2,1)S(1)} %collective-permute-done.4.refs_1_, bf16[64,896]{1,0:T(8,128)(2,1)S(1)} %collective-permute-done.5.refs_2_, ...), custom_call_target="tpu_custom_call" | custom-call | tf_op jit(solution)/shard_map/pallas_call | solution.py:332
  49.6 1.7 %collective-permute-start.9 = (bf16[64,640]{1,0:T(8,128)(2,1)S(1)}, bf16[64,640]{1,0:T(8,128)(2,1)S(1)}, u32[]{:S(2)}, u32[]{:S(2)}) collective-permute-start(bf16[64,640]{1,0:T(8,128)(2,1)S(1)} %shard_map.79.refs_0_), channel_id=1, source_target_pairs={{0,3},{1,2},{2,1},{3,0},{4,7},{5,6},{6,5},{7,4},{8,11},{9,10},{10,... | collective-permute-start | bytes 245768 | tf_op jit(solution)/shard_map/ppermute | solution.py:362
  51.4 0.8 %collective-permute-start.8 = (bf16[64,640]{1,0:T(8,128)(2,1)S(1)}, bf16[64,640]{1,0:T(8,128)(2,1)S(1)}, u32[]{:S(2)}, u32[]{:S(2)}) collective-permute-start(bf16[64,640]{1,0:T(8,128)(2,1)S(1)} %shard_map.79.refs_0_), channel_id=1, source_target_pairs={{0,2},{1,3},{2,0},{3,1},{4,6},{5,7},{6,4},{7,5},{8,10},{9,11},{10,... | collective-permute-start | bytes 245768 | tf_op jit(solution)/shard_map/ppermute | solution.py:362
  52.2 1.0 %collective-permute-start.7 = (bf16[64,640]{1,0:T(8,128)(2,1)S(1)}, bf16[64,640]{1,0:T(8,128)(2,1)S(1)}, u32[]{:S(2)}, u32[]{:S(2)}) collective-permute-start(bf16[64,640]{1,0:T(8,128)(2,1)S(1)} %shard_map.79.refs_0_), channel_id=1, source_target_pairs={{0,1},{1,0},{2,3},{3,2},{4,5},{5,4},{6,7},{7,6},{8,9},{9,8},{10,11... | collective-permute-start | bytes 245768 | tf_op jit(solution)/shard_map/ppermute | solution.py:362
  53.2 1.9 %collective-permute-done.9.refs_3_ = bf16[64,640]{1,0:T(8,128)(2,1)S(1)} collective-permute-done((bf16[64,640]{1,0:T(8,128)(2,1)S(1)}, bf16[64,640]{1,0:T(8,128)(2,1)S(1)}, u32[]{:S(2)}, u32[]{:S(2)}) %collective-permute-start.9) | collective-permute-done | bytes 81952 | tf_op jit(solution)/shard_map/ppermute | solution.py:362
  55.1 0.9 %collective-permute-done.8.refs_2_ = bf16[64,640]{1,0:T(8,128)(2,1)S(1)} collective-permute-done((bf16[64,640]{1,0:T(8,128)(2,1)S(1)}, bf16[64,640]{1,0:T(8,128)(2,1)S(1)}, u32[]{:S(2)}, u32[]{:S(2)}) %collective-permute-start.8) | collective-permute-done | bytes 81952 | tf_op jit(solution)/shard_map/ppermute | solution.py:362
  56.0 0.7 collective-permute-done.7.refs_1_
  56.6 1.6 %shard_map.80 = (f32[4,256,256]{2,1,0:T(8,128)S(1)}, bf16[4,256,256]{2,1,0:T(8,128)(2,1)S(1)}) custom-call(s32[3]{0:T(128)S(1)} %pad_add_fusion.index, bf16[64,640]{1,0:T(8,128)(2,1)S(1)} %shard_map.79.refs_0_, bf16[64,640]{1,0:T(8,128)(2,1)S(1)} %collective-permute-done.7.refs_1_, bf16[64,640]{1,0:T(8,128)(2,1)S(1)} %collective-permute-done.8.refs_2_, ...), custom_call_target="tpu_custom_call" | custom-call | tf_op jit(solution)/shard_map/pallas_call | solution.py:332
  58.2 0.1 collective-permute-start.10
  58.3 1.9 %collective-permute-done.10.come_ref = bf16[4,256,256]{2,1,0:T(8,128)(2,1)S(1)} collective-permute-done((bf16[4,256,256]{2,1,0:T(8,128)(2,1)S(1)}, bf16[4,256,256]{2,1,0:T(8,128)(2,1)S(1)}, u32[]{:S(2)}, u32[]{:S(2)}) %collective-permute-start.10) | collective-permute-done | bytes 524320 | tf_op jit(solution)/shard_map/ppermute | solution.py:358
  60.2 0.6 shard_map.81
  60.8 2.1 %collective-permute-start.11 = (bf16[256,256]{1,0:T(8,128)(2,1)S(1)}, bf16[256,256]{1,0:T(8,128)(2,1)S(1)}, u32[]{:S(2)}, u32[]{:S(2)}) collective-permute-start(bf16[256,256]{1,0:T(8,128)(2,1)S(1)} %get-tuple-element.39), channel_id=1, source_target_pairs={{0,4},{1,5},{2,6},{3,7},{4,0},{5,1},{6,2},{7,3},{8,12},{9,13},{10,... | collective-permute-start | bytes 393224 | tf_op jit(solution)/shard_map/ppermute | solution.py:355
  62.9 2.5 %collective-permute-start.12 = (bf16[256,256]{1,0:T(8,128)(2,1)S(1)}, bf16[256,256]{1,0:T(8,128)(2,1)S(1)}, u32[]{:S(2)}, u32[]{:S(2)}) collective-permute-start(bf16[256,256]{1,0:T(8,128)(2,1)S(1)} %get-tuple-element.40), channel_id=1, source_target_pairs={{0,8},{1,9},{2,10},{3,11},{4,12},{5,13},{6,14},{7,15},{8,0},{9,1},... | collective-permute-start | bytes 393224 | tf_op jit(solution)/shard_map/ppermute | solution.py:355
  65.4 0.0 collective-permute-start.13
  65.4 3.2 %collective-permute-done.11.refs_0_ = bf16[256,256]{1,0:T(8,128)(2,1)S(1)} collective-permute-done((bf16[256,256]{1,0:T(8,128)(2,1)S(1)}, bf16[256,256]{1,0:T(8,128)(2,1)S(1)}, u32[]{:S(2)}, u32[]{:S(2)}) %collective-permute-start.11) | collective-permute-done | bytes 131104 | tf_op jit(solution)/shard_map/ppermute | solution.py:355
  68.6 7.2 %collective-permute-done.12.refs_1_ = bf16[256,256]{1,0:T(8,128)(2,1)S(1)} collective-permute-done((bf16[256,256]{1,0:T(8,128)(2,1)S(1)}, bf16[256,256]{1,0:T(8,128)(2,1)S(1)}, u32[]{:S(2)}, u32[]{:S(2)}) %collective-permute-start.12) | collective-permute-done | bytes 131104 | tf_op jit(solution)/shard_map/ppermute | solution.py:355
  75.8 0.0 collective-permute-done.13.refs_2_
  75.8 0.7 shard_map.82
  (1 shorter events, 0.0 us)
Async XLA Ops:
  0.6 0.7 copy-start
  21.2 15.6 %collective-permute-start.3 = (bf16[4,272,256]{2,1,0:T(8,128)(2,1)S(1)}, bf16[4,272,256]{2,1,0:T(8,128)(2,1)S(1)}, u32[]{:S(2)}, u32[]{:S(2)}) collective-permute-start(bf16[4,272,256]{2,1,0:T(8,128)(2,1)S(1)} %bitcast.12), channel_id=1, source_target_pairs={{0,16},{16,0},{1,17},{17,1},{2,18},{18,2},{3,19},{19,3},{4,20},{20... | collective-permute-start | bytes 1671176 | tf_op jit(solution)/shard_map/ppermute | solution.py:358
  21.2 9.1 %collective-permute-start = (bf16[2,64,1024]{2,1,0:T(8,128)(2,1)S(1)}, bf16[2,64,1024]{2,1,0:T(8,128)(2,1)S(1)}, u32[]{:S(2)}, u32[]{:S(2)}) collective-permute-start(bf16[2,64,1024]{2,1,0:T(8,128)(2,1)S(1)} %get-tuple-element.24), channel_id=1, source_target_pairs={{0,1},{1,0},{2,3},{3,2},{4,5},{5,4},{6,7},{7,6},{8,9},{9,8},{10,11... | collective-permute-start | bytes 786440 | tf_op jit(solution)/shard_map/ppermute | solution.py:362
  22.7 14.1 %collective-permute-start.1 = (bf16[2,64,1024]{2,1,0:T(8,128)(2,1)S(1)}, bf16[2,64,1024]{2,1,0:T(8,128)(2,1)S(1)}, u32[]{:S(2)}, u32[]{:S(2)}) collective-permute-start(bf16[2,64,1024]{2,1,0:T(8,128)(2,1)S(1)} %get-tuple-element.25), channel_id=1, source_target_pairs={{0,2},{1,3},{2,0},{3,1},{4,6},{5,7},{6,4},{7,5},{8,10},{9,11},{10,... | collective-permute-start | bytes 786440 | tf_op jit(solution)/shard_map/ppermute | solution.py:362
  24.3 12.5 %collective-permute-start.2 = (bf16[2,64,1024]{2,1,0:T(8,128)(2,1)S(1)}, bf16[2,64,1024]{2,1,0:T(8,128)(2,1)S(1)}, u32[]{:S(2)}, u32[]{:S(2)}) collective-permute-start(bf16[2,64,1024]{2,1,0:T(8,128)(2,1)S(1)} %get-tuple-element.26), channel_id=1, source_target_pairs={{0,3},{1,2},{2,1},{3,0},{4,7},{5,6},{6,5},{7,4},{8,11},{9,10},{10,... | collective-permute-start | bytes 786440 | tf_op jit(solution)/shard_map/ppermute | solution.py:362
  38.2 5.2 %collective-permute-start.4 = (bf16[64,896]{1,0:T(8,128)(2,1)S(1)}, bf16[64,896]{1,0:T(8,128)(2,1)S(1)}, u32[]{:S(2)}, u32[]{:S(2)}) collective-permute-start(bf16[64,896]{1,0:T(8,128)(2,1)S(1)} %get-tuple-element.29), channel_id=1, source_target_pairs={{0,1},{1,0},{2,3},{3,2},{4,5},{5,4},{6,7},{7,6},{8,9},{9,8},{10,11... | collective-permute-start | bytes 344072 | tf_op jit(solution)/shard_map/ppermute | solution.py:362
  39.5 7.0 %collective-permute-start.5 = (bf16[64,896]{1,0:T(8,128)(2,1)S(1)}, bf16[64,896]{1,0:T(8,128)(2,1)S(1)}, u32[]{:S(2)}, u32[]{:S(2)}) collective-permute-start(bf16[64,896]{1,0:T(8,128)(2,1)S(1)} %get-tuple-element.30), channel_id=1, source_target_pairs={{0,2},{1,3},{2,0},{3,1},{4,6},{5,7},{6,4},{7,5},{8,10},{9,11},{10,... | collective-permute-start | bytes 344072 | tf_op jit(solution)/shard_map/ppermute | solution.py:362
  40.3 6.2 %copy-start.1 = (s32[2,1,2]{2,1,0:T(1,128)S(1)}, s32[2,1,2]{2,1,0:T(1,128)}, u32[]{:S(2)}) copy-start(s32[2,1,2]{2,1,0:T(1,128)} %docs.1) | copy-start | bytes 52
  40.3 6.2 %collective-permute-start.6 = (bf16[64,896]{1,0:T(8,128)(2,1)S(1)}, bf16[64,896]{1,0:T(8,128)(2,1)S(1)}, u32[]{:S(2)}, u32[]{:S(2)}) collective-permute-start(bf16[64,896]{1,0:T(8,128)(2,1)S(1)} %get-tuple-element.31), channel_id=1, source_target_pairs={{0,3},{1,2},{2,1},{3,0},{4,7},{5,6},{6,5},{7,4},{8,11},{9,10},{10,... | collective-permute-start | bytes 344072 | tf_op jit(solution)/shard_map/ppermute | solution.py:362
  49.6 5.5 %collective-permute-start.9 = (bf16[64,640]{1,0:T(8,128)(2,1)S(1)}, bf16[64,640]{1,0:T(8,128)(2,1)S(1)}, u32[]{:S(2)}, u32[]{:S(2)}) collective-permute-start(bf16[64,640]{1,0:T(8,128)(2,1)S(1)} %shard_map.79.refs_0_), channel_id=1, source_target_pairs={{0,3},{1,2},{2,1},{3,0},{4,7},{5,6},{6,5},{7,4},{8,11},{9,10},{10,... | collective-permute-start | bytes 245768 | tf_op jit(solution)/shard_map/ppermute | solution.py:362
  51.4 4.6 %collective-permute-start.8 = (bf16[64,640]{1,0:T(8,128)(2,1)S(1)}, bf16[64,640]{1,0:T(8,128)(2,1)S(1)}, u32[]{:S(2)}, u32[]{:S(2)}) collective-permute-start(bf16[64,640]{1,0:T(8,128)(2,1)S(1)} %shard_map.79.refs_0_), channel_id=1, source_target_pairs={{0,2},{1,3},{2,0},{3,1},{4,6},{5,7},{6,4},{7,5},{8,10},{9,11},{10,... | collective-permute-start | bytes 245768 | tf_op jit(solution)/shard_map/ppermute | solution.py:362
  52.2 4.4 %collective-permute-start.7 = (bf16[64,640]{1,0:T(8,128)(2,1)S(1)}, bf16[64,640]{1,0:T(8,128)(2,1)S(1)}, u32[]{:S(2)}, u32[]{:S(2)}) collective-permute-start(bf16[64,640]{1,0:T(8,128)(2,1)S(1)} %shard_map.79.refs_0_), channel_id=1, source_target_pairs={{0,1},{1,0},{2,3},{3,2},{4,5},{5,4},{6,7},{7,6},{8,9},{9,8},{10,11... | collective-permute-start | bytes 245768 | tf_op jit(solution)/shard_map/ppermute | solution.py:362
  58.2 2.0 %collective-permute-start.10 = (bf16[4,256,256]{2,1,0:T(8,128)(2,1)S(1)}, bf16[4,256,256]{2,1,0:T(8,128)(2,1)S(1)}, u32[]{:S(2)}, u32[]{:S(2)}) collective-permute-start(bf16[4,256,256]{2,1,0:T(8,128)(2,1)S(1)} %get-tuple-element.37), channel_id=1, source_target_pairs={{0,16},{16,0},{1,17},{17,1},{2,18},{18,2},{3,19},{19,3},{4,20},{20... | collective-permute-start | bytes 1572872 | tf_op jit(solution)/shard_map/ppermute | solution.py:358
  60.8 7.8 %collective-permute-start.11 = (bf16[256,256]{1,0:T(8,128)(2,1)S(1)}, bf16[256,256]{1,0:T(8,128)(2,1)S(1)}, u32[]{:S(2)}, u32[]{:S(2)}) collective-permute-start(bf16[256,256]{1,0:T(8,128)(2,1)S(1)} %get-tuple-element.39), channel_id=1, source_target_pairs={{0,4},{1,5},{2,6},{3,7},{4,0},{5,1},{6,2},{7,3},{8,12},{9,13},{10,... | collective-permute-start | bytes 393224 | tf_op jit(solution)/shard_map/ppermute | solution.py:355
  62.9 12.9 %collective-permute-start.12 = (bf16[256,256]{1,0:T(8,128)(2,1)S(1)}, bf16[256,256]{1,0:T(8,128)(2,1)S(1)}, u32[]{:S(2)}, u32[]{:S(2)}) collective-permute-start(bf16[256,256]{1,0:T(8,128)(2,1)S(1)} %get-tuple-element.40), channel_id=1, source_target_pairs={{0,8},{1,9},{2,10},{3,11},{4,12},{5,13},{6,14},{7,15},{8,0},{9,1},... | collective-permute-start | bytes 393224 | tf_op jit(solution)/shard_map/ppermute | solution.py:355
  65.4 10.4 %collective-permute-start.13 = (bf16[256,256]{1,0:T(8,128)(2,1)S(1)}, bf16[256,256]{1,0:T(8,128)(2,1)S(1)}, u32[]{:S(2)}, u32[]{:S(2)}) collective-permute-start(bf16[256,256]{1,0:T(8,128)(2,1)S(1)} %get-tuple-element.41), channel_id=1, source_target_pairs={{0,12},{1,13},{2,14},{3,15},{4,8},{5,9},{6,10},{7,11},{8,4},{9,5},... | collective-permute-start | bytes 393224 | tf_op jit(solution)/shard_map/ppermute | solution.py:355

commit v6 on v4

--- a/solution.py
+++ b/solution.py
@@ -125,15 +125,27 @@
     return lax.dot_general(a, b, (((1,), (1,)), ((), ())), preferred_element_type=F32)
 
 
-def blocks_kernel(planes, index, gain_ref, qkv_ref, wout_ref, x_ref, c_ref, pack_ref, *refs):
+def pack_kernel(index, gain_ref, qkv_ref, wout_ref, pack_ref, row_ref, sems):
+    qkv_rows, heads, width = qkv_ref.shape[0], wout_ref.shape[0], qkv_ref.shape[1]
+    at = pl.multiple_of((index[1] * PLANE + index[2]) * width, width)
+    copies = [
+        pltpu.make_async_copy(gain_ref.at[:, pl.ds(at, width)], row_ref, sems.at[0]),
+        pltpu.make_async_copy(qkv_ref, pack_ref.at[:qkv_rows], sems.at[1]),
+        pltpu.make_async_copy(wout_ref, pack_ref.at[qkv_rows : qkv_rows + heads], sems.at[2]),
+    ]
+    for copy in copies:
+        copy.start()
+    copies[0].wait()
+    pack_ref[qkv_rows + heads :, :] = jnp.broadcast_to(row_ref[...].astype(F32), (STATS, width)).astype(BF16)
+    copies[1].wait()
+    copies[2].wait()
+
+
+def blocks_kernel(planes, index, x_ref, c_ref, *refs):
     out_refs, sems = refs[:PLANE], refs[PLANE]
-    qkv_rows, heads = qkv_ref.shape[0], wout_ref.shape[0]
     width = x_ref.shape[-1] // (planes * PLANE)
     section, p = index[0], index[2]
-    copies = [
-        pltpu.make_async_copy(qkv_ref, pack_ref.at[:qkv_rows], sems.at[0]),
-        pltpu.make_async_copy(wout_ref, pack_ref.at[qkv_rows : qkv_rows + heads], sems.at[1]),
-    ]
+    copies = []
     for k in range(PLANE):
         for z in range(planes):
             at = pl.multiple_of((z * PLANE + (p ^ k)) * width, width)
@@ -147,7 +159,6 @@
                 )
     for copy in copies:
         copy.start()
-    pack_ref[qkv_rows + heads :, :] = jnp.broadcast_to(gain_ref[...].astype(F32), (STATS, width)).astype(BF16)
     for copy in copies:
         copy.wait()
 
@@ -176,8 +187,8 @@
         vc_ref[at, 2 * heads : 3 * heads, :] = zero[qkv : qkv + heads]
         vc_ref[at, 3 * heads :, :] = empty
     for k in range(PLANE):
-        x_ref[p ^ k] = blocks[k][0]
-        c_ref[p ^ k] = blocks[k][1]
+        x_ref[p ^ k] = blocks[-k][0]
+        c_ref[p ^ k] = blocks[-k][1]
     rows = x_ref.shape[0] * x_ref.shape[1]
     with_x = with_c = squares = products = None
     for z in range(planes):
@@ -365,24 +376,34 @@
     def exchange(value):
         return far_first(value, PLANE, along_plane)
 
-    gain = lax.dynamic_slice(norm_gain, (0, place * width), (1, width))
     smem, vmem = pl.BlockSpec(memory_space=pltpu.SMEM), pl.BlockSpec(memory_space=pltpu.VMEM)
     hbm = pl.BlockSpec(memory_space=pltpu.HBM)
-    in_hbm = [
+    params = pltpu.CompilerParams(vmem_limit_bytes=VMEM_LIMIT)
+    gain, qkv_in, out_in, x_in, c_in = [
         pltpu.with_memory_space_constraint(value, pltpu.HBM)
-        for value in (w_qkv[0].T, w_out[0], inputs, cotangent)
+        for value in (norm_gain, w_qkv[0].T, w_out[0], inputs, cotangent)
     ]
-    pack, *blocks = pl.pallas_call(
+    pack = pl.pallas_call(
+        pack_kernel,
+        out_shape=jax.ShapeDtypeStruct((qkv_rows + heads + STATS, width), BF16),
+        in_specs=[smem] + [hbm] * 3,
+        out_specs=vmem,
+        scratch_shapes=[pltpu.VMEM((1, width), BF16), pltpu.SemaphoreType.DMA((3,))],
+        compiler_params=params,
+    )(index, gain, qkv_in, out_in)
+    blocks = pl.pallas_call(
         functools.partial(blocks_kernel, planes),
-        out_shape=[jax.ShapeDtypeStruct((qkv_rows + heads + STATS, width), BF16)]
-        + [jax.ShapeDtypeStruct((2, block, cols), BF16)] * PLANE,
-        in_specs=[smem, vmem] + [hbm] * 4,
-        out_specs=[vmem] * (1 + PLANE),
-        scratch_shapes=[pltpu.SemaphoreType.DMA((2 + 2 * PLANE * planes,))],
-        compiler_params=pltpu.CompilerParams(vmem_limit_bytes=VMEM_LIMIT),
-    )(index, gain, *in_hbm)
-    own = far_first(pack, planes, along_z)
+        out_shape=[jax.ShapeDtypeStruct((2, block, cols), BF16)] * PLANE,
+        in_specs=[smem] + [hbm] * 2,
+        out_specs=[vmem] * PLANE,
+        scratch_shapes=[pltpu.SemaphoreType.DMA((2 * PLANE * planes,))],
+        compiler_params=params,
+    )(index, x_in, c_in)
     blocks = [blocks[0]] + far_first(blocks, PLANE, along_plane)[1:]
+    far = {k: along_z(pack, k) for k in reversed(range(2, planes))}
+    later, _ = lax.optimization_barrier((pack, far[planes - 1] if far else pack))
+    near = [along_z(later, 1)] if planes > 1 else []
+    own = [later] + near + [far[k] for k in range(2, planes)]
     other = [to_sibling(piece) for piece in own]
 
     split = ((PLANE, block, cols), BF16)
@@ -391,13 +412,13 @@
         functools.partial(project_kernel, planes, heads),
         [split, split, ((planes, 4 * half, width), BF16), ((planes, 8, width), F32)]
         + [((block, 7 * half), BF16)] * PLANE,
-        index, *blocks, *own, *other, scalars=1,
+        index, blocks[0], *blocks[:0:-1], *own, *other, scalars=1,
         scratch=[((planes, 2 * half, width), BF16), ((rows, 5 * half), BF16)],
     )
     (factors,) = call(
         functools.partial(chain_kernel, features, heads),
         [((block, 5 * half), BF16)],
-        index, doc_lengths, *exchange(sent), scalars=2,
+        index, doc_lengths, *exchange(sent)[::-1], scalars=2,
     )
     grads = (planes, qkv_rows + heads, width)
     keep, send = call(
@@ -415,7 +436,7 @@
     grad_qkv, grad_out = call(
         functools.partial(last_kernel, qkv_rows),
         [((qkv_rows, width), F32), ((heads, width), F32)],
-        merged[0], *parts,
+        merged[0], *parts[::-1],
     )
     return (grad_qkv.T[None], grad_out[None])
 

time: 65.6 us -> 64.5 us (0.983)
  waiting for transfers between devices: 29 us -> 26 us
  Pallas kernels: 9.72 us -> 11.1 us
  starting transfers between devices: 25.1 us -> 26.2 us
  local copies, waits for them, and re-layouts: 0.7 us -> 0.01 us
    ppermute x6, waiting for transfers between devices: 16.4 us -> 10.6 us  [along_z(): return lax.ppermute(value, 'dp', route)]
    ppermute x9, waiting for transfers between devices: 10.7 us -> 12.5 us  [along_plane(): return lax.ppermute(value, 'dp', route)]
    ppermute x9, starting transfers between devices: 12.7 us -> 14.2 us  [along_plane(): return lax.ppermute(value, 'dp', route)]
    pallas_call x0 -> x1, Pallas kernels: none -> 1.48 us  [planar(): pl.pallas_call(pack_kernel, out_shape=jax.ShapeDtypeStruct((qkv_rows + he...]
    ppermute x5, waiting for transfers between devices: 1.91 us -> 2.93 us  [to_sibling(): return lax.ppermute(value, 'section', [(0, 1), (1, 0)])]
    unnamed x4 -> x2, local copies, waits for them, and re-layouts: 0.7 us -> 0.01 us
  transfers between devices with their start and end apart: 20 -> 20, of which waited for: 12 -> 13; matrix products, arithmetic and copies ran while one was open for 0% -> 0% of each run, Pallas kernels for 0% -> 3%
where the time goes in v6:
time: 64.5 us; the launch traced here: 64.2 us
  starting transfers between devices  26.2 us (41%)
  waiting for transfers between devices  26 us (40%)
  Pallas kernels  11.1 us (17%)
  between operations  0.73 us (1%)
    ppermute x9, starting transfers between devices, along_plane(): return lax.ppermute(value, 'dp', route)  14.2 us
    ppermute x9, waiting for transfers between devices, along_plane(): return lax.ppermute(value, 'dp', route)  12.5 us
    ppermute x6, starting transfers between devices, along_z(): return lax.ppermute(value, 'dp', route)  10.9 us
    ppermute x6, waiting for transfers between devices, along_z(): return lax.ppermute(value, 'dp', route)  10.6 us
    pallas_call x5, Pallas kernels, call(): pl.pallas_call(kernel, out_shape=[jax.ShapeDtypeStruct(shape, dtype) for...  7.65 us
    ppermute x5, waiting for transfers between devices, to_sibling(): return lax.ppermute(value, 'section', [(0, 1), (1, 0)])  2.93 us
    pallas_call x1, Pallas kernels, planar(): pl.pallas_call(functools.partial(blocks_kernel, planes), out_shape=[jax.S...  2.01 us
    pallas_call x1, Pallas kernels, planar(): pl.pallas_call(pack_kernel, out_shape=jax.ShapeDtypeStruct((qkv_rows + he...  1.48 us
  transfers between devices with their start and end apart: 20, of which 13 were waited for; matrix products, arithmetic and copies ran while one was open for 0% of the time, Pallas kernels for 3%

profile of v6, /device:TPU:0, one launch (start us, length us, event | category | flops | bytes accessed | tf_op | source)
XLA Modules:
  0.0 64.2 jit_solution(6006674982742069468)
XLA Ops:
  0.6 0.1 pad_add_fusion.index
  0.7 1.5 %shard_map.78.refs_4_ = bf16[272,256]{1,0:T(8,128)(2,1)S(1)} custom-call(s32[3]{0:T(128)S(1)} %pad_add_fusion.index, bf16[1,4096]{1,0:T(2,128)(2,1)} %gain_ref.1, bf16[192,256]{1,0:T(8,128)(2,1)} %bitcast.11, bf16[64,256]{1,0:T(8,128)(2,1)} %bitcast.12), custom_call_target="tpu_custom_call" | custom-call | tf_op jit(solution)/shard_map/pallas_call | solution.py:386
  2.2 5.1 %collective-permute-start.3 = (bf16[272,256]{1,0:T(8,128)(2,1)S(1)}, bf16[272,256]{1,0:T(8,128)(2,1)S(1)}, u32[]{:S(2)}, u32[]{:S(2)}) collective-permute-start(bf16[272,256]{1,0:T(8,128)(2,1)S(1)} %shard_map.78.refs_4_), channel_id=1, source_target_pairs={{0,12},{1,13},{2,14},{3,15},{4,8},{5,9},{6,10},{7,11},{8,4},{9,5},... | collective-permute-start | bytes 417800 | tf_op jit(solution)/shard_map/ppermute | solution.py:367
  7.3 2.0 %shard_map.77 = (bf16[2,64,1024]{2,1,0:T(8,128)(2,1)S(1)}, bf16[2,64,1024]{2,1,0:T(8,128)(2,1)S(1)}, bf16[2,64,1024]{2,1,0:T(8,128)(2,1)S(1)}, bf16[2,64,1024]{2,1,0:T(8,128)(2,1)S(1)}) custom-call(s32[3]{0:T(128)S(1)} %pad_add_fusion.index, bf16[2,64,4096]{2,1,0:T(8,128)(2,1)} %x_ref.1, bf16[2,64,4096]{2,1,0:T(8,128)(2,1)} %c_ref.1), custom_call_target="tpu_custom_call" | custom-call | tf_op jit(solution)/shard_map/pallas_call | solution.py:394
  9.3 2.5 %collective-permute-start = (bf16[2,64,1024]{2,1,0:T(8,128)(2,1)S(1)}, bf16[2,64,1024]{2,1,0:T(8,128)(2,1)S(1)}, u32[]{:S(2)}, u32[]{:S(2)}) collective-permute-start(bf16[2,64,1024]{2,1,0:T(8,128)(2,1)S(1)} %get-tuple-element.24), channel_id=1, source_target_pairs={{0,3},{1,2},{2,1},{3,0},{4,7},{5,6},{6,5},{7,4},{8,11},{9,10},{10,... | collective-permute-start | bytes 786440 | tf_op jit(solution)/shard_map/ppermute | solution.py:374
  11.9 0.5 collective-permute-start.1
  12.4 0.0 collective-permute-start.5
  12.4 0.0 collective-permute-done.3.refs_7_
  12.4 1.3 %collective-permute-start.4 = (bf16[272,256]{1,0:T(8,128)(2,1)S(1)}, bf16[272,256]{1,0:T(8,128)(2,1)S(1)}, u32[]{:S(2)}, u32[]{:S(2)}) collective-permute-start(bf16[272,256]{1,0:T(8,128)(2,1)S(1)} %shard_map.78.refs_4_), channel_id=1, source_target_pairs={{0,4},{1,5},{2,6},{3,7},{4,0},{5,1},{6,2},{7,3},{8,12},{9,13},{10,... | collective-permute-start | bytes 417800 | tf_op jit(solution)/shard_map/ppermute | solution.py:367
  13.7 4.1 %collective-permute-start.2 = (bf16[2,64,1024]{2,1,0:T(8,128)(2,1)S(1)}, bf16[2,64,1024]{2,1,0:T(8,128)(2,1)S(1)}, u32[]{:S(2)}, u32[]{:S(2)}) collective-permute-start(bf16[2,64,1024]{2,1,0:T(8,128)(2,1)S(1)} %get-tuple-element.26), channel_id=1, source_target_pairs={{0,1},{1,0},{2,3},{3,2},{4,5},{5,4},{6,7},{7,6},{8,9},{9,8},{10,11... | collective-permute-start | bytes 786440 | tf_op jit(solution)/shard_map/ppermute | solution.py:374
  17.8 2.0 %collective-permute-done.5.refs_6_ = bf16[272,256]{1,0:T(8,128)(2,1)S(1)} collective-permute-done((bf16[272,256]{1,0:T(8,128)(2,1)S(1)}, bf16[272,256]{1,0:T(8,128)(2,1)S(1)}, u32[]{:S(2)}, u32[]{:S(2)}) %collective-permute-start.5) | collective-permute-done | bytes 139296 | tf_op jit(solution)/shard_map/ppermute | solution.py:367
  19.9 0.0 collective-permute-start.6
  19.9 0.0 collective-permute-done.refs_1_
  19.9 0.5 collective-permute-start.8
  20.4 3.3 %collective-permute-done.1.refs_2_ = bf16[2,64,1024]{2,1,0:T(8,128)(2,1)S(1)} collective-permute-done((bf16[2,64,1024]{2,1,0:T(8,128)(2,1)S(1)}, bf16[2,64,1024]{2,1,0:T(8,128)(2,1)S(1)}, u32[]{:S(2)}, u32[]{:S(2)}) %collective-permute-start.1) | collective-permute-done | bytes 262176 | tf_op jit(solution)/shard_map/ppermute | solution.py:374
  23.7 0.0 collective-permute-start.9
  23.7 0.0 collective-permute-done.4.refs_5_
  23.7 0.5 collective-permute-start.7
  24.2 0.0 collective-permute-done.2.refs_3_
  24.2 0.0 collective-permute-done.8.refs_10_
  24.2 0.0 collective-permute-done.6.refs_8_
  24.2 0.8 %collective-permute-done.9.refs_11_ = bf16[272,256]{1,0:T(8,128)(2,1)S(1)} collective-permute-done((bf16[272,256]{1,0:T(8,128)(2,1)S(1)}, bf16[272,256]{1,0:T(8,128)(2,1)S(1)}, u32[]{:S(2)}, u32[]{:S(2)}) %collective-permute-start.9) | collective-permute-done | bytes 139296 | tf_op jit(solution)/shard_map/ppermute | solution.py:370
  25.1 0.2 collective-permute-done.7.refs_9_
  25.3 1.6 %shard_map.79 = (bf16[4,64,1024]{2,1,0:T(8,128)(2,1)S(1)}, bf16[4,64,1024]{2,1,0:T(8,128)(2,1)S(1)}, bf16[4,512,256]{2,1,0:T(8,128)(2,1)S(1)}, f32[4,8,256]{2,1,...) custom-call(s32[3]{0:T(128)S(1)} %pad_add_fusion.index, ...), custom_call_target="tpu_custom_call" | custom-call | tf_op jit(solution)/shard_map/pallas_call | solution.py:344
  26.8 1.8 %collective-permute-start.10 = (bf16[64,896]{1,0:T(8,128)(2,1)S(1)}, bf16[64,896]{1,0:T(8,128)(2,1)S(1)}, u32[]{:S(2)}, u32[]{:S(2)}) collective-permute-start(bf16[64,896]{1,0:T(8,128)(2,1)S(1)} %get-tuple-element.28), channel_id=1, source_target_pairs={{0,3},{1,2},{2,1},{3,0},{4,7},{5,6},{6,5},{7,4},{8,11},{9,10},{10,... | collective-permute-start | bytes 344072 | tf_op jit(solution)/shard_map/ppermute | solution.py:374
  28.7 1.2 %collective-permute-start.11 = (bf16[64,896]{1,0:T(8,128)(2,1)S(1)}, bf16[64,896]{1,0:T(8,128)(2,1)S(1)}, u32[]{:S(2)}, u32[]{:S(2)}) collective-permute-start(bf16[64,896]{1,0:T(8,128)(2,1)S(1)} %get-tuple-element.29), channel_id=1, source_target_pairs={{0,2},{1,3},{2,0},{3,1},{4,6},{5,7},{6,4},{7,5},{8,10},{9,11},{10,... | collective-permute-start | bytes 344072 | tf_op jit(solution)/shard_map/ppermute | solution.py:374
  29.9 0.0 copy-start
  29.9 0.5 collective-permute-start.12
  30.4 3.4 %collective-permute-done.10.refs_0_ = bf16[64,896]{1,0:T(8,128)(2,1)S(1)} collective-permute-done((bf16[64,896]{1,0:T(8,128)(2,1)S(1)}, bf16[64,896]{1,0:T(8,128)(2,1)S(1)}, u32[]{:S(2)}, u32[]{:S(2)}) %collective-permute-start.10) | collective-permute-done | bytes 114720 | tf_op jit(solution)/shard_map/ppermute | solution.py:374
  33.8 1.9 %collective-permute-done.11.refs_1_ = bf16[64,896]{1,0:T(8,128)(2,1)S(1)} collective-permute-done((bf16[64,896]{1,0:T(8,128)(2,1)S(1)}, bf16[64,896]{1,0:T(8,128)(2,1)S(1)}, u32[]{:S(2)}, u32[]{:S(2)}) %collective-permute-start.11) | collective-permute-done | bytes 114720 | tf_op jit(solution)/shard_map/ppermute | solution.py:374
  35.6 0.1 collective-permute-done.12.refs_2_
  35.7 0.0 copy-done
  35.7 3.1 %shard_map.80.refs_0_ = bf16[64,640]{1,0:T(8,128)(2,1)S(1)} custom-call(s32[3]{0:T(128)S(1)} %pad_add_fusion.index, s32[2,1,2]{2,1,0:T(1,128)S(1)} %copy-done, bf16[64,896]{1,0:T(8,128)(2,1)S(1)} %collective-permute-done.10.refs_0_, bf16[64,896]{1,0:T(8,128)(2,1)S(1)} %collective-permute-done.11.refs_1_, ...), custom_call_target="tpu_custom_call" | custom-call | tf_op jit(solution)/shard_map/pallas_call | solution.py:344
  38.8 1.7 %collective-permute-start.15 = (bf16[64,640]{1,0:T(8,128)(2,1)S(1)}, bf16[64,640]{1,0:T(8,128)(2,1)S(1)}, u32[]{:S(2)}, u32[]{:S(2)}) collective-permute-start(bf16[64,640]{1,0:T(8,128)(2,1)S(1)} %shard_map.80.refs_0_), channel_id=1, source_target_pairs={{0,3},{1,2},{2,1},{3,0},{4,7},{5,6},{6,5},{7,4},{8,11},{9,10},{10,... | collective-permute-start | bytes 245768 | tf_op jit(solution)/shard_map/ppermute | solution.py:374
  40.6 1.2 %collective-permute-start.14 = (bf16[64,640]{1,0:T(8,128)(2,1)S(1)}, bf16[64,640]{1,0:T(8,128)(2,1)S(1)}, u32[]{:S(2)}, u32[]{:S(2)}) collective-permute-start(bf16[64,640]{1,0:T(8,128)(2,1)S(1)} %shard_map.80.refs_0_), channel_id=1, source_target_pairs={{0,2},{1,3},{2,0},{3,1},{4,6},{5,7},{6,4},{7,5},{8,10},{9,11},{10,... | collective-permute-start | bytes 245768 | tf_op jit(solution)/shard_map/ppermute | solution.py:374
  41.8 0.6 collective-permute-start.13
  42.4 2.0 %collective-permute-done.15.refs_3_ = bf16[64,640]{1,0:T(8,128)(2,1)S(1)} collective-permute-done((bf16[64,640]{1,0:T(8,128)(2,1)S(1)}, bf16[64,640]{1,0:T(8,128)(2,1)S(1)}, u32[]{:S(2)}, u32[]{:S(2)}) %collective-permute-start.15) | collective-permute-done | bytes 81952 | tf_op jit(solution)/shard_map/ppermute | solution.py:374
  44.4 1.4 %collective-permute-done.14.refs_2_ = bf16[64,640]{1,0:T(8,128)(2,1)S(1)} collective-permute-done((bf16[64,640]{1,0:T(8,128)(2,1)S(1)}, bf16[64,640]{1,0:T(8,128)(2,1)S(1)}, u32[]{:S(2)}, u32[]{:S(2)}) %collective-permute-start.14) | collective-permute-done | bytes 81952 | tf_op jit(solution)/shard_map/ppermute | solution.py:374
  45.9 0.4 collective-permute-done.13.refs_1_
  46.2 1.6 %shard_map.81 = (f32[4,256,256]{2,1,0:T(8,128)S(1)}, bf16[4,256,256]{2,1,0:T(8,128)(2,1)S(1)}) custom-call(s32[3]{0:T(128)S(1)} %pad_add_fusion.index, bf16[64,640]{1,0:T(8,128)(2,1)S(1)} %shard_map.80.refs_0_, bf16[64,640]{1,0:T(8,128)(2,1)S(1)} %collective-permute-done.13.refs_1_, bf16[64,640]{1,0:T(8,128)(2,1)S(1)} %collective-permute-done.14.refs_2_, ...), custom_call_target="tpu_custom_call" | custom-call | tf_op jit(solution)/shard_map/pallas_call | solution.py:344
  47.8 0.1 collective-permute-start.16
  47.9 1.9 %collective-permute-done.16.come_ref = bf16[4,256,256]{2,1,0:T(8,128)(2,1)S(1)} collective-permute-done((bf16[4,256,256]{2,1,0:T(8,128)(2,1)S(1)}, bf16[4,256,256]{2,1,0:T(8,128)(2,1)S(1)}, u32[]{:S(2)}, u32[]{:S(2)}) %collective-permute-start.16) | collective-permute-done | bytes 524320 | tf_op jit(solution)/shard_map/ppermute | solution.py:370
  49.8 0.6 shard_map.82
  50.4 0.4 collective-permute-start.17
  50.8 0.7 %collective-permute-start.18 = (bf16[256,256]{1,0:T(8,128)(2,1)S(1)}, bf16[256,256]{1,0:T(8,128)(2,1)S(1)}, u32[]{:S(2)}, u32[]{:S(2)}) collective-permute-start(bf16[256,256]{1,0:T(8,128)(2,1)S(1)} %get-tuple-element.40), channel_id=1, source_target_pairs={{0,8},{1,9},{2,10},{3,11},{4,12},{5,13},{6,14},{7,15},{8,0},{9,1},... | collective-permute-start | bytes 393224 | tf_op jit(solution)/shard_map/ppermute | solution.py:367
  51.5 3.4 %collective-permute-start.19 = (bf16[256,256]{1,0:T(8,128)(2,1)S(1)}, bf16[256,256]{1,0:T(8,128)(2,1)S(1)}, u32[]{:S(2)}, u32[]{:S(2)}) collective-permute-start(bf16[256,256]{1,0:T(8,128)(2,1)S(1)} %get-tuple-element.41), channel_id=1, source_target_pairs={{0,4},{1,5},{2,6},{3,7},{4,0},{5,1},{6,2},{7,3},{8,12},{9,13},{10,... | collective-permute-start | bytes 393224 | tf_op jit(solution)/shard_map/ppermute | solution.py:367
  54.9 3.9 %collective-permute-done.17.refs_0_ = bf16[256,256]{1,0:T(8,128)(2,1)S(1)} collective-permute-done((bf16[256,256]{1,0:T(8,128)(2,1)S(1)}, bf16[256,256]{1,0:T(8,128)(2,1)S(1)}, u32[]{:S(2)}, u32[]{:S(2)}) %collective-permute-start.17) | collective-permute-done | bytes 131104 | tf_op jit(solution)/shard_map/ppermute | solution.py:367
  58.8 4.7 %collective-permute-done.18.refs_1_ = bf16[256,256]{1,0:T(8,128)(2,1)S(1)} collective-permute-done((bf16[256,256]{1,0:T(8,128)(2,1)S(1)}, bf16[256,256]{1,0:T(8,128)(2,1)S(1)}, u32[]{:S(2)}, u32[]{:S(2)}) %collective-permute-start.18) | collective-permute-done | bytes 131104 | tf_op jit(solution)/shard_map/ppermute | solution.py:367
  63.5 0.0 collective-permute-done.19.refs_2_
  63.5 0.7 %shard_map.83 = (f32[192,256]{1,0:T(8,128)}, f32[64,256]{1,0:T(8,128)}) custom-call(f32[256,256]{1,0:T(8,128)S(1)} %get-tuple-element.38.keep_ref, bf16[256,256]{1,0:T(8,128)(2,1)S(1)} %collective-permute-done.17.refs_0_, bf16[256,256]{1,0:T(8,128)(2,1)S(1)} %collective-permute-done.18.refs_1_, bf16[256,256]{1,0:T(8,128)(2,1)S(1)} %collective-permute-done.19.refs_2_), custom_call_target="tpu_custom_call" | custom-call | tf_op jit(solution)/shard_map/pallas_call | solution.py:344
Async XLA Ops:
  2.2 10.2 %collective-permute-start.3 = (bf16[272,256]{1,0:T(8,128)(2,1)S(1)}, bf16[272,256]{1,0:T(8,128)(2,1)S(1)}, u32[]{:S(2)}, u32[]{:S(2)}) collective-permute-start(bf16[272,256]{1,0:T(8,128)(2,1)S(1)} %shard_map.78.refs_4_), channel_id=1, source_target_pairs={{0,12},{1,13},{2,14},{3,15},{4,8},{5,9},{6,10},{7,11},{8,4},{9,5},... | collective-permute-start | bytes 417800 | tf_op jit(solution)/shard_map/ppermute | solution.py:367
  9.3 10.5 %collective-permute-start = (bf16[2,64,1024]{2,1,0:T(8,128)(2,1)S(1)}, bf16[2,64,1024]{2,1,0:T(8,128)(2,1)S(1)}, u32[]{:S(2)}, u32[]{:S(2)}) collective-permute-start(bf16[2,64,1024]{2,1,0:T(8,128)(2,1)S(1)} %get-tuple-element.24), channel_id=1, source_target_pairs={{0,3},{1,2},{2,1},{3,0},{4,7},{5,6},{6,5},{7,4},{8,11},{9,10},{10,... | collective-permute-start | bytes 786440 | tf_op jit(solution)/shard_map/ppermute | solution.py:374
  11.9 11.8 %collective-permute-start.1 = (bf16[2,64,1024]{2,1,0:T(8,128)(2,1)S(1)}, bf16[2,64,1024]{2,1,0:T(8,128)(2,1)S(1)}, u32[]{:S(2)}, u32[]{:S(2)}) collective-permute-start(bf16[2,64,1024]{2,1,0:T(8,128)(2,1)S(1)} %get-tuple-element.25), channel_id=1, source_target_pairs={{0,2},{1,3},{2,0},{3,1},{4,6},{5,7},{6,4},{7,5},{8,10},{9,11},{10,... | collective-permute-start | bytes 786440 | tf_op jit(solution)/shard_map/ppermute | solution.py:374
  12.4 7.5 %collective-permute-start.5 = (bf16[272,256]{1,0:T(8,128)(2,1)S(1)}, bf16[272,256]{1,0:T(8,128)(2,1)S(1)}, u32[]{:S(2)}, u32[]{:S(2)}) collective-permute-start(bf16[272,256]{1,0:T(8,128)(2,1)S(1)} %shard_map.78.refs_4_), channel_id=1, source_target_pairs={{0,8},{1,9},{2,10},{3,11},{4,12},{5,13},{6,14},{7,15},{8,0},{9,1},... | collective-permute-start | bytes 417800 | tf_op jit(solution)/shard_map/ppermute | solution.py:367
  12.4 11.3 %collective-permute-start.4 = (bf16[272,256]{1,0:T(8,128)(2,1)S(1)}, bf16[272,256]{1,0:T(8,128)(2,1)S(1)}, u32[]{:S(2)}, u32[]{:S(2)}) collective-permute-start(bf16[272,256]{1,0:T(8,128)(2,1)S(1)} %shard_map.78.refs_4_), channel_id=1, source_target_pairs={{0,4},{1,5},{2,6},{3,7},{4,0},{5,1},{6,2},{7,3},{8,12},{9,13},{10,... | collective-permute-start | bytes 417800 | tf_op jit(solution)/shard_map/ppermute | solution.py:367
  13.7 10.5 %collective-permute-start.2 = (bf16[2,64,1024]{2,1,0:T(8,128)(2,1)S(1)}, bf16[2,64,1024]{2,1,0:T(8,128)(2,1)S(1)}, u32[]{:S(2)}, u32[]{:S(2)}) collective-permute-start(bf16[2,64,1024]{2,1,0:T(8,128)(2,1)S(1)} %get-tuple-element.26), channel_id=1, source_target_pairs={{0,1},{1,0},{2,3},{3,2},{4,5},{5,4},{6,7},{7,6},{8,9},{9,8},{10,11... | collective-permute-start | bytes 786440 | tf_op jit(solution)/shard_map/ppermute | solution.py:374
  19.9 4.4 %collective-permute-start.6 = (bf16[272,256]{1,0:T(8,128)(2,1)S(1)}, bf16[272,256]{1,0:T(8,128)(2,1)S(1)}, u32[]{:S(2)}, u32[]{:S(2)}) collective-permute-start(bf16[272,256]{1,0:T(8,128)(2,1)S(1)} %shard_map.78.refs_4_), channel_id=1, source_target_pairs={{0,16},{16,0},{1,17},{17,1},{2,18},{18,2},{3,19},{19,3},{4,20},{20... | collective-permute-start | bytes 417800 | tf_op jit(solution)/shard_map/ppermute | solution.py:370
  19.9 4.3 %collective-permute-start.8 = (bf16[272,256]{1,0:T(8,128)(2,1)S(1)}, bf16[272,256]{1,0:T(8,128)(2,1)S(1)}, u32[]{:S(2)}, u32[]{:S(2)}) collective-permute-start(bf16[272,256]{1,0:T(8,128)(2,1)S(1)} %collective-permute-done.5.refs_6_), channel_id=1, source_target_pairs={{0,16},{16,0},{1,17},{17,1},{2,18},{18,2},{3,19},{19,3},{4,20},{20... | collective-permute-start | bytes 417800 | tf_op jit(solution)/shard_map/ppermute | solution.py:370
  23.7 1.4 %collective-permute-start.9 = (bf16[272,256]{1,0:T(8,128)(2,1)S(1)}, bf16[272,256]{1,0:T(8,128)(2,1)S(1)}, u32[]{:S(2)}, u32[]{:S(2)}) collective-permute-start(bf16[272,256]{1,0:T(8,128)(2,1)S(1)} %collective-permute-done.3.refs_7_), channel_id=1, source_target_pairs={{0,16},{16,0},{1,17},{17,1},{2,18},{18,2},{3,19},{19,3},{4,20},{20... | collective-permute-start | bytes 417800 | tf_op jit(solution)/shard_map/ppermute | solution.py:370
  23.7 1.5 %collective-permute-start.7 = (bf16[272,256]{1,0:T(8,128)(2,1)S(1)}, bf16[272,256]{1,0:T(8,128)(2,1)S(1)}, u32[]{:S(2)}, u32[]{:S(2)}) collective-permute-start(bf16[272,256]{1,0:T(8,128)(2,1)S(1)} %collective-permute-done.4.refs_5_), channel_id=1, source_target_pairs={{0,16},{16,0},{1,17},{17,1},{2,18},{18,2},{3,19},{19,3},{4,20},{20... | collective-permute-start | bytes 417800 | tf_op jit(solution)/shard_map/ppermute | solution.py:370
  26.8 6.9 %collective-permute-start.10 = (bf16[64,896]{1,0:T(8,128)(2,1)S(1)}, bf16[64,896]{1,0:T(8,128)(2,1)S(1)}, u32[]{:S(2)}, u32[]{:S(2)}) collective-permute-start(bf16[64,896]{1,0:T(8,128)(2,1)S(1)} %get-tuple-element.28), channel_id=1, source_target_pairs={{0,3},{1,2},{2,1},{3,0},{4,7},{5,6},{6,5},{7,4},{8,11},{9,10},{10,... | collective-permute-start | bytes 344072 | tf_op jit(solution)/shard_map/ppermute | solution.py:374
  28.7 7.0 %collective-permute-start.11 = (bf16[64,896]{1,0:T(8,128)(2,1)S(1)}, bf16[64,896]{1,0:T(8,128)(2,1)S(1)}, u32[]{:S(2)}, u32[]{:S(2)}) collective-permute-start(bf16[64,896]{1,0:T(8,128)(2,1)S(1)} %get-tuple-element.29), channel_id=1, source_target_pairs={{0,2},{1,3},{2,0},{3,1},{4,6},{5,7},{6,4},{7,5},{8,10},{9,11},{10,... | collective-permute-start | bytes 344072 | tf_op jit(solution)/shard_map/ppermute | solution.py:374
  29.9 5.8 %copy-start = (s32[2,1,2]{2,1,0:T(1,128)S(1)}, s32[2,1,2]{2,1,0:T(1,128)}, u32[]{:S(2)}) copy-start(s32[2,1,2]{2,1,0:T(1,128)} %docs.1) | copy-start | bytes 52
  29.9 5.8 %collective-permute-start.12 = (bf16[64,896]{1,0:T(8,128)(2,1)S(1)}, bf16[64,896]{1,0:T(8,128)(2,1)S(1)}, u32[]{:S(2)}, u32[]{:S(2)}) collective-permute-start(bf16[64,896]{1,0:T(8,128)(2,1)S(1)} %get-tuple-element.30), channel_id=1, source_target_pairs={{0,1},{1,0},{2,3},{3,2},{4,5},{5,4},{6,7},{7,6},{8,9},{9,8},{10,11... | collective-permute-start | bytes 344072 | tf_op jit(solution)/shard_map/ppermute | solution.py:374
  38.8 5.6 %collective-permute-start.15 = (bf16[64,640]{1,0:T(8,128)(2,1)S(1)}, bf16[64,640]{1,0:T(8,128)(2,1)S(1)}, u32[]{:S(2)}, u32[]{:S(2)}) collective-permute-start(bf16[64,640]{1,0:T(8,128)(2,1)S(1)} %shard_map.80.refs_0_), channel_id=1, source_target_pairs={{0,3},{1,2},{2,1},{3,0},{4,7},{5,6},{6,5},{7,4},{8,11},{9,10},{10,... | collective-permute-start | bytes 245768 | tf_op jit(solution)/shard_map/ppermute | solution.py:374
  40.6 5.3 %collective-permute-start.14 = (bf16[64,640]{1,0:T(8,128)(2,1)S(1)}, bf16[64,640]{1,0:T(8,128)(2,1)S(1)}, u32[]{:S(2)}, u32[]{:S(2)}) collective-permute-start(bf16[64,640]{1,0:T(8,128)(2,1)S(1)} %shard_map.80.refs_0_), channel_id=1, source_target_pairs={{0,2},{1,3},{2,0},{3,1},{4,6},{5,7},{6,4},{7,5},{8,10},{9,11},{10,... | collective-permute-start | bytes 245768 | tf_op jit(solution)/shard_map/ppermute | solution.py:374
  41.8 4.4 %collective-permute-start.13 = (bf16[64,640]{1,0:T(8,128)(2,1)S(1)}, bf16[64,640]{1,0:T(8,128)(2,1)S(1)}, u32[]{:S(2)}, u32[]{:S(2)}) collective-permute-start(bf16[64,640]{1,0:T(8,128)(2,1)S(1)} %shard_map.80.refs_0_), channel_id=1, source_target_pairs={{0,1},{1,0},{2,3},{3,2},{4,5},{5,4},{6,7},{7,6},{8,9},{9,8},{10,11... | collective-permute-start | bytes 245768 | tf_op jit(solution)/shard_map/ppermute | solution.py:374
  47.8 2.0 %collective-permute-start.16 = (bf16[4,256,256]{2,1,0:T(8,128)(2,1)S(1)}, bf16[4,256,256]{2,1,0:T(8,128)(2,1)S(1)}, u32[]{:S(2)}, u32[]{:S(2)}) collective-permute-start(bf16[4,256,256]{2,1,0:T(8,128)(2,1)S(1)} %get-tuple-element.37), channel_id=1, source_target_pairs={{0,16},{16,0},{1,17},{17,1},{2,18},{18,2},{3,19},{19,3},{4,20},{20... | collective-permute-start | bytes 1572872 | tf_op jit(solution)/shard_map/ppermute | solution.py:370
  50.4 8.3 %collective-permute-start.17 = (bf16[256,256]{1,0:T(8,128)(2,1)S(1)}, bf16[256,256]{1,0:T(8,128)(2,1)S(1)}, u32[]{:S(2)}, u32[]{:S(2)}) collective-permute-start(bf16[256,256]{1,0:T(8,128)(2,1)S(1)} %get-tuple-element.39), channel_id=1, source_target_pairs={{0,12},{1,13},{2,14},{3,15},{4,8},{5,9},{6,10},{7,11},{8,4},{9,5},... | collective-permute-start | bytes 393224 | tf_op jit(solution)/shard_map/ppermute | solution.py:367
  50.8 12.7 %collective-permute-start.18 = (bf16[256,256]{1,0:T(8,128)(2,1)S(1)}, bf16[256,256]{1,0:T(8,128)(2,1)S(1)}, u32[]{:S(2)}, u32[]{:S(2)}) collective-permute-start(bf16[256,256]{1,0:T(8,128)(2,1)S(1)} %get-tuple-element.40), channel_id=1, source_target_pairs={{0,8},{1,9},{2,10},{3,11},{4,12},{5,13},{6,14},{7,15},{8,0},{9,1},... | collective-permute-start | bytes 393224 | tf_op jit(solution)/shard_map/ppermute | solution.py:367
  51.5 12.0 %collective-permute-start.19 = (bf16[256,256]{1,0:T(8,128)(2,1)S(1)}, bf16[256,256]{1,0:T(8,128)(2,1)S(1)}, u32[]{:S(2)}, u32[]{:S(2)}) collective-permute-start(bf16[256,256]{1,0:T(8,128)(2,1)S(1)} %get-tuple-element.41), channel_id=1, source_target_pairs={{0,4},{1,5},{2,6},{3,7},{4,0},{5,1},{6,2},{7,3},{8,12},{9,13},{10,... | collective-permute-start | bytes 393224 | tf_op jit(solution)/shard_map/ppermute | solution.py:367

commit v7 on v6

--- a/solution.py
+++ b/solution.py
@@ -10,6 +10,7 @@
 F32 = jnp.float32
 BF16 = jnp.bfloat16
 PLANE = 4
+NEAR = 2
 STATS = 16
 VMEM_LIMIT = 16 * 1024 * 1024
 
@@ -165,13 +166,13 @@
 
 def project_kernel(planes, heads, index, *refs):
     blocks, own, other = refs[:PLANE], refs[PLANE : PLANE + planes], refs[PLANE + planes : PLANE + 2 * planes]
-    x_ref, c_ref, vx_ref, gain_ref = refs[PLANE + 2 * planes : PLANE + 2 * planes + 4]
-    out_refs = refs[PLANE + 2 * planes + 4 : -2]
-    vc_ref, sum_ref = refs[-2:]
+    vx_ref, gain_ref, mine_ref, near_ref = refs[PLANE + 2 * planes : PLANE + 2 * planes + 4]
+    out_refs = refs[PLANE + 2 * planes + 4 : -4]
+    x_ref, c_ref, vc_ref, sum_ref = refs[-4:]
     qkv, width = 3 * heads, vx_ref.shape[-1]
-    section, z, p = index[0], index[1], index[2]
+    section, place, p = index[0], index[1], index[2]
     for k in range(planes):
-        at = z ^ k
+        at = place ^ k
         zero = jnp.where(section == 0, own[k][...], other[k][...])
         one = jnp.where(section == 0, other[k][...], own[k][...])
         gains = [w[qkv + heads :].astype(F32)[0:1] for w in (zero, one)]
@@ -216,6 +217,11 @@
         start = pl.multiple_of((p ^ k) * block, block)
         out_refs[k][:, : 5 * half] = sum_ref[pl.ds(start, block), :]
         out_refs[k][:, 5 * half :] = products.astype(BF16)
+    for h in range(planes // NEAR):
+        for to_ref, low in ((mine_ref, place & (NEAR - 1)), (near_ref, (place ^ 1) & (NEAR - 1))):
+            cols = pl.ds(pl.multiple_of((h * NEAR + low) * width, width), width)
+            to_ref[0, h] = x_ref[:, :, cols].reshape(rows, width)
+            to_ref[1, h] = c_ref[:, :, cols].reshape(rows, width)
 
 
 def exact(a, b, dims):
@@ -287,37 +293,39 @@
 
 
 def grads_kernel(planes, heads, index, *refs):
-    factors, (x_ref, c_ref, vx_ref, gain_ref) = refs[:PLANE], refs[PLANE : PLANE + 4]
-    keep_ref, send_ref, all_ref = refs[PLANE + 4 :]
-    qkv, half, width = 3 * heads, 2 * heads, vx_ref.shape[-1]
-    section, p = index[0], index[2]
-    for k in range(PLANE):
-        all_ref[p ^ k] = factors[k][...]
-    rows = x_ref.shape[0] * x_ref.shape[1]
-    turned = jnp.transpose(all_ref[...].astype(F32).reshape(rows, 5 * half)).astype(BF16)
+    groups = refs[:PLANE], refs[PLANE : NEAR * PLANE]
+    wide_refs, (vx_ref, gain_ref) = refs[NEAR * PLANE : NEAR * PLANE + NEAR], refs[NEAR * (PLANE + 1) : -3]
+    keep_ref, send_ref, all_ref = refs[-3:]
+    qkv, half = 3 * heads, 2 * heads
+    section, z, p = index[0], index[1], index[2]
+    for g, group in enumerate(groups):
+        for k in range(PLANE):
+            all_ref[g, p ^ k] = group[k][...]
+    rows = wide_refs[0].shape[2]
+    turned = jnp.transpose(all_ref[...].astype(F32).reshape(NEAR * rows, 5 * half)).astype(BF16)
     att0, att1 = turned[qkv : qkv + heads], turned[4 * half : 4 * half + heads]
     right = turned[2 * half : 4 * half]
     small = nt(right, att0).astype(BF16)
     small_t = nt(att0, right[:qkv]).astype(BF16)
-    for z in range(planes):
-        cols = slice(z * width, (z + 1) * width)
-        x = x_ref[:, :, cols].reshape(rows, width)
-        c = c_ref[:, :, cols].reshape(rows, width)
-        out = vx_ref[z, qkv : qkv + heads, :]
+    for h in range(planes // NEAR):
+        at = h * NEAR + (z & (NEAR - 1))
+        x = jnp.concatenate([ref[0, h] for ref in wide_refs], axis=0)
+        c = jnp.concatenate([ref[1, h] for ref in wide_refs], axis=0)
+        out = vx_ref[at, qkv : qkv + heads, :]
         with_x = nn(turned[: 4 * half], x)
         left = with_x[2 * half :] + nn(small, out)
-        zero = with_x[:qkv] * gain_ref[z, 0:1, :]
-        one = left[:qkv] * gain_ref[z, 1:2, :]
-        keep_ref[z, :qkv, :] = jnp.where(section == 0, zero, one)
-        send_ref[z, :qkv, :] = jnp.where(section == 0, one, zero).astype(BF16)
-        zero = nn(att0, c) + nn(small_t, vx_ref[z, qkv + heads : 2 * qkv + heads, :]) - left[qkv:]
+        zero = with_x[:qkv] * gain_ref[at, 0:1, :]
+        one = left[:qkv] * gain_ref[at, 1:2, :]
+        keep_ref[h, :qkv, :] = jnp.where(section == 0, zero, one)
+        send_ref[h, :qkv, :] = jnp.where(section == 0, one, zero).astype(BF16)
+        zero = nn(att0, c) + nn(small_t, vx_ref[at, qkv + heads : 2 * qkv + heads, :]) - left[qkv:]
         one = nn(att1, c)
-        keep_ref[z, qkv:, :] = jnp.where(section == 0, zero, one)
-        send_ref[z, qkv:, :] = jnp.where(section == 0, one, zero).astype(BF16)
+        keep_ref[h, qkv:, :] = jnp.where(section == 0, zero, one)
+        send_ref[h, qkv:, :] = jnp.where(section == 0, one, zero).astype(BF16)
 
 
 def merge_kernel(index, keep_ref, come_ref, *out_refs):
-    place = index[1]
+    place = index[1] >> (NEAR.bit_length() - 1)
     out_refs[0][...] = keep_ref[place] + come_ref[place].astype(F32)
     for k in range(1, len(out_refs)):
         out_refs[k][...] = (keep_ref[place ^ k] + come_ref[place ^ k].astype(F32)).astype(BF16)
@@ -369,8 +377,8 @@
     def to_sibling(value):
         return lax.ppermute(value, "section", [(0, 1), (1, 0)])
 
-    def along_plane(value, k):
-        route = [(a * PLANE + b, a * PLANE + (b ^ k)) for a in range(planes) for b in range(PLANE)]
+    def along_plane(value, k, up=0):
+        route = [(a * PLANE + b, (a ^ up) * PLANE + (b ^ k)) for a in range(planes) for b in range(PLANE)]
         return lax.ppermute(value, "dp", route)
 
     def exchange(value):
@@ -407,36 +415,39 @@
     other = [to_sibling(piece) for piece in own]
 
     split = ((PLANE, block, cols), BF16)
-    half = 2 * heads
-    x, c, vx, gains, *sent = call(
+    half, highs = 2 * heads, planes // NEAR
+    columns = ((2, highs, rows, width), BF16)
+    vx, gains, mine, near, *sent = call(
         functools.partial(project_kernel, planes, heads),
-        [split, split, ((planes, 4 * half, width), BF16), ((planes, 8, width), F32)]
+        [((planes, 4 * half, width), BF16), ((planes, 8, width), F32), columns, columns]
         + [((block, 7 * half), BF16)] * PLANE,
         index, blocks[0], *blocks[:0:-1], *own, *other, scalars=1,
-        scratch=[((planes, 2 * half, width), BF16), ((rows, 5 * half), BF16)],
+        scratch=[split, split, ((planes, 2 * half, width), BF16), ((rows, 5 * half), BF16)],
     )
     (factors,) = call(
         functools.partial(chain_kernel, features, heads),
         [((block, 5 * half), BF16)],
         index, doc_lengths, *exchange(sent)[::-1], scalars=2,
     )
-    grads = (planes, qkv_rows + heads, width)
+    near = along_z(near, 1)
+    gathered = [along_plane(factors, k, up) for up in range(NEAR) for k in range(PLANE) if up or k]
+    grads = (highs, qkv_rows + heads, width)
     keep, send = call(
         functools.partial(grads_kernel, planes, heads),
         [(grads, F32), (grads, BF16)],
-        index, *exchange(factors), x, c, vx, gains, scalars=1,
-        scratch=[((PLANE, block, 5 * half), BF16)],
+        index, factors, *gathered, mine, near, vx, gains, scalars=1,
+        scratch=[((NEAR, PLANE, block, 5 * half), BF16)],
     )
     merged = call(
         merge_kernel,
-        [(grads[1:], F32)] + [(grads[1:], BF16)] * (planes - 1),
+        [(grads[1:], F32)] + [(grads[1:], BF16)] * (highs - 1),
         index, keep, to_sibling(send), scalars=1,
     )
-    parts = far_first(merged, planes, along_z)[1:]
+    parts = [along_z(merged[k], k * NEAR) for k in range(1, highs)]
     grad_qkv, grad_out = call(
         functools.partial(last_kernel, qkv_rows),
         [((qkv_rows, width), F32), ((heads, width), F32)],
-        merged[0], *parts[::-1],
+        merged[0], *parts,
     )
     return (grad_qkv.T[None], grad_out[None])
 
@@ -446,7 +457,7 @@
     planes = shards // PLANE
 
     def body(inputs, *rest):
-        fits = shards % PLANE == 0 and planes & (planes - 1) == 0
+        fits = shards % (PLANE * NEAR) == 0 and planes & (planes - 1) == 0
         if sections == 2 and inputs.shape[0] == 2 and fits:
             return planar(inputs, *rest)
         return pipelined(inputs, *rest)

time: 64.5 us -> 68.3 us (1.059)
  starting transfers between devices: 26.2 us -> 28.5 us
  waiting for transfers between devices: 26 us -> 27.4 us
    ppermute x9 -> x13, starting transfers between devices: 14.2 us -> 20.8 us  [along_plane(): return lax.ppermute(value, 'dp', route)]
    ppermute x6 -> x5, starting transfers between devices: 10.9 us -> 6.59 us  [along_z(): return lax.ppermute(value, 'dp', route)]
    ppermute x9 -> x13, waiting for transfers between devices: 12.5 us -> 13.6 us  [along_plane(): return lax.ppermute(value, 'dp', route)]
    ppermute x6 -> x5, waiting for transfers between devices: 10.6 us -> 11.3 us  [along_z(): return lax.ppermute(value, 'dp', route)]
  transfers between devices with their start and end apart: 20 -> 23, of which waited for: 13 -> 15; matrix products, arithmetic and copies ran while one was open for 0% -> 0% of each run, Pallas kernels for 3% -> 8%
where the time goes in v7:
time: 68.3 us; the launch traced here: 68 us
  starting transfers between devices  28.5 us (42%)
  waiting for transfers between devices  27.4 us (40%)
  Pallas kernels  11.3 us (17%)
  between operations  0.75 us (1%)
    ppermute x13, starting transfers between devices, along_plane(): return lax.ppermute(value, 'dp', route)  20.8 us
    ppermute x13, waiting for transfers between devices, along_plane(): return lax.ppermute(value, 'dp', route)  13.6 us
    ppermute x5, waiting for transfers between devices, along_z(): return lax.ppermute(value, 'dp', route)  11.3 us
    pallas_call x5, Pallas kernels, call(): pl.pallas_call(kernel, out_shape=[jax.ShapeDtypeStruct(shape, dtype) for...  7.79 us
    ppermute x5, starting transfers between devices, along_z(): return lax.ppermute(value, 'dp', route)  6.59 us
    ppermute x5, waiting for transfers between devices, to_sibling(): return lax.ppermute(value, 'section', [(0, 1), (1, 0)])  2.56 us
    pallas_call x1, Pallas kernels, planar(): pl.pallas_call(functools.partial(blocks_kernel, planes), out_shape=[jax.S...  2.01 us
    pallas_call x1, Pallas kernels, planar(): pl.pallas_call(pack_kernel, out_shape=jax.ShapeDtypeStruct((qkv_rows + he...  1.48 us
  transfers between devices with their start and end apart: 23, of which 15 were waited for; matrix products, arithmetic and copies ran while one was open for 0% of the time, Pallas kernels for 8%

profile of v7, /device:TPU:0, one launch (start us, length us, event | category | flops | bytes accessed | tf_op | source)
XLA Modules:
  0.0 68.0 jit_solution(8242683652459646340)
XLA Ops:
  0.6 0.1 pad_add_fusion.index
  0.7 1.5 %shard_map.78.refs_4_ = bf16[272,256]{1,0:T(8,128)(2,1)S(1)} custom-call(s32[3]{0:T(128)S(1)} %pad_add_fusion.index, bf16[1,4096]{1,0:T(2,128)(2,1)} %gain_ref.1, bf16[192,256]{1,0:T(8,128)(2,1)} %bitcast.11, bf16[64,256]{1,0:T(8,128)(2,1)} %bitcast.12), custom_call_target="tpu_custom_call" | custom-call | tf_op jit(solution)/shard_map/pallas_call | solution.py:394
  2.2 5.1 %collective-permute-start.3 = (bf16[272,256]{1,0:T(8,128)(2,1)S(1)}, bf16[272,256]{1,0:T(8,128)(2,1)S(1)}, u32[]{:S(2)}, u32[]{:S(2)}) collective-permute-start(bf16[272,256]{1,0:T(8,128)(2,1)S(1)} %shard_map.78.refs_4_), channel_id=1, source_target_pairs={{0,12},{1,13},{2,14},{3,15},{4,8},{5,9},{6,10},{7,11},{8,4},{9,5},... | collective-permute-start | bytes 417800 | tf_op jit(solution)/shard_map/ppermute | solution.py:375
  7.3 2.0 %shard_map.77 = (bf16[2,64,1024]{2,1,0:T(8,128)(2,1)S(1)}, bf16[2,64,1024]{2,1,0:T(8,128)(2,1)S(1)}, bf16[2,64,1024]{2,1,0:T(8,128)(2,1)S(1)}, bf16[2,64,1024]{2,1,0:T(8,128)(2,1)S(1)}) custom-call(s32[3]{0:T(128)S(1)} %pad_add_fusion.index, bf16[2,64,4096]{2,1,0:T(8,128)(2,1)} %x_ref.1, bf16[2,64,4096]{2,1,0:T(8,128)(2,1)} %c_ref.1), custom_call_target="tpu_custom_call" | custom-call | tf_op jit(solution)/shard_map/pallas_call | solution.py:402
  9.3 2.5 %collective-permute-start = (bf16[2,64,1024]{2,1,0:T(8,128)(2,1)S(1)}, bf16[2,64,1024]{2,1,0:T(8,128)(2,1)S(1)}, u32[]{:S(2)}, u32[]{:S(2)}) collective-permute-start(bf16[2,64,1024]{2,1,0:T(8,128)(2,1)S(1)} %get-tuple-element.22), channel_id=1, source_target_pairs={{0,3},{1,2},{2,1},{3,0},{4,7},{5,6},{6,5},{7,4},{8,11},{9,10},{10,... | collective-permute-start | bytes 786440 | tf_op jit(solution)/shard_map/ppermute | solution.py:382
  11.9 0.5 collective-permute-start.1
  12.4 0.0 collective-permute-start.5
  12.4 0.0 collective-permute-done.3.refs_7_
  12.4 1.3 %collective-permute-start.4 = (bf16[272,256]{1,0:T(8,128)(2,1)S(1)}, bf16[272,256]{1,0:T(8,128)(2,1)S(1)}, u32[]{:S(2)}, u32[]{:S(2)}) collective-permute-start(bf16[272,256]{1,0:T(8,128)(2,1)S(1)} %shard_map.78.refs_4_), channel_id=1, source_target_pairs={{0,4},{1,5},{2,6},{3,7},{4,0},{5,1},{6,2},{7,3},{8,12},{9,13},{10,... | collective-permute-start | bytes 417800 | tf_op jit(solution)/shard_map/ppermute | solution.py:375
  13.7 4.1 %collective-permute-start.2 = (bf16[2,64,1024]{2,1,0:T(8,128)(2,1)S(1)}, bf16[2,64,1024]{2,1,0:T(8,128)(2,1)S(1)}, u32[]{:S(2)}, u32[]{:S(2)}) collective-permute-start(bf16[2,64,1024]{2,1,0:T(8,128)(2,1)S(1)} %get-tuple-element.24), channel_id=1, source_target_pairs={{0,1},{1,0},{2,3},{3,2},{4,5},{5,4},{6,7},{7,6},{8,9},{9,8},{10,11... | collective-permute-start | bytes 786440 | tf_op jit(solution)/shard_map/ppermute | solution.py:382
  17.8 2.0 %collective-permute-done.5.refs_6_ = bf16[272,256]{1,0:T(8,128)(2,1)S(1)} collective-permute-done((bf16[272,256]{1,0:T(8,128)(2,1)S(1)}, bf16[272,256]{1,0:T(8,128)(2,1)S(1)}, u32[]{:S(2)}, u32[]{:S(2)}) %collective-permute-start.5) | collective-permute-done | bytes 139296 | tf_op jit(solution)/shard_map/ppermute | solution.py:375
  19.9 0.0 collective-permute-start.6
  19.9 0.0 collective-permute-done.refs_1_
  19.9 0.5 collective-permute-start.8
  20.4 3.3 %collective-permute-done.1.refs_2_ = bf16[2,64,1024]{2,1,0:T(8,128)(2,1)S(1)} collective-permute-done((bf16[2,64,1024]{2,1,0:T(8,128)(2,1)S(1)}, bf16[2,64,1024]{2,1,0:T(8,128)(2,1)S(1)}, u32[]{:S(2)}, u32[]{:S(2)}) %collective-permute-start.1) | collective-permute-done | bytes 262176 | tf_op jit(solution)/shard_map/ppermute | solution.py:382
  23.7 0.0 collective-permute-start.9
  23.7 0.0 collective-permute-done.4.refs_5_
  23.7 0.5 collective-permute-start.7
  24.2 0.0 collective-permute-done.2.refs_3_
  24.2 0.0 collective-permute-done.8.refs_10_
  24.2 0.0 collective-permute-done.6.refs_8_
  24.2 0.8 %collective-permute-done.9.refs_11_ = bf16[272,256]{1,0:T(8,128)(2,1)S(1)} collective-permute-done((bf16[272,256]{1,0:T(8,128)(2,1)S(1)}, bf16[272,256]{1,0:T(8,128)(2,1)S(1)}, u32[]{:S(2)}, u32[]{:S(2)}) %collective-permute-start.9) | collective-permute-done | bytes 139296 | tf_op jit(solution)/shard_map/ppermute | solution.py:378
  25.1 0.2 collective-permute-done.7.refs_9_
  25.3 1.7 %shard_map.79 = (bf16[4,512,256]{2,1,0:T(8,128)(2,1)S(1)}, f32[4,8,256]{2,1,0:T(8,128)S(1)}, bf16[2,2,256,256]{3,2,1,0:T(8,128)(2,1)S(1)}, bf16[2,2,256,256]{3,2...) custom-call(s32[3]{0:T(128)S(1)} %pad_add_fusion.index, ...), custom_call_target="tpu_custom_call" | custom-call | tf_op jit(solution)/shard_map/pallas_call | solution.py:352
  27.0 0.1 collective-permute-start.20
  27.1 1.8 %collective-permute-start.10 = (bf16[64,896]{1,0:T(8,128)(2,1)S(1)}, bf16[64,896]{1,0:T(8,128)(2,1)S(1)}, u32[]{:S(2)}, u32[]{:S(2)}) collective-permute-start(bf16[64,896]{1,0:T(8,128)(2,1)S(1)} %get-tuple-element.26), channel_id=1, source_target_pairs={{0,3},{1,2},{2,1},{3,0},{4,7},{5,6},{6,5},{7,4},{8,11},{9,10},{10,... | collective-permute-start | bytes 344072 | tf_op jit(solution)/shard_map/ppermute | solution.py:382
  28.9 1.2 %collective-permute-start.11 = (bf16[64,896]{1,0:T(8,128)(2,1)S(1)}, bf16[64,896]{1,0:T(8,128)(2,1)S(1)}, u32[]{:S(2)}, u32[]{:S(2)}) collective-permute-start(bf16[64,896]{1,0:T(8,128)(2,1)S(1)} %get-tuple-element.27), channel_id=1, source_target_pairs={{0,2},{1,3},{2,0},{3,1},{4,6},{5,7},{6,4},{7,5},{8,10},{9,11},{10,... | collective-permute-start | bytes 344072 | tf_op jit(solution)/shard_map/ppermute | solution.py:382
  30.1 0.0 copy-start
  30.1 0.5 collective-permute-start.12
  30.6 3.4 %collective-permute-done.10.refs_0_ = bf16[64,896]{1,0:T(8,128)(2,1)S(1)} collective-permute-done((bf16[64,896]{1,0:T(8,128)(2,1)S(1)}, bf16[64,896]{1,0:T(8,128)(2,1)S(1)}, u32[]{:S(2)}, u32[]{:S(2)}) %collective-permute-start.10) | collective-permute-done | bytes 114720 | tf_op jit(solution)/shard_map/ppermute | solution.py:382
  34.0 1.9 %collective-permute-done.11.refs_1_ = bf16[64,896]{1,0:T(8,128)(2,1)S(1)} collective-permute-done((bf16[64,896]{1,0:T(8,128)(2,1)S(1)}, bf16[64,896]{1,0:T(8,128)(2,1)S(1)}, u32[]{:S(2)}, u32[]{:S(2)}) %collective-permute-start.11) | collective-permute-done | bytes 114720 | tf_op jit(solution)/shard_map/ppermute | solution.py:382
  35.9 0.1 collective-permute-done.12.refs_2_
  35.9 0.0 copy-done
  35.9 3.1 %shard_map.80.refs_0_ = bf16[64,640]{1,0:T(8,128)(2,1)S(1)} custom-call(s32[3]{0:T(128)S(1)} %pad_add_fusion.index, s32[2,1,2]{2,1,0:T(1,128)S(1)} %copy-done, bf16[64,896]{1,0:T(8,128)(2,1)S(1)} %collective-permute-done.10.refs_0_, bf16[64,896]{1,0:T(8,128)(2,1)S(1)} %collective-permute-done.11.refs_1_, ...), custom_call_target="tpu_custom_call" | custom-call | tf_op jit(solution)/shard_map/pallas_call | solution.py:352
  39.1 2.9 %collective-permute-start.19 = (bf16[64,640]{1,0:T(8,128)(2,1)S(1)}, bf16[64,640]{1,0:T(8,128)(2,1)S(1)}, u32[]{:S(2)}, u32[]{:S(2)}) collective-permute-start(bf16[64,640]{1,0:T(8,128)(2,1)S(1)} %shard_map.80.refs_0_), channel_id=1, source_target_pairs={{0,7},{1,6},{2,5},{3,4},{4,3},{5,2},{6,1},{7,0},{8,15},{9,14},{10,... | collective-permute-start | bytes 245768 | tf_op jit(solution)/shard_map/ppermute | solution.py:382
  41.9 1.0 %collective-permute-start.18 = (bf16[64,640]{1,0:T(8,128)(2,1)S(1)}, bf16[64,640]{1,0:T(8,128)(2,1)S(1)}, u32[]{:S(2)}, u32[]{:S(2)}) collective-permute-start(bf16[64,640]{1,0:T(8,128)(2,1)S(1)} %shard_map.80.refs_0_), channel_id=1, source_target_pairs={{0,6},{1,7},{2,4},{3,5},{4,2},{5,3},{6,0},{7,1},{8,14},{9,15},{10,... | collective-permute-start | bytes 245768 | tf_op jit(solution)/shard_map/ppermute | solution.py:382
  42.9 1.7 %collective-permute-start.17 = (bf16[64,640]{1,0:T(8,128)(2,1)S(1)}, bf16[64,640]{1,0:T(8,128)(2,1)S(1)}, u32[]{:S(2)}, u32[]{:S(2)}) collective-permute-start(bf16[64,640]{1,0:T(8,128)(2,1)S(1)} %shard_map.80.refs_0_), channel_id=1, source_target_pairs={{0,5},{1,4},{2,7},{3,6},{4,1},{5,0},{6,3},{7,2},{8,13},{9,12},{10,... | collective-permute-start | bytes 245768 | tf_op jit(solution)/shard_map/ppermute | solution.py:382
  44.6 0.4 collective-permute-start.16
  45.0 0.5 collective-permute-done.19.refs_7_
  45.5 2.0 %collective-permute-start.15 = (bf16[64,640]{1,0:T(8,128)(2,1)S(1)}, bf16[64,640]{1,0:T(8,128)(2,1)S(1)}, u32[]{:S(2)}, u32[]{:S(2)}) collective-permute-start(bf16[64,640]{1,0:T(8,128)(2,1)S(1)} %shard_map.80.refs_0_), channel_id=1, source_target_pairs={{0,3},{1,2},{2,1},{3,0},{4,7},{5,6},{6,5},{7,4},{8,11},{9,10},{10,... | collective-permute-start | bytes 245768 | tf_op jit(solution)/shard_map/ppermute | solution.py:382
  47.5 0.8 %collective-permute-done.18.refs_6_ = bf16[64,640]{1,0:T(8,128)(2,1)S(1)} collective-permute-done((bf16[64,640]{1,0:T(8,128)(2,1)S(1)}, bf16[64,640]{1,0:T(8,128)(2,1)S(1)}, u32[]{:S(2)}, u32[]{:S(2)}) %collective-permute-start.18) | collective-permute-done | bytes 81952 | tf_op jit(solution)/shard_map/ppermute | solution.py:382
  48.2 1.2 %collective-permute-start.14 = (bf16[64,640]{1,0:T(8,128)(2,1)S(1)}, bf16[64,640]{1,0:T(8,128)(2,1)S(1)}, u32[]{:S(2)}, u32[]{:S(2)}) collective-permute-start(bf16[64,640]{1,0:T(8,128)(2,1)S(1)} %shard_map.80.refs_0_), channel_id=1, source_target_pairs={{0,2},{1,3},{2,0},{3,1},{4,6},{5,7},{6,4},{7,5},{8,10},{9,11},{10,... | collective-permute-start | bytes 245768 | tf_op jit(solution)/shard_map/ppermute | solution.py:382
  49.4 0.3 collective-permute-done.17.refs_5_
  49.7 1.0 %collective-permute-start.13 = (bf16[64,640]{1,0:T(8,128)(2,1)S(1)}, bf16[64,640]{1,0:T(8,128)(2,1)S(1)}, u32[]{:S(2)}, u32[]{:S(2)}) collective-permute-start(bf16[64,640]{1,0:T(8,128)(2,1)S(1)} %shard_map.80.refs_0_), channel_id=1, source_target_pairs={{0,1},{1,0},{2,3},{3,2},{4,5},{5,4},{6,7},{7,6},{8,9},{9,8},{10,11... | collective-permute-start | bytes 245768 | tf_op jit(solution)/shard_map/ppermute | solution.py:382
  50.7 0.0 collective-permute-done.16.refs_4_
  50.7 0.7 collective-permute-done.15.refs_3_
  51.4 1.2 %collective-permute-done.14.refs_2_ = bf16[64,640]{1,0:T(8,128)(2,1)S(1)} collective-permute-done((bf16[64,640]{1,0:T(8,128)(2,1)S(1)}, bf16[64,640]{1,0:T(8,128)(2,1)S(1)}, u32[]{:S(2)}, u32[]{:S(2)}) %collective-permute-start.14) | collective-permute-done | bytes 81952 | tf_op jit(solution)/shard_map/ppermute | solution.py:382
  52.6 1.5 %collective-permute-done.13.refs_1_ = bf16[64,640]{1,0:T(8,128)(2,1)S(1)} collective-permute-done((bf16[64,640]{1,0:T(8,128)(2,1)S(1)}, bf16[64,640]{1,0:T(8,128)(2,1)S(1)}, u32[]{:S(2)}, u32[]{:S(2)}) %collective-permute-start.13) | collective-permute-done | bytes 81952 | tf_op jit(solution)/shard_map/ppermute | solution.py:382
  54.1 0.0 collective-permute-done.20.refs_9_
  54.1 1.6 %shard_map.81 = (f32[2,256,256]{2,1,0:T(8,128)S(1)}, bf16[2,256,256]{2,1,0:T(8,128)(2,1)S(1)}) custom-call(s32[3]{0:T(128)S(1)} %pad_add_fusion.index, bf16[64,640]{1,0:T(8,128)(2,1)S(1)} %shard_map.80.refs_0_, bf16[64,640]{1,0:T(8,128)(2,1)S(1)} %collective-permute-done.13.refs_1_, bf16[64,640]{1,0:T(8,128)(2,1)S(1)} %collective-permute-done.14.refs_2_, ...), custom_call_target="tpu_custom_call" | custom-call | tf_op jit(solution)/shard_map/pallas_call | solution.py:352
  55.8 0.1 collective-permute-start.21
  55.8 1.5 %collective-permute-done.21.come_ref = bf16[2,256,256]{2,1,0:T(8,128)(2,1)S(1)} collective-permute-done((bf16[2,256,256]{2,1,0:T(8,128)(2,1)S(1)}, bf16[2,256,256]{2,1,0:T(8,128)(2,1)S(1)}, u32[]{:S(2)}, u32[]{:S(2)}) %collective-permute-start.21) | collective-permute-done | bytes 262176 | tf_op jit(solution)/shard_map/ppermute | solution.py:378
  57.4 0.6 shard_map.82
  58.0 0.1 collective-permute-start.22
  58.0 9.2 %collective-permute-done.22.refs_0_ = bf16[256,256]{1,0:T(8,128)(2,1)S(1)} collective-permute-done((bf16[256,256]{1,0:T(8,128)(2,1)S(1)}, bf16[256,256]{1,0:T(8,128)(2,1)S(1)}, u32[]{:S(2)}, u32[]{:S(2)}) %collective-permute-start.22) | collective-permute-done | bytes 131104 | tf_op jit(solution)/shard_map/ppermute | solution.py:375
  67.3 0.7 %shard_map.83 = (f32[192,256]{1,0:T(8,128)}, f32[64,256]{1,0:T(8,128)}) custom-call(f32[256,256]{1,0:T(8,128)S(1)} %get-tuple-element.36.keep_ref, bf16[256,256]{1,0:T(8,128)(2,1)S(1)} %collective-permute-done.22.refs_0_), custom_call_target="tpu_custom_call" | custom-call | tf_op jit(solution)/shard_map/pallas_call | solution.py:352
Async XLA Ops:
  2.2 10.2 %collective-permute-start.3 = (bf16[272,256]{1,0:T(8,128)(2,1)S(1)}, bf16[272,256]{1,0:T(8,128)(2,1)S(1)}, u32[]{:S(2)}, u32[]{:S(2)}) collective-permute-start(bf16[272,256]{1,0:T(8,128)(2,1)S(1)} %shard_map.78.refs_4_), channel_id=1, source_target_pairs={{0,12},{1,13},{2,14},{3,15},{4,8},{5,9},{6,10},{7,11},{8,4},{9,5},... | collective-permute-start | bytes 417800 | tf_op jit(solution)/shard_map/ppermute | solution.py:375
  9.3 10.5 %collective-permute-start = (bf16[2,64,1024]{2,1,0:T(8,128)(2,1)S(1)}, bf16[2,64,1024]{2,1,0:T(8,128)(2,1)S(1)}, u32[]{:S(2)}, u32[]{:S(2)}) collective-permute-start(bf16[2,64,1024]{2,1,0:T(8,128)(2,1)S(1)} %get-tuple-element.22), channel_id=1, source_target_pairs={{0,3},{1,2},{2,1},{3,0},{4,7},{5,6},{6,5},{7,4},{8,11},{9,10},{10,... | collective-permute-start | bytes 786440 | tf_op jit(solution)/shard_map/ppermute | solution.py:382
  11.9 11.8 %collective-permute-start.1 = (bf16[2,64,1024]{2,1,0:T(8,128)(2,1)S(1)}, bf16[2,64,1024]{2,1,0:T(8,128)(2,1)S(1)}, u32[]{:S(2)}, u32[]{:S(2)}) collective-permute-start(bf16[2,64,1024]{2,1,0:T(8,128)(2,1)S(1)} %get-tuple-element.23), channel_id=1, source_target_pairs={{0,2},{1,3},{2,0},{3,1},{4,6},{5,7},{6,4},{7,5},{8,10},{9,11},{10,... | collective-permute-start | bytes 786440 | tf_op jit(solution)/shard_map/ppermute | solution.py:382
  12.4 7.5 %collective-permute-start.5 = (bf16[272,256]{1,0:T(8,128)(2,1)S(1)}, bf16[272,256]{1,0:T(8,128)(2,1)S(1)}, u32[]{:S(2)}, u32[]{:S(2)}) collective-permute-start(bf16[272,256]{1,0:T(8,128)(2,1)S(1)} %shard_map.78.refs_4_), channel_id=1, source_target_pairs={{0,8},{1,9},{2,10},{3,11},{4,12},{5,13},{6,14},{7,15},{8,0},{9,1},... | collective-permute-start | bytes 417800 | tf_op jit(solution)/shard_map/ppermute | solution.py:375
  12.4 11.3 %collective-permute-start.4 = (bf16[272,256]{1,0:T(8,128)(2,1)S(1)}, bf16[272,256]{1,0:T(8,128)(2,1)S(1)}, u32[]{:S(2)}, u32[]{:S(2)}) collective-permute-start(bf16[272,256]{1,0:T(8,128)(2,1)S(1)} %shard_map.78.refs_4_), channel_id=1, source_target_pairs={{0,4},{1,5},{2,6},{3,7},{4,0},{5,1},{6,2},{7,3},{8,12},{9,13},{10,... | collective-permute-start | bytes 417800 | tf_op jit(solution)/shard_map/ppermute | solution.py:375
  13.7 10.5 %collective-permute-start.2 = (bf16[2,64,1024]{2,1,0:T(8,128)(2,1)S(1)}, bf16[2,64,1024]{2,1,0:T(8,128)(2,1)S(1)}, u32[]{:S(2)}, u32[]{:S(2)}) collective-permute-start(bf16[2,64,1024]{2,1,0:T(8,128)(2,1)S(1)} %get-tuple-element.24), channel_id=1, source_target_pairs={{0,1},{1,0},{2,3},{3,2},{4,5},{5,4},{6,7},{7,6},{8,9},{9,8},{10,11... | collective-permute-start | bytes 786440 | tf_op jit(solution)/shard_map/ppermute | solution.py:382
  19.9 4.4 %collective-permute-start.6 = (bf16[272,256]{1,0:T(8,128)(2,1)S(1)}, bf16[272,256]{1,0:T(8,128)(2,1)S(1)}, u32[]{:S(2)}, u32[]{:S(2)}) collective-permute-start(bf16[272,256]{1,0:T(8,128)(2,1)S(1)} %shard_map.78.refs_4_), channel_id=1, source_target_pairs={{0,16},{16,0},{1,17},{17,1},{2,18},{18,2},{3,19},{19,3},{4,20},{20... | collective-permute-start | bytes 417800 | tf_op jit(solution)/shard_map/ppermute | solution.py:378
  19.9 4.3 %collective-permute-start.8 = (bf16[272,256]{1,0:T(8,128)(2,1)S(1)}, bf16[272,256]{1,0:T(8,128)(2,1)S(1)}, u32[]{:S(2)}, u32[]{:S(2)}) collective-permute-start(bf16[272,256]{1,0:T(8,128)(2,1)S(1)} %collective-permute-done.5.refs_6_), channel_id=1, source_target_pairs={{0,16},{16,0},{1,17},{17,1},{2,18},{18,2},{3,19},{19,3},{4,20},{20... | collective-permute-start | bytes 417800 | tf_op jit(solution)/shard_map/ppermute | solution.py:378
  23.7 1.4 %collective-permute-start.9 = (bf16[272,256]{1,0:T(8,128)(2,1)S(1)}, bf16[272,256]{1,0:T(8,128)(2,1)S(1)}, u32[]{:S(2)}, u32[]{:S(2)}) collective-permute-start(bf16[272,256]{1,0:T(8,128)(2,1)S(1)} %collective-permute-done.3.refs_7_), channel_id=1, source_target_pairs={{0,16},{16,0},{1,17},{17,1},{2,18},{18,2},{3,19},{19,3},{4,20},{20... | collective-permute-start | bytes 417800 | tf_op jit(solution)/shard_map/ppermute | solution.py:378
  23.7 1.5 %collective-permute-start.7 = (bf16[272,256]{1,0:T(8,128)(2,1)S(1)}, bf16[272,256]{1,0:T(8,128)(2,1)S(1)}, u32[]{:S(2)}, u32[]{:S(2)}) collective-permute-start(bf16[272,256]{1,0:T(8,128)(2,1)S(1)} %collective-permute-done.4.refs_5_), channel_id=1, source_target_pairs={{0,16},{16,0},{1,17},{17,1},{2,18},{18,2},{3,19},{19,3},{4,20},{20... | collective-permute-start | bytes 417800 | tf_op jit(solution)/shard_map/ppermute | solution.py:378
  27.0 27.1 %collective-permute-start.20 = (bf16[2,2,256,256]{3,2,1,0:T(8,128)(2,1)S(1)}, bf16[2,2,256,256]{3,2,1,0:T(8,128)(2,1)S(1)}, u32[]{:S(2)}, u32[]{:S(2)}) collective-permute-start(bf16[2,2,256,256]{3,2,1,0:T(8,128)(2,1)S(1)} %get-tuple-element.31), channel_id=1, source_target_pairs={{0,4},{1,5},{2,6},{3,7},{4,0},{5,1},{6,2},{7,3},{8,12},{9,13},{10,... | collective-permute-start | bytes 1572872 | tf_op jit(solution)/shard_map/ppermute | solution.py:375
  27.1 6.9 %collective-permute-start.10 = (bf16[64,896]{1,0:T(8,128)(2,1)S(1)}, bf16[64,896]{1,0:T(8,128)(2,1)S(1)}, u32[]{:S(2)}, u32[]{:S(2)}) collective-permute-start(bf16[64,896]{1,0:T(8,128)(2,1)S(1)} %get-tuple-element.26), channel_id=1, source_target_pairs={{0,3},{1,2},{2,1},{3,0},{4,7},{5,6},{6,5},{7,4},{8,11},{9,10},{10,... | collective-permute-start | bytes 344072 | tf_op jit(solution)/shard_map/ppermute | solution.py:382
  28.9 7.0 %collective-permute-start.11 = (bf16[64,896]{1,0:T(8,128)(2,1)S(1)}, bf16[64,896]{1,0:T(8,128)(2,1)S(1)}, u32[]{:S(2)}, u32[]{:S(2)}) collective-permute-start(bf16[64,896]{1,0:T(8,128)(2,1)S(1)} %get-tuple-element.27), channel_id=1, source_target_pairs={{0,2},{1,3},{2,0},{3,1},{4,6},{5,7},{6,4},{7,5},{8,10},{9,11},{10,... | collective-permute-start | bytes 344072 | tf_op jit(solution)/shard_map/ppermute | solution.py:382
  30.1 5.8 %copy-start = (s32[2,1,2]{2,1,0:T(1,128)S(1)}, s32[2,1,2]{2,1,0:T(1,128)}, u32[]{:S(2)}) copy-start(s32[2,1,2]{2,1,0:T(1,128)} %docs.1) | copy-start | bytes 52
  30.1 5.8 %collective-permute-start.12 = (bf16[64,896]{1,0:T(8,128)(2,1)S(1)}, bf16[64,896]{1,0:T(8,128)(2,1)S(1)}, u32[]{:S(2)}, u32[]{:S(2)}) collective-permute-start(bf16[64,896]{1,0:T(8,128)(2,1)S(1)} %get-tuple-element.28), channel_id=1, source_target_pairs={{0,1},{1,0},{2,3},{3,2},{4,5},{5,4},{6,7},{7,6},{8,9},{9,8},{10,11... | collective-permute-start | bytes 344072 | tf_op jit(solution)/shard_map/ppermute | solution.py:382
  39.1 6.4 %collective-permute-start.19 = (bf16[64,640]{1,0:T(8,128)(2,1)S(1)}, bf16[64,640]{1,0:T(8,128)(2,1)S(1)}, u32[]{:S(2)}, u32[]{:S(2)}) collective-permute-start(bf16[64,640]{1,0:T(8,128)(2,1)S(1)} %shard_map.80.refs_0_), channel_id=1, source_target_pairs={{0,7},{1,6},{2,5},{3,4},{4,3},{5,2},{6,1},{7,0},{8,15},{9,14},{10,... | collective-permute-start | bytes 245768 | tf_op jit(solution)/shard_map/ppermute | solution.py:382
  41.9 6.3 %collective-permute-start.18 = (bf16[64,640]{1,0:T(8,128)(2,1)S(1)}, bf16[64,640]{1,0:T(8,128)(2,1)S(1)}, u32[]{:S(2)}, u32[]{:S(2)}) collective-permute-start(bf16[64,640]{1,0:T(8,128)(2,1)S(1)} %shard_map.80.refs_0_), channel_id=1, source_target_pairs={{0,6},{1,7},{2,4},{3,5},{4,2},{5,3},{6,0},{7,1},{8,14},{9,15},{10,... | collective-permute-start | bytes 245768 | tf_op jit(solution)/shard_map/ppermute | solution.py:382
  42.9 6.8 %collective-permute-start.17 = (bf16[64,640]{1,0:T(8,128)(2,1)S(1)}, bf16[64,640]{1,0:T(8,128)(2,1)S(1)}, u32[]{:S(2)}, u32[]{:S(2)}) collective-permute-start(bf16[64,640]{1,0:T(8,128)(2,1)S(1)} %shard_map.80.refs_0_), channel_id=1, source_target_pairs={{0,5},{1,4},{2,7},{3,6},{4,1},{5,0},{6,3},{7,2},{8,13},{9,12},{10,... | collective-permute-start | bytes 245768 | tf_op jit(solution)/shard_map/ppermute | solution.py:382
  44.6 6.1 %collective-permute-start.16 = (bf16[64,640]{1,0:T(8,128)(2,1)S(1)}, bf16[64,640]{1,0:T(8,128)(2,1)S(1)}, u32[]{:S(2)}, u32[]{:S(2)}) collective-permute-start(bf16[64,640]{1,0:T(8,128)(2,1)S(1)} %shard_map.80.refs_0_), channel_id=1, source_target_pairs={{0,4},{1,5},{2,6},{3,7},{4,0},{5,1},{6,2},{7,3},{8,12},{9,13},{10,... | collective-permute-start | bytes 245768 | tf_op jit(solution)/shard_map/ppermute | solution.py:382
  45.5 5.9 %collective-permute-start.15 = (bf16[64,640]{1,0:T(8,128)(2,1)S(1)}, bf16[64,640]{1,0:T(8,128)(2,1)S(1)}, u32[]{:S(2)}, u32[]{:S(2)}) collective-permute-start(bf16[64,640]{1,0:T(8,128)(2,1)S(1)} %shard_map.80.refs_0_), channel_id=1, source_target_pairs={{0,3},{1,2},{2,1},{3,0},{4,7},{5,6},{6,5},{7,4},{8,11},{9,10},{10,... | collective-permute-start | bytes 245768 | tf_op jit(solution)/shard_map/ppermute | solution.py:382
  48.2 4.4 %collective-permute-start.14 = (bf16[64,640]{1,0:T(8,128)(2,1)S(1)}, bf16[64,640]{1,0:T(8,128)(2,1)S(1)}, u32[]{:S(2)}, u32[]{:S(2)}) collective-permute-start(bf16[64,640]{1,0:T(8,128)(2,1)S(1)} %shard_map.80.refs_0_), channel_id=1, source_target_pairs={{0,2},{1,3},{2,0},{3,1},{4,6},{5,7},{6,4},{7,5},{8,10},{9,11},{10,... | collective-permute-start | bytes 245768 | tf_op jit(solution)/shard_map/ppermute | solution.py:382
  49.7 4.4 %collective-permute-start.13 = (bf16[64,640]{1,0:T(8,128)(2,1)S(1)}, bf16[64,640]{1,0:T(8,128)(2,1)S(1)}, u32[]{:S(2)}, u32[]{:S(2)}) collective-permute-start(bf16[64,640]{1,0:T(8,128)(2,1)S(1)} %shard_map.80.refs_0_), channel_id=1, source_target_pairs={{0,1},{1,0},{2,3},{3,2},{4,5},{5,4},{6,7},{7,6},{8,9},{9,8},{10,11... | collective-permute-start | bytes 245768 | tf_op jit(solution)/shard_map/ppermute | solution.py:382
  55.8 1.6 %collective-permute-start.21 = (bf16[2,256,256]{2,1,0:T(8,128)(2,1)S(1)}, bf16[2,256,256]{2,1,0:T(8,128)(2,1)S(1)}, u32[]{:S(2)}, u32[]{:S(2)}) collective-permute-start(bf16[2,256,256]{2,1,0:T(8,128)(2,1)S(1)} %get-tuple-element.35), channel_id=1, source_target_pairs={{0,16},{16,0},{1,17},{17,1},{2,18},{18,2},{3,19},{19,3},{4,20},{20... | collective-permute-start | bytes 786440 | tf_op jit(solution)/shard_map/ppermute | solution.py:378
  58.0 9.3 %collective-permute-start.22 = (bf16[256,256]{1,0:T(8,128)(2,1)S(1)}, bf16[256,256]{1,0:T(8,128)(2,1)S(1)}, u32[]{:S(2)}, u32[]{:S(2)}) collective-permute-start(bf16[256,256]{1,0:T(8,128)(2,1)S(1)} %get-tuple-element.37), channel_id=1, source_target_pairs={{0,8},{1,9},{2,10},{3,11},{4,12},{5,13},{6,14},{7,15},{8,0},{9,1},... | collective-permute-start | bytes 393224 | tf_op jit(solution)/shard_map/ppermute | solution.py:375

commit v8 on v6

--- a/solution.py
+++ b/solution.py
@@ -10,6 +10,7 @@
 F32 = jnp.float32
 BF16 = jnp.bfloat16
 PLANE = 4
+RING = (0, 1, 3, 2)
 STATS = 16
 VMEM_LIMIT = 16 * 1024 * 1024
 
@@ -287,14 +288,12 @@
 
 
 def grads_kernel(planes, heads, index, *refs):
-    factors, (x_ref, c_ref, vx_ref, gain_ref) = refs[:PLANE], refs[PLANE : PLANE + 4]
-    keep_ref, send_ref, all_ref = refs[PLANE + 4 :]
+    ring_ref, x_ref, c_ref, vx_ref, gain_ref, keep_ref, send_ref = refs
     qkv, half, width = 3 * heads, 2 * heads, vx_ref.shape[-1]
-    section, p = index[0], index[2]
-    for k in range(PLANE):
-        all_ref[p ^ k] = factors[k][...]
+    section = index[0]
     rows = x_ref.shape[0] * x_ref.shape[1]
-    turned = jnp.transpose(all_ref[...].astype(F32).reshape(rows, 5 * half)).astype(BF16)
+    in_order = jnp.concatenate([ring_ref[RING.index(b)] for b in range(PLANE)], axis=0)
+    turned = jnp.transpose(in_order.astype(F32)).astype(BF16)
     att0, att1 = turned[qkv : qkv + heads], turned[4 * half : 4 * half + heads]
     right = turned[2 * half : 4 * half]
     small = nt(right, att0).astype(BF16)
@@ -372,6 +371,8 @@
     def along_plane(value, k):
         route = [(a * PLANE + b, a * PLANE + (b ^ k)) for a in range(planes) for b in range(PLANE)]
         return lax.ppermute(value, "dp", route)
+
+    in_ring = [[a * PLANE + b for b in RING] for a in range(planes)]
 
     def exchange(value):
         return far_first(value, PLANE, along_plane)
@@ -424,8 +425,7 @@
     keep, send = call(
         functools.partial(grads_kernel, planes, heads),
         [(grads, F32), (grads, BF16)],
-        index, *exchange(factors), x, c, vx, gains, scalars=1,
-        scratch=[((PLANE, block, 5 * half), BF16)],
+        index, lax.all_gather(factors, "dp", axis=0, axis_index_groups=in_ring), x, c, vx, gains, scalars=1,
     )
     merged = call(
         merge_kernel,

time: 64.5 us -> 67.5 us (1.047)
  blocking collectives: 0 us -> 10.4 us
  waiting for transfers between devices: 26 us -> 22.2 us
  starting transfers between devices: 26.2 us -> 22.7 us
    all_gather x0 -> x1, blocking collectives: none -> 10.4 us  [planar(): lax.all_gather(factors, 'dp', axis=0, axis_index_groups=in_ring)]
    ppermute x9 -> x6, waiting for transfers between devices: 12.5 us -> 8.62 us  [along_plane(): return lax.ppermute(value, 'dp', route)]
    ppermute x9 -> x6, starting transfers between devices: 14.2 us -> 10.7 us  [along_plane(): return lax.ppermute(value, 'dp', route)]
  transfers between devices with their start and end apart: 20 -> 17, of which waited for: 13 -> 10; matrix products, arithmetic and copies ran while one was open for 0% -> 0% of each run, Pallas kernels for 3% -> 3%
where the time goes in v8:
time: 67.5 us; the launch traced here: 67.2 us
  starting transfers between devices  22.7 us (34%)
  waiting for transfers between devices  22.2 us (33%)
  Pallas kernels  11.1 us (16%)
  blocking collectives  10.4 us (15%)
  between operations  0.73 us (1%)
    ppermute x6, starting transfers between devices, along_z(): return lax.ppermute(value, 'dp', route)  10.9 us
    ppermute x6, starting transfers between devices, along_plane(): return lax.ppermute(value, 'dp', route)  10.7 us
    ppermute x6, waiting for transfers between devices, along_z(): return lax.ppermute(value, 'dp', route)  10.7 us
    all_gather x1, blocking collectives, planar(): lax.all_gather(factors, 'dp', axis=0, axis_index_groups=in_ring)  10.4 us
    ppermute x6, waiting for transfers between devices, along_plane(): return lax.ppermute(value, 'dp', route)  8.62 us
    pallas_call x5, Pallas kernels, call(): pl.pallas_call(kernel, out_shape=[jax.ShapeDtypeStruct(shape, dtype) for...  7.62 us
    ppermute x5, waiting for transfers between devices, to_sibling(): return lax.ppermute(value, 'section', [(0, 1), (1, 0)])  2.93 us
    pallas_call x1, Pallas kernels, planar(): pl.pallas_call(functools.partial(blocks_kernel, planes), out_shape=[jax.S...  2.01 us
  transfers between devices with their start and end apart: 17, of which 10 were waited for; matrix products, arithmetic and copies ran while one was open for 0% of the time, Pallas kernels for 3%

profile of v8, /device:TPU:0, one launch (start us, length us, event | category | flops | bytes accessed | tf_op | source)
XLA Modules:
  0.0 67.2 jit_solution(6449936285921465140)
XLA Ops:
  0.6 0.1 pad_add_fusion.index
  0.7 1.5 %shard_map.78.refs_4_ = bf16[272,256]{1,0:T(8,128)(2,1)S(1)} custom-call(s32[3]{0:T(128)S(1)} %pad_add_fusion.index, bf16[1,4096]{1,0:T(2,128)(2,1)} %gain_ref.1, bf16[192,256]{1,0:T(8,128)(2,1)} %bitcast.13, bf16[64,256]{1,0:T(8,128)(2,1)} %bitcast.14), custom_call_target="tpu_custom_call" | custom-call | tf_op jit(solution)/shard_map/pallas_call | solution.py:387
  2.2 5.1 %collective-permute-start.3 = (bf16[272,256]{1,0:T(8,128)(2,1)S(1)}, bf16[272,256]{1,0:T(8,128)(2,1)S(1)}, u32[]{:S(2)}, u32[]{:S(2)}) collective-permute-start(bf16[272,256]{1,0:T(8,128)(2,1)S(1)} %shard_map.78.refs_4_), channel_id=1, source_target_pairs={{0,12},{1,13},{2,14},{3,15},{4,8},{5,9},{6,10},{7,11},{8,4},{9,5},... | collective-permute-start | bytes 417800 | tf_op jit(solution)/shard_map/ppermute | solution.py:366
  7.3 2.0 %shard_map.77 = (bf16[2,64,1024]{2,1,0:T(8,128)(2,1)S(1)}, bf16[2,64,1024]{2,1,0:T(8,128)(2,1)S(1)}, bf16[2,64,1024]{2,1,0:T(8,128)(2,1)S(1)}, bf16[2,64,1024]{2,1,0:T(8,128)(2,1)S(1)}) custom-call(s32[3]{0:T(128)S(1)} %pad_add_fusion.index, bf16[2,64,4096]{2,1,0:T(8,128)(2,1)} %x_ref.1, bf16[2,64,4096]{2,1,0:T(8,128)(2,1)} %c_ref.1), custom_call_target="tpu_custom_call" | custom-call | tf_op jit(solution)/shard_map/pallas_call | solution.py:395
  9.3 2.5 %collective-permute-start = (bf16[2,64,1024]{2,1,0:T(8,128)(2,1)S(1)}, bf16[2,64,1024]{2,1,0:T(8,128)(2,1)S(1)}, u32[]{:S(2)}, u32[]{:S(2)}) collective-permute-start(bf16[2,64,1024]{2,1,0:T(8,128)(2,1)S(1)} %get-tuple-element.24), channel_id=1, source_target_pairs={{0,3},{1,2},{2,1},{3,0},{4,7},{5,6},{6,5},{7,4},{8,11},{9,10},{10,... | collective-permute-start | bytes 786440 | tf_op jit(solution)/shard_map/ppermute | solution.py:373
  11.9 0.5 collective-permute-start.1
  12.4 0.0 collective-permute-start.5
  12.4 0.0 collective-permute-done.3.refs_7_
  12.4 1.3 %collective-permute-start.4 = (bf16[272,256]{1,0:T(8,128)(2,1)S(1)}, bf16[272,256]{1,0:T(8,128)(2,1)S(1)}, u32[]{:S(2)}, u32[]{:S(2)}) collective-permute-start(bf16[272,256]{1,0:T(8,128)(2,1)S(1)} %shard_map.78.refs_4_), channel_id=1, source_target_pairs={{0,4},{1,5},{2,6},{3,7},{4,0},{5,1},{6,2},{7,3},{8,12},{9,13},{10,... | collective-permute-start | bytes 417800 | tf_op jit(solution)/shard_map/ppermute | solution.py:366
  13.7 4.1 %collective-permute-start.2 = (bf16[2,64,1024]{2,1,0:T(8,128)(2,1)S(1)}, bf16[2,64,1024]{2,1,0:T(8,128)(2,1)S(1)}, u32[]{:S(2)}, u32[]{:S(2)}) collective-permute-start(bf16[2,64,1024]{2,1,0:T(8,128)(2,1)S(1)} %get-tuple-element.26), channel_id=1, source_target_pairs={{0,1},{1,0},{2,3},{3,2},{4,5},{5,4},{6,7},{7,6},{8,9},{9,8},{10,11... | collective-permute-start | bytes 786440 | tf_op jit(solution)/shard_map/ppermute | solution.py:373
  17.8 2.0 %collective-permute-done.5.refs_6_ = bf16[272,256]{1,0:T(8,128)(2,1)S(1)} collective-permute-done((bf16[272,256]{1,0:T(8,128)(2,1)S(1)}, bf16[272,256]{1,0:T(8,128)(2,1)S(1)}, u32[]{:S(2)}, u32[]{:S(2)}) %collective-permute-start.5) | collective-permute-done | bytes 139296 | tf_op jit(solution)/shard_map/ppermute | solution.py:366
  19.9 0.0 collective-permute-start.6
  19.9 0.0 collective-permute-done.refs_1_
  19.9 0.5 collective-permute-start.8
  20.4 3.3 %collective-permute-done.1.refs_2_ = bf16[2,64,1024]{2,1,0:T(8,128)(2,1)S(1)} collective-permute-done((bf16[2,64,1024]{2,1,0:T(8,128)(2,1)S(1)}, bf16[2,64,1024]{2,1,0:T(8,128)(2,1)S(1)}, u32[]{:S(2)}, u32[]{:S(2)}) %collective-permute-start.1) | collective-permute-done | bytes 262176 | tf_op jit(solution)/shard_map/ppermute | solution.py:373
  23.7 0.0 collective-permute-start.9
  23.7 0.0 collective-permute-done.4.refs_5_
  23.7 0.5 collective-permute-start.7
  24.2 0.0 collective-permute-done.2.refs_3_
  24.2 0.0 collective-permute-done.8.refs_10_
  24.2 0.0 collective-permute-done.6.refs_8_
  24.2 0.8 %collective-permute-done.9.refs_11_ = bf16[272,256]{1,0:T(8,128)(2,1)S(1)} collective-permute-done((bf16[272,256]{1,0:T(8,128)(2,1)S(1)}, bf16[272,256]{1,0:T(8,128)(2,1)S(1)}, u32[]{:S(2)}, u32[]{:S(2)}) %collective-permute-start.9) | collective-permute-done | bytes 139296 | tf_op jit(solution)/shard_map/ppermute | solution.py:369
  25.1 0.2 collective-permute-done.7.refs_9_
  25.3 1.6 %shard_map.79 = (bf16[4,64,1024]{2,1,0:T(8,128)(2,1)S(1)}, bf16[4,64,1024]{2,1,0:T(8,128)(2,1)S(1)}, bf16[4,512,256]{2,1,0:T(8,128)(2,1)S(1)}, f32[4,8,256]{2,1,...) custom-call(s32[3]{0:T(128)S(1)} %pad_add_fusion.index, ...), custom_call_target="tpu_custom_call" | custom-call | tf_op jit(solution)/shard_map/pallas_call | solution.py:343
  26.8 1.8 %collective-permute-start.10 = (bf16[64,896]{1,0:T(8,128)(2,1)S(1)}, bf16[64,896]{1,0:T(8,128)(2,1)S(1)}, u32[]{:S(2)}, u32[]{:S(2)}) collective-permute-start(bf16[64,896]{1,0:T(8,128)(2,1)S(1)} %get-tuple-element.28), channel_id=1, source_target_pairs={{0,3},{1,2},{2,1},{3,0},{4,7},{5,6},{6,5},{7,4},{8,11},{9,10},{10,... | collective-permute-start | bytes 344072 | tf_op jit(solution)/shard_map/ppermute | solution.py:373
  28.7 1.2 %collective-permute-start.11 = (bf16[64,896]{1,0:T(8,128)(2,1)S(1)}, bf16[64,896]{1,0:T(8,128)(2,1)S(1)}, u32[]{:S(2)}, u32[]{:S(2)}) collective-permute-start(bf16[64,896]{1,0:T(8,128)(2,1)S(1)} %get-tuple-element.29), channel_id=1, source_target_pairs={{0,2},{1,3},{2,0},{3,1},{4,6},{5,7},{6,4},{7,5},{8,10},{9,11},{10,... | collective-permute-start | bytes 344072 | tf_op jit(solution)/shard_map/ppermute | solution.py:373
  29.9 0.0 copy-start
  29.9 0.5 collective-permute-start.12
  30.4 3.4 %collective-permute-done.10.refs_0_ = bf16[64,896]{1,0:T(8,128)(2,1)S(1)} collective-permute-done((bf16[64,896]{1,0:T(8,128)(2,1)S(1)}, bf16[64,896]{1,0:T(8,128)(2,1)S(1)}, u32[]{:S(2)}, u32[]{:S(2)}) %collective-permute-start.10) | collective-permute-done | bytes 114720 | tf_op jit(solution)/shard_map/ppermute | solution.py:373
  33.8 1.9 %collective-permute-done.11.refs_1_ = bf16[64,896]{1,0:T(8,128)(2,1)S(1)} collective-permute-done((bf16[64,896]{1,0:T(8,128)(2,1)S(1)}, bf16[64,896]{1,0:T(8,128)(2,1)S(1)}, u32[]{:S(2)}, u32[]{:S(2)}) %collective-permute-start.11) | collective-permute-done | bytes 114720 | tf_op jit(solution)/shard_map/ppermute | solution.py:373
  35.6 0.1 collective-permute-done.12.refs_2_
  35.7 0.0 copy-done
  35.7 3.1 %shard_map.80 = bf16[64,640]{1,0:T(8,128)(2,1)S(1)} custom-call(s32[3]{0:T(128)S(1)} %pad_add_fusion.index, s32[2,1,2]{2,1,0:T(1,128)S(1)} %copy-done, bf16[64,896]{1,0:T(8,128)(2,1)S(1)} %collective-permute-done.10.refs_0_, bf16[64,896]{1,0:T(8,128)(2,1)S(1)} %collective-permute-done.11.refs_1_, bf16[64,896]{1,0:T(8,128)(2,1)S(1)} %collective-permute-done.12.refs_2_, ...), custom_call_target="tpu_custom_call" | custom-call | tf_op jit(solution)/shard_map/pallas_call | solution.py:343
  38.8 10.4 %all-gather = bf16[256,640]{1,0:T(8,128)(2,1)S(1)} all-gather(bf16[64,640]{1,0:T(8,128)(2,1)S(1)} %shard_map.80), channel_id=2, replica_groups={{0,1,3,2},{4,5,7,6},{8,9,11,10},{12,13,15,14},{16,17,19,18},{20,21,23,2..., dimensions={0}, use_global_device_ids=true | all-gather | bytes 409600 | tf_op jit(solution)/shard_map/all_gather | solution.py:428
  49.3 1.6 %shard_map.81 = (f32[4,256,256]{2,1,0:T(8,128)S(1)}, bf16[4,256,256]{2,1,0:T(8,128)(2,1)S(1)}) custom-call(s32[3]{0:T(128)S(1)} %pad_add_fusion.index, bf16[4,64,640]{2,1,0:T(8,128)(2,1)S(1)} %bitcast.12, bf16[4,64,1024]{2,1,0:T(8,128)(2,1)S(1)} %get-tuple-element.32.refs_1_, bf16[4,64,1024]{2,1,0:T(8,128)(2,1)S(1)} %get-tuple-element.33.refs_2_, ...), custom_call_target="tpu_custom_call" | custom-call | tf_op jit(solution)/shard_map/pallas_call | solution.py:343
  50.8 0.1 collective-permute-start.13
  50.9 1.9 %collective-permute-done.13.come_ref = bf16[4,256,256]{2,1,0:T(8,128)(2,1)S(1)} collective-permute-done((bf16[4,256,256]{2,1,0:T(8,128)(2,1)S(1)}, bf16[4,256,256]{2,1,0:T(8,128)(2,1)S(1)}, u32[]{:S(2)}, u32[]{:S(2)}) %collective-permute-start.13) | collective-permute-done | bytes 524320 | tf_op jit(solution)/shard_map/ppermute | solution.py:369
  52.8 0.6 shard_map.82
  53.4 0.5 collective-permute-start.14
  53.9 0.6 collective-permute-start.15
  54.5 3.4 %collective-permute-start.16 = (bf16[256,256]{1,0:T(8,128)(2,1)S(1)}, bf16[256,256]{1,0:T(8,128)(2,1)S(1)}, u32[]{:S(2)}, u32[]{:S(2)}) collective-permute-start(bf16[256,256]{1,0:T(8,128)(2,1)S(1)} %get-tuple-element.41), channel_id=1, source_target_pairs={{0,4},{1,5},{2,6},{3,7},{4,0},{5,1},{6,2},{7,3},{8,12},{9,13},{10,... | collective-permute-start | bytes 393224 | tf_op jit(solution)/shard_map/ppermute | solution.py:366
  57.9 3.9 %collective-permute-done.14.refs_0_ = bf16[256,256]{1,0:T(8,128)(2,1)S(1)} collective-permute-done((bf16[256,256]{1,0:T(8,128)(2,1)S(1)}, bf16[256,256]{1,0:T(8,128)(2,1)S(1)}, u32[]{:S(2)}, u32[]{:S(2)}) %collective-permute-start.14) | collective-permute-done | bytes 131104 | tf_op jit(solution)/shard_map/ppermute | solution.py:366
  61.8 4.7 %collective-permute-done.15.refs_1_ = bf16[256,256]{1,0:T(8,128)(2,1)S(1)} collective-permute-done((bf16[256,256]{1,0:T(8,128)(2,1)S(1)}, bf16[256,256]{1,0:T(8,128)(2,1)S(1)}, u32[]{:S(2)}, u32[]{:S(2)}) %collective-permute-start.15) | collective-permute-done | bytes 131104 | tf_op jit(solution)/shard_map/ppermute | solution.py:366
  66.5 0.0 collective-permute-done.16.refs_2_
  66.5 0.7 %shard_map.83 = (f32[192,256]{1,0:T(8,128)}, f32[64,256]{1,0:T(8,128)}) custom-call(f32[256,256]{1,0:T(8,128)S(1)} %get-tuple-element.38.keep_ref, bf16[256,256]{1,0:T(8,128)(2,1)S(1)} %collective-permute-done.14.refs_0_, bf16[256,256]{1,0:T(8,128)(2,1)S(1)} %collective-permute-done.15.refs_1_, bf16[256,256]{1,0:T(8,128)(2,1)S(1)} %collective-permute-done.16.refs_2_), custom_call_target="tpu_custom_call" | custom-call | tf_op jit(solution)/shard_map/pallas_call | solution.py:343
Async XLA Ops:
  2.2 10.2 %collective-permute-start.3 = (bf16[272,256]{1,0:T(8,128)(2,1)S(1)}, bf16[272,256]{1,0:T(8,128)(2,1)S(1)}, u32[]{:S(2)}, u32[]{:S(2)}) collective-permute-start(bf16[272,256]{1,0:T(8,128)(2,1)S(1)} %shard_map.78.refs_4_), channel_id=1, source_target_pairs={{0,12},{1,13},{2,14},{3,15},{4,8},{5,9},{6,10},{7,11},{8,4},{9,5},... | collective-permute-start | bytes 417800 | tf_op jit(solution)/shard_map/ppermute | solution.py:366
  9.3 10.5 %collective-permute-start = (bf16[2,64,1024]{2,1,0:T(8,128)(2,1)S(1)}, bf16[2,64,1024]{2,1,0:T(8,128)(2,1)S(1)}, u32[]{:S(2)}, u32[]{:S(2)}) collective-permute-start(bf16[2,64,1024]{2,1,0:T(8,128)(2,1)S(1)} %get-tuple-element.24), channel_id=1, source_target_pairs={{0,3},{1,2},{2,1},{3,0},{4,7},{5,6},{6,5},{7,4},{8,11},{9,10},{10,... | collective-permute-start | bytes 786440 | tf_op jit(solution)/shard_map/ppermute | solution.py:373
  11.9 11.8 %collective-permute-start.1 = (bf16[2,64,1024]{2,1,0:T(8,128)(2,1)S(1)}, bf16[2,64,1024]{2,1,0:T(8,128)(2,1)S(1)}, u32[]{:S(2)}, u32[]{:S(2)}) collective-permute-start(bf16[2,64,1024]{2,1,0:T(8,128)(2,1)S(1)} %get-tuple-element.25), channel_id=1, source_target_pairs={{0,2},{1,3},{2,0},{3,1},{4,6},{5,7},{6,4},{7,5},{8,10},{9,11},{10,... | collective-permute-start | bytes 786440 | tf_op jit(solution)/shard_map/ppermute | solution.py:373
  12.4 7.5 %collective-permute-start.5 = (bf16[272,256]{1,0:T(8,128)(2,1)S(1)}, bf16[272,256]{1,0:T(8,128)(2,1)S(1)}, u32[]{:S(2)}, u32[]{:S(2)}) collective-permute-start(bf16[272,256]{1,0:T(8,128)(2,1)S(1)} %shard_map.78.refs_4_), channel_id=1, source_target_pairs={{0,8},{1,9},{2,10},{3,11},{4,12},{5,13},{6,14},{7,15},{8,0},{9,1},... | collective-permute-start | bytes 417800 | tf_op jit(solution)/shard_map/ppermute | solution.py:366
  12.4 11.3 %collective-permute-start.4 = (bf16[272,256]{1,0:T(8,128)(2,1)S(1)}, bf16[272,256]{1,0:T(8,128)(2,1)S(1)}, u32[]{:S(2)}, u32[]{:S(2)}) collective-permute-start(bf16[272,256]{1,0:T(8,128)(2,1)S(1)} %shard_map.78.refs_4_), channel_id=1, source_target_pairs={{0,4},{1,5},{2,6},{3,7},{4,0},{5,1},{6,2},{7,3},{8,12},{9,13},{10,... | collective-permute-start | bytes 417800 | tf_op jit(solution)/shard_map/ppermute | solution.py:366
  13.7 10.5 %collective-permute-start.2 = (bf16[2,64,1024]{2,1,0:T(8,128)(2,1)S(1)}, bf16[2,64,1024]{2,1,0:T(8,128)(2,1)S(1)}, u32[]{:S(2)}, u32[]{:S(2)}) collective-permute-start(bf16[2,64,1024]{2,1,0:T(8,128)(2,1)S(1)} %get-tuple-element.26), channel_id=1, source_target_pairs={{0,1},{1,0},{2,3},{3,2},{4,5},{5,4},{6,7},{7,6},{8,9},{9,8},{10,11... | collective-permute-start | bytes 786440 | tf_op jit(solution)/shard_map/ppermute | solution.py:373
  19.9 4.4 %collective-permute-start.6 = (bf16[272,256]{1,0:T(8,128)(2,1)S(1)}, bf16[272,256]{1,0:T(8,128)(2,1)S(1)}, u32[]{:S(2)}, u32[]{:S(2)}) collective-permute-start(bf16[272,256]{1,0:T(8,128)(2,1)S(1)} %shard_map.78.refs_4_), channel_id=1, source_target_pairs={{0,16},{16,0},{1,17},{17,1},{2,18},{18,2},{3,19},{19,3},{4,20},{20... | collective-permute-start | bytes 417800 | tf_op jit(solution)/shard_map/ppermute | solution.py:369
  19.9 4.3 %collective-permute-start.8 = (bf16[272,256]{1,0:T(8,128)(2,1)S(1)}, bf16[272,256]{1,0:T(8,128)(2,1)S(1)}, u32[]{:S(2)}, u32[]{:S(2)}) collective-permute-start(bf16[272,256]{1,0:T(8,128)(2,1)S(1)} %collective-permute-done.5.refs_6_), channel_id=1, source_target_pairs={{0,16},{16,0},{1,17},{17,1},{2,18},{18,2},{3,19},{19,3},{4,20},{20... | collective-permute-start | bytes 417800 | tf_op jit(solution)/shard_map/ppermute | solution.py:369
  23.7 1.4 %collective-permute-start.9 = (bf16[272,256]{1,0:T(8,128)(2,1)S(1)}, bf16[272,256]{1,0:T(8,128)(2,1)S(1)}, u32[]{:S(2)}, u32[]{:S(2)}) collective-permute-start(bf16[272,256]{1,0:T(8,128)(2,1)S(1)} %collective-permute-done.3.refs_7_), channel_id=1, source_target_pairs={{0,16},{16,0},{1,17},{17,1},{2,18},{18,2},{3,19},{19,3},{4,20},{20... | collective-permute-start | bytes 417800 | tf_op jit(solution)/shard_map/ppermute | solution.py:369
  23.7 1.5 %collective-permute-start.7 = (bf16[272,256]{1,0:T(8,128)(2,1)S(1)}, bf16[272,256]{1,0:T(8,128)(2,1)S(1)}, u32[]{:S(2)}, u32[]{:S(2)}) collective-permute-start(bf16[272,256]{1,0:T(8,128)(2,1)S(1)} %collective-permute-done.4.refs_5_), channel_id=1, source_target_pairs={{0,16},{16,0},{1,17},{17,1},{2,18},{18,2},{3,19},{19,3},{4,20},{20... | collective-permute-start | bytes 417800 | tf_op jit(solution)/shard_map/ppermute | solution.py:369
  26.8 6.9 %collective-permute-start.10 = (bf16[64,896]{1,0:T(8,128)(2,1)S(1)}, bf16[64,896]{1,0:T(8,128)(2,1)S(1)}, u32[]{:S(2)}, u32[]{:S(2)}) collective-permute-start(bf16[64,896]{1,0:T(8,128)(2,1)S(1)} %get-tuple-element.28), channel_id=1, source_target_pairs={{0,3},{1,2},{2,1},{3,0},{4,7},{5,6},{6,5},{7,4},{8,11},{9,10},{10,... | collective-permute-start | bytes 344072 | tf_op jit(solution)/shard_map/ppermute | solution.py:373
  28.7 7.0 %collective-permute-start.11 = (bf16[64,896]{1,0:T(8,128)(2,1)S(1)}, bf16[64,896]{1,0:T(8,128)(2,1)S(1)}, u32[]{:S(2)}, u32[]{:S(2)}) collective-permute-start(bf16[64,896]{1,0:T(8,128)(2,1)S(1)} %get-tuple-element.29), channel_id=1, source_target_pairs={{0,2},{1,3},{2,0},{3,1},{4,6},{5,7},{6,4},{7,5},{8,10},{9,11},{10,... | collective-permute-start | bytes 344072 | tf_op jit(solution)/shard_map/ppermute | solution.py:373
  29.9 5.8 %copy-start = (s32[2,1,2]{2,1,0:T(1,128)S(1)}, s32[2,1,2]{2,1,0:T(1,128)}, u32[]{:S(2)}) copy-start(s32[2,1,2]{2,1,0:T(1,128)} %docs.1) | copy-start | bytes 52
  29.9 5.8 %collective-permute-start.12 = (bf16[64,896]{1,0:T(8,128)(2,1)S(1)}, bf16[64,896]{1,0:T(8,128)(2,1)S(1)}, u32[]{:S(2)}, u32[]{:S(2)}) collective-permute-start(bf16[64,896]{1,0:T(8,128)(2,1)S(1)} %get-tuple-element.30), channel_id=1, source_target_pairs={{0,1},{1,0},{2,3},{3,2},{4,5},{5,4},{6,7},{7,6},{8,9},{9,8},{10,11... | collective-permute-start | bytes 344072 | tf_op jit(solution)/shard_map/ppermute | solution.py:373
  50.8 2.0 %collective-permute-start.13 = (bf16[4,256,256]{2,1,0:T(8,128)(2,1)S(1)}, bf16[4,256,256]{2,1,0:T(8,128)(2,1)S(1)}, u32[]{:S(2)}, u32[]{:S(2)}) collective-permute-start(bf16[4,256,256]{2,1,0:T(8,128)(2,1)S(1)} %get-tuple-element.37), channel_id=1, source_target_pairs={{0,16},{16,0},{1,17},{17,1},{2,18},{18,2},{3,19},{19,3},{4,20},{20... | collective-permute-start | bytes 1572872 | tf_op jit(solution)/shard_map/ppermute | solution.py:369
  53.4 8.3 %collective-permute-start.14 = (bf16[256,256]{1,0:T(8,128)(2,1)S(1)}, bf16[256,256]{1,0:T(8,128)(2,1)S(1)}, u32[]{:S(2)}, u32[]{:S(2)}) collective-permute-start(bf16[256,256]{1,0:T(8,128)(2,1)S(1)} %get-tuple-element.39), channel_id=1, source_target_pairs={{0,12},{1,13},{2,14},{3,15},{4,8},{5,9},{6,10},{7,11},{8,4},{9,5},... | collective-permute-start | bytes 393224 | tf_op jit(solution)/shard_map/ppermute | solution.py:366
  53.9 12.5 %collective-permute-start.15 = (bf16[256,256]{1,0:T(8,128)(2,1)S(1)}, bf16[256,256]{1,0:T(8,128)(2,1)S(1)}, u32[]{:S(2)}, u32[]{:S(2)}) collective-permute-start(bf16[256,256]{1,0:T(8,128)(2,1)S(1)} %get-tuple-element.40), channel_id=1, source_target_pairs={{0,8},{1,9},{2,10},{3,11},{4,12},{5,13},{6,14},{7,15},{8,0},{9,1},... | collective-permute-start | bytes 393224 | tf_op jit(solution)/shard_map/ppermute | solution.py:366
  54.5 12.0 %collective-permute-start.16 = (bf16[256,256]{1,0:T(8,128)(2,1)S(1)}, bf16[256,256]{1,0:T(8,128)(2,1)S(1)}, u32[]{:S(2)}, u32[]{:S(2)}) collective-permute-start(bf16[256,256]{1,0:T(8,128)(2,1)S(1)} %get-tuple-element.41), channel_id=1, source_target_pairs={{0,4},{1,5},{2,6},{3,7},{4,0},{5,1},{6,2},{7,3},{8,12},{9,13},{10,... | collective-permute-start | bytes 393224 | tf_op jit(solution)/shard_map/ppermute | solution.py:366

commit v9 on v6

--- a/solution.py
+++ b/solution.py
@@ -125,23 +125,19 @@
     return lax.dot_general(a, b, (((1,), (1,)), ((), ())), preferred_element_type=F32)
 
 
-def pack_kernel(index, gain_ref, qkv_ref, wout_ref, pack_ref, row_ref, sems):
-    qkv_rows, heads, width = qkv_ref.shape[0], wout_ref.shape[0], qkv_ref.shape[1]
-    at = pl.multiple_of((index[1] * PLANE + index[2]) * width, width)
+def pack_kernel(qkv_ref, wout_ref, pack_ref, sems):
+    qkv_rows = qkv_ref.shape[0]
     copies = [
-        pltpu.make_async_copy(gain_ref.at[:, pl.ds(at, width)], row_ref, sems.at[0]),
-        pltpu.make_async_copy(qkv_ref, pack_ref.at[:qkv_rows], sems.at[1]),
-        pltpu.make_async_copy(wout_ref, pack_ref.at[qkv_rows : qkv_rows + heads], sems.at[2]),
+        pltpu.make_async_copy(qkv_ref, pack_ref.at[:qkv_rows], sems.at[0]),
+        pltpu.make_async_copy(wout_ref, pack_ref.at[qkv_rows:], sems.at[1]),
     ]
     for copy in copies:
         copy.start()
-    copies[0].wait()
-    pack_ref[qkv_rows + heads :, :] = jnp.broadcast_to(row_ref[...].astype(F32), (STATS, width)).astype(BF16)
-    copies[1].wait()
-    copies[2].wait()
-
-
-def blocks_kernel(planes, index, x_ref, c_ref, *refs):
+    for copy in copies:
+        copy.wait()
+
+
+def blocks_kernel(planes, index, x_ref, *refs):
     out_refs, sems = refs[:PLANE], refs[PLANE]
     width = x_ref.shape[-1] // (planes * PLANE)
     section, p = index[0], index[2]
@@ -149,14 +145,13 @@
     for k in range(PLANE):
         for z in range(planes):
             at = pl.multiple_of((z * PLANE + (p ^ k)) * width, width)
-            for half, ref in enumerate((x_ref, c_ref)):
-                copies.append(
-                    pltpu.make_async_copy(
-                        ref.at[section, :, pl.ds(at, width)],
-                        out_refs[k].at[half, :, pl.ds(z * width, width)],
-                        sems.at[len(copies)],
-                    )
+            copies.append(
+                pltpu.make_async_copy(
+                    x_ref.at[section, :, pl.ds(at, width)],
+                    out_refs[k].at[:, pl.ds(z * width, width)],
+                    sems.at[len(copies)],
                 )
+            )
     for copy in copies:
         copy.start()
     for copy in copies:
@@ -165,63 +160,67 @@
 
 def project_kernel(planes, heads, index, *refs):
     blocks, own, other = refs[:PLANE], refs[PLANE : PLANE + planes], refs[PLANE + planes : PLANE + 2 * planes]
-    x_ref, c_ref, vx_ref, gain_ref = refs[PLANE + 2 * planes : PLANE + 2 * planes + 4]
-    out_refs = refs[PLANE + 2 * planes + 4 : -2]
-    vc_ref, sum_ref = refs[-2:]
+    gain_refs = refs[PLANE + 2 * planes : PLANE + 2 * planes + 2]
+    x_ref, vx_ref, vc_ref, gain_ref = refs[PLANE + 2 * planes + 2 : PLANE + 2 * planes + 6]
+    out_refs, sum_ref = refs[PLANE + 2 * planes + 6 : -1], refs[-1]
     qkv, width = 3 * heads, vx_ref.shape[-1]
-    section, z, p = index[0], index[1], index[2]
+    section, place, p = index[0], index[1], index[2]
+    for z in range(planes):
+        mine, theirs = (ref[pl.ds(z * PLANE + p, 1), :] for ref in gain_refs)
+        gain_ref[z, 0:1, :] = jnp.where(section == 0, mine, theirs)
+        gain_ref[z, 1:2, :] = jnp.where(section == 0, theirs, mine)
     for k in range(planes):
-        at = z ^ k
+        at = place ^ k
         zero = jnp.where(section == 0, own[k][...], other[k][...])
         one = jnp.where(section == 0, other[k][...], own[k][...])
-        gains = [w[qkv + heads :].astype(F32)[0:1] for w in (zero, one)]
-        gain_ref[at, 0:1, :] = gains[0]
-        gain_ref[at, 1:2, :] = gains[1]
-        empty = jnp.zeros((heads, width), BF16)
-        vx_ref[at, :qkv, :] = (zero[:qkv].astype(F32) * gains[0]).astype(BF16)
-        vx_ref[at, qkv : qkv + heads, :] = zero[qkv : qkv + heads]
-        vx_ref[at, qkv + heads : 2 * qkv + heads, :] = (one[:qkv].astype(F32) * gains[1]).astype(BF16)
-        vx_ref[at, 2 * qkv + heads :, :] = empty
-        vc_ref[at, :heads, :] = empty
-        vc_ref[at, heads : 2 * heads, :] = one[qkv : qkv + heads]
-        vc_ref[at, 2 * heads : 3 * heads, :] = zero[qkv : qkv + heads]
-        vc_ref[at, 3 * heads :, :] = empty
-    for k in range(PLANE):
-        x_ref[p ^ k] = blocks[-k][0]
-        c_ref[p ^ k] = blocks[-k][1]
+        vx_ref[at, :qkv, :] = (zero[:qkv].astype(F32) * gain_ref[at, 0:1, :]).astype(BF16)
+        vx_ref[at, qkv : qkv + heads, :] = zero[qkv:]
+        vx_ref[at, qkv + heads : 2 * qkv + heads, :] = (one[:qkv].astype(F32) * gain_ref[at, 1:2, :]).astype(BF16)
+        vx_ref[at, 2 * qkv + heads :, :] = jnp.zeros((heads, width), BF16)
+        vc_ref[at, :heads, :] = one[qkv:]
+        vc_ref[at, heads:, :] = zero[qkv:]
+    for k in range(PLANE):
+        x_ref[p ^ k] = blocks[-k][...]
     rows = x_ref.shape[0] * x_ref.shape[1]
-    with_x = with_c = squares = products = None
+    with_x = squares = products = None
     for z in range(planes):
-        cols = slice(z * width, (z + 1) * width)
-        x = x_ref[:, :, cols].reshape(rows, width)
-        c = c_ref[:, :, cols].reshape(rows, width)
+        x = x_ref[:, :, z * width : (z + 1) * width].reshape(rows, width)
         wide = x.astype(F32)
         out = vx_ref[z, qkv : qkv + heads, :]
         right = jnp.concatenate([vx_ref[z, qkv + heads : 2 * qkv + heads, :], out], axis=0)
-        new = nt(x, vx_ref[z]), nt(c, vc_ref[z]), jnp.sum(wide * wide, axis=1, keepdims=True), nt(out, right)
+        new = nt(x, vx_ref[z]), jnp.sum(wide * wide, axis=1, keepdims=True), nt(out, right)
         if with_x is None:
-            with_x, with_c, squares, products = new
+            with_x, squares, products = new
         else:
-            with_x, with_c = with_x + new[0], with_c + new[1]
-            squares, products = squares + new[2], products + new[3]
+            with_x, squares, products = with_x + new[0], squares + new[1], products + new[2]
     half = 2 * heads
     lane = lax.broadcasted_iota(jnp.int32, (rows, half), 1)
     high = squares.astype(BF16).astype(F32)
-    last = jnp.where(lane == heads, high, jnp.where(lane == heads + 1, squares - high, with_c[:, half:]))
+    last = jnp.where(lane == heads, high, jnp.where(lane == heads + 1, squares - high, with_x[:, 3 * half :]))
     sum_ref[:, : 3 * half] = with_x[:, : 3 * half].astype(BF16)
-    sum_ref[:, 3 * half : 4 * half] = (with_x[:, 3 * half :] + with_c[:, :half]).astype(BF16)
-    sum_ref[:, 4 * half :] = last.astype(BF16)
+    sum_ref[:, 3 * half :] = last.astype(BF16)
     block = rows // PLANE
     for k in range(PLANE):
         start = pl.multiple_of((p ^ k) * block, block)
-        out_refs[k][:, : 5 * half] = sum_ref[pl.ds(start, block), :]
-        out_refs[k][:, 5 * half :] = products.astype(BF16)
-
-
-def exact(a, b, dims):
-    return lax.dot_general(
-        a, b, (dims, ((), ())), precision=lax.Precision.HIGHEST, preferred_element_type=F32
-    )
+        out_refs[k][:, : 4 * half] = sum_ref[pl.ds(start, block), :]
+        out_refs[k][:, 4 * half :] = products.astype(BF16)
+
+
+def cotangent_kernel(planes, index, *refs):
+    blocks, vc_ref, c_ref = refs[:PLANE], refs[PLANE], refs[PLANE + 1]
+    out_refs, sum_ref = refs[PLANE + 2 : -1], refs[-1]
+    p, width = index[2], vc_ref.shape[-1]
+    for k in range(PLANE):
+        c_ref[p ^ k] = blocks[-k][...]
+    rows = c_ref.shape[0] * c_ref.shape[1]
+    total = None
+    for z in range(planes):
+        part = nt(c_ref[:, :, z * width : (z + 1) * width].reshape(rows, width), vc_ref[z])
+        total = part if total is None else total + part
+    sum_ref[...] = total.astype(BF16)
+    block = rows // PLANE
+    for k in range(PLANE):
+        out_refs[k][...] = sum_ref[pl.ds(pl.multiple_of((p ^ k) * block, block), block), :]
 
 
 def attention(qkv, allowed, heads):
@@ -232,23 +231,27 @@
     return probs, nn(probs.astype(BF16), values).astype(BF16)
 
 
-def attention_grad(qkv, probs, d_att, heads):
+def attention_grad(qkv, probs, att, d_att, heads):
     query, keys, values = (qkv[:, i * heads : (i + 1) * heads].astype(BF16) for i in range(3))
+    inner = jnp.sum(att.astype(F32) * d_att.astype(F32), axis=1, keepdims=True)
     d_values = nn(jnp.transpose(probs).astype(BF16), d_att)
-    d_probs = nt(d_att, values).astype(BF16).astype(F32)
-    inner = jnp.sum(probs * d_probs, axis=1, keepdims=True)
-    d_scores = probs * (d_probs - inner) * heads ** (-0.5)
+    d_scores = probs * (nt(d_att, values) - inner) * heads ** (-0.5)
     d_query = nn(d_scores.astype(BF16), keys)
     d_keys = nn(jnp.transpose(d_scores).astype(BF16), query)
     return jnp.concatenate([d_query, d_keys, d_values], axis=1).astype(BF16).astype(F32)
 
 
-def chain_kernel(features, heads, index, docs, *refs):
-    parts, out_ref = refs[:-1], refs[-1]
-    qkv, half = 3 * heads, 2 * heads
+def summed(parts):
     total = parts[0][...].astype(F32)
     for part in parts[1:]:
         total = total + part[...].astype(F32)
+    return total
+
+
+def chain_kernel(features, heads, index, docs, *refs):
+    out_ref = refs[-1]
+    qkv, half = 3 * heads, 2 * heads
+    total, from_c = summed(refs[:PLANE]), summed(refs[PLANE:-1])
     rows = total.shape[0]
     section = index[0]
     query_at = lax.broadcasted_iota(jnp.int32, (rows, rows), 0)
@@ -260,28 +263,27 @@
         allowed = allowed & ((query_at >= end) == (key_at >= end))
     x_out = total[:, qkv : 2 * half]
     x_one = total[:, 2 * half : 2 * half + qkv]
-    c_one = total[:, 4 * half - heads : 4 * half].astype(BF16)
-    tail = total[:, 4 * half : 5 * half]
-    c_zero = tail[:, :heads]
+    tail = total[:, 3 * half : 4 * half]
     lane = lax.broadcasted_iota(jnp.int32, tail.shape, 1)
     squares = jnp.sum(jnp.where((lane == heads) | (lane == heads + 1), tail, 0.0), axis=1, keepdims=True)
-    mixed = total[:, 5 * half : 5 * half + qkv]
-    gram = total[:, 5 * half + qkv :]
+    mixed = total[:, 4 * half : 4 * half + qkv].astype(BF16)
+    gram = total[:, 4 * half + qkv :].astype(BF16)
+    c_one, c_zero = from_c[:, :heads].astype(BF16), from_c[:, heads:]
 
     scale0 = lax.rsqrt(squares / features + 1e-05)
     qkv0 = (total[:, :qkv] * scale0).astype(BF16).astype(F32)
     probs0, att0 = attention(qkv0, allowed, heads)
     wide0 = att0.astype(F32)
-    y_out = x_out + exact(wide0, gram, ((1,), (0,)))
+    y_out = x_out + nn(att0, gram)
     squares = squares + jnp.sum(wide0 * (x_out + y_out), axis=1, keepdims=True)
     scale1 = lax.rsqrt(jnp.maximum(squares, 0.0) / features + 1e-05)
-    qkv1 = ((x_one + exact(wide0, mixed, ((1,), (0,)))) * scale1).astype(BF16).astype(F32)
+    qkv1 = ((x_one + nn(att0, mixed)) * scale1).astype(BF16).astype(F32)
     probs1, att1 = attention(qkv1, allowed, heads)
-    d_qkv1 = attention_grad(qkv1, probs1, c_one, heads)
+    d_qkv1 = attention_grad(qkv1, probs1, att1, c_one, heads)
     inner = jnp.sum(d_qkv1 * qkv1, axis=1, keepdims=True) * scale1 * scale1 / features
     e1 = d_qkv1 * scale1
-    d_att0 = c_zero + exact(e1, mixed, ((1,), (1,))) - inner * y_out
-    e0 = attention_grad(qkv0, probs0, d_att0.astype(BF16), heads) * scale0
+    d_att0 = c_zero + nt(e1.astype(BF16), mixed) - inner * y_out
+    e0 = attention_grad(qkv0, probs0, att0, d_att0.astype(BF16), heads) * scale0
     factors = [e0, wide0, e1, wide0 * inner, att1.astype(F32), jnp.zeros((rows, heads), F32)]
     out_ref[...] = jnp.concatenate(factors, axis=1).astype(BF16)
 
@@ -379,46 +381,59 @@
     smem, vmem = pl.BlockSpec(memory_space=pltpu.SMEM), pl.BlockSpec(memory_space=pltpu.VMEM)
     hbm = pl.BlockSpec(memory_space=pltpu.HBM)
     params = pltpu.CompilerParams(vmem_limit_bytes=VMEM_LIMIT)
-    gain, qkv_in, out_in, x_in, c_in = [
+    qkv_in, out_in, x_in, c_in = [
         pltpu.with_memory_space_constraint(value, pltpu.HBM)
-        for value in (norm_gain, w_qkv[0].T, w_out[0], inputs, cotangent)
+        for value in (w_qkv[0].T, w_out[0], inputs, cotangent)
     ]
     pack = pl.pallas_call(
         pack_kernel,
-        out_shape=jax.ShapeDtypeStruct((qkv_rows + heads + STATS, width), BF16),
-        in_specs=[smem] + [hbm] * 3,
+        out_shape=jax.ShapeDtypeStruct((qkv_rows + heads, width), BF16),
+        in_specs=[hbm] * 2,
         out_specs=vmem,
-        scratch_shapes=[pltpu.VMEM((1, width), BF16), pltpu.SemaphoreType.DMA((3,))],
+        scratch_shapes=[pltpu.SemaphoreType.DMA((2,))],
         compiler_params=params,
-    )(index, gain, qkv_in, out_in)
-    blocks = pl.pallas_call(
+    )(qkv_in, out_in)
+    split_blocks = pl.pallas_call(
         functools.partial(blocks_kernel, planes),
-        out_shape=[jax.ShapeDtypeStruct((2, block, cols), BF16)] * PLANE,
-        in_specs=[smem] + [hbm] * 2,
+        out_shape=[jax.ShapeDtypeStruct((block, cols), BF16)] * PLANE,
+        in_specs=[smem, hbm],
         out_specs=[vmem] * PLANE,
-        scratch_shapes=[pltpu.SemaphoreType.DMA((2 * PLANE * planes,))],
+        scratch_shapes=[pltpu.SemaphoreType.DMA((PLANE * planes,))],
         compiler_params=params,
-    )(index, x_in, c_in)
-    blocks = [blocks[0]] + far_first(blocks, PLANE, along_plane)[1:]
+    )
+
+    def swapped(value):
+        out = split_blocks(index, value)
+        return [out[0]] + far_first(out, PLANE, along_plane)[:0:-1]
+
     far = {k: along_z(pack, k) for k in reversed(range(2, planes))}
-    later, _ = lax.optimization_barrier((pack, far[planes - 1] if far else pack))
+    x_blocks, c_blocks = swapped(x_in), swapped(c_in)
+    later, late_gain, _ = lax.optimization_barrier((pack, norm_gain, far[planes - 1] if far else pack))
     near = [along_z(later, 1)] if planes > 1 else []
-    own = [later] + near + [far[k] for k in range(2, planes)]
-    other = [to_sibling(piece) for piece in own]
+    own = [pack] + near + [far[k] for k in range(2, planes)]
+    other = [to_sibling(piece) for piece in [later] + own[1:]]
+    gains = [value[0].reshape(shards, width).astype(F32) for value in (norm_gain, to_sibling(late_gain))]
 
     split = ((PLANE, block, cols), BF16)
     half = 2 * heads
-    x, c, vx, gains, *sent = call(
+    x, vx, vc, gains, *sent = call(
         functools.partial(project_kernel, planes, heads),
-        [split, split, ((planes, 4 * half, width), BF16), ((planes, 8, width), F32)]
-        + [((block, 7 * half), BF16)] * PLANE,
-        index, blocks[0], *blocks[:0:-1], *own, *other, scalars=1,
-        scratch=[((planes, 2 * half, width), BF16), ((rows, 5 * half), BF16)],
+        [split, ((planes, 4 * half, width), BF16), ((planes, half, width), BF16), ((planes, 8, width), F32)]
+        + [((block, 6 * half), BF16)] * PLANE,
+        index, *x_blocks, *own, *other, *gains, scalars=1,
+        scratch=[((rows, 4 * half), BF16)],
+    )
+    first = exchange(sent)[::-1]
+    c, *sent = call(
+        functools.partial(cotangent_kernel, planes),
+        [split] + [((block, half), BF16)] * PLANE,
+        index, *c_blocks, vc, scalars=1,
+        scratch=[((rows, half), BF16)],
     )
     (factors,) = call(
         functools.partial(chain_kernel, features, heads),
         [((block, 5 * half), BF16)],
-        index, doc_lengths, *exchange(sent)[::-1], scalars=2,
+        index, doc_lengths, *first, *exchange(sent)[::-1], scalars=2,
     )
     grads = (planes, qkv_rows + heads, width)
     keep, send = call(

time: 64.5 us -> 68.3 us (1.059)
  starting transfers between devices: 26.2 us -> 30.2 us
  waiting for transfers between devices: 26 us -> 23.5 us
  Pallas kernels: 11.1 us -> 12.5 us
    ppermute x9 -> x15, starting transfers between devices: 14.2 us -> 18.9 us  [along_plane(): return lax.ppermute(value, 'dp', route)]
    ppermute x6, waiting for transfers between devices: 10.6 us -> 8.84 us  [along_z(): return lax.ppermute(value, 'dp', route)]
    pallas_call x1 -> x2, Pallas kernels: 2.01 us -> 3.38 us  [swapped(): out = split_blocks(index, value)]
    ppermute x5 -> x6, waiting for transfers between devices: 2.93 us -> 1.91 us  [to_sibling(): return lax.ppermute(value, 'section', [(0, 1), (1, 0)])]
    pallas_call x5 -> x6, Pallas kernels: 7.65 us -> 8.24 us  [call(): pl.pallas_call(kernel, out_shape=[jax.ShapeDtypeStruct(shape, dtype) for...]
    ppermute x9 -> x15, waiting for transfers between devices: 12.5 us -> 12.8 us  [along_plane(): return lax.ppermute(value, 'dp', route)]
  transfers between devices with their start and end apart: 20 -> 27, of which waited for: 13 -> 12; matrix products, arithmetic and copies ran while one was open for 0% -> 0% of each run, Pallas kernels for 3% -> 8%
where the time goes in v9:
time: 68.3 us; the launch traced here: 68 us
  starting transfers between devices  30.2 us (44%)
  waiting for transfers between devices  23.5 us (34%)
  Pallas kernels  12.5 us (18%)
  between operations  0.79 us (1%)
  local copies, waits for them, and re-layouts  0.69 us (1%)
    ppermute x15, starting transfers between devices, along_plane(): return lax.ppermute(value, 'dp', route)  18.9 us
    ppermute x15, waiting for transfers between devices, along_plane(): return lax.ppermute(value, 'dp', route)  12.8 us
    ppermute x6, starting transfers between devices, along_z(): return lax.ppermute(value, 'dp', route)  10.3 us
    ppermute x6, waiting for transfers between devices, along_z(): return lax.ppermute(value, 'dp', route)  8.84 us
    pallas_call x6, Pallas kernels, call(): pl.pallas_call(kernel, out_shape=[jax.ShapeDtypeStruct(shape, dtype) for...  8.24 us
    pallas_call x2, Pallas kernels, swapped(): out = split_blocks(index, value)  3.38 us
    ppermute x6, waiting for transfers between devices, to_sibling(): return lax.ppermute(value, 'section', [(0, 1), (1, 0)])  1.91 us
  transfers between devices with their start and end apart: 27, of which 12 were waited for; matrix products, arithmetic and copies ran while one was open for 0% of the time, Pallas kernels for 8%

profile of v9, /device:TPU:0, one launch (start us, length us, event | category | flops | bytes accessed | tf_op | source)
XLA Modules:
  0.0 68.0 jit_solution(8011635432864646591)
XLA Ops:
  0.6 0.9 %shard_map.78.refs_4_ = bf16[256,256]{1,0:T(8,128)(2,1)S(1)} custom-call(bf16[192,256]{1,0:T(8,128)(2,1)} %bitcast.11, bf16[64,256]{1,0:T(8,128)(2,1)} %bitcast.12), custom_call_target="tpu_custom_call" | custom-call | tf_op jit(solution)/shard_map/pallas_call | solution.py:388
  1.6 5.1 %collective-permute-start.3 = (bf16[256,256]{1,0:T(8,128)(2,1)S(1)}, bf16[256,256]{1,0:T(8,128)(2,1)S(1)}, u32[]{:S(2)}, u32[]{:S(2)}) collective-permute-start(bf16[256,256]{1,0:T(8,128)(2,1)S(1)} %shard_map.78.refs_4_), channel_id=1, source_target_pairs={{0,12},{1,13},{2,14},{3,15},{4,8},{5,9},{6,10},{7,11},{8,4},{9,5},... | collective-permute-start | bytes 393224 | tf_op jit(solution)/shard_map/ppermute | solution.py:369
  6.7 0.1 pad_add_fusion.index
  6.7 1.7 %shard_map.77 = (bf16[64,1024]{1,0:T(8,128)(2,1)S(1)}, bf16[64,1024]{1,0:T(8,128)(2,1)S(1)}, bf16[64,1024]{1,0:T(8,128)(2,1)S(1)}, bf16[64,1024]{1,0:T(8,128)(2,1)S(1)}) custom-call(s32[3]{0:T(128)S(1)} %pad_add_fusion.index, bf16[2,64,4096]{2,1,0:T(8,128)(2,1)} %x_ref.2), custom_call_target="tpu_custom_call" | custom-call | tf_op jit(solution)/shard_map/pallas_call | solution.py:406
  8.4 2.5 %collective-permute-start = (bf16[64,1024]{1,0:T(8,128)(2,1)S(1)}, bf16[64,1024]{1,0:T(8,128)(2,1)S(1)}, u32[]{:S(2)}, u32[]{:S(2)}) collective-permute-start(bf16[64,1024]{1,0:T(8,128)(2,1)S(1)} %get-tuple-element.34), channel_id=1, source_target_pairs={{0,3},{1,2},{2,1},{3,0},{4,7},{5,6},{6,5},{7,4},{8,11},{9,10},{10,... | collective-permute-start | bytes 393224 | tf_op jit(solution)/shard_map/ppermute | solution.py:376
  11.0 0.5 collective-permute-start.1
  11.5 0.5 collective-permute-start.2
  12.0 0.0 collective-permute-start.5
  12.0 0.0 collective-permute-done.3.refs_7_
  12.0 0.7 %collective-permute-start.4 = (bf16[256,256]{1,0:T(8,128)(2,1)S(1)}, bf16[256,256]{1,0:T(8,128)(2,1)S(1)}, u32[]{:S(2)}, u32[]{:S(2)}) collective-permute-start(bf16[256,256]{1,0:T(8,128)(2,1)S(1)} %shard_map.78.refs_4_), channel_id=1, source_target_pairs={{0,4},{1,5},{2,6},{3,7},{4,0},{5,1},{6,2},{7,3},{8,12},{9,13},{10,... | collective-permute-start | bytes 393224 | tf_op jit(solution)/shard_map/ppermute | solution.py:369
  12.7 2.2 %collective-permute-done.refs_1_ = bf16[64,1024]{1,0:T(8,128)(2,1)S(1)} collective-permute-done((bf16[64,1024]{1,0:T(8,128)(2,1)S(1)}, bf16[64,1024]{1,0:T(8,128)(2,1)S(1)}, u32[]{:S(2)}, u32[]{:S(2)}) %collective-permute-start) | collective-permute-done | bytes 131104 | tf_op jit(solution)/shard_map/ppermute | solution.py:376
  14.9 0.0 collective-permute-start.6
  14.9 2.3 %collective-permute-done.1.refs_2_ = bf16[64,1024]{1,0:T(8,128)(2,1)S(1)} collective-permute-done((bf16[64,1024]{1,0:T(8,128)(2,1)S(1)}, bf16[64,1024]{1,0:T(8,128)(2,1)S(1)}, u32[]{:S(2)}, u32[]{:S(2)}) %collective-permute-start.1) | collective-permute-done | bytes 131104 | tf_op jit(solution)/shard_map/ppermute | solution.py:376
  17.2 0.0 collective-permute-start.9
  17.2 0.1 collective-permute-done.2.refs_3_
  17.2 0.4 collective-permute-start.10
  17.7 1.7 %shard_map.80 = (bf16[64,1024]{1,0:T(8,128)(2,1)S(1)}, bf16[64,1024]{1,0:T(8,128)(2,1)S(1)}, bf16[64,1024]{1,0:T(8,128)(2,1)S(1)}, bf16[64,1024]{1,0:T(8,128)(2,1)S(1)}) custom-call(s32[3]{0:T(128)S(1)} %pad_add_fusion.index, bf16[2,64,4096]{2,1,0:T(8,128)(2,1)} %x_ref.3), custom_call_target="tpu_custom_call" | custom-call | tf_op jit(solution)/shard_map/pallas_call | solution.py:406
  19.4 0.0 collective-permute-done.5.refs_6_
  19.4 1.9 %collective-permute-start.14 = (bf16[64,1024]{1,0:T(8,128)(2,1)S(1)}, bf16[64,1024]{1,0:T(8,128)(2,1)S(1)}, u32[]{:S(2)}, u32[]{:S(2)}) collective-permute-start(bf16[64,1024]{1,0:T(8,128)(2,1)S(1)} %get-tuple-element.44), channel_id=1, source_target_pairs={{0,3},{1,2},{2,1},{3,0},{4,7},{5,6},{6,5},{7,4},{8,11},{9,10},{10,... | collective-permute-start | bytes 393224 | tf_op jit(solution)/shard_map/ppermute | solution.py:376
  21.3 0.0 collective-permute-done.10
  21.3 0.0 collective-permute-start.8
  21.3 0.0 collective-permute-done.4.refs_5_
  21.3 0.5 collective-permute-start.7
  21.9 0.0 collective-permute-done.6.refs_8_
  21.9 1.2 %collective-permute-start.15 = (bf16[64,1024]{1,0:T(8,128)(2,1)S(1)}, bf16[64,1024]{1,0:T(8,128)(2,1)S(1)}, u32[]{:S(2)}, u32[]{:S(2)}) collective-permute-start(bf16[64,1024]{1,0:T(8,128)(2,1)S(1)} %get-tuple-element.45), channel_id=1, source_target_pairs={{0,2},{1,3},{2,0},{3,1},{4,6},{5,7},{6,4},{7,5},{8,10},{9,11},{10,... | collective-permute-start | bytes 393224 | tf_op jit(solution)/shard_map/ppermute | solution.py:376
  23.1 0.0 collective-permute-done.9.refs_11_
  23.1 0.5 collective-permute-start.16
  23.7 0.0 collective-permute-done.8.refs_10_
  23.7 1.4 %shard_map.79 = (bf16[4,64,1024]{2,1,0:T(8,128)(2,1)S(1)}, bf16[4,512,256]{2,1,0:T(8,128)(2,1)S(1)}, bf16[4,128,256]{2,1,0:T(8,128)(2,1)S(1)}, f32[4,8,256]{2,1,...) custom-call(s32[3]{0:T(128)S(1)} %pad_add_fusion.index, ...), custom_call_target="tpu_custom_call" | custom-call | tf_op jit(solution)/shard_map/pallas_call | solution.py:346
  25.1 1.9 %collective-permute-start.11 = (bf16[64,768]{1,0:T(8,128)(2,1)S(1)}, bf16[64,768]{1,0:T(8,128)(2,1)S(1)}, u32[]{:S(2)}, u32[]{:S(2)}) collective-permute-start(bf16[64,768]{1,0:T(8,128)(2,1)S(1)} %get-tuple-element.39), channel_id=1, source_target_pairs={{0,3},{1,2},{2,1},{3,0},{4,7},{5,6},{6,5},{7,4},{8,11},{9,10},{10,... | collective-permute-start | bytes 294920 | tf_op jit(solution)/shard_map/ppermute | solution.py:376
  27.1 1.1 %collective-permute-start.12 = (bf16[64,768]{1,0:T(8,128)(2,1)S(1)}, bf16[64,768]{1,0:T(8,128)(2,1)S(1)}, u32[]{:S(2)}, u32[]{:S(2)}) collective-permute-start(bf16[64,768]{1,0:T(8,128)(2,1)S(1)} %get-tuple-element.40), channel_id=1, source_target_pairs={{0,2},{1,3},{2,0},{3,1},{4,6},{5,7},{6,4},{7,5},{8,10},{9,11},{10,... | collective-permute-start | bytes 294920 | tf_op jit(solution)/shard_map/ppermute | solution.py:376
  28.2 0.0 collective-permute-done.14.refs_1_
  28.2 0.5 collective-permute-start.13
  28.7 0.4 collective-permute-done.15.refs_2_
  29.1 0.9 %shard_map.81 = (bf16[4,64,1024]{2,1,0:T(8,128)(2,1)S(1)}, bf16[64,128]{1,0:T(8,128)(2,1)S(1)}, bf16[64,128]{1,0:T(8,128)(2,1)S(1)}, bf16[64,128]{1,0:T(8,128)(2,1)S(1)}, bf16[64,128]{1,0:T(8,128)(2,1)S(1)}) custom-call(s32[3]{0:T(128)S(1)} %pad_add_fusion.index, bf16[64,1024]{1,0:T(8,128)(2,1)S(1)} %get-tuple-element.43.refs_0_, ...), custom_call_target="tpu_custom_call" | custom-call | tf_op jit(solution)/shard_map/pallas_call | solution.py:346
  29.9 1.7 %collective-permute-start.17 = (bf16[64,128]{1,0:T(8,128)(2,1)S(1)}, bf16[64,128]{1,0:T(8,128)(2,1)S(1)}, u32[]{:S(2)}, u32[]{:S(2)}) collective-permute-start(bf16[64,128]{1,0:T(8,128)(2,1)S(1)} %get-tuple-element.48), channel_id=1, source_target_pairs={{0,3},{1,2},{2,1},{3,0},{4,7},{5,6},{6,5},{7,4},{8,11},{9,10},{10,... | collective-permute-start | bytes 49160 | tf_op jit(solution)/shard_map/ppermute | solution.py:376
  31.7 1.4 %collective-permute-start.18 = (bf16[64,128]{1,0:T(8,128)(2,1)S(1)}, bf16[64,128]{1,0:T(8,128)(2,1)S(1)}, u32[]{:S(2)}, u32[]{:S(2)}) collective-permute-start(bf16[64,128]{1,0:T(8,128)(2,1)S(1)} %get-tuple-element.49), channel_id=1, source_target_pairs={{0,2},{1,3},{2,0},{3,1},{4,6},{5,7},{6,4},{7,5},{8,10},{9,11},{10,... | collective-permute-start | bytes 49160 | tf_op jit(solution)/shard_map/ppermute | solution.py:376
  33.0 1.6 %collective-permute-done.17.refs_4_ = bf16[64,128]{1,0:T(8,128)(2,1)S(1)} collective-permute-done((bf16[64,128]{1,0:T(8,128)(2,1)S(1)}, bf16[64,128]{1,0:T(8,128)(2,1)S(1)}, u32[]{:S(2)}, u32[]{:S(2)}) %collective-permute-start.17) | collective-permute-done | bytes 16416 | tf_op jit(solution)/shard_map/ppermute | solution.py:376
  34.7 1.6 %collective-permute-start.19 = (bf16[64,128]{1,0:T(8,128)(2,1)S(1)}, bf16[64,128]{1,0:T(8,128)(2,1)S(1)}, u32[]{:S(2)}, u32[]{:S(2)}) collective-permute-start(bf16[64,128]{1,0:T(8,128)(2,1)S(1)} %get-tuple-element.50), channel_id=1, source_target_pairs={{0,1},{1,0},{2,3},{3,2},{4,5},{5,4},{6,7},{7,6},{8,9},{9,8},{10,11... | collective-permute-start | bytes 49160 | tf_op jit(solution)/shard_map/ppermute | solution.py:376
  36.2 0.0 collective-permute-done.18.refs_5_
  36.2 2.2 %collective-permute-done.19.refs_6_ = bf16[64,128]{1,0:T(8,128)(2,1)S(1)} collective-permute-done((bf16[64,128]{1,0:T(8,128)(2,1)S(1)}, bf16[64,128]{1,0:T(8,128)(2,1)S(1)}, u32[]{:S(2)}, u32[]{:S(2)}) %collective-permute-start.19) | collective-permute-done | bytes 16416 | tf_op jit(solution)/shard_map/ppermute | solution.py:376
  38.4 0.0 collective-permute-done.11.refs_0_
  38.4 0.0 collective-permute-done.12.refs_1_
  38.4 0.0 collective-permute-done.13.refs_2_
  38.4 0.0 copy-start
  38.4 0.7 copy-done
  39.1 3.0 %shard_map.82.refs_0_ = bf16[64,640]{1,0:T(8,128)(2,1)S(1)} custom-call(s32[3]{0:T(128)S(1)} %pad_add_fusion.index, s32[2,1,2]{2,1,0:T(1,128)S(1)} %copy-done, bf16[64,768]{1,0:T(8,128)(2,1)S(1)} %collective-permute-done.11.refs_0_, bf16[64,768]{1,0:T(8,128)(2,1)S(1)} %collective-permute-done.12.refs_1_, ...), custom_call_target="tpu_custom_call" | custom-call | tf_op jit(solution)/shard_map/pallas_call | solution.py:346
  42.1 1.6 %collective-permute-start.20 = (bf16[64,640]{1,0:T(8,128)(2,1)S(1)}, bf16[64,640]{1,0:T(8,128)(2,1)S(1)}, u32[]{:S(2)}, u32[]{:S(2)}) collective-permute-start(bf16[64,640]{1,0:T(8,128)(2,1)S(1)} %shard_map.82.refs_0_), channel_id=1, source_target_pairs={{0,1},{1,0},{2,3},{3,2},{4,5},{5,4},{6,7},{7,6},{8,9},{9,8},{10,11... | collective-permute-start | bytes 245768 | tf_op jit(solution)/shard_map/ppermute | solution.py:376
  43.7 0.7 collective-permute-start.21
  44.4 1.3 %collective-permute-start.22 = (bf16[64,640]{1,0:T(8,128)(2,1)S(1)}, bf16[64,640]{1,0:T(8,128)(2,1)S(1)}, u32[]{:S(2)}, u32[]{:S(2)}) collective-permute-start(bf16[64,640]{1,0:T(8,128)(2,1)S(1)} %shard_map.82.refs_0_), channel_id=1, source_target_pairs={{0,3},{1,2},{2,1},{3,0},{4,7},{5,6},{6,5},{7,4},{8,11},{9,10},{10,... | collective-permute-start | bytes 245768 | tf_op jit(solution)/shard_map/ppermute | solution.py:376
  45.6 1.0 %collective-permute-done.20.refs_1_ = bf16[64,640]{1,0:T(8,128)(2,1)S(1)} collective-permute-done((bf16[64,640]{1,0:T(8,128)(2,1)S(1)}, bf16[64,640]{1,0:T(8,128)(2,1)S(1)}, u32[]{:S(2)}, u32[]{:S(2)}) %collective-permute-start.20) | collective-permute-done | bytes 81952 | tf_op jit(solution)/shard_map/ppermute | solution.py:376
  46.6 1.6 %collective-permute-done.21.refs_2_ = bf16[64,640]{1,0:T(8,128)(2,1)S(1)} collective-permute-done((bf16[64,640]{1,0:T(8,128)(2,1)S(1)}, bf16[64,640]{1,0:T(8,128)(2,1)S(1)}, u32[]{:S(2)}, u32[]{:S(2)}) %collective-permute-start.21) | collective-permute-done | bytes 81952 | tf_op jit(solution)/shard_map/ppermute | solution.py:376
  48.2 1.6 %collective-permute-done.22.refs_3_ = bf16[64,640]{1,0:T(8,128)(2,1)S(1)} collective-permute-done((bf16[64,640]{1,0:T(8,128)(2,1)S(1)}, bf16[64,640]{1,0:T(8,128)(2,1)S(1)}, u32[]{:S(2)}, u32[]{:S(2)}) %collective-permute-start.22) | collective-permute-done | bytes 81952 | tf_op jit(solution)/shard_map/ppermute | solution.py:376
  49.7 1.6 %shard_map.83 = (f32[4,256,256]{2,1,0:T(8,128)S(1)}, bf16[4,256,256]{2,1,0:T(8,128)(2,1)S(1)}) custom-call(s32[3]{0:T(128)S(1)} %pad_add_fusion.index, bf16[64,640]{1,0:T(8,128)(2,1)S(1)} %shard_map.82.refs_0_, bf16[64,640]{1,0:T(8,128)(2,1)S(1)} %collective-permute-done.20.refs_1_, bf16[64,640]{1,0:T(8,128)(2,1)S(1)} %collective-permute-done.21.refs_2_, ...), custom_call_target="tpu_custom_call" | custom-call | tf_op jit(solution)/shard_map/pallas_call | solution.py:346
  51.3 0.1 collective-permute-start.23
  51.4 1.9 %collective-permute-done.23.come_ref = bf16[4,256,256]{2,1,0:T(8,128)(2,1)S(1)} collective-permute-done((bf16[4,256,256]{2,1,0:T(8,128)(2,1)S(1)}, bf16[4,256,256]{2,1,0:T(8,128)(2,1)S(1)}, u32[]{:S(2)}, u32[]{:S(2)}) %collective-permute-start.23) | collective-permute-done | bytes 524320 | tf_op jit(solution)/shard_map/ppermute | solution.py:372
  53.3 0.6 shard_map.84
  53.9 1.3 %collective-permute-start.24 = (bf16[256,256]{1,0:T(8,128)(2,1)S(1)}, bf16[256,256]{1,0:T(8,128)(2,1)S(1)}, u32[]{:S(2)}, u32[]{:S(2)}) collective-permute-start(bf16[256,256]{1,0:T(8,128)(2,1)S(1)} %get-tuple-element.59), channel_id=1, source_target_pairs={{0,12},{1,13},{2,14},{3,15},{4,8},{5,9},{6,10},{7,11},{8,4},{9,5},... | collective-permute-start | bytes 393224 | tf_op jit(solution)/shard_map/ppermute | solution.py:369
  55.3 0.0 collective-permute-start.25
  55.3 3.1 %collective-permute-start.26 = (bf16[256,256]{1,0:T(8,128)(2,1)S(1)}, bf16[256,256]{1,0:T(8,128)(2,1)S(1)}, u32[]{:S(2)}, u32[]{:S(2)}) collective-permute-start(bf16[256,256]{1,0:T(8,128)(2,1)S(1)} %get-tuple-element.61), channel_id=1, source_target_pairs={{0,4},{1,5},{2,6},{3,7},{4,0},{5,1},{6,2},{7,3},{8,12},{9,13},{10,... | collective-permute-start | bytes 393224 | tf_op jit(solution)/shard_map/ppermute | solution.py:369
  58.4 3.9 %collective-permute-done.24.refs_0_ = bf16[256,256]{1,0:T(8,128)(2,1)S(1)} collective-permute-done((bf16[256,256]{1,0:T(8,128)(2,1)S(1)}, bf16[256,256]{1,0:T(8,128)(2,1)S(1)}, u32[]{:S(2)}, u32[]{:S(2)}) %collective-permute-start.24) | collective-permute-done | bytes 131104 | tf_op jit(solution)/shard_map/ppermute | solution.py:369
  62.3 4.9 %collective-permute-done.25.refs_1_ = bf16[256,256]{1,0:T(8,128)(2,1)S(1)} collective-permute-done((bf16[256,256]{1,0:T(8,128)(2,1)S(1)}, bf16[256,256]{1,0:T(8,128)(2,1)S(1)}, u32[]{:S(2)}, u32[]{:S(2)}) %collective-permute-start.25) | collective-permute-done | bytes 131104 | tf_op jit(solution)/shard_map/ppermute | solution.py:369
  67.2 0.0 collective-permute-done.26.refs_2_
  67.2 0.7 %shard_map.85 = (f32[192,256]{1,0:T(8,128)}, f32[64,256]{1,0:T(8,128)}) custom-call(f32[256,256]{1,0:T(8,128)S(1)} %get-tuple-element.58.keep_ref, bf16[256,256]{1,0:T(8,128)(2,1)S(1)} %collective-permute-done.24.refs_0_, bf16[256,256]{1,0:T(8,128)(2,1)S(1)} %collective-permute-done.25.refs_1_, bf16[256,256]{1,0:T(8,128)(2,1)S(1)} %collective-permute-done.26.refs_2_), custom_call_target="tpu_custom_call" | custom-call | tf_op jit(solution)/shard_map/pallas_call | solution.py:346
  (8 shorter events, 0.1 us)
Async XLA Ops:
  1.6 10.5 %collective-permute-start.3 = (bf16[256,256]{1,0:T(8,128)(2,1)S(1)}, bf16[256,256]{1,0:T(8,128)(2,1)S(1)}, u32[]{:S(2)}, u32[]{:S(2)}) collective-permute-start(bf16[256,256]{1,0:T(8,128)(2,1)S(1)} %shard_map.78.refs_4_), channel_id=1, source_target_pairs={{0,12},{1,13},{2,14},{3,15},{4,8},{5,9},{6,10},{7,11},{8,4},{9,5},... | collective-permute-start | bytes 393224 | tf_op jit(solution)/shard_map/ppermute | solution.py:369
  6.7 10.5 %copy-start.1 = (bf16[1,4096]{1,0:T(2,128)(2,1)S(1)}, bf16[1,4096]{1,0:T(2,128)(2,1)}, u32[]{:S(2)}) copy-start(bf16[1,4096]{1,0:T(2,128)(2,1)} %param.9) | copy-start | bytes 24580
  8.4 6.5 %collective-permute-start = (bf16[64,1024]{1,0:T(8,128)(2,1)S(1)}, bf16[64,1024]{1,0:T(8,128)(2,1)S(1)}, u32[]{:S(2)}, u32[]{:S(2)}) collective-permute-start(bf16[64,1024]{1,0:T(8,128)(2,1)S(1)} %get-tuple-element.34), channel_id=1, source_target_pairs={{0,3},{1,2},{2,1},{3,0},{4,7},{5,6},{6,5},{7,4},{8,11},{9,10},{10,... | collective-permute-start | bytes 393224 | tf_op jit(solution)/shard_map/ppermute | solution.py:376
  11.0 6.2 %collective-permute-start.1 = (bf16[64,1024]{1,0:T(8,128)(2,1)S(1)}, bf16[64,1024]{1,0:T(8,128)(2,1)S(1)}, u32[]{:S(2)}, u32[]{:S(2)}) collective-permute-start(bf16[64,1024]{1,0:T(8,128)(2,1)S(1)} %get-tuple-element.35), channel_id=1, source_target_pairs={{0,2},{1,3},{2,0},{3,1},{4,6},{5,7},{6,4},{7,5},{8,10},{9,11},{10,... | collective-permute-start | bytes 393224 | tf_op jit(solution)/shard_map/ppermute | solution.py:376
  11.5 5.8 %collective-permute-start.2 = (bf16[64,1024]{1,0:T(8,128)(2,1)S(1)}, bf16[64,1024]{1,0:T(8,128)(2,1)S(1)}, u32[]{:S(2)}, u32[]{:S(2)}) collective-permute-start(bf16[64,1024]{1,0:T(8,128)(2,1)S(1)} %get-tuple-element.36), channel_id=1, source_target_pairs={{0,1},{1,0},{2,3},{3,2},{4,5},{5,4},{6,7},{7,6},{8,9},{9,8},{10,11... | collective-permute-start | bytes 393224 | tf_op jit(solution)/shard_map/ppermute | solution.py:376
  12.0 7.4 %collective-permute-start.5 = (bf16[256,256]{1,0:T(8,128)(2,1)S(1)}, bf16[256,256]{1,0:T(8,128)(2,1)S(1)}, u32[]{:S(2)}, u32[]{:S(2)}) collective-permute-start(bf16[256,256]{1,0:T(8,128)(2,1)S(1)} %shard_map.78.refs_4_), channel_id=1, source_target_pairs={{0,8},{1,9},{2,10},{3,11},{4,12},{5,13},{6,14},{7,15},{8,0},{9,1},... | collective-permute-start | bytes 393224 | tf_op jit(solution)/shard_map/ppermute | solution.py:369
  12.0 9.3 %collective-permute-start.4 = (bf16[256,256]{1,0:T(8,128)(2,1)S(1)}, bf16[256,256]{1,0:T(8,128)(2,1)S(1)}, u32[]{:S(2)}, u32[]{:S(2)}) collective-permute-start(bf16[256,256]{1,0:T(8,128)(2,1)S(1)} %shard_map.78.refs_4_), channel_id=1, source_target_pairs={{0,4},{1,5},{2,6},{3,7},{4,0},{5,1},{6,2},{7,3},{8,12},{9,13},{10,... | collective-permute-start | bytes 393224 | tf_op jit(solution)/shard_map/ppermute | solution.py:369
  14.9 7.0 %collective-permute-start.6 = (bf16[256,256]{1,0:T(8,128)(2,1)S(1)}, bf16[256,256]{1,0:T(8,128)(2,1)S(1)}, u32[]{:S(2)}, u32[]{:S(2)}) collective-permute-start(bf16[256,256]{1,0:T(8,128)(2,1)S(1)} %shard_map.78.refs_4_), channel_id=1, source_target_pairs={{0,16},{16,0},{1,17},{17,1},{2,18},{18,2},{3,19},{19,3},{4,20},{20... | collective-permute-start | bytes 393224 | tf_op jit(solution)/shard_map/ppermute | solution.py:372
  17.2 5.9 %collective-permute-start.9 = (bf16[256,256]{1,0:T(8,128)(2,1)S(1)}, bf16[256,256]{1,0:T(8,128)(2,1)S(1)}, u32[]{:S(2)}, u32[]{:S(2)}) collective-permute-start(bf16[256,256]{1,0:T(8,128)(2,1)S(1)} %collective-permute-done.3.refs_7_), channel_id=1, source_target_pairs={{0,16},{16,0},{1,17},{17,1},{2,18},{18,2},{3,19},{19,3},{4,20},{20... | collective-permute-start | bytes 393224 | tf_op jit(solution)/shard_map/ppermute | solution.py:372
  17.2 4.1 %collective-permute-start.10 = (bf16[1,4096]{1,0:T(2,128)(2,1)S(1)}, bf16[1,4096]{1,0:T(2,128)(2,1)S(1)}, u32[]{:S(2)}, u32[]{:S(2)}) collective-permute-start(bf16[1,4096]{1,0:T(2,128)(2,1)S(1)} %copy-done.1), channel_id=1, source_target_pairs={{0,16},{16,0},{1,17},{17,1},{2,18},{18,2},{3,19},{19,3},{4,20},{20... | collective-permute-start | bytes 24584 | tf_op jit(solution)/shard_map/ppermute | solution.py:372
  19.4 8.8 %collective-permute-start.14 = (bf16[64,1024]{1,0:T(8,128)(2,1)S(1)}, bf16[64,1024]{1,0:T(8,128)(2,1)S(1)}, u32[]{:S(2)}, u32[]{:S(2)}) collective-permute-start(bf16[64,1024]{1,0:T(8,128)(2,1)S(1)} %get-tuple-element.44), channel_id=1, source_target_pairs={{0,3},{1,2},{2,1},{3,0},{4,7},{5,6},{6,5},{7,4},{8,11},{9,10},{10,... | collective-permute-start | bytes 393224 | tf_op jit(solution)/shard_map/ppermute | solution.py:376
  21.3 2.4 %collective-permute-start.8 = (bf16[256,256]{1,0:T(8,128)(2,1)S(1)}, bf16[256,256]{1,0:T(8,128)(2,1)S(1)}, u32[]{:S(2)}, u32[]{:S(2)}) collective-permute-start(bf16[256,256]{1,0:T(8,128)(2,1)S(1)} %collective-permute-done.5.refs_6_), channel_id=1, source_target_pairs={{0,16},{16,0},{1,17},{17,1},{2,18},{18,2},{3,19},{19,3},{4,20},{20... | collective-permute-start | bytes 393224 | tf_op jit(solution)/shard_map/ppermute | solution.py:372
  21.3 2.4 %collective-permute-start.7 = (bf16[256,256]{1,0:T(8,128)(2,1)S(1)}, bf16[256,256]{1,0:T(8,128)(2,1)S(1)}, u32[]{:S(2)}, u32[]{:S(2)}) collective-permute-start(bf16[256,256]{1,0:T(8,128)(2,1)S(1)} %collective-permute-done.4.refs_5_), channel_id=1, source_target_pairs={{0,16},{16,0},{1,17},{17,1},{2,18},{18,2},{3,19},{19,3},{4,20},{20... | collective-permute-start | bytes 393224 | tf_op jit(solution)/shard_map/ppermute | solution.py:372
  21.9 7.2 %collective-permute-start.15 = (bf16[64,1024]{1,0:T(8,128)(2,1)S(1)}, bf16[64,1024]{1,0:T(8,128)(2,1)S(1)}, u32[]{:S(2)}, u32[]{:S(2)}) collective-permute-start(bf16[64,1024]{1,0:T(8,128)(2,1)S(1)} %get-tuple-element.45), channel_id=1, source_target_pairs={{0,2},{1,3},{2,0},{3,1},{4,6},{5,7},{6,4},{7,5},{8,10},{9,11},{10,... | collective-permute-start | bytes 393224 | tf_op jit(solution)/shard_map/ppermute | solution.py:376
  23.1 6.0 %collective-permute-start.16 = (bf16[64,1024]{1,0:T(8,128)(2,1)S(1)}, bf16[64,1024]{1,0:T(8,128)(2,1)S(1)}, u32[]{:S(2)}, u32[]{:S(2)}) collective-permute-start(bf16[64,1024]{1,0:T(8,128)(2,1)S(1)} %get-tuple-element.46), channel_id=1, source_target_pairs={{0,1},{1,0},{2,3},{3,2},{4,5},{5,4},{6,7},{7,6},{8,9},{9,8},{10,11... | collective-permute-start | bytes 393224 | tf_op jit(solution)/shard_map/ppermute | solution.py:376
  25.1 13.3 %collective-permute-start.11 = (bf16[64,768]{1,0:T(8,128)(2,1)S(1)}, bf16[64,768]{1,0:T(8,128)(2,1)S(1)}, u32[]{:S(2)}, u32[]{:S(2)}) collective-permute-start(bf16[64,768]{1,0:T(8,128)(2,1)S(1)} %get-tuple-element.39), channel_id=1, source_target_pairs={{0,3},{1,2},{2,1},{3,0},{4,7},{5,6},{6,5},{7,4},{8,11},{9,10},{10,... | collective-permute-start | bytes 294920 | tf_op jit(solution)/shard_map/ppermute | solution.py:376
  27.1 11.3 %collective-permute-start.12 = (bf16[64,768]{1,0:T(8,128)(2,1)S(1)}, bf16[64,768]{1,0:T(8,128)(2,1)S(1)}, u32[]{:S(2)}, u32[]{:S(2)}) collective-permute-start(bf16[64,768]{1,0:T(8,128)(2,1)S(1)} %get-tuple-element.40), channel_id=1, source_target_pairs={{0,2},{1,3},{2,0},{3,1},{4,6},{5,7},{6,4},{7,5},{8,10},{9,11},{10,... | collective-permute-start | bytes 294920 | tf_op jit(solution)/shard_map/ppermute | solution.py:376
  28.2 10.2 %collective-permute-start.13 = (bf16[64,768]{1,0:T(8,128)(2,1)S(1)}, bf16[64,768]{1,0:T(8,128)(2,1)S(1)}, u32[]{:S(2)}, u32[]{:S(2)}) collective-permute-start(bf16[64,768]{1,0:T(8,128)(2,1)S(1)} %get-tuple-element.41), channel_id=1, source_target_pairs={{0,1},{1,0},{2,3},{3,2},{4,5},{5,4},{6,7},{7,6},{8,9},{9,8},{10,11... | collective-permute-start | bytes 294920 | tf_op jit(solution)/shard_map/ppermute | solution.py:376
  29.9 4.7 %collective-permute-start.17 = (bf16[64,128]{1,0:T(8,128)(2,1)S(1)}, bf16[64,128]{1,0:T(8,128)(2,1)S(1)}, u32[]{:S(2)}, u32[]{:S(2)}) collective-permute-start(bf16[64,128]{1,0:T(8,128)(2,1)S(1)} %get-tuple-element.48), channel_id=1, source_target_pairs={{0,3},{1,2},{2,1},{3,0},{4,7},{5,6},{6,5},{7,4},{8,11},{9,10},{10,... | collective-permute-start | bytes 49160 | tf_op jit(solution)/shard_map/ppermute | solution.py:376
  31.7 4.5 %collective-permute-start.18 = (bf16[64,128]{1,0:T(8,128)(2,1)S(1)}, bf16[64,128]{1,0:T(8,128)(2,1)S(1)}, u32[]{:S(2)}, u32[]{:S(2)}) collective-permute-start(bf16[64,128]{1,0:T(8,128)(2,1)S(1)} %get-tuple-element.49), channel_id=1, source_target_pairs={{0,2},{1,3},{2,0},{3,1},{4,6},{5,7},{6,4},{7,5},{8,10},{9,11},{10,... | collective-permute-start | bytes 49160 | tf_op jit(solution)/shard_map/ppermute | solution.py:376
  34.7 3.7 %collective-permute-start.19 = (bf16[64,128]{1,0:T(8,128)(2,1)S(1)}, bf16[64,128]{1,0:T(8,128)(2,1)S(1)}, u32[]{:S(2)}, u32[]{:S(2)}) collective-permute-start(bf16[64,128]{1,0:T(8,128)(2,1)S(1)} %get-tuple-element.50), channel_id=1, source_target_pairs={{0,1},{1,0},{2,3},{3,2},{4,5},{5,4},{6,7},{7,6},{8,9},{9,8},{10,11... | collective-permute-start | bytes 49160 | tf_op jit(solution)/shard_map/ppermute | solution.py:376
  38.4 0.7 %copy-start = (s32[2,1,2]{2,1,0:T(1,128)S(1)}, s32[2,1,2]{2,1,0:T(1,128)}, u32[]{:S(2)}) copy-start(s32[2,1,2]{2,1,0:T(1,128)} %docs.1) | copy-start | bytes 52
  42.1 4.5 %collective-permute-start.20 = (bf16[64,640]{1,0:T(8,128)(2,1)S(1)}, bf16[64,640]{1,0:T(8,128)(2,1)S(1)}, u32[]{:S(2)}, u32[]{:S(2)}) collective-permute-start(bf16[64,640]{1,0:T(8,128)(2,1)S(1)} %shard_map.82.refs_0_), channel_id=1, source_target_pairs={{0,1},{1,0},{2,3},{3,2},{4,5},{5,4},{6,7},{7,6},{8,9},{9,8},{10,11... | collective-permute-start | bytes 245768 | tf_op jit(solution)/shard_map/ppermute | solution.py:376
  43.7 4.4 %collective-permute-start.21 = (bf16[64,640]{1,0:T(8,128)(2,1)S(1)}, bf16[64,640]{1,0:T(8,128)(2,1)S(1)}, u32[]{:S(2)}, u32[]{:S(2)}) collective-permute-start(bf16[64,640]{1,0:T(8,128)(2,1)S(1)} %shard_map.82.refs_0_), channel_id=1, source_target_pairs={{0,2},{1,3},{2,0},{3,1},{4,6},{5,7},{6,4},{7,5},{8,10},{9,11},{10,... | collective-permute-start | bytes 245768 | tf_op jit(solution)/shard_map/ppermute | solution.py:376
  44.4 5.3 %collective-permute-start.22 = (bf16[64,640]{1,0:T(8,128)(2,1)S(1)}, bf16[64,640]{1,0:T(8,128)(2,1)S(1)}, u32[]{:S(2)}, u32[]{:S(2)}) collective-permute-start(bf16[64,640]{1,0:T(8,128)(2,1)S(1)} %shard_map.82.refs_0_), channel_id=1, source_target_pairs={{0,3},{1,2},{2,1},{3,0},{4,7},{5,6},{6,5},{7,4},{8,11},{9,10},{10,... | collective-permute-start | bytes 245768 | tf_op jit(solution)/shard_map/ppermute | solution.py:376
  51.3 2.0 %collective-permute-start.23 = (bf16[4,256,256]{2,1,0:T(8,128)(2,1)S(1)}, bf16[4,256,256]{2,1,0:T(8,128)(2,1)S(1)}, u32[]{:S(2)}, u32[]{:S(2)}) collective-permute-start(bf16[4,256,256]{2,1,0:T(8,128)(2,1)S(1)} %get-tuple-element.57), channel_id=1, source_target_pairs={{0,16},{16,0},{1,17},{17,1},{2,18},{18,2},{3,19},{19,3},{4,20},{20... | collective-permute-start | bytes 1572872 | tf_op jit(solution)/shard_map/ppermute | solution.py:372
  53.9 8.3 %collective-permute-start.24 = (bf16[256,256]{1,0:T(8,128)(2,1)S(1)}, bf16[256,256]{1,0:T(8,128)(2,1)S(1)}, u32[]{:S(2)}, u32[]{:S(2)}) collective-permute-start(bf16[256,256]{1,0:T(8,128)(2,1)S(1)} %get-tuple-element.59), channel_id=1, source_target_pairs={{0,12},{1,13},{2,14},{3,15},{4,8},{5,9},{6,10},{7,11},{8,4},{9,5},... | collective-permute-start | bytes 393224 | tf_op jit(solution)/shard_map/ppermute | solution.py:369
  55.3 12.0 %collective-permute-start.25 = (bf16[256,256]{1,0:T(8,128)(2,1)S(1)}, bf16[256,256]{1,0:T(8,128)(2,1)S(1)}, u32[]{:S(2)}, u32[]{:S(2)}) collective-permute-start(bf16[256,256]{1,0:T(8,128)(2,1)S(1)} %get-tuple-element.60), channel_id=1, source_target_pairs={{0,8},{1,9},{2,10},{3,11},{4,12},{5,13},{6,14},{7,15},{8,0},{9,1},... | collective-permute-start | bytes 393224 | tf_op jit(solution)/shard_map/ppermute | solution.py:369
  55.3 11.9 %collective-permute-start.26 = (bf16[256,256]{1,0:T(8,128)(2,1)S(1)}, bf16[256,256]{1,0:T(8,128)(2,1)S(1)}, u32[]{:S(2)}, u32[]{:S(2)}) collective-permute-start(bf16[256,256]{1,0:T(8,128)(2,1)S(1)} %get-tuple-element.61), channel_id=1, source_target_pairs={{0,4},{1,5},{2,6},{3,7},{4,0},{5,1},{6,2},{7,3},{8,12},{9,13},{10,... | collective-permute-start | bytes 393224 | tf_op jit(solution)/shard_map/ppermute | solution.py:369

commit v10 on v4

--- a/solution.py
+++ b/solution.py
@@ -10,7 +10,6 @@
 F32 = jnp.float32
 BF16 = jnp.bfloat16
 PLANE = 4
-STATS = 16
 VMEM_LIMIT = 16 * 1024 * 1024
 
 
@@ -125,29 +124,39 @@
     return lax.dot_general(a, b, (((1,), (1,)), ((), ())), preferred_element_type=F32)
 
 
-def blocks_kernel(planes, index, gain_ref, qkv_ref, wout_ref, x_ref, c_ref, pack_ref, *refs):
-    out_refs, sems = refs[:PLANE], refs[PLANE]
-    qkv_rows, heads = qkv_ref.shape[0], wout_ref.shape[0]
-    width = x_ref.shape[-1] // (planes * PLANE)
+def block_copies(planes, index, k, refs, out_ref, sems):
+    width = refs[0].shape[-1] // (planes * PLANE)
     section, p = index[0], index[2]
+    copies = []
+    for z in range(planes):
+        at = pl.multiple_of((z * PLANE + (p ^ k)) * width, width)
+        for half, ref in enumerate(refs):
+            copies.append(
+                pltpu.make_async_copy(
+                    ref.at[section, :, pl.ds(at, width)],
+                    out_ref.at[half, :, pl.ds(z * width, width)],
+                    sems.at[len(copies)],
+                )
+            )
+    return copies
+
+
+def mark_kernel(pack_ref, gain_ref, out_ref):
+    out_ref[: pack_ref.shape[0], :] = pack_ref[...]
+    out_ref[pack_ref.shape[0] :, :] = gain_ref[...]
+
+
+def blocks_kernel(planes, index, qkv_ref, wout_ref, x_ref, c_ref, pack_ref, *refs):
+    out_refs, pack_sems, sems = refs[:-2], refs[-2], refs[-1]
+    qkv_rows = qkv_ref.shape[0]
     copies = [
-        pltpu.make_async_copy(qkv_ref, pack_ref.at[:qkv_rows], sems.at[0]),
-        pltpu.make_async_copy(wout_ref, pack_ref.at[qkv_rows : qkv_rows + heads], sems.at[1]),
+        pltpu.make_async_copy(qkv_ref, pack_ref.at[:qkv_rows], pack_sems.at[0]),
+        pltpu.make_async_copy(wout_ref, pack_ref.at[qkv_rows:], pack_sems.at[1]),
     ]
-    for k in range(PLANE):
-        for z in range(planes):
-            at = pl.multiple_of((z * PLANE + (p ^ k)) * width, width)
-            for half, ref in enumerate((x_ref, c_ref)):
-                copies.append(
-                    pltpu.make_async_copy(
-                        ref.at[section, :, pl.ds(at, width)],
-                        out_refs[k].at[half, :, pl.ds(z * width, width)],
-                        sems.at[len(copies)],
-                    )
-                )
+    for k, out_ref in enumerate(out_refs):
+        copies += block_copies(planes, index, k, (x_ref, c_ref), out_ref, sems.at[k])
     for copy in copies:
         copy.start()
-    pack_ref[qkv_rows + heads :, :] = jnp.broadcast_to(gain_ref[...].astype(F32), (STATS, width)).astype(BF16)
     for copy in copies:
         copy.wait()
 
@@ -155,29 +164,33 @@
 def project_kernel(planes, heads, index, *refs):
     blocks, own, other = refs[:PLANE], refs[PLANE : PLANE + planes], refs[PLANE + planes : PLANE + 2 * planes]
     x_ref, c_ref, vx_ref, gain_ref = refs[PLANE + 2 * planes : PLANE + 2 * planes + 4]
-    out_refs = refs[PLANE + 2 * planes + 4 : -2]
-    vc_ref, sum_ref = refs[-2:]
+    out_refs = refs[PLANE + 2 * planes + 4 : -4]
+    vc_ref, sum_ref, *wide_refs = refs[-4:]
     qkv, width = 3 * heads, vx_ref.shape[-1]
-    section, z, p = index[0], index[1], index[2]
+    section, place, p = index[0], index[1], index[2]
+    for ref, wide_ref in zip((own[0], other[0]), wide_refs):
+        wide_ref[...] = ref[qkv + heads :, :].astype(F32)
+    for z in range(planes):
+        mine, theirs = (ref[pl.ds(z * PLANE + p, 1), :] for ref in wide_refs)
+        gain_ref[z, 0:1, :] = jnp.where(section == 0, mine, theirs)
+        gain_ref[z, 1:2, :] = jnp.where(section == 0, theirs, mine)
     for k in range(planes):
-        at = z ^ k
-        zero = jnp.where(section == 0, own[k][...], other[k][...])
-        one = jnp.where(section == 0, other[k][...], own[k][...])
-        gains = [w[qkv + heads :].astype(F32)[0:1] for w in (zero, one)]
-        gain_ref[at, 0:1, :] = gains[0]
-        gain_ref[at, 1:2, :] = gains[1]
+        at = place ^ k
+        mine, theirs = own[k][: qkv + heads, :], other[k][: qkv + heads, :]
+        zero = jnp.where(section == 0, mine, theirs)
+        one = jnp.where(section == 0, theirs, mine)
         empty = jnp.zeros((heads, width), BF16)
-        vx_ref[at, :qkv, :] = (zero[:qkv].astype(F32) * gains[0]).astype(BF16)
+        vx_ref[at, :qkv, :] = (zero[:qkv].astype(F32) * gain_ref[at, 0:1, :]).astype(BF16)
         vx_ref[at, qkv : qkv + heads, :] = zero[qkv : qkv + heads]
-        vx_ref[at, qkv + heads : 2 * qkv + heads, :] = (one[:qkv].astype(F32) * gains[1]).astype(BF16)
+        vx_ref[at, qkv + heads : 2 * qkv + heads, :] = (one[:qkv].astype(F32) * gain_ref[at, 1:2, :]).astype(BF16)
         vx_ref[at, 2 * qkv + heads :, :] = empty
         vc_ref[at, :heads, :] = empty
         vc_ref[at, heads : 2 * heads, :] = one[qkv : qkv + heads]
         vc_ref[at, 2 * heads : 3 * heads, :] = zero[qkv : qkv + heads]
         vc_ref[at, 3 * heads :, :] = empty
     for k in range(PLANE):
-        x_ref[p ^ k] = blocks[k][0]
-        c_ref[p ^ k] = blocks[k][1]
+        x_ref[p ^ k] = blocks[-k][0]
+        c_ref[p ^ k] = blocks[-k][1]
     rows = x_ref.shape[0] * x_ref.shape[1]
     with_x = with_c = squares = products = None
     for z in range(planes):
@@ -207,12 +220,6 @@
         out_refs[k][:, 5 * half :] = products.astype(BF16)
 
 
-def exact(a, b, dims):
-    return lax.dot_general(
-        a, b, (dims, ((), ())), precision=lax.Precision.HIGHEST, preferred_element_type=F32
-    )
-
-
 def attention(qkv, allowed, heads):
     query, keys, values = (qkv[:, i * heads : (i + 1) * heads].astype(BF16) for i in range(3))
     scores = jnp.where(allowed, nt(query, keys) * heads ** (-0.5), -1e30)
@@ -221,23 +228,27 @@
     return probs, nn(probs.astype(BF16), values).astype(BF16)
 
 
-def attention_grad(qkv, probs, d_att, heads):
+def attention_grad(qkv, probs, att, d_att, heads):
     query, keys, values = (qkv[:, i * heads : (i + 1) * heads].astype(BF16) for i in range(3))
+    inner = jnp.sum(att.astype(F32) * d_att.astype(F32), axis=1, keepdims=True)
     d_values = nn(jnp.transpose(probs).astype(BF16), d_att)
-    d_probs = nt(d_att, values).astype(BF16).astype(F32)
-    inner = jnp.sum(probs * d_probs, axis=1, keepdims=True)
-    d_scores = probs * (d_probs - inner) * heads ** (-0.5)
+    d_scores = probs * (nt(d_att, values) - inner) * heads ** (-0.5)
     d_query = nn(d_scores.astype(BF16), keys)
     d_keys = nn(jnp.transpose(d_scores).astype(BF16), query)
     return jnp.concatenate([d_query, d_keys, d_values], axis=1).astype(BF16).astype(F32)
 
 
-def chain_kernel(features, heads, index, docs, *refs):
-    parts, out_ref = refs[:-1], refs[-1]
-    qkv, half = 3 * heads, 2 * heads
+def summed(parts):
     total = parts[0][...].astype(F32)
     for part in parts[1:]:
         total = total + part[...].astype(F32)
+    return total
+
+
+def chain_kernel(features, heads, index, docs, *refs):
+    out_ref = refs[-1]
+    qkv, half = 3 * heads, 2 * heads
+    total = summed(refs[:-1])
     rows = total.shape[0]
     section = index[0]
     query_at = lax.broadcasted_iota(jnp.int32, (rows, rows), 0)
@@ -249,28 +260,27 @@
         allowed = allowed & ((query_at >= end) == (key_at >= end))
     x_out = total[:, qkv : 2 * half]
     x_one = total[:, 2 * half : 2 * half + qkv]
-    c_one = total[:, 4 * half - heads : 4 * half].astype(BF16)
     tail = total[:, 4 * half : 5 * half]
-    c_zero = tail[:, :heads]
+    c_one, c_zero = total[:, 4 * half - heads : 4 * half].astype(BF16), tail[:, :heads]
     lane = lax.broadcasted_iota(jnp.int32, tail.shape, 1)
     squares = jnp.sum(jnp.where((lane == heads) | (lane == heads + 1), tail, 0.0), axis=1, keepdims=True)
-    mixed = total[:, 5 * half : 5 * half + qkv]
-    gram = total[:, 5 * half + qkv :]
+    mixed = total[:, 5 * half : 5 * half + qkv].astype(BF16)
+    gram = total[:, 5 * half + qkv :].astype(BF16)
 
     scale0 = lax.rsqrt(squares / features + 1e-05)
     qkv0 = (total[:, :qkv] * scale0).astype(BF16).astype(F32)
     probs0, att0 = attention(qkv0, allowed, heads)
     wide0 = att0.astype(F32)
-    y_out = x_out + exact(wide0, gram, ((1,), (0,)))
+    y_out = x_out + nn(att0, gram)
     squares = squares + jnp.sum(wide0 * (x_out + y_out), axis=1, keepdims=True)
     scale1 = lax.rsqrt(jnp.maximum(squares, 0.0) / features + 1e-05)
-    qkv1 = ((x_one + exact(wide0, mixed, ((1,), (0,)))) * scale1).astype(BF16).astype(F32)
+    qkv1 = ((x_one + nn(att0, mixed)) * scale1).astype(BF16).astype(F32)
     probs1, att1 = attention(qkv1, allowed, heads)
-    d_qkv1 = attention_grad(qkv1, probs1, c_one, heads)
+    d_qkv1 = attention_grad(qkv1, probs1, att1, c_one, heads)
     inner = jnp.sum(d_qkv1 * qkv1, axis=1, keepdims=True) * scale1 * scale1 / features
     e1 = d_qkv1 * scale1
-    d_att0 = c_zero + exact(e1, mixed, ((1,), (1,))) - inner * y_out
-    e0 = attention_grad(qkv0, probs0, d_att0.astype(BF16), heads) * scale0
+    d_att0 = c_zero + nt(e1.astype(BF16), mixed) - inner * y_out
+    e0 = attention_grad(qkv0, probs0, att0, d_att0.astype(BF16), heads) * scale0
     factors = [e0, wide0, e1, wide0 * inner, att1.astype(F32), jnp.zeros((rows, heads), F32)]
     out_ref[...] = jnp.concatenate(factors, axis=1).astype(BF16)
 
@@ -365,24 +375,30 @@
     def exchange(value):
         return far_first(value, PLANE, along_plane)
 
-    gain = lax.dynamic_slice(norm_gain, (0, place * width), (1, width))
     smem, vmem = pl.BlockSpec(memory_space=pltpu.SMEM), pl.BlockSpec(memory_space=pltpu.VMEM)
     hbm = pl.BlockSpec(memory_space=pltpu.HBM)
-    in_hbm = [
+    params = pltpu.CompilerParams(vmem_limit_bytes=VMEM_LIMIT)
+    qkv_in, out_in, x_in, c_in = [
         pltpu.with_memory_space_constraint(value, pltpu.HBM)
         for value in (w_qkv[0].T, w_out[0], inputs, cotangent)
     ]
+    one_block = jax.ShapeDtypeStruct((2, block, cols), BF16)
     pack, *blocks = pl.pallas_call(
         functools.partial(blocks_kernel, planes),
-        out_shape=[jax.ShapeDtypeStruct((qkv_rows + heads + STATS, width), BF16)]
-        + [jax.ShapeDtypeStruct((2, block, cols), BF16)] * PLANE,
-        in_specs=[smem, vmem] + [hbm] * 4,
-        out_specs=[vmem] * (1 + PLANE),
-        scratch_shapes=[pltpu.SemaphoreType.DMA((2 + 2 * PLANE * planes,))],
-        compiler_params=pltpu.CompilerParams(vmem_limit_bytes=VMEM_LIMIT),
-    )(index, gain, *in_hbm)
-    own = far_first(pack, planes, along_z)
+        out_shape=[jax.ShapeDtypeStruct((qkv_rows + heads, width), BF16)] + [one_block] * PLANE,
+        in_specs=[smem] + [hbm] * 4,
+        out_specs=[vmem] * (PLANE + 1),
+        scratch_shapes=[pltpu.SemaphoreType.DMA((2,)), pltpu.SemaphoreType.DMA((PLANE, 2 * planes))],
+        compiler_params=params,
+    )(index, qkv_in, out_in, x_in, c_in)
+    gain = norm_gain[0].reshape(shards, width)
     blocks = [blocks[0]] + far_first(blocks, PLANE, along_plane)[1:]
+    far = {k: along_z(pack, k) for k in reversed(range(2, planes))}
+    later, _ = lax.optimization_barrier((pack, blocks[3]))
+    near = [along_z(later, 1)] if planes > 1 else []
+    mine, late_gain, _ = lax.optimization_barrier((pack, gain, blocks[3]))
+    (marked,) = call(mark_kernel, [((qkv_rows + heads + shards, width), BF16)], mine, late_gain)
+    own = [marked] + near + [far[k] for k in range(2, planes)]
     other = [to_sibling(piece) for piece in own]
 
     split = ((PLANE, block, cols), BF16)
@@ -391,13 +407,13 @@
         functools.partial(project_kernel, planes, heads),
         [split, split, ((planes, 4 * half, width), BF16), ((planes, 8, width), F32)]
         + [((block, 7 * half), BF16)] * PLANE,
-        index, *blocks, *own, *other, scalars=1,
-        scratch=[((planes, 2 * half, width), BF16), ((rows, 5 * half), BF16)],
+        index, blocks[0], *blocks[:0:-1], *own, *other, scalars=1,
+        scratch=[((planes, 2 * half, width), BF16), ((rows, 5 * half), BF16)] + [((shards, width), F32)] * 2,
     )
     (factors,) = call(
         functools.partial(chain_kernel, features, heads),
         [((block, 5 * half), BF16)],
-        index, doc_lengths, *exchange(sent), scalars=2,
+        index, doc_lengths, *exchange(sent)[::-1], scalars=2,
     )
     grads = (planes, qkv_rows + heads, width)
     keep, send = call(
@@ -415,7 +431,7 @@
     grad_qkv, grad_out = call(
         functools.partial(last_kernel, qkv_rows),
         [((qkv_rows, width), F32), ((heads, width), F32)],
-        merged[0], *parts,
+        merged[0], *parts[::-1],
     )
     return (grad_qkv.T[None], grad_out[None])
 

time: 65.6 us -> 65.8 us (level)
  local copies, waits for them, and re-layouts: 0.7 us -> 0.02 us
    ppermute x9, waiting for transfers between devices: 10.7 us -> 8.02 us  [along_plane(): return lax.ppermute(value, 'dp', route)]
    ppermute x6, waiting for transfers between devices: 16.4 us -> 18.2 us  [along_z(): return lax.ppermute(value, 'dp', route)]
    ppermute x6, starting transfers between devices: 11.2 us -> 12.9 us  [along_z(): return lax.ppermute(value, 'dp', route)]
    ppermute x5, waiting for transfers between devices: 1.91 us -> 3.22 us  [to_sibling(): return lax.ppermute(value, 'section', [(0, 1), (1, 0)])]
    unnamed x4, local copies, waits for them, and re-layouts: 0.7 us -> 0.01 us
    pallas_call x5 -> x6, Pallas kernels: 7.67 us -> 7.44 us  [call(): pl.pallas_call(kernel, out_shape=[jax.ShapeDtypeStruct(shape, dtype) for...]
where the time goes in v10:
time: 65.8 us; the launch traced here: 65.6 us
  waiting for transfers between devices  29.4 us (45%)
  starting transfers between devices  25.6 us (39%)
  Pallas kernels  9.67 us (15%)
  between operations  0.75 us (1%)
    ppermute x6, waiting for transfers between devices, along_z(): return lax.ppermute(value, 'dp', route)  18.2 us
    ppermute x6, starting transfers between devices, along_z(): return lax.ppermute(value, 'dp', route)  12.9 us
    ppermute x9, starting transfers between devices, along_plane(): return lax.ppermute(value, 'dp', route)  12.1 us
    ppermute x9, waiting for transfers between devices, along_plane(): return lax.ppermute(value, 'dp', route)  8.02 us
    pallas_call x6, Pallas kernels, call(): pl.pallas_call(kernel, out_shape=[jax.ShapeDtypeStruct(shape, dtype) for...  7.44 us
    ppermute x5, waiting for transfers between devices, to_sibling(): return lax.ppermute(value, 'section', [(0, 1), (1, 0)])  3.22 us
    pallas_call x1, Pallas kernels, planar(): pl.pallas_call(functools.partial(blocks_kernel, planes), out_shape=[jax.S...  2.23 us
  transfers between devices with their start and end apart: 20, of which 12 were waited for; matrix products, arithmetic and copies ran while one was open for 0% of the time, Pallas kernels for 0%

profile of v10, /device:TPU:0, one launch (start us, length us, event | category | flops | bytes accessed | tf_op | source)
XLA Modules:
  0.0 65.6 jit_solution(7700313041475755959)
XLA Ops:
  0.6 0.1 pad_add_fusion.index
  0.7 0.0 copy-start.1
  0.7 2.2 %shard_map.77 = (bf16[256,256]{1,0:T(8,128)(2,1)S(1)}, bf16[2,64,1024]{2,1,0:T(8,128)(2,1)S(1)}, bf16[2,64,1024]{2,1,0:T(8,128)(2,1)S(1)}, bf16[2,64,1024]{2,1,0:T(8,128)(2,1)S(1)}, bf16[2,64,1024]{2,1,0:T(8,128)(2,1)S(1)}) custom-call(s32[3]{0:T(128)S(1)} %pad_add_fusion.index, bf16[192,256]{1,0:T(8,128)(2,1)} %bitcast.11, bf16[64,256]{1,0:T(8,128)(2,1)} %bitcast.12, ...), custom_call_target="tpu_custom_call" | custom-call | tf_op jit(solution)/shard_map/pallas_call | solution.py:386
  3.0 4.0 %collective-permute-start = (bf16[2,64,1024]{2,1,0:T(8,128)(2,1)S(1)}, bf16[2,64,1024]{2,1,0:T(8,128)(2,1)S(1)}, u32[]{:S(2)}, u32[]{:S(2)}) collective-permute-start(bf16[2,64,1024]{2,1,0:T(8,128)(2,1)S(1)} %get-tuple-element.27), channel_id=1, source_target_pairs={{0,3},{1,2},{2,1},{3,0},{4,7},{5,6},{6,5},{7,4},{8,11},{9,10},{10,... | collective-permute-start | bytes 786440 | tf_op jit(solution)/shard_map/ppermute | solution.py:373
  6.9 3.6 %collective-permute-start.5 = (bf16[256,256]{1,0:T(8,128)(2,1)S(1)}, bf16[256,256]{1,0:T(8,128)(2,1)S(1)}, u32[]{:S(2)}, u32[]{:S(2)}) collective-permute-start(bf16[256,256]{1,0:T(8,128)(2,1)S(1)} %get-tuple-element.33.pack_ref), channel_id=1, source_target_pairs={{0,12},{1,13},{2,14},{3,15},{4,8},{5,9},{6,10},{7,11},{8,4},{9,5},... | collective-permute-start | bytes 393224 | tf_op jit(solution)/shard_map/ppermute | solution.py:366
  10.5 0.0 collective-permute-start.4
  10.5 0.5 collective-permute-start.1
  11.0 0.5 collective-permute-start.2
  11.6 3.6 %collective-permute-done.5.refs_7_ = bf16[256,256]{1,0:T(8,128)(2,1)S(1)} collective-permute-done((bf16[256,256]{1,0:T(8,128)(2,1)S(1)}, bf16[256,256]{1,0:T(8,128)(2,1)S(1)}, u32[]{:S(2)}, u32[]{:S(2)}) %collective-permute-start.5) | collective-permute-done | bytes 131104 | tf_op jit(solution)/shard_map/ppermute | solution.py:366
  15.2 0.0 collective-permute-start.9
  15.2 0.0 collective-permute-done.refs_1_
  15.2 4.9 %collective-permute-start.3 = (bf16[256,256]{1,0:T(8,128)(2,1)S(1)}, bf16[256,256]{1,0:T(8,128)(2,1)S(1)}, u32[]{:S(2)}, u32[]{:S(2)}) collective-permute-start(bf16[256,256]{1,0:T(8,128)(2,1)S(1)} %get-tuple-element.33.pack_ref), channel_id=1, source_target_pairs={{0,4},{1,5},{2,6},{3,7},{4,0},{5,1},{6,2},{7,3},{8,12},{9,13},{10,... | collective-permute-start | bytes 393224 | tf_op jit(solution)/shard_map/ppermute | solution.py:366
  20.1 0.0 copy-done.1
  20.1 0.1 reduce
  20.2 1.2 %collective-permute-done.4.refs_6_ = bf16[256,256]{1,0:T(8,128)(2,1)S(1)} collective-permute-done((bf16[256,256]{1,0:T(8,128)(2,1)S(1)}, bf16[256,256]{1,0:T(8,128)(2,1)S(1)}, u32[]{:S(2)}, u32[]{:S(2)}) %collective-permute-start.4) | collective-permute-done | bytes 131104 | tf_op jit(solution)/shard_map/ppermute | solution.py:366
  21.3 0.0 collective-permute-start.6
  21.3 0.0 collective-permute-done.9.refs_11_
  21.3 0.5 collective-permute-start.8
  21.8 2.4 %collective-permute-done.3.refs_5_ = bf16[256,256]{1,0:T(8,128)(2,1)S(1)} collective-permute-done((bf16[256,256]{1,0:T(8,128)(2,1)S(1)}, bf16[256,256]{1,0:T(8,128)(2,1)S(1)}, u32[]{:S(2)}, u32[]{:S(2)}) %collective-permute-start.3) | collective-permute-done | bytes 131104 | tf_op jit(solution)/shard_map/ppermute | solution.py:366
  24.2 0.0 collective-permute-start.7
  24.2 0.0 collective-permute-done.8.refs_10_
  24.3 0.0 collective-permute-done.1.refs_2_
  24.3 0.0 collective-permute-done.2.refs_3_
  24.3 0.0 collective-permute-done.6.refs_8_
  24.3 1.3 %collective-permute-done.7.refs_9_ = bf16[256,256]{1,0:T(8,128)(2,1)S(1)} collective-permute-done((bf16[256,256]{1,0:T(8,128)(2,1)S(1)}, bf16[256,256]{1,0:T(8,128)(2,1)S(1)}, u32[]{:S(2)}, u32[]{:S(2)}) %collective-permute-start.7) | collective-permute-done | bytes 131104 | tf_op jit(solution)/shard_map/ppermute | solution.py:369
  25.6 1.6 %shard_map.79 = (bf16[4,64,1024]{2,1,0:T(8,128)(2,1)S(1)}, bf16[4,64,1024]{2,1,0:T(8,128)(2,1)S(1)}, bf16[4,512,256]{2,1,0:T(8,128)(2,1)S(1)}, f32[4,8,256]{2,1,...) custom-call(s32[3]{0:T(128)S(1)} %pad_add_fusion.index, ...), custom_call_target="tpu_custom_call" | custom-call | tf_op jit(solution)/shard_map/pallas_call | solution.py:343
  27.2 0.5 collective-permute-start.10
  27.7 1.5 %collective-permute-start.11 = (bf16[64,896]{1,0:T(8,128)(2,1)S(1)}, bf16[64,896]{1,0:T(8,128)(2,1)S(1)}, u32[]{:S(2)}, u32[]{:S(2)}) collective-permute-start(bf16[64,896]{1,0:T(8,128)(2,1)S(1)} %get-tuple-element.35), channel_id=1, source_target_pairs={{0,2},{1,3},{2,0},{3,1},{4,6},{5,7},{6,4},{7,5},{8,10},{9,11},{10,... | collective-permute-start | bytes 344072 | tf_op jit(solution)/shard_map/ppermute | solution.py:373
  29.3 0.0 copy-start
  29.3 1.5 %collective-permute-start.12 = (bf16[64,896]{1,0:T(8,128)(2,1)S(1)}, bf16[64,896]{1,0:T(8,128)(2,1)S(1)}, u32[]{:S(2)}, u32[]{:S(2)}) collective-permute-start(bf16[64,896]{1,0:T(8,128)(2,1)S(1)} %get-tuple-element.36), channel_id=1, source_target_pairs={{0,1},{1,0},{2,3},{3,2},{4,5},{5,4},{6,7},{7,6},{8,9},{9,8},{10,11... | collective-permute-start | bytes 344072 | tf_op jit(solution)/shard_map/ppermute | solution.py:373
  30.8 3.4 %collective-permute-done.10.refs_0_ = bf16[64,896]{1,0:T(8,128)(2,1)S(1)} collective-permute-done((bf16[64,896]{1,0:T(8,128)(2,1)S(1)}, bf16[64,896]{1,0:T(8,128)(2,1)S(1)}, u32[]{:S(2)}, u32[]{:S(2)}) %collective-permute-start.10) | collective-permute-done | bytes 114720 | tf_op jit(solution)/shard_map/ppermute | solution.py:373
  34.2 0.9 %collective-permute-done.11.refs_1_ = bf16[64,896]{1,0:T(8,128)(2,1)S(1)} collective-permute-done((bf16[64,896]{1,0:T(8,128)(2,1)S(1)}, bf16[64,896]{1,0:T(8,128)(2,1)S(1)}, u32[]{:S(2)}, u32[]{:S(2)}) %collective-permute-start.11) | collective-permute-done | bytes 114720 | tf_op jit(solution)/shard_map/ppermute | solution.py:373
  35.1 0.0 collective-permute-done.12.refs_2_
  35.1 0.0 copy-done
  35.1 2.9 %shard_map.80.refs_0_ = bf16[64,640]{1,0:T(8,128)(2,1)S(1)} custom-call(s32[3]{0:T(128)S(1)} %pad_add_fusion.index, s32[2,1,2]{2,1,0:T(1,128)S(1)} %copy-done, bf16[64,896]{1,0:T(8,128)(2,1)S(1)} %collective-permute-done.10.refs_0_, bf16[64,896]{1,0:T(8,128)(2,1)S(1)} %collective-permute-done.11.refs_1_, ...), custom_call_target="tpu_custom_call" | custom-call | tf_op jit(solution)/shard_map/pallas_call | solution.py:343
  38.0 1.3 %collective-permute-start.15 = (bf16[64,640]{1,0:T(8,128)(2,1)S(1)}, bf16[64,640]{1,0:T(8,128)(2,1)S(1)}, u32[]{:S(2)}, u32[]{:S(2)}) collective-permute-start(bf16[64,640]{1,0:T(8,128)(2,1)S(1)} %shard_map.80.refs_0_), channel_id=1, source_target_pairs={{0,3},{1,2},{2,1},{3,0},{4,7},{5,6},{6,5},{7,4},{8,11},{9,10},{10,... | collective-permute-start | bytes 245768 | tf_op jit(solution)/shard_map/ppermute | solution.py:373
  39.3 1.5 %collective-permute-start.14 = (bf16[64,640]{1,0:T(8,128)(2,1)S(1)}, bf16[64,640]{1,0:T(8,128)(2,1)S(1)}, u32[]{:S(2)}, u32[]{:S(2)}) collective-permute-start(bf16[64,640]{1,0:T(8,128)(2,1)S(1)} %shard_map.80.refs_0_), channel_id=1, source_target_pairs={{0,2},{1,3},{2,0},{3,1},{4,6},{5,7},{6,4},{7,5},{8,10},{9,11},{10,... | collective-permute-start | bytes 245768 | tf_op jit(solution)/shard_map/ppermute | solution.py:373
  40.8 0.8 %collective-permute-start.13 = (bf16[64,640]{1,0:T(8,128)(2,1)S(1)}, bf16[64,640]{1,0:T(8,128)(2,1)S(1)}, u32[]{:S(2)}, u32[]{:S(2)}) collective-permute-start(bf16[64,640]{1,0:T(8,128)(2,1)S(1)} %shard_map.80.refs_0_), channel_id=1, source_target_pairs={{0,1},{1,0},{2,3},{3,2},{4,5},{5,4},{6,7},{7,6},{8,9},{9,8},{10,11... | collective-permute-start | bytes 245768 | tf_op jit(solution)/shard_map/ppermute | solution.py:373
  41.6 2.5 %collective-permute-done.15.refs_3_ = bf16[64,640]{1,0:T(8,128)(2,1)S(1)} collective-permute-done((bf16[64,640]{1,0:T(8,128)(2,1)S(1)}, bf16[64,640]{1,0:T(8,128)(2,1)S(1)}, u32[]{:S(2)}, u32[]{:S(2)}) %collective-permute-start.15) | collective-permute-done | bytes 81952 | tf_op jit(solution)/shard_map/ppermute | solution.py:373
  44.1 0.3 collective-permute-done.14.refs_2_
  44.4 0.8 %collective-permute-done.13.refs_1_ = bf16[64,640]{1,0:T(8,128)(2,1)S(1)} collective-permute-done((bf16[64,640]{1,0:T(8,128)(2,1)S(1)}, bf16[64,640]{1,0:T(8,128)(2,1)S(1)}, u32[]{:S(2)}, u32[]{:S(2)}) %collective-permute-start.13) | collective-permute-done | bytes 81952 | tf_op jit(solution)/shard_map/ppermute | solution.py:373
  45.2 1.6 %shard_map.81 = (f32[4,256,256]{2,1,0:T(8,128)S(1)}, bf16[4,256,256]{2,1,0:T(8,128)(2,1)S(1)}) custom-call(s32[3]{0:T(128)S(1)} %pad_add_fusion.index, bf16[64,640]{1,0:T(8,128)(2,1)S(1)} %shard_map.80.refs_0_, bf16[64,640]{1,0:T(8,128)(2,1)S(1)} %collective-permute-done.13.refs_1_, bf16[64,640]{1,0:T(8,128)(2,1)S(1)} %collective-permute-done.14.refs_2_, ...), custom_call_target="tpu_custom_call" | custom-call | tf_op jit(solution)/shard_map/pallas_call | solution.py:343
  46.8 0.1 collective-permute-start.16
  46.9 1.9 %collective-permute-done.16.come_ref = bf16[4,256,256]{2,1,0:T(8,128)(2,1)S(1)} collective-permute-done((bf16[4,256,256]{2,1,0:T(8,128)(2,1)S(1)}, bf16[4,256,256]{2,1,0:T(8,128)(2,1)S(1)}, u32[]{:S(2)}, u32[]{:S(2)}) %collective-permute-start.16) | collective-permute-done | bytes 524320 | tf_op jit(solution)/shard_map/ppermute | solution.py:369
  48.8 0.6 shard_map.82
  49.4 2.9 %collective-permute-start.17 = (bf16[256,256]{1,0:T(8,128)(2,1)S(1)}, bf16[256,256]{1,0:T(8,128)(2,1)S(1)}, u32[]{:S(2)}, u32[]{:S(2)}) collective-permute-start(bf16[256,256]{1,0:T(8,128)(2,1)S(1)} %get-tuple-element.45), channel_id=1, source_target_pairs={{0,12},{1,13},{2,14},{3,15},{4,8},{5,9},{6,10},{7,11},{8,4},{9,5},... | collective-permute-start | bytes 393224 | tf_op jit(solution)/shard_map/ppermute | solution.py:366
  52.4 0.4 collective-permute-start.18
  52.7 1.1 %collective-permute-start.19 = (bf16[256,256]{1,0:T(8,128)(2,1)S(1)}, bf16[256,256]{1,0:T(8,128)(2,1)S(1)}, u32[]{:S(2)}, u32[]{:S(2)}) collective-permute-start(bf16[256,256]{1,0:T(8,128)(2,1)S(1)} %get-tuple-element.47), channel_id=1, source_target_pairs={{0,4},{1,5},{2,6},{3,7},{4,0},{5,1},{6,2},{7,3},{8,12},{9,13},{10,... | collective-permute-start | bytes 393224 | tf_op jit(solution)/shard_map/ppermute | solution.py:366
  53.9 3.9 %collective-permute-done.17.refs_0_ = bf16[256,256]{1,0:T(8,128)(2,1)S(1)} collective-permute-done((bf16[256,256]{1,0:T(8,128)(2,1)S(1)}, bf16[256,256]{1,0:T(8,128)(2,1)S(1)}, u32[]{:S(2)}, u32[]{:S(2)}) %collective-permute-start.17) | collective-permute-done | bytes 131104 | tf_op jit(solution)/shard_map/ppermute | solution.py:366
  57.7 7.1 %collective-permute-done.18.refs_1_ = bf16[256,256]{1,0:T(8,128)(2,1)S(1)} collective-permute-done((bf16[256,256]{1,0:T(8,128)(2,1)S(1)}, bf16[256,256]{1,0:T(8,128)(2,1)S(1)}, u32[]{:S(2)}, u32[]{:S(2)}) %collective-permute-start.18) | collective-permute-done | bytes 131104 | tf_op jit(solution)/shard_map/ppermute | solution.py:366
  64.9 0.0 collective-permute-done.19.refs_2_
  64.9 0.7 %shard_map.83 = (f32[192,256]{1,0:T(8,128)}, f32[64,256]{1,0:T(8,128)}) custom-call(f32[256,256]{1,0:T(8,128)S(1)} %get-tuple-element.44.keep_ref, bf16[256,256]{1,0:T(8,128)(2,1)S(1)} %collective-permute-done.17.refs_0_, bf16[256,256]{1,0:T(8,128)(2,1)S(1)} %collective-permute-done.18.refs_1_, bf16[256,256]{1,0:T(8,128)(2,1)S(1)} %collective-permute-done.19.refs_2_), custom_call_target="tpu_custom_call" | custom-call | tf_op jit(solution)/shard_map/pallas_call | solution.py:343
  (2 shorter events, 0.0 us)
Async XLA Ops:
  0.7 19.4 %copy-start.1 = (bf16[1,4096]{1,0:T(2,128)(2,1)S(1)}, bf16[1,4096]{1,0:T(2,128)(2,1)}, u32[]{:S(2)}) copy-start(bf16[1,4096]{1,0:T(2,128)(2,1)} %param.9) | copy-start | bytes 24580
  3.0 12.2 %collective-permute-start = (bf16[2,64,1024]{2,1,0:T(8,128)(2,1)S(1)}, bf16[2,64,1024]{2,1,0:T(8,128)(2,1)S(1)}, u32[]{:S(2)}, u32[]{:S(2)}) collective-permute-start(bf16[2,64,1024]{2,1,0:T(8,128)(2,1)S(1)} %get-tuple-element.27), channel_id=1, source_target_pairs={{0,3},{1,2},{2,1},{3,0},{4,7},{5,6},{6,5},{7,4},{8,11},{9,10},{10,... | collective-permute-start | bytes 786440 | tf_op jit(solution)/shard_map/ppermute | solution.py:373
  6.9 8.3 %collective-permute-start.5 = (bf16[256,256]{1,0:T(8,128)(2,1)S(1)}, bf16[256,256]{1,0:T(8,128)(2,1)S(1)}, u32[]{:S(2)}, u32[]{:S(2)}) collective-permute-start(bf16[256,256]{1,0:T(8,128)(2,1)S(1)} %get-tuple-element.33.pack_ref), channel_id=1, source_target_pairs={{0,12},{1,13},{2,14},{3,15},{4,8},{5,9},{6,10},{7,11},{8,4},{9,5},... | collective-permute-start | bytes 393224 | tf_op jit(solution)/shard_map/ppermute | solution.py:366
  10.5 10.8 %collective-permute-start.4 = (bf16[256,256]{1,0:T(8,128)(2,1)S(1)}, bf16[256,256]{1,0:T(8,128)(2,1)S(1)}, u32[]{:S(2)}, u32[]{:S(2)}) collective-permute-start(bf16[256,256]{1,0:T(8,128)(2,1)S(1)} %get-tuple-element.33.pack_ref), channel_id=1, source_target_pairs={{0,8},{1,9},{2,10},{3,11},{4,12},{5,13},{6,14},{7,15},{8,0},{9,1},... | collective-permute-start | bytes 393224 | tf_op jit(solution)/shard_map/ppermute | solution.py:366
  10.5 13.7 %collective-permute-start.1 = (bf16[2,64,1024]{2,1,0:T(8,128)(2,1)S(1)}, bf16[2,64,1024]{2,1,0:T(8,128)(2,1)S(1)}, u32[]{:S(2)}, u32[]{:S(2)}) collective-permute-start(bf16[2,64,1024]{2,1,0:T(8,128)(2,1)S(1)} %get-tuple-element.28), channel_id=1, source_target_pairs={{0,2},{1,3},{2,0},{3,1},{4,6},{5,7},{6,4},{7,5},{8,10},{9,11},{10,... | collective-permute-start | bytes 786440 | tf_op jit(solution)/shard_map/ppermute | solution.py:373
  11.0 13.2 %collective-permute-start.2 = (bf16[2,64,1024]{2,1,0:T(8,128)(2,1)S(1)}, bf16[2,64,1024]{2,1,0:T(8,128)(2,1)S(1)}, u32[]{:S(2)}, u32[]{:S(2)}) collective-permute-start(bf16[2,64,1024]{2,1,0:T(8,128)(2,1)S(1)} %get-tuple-element.29), channel_id=1, source_target_pairs={{0,1},{1,0},{2,3},{3,2},{4,5},{5,4},{6,7},{7,6},{8,9},{9,8},{10,11... | collective-permute-start | bytes 786440 | tf_op jit(solution)/shard_map/ppermute | solution.py:373
  15.2 6.1 %collective-permute-start.9 = (bf16[256,256]{1,0:T(8,128)(2,1)S(1)}, bf16[256,256]{1,0:T(8,128)(2,1)S(1)}, u32[]{:S(2)}, u32[]{:S(2)}) collective-permute-start(bf16[256,256]{1,0:T(8,128)(2,1)S(1)} %collective-permute-done.5.refs_7_), channel_id=1, source_target_pairs={{0,16},{16,0},{1,17},{17,1},{2,18},{18,2},{3,19},{19,3},{4,20},{20... | collective-permute-start | bytes 393224 | tf_op jit(solution)/shard_map/ppermute | solution.py:369
  15.2 9.0 %collective-permute-start.3 = (bf16[256,256]{1,0:T(8,128)(2,1)S(1)}, bf16[256,256]{1,0:T(8,128)(2,1)S(1)}, u32[]{:S(2)}, u32[]{:S(2)}) collective-permute-start(bf16[256,256]{1,0:T(8,128)(2,1)S(1)} %get-tuple-element.33.pack_ref), channel_id=1, source_target_pairs={{0,4},{1,5},{2,6},{3,7},{4,0},{5,1},{6,2},{7,3},{8,12},{9,13},{10,... | collective-permute-start | bytes 393224 | tf_op jit(solution)/shard_map/ppermute | solution.py:366
  21.3 3.0 %collective-permute-start.6 = (bf16[272,256]{1,0:T(8,128)(2,1)S(1)}, bf16[272,256]{1,0:T(8,128)(2,1)S(1)}, u32[]{:S(2)}, u32[]{:S(2)}) collective-permute-start(bf16[272,256]{1,0:T(8,128)(2,1)S(1)} %shard_map.78.refs_4_), channel_id=1, source_target_pairs={{0,16},{16,0},{1,17},{17,1},{2,18},{18,2},{3,19},{19,3},{4,20},{20... | collective-permute-start | bytes 417800 | tf_op jit(solution)/shard_map/ppermute | solution.py:369
  21.3 2.9 %collective-permute-start.8 = (bf16[256,256]{1,0:T(8,128)(2,1)S(1)}, bf16[256,256]{1,0:T(8,128)(2,1)S(1)}, u32[]{:S(2)}, u32[]{:S(2)}) collective-permute-start(bf16[256,256]{1,0:T(8,128)(2,1)S(1)} %collective-permute-done.4.refs_6_), channel_id=1, source_target_pairs={{0,16},{16,0},{1,17},{17,1},{2,18},{18,2},{3,19},{19,3},{4,20},{20... | collective-permute-start | bytes 393224 | tf_op jit(solution)/shard_map/ppermute | solution.py:369
  24.2 1.3 %collective-permute-start.7 = (bf16[256,256]{1,0:T(8,128)(2,1)S(1)}, bf16[256,256]{1,0:T(8,128)(2,1)S(1)}, u32[]{:S(2)}, u32[]{:S(2)}) collective-permute-start(bf16[256,256]{1,0:T(8,128)(2,1)S(1)} %collective-permute-done.3.refs_5_), channel_id=1, source_target_pairs={{0,16},{16,0},{1,17},{17,1},{2,18},{18,2},{3,19},{19,3},{4,20},{20... | collective-permute-start | bytes 393224 | tf_op jit(solution)/shard_map/ppermute | solution.py:369
  27.2 7.0 %collective-permute-start.10 = (bf16[64,896]{1,0:T(8,128)(2,1)S(1)}, bf16[64,896]{1,0:T(8,128)(2,1)S(1)}, u32[]{:S(2)}, u32[]{:S(2)}) collective-permute-start(bf16[64,896]{1,0:T(8,128)(2,1)S(1)} %get-tuple-element.34), channel_id=1, source_target_pairs={{0,3},{1,2},{2,1},{3,0},{4,7},{5,6},{6,5},{7,4},{8,11},{9,10},{10,... | collective-permute-start | bytes 344072 | tf_op jit(solution)/shard_map/ppermute | solution.py:373
  27.7 7.4 %collective-permute-start.11 = (bf16[64,896]{1,0:T(8,128)(2,1)S(1)}, bf16[64,896]{1,0:T(8,128)(2,1)S(1)}, u32[]{:S(2)}, u32[]{:S(2)}) collective-permute-start(bf16[64,896]{1,0:T(8,128)(2,1)S(1)} %get-tuple-element.35), channel_id=1, source_target_pairs={{0,2},{1,3},{2,0},{3,1},{4,6},{5,7},{6,4},{7,5},{8,10},{9,11},{10,... | collective-permute-start | bytes 344072 | tf_op jit(solution)/shard_map/ppermute | solution.py:373
  29.3 5.9 %copy-start = (s32[2,1,2]{2,1,0:T(1,128)S(1)}, s32[2,1,2]{2,1,0:T(1,128)}, u32[]{:S(2)}) copy-start(s32[2,1,2]{2,1,0:T(1,128)} %docs.1) | copy-start | bytes 52
  29.3 5.9 %collective-permute-start.12 = (bf16[64,896]{1,0:T(8,128)(2,1)S(1)}, bf16[64,896]{1,0:T(8,128)(2,1)S(1)}, u32[]{:S(2)}, u32[]{:S(2)}) collective-permute-start(bf16[64,896]{1,0:T(8,128)(2,1)S(1)} %get-tuple-element.36), channel_id=1, source_target_pairs={{0,1},{1,0},{2,3},{3,2},{4,5},{5,4},{6,7},{7,6},{8,9},{9,8},{10,11... | collective-permute-start | bytes 344072 | tf_op jit(solution)/shard_map/ppermute | solution.py:373
  38.0 6.1 %collective-permute-start.15 = (bf16[64,640]{1,0:T(8,128)(2,1)S(1)}, bf16[64,640]{1,0:T(8,128)(2,1)S(1)}, u32[]{:S(2)}, u32[]{:S(2)}) collective-permute-start(bf16[64,640]{1,0:T(8,128)(2,1)S(1)} %shard_map.80.refs_0_), channel_id=1, source_target_pairs={{0,3},{1,2},{2,1},{3,0},{4,7},{5,6},{6,5},{7,4},{8,11},{9,10},{10,... | collective-permute-start | bytes 245768 | tf_op jit(solution)/shard_map/ppermute | solution.py:373
  39.3 5.1 %collective-permute-start.14 = (bf16[64,640]{1,0:T(8,128)(2,1)S(1)}, bf16[64,640]{1,0:T(8,128)(2,1)S(1)}, u32[]{:S(2)}, u32[]{:S(2)}) collective-permute-start(bf16[64,640]{1,0:T(8,128)(2,1)S(1)} %shard_map.80.refs_0_), channel_id=1, source_target_pairs={{0,2},{1,3},{2,0},{3,1},{4,6},{5,7},{6,4},{7,5},{8,10},{9,11},{10,... | collective-permute-start | bytes 245768 | tf_op jit(solution)/shard_map/ppermute | solution.py:373
  40.8 4.4 %collective-permute-start.13 = (bf16[64,640]{1,0:T(8,128)(2,1)S(1)}, bf16[64,640]{1,0:T(8,128)(2,1)S(1)}, u32[]{:S(2)}, u32[]{:S(2)}) collective-permute-start(bf16[64,640]{1,0:T(8,128)(2,1)S(1)} %shard_map.80.refs_0_), channel_id=1, source_target_pairs={{0,1},{1,0},{2,3},{3,2},{4,5},{5,4},{6,7},{7,6},{8,9},{9,8},{10,11... | collective-permute-start | bytes 245768 | tf_op jit(solution)/shard_map/ppermute | solution.py:373
  46.8 2.0 %collective-permute-start.16 = (bf16[4,256,256]{2,1,0:T(8,128)(2,1)S(1)}, bf16[4,256,256]{2,1,0:T(8,128)(2,1)S(1)}, u32[]{:S(2)}, u32[]{:S(2)}) collective-permute-start(bf16[4,256,256]{2,1,0:T(8,128)(2,1)S(1)} %get-tuple-element.43), channel_id=1, source_target_pairs={{0,16},{16,0},{1,17},{17,1},{2,18},{18,2},{3,19},{19,3},{4,20},{20... | collective-permute-start | bytes 1572872 | tf_op jit(solution)/shard_map/ppermute | solution.py:369
  49.4 8.3 %collective-permute-start.17 = (bf16[256,256]{1,0:T(8,128)(2,1)S(1)}, bf16[256,256]{1,0:T(8,128)(2,1)S(1)}, u32[]{:S(2)}, u32[]{:S(2)}) collective-permute-start(bf16[256,256]{1,0:T(8,128)(2,1)S(1)} %get-tuple-element.45), channel_id=1, source_target_pairs={{0,12},{1,13},{2,14},{3,15},{4,8},{5,9},{6,10},{7,11},{8,4},{9,5},... | collective-permute-start | bytes 393224 | tf_op jit(solution)/shard_map/ppermute | solution.py:366
  52.4 12.5 %collective-permute-start.18 = (bf16[256,256]{1,0:T(8,128)(2,1)S(1)}, bf16[256,256]{1,0:T(8,128)(2,1)S(1)}, u32[]{:S(2)}, u32[]{:S(2)}) collective-permute-start(bf16[256,256]{1,0:T(8,128)(2,1)S(1)} %get-tuple-element.46), channel_id=1, source_target_pairs={{0,8},{1,9},{2,10},{3,11},{4,12},{5,13},{6,14},{7,15},{8,0},{9,1},... | collective-permute-start | bytes 393224 | tf_op jit(solution)/shard_map/ppermute | solution.py:366
  52.7 12.1 %collective-permute-start.19 = (bf16[256,256]{1,0:T(8,128)(2,1)S(1)}, bf16[256,256]{1,0:T(8,128)(2,1)S(1)}, u32[]{:S(2)}, u32[]{:S(2)}) collective-permute-start(bf16[256,256]{1,0:T(8,128)(2,1)S(1)} %get-tuple-element.47), channel_id=1, source_target_pairs={{0,4},{1,5},{2,6},{3,7},{4,0},{5,1},{6,2},{7,3},{8,12},{9,13},{10,... | collective-permute-start | bytes 393224 | tf_op jit(solution)/shard_map/ppermute | solution.py:366

commit v11 on v10

--- a/solution.py
+++ b/solution.py
@@ -393,12 +393,14 @@
     )(index, qkv_in, out_in, x_in, c_in)
     gain = norm_gain[0].reshape(shards, width)
     blocks = [blocks[0]] + far_first(blocks, PLANE, along_plane)[1:]
-    far = {k: along_z(pack, k) for k in reversed(range(2, planes))}
-    later, _ = lax.optimization_barrier((pack, blocks[3]))
-    near = [along_z(later, 1)] if planes > 1 else []
+    pieces = {0: pack}
+    for step in reversed([1 << bit for bit in range(planes.bit_length() - 1)]):
+        for k in list(pieces):
+            pieces[k ^ step] = along_z(pieces[k], step)
     mine, late_gain, _ = lax.optimization_barrier((pack, gain, blocks[3]))
     (marked,) = call(mark_kernel, [((qkv_rows + heads + shards, width), BF16)], mine, late_gain)
-    own = [marked] + near + [far[k] for k in range(2, planes)]
+    pieces[planes // 2], _ = lax.optimization_barrier((pieces[planes // 2], blocks[3]))
+    own = [marked] + [pieces[k] for k in range(1, planes)]
     other = [to_sibling(piece) for piece in own]
 
     split = ((PLANE, block, cols), BF16)

time: 65.8 us -> 62.1 us (0.944)
  starting transfers between devices: 25.6 us -> 22.5 us
    ppermute x6, starting transfers between devices: 12.9 us -> 9.27 us  [along_z(): return lax.ppermute(value, 'dp', route)]
where the time goes in v11:
time: 62.1 us; the launch traced here: 61.9 us
  waiting for transfers between devices  28.8 us (46%)
  starting transfers between devices  22.5 us (36%)
  Pallas kernels  9.67 us (16%)
  between operations  0.74 us (1%)
    ppermute x6, waiting for transfers between devices, along_z(): return lax.ppermute(value, 'dp', route)  17.7 us
    ppermute x9, starting transfers between devices, along_plane(): return lax.ppermute(value, 'dp', route)  12.1 us
    ppermute x6, starting transfers between devices, along_z(): return lax.ppermute(value, 'dp', route)  9.27 us
    ppermute x9, waiting for transfers between devices, along_plane(): return lax.ppermute(value, 'dp', route)  8.2 us
    pallas_call x6, Pallas kernels, call(): pl.pallas_call(kernel, out_shape=[jax.ShapeDtypeStruct(shape, dtype) for...  7.44 us
    ppermute x5, waiting for transfers between devices, to_sibling(): return lax.ppermute(value, 'section', [(0, 1), (1, 0)])  2.92 us
    pallas_call x1, Pallas kernels, planar(): pl.pallas_call(functools.partial(blocks_kernel, planes), out_shape=[jax.S...  2.23 us
  transfers between devices with their start and end apart: 20, of which 12 were waited for; matrix products, arithmetic and copies ran while one was open for 0% of the time, Pallas kernels for 0%

profile of v11, /device:TPU:0, one launch (start us, length us, event | category | flops | bytes accessed | tf_op | source)
XLA Modules:
  0.0 61.9 jit_solution(2560428671204452143)
XLA Ops:
  0.6 0.1 pad_add_fusion.index
  0.7 0.0 copy-start.1
  0.7 2.2 %shard_map.77 = (bf16[256,256]{1,0:T(8,128)(2,1)S(1)}, bf16[2,64,1024]{2,1,0:T(8,128)(2,1)S(1)}, bf16[2,64,1024]{2,1,0:T(8,128)(2,1)S(1)}, bf16[2,64,1024]{2,1,0:T(8,128)(2,1)S(1)}, bf16[2,64,1024]{2,1,0:T(8,128)(2,1)S(1)}) custom-call(s32[3]{0:T(128)S(1)} %pad_add_fusion.index, bf16[192,256]{1,0:T(8,128)(2,1)} %bitcast.11, bf16[64,256]{1,0:T(8,128)(2,1)} %bitcast.12, ...), custom_call_target="tpu_custom_call" | custom-call | tf_op jit(solution)/shard_map/pallas_call | solution.py:386
  3.0 4.0 %collective-permute-start = (bf16[2,64,1024]{2,1,0:T(8,128)(2,1)S(1)}, bf16[2,64,1024]{2,1,0:T(8,128)(2,1)S(1)}, u32[]{:S(2)}, u32[]{:S(2)}) collective-permute-start(bf16[2,64,1024]{2,1,0:T(8,128)(2,1)S(1)} %get-tuple-element.27), channel_id=1, source_target_pairs={{0,3},{1,2},{2,1},{3,0},{4,7},{5,6},{6,5},{7,4},{8,11},{9,10},{10,... | collective-permute-start | bytes 786440 | tf_op jit(solution)/shard_map/ppermute | solution.py:373
  6.9 2.6 %collective-permute-start.4 = (bf16[256,256]{1,0:T(8,128)(2,1)S(1)}, bf16[256,256]{1,0:T(8,128)(2,1)S(1)}, u32[]{:S(2)}, u32[]{:S(2)}) collective-permute-start(bf16[256,256]{1,0:T(8,128)(2,1)S(1)} %get-tuple-element.31.pack_ref), channel_id=1, source_target_pairs={{0,8},{1,9},{2,10},{3,11},{4,12},{5,13},{6,14},{7,15},{8,0},{9,1},... | collective-permute-start | bytes 393224 | tf_op jit(solution)/shard_map/ppermute | solution.py:366
  9.5 1.6 %collective-permute-start.3 = (bf16[256,256]{1,0:T(8,128)(2,1)S(1)}, bf16[256,256]{1,0:T(8,128)(2,1)S(1)}, u32[]{:S(2)}, u32[]{:S(2)}) collective-permute-start(bf16[256,256]{1,0:T(8,128)(2,1)S(1)} %get-tuple-element.31.pack_ref), channel_id=1, source_target_pairs={{0,4},{1,5},{2,6},{3,7},{4,0},{5,1},{6,2},{7,3},{8,12},{9,13},{10,... | collective-permute-start | bytes 393224 | tf_op jit(solution)/shard_map/ppermute | solution.py:366
  11.1 0.5 collective-permute-start.1
  11.6 0.5 collective-permute-start.2
  12.1 3.6 %collective-permute-done.4.refs_6_ = bf16[256,256]{1,0:T(8,128)(2,1)S(1)} collective-permute-done((bf16[256,256]{1,0:T(8,128)(2,1)S(1)}, bf16[256,256]{1,0:T(8,128)(2,1)S(1)}, u32[]{:S(2)}, u32[]{:S(2)}) %collective-permute-start.4) | collective-permute-done | bytes 131104 | tf_op jit(solution)/shard_map/ppermute | solution.py:366
  15.7 0.6 collective-permute-start.5
  16.3 0.0 collective-permute-done.3.refs_5_
  16.3 0.0 collective-permute-start.7
  16.3 0.0 copy-done.1
  16.3 0.1 reduce
  16.3 0.0 collective-permute-done.refs_1_
  16.4 0.6 collective-permute-start.6
  16.9 3.7 %collective-permute-done.5.refs_7_ = bf16[256,256]{1,0:T(8,128)(2,1)S(1)} collective-permute-done((bf16[256,256]{1,0:T(8,128)(2,1)S(1)}, bf16[256,256]{1,0:T(8,128)(2,1)S(1)}, u32[]{:S(2)}, u32[]{:S(2)}) %collective-permute-start.5) | collective-permute-done | bytes 131104 | tf_op jit(solution)/shard_map/ppermute | solution.py:366
  20.7 0.0 collective-permute-start.9
  20.7 0.0 collective-permute-done.7.refs_9_
  20.7 0.5 collective-permute-start.8
  21.2 0.0 collective-permute-done.1.refs_2_
  21.2 0.0 collective-permute-done.2.refs_3_
  21.2 0.8 %collective-permute-done.9.refs_11_ = bf16[256,256]{1,0:T(8,128)(2,1)S(1)} collective-permute-done((bf16[256,256]{1,0:T(8,128)(2,1)S(1)}, bf16[256,256]{1,0:T(8,128)(2,1)S(1)}, u32[]{:S(2)}, u32[]{:S(2)}) %collective-permute-start.9) | collective-permute-done | bytes 131104 | tf_op jit(solution)/shard_map/ppermute | solution.py:369
  22.0 0.2 collective-permute-done.8.refs_10_
  22.2 0.0 collective-permute-done.6.refs_8_
  22.2 1.6 %shard_map.79 = (bf16[4,64,1024]{2,1,0:T(8,128)(2,1)S(1)}, bf16[4,64,1024]{2,1,0:T(8,128)(2,1)S(1)}, bf16[4,512,256]{2,1,0:T(8,128)(2,1)S(1)}, f32[4,8,256]{2,1,...) custom-call(s32[3]{0:T(128)S(1)} %pad_add_fusion.index, ...), custom_call_target="tpu_custom_call" | custom-call | tf_op jit(solution)/shard_map/pallas_call | solution.py:343
  23.8 0.5 collective-permute-start.10
  24.3 1.6 %collective-permute-start.11 = (bf16[64,896]{1,0:T(8,128)(2,1)S(1)}, bf16[64,896]{1,0:T(8,128)(2,1)S(1)}, u32[]{:S(2)}, u32[]{:S(2)}) collective-permute-start(bf16[64,896]{1,0:T(8,128)(2,1)S(1)} %get-tuple-element.35), channel_id=1, source_target_pairs={{0,2},{1,3},{2,0},{3,1},{4,6},{5,7},{6,4},{7,5},{8,10},{9,11},{10,... | collective-permute-start | bytes 344072 | tf_op jit(solution)/shard_map/ppermute | solution.py:373
  25.9 0.0 copy-start
  25.9 1.5 %collective-permute-start.12 = (bf16[64,896]{1,0:T(8,128)(2,1)S(1)}, bf16[64,896]{1,0:T(8,128)(2,1)S(1)}, u32[]{:S(2)}, u32[]{:S(2)}) collective-permute-start(bf16[64,896]{1,0:T(8,128)(2,1)S(1)} %get-tuple-element.36), channel_id=1, source_target_pairs={{0,1},{1,0},{2,3},{3,2},{4,5},{5,4},{6,7},{7,6},{8,9},{9,8},{10,11... | collective-permute-start | bytes 344072 | tf_op jit(solution)/shard_map/ppermute | solution.py:373
  27.4 3.4 %collective-permute-done.10.refs_0_ = bf16[64,896]{1,0:T(8,128)(2,1)S(1)} collective-permute-done((bf16[64,896]{1,0:T(8,128)(2,1)S(1)}, bf16[64,896]{1,0:T(8,128)(2,1)S(1)}, u32[]{:S(2)}, u32[]{:S(2)}) %collective-permute-start.10) | collective-permute-done | bytes 114720 | tf_op jit(solution)/shard_map/ppermute | solution.py:373
  30.8 1.1 %collective-permute-done.11.refs_1_ = bf16[64,896]{1,0:T(8,128)(2,1)S(1)} collective-permute-done((bf16[64,896]{1,0:T(8,128)(2,1)S(1)}, bf16[64,896]{1,0:T(8,128)(2,1)S(1)}, u32[]{:S(2)}, u32[]{:S(2)}) %collective-permute-start.11) | collective-permute-done | bytes 114720 | tf_op jit(solution)/shard_map/ppermute | solution.py:373
  31.9 0.0 collective-permute-done.12.refs_2_
  31.9 0.0 copy-done
  31.9 2.9 %shard_map.80.refs_0_ = bf16[64,640]{1,0:T(8,128)(2,1)S(1)} custom-call(s32[3]{0:T(128)S(1)} %pad_add_fusion.index, s32[2,1,2]{2,1,0:T(1,128)S(1)} %copy-done, bf16[64,896]{1,0:T(8,128)(2,1)S(1)} %collective-permute-done.10.refs_0_, bf16[64,896]{1,0:T(8,128)(2,1)S(1)} %collective-permute-done.11.refs_1_, ...), custom_call_target="tpu_custom_call" | custom-call | tf_op jit(solution)/shard_map/pallas_call | solution.py:343
  34.8 1.4 %collective-permute-start.15 = (bf16[64,640]{1,0:T(8,128)(2,1)S(1)}, bf16[64,640]{1,0:T(8,128)(2,1)S(1)}, u32[]{:S(2)}, u32[]{:S(2)}) collective-permute-start(bf16[64,640]{1,0:T(8,128)(2,1)S(1)} %shard_map.80.refs_0_), channel_id=1, source_target_pairs={{0,3},{1,2},{2,1},{3,0},{4,7},{5,6},{6,5},{7,4},{8,11},{9,10},{10,... | collective-permute-start | bytes 245768 | tf_op jit(solution)/shard_map/ppermute | solution.py:373
  36.1 1.5 %collective-permute-start.14 = (bf16[64,640]{1,0:T(8,128)(2,1)S(1)}, bf16[64,640]{1,0:T(8,128)(2,1)S(1)}, u32[]{:S(2)}, u32[]{:S(2)}) collective-permute-start(bf16[64,640]{1,0:T(8,128)(2,1)S(1)} %shard_map.80.refs_0_), channel_id=1, source_target_pairs={{0,2},{1,3},{2,0},{3,1},{4,6},{5,7},{6,4},{7,5},{8,10},{9,11},{10,... | collective-permute-start | bytes 245768 | tf_op jit(solution)/shard_map/ppermute | solution.py:373
  37.6 0.7 %collective-permute-start.13 = (bf16[64,640]{1,0:T(8,128)(2,1)S(1)}, bf16[64,640]{1,0:T(8,128)(2,1)S(1)}, u32[]{:S(2)}, u32[]{:S(2)}) collective-permute-start(bf16[64,640]{1,0:T(8,128)(2,1)S(1)} %shard_map.80.refs_0_), channel_id=1, source_target_pairs={{0,1},{1,0},{2,3},{3,2},{4,5},{5,4},{6,7},{7,6},{8,9},{9,8},{10,11... | collective-permute-start | bytes 245768 | tf_op jit(solution)/shard_map/ppermute | solution.py:373
  38.3 2.5 %collective-permute-done.15.refs_3_ = bf16[64,640]{1,0:T(8,128)(2,1)S(1)} collective-permute-done((bf16[64,640]{1,0:T(8,128)(2,1)S(1)}, bf16[64,640]{1,0:T(8,128)(2,1)S(1)}, u32[]{:S(2)}, u32[]{:S(2)}) %collective-permute-start.15) | collective-permute-done | bytes 81952 | tf_op jit(solution)/shard_map/ppermute | solution.py:373
  40.8 0.3 collective-permute-done.14.refs_2_
  41.1 0.9 %collective-permute-done.13.refs_1_ = bf16[64,640]{1,0:T(8,128)(2,1)S(1)} collective-permute-done((bf16[64,640]{1,0:T(8,128)(2,1)S(1)}, bf16[64,640]{1,0:T(8,128)(2,1)S(1)}, u32[]{:S(2)}, u32[]{:S(2)}) %collective-permute-start.13) | collective-permute-done | bytes 81952 | tf_op jit(solution)/shard_map/ppermute | solution.py:373
  42.0 1.6 %shard_map.81 = (f32[4,256,256]{2,1,0:T(8,128)S(1)}, bf16[4,256,256]{2,1,0:T(8,128)(2,1)S(1)}) custom-call(s32[3]{0:T(128)S(1)} %pad_add_fusion.index, bf16[64,640]{1,0:T(8,128)(2,1)S(1)} %shard_map.80.refs_0_, bf16[64,640]{1,0:T(8,128)(2,1)S(1)} %collective-permute-done.13.refs_1_, bf16[64,640]{1,0:T(8,128)(2,1)S(1)} %collective-permute-done.14.refs_2_, ...), custom_call_target="tpu_custom_call" | custom-call | tf_op jit(solution)/shard_map/pallas_call | solution.py:343
  43.6 0.1 collective-permute-start.16
  43.7 1.9 %collective-permute-done.16.come_ref = bf16[4,256,256]{2,1,0:T(8,128)(2,1)S(1)} collective-permute-done((bf16[4,256,256]{2,1,0:T(8,128)(2,1)S(1)}, bf16[4,256,256]{2,1,0:T(8,128)(2,1)S(1)}, u32[]{:S(2)}, u32[]{:S(2)}) %collective-permute-start.16) | collective-permute-done | bytes 524320 | tf_op jit(solution)/shard_map/ppermute | solution.py:369
  45.6 0.6 %shard_map.82 = (f32[256,256]{1,0:T(8,128)S(1)}, bf16[256,256]{1,0:T(8,128)(2,1)S(1)}, bf16[256,256]{1,0:T(8,128)(2,1)S(1)}, bf16[256,256]{1,0:T(8,128)(2,1)S(1)}) custom-call(s32[3]{0:T(128)S(1)} %pad_add_fusion.index, f32[4,256,256]{2,1,0:T(8,128)S(1)} %get-tuple-element.42.keep_ref, bf16[4,256,256]{2,1,0:T(8,128)(2,1)S(1)} %collective-permute-done.16.come_ref), custom_call_target="tpu_custom_call" | custom-call | tf_op jit(solution)/shard_map/pallas_call | solution.py:343
  46.2 3.9 %collective-permute-start.17 = (bf16[256,256]{1,0:T(8,128)(2,1)S(1)}, bf16[256,256]{1,0:T(8,128)(2,1)S(1)}, u32[]{:S(2)}, u32[]{:S(2)}) collective-permute-start(bf16[256,256]{1,0:T(8,128)(2,1)S(1)} %get-tuple-element.45), channel_id=1, source_target_pairs={{0,12},{1,13},{2,14},{3,15},{4,8},{5,9},{6,10},{7,11},{8,4},{9,5},... | collective-permute-start | bytes 393224 | tf_op jit(solution)/shard_map/ppermute | solution.py:366
  50.1 0.0 collective-permute-start.18
  50.1 0.6 %collective-permute-start.19 = (bf16[256,256]{1,0:T(8,128)(2,1)S(1)}, bf16[256,256]{1,0:T(8,128)(2,1)S(1)}, u32[]{:S(2)}, u32[]{:S(2)}) collective-permute-start(bf16[256,256]{1,0:T(8,128)(2,1)S(1)} %get-tuple-element.47), channel_id=1, source_target_pairs={{0,4},{1,5},{2,6},{3,7},{4,0},{5,1},{6,2},{7,3},{8,12},{9,13},{10,... | collective-permute-start | bytes 393224 | tf_op jit(solution)/shard_map/ppermute | solution.py:366
  50.8 3.7 %collective-permute-done.17.refs_0_ = bf16[256,256]{1,0:T(8,128)(2,1)S(1)} collective-permute-done((bf16[256,256]{1,0:T(8,128)(2,1)S(1)}, bf16[256,256]{1,0:T(8,128)(2,1)S(1)}, u32[]{:S(2)}, u32[]{:S(2)}) %collective-permute-start.17) | collective-permute-done | bytes 131104 | tf_op jit(solution)/shard_map/ppermute | solution.py:366
  54.5 6.7 %collective-permute-done.18.refs_1_ = bf16[256,256]{1,0:T(8,128)(2,1)S(1)} collective-permute-done((bf16[256,256]{1,0:T(8,128)(2,1)S(1)}, bf16[256,256]{1,0:T(8,128)(2,1)S(1)}, u32[]{:S(2)}, u32[]{:S(2)}) %collective-permute-start.18) | collective-permute-done | bytes 131104 | tf_op jit(solution)/shard_map/ppermute | solution.py:366
  61.2 0.0 collective-permute-done.19.refs_2_
  61.2 0.7 %shard_map.83 = (f32[192,256]{1,0:T(8,128)}, f32[64,256]{1,0:T(8,128)}) custom-call(f32[256,256]{1,0:T(8,128)S(1)} %get-tuple-element.44.keep_ref, bf16[256,256]{1,0:T(8,128)(2,1)S(1)} %collective-permute-done.17.refs_0_, bf16[256,256]{1,0:T(8,128)(2,1)S(1)} %collective-permute-done.18.refs_1_, bf16[256,256]{1,0:T(8,128)(2,1)S(1)} %collective-permute-done.19.refs_2_), custom_call_target="tpu_custom_call" | custom-call | tf_op jit(solution)/shard_map/pallas_call | solution.py:343
  (2 shorter events, 0.0 us)
Async XLA Ops:
  0.7 15.5 %copy-start.1 = (bf16[1,4096]{1,0:T(2,128)(2,1)S(1)}, bf16[1,4096]{1,0:T(2,128)(2,1)}, u32[]{:S(2)}) copy-start(bf16[1,4096]{1,0:T(2,128)(2,1)} %param.9) | copy-start | bytes 24580
  3.0 13.4 %collective-permute-start = (bf16[2,64,1024]{2,1,0:T(8,128)(2,1)S(1)}, bf16[2,64,1024]{2,1,0:T(8,128)(2,1)S(1)}, u32[]{:S(2)}, u32[]{:S(2)}) collective-permute-start(bf16[2,64,1024]{2,1,0:T(8,128)(2,1)S(1)} %get-tuple-element.27), channel_id=1, source_target_pairs={{0,3},{1,2},{2,1},{3,0},{4,7},{5,6},{6,5},{7,4},{8,11},{9,10},{10,... | collective-permute-start | bytes 786440 | tf_op jit(solution)/shard_map/ppermute | solution.py:373
  6.9 8.8 %collective-permute-start.4 = (bf16[256,256]{1,0:T(8,128)(2,1)S(1)}, bf16[256,256]{1,0:T(8,128)(2,1)S(1)}, u32[]{:S(2)}, u32[]{:S(2)}) collective-permute-start(bf16[256,256]{1,0:T(8,128)(2,1)S(1)} %get-tuple-element.31.pack_ref), channel_id=1, source_target_pairs={{0,8},{1,9},{2,10},{3,11},{4,12},{5,13},{6,14},{7,15},{8,0},{9,1},... | collective-permute-start | bytes 393224 | tf_op jit(solution)/shard_map/ppermute | solution.py:366
  9.5 6.7 %collective-permute-start.3 = (bf16[256,256]{1,0:T(8,128)(2,1)S(1)}, bf16[256,256]{1,0:T(8,128)(2,1)S(1)}, u32[]{:S(2)}, u32[]{:S(2)}) collective-permute-start(bf16[256,256]{1,0:T(8,128)(2,1)S(1)} %get-tuple-element.31.pack_ref), channel_id=1, source_target_pairs={{0,4},{1,5},{2,6},{3,7},{4,0},{5,1},{6,2},{7,3},{8,12},{9,13},{10,... | collective-permute-start | bytes 393224 | tf_op jit(solution)/shard_map/ppermute | solution.py:366
  11.1 10.1 %collective-permute-start.1 = (bf16[2,64,1024]{2,1,0:T(8,128)(2,1)S(1)}, bf16[2,64,1024]{2,1,0:T(8,128)(2,1)S(1)}, u32[]{:S(2)}, u32[]{:S(2)}) collective-permute-start(bf16[2,64,1024]{2,1,0:T(8,128)(2,1)S(1)} %get-tuple-element.28), channel_id=1, source_target_pairs={{0,2},{1,3},{2,0},{3,1},{4,6},{5,7},{6,4},{7,5},{8,10},{9,11},{10,... | collective-permute-start | bytes 786440 | tf_op jit(solution)/shard_map/ppermute | solution.py:373
  11.6 9.6 %collective-permute-start.2 = (bf16[2,64,1024]{2,1,0:T(8,128)(2,1)S(1)}, bf16[2,64,1024]{2,1,0:T(8,128)(2,1)S(1)}, u32[]{:S(2)}, u32[]{:S(2)}) collective-permute-start(bf16[2,64,1024]{2,1,0:T(8,128)(2,1)S(1)} %get-tuple-element.29), channel_id=1, source_target_pairs={{0,1},{1,0},{2,3},{3,2},{4,5},{5,4},{6,7},{7,6},{8,9},{9,8},{10,11... | collective-permute-start | bytes 786440 | tf_op jit(solution)/shard_map/ppermute | solution.py:373
  15.7 5.0 %collective-permute-start.5 = (bf16[256,256]{1,0:T(8,128)(2,1)S(1)}, bf16[256,256]{1,0:T(8,128)(2,1)S(1)}, u32[]{:S(2)}, u32[]{:S(2)}) collective-permute-start(bf16[256,256]{1,0:T(8,128)(2,1)S(1)} %collective-permute-done.4.refs_6_), channel_id=1, source_target_pairs={{0,4},{1,5},{2,6},{3,7},{4,0},{5,1},{6,2},{7,3},{8,12},{9,13},{10,... | collective-permute-start | bytes 393224 | tf_op jit(solution)/shard_map/ppermute | solution.py:366
  16.3 4.4 %collective-permute-start.7 = (bf16[256,256]{1,0:T(8,128)(2,1)S(1)}, bf16[256,256]{1,0:T(8,128)(2,1)S(1)}, u32[]{:S(2)}, u32[]{:S(2)}) collective-permute-start(bf16[256,256]{1,0:T(8,128)(2,1)S(1)} %collective-permute-done.3.refs_5_), channel_id=1, source_target_pairs={{0,16},{16,0},{1,17},{17,1},{2,18},{18,2},{3,19},{19,3},{4,20},{20... | collective-permute-start | bytes 393224 | tf_op jit(solution)/shard_map/ppermute | solution.py:369
  16.4 5.8 %collective-permute-start.6 = (bf16[272,256]{1,0:T(8,128)(2,1)S(1)}, bf16[272,256]{1,0:T(8,128)(2,1)S(1)}, u32[]{:S(2)}, u32[]{:S(2)}) collective-permute-start(bf16[272,256]{1,0:T(8,128)(2,1)S(1)} %shard_map.78.refs_4_), channel_id=1, source_target_pairs={{0,16},{16,0},{1,17},{17,1},{2,18},{18,2},{3,19},{19,3},{4,20},{20... | collective-permute-start | bytes 417800 | tf_op jit(solution)/shard_map/ppermute | solution.py:369
  20.7 1.3 %collective-permute-start.9 = (bf16[256,256]{1,0:T(8,128)(2,1)S(1)}, bf16[256,256]{1,0:T(8,128)(2,1)S(1)}, u32[]{:S(2)}, u32[]{:S(2)}) collective-permute-start(bf16[256,256]{1,0:T(8,128)(2,1)S(1)} %collective-permute-done.5.refs_7_), channel_id=1, source_target_pairs={{0,16},{16,0},{1,17},{17,1},{2,18},{18,2},{3,19},{19,3},{4,20},{20... | collective-permute-start | bytes 393224 | tf_op jit(solution)/shard_map/ppermute | solution.py:369
  20.7 1.5 %collective-permute-start.8 = (bf16[256,256]{1,0:T(8,128)(2,1)S(1)}, bf16[256,256]{1,0:T(8,128)(2,1)S(1)}, u32[]{:S(2)}, u32[]{:S(2)}) collective-permute-start(bf16[256,256]{1,0:T(8,128)(2,1)S(1)} %collective-permute-done.4.refs_6_), channel_id=1, source_target_pairs={{0,16},{16,0},{1,17},{17,1},{2,18},{18,2},{3,19},{19,3},{4,20},{20... | collective-permute-start | bytes 393224 | tf_op jit(solution)/shard_map/ppermute | solution.py:369
  23.8 7.0 %collective-permute-start.10 = (bf16[64,896]{1,0:T(8,128)(2,1)S(1)}, bf16[64,896]{1,0:T(8,128)(2,1)S(1)}, u32[]{:S(2)}, u32[]{:S(2)}) collective-permute-start(bf16[64,896]{1,0:T(8,128)(2,1)S(1)} %get-tuple-element.34), channel_id=1, source_target_pairs={{0,3},{1,2},{2,1},{3,0},{4,7},{5,6},{6,5},{7,4},{8,11},{9,10},{10,... | collective-permute-start | bytes 344072 | tf_op jit(solution)/shard_map/ppermute | solution.py:373
  24.3 7.6 %collective-permute-start.11 = (bf16[64,896]{1,0:T(8,128)(2,1)S(1)}, bf16[64,896]{1,0:T(8,128)(2,1)S(1)}, u32[]{:S(2)}, u32[]{:S(2)}) collective-permute-start(bf16[64,896]{1,0:T(8,128)(2,1)S(1)} %get-tuple-element.35), channel_id=1, source_target_pairs={{0,2},{1,3},{2,0},{3,1},{4,6},{5,7},{6,4},{7,5},{8,10},{9,11},{10,... | collective-permute-start | bytes 344072 | tf_op jit(solution)/shard_map/ppermute | solution.py:373
  25.9 6.0 %copy-start = (s32[2,1,2]{2,1,0:T(1,128)S(1)}, s32[2,1,2]{2,1,0:T(1,128)}, u32[]{:S(2)}) copy-start(s32[2,1,2]{2,1,0:T(1,128)} %docs.1) | copy-start | bytes 52
  25.9 6.0 %collective-permute-start.12 = (bf16[64,896]{1,0:T(8,128)(2,1)S(1)}, bf16[64,896]{1,0:T(8,128)(2,1)S(1)}, u32[]{:S(2)}, u32[]{:S(2)}) collective-permute-start(bf16[64,896]{1,0:T(8,128)(2,1)S(1)} %get-tuple-element.36), channel_id=1, source_target_pairs={{0,1},{1,0},{2,3},{3,2},{4,5},{5,4},{6,7},{7,6},{8,9},{9,8},{10,11... | collective-permute-start | bytes 344072 | tf_op jit(solution)/shard_map/ppermute | solution.py:373
  34.8 6.0 %collective-permute-start.15 = (bf16[64,640]{1,0:T(8,128)(2,1)S(1)}, bf16[64,640]{1,0:T(8,128)(2,1)S(1)}, u32[]{:S(2)}, u32[]{:S(2)}) collective-permute-start(bf16[64,640]{1,0:T(8,128)(2,1)S(1)} %shard_map.80.refs_0_), channel_id=1, source_target_pairs={{0,3},{1,2},{2,1},{3,0},{4,7},{5,6},{6,5},{7,4},{8,11},{9,10},{10,... | collective-permute-start | bytes 245768 | tf_op jit(solution)/shard_map/ppermute | solution.py:373
  36.1 5.0 %collective-permute-start.14 = (bf16[64,640]{1,0:T(8,128)(2,1)S(1)}, bf16[64,640]{1,0:T(8,128)(2,1)S(1)}, u32[]{:S(2)}, u32[]{:S(2)}) collective-permute-start(bf16[64,640]{1,0:T(8,128)(2,1)S(1)} %shard_map.80.refs_0_), channel_id=1, source_target_pairs={{0,2},{1,3},{2,0},{3,1},{4,6},{5,7},{6,4},{7,5},{8,10},{9,11},{10,... | collective-permute-start | bytes 245768 | tf_op jit(solution)/shard_map/ppermute | solution.py:373
  37.6 4.4 %collective-permute-start.13 = (bf16[64,640]{1,0:T(8,128)(2,1)S(1)}, bf16[64,640]{1,0:T(8,128)(2,1)S(1)}, u32[]{:S(2)}, u32[]{:S(2)}) collective-permute-start(bf16[64,640]{1,0:T(8,128)(2,1)S(1)} %shard_map.80.refs_0_), channel_id=1, source_target_pairs={{0,1},{1,0},{2,3},{3,2},{4,5},{5,4},{6,7},{7,6},{8,9},{9,8},{10,11... | collective-permute-start | bytes 245768 | tf_op jit(solution)/shard_map/ppermute | solution.py:373
  43.6 2.0 %collective-permute-start.16 = (bf16[4,256,256]{2,1,0:T(8,128)(2,1)S(1)}, bf16[4,256,256]{2,1,0:T(8,128)(2,1)S(1)}, u32[]{:S(2)}, u32[]{:S(2)}) collective-permute-start(bf16[4,256,256]{2,1,0:T(8,128)(2,1)S(1)} %get-tuple-element.43), channel_id=1, source_target_pairs={{0,16},{16,0},{1,17},{17,1},{2,18},{18,2},{3,19},{19,3},{4,20},{20... | collective-permute-start | bytes 1572872 | tf_op jit(solution)/shard_map/ppermute | solution.py:369
  46.2 8.3 %collective-permute-start.17 = (bf16[256,256]{1,0:T(8,128)(2,1)S(1)}, bf16[256,256]{1,0:T(8,128)(2,1)S(1)}, u32[]{:S(2)}, u32[]{:S(2)}) collective-permute-start(bf16[256,256]{1,0:T(8,128)(2,1)S(1)} %get-tuple-element.45), channel_id=1, source_target_pairs={{0,12},{1,13},{2,14},{3,15},{4,8},{5,9},{6,10},{7,11},{8,4},{9,5},... | collective-permute-start | bytes 393224 | tf_op jit(solution)/shard_map/ppermute | solution.py:366
  50.1 11.1 %collective-permute-start.18 = (bf16[256,256]{1,0:T(8,128)(2,1)S(1)}, bf16[256,256]{1,0:T(8,128)(2,1)S(1)}, u32[]{:S(2)}, u32[]{:S(2)}) collective-permute-start(bf16[256,256]{1,0:T(8,128)(2,1)S(1)} %get-tuple-element.46), channel_id=1, source_target_pairs={{0,8},{1,9},{2,10},{3,11},{4,12},{5,13},{6,14},{7,15},{8,0},{9,1},... | collective-permute-start | bytes 393224 | tf_op jit(solution)/shard_map/ppermute | solution.py:366
  50.1 11.1 %collective-permute-start.19 = (bf16[256,256]{1,0:T(8,128)(2,1)S(1)}, bf16[256,256]{1,0:T(8,128)(2,1)S(1)}, u32[]{:S(2)}, u32[]{:S(2)}) collective-permute-start(bf16[256,256]{1,0:T(8,128)(2,1)S(1)} %get-tuple-element.47), channel_id=1, source_target_pairs={{0,4},{1,5},{2,6},{3,7},{4,0},{5,1},{6,2},{7,3},{8,12},{9,13},{10,... | collective-permute-start | bytes 393224 | tf_op jit(solution)/shard_map/ppermute | solution.py:366

commit v12 on v11

--- a/solution.py
+++ b/solution.py
@@ -141,9 +141,14 @@
     return copies
 
 
-def mark_kernel(pack_ref, gain_ref, out_ref):
+def mark_kernel(planes, index, pack_ref, gain_ref, x_ref, c_ref, out_ref, block_ref, sems):
+    copies = block_copies(planes, index, 0, (x_ref, c_ref), block_ref, sems)
+    for copy in copies:
+        copy.start()
     out_ref[: pack_ref.shape[0], :] = pack_ref[...]
     out_ref[pack_ref.shape[0] :, :] = gain_ref[...]
+    for copy in copies:
+        copy.wait()
 
 
 def blocks_kernel(planes, index, qkv_ref, wout_ref, x_ref, c_ref, pack_ref, *refs):
@@ -153,8 +158,8 @@
         pltpu.make_async_copy(qkv_ref, pack_ref.at[:qkv_rows], pack_sems.at[0]),
         pltpu.make_async_copy(wout_ref, pack_ref.at[qkv_rows:], pack_sems.at[1]),
     ]
-    for k, out_ref in enumerate(out_refs):
-        copies += block_copies(planes, index, k, (x_ref, c_ref), out_ref, sems.at[k])
+    for k, out_ref in enumerate(out_refs, 1):
+        copies += block_copies(planes, index, k, (x_ref, c_ref), out_ref, sems.at[k - 1])
     for copy in copies:
         copy.start()
     for copy in copies:
@@ -316,10 +321,11 @@
 
 
 def merge_kernel(index, keep_ref, come_ref, *out_refs):
-    place = index[1]
+    place, count = index[1], len(out_refs)
     out_refs[0][...] = keep_ref[place] + come_ref[place].astype(F32)
-    for k in range(1, len(out_refs)):
-        out_refs[k][...] = (keep_ref[place ^ k] + come_ref[place ^ k].astype(F32)).astype(BF16)
+    for k in range(1, count):
+        at = (place + k) & (count - 1)
+        out_refs[k][...] = (keep_ref[at] + come_ref[at].astype(F32)).astype(BF16)
 
 
 def last_kernel(qkv_rows, keep_ref, *refs):
@@ -365,6 +371,10 @@
         route = [(a * PLANE + b, (a ^ k) * PLANE + b) for a in range(planes) for b in range(PLANE)]
         return lax.ppermute(value, "dp", route)
 
+    def round_z(value, k):
+        route = [(a * PLANE + b, (a + k) % planes * PLANE + b) for a in range(planes) for b in range(PLANE)]
+        return lax.ppermute(value, "dp", route)
+
     def to_sibling(value):
         return lax.ppermute(value, "section", [(0, 1), (1, 0)])
 
@@ -385,20 +395,27 @@
     one_block = jax.ShapeDtypeStruct((2, block, cols), BF16)
     pack, *blocks = pl.pallas_call(
         functools.partial(blocks_kernel, planes),
-        out_shape=[jax.ShapeDtypeStruct((qkv_rows + heads, width), BF16)] + [one_block] * PLANE,
+        out_shape=[jax.ShapeDtypeStruct((qkv_rows + heads, width), BF16)] + [one_block] * (PLANE - 1),
         in_specs=[smem] + [hbm] * 4,
-        out_specs=[vmem] * (PLANE + 1),
-        scratch_shapes=[pltpu.SemaphoreType.DMA((2,)), pltpu.SemaphoreType.DMA((PLANE, 2 * planes))],
+        out_specs=[vmem] * PLANE,
+        scratch_shapes=[pltpu.SemaphoreType.DMA((2,)), pltpu.SemaphoreType.DMA((PLANE - 1, 2 * planes))],
         compiler_params=params,
     )(index, qkv_in, out_in, x_in, c_in)
     gain = norm_gain[0].reshape(shards, width)
-    blocks = [blocks[0]] + far_first(blocks, PLANE, along_plane)[1:]
+    blocks = far_first([None] + blocks, PLANE, along_plane)
     pieces = {0: pack}
     for step in reversed([1 << bit for bit in range(planes.bit_length() - 1)]):
         for k in list(pieces):
             pieces[k ^ step] = along_z(pieces[k], step)
     mine, late_gain, _ = lax.optimization_barrier((pack, gain, blocks[3]))
-    (marked,) = call(mark_kernel, [((qkv_rows + heads + shards, width), BF16)], mine, late_gain)
+    marked, blocks[0] = pl.pallas_call(
+        functools.partial(mark_kernel, planes),
+        out_shape=[jax.ShapeDtypeStruct((qkv_rows + heads + shards, width), BF16), one_block],
+        in_specs=[smem] + [vmem] * 2 + [hbm] * 2,
+        out_specs=[vmem] * 2,
+        scratch_shapes=[pltpu.SemaphoreType.DMA((2 * planes,))],
+        compiler_params=params,
+    )(index, mine, late_gain, x_in, c_in)
     pieces[planes // 2], _ = lax.optimization_barrier((pieces[planes // 2], blocks[3]))
     own = [marked] + [pieces[k] for k in range(1, planes)]
     other = [to_sibling(piece) for piece in own]
@@ -429,11 +446,11 @@
         [(grads[1:], F32)] + [(grads[1:], BF16)] * (planes - 1),
         index, keep, to_sibling(send), scalars=1,
     )
-    parts = far_first(merged, planes, along_z)[1:]
+    parts = [round_z(merged[k], k) for k in range(1, planes)]
     grad_qkv, grad_out = call(
         functools.partial(last_kernel, qkv_rows),
         [((qkv_rows, width), F32), ((heads, width), F32)],
-        merged[0], *parts[::-1],
+        merged[0], *parts,
     )
     return (grad_qkv.T[None], grad_out[None])
 

time: 62.1 us -> 60.9 us (0.981)
  waiting for transfers between devices: 28.8 us -> 24.7 us
  Pallas kernels: 9.67 us -> 11 us
  starting transfers between devices: 22.5 us -> 23.6 us
    ppermute x6 -> x3, waiting for transfers between devices: 17.7 us -> 5.81 us  [along_z(): return lax.ppermute(value, 'dp', route)]
    ppermute x0 -> x3, waiting for transfers between devices: none -> 7.75 us  [round_z(): return lax.ppermute(value, 'dp', route)]
    ppermute x0 -> x3, starting transfers between devices: none -> 5.63 us  [round_z(): return lax.ppermute(value, 'dp', route)]
    ppermute x6 -> x3, starting transfers between devices: 9.27 us -> 4.73 us  [along_z(): return lax.ppermute(value, 'dp', route)]
    pallas_call x0 -> x1, Pallas kernels: none -> 1.49 us  [planar(): pl.pallas_call(functools.partial(mark_kernel, planes), out_shape=[jax.Sha...]
    pallas_call x6 -> x5, Pallas kernels: 7.44 us -> 7.43 us  [call(): pl.pallas_call(kernel, out_shape=[jax.ShapeDtypeStruct(shape, dtype) for...]
  transfers between devices with their start and end apart: 20 -> 20, of which waited for: 12 -> 12; matrix products, arithmetic and copies ran while one was open for 0% -> 0% of each run, Pallas kernels for 0% -> 2%
where the time goes in v12:
time: 60.9 us; the launch traced here: 60.2 us
  waiting for transfers between devices  24.7 us (41%)
  starting transfers between devices  23.6 us (39%)
  Pallas kernels  11 us (18%)
  between operations  0.74 us (1%)
    ppermute x9, starting transfers between devices, along_plane(): return lax.ppermute(value, 'dp', route)  12.1 us
    ppermute x9, waiting for transfers between devices, along_plane(): return lax.ppermute(value, 'dp', route)  8.2 us
    ppermute x3, waiting for transfers between devices, round_z(): return lax.ppermute(value, 'dp', route)  7.75 us
    pallas_call x5, Pallas kernels, call(): pl.pallas_call(kernel, out_shape=[jax.ShapeDtypeStruct(shape, dtype) for...  7.43 us
    ppermute x3, waiting for transfers between devices, along_z(): return lax.ppermute(value, 'dp', route)  5.81 us
    ppermute x3, starting transfers between devices, round_z(): return lax.ppermute(value, 'dp', route)  5.63 us
    ppermute x3, starting transfers between devices, along_z(): return lax.ppermute(value, 'dp', route)  4.73 us
    ppermute x5, waiting for transfers between devices, to_sibling(): return lax.ppermute(value, 'section', [(0, 1), (1, 0)])  2.92 us
  transfers between devices with their start and end apart: 20, of which 12 were waited for; matrix products, arithmetic and copies ran while one was open for 0% of the time, Pallas kernels for 2%

profile of v12, /device:TPU:0, one launch (start us, length us, event | category | flops | bytes accessed | tf_op | source)
XLA Modules:
  0.0 60.2 jit_solution(16267141016003920100)
XLA Ops:
  0.6 0.1 pad_add_fusion.index
  0.7 0.0 copy-start.1
  0.7 2.1 %shard_map.77 = (bf16[256,256]{1,0:T(8,128)(2,1)S(1)}, bf16[2,64,1024]{2,1,0:T(8,128)(2,1)S(1)}, bf16[2,64,1024]{2,1,0:T(8,128)(2,1)S(1)}, bf16[2,64,1024]{2,1,0:T(8,128)(2,1)S(1)}) custom-call(s32[3]{0:T(128)S(1)} %pad_add_fusion.index, bf16[192,256]{1,0:T(8,128)(2,1)} %bitcast.11, bf16[64,256]{1,0:T(8,128)(2,1)} %bitcast.12, bf16[2,64,4096]{2,1,0:T(8,128)(2,1)} %x_ref.3, ...), custom_call_target="tpu_custom_call" | custom-call | tf_op jit(solution)/shard_map/pallas_call | solution.py:396
  2.8 4.0 %collective-permute-start = (bf16[2,64,1024]{2,1,0:T(8,128)(2,1)S(1)}, bf16[2,64,1024]{2,1,0:T(8,128)(2,1)S(1)}, u32[]{:S(2)}, u32[]{:S(2)}) collective-permute-start(bf16[2,64,1024]{2,1,0:T(8,128)(2,1)S(1)} %get-tuple-element.28), channel_id=1, source_target_pairs={{0,3},{1,2},{2,1},{3,0},{4,7},{5,6},{6,5},{7,4},{8,11},{9,10},{10,... | collective-permute-start | bytes 786440 | tf_op jit(solution)/shard_map/ppermute | solution.py:383
  6.8 2.6 %collective-permute-start.4 = (bf16[256,256]{1,0:T(8,128)(2,1)S(1)}, bf16[256,256]{1,0:T(8,128)(2,1)S(1)}, u32[]{:S(2)}, u32[]{:S(2)}) collective-permute-start(bf16[256,256]{1,0:T(8,128)(2,1)S(1)} %get-tuple-element.29.pack_ref), channel_id=1, source_target_pairs={{0,8},{1,9},{2,10},{3,11},{4,12},{5,13},{6,14},{7,15},{8,0},{9,1},... | collective-permute-start | bytes 393224 | tf_op jit(solution)/shard_map/ppermute | solution.py:372
  9.3 1.6 %collective-permute-start.3 = (bf16[256,256]{1,0:T(8,128)(2,1)S(1)}, bf16[256,256]{1,0:T(8,128)(2,1)S(1)}, u32[]{:S(2)}, u32[]{:S(2)}) collective-permute-start(bf16[256,256]{1,0:T(8,128)(2,1)S(1)} %get-tuple-element.29.pack_ref), channel_id=1, source_target_pairs={{0,4},{1,5},{2,6},{3,7},{4,0},{5,1},{6,2},{7,3},{8,12},{9,13},{10,... | collective-permute-start | bytes 393224 | tf_op jit(solution)/shard_map/ppermute | solution.py:372
  10.9 0.5 collective-permute-start.1
  11.4 0.5 collective-permute-start.2
  12.0 3.6 %collective-permute-done.4.refs_6_ = bf16[256,256]{1,0:T(8,128)(2,1)S(1)} collective-permute-done((bf16[256,256]{1,0:T(8,128)(2,1)S(1)}, bf16[256,256]{1,0:T(8,128)(2,1)S(1)}, u32[]{:S(2)}, u32[]{:S(2)}) %collective-permute-start.4) | collective-permute-done | bytes 131104 | tf_op jit(solution)/shard_map/ppermute | solution.py:372
  15.5 0.6 collective-permute-start.5
  16.1 0.0 collective-permute-done.3.refs_5_
  16.1 0.0 collective-permute-start.7
  16.1 0.0 copy-done.1
  16.1 0.1 reduce
  16.2 0.0 collective-permute-done.refs_1_
  16.2 1.5 %shard_map.78 = (bf16[272,256]{1,0:T(8,128)(2,1)S(1)}, bf16[2,64,1024]{2,1,0:T(8,128)(2,1)S(1)}) custom-call(s32[3]{0:T(128)S(1)} %pad_add_fusion.index, bf16[256,256]{1,0:T(8,128)(2,1)S(1)} %get-tuple-element.29.pack_ref, bf16[16,256]{1,0:T(8,128)(2,1)S(1)} %reshape_squeeze.3.gain_ref, bf16[2,64,4096]{2,1,0:T(8,128)(2,1)} %x_ref.3, bf16[2,64,4096]{2,1,0:T(8,128)(2,1)} %c_ref.3), custom_call_target="tpu_custom_call" | custom-call | tf_op jit(solution)/shard_map/pallas_call | solution.py:411
  17.7 0.6 collective-permute-start.6
  18.2 2.2 %collective-permute-done.5.refs_7_ = bf16[256,256]{1,0:T(8,128)(2,1)S(1)} collective-permute-done((bf16[256,256]{1,0:T(8,128)(2,1)S(1)}, bf16[256,256]{1,0:T(8,128)(2,1)S(1)}, u32[]{:S(2)}, u32[]{:S(2)}) %collective-permute-start.5) | collective-permute-done | bytes 131104 | tf_op jit(solution)/shard_map/ppermute | solution.py:372
  20.5 0.0 collective-permute-start.9
  20.5 0.0 collective-permute-done.7.refs_9_
  20.5 0.5 collective-permute-start.8
  21.0 0.0 collective-permute-done.1.refs_2_
  21.0 0.0 collective-permute-done.2.refs_3_
  21.0 0.8 %collective-permute-done.9.refs_11_ = bf16[256,256]{1,0:T(8,128)(2,1)S(1)} collective-permute-done((bf16[256,256]{1,0:T(8,128)(2,1)S(1)}, bf16[256,256]{1,0:T(8,128)(2,1)S(1)}, u32[]{:S(2)}, u32[]{:S(2)}) %collective-permute-start.9) | collective-permute-done | bytes 131104 | tf_op jit(solution)/shard_map/ppermute | solution.py:379
  21.8 0.2 collective-permute-done.8.refs_10_
  22.0 0.0 collective-permute-done.6.refs_8_
  22.0 1.6 %shard_map.79 = (bf16[4,64,1024]{2,1,0:T(8,128)(2,1)S(1)}, bf16[4,64,1024]{2,1,0:T(8,128)(2,1)S(1)}, bf16[4,512,256]{2,1,0:T(8,128)(2,1)S(1)}, f32[4,8,256]{2,1,...) custom-call(s32[3]{0:T(128)S(1)} %pad_add_fusion.index, ...), custom_call_target="tpu_custom_call" | custom-call | tf_op jit(solution)/shard_map/pallas_call | solution.py:349
  23.6 0.5 collective-permute-start.10
  24.1 1.6 %collective-permute-start.11 = (bf16[64,896]{1,0:T(8,128)(2,1)S(1)}, bf16[64,896]{1,0:T(8,128)(2,1)S(1)}, u32[]{:S(2)}, u32[]{:S(2)}) collective-permute-start(bf16[64,896]{1,0:T(8,128)(2,1)S(1)} %get-tuple-element.37), channel_id=1, source_target_pairs={{0,2},{1,3},{2,0},{3,1},{4,6},{5,7},{6,4},{7,5},{8,10},{9,11},{10,... | collective-permute-start | bytes 344072 | tf_op jit(solution)/shard_map/ppermute | solution.py:383
  25.7 0.0 copy-start
  25.7 1.5 %collective-permute-start.12 = (bf16[64,896]{1,0:T(8,128)(2,1)S(1)}, bf16[64,896]{1,0:T(8,128)(2,1)S(1)}, u32[]{:S(2)}, u32[]{:S(2)}) collective-permute-start(bf16[64,896]{1,0:T(8,128)(2,1)S(1)} %get-tuple-element.38), channel_id=1, source_target_pairs={{0,1},{1,0},{2,3},{3,2},{4,5},{5,4},{6,7},{7,6},{8,9},{9,8},{10,11... | collective-permute-start | bytes 344072 | tf_op jit(solution)/shard_map/ppermute | solution.py:383
  27.2 3.4 %collective-permute-done.10.refs_0_ = bf16[64,896]{1,0:T(8,128)(2,1)S(1)} collective-permute-done((bf16[64,896]{1,0:T(8,128)(2,1)S(1)}, bf16[64,896]{1,0:T(8,128)(2,1)S(1)}, u32[]{:S(2)}, u32[]{:S(2)}) %collective-permute-start.10) | collective-permute-done | bytes 114720 | tf_op jit(solution)/shard_map/ppermute | solution.py:383
  30.6 1.1 %collective-permute-done.11.refs_1_ = bf16[64,896]{1,0:T(8,128)(2,1)S(1)} collective-permute-done((bf16[64,896]{1,0:T(8,128)(2,1)S(1)}, bf16[64,896]{1,0:T(8,128)(2,1)S(1)}, u32[]{:S(2)}, u32[]{:S(2)}) %collective-permute-start.11) | collective-permute-done | bytes 114720 | tf_op jit(solution)/shard_map/ppermute | solution.py:383
  31.7 0.0 collective-permute-done.12.refs_2_
  31.7 0.0 copy-done
  31.7 2.9 %shard_map.80.refs_0_ = bf16[64,640]{1,0:T(8,128)(2,1)S(1)} custom-call(s32[3]{0:T(128)S(1)} %pad_add_fusion.index, s32[2,1,2]{2,1,0:T(1,128)S(1)} %copy-done, bf16[64,896]{1,0:T(8,128)(2,1)S(1)} %collective-permute-done.10.refs_0_, bf16[64,896]{1,0:T(8,128)(2,1)S(1)} %collective-permute-done.11.refs_1_, ...), custom_call_target="tpu_custom_call" | custom-call | tf_op jit(solution)/shard_map/pallas_call | solution.py:349
  34.6 1.4 %collective-permute-start.15 = (bf16[64,640]{1,0:T(8,128)(2,1)S(1)}, bf16[64,640]{1,0:T(8,128)(2,1)S(1)}, u32[]{:S(2)}, u32[]{:S(2)}) collective-permute-start(bf16[64,640]{1,0:T(8,128)(2,1)S(1)} %shard_map.80.refs_0_), channel_id=1, source_target_pairs={{0,3},{1,2},{2,1},{3,0},{4,7},{5,6},{6,5},{7,4},{8,11},{9,10},{10,... | collective-permute-start | bytes 245768 | tf_op jit(solution)/shard_map/ppermute | solution.py:383
  35.9 1.5 %collective-permute-start.14 = (bf16[64,640]{1,0:T(8,128)(2,1)S(1)}, bf16[64,640]{1,0:T(8,128)(2,1)S(1)}, u32[]{:S(2)}, u32[]{:S(2)}) collective-permute-start(bf16[64,640]{1,0:T(8,128)(2,1)S(1)} %shard_map.80.refs_0_), channel_id=1, source_target_pairs={{0,2},{1,3},{2,0},{3,1},{4,6},{5,7},{6,4},{7,5},{8,10},{9,11},{10,... | collective-permute-start | bytes 245768 | tf_op jit(solution)/shard_map/ppermute | solution.py:383
  37.4 0.7 %collective-permute-start.13 = (bf16[64,640]{1,0:T(8,128)(2,1)S(1)}, bf16[64,640]{1,0:T(8,128)(2,1)S(1)}, u32[]{:S(2)}, u32[]{:S(2)}) collective-permute-start(bf16[64,640]{1,0:T(8,128)(2,1)S(1)} %shard_map.80.refs_0_), channel_id=1, source_target_pairs={{0,1},{1,0},{2,3},{3,2},{4,5},{5,4},{6,7},{7,6},{8,9},{9,8},{10,11... | collective-permute-start | bytes 245768 | tf_op jit(solution)/shard_map/ppermute | solution.py:383
  38.1 2.5 %collective-permute-done.15.refs_3_ = bf16[64,640]{1,0:T(8,128)(2,1)S(1)} collective-permute-done((bf16[64,640]{1,0:T(8,128)(2,1)S(1)}, bf16[64,640]{1,0:T(8,128)(2,1)S(1)}, u32[]{:S(2)}, u32[]{:S(2)}) %collective-permute-start.15) | collective-permute-done | bytes 81952 | tf_op jit(solution)/shard_map/ppermute | solution.py:383
  40.6 0.3 collective-permute-done.14.refs_2_
  41.0 0.9 %collective-permute-done.13.refs_1_ = bf16[64,640]{1,0:T(8,128)(2,1)S(1)} collective-permute-done((bf16[64,640]{1,0:T(8,128)(2,1)S(1)}, bf16[64,640]{1,0:T(8,128)(2,1)S(1)}, u32[]{:S(2)}, u32[]{:S(2)}) %collective-permute-start.13) | collective-permute-done | bytes 81952 | tf_op jit(solution)/shard_map/ppermute | solution.py:383
  41.8 1.6 %shard_map.81 = (f32[4,256,256]{2,1,0:T(8,128)S(1)}, bf16[4,256,256]{2,1,0:T(8,128)(2,1)S(1)}) custom-call(s32[3]{0:T(128)S(1)} %pad_add_fusion.index, bf16[64,640]{1,0:T(8,128)(2,1)S(1)} %shard_map.80.refs_0_, bf16[64,640]{1,0:T(8,128)(2,1)S(1)} %collective-permute-done.13.refs_1_, bf16[64,640]{1,0:T(8,128)(2,1)S(1)} %collective-permute-done.14.refs_2_, ...), custom_call_target="tpu_custom_call" | custom-call | tf_op jit(solution)/shard_map/pallas_call | solution.py:349
  43.4 0.1 collective-permute-start.16
  43.5 1.9 %collective-permute-done.16.come_ref = bf16[4,256,256]{2,1,0:T(8,128)(2,1)S(1)} collective-permute-done((bf16[4,256,256]{2,1,0:T(8,128)(2,1)S(1)}, bf16[4,256,256]{2,1,0:T(8,128)(2,1)S(1)}, u32[]{:S(2)}, u32[]{:S(2)}) %collective-permute-start.16) | collective-permute-done | bytes 524320 | tf_op jit(solution)/shard_map/ppermute | solution.py:379
  45.4 0.6 %shard_map.82 = (f32[256,256]{1,0:T(8,128)S(1)}, bf16[256,256]{1,0:T(8,128)(2,1)S(1)}, bf16[256,256]{1,0:T(8,128)(2,1)S(1)}, bf16[256,256]{1,0:T(8,128)(2,1)S(1)}) custom-call(s32[3]{0:T(128)S(1)} %pad_add_fusion.index, f32[4,256,256]{2,1,0:T(8,128)S(1)} %get-tuple-element.44.keep_ref, bf16[4,256,256]{2,1,0:T(8,128)(2,1)S(1)} %collective-permute-done.16.come_ref), custom_call_target="tpu_custom_call" | custom-call | tf_op jit(solution)/shard_map/pallas_call | solution.py:349
  46.0 1.1 %collective-permute-start.17 = (bf16[256,256]{1,0:T(8,128)(2,1)S(1)}, bf16[256,256]{1,0:T(8,128)(2,1)S(1)}, u32[]{:S(2)}, u32[]{:S(2)}) collective-permute-start(bf16[256,256]{1,0:T(8,128)(2,1)S(1)} %get-tuple-element.47), channel_id=1, source_target_pairs={{0,4},{1,5},{2,6},{3,7},{4,8},{5,9},{6,10},{7,11},{8,12},{9,13},{1... | collective-permute-start | bytes 393224 | tf_op jit(solution)/shard_map/ppermute | solution.py:376
  47.1 3.4 %collective-permute-start.18 = (bf16[256,256]{1,0:T(8,128)(2,1)S(1)}, bf16[256,256]{1,0:T(8,128)(2,1)S(1)}, u32[]{:S(2)}, u32[]{:S(2)}) collective-permute-start(bf16[256,256]{1,0:T(8,128)(2,1)S(1)} %get-tuple-element.48), channel_id=1, source_target_pairs={{0,8},{1,9},{2,10},{3,11},{4,12},{5,13},{6,14},{7,15},{8,0},{9,1},... | collective-permute-start | bytes 393224 | tf_op jit(solution)/shard_map/ppermute | solution.py:376
  50.5 1.2 %collective-permute-start.19 = (bf16[256,256]{1,0:T(8,128)(2,1)S(1)}, bf16[256,256]{1,0:T(8,128)(2,1)S(1)}, u32[]{:S(2)}, u32[]{:S(2)}) collective-permute-start(bf16[256,256]{1,0:T(8,128)(2,1)S(1)} %get-tuple-element.49), channel_id=1, source_target_pairs={{0,12},{1,13},{2,14},{3,15},{4,0},{5,1},{6,2},{7,3},{8,4},{9,5},{1... | collective-permute-start | bytes 393224 | tf_op jit(solution)/shard_map/ppermute | solution.py:376
  51.7 2.6 %collective-permute-done.17.refs_0_ = bf16[256,256]{1,0:T(8,128)(2,1)S(1)} collective-permute-done((bf16[256,256]{1,0:T(8,128)(2,1)S(1)}, bf16[256,256]{1,0:T(8,128)(2,1)S(1)}, u32[]{:S(2)}, u32[]{:S(2)}) %collective-permute-start.17) | collective-permute-done | bytes 131104 | tf_op jit(solution)/shard_map/ppermute | solution.py:376
  54.3 5.1 %collective-permute-done.18.refs_1_ = bf16[256,256]{1,0:T(8,128)(2,1)S(1)} collective-permute-done((bf16[256,256]{1,0:T(8,128)(2,1)S(1)}, bf16[256,256]{1,0:T(8,128)(2,1)S(1)}, u32[]{:S(2)}, u32[]{:S(2)}) %collective-permute-start.18) | collective-permute-done | bytes 131104 | tf_op jit(solution)/shard_map/ppermute | solution.py:376
  59.4 0.0 collective-permute-done.19.refs_2_
  59.4 0.7 %shard_map.83 = (f32[192,256]{1,0:T(8,128)}, f32[64,256]{1,0:T(8,128)}) custom-call(f32[256,256]{1,0:T(8,128)S(1)} %get-tuple-element.46.keep_ref, bf16[256,256]{1,0:T(8,128)(2,1)S(1)} %collective-permute-done.17.refs_0_, bf16[256,256]{1,0:T(8,128)(2,1)S(1)} %collective-permute-done.18.refs_1_, bf16[256,256]{1,0:T(8,128)(2,1)S(1)} %collective-permute-done.19.refs_2_), custom_call_target="tpu_custom_call" | custom-call | tf_op jit(solution)/shard_map/pallas_call | solution.py:349
  (1 shorter events, 0.0 us)
Async XLA Ops:
  0.7 15.4 %copy-start.1 = (bf16[1,4096]{1,0:T(2,128)(2,1)S(1)}, bf16[1,4096]{1,0:T(2,128)(2,1)}, u32[]{:S(2)}) copy-start(bf16[1,4096]{1,0:T(2,128)(2,1)} %param.9) | copy-start | bytes 24580
  2.8 13.4 %collective-permute-start = (bf16[2,64,1024]{2,1,0:T(8,128)(2,1)S(1)}, bf16[2,64,1024]{2,1,0:T(8,128)(2,1)S(1)}, u32[]{:S(2)}, u32[]{:S(2)}) collective-permute-start(bf16[2,64,1024]{2,1,0:T(8,128)(2,1)S(1)} %get-tuple-element.28), channel_id=1, source_target_pairs={{0,3},{1,2},{2,1},{3,0},{4,7},{5,6},{6,5},{7,4},{8,11},{9,10},{10,... | collective-permute-start | bytes 786440 | tf_op jit(solution)/shard_map/ppermute | solution.py:383
  6.8 8.8 %collective-permute-start.4 = (bf16[256,256]{1,0:T(8,128)(2,1)S(1)}, bf16[256,256]{1,0:T(8,128)(2,1)S(1)}, u32[]{:S(2)}, u32[]{:S(2)}) collective-permute-start(bf16[256,256]{1,0:T(8,128)(2,1)S(1)} %get-tuple-element.29.pack_ref), channel_id=1, source_target_pairs={{0,8},{1,9},{2,10},{3,11},{4,12},{5,13},{6,14},{7,15},{8,0},{9,1},... | collective-permute-start | bytes 393224 | tf_op jit(solution)/shard_map/ppermute | solution.py:372
  9.3 6.8 %collective-permute-start.3 = (bf16[256,256]{1,0:T(8,128)(2,1)S(1)}, bf16[256,256]{1,0:T(8,128)(2,1)S(1)}, u32[]{:S(2)}, u32[]{:S(2)}) collective-permute-start(bf16[256,256]{1,0:T(8,128)(2,1)S(1)} %get-tuple-element.29.pack_ref), channel_id=1, source_target_pairs={{0,4},{1,5},{2,6},{3,7},{4,0},{5,1},{6,2},{7,3},{8,12},{9,13},{10,... | collective-permute-start | bytes 393224 | tf_op jit(solution)/shard_map/ppermute | solution.py:372
  10.9 10.1 %collective-permute-start.1 = (bf16[2,64,1024]{2,1,0:T(8,128)(2,1)S(1)}, bf16[2,64,1024]{2,1,0:T(8,128)(2,1)S(1)}, u32[]{:S(2)}, u32[]{:S(2)}) collective-permute-start(bf16[2,64,1024]{2,1,0:T(8,128)(2,1)S(1)} %get-tuple-element.32), channel_id=1, source_target_pairs={{0,2},{1,3},{2,0},{3,1},{4,6},{5,7},{6,4},{7,5},{8,10},{9,11},{10,... | collective-permute-start | bytes 786440 | tf_op jit(solution)/shard_map/ppermute | solution.py:383
  11.4 9.6 %collective-permute-start.2 = (bf16[2,64,1024]{2,1,0:T(8,128)(2,1)S(1)}, bf16[2,64,1024]{2,1,0:T(8,128)(2,1)S(1)}, u32[]{:S(2)}, u32[]{:S(2)}) collective-permute-start(bf16[2,64,1024]{2,1,0:T(8,128)(2,1)S(1)} %get-tuple-element.33), channel_id=1, source_target_pairs={{0,1},{1,0},{2,3},{3,2},{4,5},{5,4},{6,7},{7,6},{8,9},{9,8},{10,11... | collective-permute-start | bytes 786440 | tf_op jit(solution)/shard_map/ppermute | solution.py:383
  15.5 5.0 %collective-permute-start.5 = (bf16[256,256]{1,0:T(8,128)(2,1)S(1)}, bf16[256,256]{1,0:T(8,128)(2,1)S(1)}, u32[]{:S(2)}, u32[]{:S(2)}) collective-permute-start(bf16[256,256]{1,0:T(8,128)(2,1)S(1)} %collective-permute-done.4.refs_6_), channel_id=1, source_target_pairs={{0,4},{1,5},{2,6},{3,7},{4,0},{5,1},{6,2},{7,3},{8,12},{9,13},{10,... | collective-permute-start | bytes 393224 | tf_op jit(solution)/shard_map/ppermute | solution.py:372
  16.1 4.4 %collective-permute-start.7 = (bf16[256,256]{1,0:T(8,128)(2,1)S(1)}, bf16[256,256]{1,0:T(8,128)(2,1)S(1)}, u32[]{:S(2)}, u32[]{:S(2)}) collective-permute-start(bf16[256,256]{1,0:T(8,128)(2,1)S(1)} %collective-permute-done.3.refs_5_), channel_id=1, source_target_pairs={{0,16},{16,0},{1,17},{17,1},{2,18},{18,2},{3,19},{19,3},{4,20},{20... | collective-permute-start | bytes 393224 | tf_op jit(solution)/shard_map/ppermute | solution.py:379
  17.7 4.3 %collective-permute-start.6 = (bf16[272,256]{1,0:T(8,128)(2,1)S(1)}, bf16[272,256]{1,0:T(8,128)(2,1)S(1)}, u32[]{:S(2)}, u32[]{:S(2)}) collective-permute-start(bf16[272,256]{1,0:T(8,128)(2,1)S(1)} %get-tuple-element.34.refs_4_), channel_id=1, source_target_pairs={{0,16},{16,0},{1,17},{17,1},{2,18},{18,2},{3,19},{19,3},{4,20},{20... | collective-permute-start | bytes 417800 | tf_op jit(solution)/shard_map/ppermute | solution.py:379
  20.5 1.3 %collective-permute-start.9 = (bf16[256,256]{1,0:T(8,128)(2,1)S(1)}, bf16[256,256]{1,0:T(8,128)(2,1)S(1)}, u32[]{:S(2)}, u32[]{:S(2)}) collective-permute-start(bf16[256,256]{1,0:T(8,128)(2,1)S(1)} %collective-permute-done.5.refs_7_), channel_id=1, source_target_pairs={{0,16},{16,0},{1,17},{17,1},{2,18},{18,2},{3,19},{19,3},{4,20},{20... | collective-permute-start | bytes 393224 | tf_op jit(solution)/shard_map/ppermute | solution.py:379
  20.5 1.5 %collective-permute-start.8 = (bf16[256,256]{1,0:T(8,128)(2,1)S(1)}, bf16[256,256]{1,0:T(8,128)(2,1)S(1)}, u32[]{:S(2)}, u32[]{:S(2)}) collective-permute-start(bf16[256,256]{1,0:T(8,128)(2,1)S(1)} %collective-permute-done.4.refs_6_), channel_id=1, source_target_pairs={{0,16},{16,0},{1,17},{17,1},{2,18},{18,2},{3,19},{19,3},{4,20},{20... | collective-permute-start | bytes 393224 | tf_op jit(solution)/shard_map/ppermute | solution.py:379
  23.6 7.0 %collective-permute-start.10 = (bf16[64,896]{1,0:T(8,128)(2,1)S(1)}, bf16[64,896]{1,0:T(8,128)(2,1)S(1)}, u32[]{:S(2)}, u32[]{:S(2)}) collective-permute-start(bf16[64,896]{1,0:T(8,128)(2,1)S(1)} %get-tuple-element.36), channel_id=1, source_target_pairs={{0,3},{1,2},{2,1},{3,0},{4,7},{5,6},{6,5},{7,4},{8,11},{9,10},{10,... | collective-permute-start | bytes 344072 | tf_op jit(solution)/shard_map/ppermute | solution.py:383
  24.1 7.6 %collective-permute-start.11 = (bf16[64,896]{1,0:T(8,128)(2,1)S(1)}, bf16[64,896]{1,0:T(8,128)(2,1)S(1)}, u32[]{:S(2)}, u32[]{:S(2)}) collective-permute-start(bf16[64,896]{1,0:T(8,128)(2,1)S(1)} %get-tuple-element.37), channel_id=1, source_target_pairs={{0,2},{1,3},{2,0},{3,1},{4,6},{5,7},{6,4},{7,5},{8,10},{9,11},{10,... | collective-permute-start | bytes 344072 | tf_op jit(solution)/shard_map/ppermute | solution.py:383
  25.7 6.0 %copy-start = (s32[2,1,2]{2,1,0:T(1,128)S(1)}, s32[2,1,2]{2,1,0:T(1,128)}, u32[]{:S(2)}) copy-start(s32[2,1,2]{2,1,0:T(1,128)} %docs.1) | copy-start | bytes 52
  25.7 6.0 %collective-permute-start.12 = (bf16[64,896]{1,0:T(8,128)(2,1)S(1)}, bf16[64,896]{1,0:T(8,128)(2,1)S(1)}, u32[]{:S(2)}, u32[]{:S(2)}) collective-permute-start(bf16[64,896]{1,0:T(8,128)(2,1)S(1)} %get-tuple-element.38), channel_id=1, source_target_pairs={{0,1},{1,0},{2,3},{3,2},{4,5},{5,4},{6,7},{7,6},{8,9},{9,8},{10,11... | collective-permute-start | bytes 344072 | tf_op jit(solution)/shard_map/ppermute | solution.py:383
  34.6 6.0 %collective-permute-start.15 = (bf16[64,640]{1,0:T(8,128)(2,1)S(1)}, bf16[64,640]{1,0:T(8,128)(2,1)S(1)}, u32[]{:S(2)}, u32[]{:S(2)}) collective-permute-start(bf16[64,640]{1,0:T(8,128)(2,1)S(1)} %shard_map.80.refs_0_), channel_id=1, source_target_pairs={{0,3},{1,2},{2,1},{3,0},{4,7},{5,6},{6,5},{7,4},{8,11},{9,10},{10,... | collective-permute-start | bytes 245768 | tf_op jit(solution)/shard_map/ppermute | solution.py:383
  35.9 5.0 %collective-permute-start.14 = (bf16[64,640]{1,0:T(8,128)(2,1)S(1)}, bf16[64,640]{1,0:T(8,128)(2,1)S(1)}, u32[]{:S(2)}, u32[]{:S(2)}) collective-permute-start(bf16[64,640]{1,0:T(8,128)(2,1)S(1)} %shard_map.80.refs_0_), channel_id=1, source_target_pairs={{0,2},{1,3},{2,0},{3,1},{4,6},{5,7},{6,4},{7,5},{8,10},{9,11},{10,... | collective-permute-start | bytes 245768 | tf_op jit(solution)/shard_map/ppermute | solution.py:383
  37.4 4.4 %collective-permute-start.13 = (bf16[64,640]{1,0:T(8,128)(2,1)S(1)}, bf16[64,640]{1,0:T(8,128)(2,1)S(1)}, u32[]{:S(2)}, u32[]{:S(2)}) collective-permute-start(bf16[64,640]{1,0:T(8,128)(2,1)S(1)} %shard_map.80.refs_0_), channel_id=1, source_target_pairs={{0,1},{1,0},{2,3},{3,2},{4,5},{5,4},{6,7},{7,6},{8,9},{9,8},{10,11... | collective-permute-start | bytes 245768 | tf_op jit(solution)/shard_map/ppermute | solution.py:383
  43.4 2.0 %collective-permute-start.16 = (bf16[4,256,256]{2,1,0:T(8,128)(2,1)S(1)}, bf16[4,256,256]{2,1,0:T(8,128)(2,1)S(1)}, u32[]{:S(2)}, u32[]{:S(2)}) collective-permute-start(bf16[4,256,256]{2,1,0:T(8,128)(2,1)S(1)} %get-tuple-element.45), channel_id=1, source_target_pairs={{0,16},{16,0},{1,17},{17,1},{2,18},{18,2},{3,19},{19,3},{4,20},{20... | collective-permute-start | bytes 1572872 | tf_op jit(solution)/shard_map/ppermute | solution.py:379
  46.0 8.3 %collective-permute-start.17 = (bf16[256,256]{1,0:T(8,128)(2,1)S(1)}, bf16[256,256]{1,0:T(8,128)(2,1)S(1)}, u32[]{:S(2)}, u32[]{:S(2)}) collective-permute-start(bf16[256,256]{1,0:T(8,128)(2,1)S(1)} %get-tuple-element.47), channel_id=1, source_target_pairs={{0,4},{1,5},{2,6},{3,7},{4,8},{5,9},{6,10},{7,11},{8,12},{9,13},{1... | collective-permute-start | bytes 393224 | tf_op jit(solution)/shard_map/ppermute | solution.py:376
  47.1 12.3 %collective-permute-start.18 = (bf16[256,256]{1,0:T(8,128)(2,1)S(1)}, bf16[256,256]{1,0:T(8,128)(2,1)S(1)}, u32[]{:S(2)}, u32[]{:S(2)}) collective-permute-start(bf16[256,256]{1,0:T(8,128)(2,1)S(1)} %get-tuple-element.48), channel_id=1, source_target_pairs={{0,8},{1,9},{2,10},{3,11},{4,12},{5,13},{6,14},{7,15},{8,0},{9,1},... | collective-permute-start | bytes 393224 | tf_op jit(solution)/shard_map/ppermute | solution.py:376
  50.5 8.9 %collective-permute-start.19 = (bf16[256,256]{1,0:T(8,128)(2,1)S(1)}, bf16[256,256]{1,0:T(8,128)(2,1)S(1)}, u32[]{:S(2)}, u32[]{:S(2)}) collective-permute-start(bf16[256,256]{1,0:T(8,128)(2,1)S(1)} %get-tuple-element.49), channel_id=1, source_target_pairs={{0,12},{1,13},{2,14},{3,15},{4,0},{5,1},{6,2},{7,3},{8,4},{9,5},{1... | collective-permute-start | bytes 393224 | tf_op jit(solution)/shard_map/ppermute | solution.py:376

commit v13 on v12

--- a/solution.py
+++ b/solution.py
@@ -151,13 +151,21 @@
         copy.wait()
 
 
-def blocks_kernel(planes, index, qkv_ref, wout_ref, x_ref, c_ref, pack_ref, *refs):
-    out_refs, pack_sems, sems = refs[:-2], refs[-2], refs[-1]
+def first_kernel(planes, index, qkv_ref, wout_ref, x_ref, c_ref, pack_ref, far_ref, pack_sems, sems):
     qkv_rows = qkv_ref.shape[0]
     copies = [
         pltpu.make_async_copy(qkv_ref, pack_ref.at[:qkv_rows], pack_sems.at[0]),
         pltpu.make_async_copy(wout_ref, pack_ref.at[qkv_rows:], pack_sems.at[1]),
-    ]
+    ] + block_copies(planes, index, PLANE - 1, (x_ref, c_ref), far_ref, sems)
+    for copy in copies:
+        copy.start()
+    for copy in copies:
+        copy.wait()
+
+
+def blocks_kernel(planes, index, x_ref, c_ref, *refs):
+    out_refs, sems = refs[:-1], refs[-1]
+    copies = []
     for k, out_ref in enumerate(out_refs, 1):
         copies += block_copies(planes, index, k, (x_ref, c_ref), out_ref, sems.at[k - 1])
     for copy in copies:
@@ -321,11 +329,14 @@
 
 
 def merge_kernel(index, keep_ref, come_ref, *out_refs):
-    place, count = index[1], len(out_refs)
+    place = index[1]
     out_refs[0][...] = keep_ref[place] + come_ref[place].astype(F32)
-    for k in range(1, count):
-        at = (place + k) & (count - 1)
-        out_refs[k][...] = (keep_ref[at] + come_ref[at].astype(F32)).astype(BF16)
+    for k in range(1, len(out_refs)):
+        out_refs[k][...] = (keep_ref[place ^ k] + come_ref[place ^ k].astype(F32)).astype(BF16)
+
+
+def add_kernel(a_ref, b_ref, out_ref):
+    out_ref[...] = (a_ref[...].astype(F32) + b_ref[...].astype(F32)).astype(BF16)
 
 
 def last_kernel(qkv_rows, keep_ref, *refs):
@@ -371,10 +382,6 @@
         route = [(a * PLANE + b, (a ^ k) * PLANE + b) for a in range(planes) for b in range(PLANE)]
         return lax.ppermute(value, "dp", route)
 
-    def round_z(value, k):
-        route = [(a * PLANE + b, (a + k) % planes * PLANE + b) for a in range(planes) for b in range(PLANE)]
-        return lax.ppermute(value, "dp", route)
-
     def to_sibling(value):
         return lax.ppermute(value, "section", [(0, 1), (1, 0)])
 
@@ -393,14 +400,23 @@
         for value in (w_qkv[0].T, w_out[0], inputs, cotangent)
     ]
     one_block = jax.ShapeDtypeStruct((2, block, cols), BF16)
-    pack, *blocks = pl.pallas_call(
-        functools.partial(blocks_kernel, planes),
-        out_shape=[jax.ShapeDtypeStruct((qkv_rows + heads, width), BF16)] + [one_block] * (PLANE - 1),
+    pack, far_block = pl.pallas_call(
+        functools.partial(first_kernel, planes),
+        out_shape=[jax.ShapeDtypeStruct((qkv_rows + heads, width), BF16), one_block],
         in_specs=[smem] + [hbm] * 4,
-        out_specs=[vmem] * PLANE,
-        scratch_shapes=[pltpu.SemaphoreType.DMA((2,)), pltpu.SemaphoreType.DMA((PLANE - 1, 2 * planes))],
+        out_specs=[vmem] * 2,
+        scratch_shapes=[pltpu.SemaphoreType.DMA((2,)), pltpu.SemaphoreType.DMA((2 * planes,))],
         compiler_params=params,
     )(index, qkv_in, out_in, x_in, c_in)
+    blocks = pl.pallas_call(
+        functools.partial(blocks_kernel, planes),
+        out_shape=[one_block] * (PLANE - 2),
+        in_specs=[smem] + [hbm] * 2,
+        out_specs=[vmem] * (PLANE - 2),
+        scratch_shapes=[pltpu.SemaphoreType.DMA((PLANE - 2, 2 * planes))],
+        compiler_params=params,
+    )(index, x_in, c_in)
+    blocks = [*blocks, far_block]
     gain = norm_gain[0].reshape(shards, width)
     blocks = far_first([None] + blocks, PLANE, along_plane)
     pieces = {0: pack}
@@ -446,7 +462,12 @@
         [(grads[1:], F32)] + [(grads[1:], BF16)] * (planes - 1),
         index, keep, to_sibling(send), scalars=1,
     )
-    parts = [round_z(merged[k], k) for k in range(1, planes)]
+    pieces, parts = dict(enumerate(merged)), []
+    for step in [1 << bit for bit in range(planes.bit_length() - 1)]:
+        got = {k ^ step: along_z(pieces.pop(k), step) for k in sorted(pieces, reverse=True) if k & step}
+        parts.append(got.pop(0))
+        for k, part in got.items():
+            (pieces[k],) = call(add_kernel, [(grads[1:], BF16)], pieces[k], part)
     grad_qkv, grad_out = call(
         functools.partial(last_kernel, qkv_rows),
         [((qkv_rows, width), F32), ((heads, width), F32)],

time: 60.9 us -> 61.3 us (level)
  Pallas kernels: 11 us -> 12.3 us
  starting transfers between devices: 23.6 us -> 22.9 us
    ppermute x3 -> x6, waiting for transfers between devices: 5.81 us -> 13.8 us  [along_z(): return lax.ppermute(value, 'dp', route)]
    ppermute x3 -> x0, waiting for transfers between devices: 7.75 us -> none  [round_z(): return lax.ppermute(value, 'dp', route)]
    ppermute x3 -> x0, starting transfers between devices: 5.63 us -> none  [round_z(): return lax.ppermute(value, 'dp', route)]
    ppermute x3 -> x6, starting transfers between devices: 4.73 us -> 9.55 us  [along_z(): return lax.ppermute(value, 'dp', route)]
    pallas_call x1 -> x2, Pallas kernels: 2.06 us -> 3.35 us  [the longest x1 1.69 us: planar(): pl.pallas_call(functools.partial(blocks_kernel, planes), out_shape=[one_b...]
    pallas_call x5 -> x6, Pallas kernels: 7.43 us -> 7.46 us  [call(): pl.pallas_call(kernel, out_shape=[jax.ShapeDtypeStruct(shape, dtype) for...]
  transfers between devices with their start and end apart: 20 -> 20, of which waited for: 12 -> 12; matrix products, arithmetic and copies ran while one was open for 0% -> 0% of each run, Pallas kernels for 2% -> 5%
where the time goes in v13:
time: 61.3 us; the launch traced here: 61 us
  waiting for transfers between devices  24.9 us (41%)
  starting transfers between devices  22.9 us (37%)
  Pallas kernels  12.3 us (20%)
  between operations  0.75 us (1%)
    ppermute x6, waiting for transfers between devices, along_z(): return lax.ppermute(value, 'dp', route)  13.8 us
    ppermute x9, starting transfers between devices, along_plane(): return lax.ppermute(value, 'dp', route)  12.2 us
    ppermute x6, starting transfers between devices, along_z(): return lax.ppermute(value, 'dp', route)  9.55 us
    ppermute x9, waiting for transfers between devices, along_plane(): return lax.ppermute(value, 'dp', route)  8.2 us
    pallas_call x6, Pallas kernels, call(): pl.pallas_call(kernel, out_shape=[jax.ShapeDtypeStruct(shape, dtype) for...  7.46 us
    ppermute x5, waiting for transfers between devices, to_sibling(): return lax.ppermute(value, 'section', [(0, 1), (1, 0)])  2.92 us
    pallas_call x1, Pallas kernels, planar(): pl.pallas_call(functools.partial(blocks_kernel, planes), out_shape=[one_b...  1.69 us
    pallas_call x1, Pallas kernels, planar(): pl.pallas_call(functools.partial(first_kernel, planes), out_shape=[jax.Sh...  1.66 us
  transfers between devices with their start and end apart: 20, of which 12 were waited for; matrix products, arithmetic and copies ran while one was open for 0% of the time, Pallas kernels for 5%

profile of v13, /device:TPU:0, one launch (start us, length us, event | category | flops | bytes accessed | tf_op | source)
XLA Modules:
  0.0 61.0 jit_solution(11653746041742404131)
XLA Ops:
  0.6 0.1 pad_add_fusion.index
  0.7 1.7 %shard_map.77 = (bf16[256,256]{1,0:T(8,128)(2,1)S(1)}, bf16[2,64,1024]{2,1,0:T(8,128)(2,1)S(1)}) custom-call(s32[3]{0:T(128)S(1)} %pad_add_fusion.index, bf16[192,256]{1,0:T(8,128)(2,1)} %bitcast.11, bf16[64,256]{1,0:T(8,128)(2,1)} %bitcast.12, bf16[2,64,4096]{2,1,0:T(8,128)(2,1)} %x_ref.5, bf16[2,64,4096]{2,1,0:T(8,128)(2,1)} %c_ref.5), custom_call_target="tpu_custom_call" | custom-call | tf_op jit(solution)/shard_map/pallas_call | solution.py:403
  2.4 4.0 %collective-permute-start = (bf16[2,64,1024]{2,1,0:T(8,128)(2,1)S(1)}, bf16[2,64,1024]{2,1,0:T(8,128)(2,1)S(1)}, u32[]{:S(2)}, u32[]{:S(2)}) collective-permute-start(bf16[2,64,1024]{2,1,0:T(8,128)(2,1)S(1)} %get-tuple-element.28), channel_id=1, source_target_pairs={{0,3},{1,2},{2,1},{3,0},{4,7},{5,6},{6,5},{7,4},{8,11},{9,10},{10,... | collective-permute-start | bytes 786440 | tf_op jit(solution)/shard_map/ppermute | solution.py:390
  6.4 0.0 copy-start.1
  6.4 2.6 %collective-permute-start.4 = (bf16[256,256]{1,0:T(8,128)(2,1)S(1)}, bf16[256,256]{1,0:T(8,128)(2,1)S(1)}, u32[]{:S(2)}, u32[]{:S(2)}) collective-permute-start(bf16[256,256]{1,0:T(8,128)(2,1)S(1)} %get-tuple-element.29.pack_ref), channel_id=1, source_target_pairs={{0,8},{1,9},{2,10},{3,11},{4,12},{5,13},{6,14},{7,15},{8,0},{9,1},... | collective-permute-start | bytes 393224 | tf_op jit(solution)/shard_map/ppermute | solution.py:383
  8.9 1.6 %collective-permute-start.3 = (bf16[256,256]{1,0:T(8,128)(2,1)S(1)}, bf16[256,256]{1,0:T(8,128)(2,1)S(1)}, u32[]{:S(2)}, u32[]{:S(2)}) collective-permute-start(bf16[256,256]{1,0:T(8,128)(2,1)S(1)} %get-tuple-element.29.pack_ref), channel_id=1, source_target_pairs={{0,4},{1,5},{2,6},{3,7},{4,0},{5,1},{6,2},{7,3},{8,12},{9,13},{10,... | collective-permute-start | bytes 393224 | tf_op jit(solution)/shard_map/ppermute | solution.py:383
  10.5 1.7 %shard_map.79 = (bf16[2,64,1024]{2,1,0:T(8,128)(2,1)S(1)}, bf16[2,64,1024]{2,1,0:T(8,128)(2,1)S(1)}) custom-call(s32[3]{0:T(128)S(1)} %pad_add_fusion.index, bf16[2,64,4096]{2,1,0:T(8,128)(2,1)} %x_ref.5, bf16[2,64,4096]{2,1,0:T(8,128)(2,1)} %c_ref.5), custom_call_target="tpu_custom_call" | custom-call | tf_op jit(solution)/shard_map/pallas_call | solution.py:411
  12.2 0.6 collective-permute-start.1
  12.8 0.5 collective-permute-start.2
  13.3 1.8 %collective-permute-done.4.refs_6_ = bf16[256,256]{1,0:T(8,128)(2,1)S(1)} collective-permute-done((bf16[256,256]{1,0:T(8,128)(2,1)S(1)}, bf16[256,256]{1,0:T(8,128)(2,1)S(1)}, u32[]{:S(2)}, u32[]{:S(2)}) %collective-permute-start.4) | collective-permute-done | bytes 131104 | tf_op jit(solution)/shard_map/ppermute | solution.py:383
  15.1 0.6 collective-permute-start.5
  15.7 0.0 collective-permute-done.3.refs_5_
  15.7 0.0 collective-permute-start.7
  15.7 0.0 copy-done.1
  15.7 0.1 reduce
  15.8 0.0 collective-permute-done.refs_1_
  15.8 1.5 %shard_map.78 = (bf16[272,256]{1,0:T(8,128)(2,1)S(1)}, bf16[2,64,1024]{2,1,0:T(8,128)(2,1)S(1)}) custom-call(s32[3]{0:T(128)S(1)} %pad_add_fusion.index, bf16[256,256]{1,0:T(8,128)(2,1)S(1)} %get-tuple-element.29.pack_ref, bf16[16,256]{1,0:T(8,128)(2,1)S(1)} %reshape_squeeze.3.gain_ref, bf16[2,64,4096]{2,1,0:T(8,128)(2,1)} %x_ref.5, bf16[2,64,4096]{2,1,0:T(8,128)(2,1)} %c_ref.5), custom_call_target="tpu_custom_call" | custom-call | tf_op jit(solution)/shard_map/pallas_call | solution.py:427
  17.3 0.6 collective-permute-start.6
  17.8 2.2 %collective-permute-done.5.refs_7_ = bf16[256,256]{1,0:T(8,128)(2,1)S(1)} collective-permute-done((bf16[256,256]{1,0:T(8,128)(2,1)S(1)}, bf16[256,256]{1,0:T(8,128)(2,1)S(1)}, u32[]{:S(2)}, u32[]{:S(2)}) %collective-permute-start.5) | collective-permute-done | bytes 131104 | tf_op jit(solution)/shard_map/ppermute | solution.py:383
  20.1 0.0 collective-permute-start.9
  20.1 0.0 collective-permute-done.7.refs_9_
  20.1 0.5 collective-permute-start.8
  20.6 0.0 collective-permute-done.1.refs_2_
  20.6 0.0 collective-permute-done.2.refs_3_
  20.6 0.8 %collective-permute-done.9.refs_11_ = bf16[256,256]{1,0:T(8,128)(2,1)S(1)} collective-permute-done((bf16[256,256]{1,0:T(8,128)(2,1)S(1)}, bf16[256,256]{1,0:T(8,128)(2,1)S(1)}, u32[]{:S(2)}, u32[]{:S(2)}) %collective-permute-start.9) | collective-permute-done | bytes 131104 | tf_op jit(solution)/shard_map/ppermute | solution.py:386
  21.4 0.2 collective-permute-done.8.refs_10_
  21.6 0.0 collective-permute-done.6.refs_8_
  21.6 1.6 %shard_map.80 = (bf16[4,64,1024]{2,1,0:T(8,128)(2,1)S(1)}, bf16[4,64,1024]{2,1,0:T(8,128)(2,1)S(1)}, bf16[4,512,256]{2,1,0:T(8,128)(2,1)S(1)}, f32[4,8,256]{2,1,...) custom-call(s32[3]{0:T(128)S(1)} %pad_add_fusion.index, ...), custom_call_target="tpu_custom_call" | custom-call | tf_op jit(solution)/shard_map/pallas_call | solution.py:360
  23.2 0.7 %collective-permute-start.10 = (bf16[64,896]{1,0:T(8,128)(2,1)S(1)}, bf16[64,896]{1,0:T(8,128)(2,1)S(1)}, u32[]{:S(2)}, u32[]{:S(2)}) collective-permute-start(bf16[64,896]{1,0:T(8,128)(2,1)S(1)} %get-tuple-element.36), channel_id=1, source_target_pairs={{0,3},{1,2},{2,1},{3,0},{4,7},{5,6},{6,5},{7,4},{8,11},{9,10},{10,... | collective-permute-start | bytes 344072 | tf_op jit(solution)/shard_map/ppermute | solution.py:390
  23.9 1.3 %collective-permute-start.11 = (bf16[64,896]{1,0:T(8,128)(2,1)S(1)}, bf16[64,896]{1,0:T(8,128)(2,1)S(1)}, u32[]{:S(2)}, u32[]{:S(2)}) collective-permute-start(bf16[64,896]{1,0:T(8,128)(2,1)S(1)} %get-tuple-element.37), channel_id=1, source_target_pairs={{0,2},{1,3},{2,0},{3,1},{4,6},{5,7},{6,4},{7,5},{8,10},{9,11},{10,... | collective-permute-start | bytes 344072 | tf_op jit(solution)/shard_map/ppermute | solution.py:390
  25.3 0.0 copy-start
  25.3 1.5 %collective-permute-start.12 = (bf16[64,896]{1,0:T(8,128)(2,1)S(1)}, bf16[64,896]{1,0:T(8,128)(2,1)S(1)}, u32[]{:S(2)}, u32[]{:S(2)}) collective-permute-start(bf16[64,896]{1,0:T(8,128)(2,1)S(1)} %get-tuple-element.38), channel_id=1, source_target_pairs={{0,1},{1,0},{2,3},{3,2},{4,5},{5,4},{6,7},{7,6},{8,9},{9,8},{10,11... | collective-permute-start | bytes 344072 | tf_op jit(solution)/shard_map/ppermute | solution.py:390
  26.8 3.4 %collective-permute-done.10.refs_0_ = bf16[64,896]{1,0:T(8,128)(2,1)S(1)} collective-permute-done((bf16[64,896]{1,0:T(8,128)(2,1)S(1)}, bf16[64,896]{1,0:T(8,128)(2,1)S(1)}, u32[]{:S(2)}, u32[]{:S(2)}) %collective-permute-start.10) | collective-permute-done | bytes 114720 | tf_op jit(solution)/shard_map/ppermute | solution.py:390
  30.2 1.3 %collective-permute-done.11.refs_1_ = bf16[64,896]{1,0:T(8,128)(2,1)S(1)} collective-permute-done((bf16[64,896]{1,0:T(8,128)(2,1)S(1)}, bf16[64,896]{1,0:T(8,128)(2,1)S(1)}, u32[]{:S(2)}, u32[]{:S(2)}) %collective-permute-start.11) | collective-permute-done | bytes 114720 | tf_op jit(solution)/shard_map/ppermute | solution.py:390
  31.5 0.0 collective-permute-done.12.refs_2_
  31.5 0.0 copy-done
  31.5 2.9 %shard_map.81.refs_0_ = bf16[64,640]{1,0:T(8,128)(2,1)S(1)} custom-call(s32[3]{0:T(128)S(1)} %pad_add_fusion.index, s32[2,1,2]{2,1,0:T(1,128)S(1)} %copy-done, bf16[64,896]{1,0:T(8,128)(2,1)S(1)} %collective-permute-done.10.refs_0_, bf16[64,896]{1,0:T(8,128)(2,1)S(1)} %collective-permute-done.11.refs_1_, ...), custom_call_target="tpu_custom_call" | custom-call | tf_op jit(solution)/shard_map/pallas_call | solution.py:360
  34.4 1.2 %collective-permute-start.15 = (bf16[64,640]{1,0:T(8,128)(2,1)S(1)}, bf16[64,640]{1,0:T(8,128)(2,1)S(1)}, u32[]{:S(2)}, u32[]{:S(2)}) collective-permute-start(bf16[64,640]{1,0:T(8,128)(2,1)S(1)} %shard_map.81.refs_0_), channel_id=1, source_target_pairs={{0,3},{1,2},{2,1},{3,0},{4,7},{5,6},{6,5},{7,4},{8,11},{9,10},{10,... | collective-permute-start | bytes 245768 | tf_op jit(solution)/shard_map/ppermute | solution.py:390
  35.7 1.3 %collective-permute-start.14 = (bf16[64,640]{1,0:T(8,128)(2,1)S(1)}, bf16[64,640]{1,0:T(8,128)(2,1)S(1)}, u32[]{:S(2)}, u32[]{:S(2)}) collective-permute-start(bf16[64,640]{1,0:T(8,128)(2,1)S(1)} %shard_map.81.refs_0_), channel_id=1, source_target_pairs={{0,2},{1,3},{2,0},{3,1},{4,6},{5,7},{6,4},{7,5},{8,10},{9,11},{10,... | collective-permute-start | bytes 245768 | tf_op jit(solution)/shard_map/ppermute | solution.py:390
  37.0 1.0 %collective-permute-start.13 = (bf16[64,640]{1,0:T(8,128)(2,1)S(1)}, bf16[64,640]{1,0:T(8,128)(2,1)S(1)}, u32[]{:S(2)}, u32[]{:S(2)}) collective-permute-start(bf16[64,640]{1,0:T(8,128)(2,1)S(1)} %shard_map.81.refs_0_), channel_id=1, source_target_pairs={{0,1},{1,0},{2,3},{3,2},{4,5},{5,4},{6,7},{7,6},{8,9},{9,8},{10,11... | collective-permute-start | bytes 245768 | tf_op jit(solution)/shard_map/ppermute | solution.py:390
  38.0 2.5 %collective-permute-done.15.refs_3_ = bf16[64,640]{1,0:T(8,128)(2,1)S(1)} collective-permute-done((bf16[64,640]{1,0:T(8,128)(2,1)S(1)}, bf16[64,640]{1,0:T(8,128)(2,1)S(1)}, u32[]{:S(2)}, u32[]{:S(2)}) %collective-permute-start.15) | collective-permute-done | bytes 81952 | tf_op jit(solution)/shard_map/ppermute | solution.py:390
  40.5 0.5 collective-permute-done.14.refs_2_
  41.0 0.5 collective-permute-done.13.refs_1_
  41.4 1.6 %shard_map.82 = (f32[4,256,256]{2,1,0:T(8,128)S(1)}, bf16[4,256,256]{2,1,0:T(8,128)(2,1)S(1)}) custom-call(s32[3]{0:T(128)S(1)} %pad_add_fusion.index, bf16[64,640]{1,0:T(8,128)(2,1)S(1)} %shard_map.81.refs_0_, bf16[64,640]{1,0:T(8,128)(2,1)S(1)} %collective-permute-done.13.refs_1_, bf16[64,640]{1,0:T(8,128)(2,1)S(1)} %collective-permute-done.14.refs_2_, ...), custom_call_target="tpu_custom_call" | custom-call | tf_op jit(solution)/shard_map/pallas_call | solution.py:360
  43.0 0.1 collective-permute-start.16
  43.1 1.9 %collective-permute-done.16.come_ref = bf16[4,256,256]{2,1,0:T(8,128)(2,1)S(1)} collective-permute-done((bf16[4,256,256]{2,1,0:T(8,128)(2,1)S(1)}, bf16[4,256,256]{2,1,0:T(8,128)(2,1)S(1)}, u32[]{:S(2)}, u32[]{:S(2)}) %collective-permute-start.16) | collective-permute-done | bytes 524320 | tf_op jit(solution)/shard_map/ppermute | solution.py:386
  45.0 0.6 %shard_map.83 = (f32[256,256]{1,0:T(8,128)S(1)}, bf16[256,256]{1,0:T(8,128)(2,1)S(1)}, bf16[256,256]{1,0:T(8,128)(2,1)S(1)}, bf16[256,256]{1,0:T(8,128)(2,1)S(1)}) custom-call(s32[3]{0:T(128)S(1)} %pad_add_fusion.index, f32[4,256,256]{2,1,0:T(8,128)S(1)} %get-tuple-element.44.keep_ref, bf16[4,256,256]{2,1,0:T(8,128)(2,1)S(1)} %collective-permute-done.16.come_ref), custom_call_target="tpu_custom_call" | custom-call | tf_op jit(solution)/shard_map/pallas_call | solution.py:360
  45.6 1.1 %collective-permute-start.18 = (bf16[256,256]{1,0:T(8,128)(2,1)S(1)}, bf16[256,256]{1,0:T(8,128)(2,1)S(1)}, u32[]{:S(2)}, u32[]{:S(2)}) collective-permute-start(bf16[256,256]{1,0:T(8,128)(2,1)S(1)} %get-tuple-element.49), channel_id=1, source_target_pairs={{0,4},{1,5},{2,6},{3,7},{4,0},{5,1},{6,2},{7,3},{8,12},{9,13},{10,... | collective-permute-start | bytes 393224 | tf_op jit(solution)/shard_map/ppermute | solution.py:383
  46.7 1.0 %collective-permute-start.17 = (bf16[256,256]{1,0:T(8,128)(2,1)S(1)}, bf16[256,256]{1,0:T(8,128)(2,1)S(1)}, u32[]{:S(2)}, u32[]{:S(2)}) collective-permute-start(bf16[256,256]{1,0:T(8,128)(2,1)S(1)} %get-tuple-element.47), channel_id=1, source_target_pairs={{0,4},{1,5},{2,6},{3,7},{4,0},{5,1},{6,2},{7,3},{8,12},{9,13},{10,... | collective-permute-start | bytes 393224 | tf_op jit(solution)/shard_map/ppermute | solution.py:383
  47.7 4.3 %collective-permute-done.18.b_ref = bf16[256,256]{1,0:T(8,128)(2,1)S(1)} collective-permute-done((bf16[256,256]{1,0:T(8,128)(2,1)S(1)}, bf16[256,256]{1,0:T(8,128)(2,1)S(1)}, u32[]{:S(2)}, u32[]{:S(2)}) %collective-permute-start.18) | collective-permute-done | bytes 131104 | tf_op jit(solution)/shard_map/ppermute | solution.py:383
  52.1 2.7 %collective-permute-start.19 = (bf16[256,256]{1,0:T(8,128)(2,1)S(1)}, bf16[256,256]{1,0:T(8,128)(2,1)S(1)}, u32[]{:S(2)}, u32[]{:S(2)}) collective-permute-start(bf16[256,256]{1,0:T(8,128)(2,1)S(1)} %shard_map.84), channel_id=1, source_target_pairs={{0,8},{1,9},{2,10},{3,11},{4,12},{5,13},{6,14},{7,15},{8,0},{9,1},... | collective-permute-start | bytes 393224 | tf_op jit(solution)/shard_map/ppermute | solution.py:383
  54.8 0.0 collective-permute-done.17.refs_0_
  54.8 5.4 %collective-permute-done.19.refs_1_ = bf16[256,256]{1,0:T(8,128)(2,1)S(1)} collective-permute-done((bf16[256,256]{1,0:T(8,128)(2,1)S(1)}, bf16[256,256]{1,0:T(8,128)(2,1)S(1)}, u32[]{:S(2)}, u32[]{:S(2)}) %collective-permute-start.19) | collective-permute-done | bytes 131104 | tf_op jit(solution)/shard_map/ppermute | solution.py:383
  60.2 0.7 %shard_map.85 = (f32[192,256]{1,0:T(8,128)}, f32[64,256]{1,0:T(8,128)}) custom-call(f32[256,256]{1,0:T(8,128)S(1)} %get-tuple-element.46.keep_ref, bf16[256,256]{1,0:T(8,128)(2,1)S(1)} %collective-permute-done.17.refs_0_, bf16[256,256]{1,0:T(8,128)(2,1)S(1)} %collective-permute-done.19.refs_1_), custom_call_target="tpu_custom_call" | custom-call | tf_op jit(solution)/shard_map/pallas_call | solution.py:360
  (2 shorter events, 0.0 us)
Async XLA Ops:
  2.4 13.4 %collective-permute-start = (bf16[2,64,1024]{2,1,0:T(8,128)(2,1)S(1)}, bf16[2,64,1024]{2,1,0:T(8,128)(2,1)S(1)}, u32[]{:S(2)}, u32[]{:S(2)}) collective-permute-start(bf16[2,64,1024]{2,1,0:T(8,128)(2,1)S(1)} %get-tuple-element.28), channel_id=1, source_target_pairs={{0,3},{1,2},{2,1},{3,0},{4,7},{5,6},{6,5},{7,4},{8,11},{9,10},{10,... | collective-permute-start | bytes 786440 | tf_op jit(solution)/shard_map/ppermute | solution.py:390
  6.4 9.3 %copy-start.1 = (bf16[1,4096]{1,0:T(2,128)(2,1)S(1)}, bf16[1,4096]{1,0:T(2,128)(2,1)}, u32[]{:S(2)}) copy-start(bf16[1,4096]{1,0:T(2,128)(2,1)} %param.9) | copy-start | bytes 24580
  6.4 8.8 %collective-permute-start.4 = (bf16[256,256]{1,0:T(8,128)(2,1)S(1)}, bf16[256,256]{1,0:T(8,128)(2,1)S(1)}, u32[]{:S(2)}, u32[]{:S(2)}) collective-permute-start(bf16[256,256]{1,0:T(8,128)(2,1)S(1)} %get-tuple-element.29.pack_ref), channel_id=1, source_target_pairs={{0,8},{1,9},{2,10},{3,11},{4,12},{5,13},{6,14},{7,15},{8,0},{9,1},... | collective-permute-start | bytes 393224 | tf_op jit(solution)/shard_map/ppermute | solution.py:383
  8.9 6.8 %collective-permute-start.3 = (bf16[256,256]{1,0:T(8,128)(2,1)S(1)}, bf16[256,256]{1,0:T(8,128)(2,1)S(1)}, u32[]{:S(2)}, u32[]{:S(2)}) collective-permute-start(bf16[256,256]{1,0:T(8,128)(2,1)S(1)} %get-tuple-element.29.pack_ref), channel_id=1, source_target_pairs={{0,4},{1,5},{2,6},{3,7},{4,0},{5,1},{6,2},{7,3},{8,12},{9,13},{10,... | collective-permute-start | bytes 393224 | tf_op jit(solution)/shard_map/ppermute | solution.py:383
  12.2 8.4 %collective-permute-start.1 = (bf16[2,64,1024]{2,1,0:T(8,128)(2,1)S(1)}, bf16[2,64,1024]{2,1,0:T(8,128)(2,1)S(1)}, u32[]{:S(2)}, u32[]{:S(2)}) collective-permute-start(bf16[2,64,1024]{2,1,0:T(8,128)(2,1)S(1)} %get-tuple-element.32), channel_id=1, source_target_pairs={{0,2},{1,3},{2,0},{3,1},{4,6},{5,7},{6,4},{7,5},{8,10},{9,11},{10,... | collective-permute-start | bytes 786440 | tf_op jit(solution)/shard_map/ppermute | solution.py:390
  12.8 7.8 %collective-permute-start.2 = (bf16[2,64,1024]{2,1,0:T(8,128)(2,1)S(1)}, bf16[2,64,1024]{2,1,0:T(8,128)(2,1)S(1)}, u32[]{:S(2)}, u32[]{:S(2)}) collective-permute-start(bf16[2,64,1024]{2,1,0:T(8,128)(2,1)S(1)} %get-tuple-element.33), channel_id=1, source_target_pairs={{0,1},{1,0},{2,3},{3,2},{4,5},{5,4},{6,7},{7,6},{8,9},{9,8},{10,11... | collective-permute-start | bytes 786440 | tf_op jit(solution)/shard_map/ppermute | solution.py:390
  15.1 5.0 %collective-permute-start.5 = (bf16[256,256]{1,0:T(8,128)(2,1)S(1)}, bf16[256,256]{1,0:T(8,128)(2,1)S(1)}, u32[]{:S(2)}, u32[]{:S(2)}) collective-permute-start(bf16[256,256]{1,0:T(8,128)(2,1)S(1)} %collective-permute-done.4.refs_6_), channel_id=1, source_target_pairs={{0,4},{1,5},{2,6},{3,7},{4,0},{5,1},{6,2},{7,3},{8,12},{9,13},{10,... | collective-permute-start | bytes 393224 | tf_op jit(solution)/shard_map/ppermute | solution.py:383
  15.7 4.4 %collective-permute-start.7 = (bf16[256,256]{1,0:T(8,128)(2,1)S(1)}, bf16[256,256]{1,0:T(8,128)(2,1)S(1)}, u32[]{:S(2)}, u32[]{:S(2)}) collective-permute-start(bf16[256,256]{1,0:T(8,128)(2,1)S(1)} %collective-permute-done.3.refs_5_), channel_id=1, source_target_pairs={{0,16},{16,0},{1,17},{17,1},{2,18},{18,2},{3,19},{19,3},{4,20},{20... | collective-permute-start | bytes 393224 | tf_op jit(solution)/shard_map/ppermute | solution.py:386
  17.3 4.3 %collective-permute-start.6 = (bf16[272,256]{1,0:T(8,128)(2,1)S(1)}, bf16[272,256]{1,0:T(8,128)(2,1)S(1)}, u32[]{:S(2)}, u32[]{:S(2)}) collective-permute-start(bf16[272,256]{1,0:T(8,128)(2,1)S(1)} %get-tuple-element.34.refs_4_), channel_id=1, source_target_pairs={{0,16},{16,0},{1,17},{17,1},{2,18},{18,2},{3,19},{19,3},{4,20},{20... | collective-permute-start | bytes 417800 | tf_op jit(solution)/shard_map/ppermute | solution.py:386
  20.1 1.3 %collective-permute-start.9 = (bf16[256,256]{1,0:T(8,128)(2,1)S(1)}, bf16[256,256]{1,0:T(8,128)(2,1)S(1)}, u32[]{:S(2)}, u32[]{:S(2)}) collective-permute-start(bf16[256,256]{1,0:T(8,128)(2,1)S(1)} %collective-permute-done.5.refs_7_), channel_id=1, source_target_pairs={{0,16},{16,0},{1,17},{17,1},{2,18},{18,2},{3,19},{19,3},{4,20},{20... | collective-permute-start | bytes 393224 | tf_op jit(solution)/shard_map/ppermute | solution.py:386
  20.1 1.5 %collective-permute-start.8 = (bf16[256,256]{1,0:T(8,128)(2,1)S(1)}, bf16[256,256]{1,0:T(8,128)(2,1)S(1)}, u32[]{:S(2)}, u32[]{:S(2)}) collective-permute-start(bf16[256,256]{1,0:T(8,128)(2,1)S(1)} %collective-permute-done.4.refs_6_), channel_id=1, source_target_pairs={{0,16},{16,0},{1,17},{17,1},{2,18},{18,2},{3,19},{19,3},{4,20},{20... | collective-permute-start | bytes 393224 | tf_op jit(solution)/shard_map/ppermute | solution.py:386
  23.2 7.0 %collective-permute-start.10 = (bf16[64,896]{1,0:T(8,128)(2,1)S(1)}, bf16[64,896]{1,0:T(8,128)(2,1)S(1)}, u32[]{:S(2)}, u32[]{:S(2)}) collective-permute-start(bf16[64,896]{1,0:T(8,128)(2,1)S(1)} %get-tuple-element.36), channel_id=1, source_target_pairs={{0,3},{1,2},{2,1},{3,0},{4,7},{5,6},{6,5},{7,4},{8,11},{9,10},{10,... | collective-permute-start | bytes 344072 | tf_op jit(solution)/shard_map/ppermute | solution.py:390
  23.9 7.6 %collective-permute-start.11 = (bf16[64,896]{1,0:T(8,128)(2,1)S(1)}, bf16[64,896]{1,0:T(8,128)(2,1)S(1)}, u32[]{:S(2)}, u32[]{:S(2)}) collective-permute-start(bf16[64,896]{1,0:T(8,128)(2,1)S(1)} %get-tuple-element.37), channel_id=1, source_target_pairs={{0,2},{1,3},{2,0},{3,1},{4,6},{5,7},{6,4},{7,5},{8,10},{9,11},{10,... | collective-permute-start | bytes 344072 | tf_op jit(solution)/shard_map/ppermute | solution.py:390
  25.3 6.2 %copy-start = (s32[2,1,2]{2,1,0:T(1,128)S(1)}, s32[2,1,2]{2,1,0:T(1,128)}, u32[]{:S(2)}) copy-start(s32[2,1,2]{2,1,0:T(1,128)} %docs.1) | copy-start | bytes 52
  25.3 6.2 %collective-permute-start.12 = (bf16[64,896]{1,0:T(8,128)(2,1)S(1)}, bf16[64,896]{1,0:T(8,128)(2,1)S(1)}, u32[]{:S(2)}, u32[]{:S(2)}) collective-permute-start(bf16[64,896]{1,0:T(8,128)(2,1)S(1)} %get-tuple-element.38), channel_id=1, source_target_pairs={{0,1},{1,0},{2,3},{3,2},{4,5},{5,4},{6,7},{7,6},{8,9},{9,8},{10,11... | collective-permute-start | bytes 344072 | tf_op jit(solution)/shard_map/ppermute | solution.py:390
  34.4 6.0 %collective-permute-start.15 = (bf16[64,640]{1,0:T(8,128)(2,1)S(1)}, bf16[64,640]{1,0:T(8,128)(2,1)S(1)}, u32[]{:S(2)}, u32[]{:S(2)}) collective-permute-start(bf16[64,640]{1,0:T(8,128)(2,1)S(1)} %shard_map.81.refs_0_), channel_id=1, source_target_pairs={{0,3},{1,2},{2,1},{3,0},{4,7},{5,6},{6,5},{7,4},{8,11},{9,10},{10,... | collective-permute-start | bytes 245768 | tf_op jit(solution)/shard_map/ppermute | solution.py:390
  35.7 5.3 %collective-permute-start.14 = (bf16[64,640]{1,0:T(8,128)(2,1)S(1)}, bf16[64,640]{1,0:T(8,128)(2,1)S(1)}, u32[]{:S(2)}, u32[]{:S(2)}) collective-permute-start(bf16[64,640]{1,0:T(8,128)(2,1)S(1)} %shard_map.81.refs_0_), channel_id=1, source_target_pairs={{0,2},{1,3},{2,0},{3,1},{4,6},{5,7},{6,4},{7,5},{8,10},{9,11},{10,... | collective-permute-start | bytes 245768 | tf_op jit(solution)/shard_map/ppermute | solution.py:390
  37.0 4.4 %collective-permute-start.13 = (bf16[64,640]{1,0:T(8,128)(2,1)S(1)}, bf16[64,640]{1,0:T(8,128)(2,1)S(1)}, u32[]{:S(2)}, u32[]{:S(2)}) collective-permute-start(bf16[64,640]{1,0:T(8,128)(2,1)S(1)} %shard_map.81.refs_0_), channel_id=1, source_target_pairs={{0,1},{1,0},{2,3},{3,2},{4,5},{5,4},{6,7},{7,6},{8,9},{9,8},{10,11... | collective-permute-start | bytes 245768 | tf_op jit(solution)/shard_map/ppermute | solution.py:390
  43.0 2.0 %collective-permute-start.16 = (bf16[4,256,256]{2,1,0:T(8,128)(2,1)S(1)}, bf16[4,256,256]{2,1,0:T(8,128)(2,1)S(1)}, u32[]{:S(2)}, u32[]{:S(2)}) collective-permute-start(bf16[4,256,256]{2,1,0:T(8,128)(2,1)S(1)} %get-tuple-element.45), channel_id=1, source_target_pairs={{0,16},{16,0},{1,17},{17,1},{2,18},{18,2},{3,19},{19,3},{4,20},{20... | collective-permute-start | bytes 1572872 | tf_op jit(solution)/shard_map/ppermute | solution.py:386
  45.6 6.4 %collective-permute-start.18 = (bf16[256,256]{1,0:T(8,128)(2,1)S(1)}, bf16[256,256]{1,0:T(8,128)(2,1)S(1)}, u32[]{:S(2)}, u32[]{:S(2)}) collective-permute-start(bf16[256,256]{1,0:T(8,128)(2,1)S(1)} %get-tuple-element.49), channel_id=1, source_target_pairs={{0,4},{1,5},{2,6},{3,7},{4,0},{5,1},{6,2},{7,3},{8,12},{9,13},{10,... | collective-permute-start | bytes 393224 | tf_op jit(solution)/shard_map/ppermute | solution.py:383
  46.7 8.1 %collective-permute-start.17 = (bf16[256,256]{1,0:T(8,128)(2,1)S(1)}, bf16[256,256]{1,0:T(8,128)(2,1)S(1)}, u32[]{:S(2)}, u32[]{:S(2)}) collective-permute-start(bf16[256,256]{1,0:T(8,128)(2,1)S(1)} %get-tuple-element.47), channel_id=1, source_target_pairs={{0,4},{1,5},{2,6},{3,7},{4,0},{5,1},{6,2},{7,3},{8,12},{9,13},{10,... | collective-permute-start | bytes 393224 | tf_op jit(solution)/shard_map/ppermute | solution.py:383
  52.1 8.1 %collective-permute-start.19 = (bf16[256,256]{1,0:T(8,128)(2,1)S(1)}, bf16[256,256]{1,0:T(8,128)(2,1)S(1)}, u32[]{:S(2)}, u32[]{:S(2)}) collective-permute-start(bf16[256,256]{1,0:T(8,128)(2,1)S(1)} %shard_map.84), channel_id=1, source_target_pairs={{0,8},{1,9},{2,10},{3,11},{4,12},{5,13},{6,14},{7,15},{8,0},{9,1},... | collective-permute-start | bytes 393224 | tf_op jit(solution)/shard_map/ppermute | solution.py:383

commit v14 on v13

--- a/solution.py
+++ b/solution.py
@@ -237,8 +237,8 @@
     query, keys, values = (qkv[:, i * heads : (i + 1) * heads].astype(BF16) for i in range(3))
     scores = jnp.where(allowed, nt(query, keys) * heads ** (-0.5), -1e30)
     raised = jnp.exp(scores - jnp.max(scores, axis=1, keepdims=True))
-    probs = raised / jnp.sum(raised, axis=1, keepdims=True)
-    return probs, nn(probs.astype(BF16), values).astype(BF16)
+    scale = 1.0 / jnp.sum(raised, axis=1, keepdims=True)
+    return raised * scale, (nn(raised.astype(BF16), values) * scale).astype(BF16)
 
 
 def attention_grad(qkv, probs, att, d_att, heads):
@@ -298,21 +298,14 @@
     out_ref[...] = jnp.concatenate(factors, axis=1).astype(BF16)
 
 
-def grads_kernel(planes, heads, index, *refs):
-    factors, (x_ref, c_ref, vx_ref, gain_ref) = refs[:PLANE], refs[PLANE : PLANE + 4]
-    keep_ref, send_ref, all_ref = refs[PLANE + 4 :]
+def pieces_of(planes, heads, order, index, turned, small, small_t, x_ref, c_ref, vx_ref, gain_ref, keep_ref, send_ref):
     qkv, half, width = 3 * heads, 2 * heads, vx_ref.shape[-1]
-    section, p = index[0], index[2]
-    for k in range(PLANE):
-        all_ref[p ^ k] = factors[k][...]
+    section, place = index[0], index[1]
     rows = x_ref.shape[0] * x_ref.shape[1]
-    turned = jnp.transpose(all_ref[...].astype(F32).reshape(rows, 5 * half)).astype(BF16)
     att0, att1 = turned[qkv : qkv + heads], turned[4 * half : 4 * half + heads]
-    right = turned[2 * half : 4 * half]
-    small = nt(right, att0).astype(BF16)
-    small_t = nt(att0, right[:qkv]).astype(BF16)
-    for z in range(planes):
-        cols = slice(z * width, (z + 1) * width)
+    for i, k in enumerate(order):
+        z = place ^ k
+        cols = pl.ds(pl.multiple_of(z * width, width), width)
         x = x_ref[:, :, cols].reshape(rows, width)
         c = c_ref[:, :, cols].reshape(rows, width)
         out = vx_ref[z, qkv : qkv + heads, :]
@@ -320,19 +313,39 @@
         left = with_x[2 * half :] + nn(small, out)
         zero = with_x[:qkv] * gain_ref[z, 0:1, :]
         one = left[:qkv] * gain_ref[z, 1:2, :]
-        keep_ref[z, :qkv, :] = jnp.where(section == 0, zero, one)
-        send_ref[z, :qkv, :] = jnp.where(section == 0, one, zero).astype(BF16)
+        keep_ref[i, :qkv, :] = jnp.where(section == 0, zero, one)
+        send_ref[i, :qkv, :] = jnp.where(section == 0, one, zero).astype(BF16)
         zero = nn(att0, c) + nn(small_t, vx_ref[z, qkv + heads : 2 * qkv + heads, :]) - left[qkv:]
         one = nn(att1, c)
-        keep_ref[z, qkv:, :] = jnp.where(section == 0, zero, one)
-        send_ref[z, qkv:, :] = jnp.where(section == 0, one, zero).astype(BF16)
-
-
-def merge_kernel(index, keep_ref, come_ref, *out_refs):
-    place = index[1]
-    out_refs[0][...] = keep_ref[place] + come_ref[place].astype(F32)
-    for k in range(1, len(out_refs)):
-        out_refs[k][...] = (keep_ref[place ^ k] + come_ref[place ^ k].astype(F32)).astype(BF16)
+        keep_ref[i, qkv:, :] = jnp.where(section == 0, zero, one)
+        send_ref[i, qkv:, :] = jnp.where(section == 0, one, zero).astype(BF16)
+
+
+def far_grads_kernel(planes, heads, order, index, *refs):
+    factors, arrays = refs[:PLANE], refs[PLANE : PLANE + 4]
+    keep_ref, send_ref, turned_ref, small_ref, small_t_ref, all_ref = refs[PLANE + 4 :]
+    qkv, half = 3 * heads, 2 * heads
+    p = index[2]
+    for k in range(PLANE):
+        all_ref[p ^ k] = factors[k][...]
+    rows = all_ref.shape[0] * all_ref.shape[1]
+    turned = jnp.transpose(all_ref[...].astype(F32).reshape(rows, 5 * half)).astype(BF16)
+    att0, right = turned[qkv : qkv + heads], turned[2 * half : 4 * half]
+    small = nt(right, att0).astype(BF16)
+    small_t = nt(att0, right[:qkv]).astype(BF16)
+    turned_ref[...] = turned
+    small_ref[...] = small
+    small_t_ref[...] = small_t
+    pieces_of(planes, heads, order, index, turned, small, small_t, *arrays, keep_ref, send_ref)
+
+
+def near_grads_kernel(planes, heads, order, index, turned_ref, small_ref, small_t_ref, *refs):
+    pieces_of(planes, heads, order, index, turned_ref[...], small_ref[...], small_t_ref[...], *refs)
+
+
+def merge_kernel(keep_ref, come_ref, *out_refs):
+    for i, out_ref in enumerate(out_refs):
+        out_ref[...] = (keep_ref[i] + come_ref[i].astype(F32)).astype(out_ref.dtype)
 
 
 def add_kernel(a_ref, b_ref, out_ref):
@@ -450,28 +463,38 @@
         [((block, 5 * half), BF16)],
         index, doc_lengths, *exchange(sent)[::-1], scalars=2,
     )
-    grads = (planes, qkv_rows + heads, width)
-    keep, send = call(
-        functools.partial(grads_kernel, planes, heads),
-        [(grads, F32), (grads, BF16)],
+    piece = (qkv_rows + heads, width)
+    far_order = tuple(reversed(range(planes - planes // 2, planes)))
+    near_order = tuple(reversed(range(planes - planes // 2)))
+
+    def swap_and_merge(order, keep, send):
+        outs = [(piece, BF16 if k else F32) for k in order]
+        return zip(order, call(merge_kernel, outs, keep, to_sibling(send)))
+
+    keep, send, turned, small, small_t = call(
+        functools.partial(far_grads_kernel, planes, heads, far_order),
+        [((len(far_order),) + piece, F32), ((len(far_order),) + piece, BF16)]
+        + [((5 * half, rows), BF16), ((2 * half, heads), BF16), ((heads, qkv_rows), BF16)],
         index, *exchange(factors), x, c, vx, gains, scalars=1,
         scratch=[((PLANE, block, 5 * half), BF16)],
     )
-    merged = call(
-        merge_kernel,
-        [(grads[1:], F32)] + [(grads[1:], BF16)] * (planes - 1),
-        index, keep, to_sibling(send), scalars=1,
-    )
-    pieces, parts = dict(enumerate(merged)), []
+    pieces = dict(swap_and_merge(far_order, keep, send))
+    keep, send = call(
+        functools.partial(near_grads_kernel, planes, heads, near_order),
+        [((len(near_order),) + piece, F32), ((len(near_order),) + piece, BF16)],
+        index, turned, small, small_t, x, c, vx, gains, scalars=1,
+    )
+    pieces.update(swap_and_merge(near_order, keep, send))
+    kept, parts = pieces[0], []
     for step in [1 << bit for bit in range(planes.bit_length() - 1)]:
         got = {k ^ step: along_z(pieces.pop(k), step) for k in sorted(pieces, reverse=True) if k & step}
         parts.append(got.pop(0))
         for k, part in got.items():
-            (pieces[k],) = call(add_kernel, [(grads[1:], BF16)], pieces[k], part)
+            (pieces[k],) = call(add_kernel, [(piece, BF16)], pieces[k], part)
     grad_qkv, grad_out = call(
         functools.partial(last_kernel, qkv_rows),
         [((qkv_rows, width), F32), ((heads, width), F32)],
-        merged[0], *parts,
+        kept, *parts,
     )
     return (grad_qkv.T[None], grad_out[None])
 

time: 61.3 us -> 59.8 us (0.976)
  waiting for transfers between devices: 24.9 us -> 22.7 us
    ppermute x5 -> x6, waiting for transfers between devices: 2.92 us -> 1.03 us  [to_sibling(): return lax.ppermute(value, 'section', [(0, 1), (1, 0)])]
    ppermute x5 -> x6, starting transfers between devices: 1.15 us -> 1.71 us  [to_sibling(): return lax.ppermute(value, 'section', [(0, 1), (1, 0)])]
    pallas_call x6 -> x8, Pallas kernels: 7.46 us -> 7.48 us  [call(): pl.pallas_call(kernel, out_shape=[jax.ShapeDtypeStruct(shape, dtype) for...]
  transfers between devices with their start and end apart: 20 -> 21, of which waited for: 12 -> 11; matrix products, arithmetic and copies ran while one was open for 0% -> 0% of each run, Pallas kernels for 5% -> 7%
where the time goes in v14:
time: 59.8 us; the launch traced here: 59.5 us
  starting transfers between devices  23.5 us (39%)
  waiting for transfers between devices  22.7 us (38%)
  Pallas kernels  12.3 us (21%)
  between operations  0.76 us (1%)
    ppermute x6, waiting for transfers between devices, along_z(): return lax.ppermute(value, 'dp', route)  13.5 us
    ppermute x9, starting transfers between devices, along_plane(): return lax.ppermute(value, 'dp', route)  12.2 us
    ppermute x6, starting transfers between devices, along_z(): return lax.ppermute(value, 'dp', route)  9.64 us
    ppermute x9, waiting for transfers between devices, along_plane(): return lax.ppermute(value, 'dp', route)  8.2 us
    pallas_call x8, Pallas kernels, call(): pl.pallas_call(kernel, out_shape=[jax.ShapeDtypeStruct(shape, dtype) for...  7.48 us
    ppermute x6, starting transfers between devices, to_sibling(): return lax.ppermute(value, 'section', [(0, 1), (1, 0)])  1.71 us
    pallas_call x1, Pallas kernels, planar(): pl.pallas_call(functools.partial(blocks_kernel, planes), out_shape=[one_b...  1.69 us
    pallas_call x1, Pallas kernels, planar(): pl.pallas_call(functools.partial(first_kernel, planes), out_shape=[jax.Sh...  1.66 us
  transfers between devices with their start and end apart: 21, of which 11 were waited for; matrix products, arithmetic and copies ran while one was open for 0% of the time, Pallas kernels for 7%

profile of v14, /device:TPU:0, one launch (start us, length us, event | category | flops | bytes accessed | tf_op | source)
XLA Modules:
  0.0 59.5 jit_solution(3090161663415533931)
XLA Ops:
  0.6 0.1 pad_add_fusion.index
  0.7 1.7 %shard_map.77 = (bf16[256,256]{1,0:T(8,128)(2,1)S(1)}, bf16[2,64,1024]{2,1,0:T(8,128)(2,1)S(1)}) custom-call(s32[3]{0:T(128)S(1)} %pad_add_fusion.index, bf16[192,256]{1,0:T(8,128)(2,1)} %bitcast.11, bf16[64,256]{1,0:T(8,128)(2,1)} %bitcast.12, bf16[2,64,4096]{2,1,0:T(8,128)(2,1)} %x_ref.5, bf16[2,64,4096]{2,1,0:T(8,128)(2,1)} %c_ref.5), custom_call_target="tpu_custom_call" | custom-call | tf_op jit(solution)/shard_map/pallas_call | solution.py:416
  2.4 4.0 %collective-permute-start = (bf16[2,64,1024]{2,1,0:T(8,128)(2,1)S(1)}, bf16[2,64,1024]{2,1,0:T(8,128)(2,1)S(1)}, u32[]{:S(2)}, u32[]{:S(2)}) collective-permute-start(bf16[2,64,1024]{2,1,0:T(8,128)(2,1)S(1)} %get-tuple-element.33), channel_id=1, source_target_pairs={{0,3},{1,2},{2,1},{3,0},{4,7},{5,6},{6,5},{7,4},{8,11},{9,10},{10,... | collective-permute-start | bytes 786440 | tf_op jit(solution)/shard_map/ppermute | solution.py:403
  6.4 0.0 copy-start.1
  6.4 2.6 %collective-permute-start.4 = (bf16[256,256]{1,0:T(8,128)(2,1)S(1)}, bf16[256,256]{1,0:T(8,128)(2,1)S(1)}, u32[]{:S(2)}, u32[]{:S(2)}) collective-permute-start(bf16[256,256]{1,0:T(8,128)(2,1)S(1)} %get-tuple-element.34.pack_ref), channel_id=1, source_target_pairs={{0,8},{1,9},{2,10},{3,11},{4,12},{5,13},{6,14},{7,15},{8,0},{9,1},... | collective-permute-start | bytes 393224 | tf_op jit(solution)/shard_map/ppermute | solution.py:396
  8.9 1.6 %collective-permute-start.3 = (bf16[256,256]{1,0:T(8,128)(2,1)S(1)}, bf16[256,256]{1,0:T(8,128)(2,1)S(1)}, u32[]{:S(2)}, u32[]{:S(2)}) collective-permute-start(bf16[256,256]{1,0:T(8,128)(2,1)S(1)} %get-tuple-element.34.pack_ref), channel_id=1, source_target_pairs={{0,4},{1,5},{2,6},{3,7},{4,0},{5,1},{6,2},{7,3},{8,12},{9,13},{10,... | collective-permute-start | bytes 393224 | tf_op jit(solution)/shard_map/ppermute | solution.py:396
  10.5 1.7 %shard_map.79 = (bf16[2,64,1024]{2,1,0:T(8,128)(2,1)S(1)}, bf16[2,64,1024]{2,1,0:T(8,128)(2,1)S(1)}) custom-call(s32[3]{0:T(128)S(1)} %pad_add_fusion.index, bf16[2,64,4096]{2,1,0:T(8,128)(2,1)} %x_ref.5, bf16[2,64,4096]{2,1,0:T(8,128)(2,1)} %c_ref.5), custom_call_target="tpu_custom_call" | custom-call | tf_op jit(solution)/shard_map/pallas_call | solution.py:424
  12.2 0.6 collective-permute-start.1
  12.8 0.5 collective-permute-start.2
  13.3 1.8 %collective-permute-done.4.refs_6_ = bf16[256,256]{1,0:T(8,128)(2,1)S(1)} collective-permute-done((bf16[256,256]{1,0:T(8,128)(2,1)S(1)}, bf16[256,256]{1,0:T(8,128)(2,1)S(1)}, u32[]{:S(2)}, u32[]{:S(2)}) %collective-permute-start.4) | collective-permute-done | bytes 131104 | tf_op jit(solution)/shard_map/ppermute | solution.py:396
  15.1 0.6 collective-permute-start.5
  15.7 0.0 collective-permute-done.3.refs_5_
  15.7 0.0 collective-permute-start.7
  15.7 0.0 copy-done.1
  15.7 0.1 reduce
  15.8 0.0 collective-permute-done.refs_1_
  15.8 1.5 %shard_map.78 = (bf16[272,256]{1,0:T(8,128)(2,1)S(1)}, bf16[2,64,1024]{2,1,0:T(8,128)(2,1)S(1)}) custom-call(s32[3]{0:T(128)S(1)} %pad_add_fusion.index, bf16[256,256]{1,0:T(8,128)(2,1)S(1)} %get-tuple-element.34.pack_ref, bf16[16,256]{1,0:T(8,128)(2,1)S(1)} %reshape_squeeze.3.gain_ref, bf16[2,64,4096]{2,1,0:T(8,128)(2,1)} %x_ref.5, bf16[2,64,4096]{2,1,0:T(8,128)(2,1)} %c_ref.5), custom_call_target="tpu_custom_call" | custom-call | tf_op jit(solution)/shard_map/pallas_call | solution.py:440
  17.3 0.6 collective-permute-start.6
  17.8 2.2 %collective-permute-done.5.refs_7_ = bf16[256,256]{1,0:T(8,128)(2,1)S(1)} collective-permute-done((bf16[256,256]{1,0:T(8,128)(2,1)S(1)}, bf16[256,256]{1,0:T(8,128)(2,1)S(1)}, u32[]{:S(2)}, u32[]{:S(2)}) %collective-permute-start.5) | collective-permute-done | bytes 131104 | tf_op jit(solution)/shard_map/ppermute | solution.py:396
  20.1 0.0 collective-permute-start.9
  20.1 0.0 collective-permute-done.7.refs_9_
  20.1 0.5 collective-permute-start.8
  20.6 0.0 collective-permute-done.1.refs_2_
  20.6 0.0 collective-permute-done.2.refs_3_
  20.6 0.8 %collective-permute-done.9.refs_11_ = bf16[256,256]{1,0:T(8,128)(2,1)S(1)} collective-permute-done((bf16[256,256]{1,0:T(8,128)(2,1)S(1)}, bf16[256,256]{1,0:T(8,128)(2,1)S(1)}, u32[]{:S(2)}, u32[]{:S(2)}) %collective-permute-start.9) | collective-permute-done | bytes 131104 | tf_op jit(solution)/shard_map/ppermute | solution.py:399
  21.4 0.2 collective-permute-done.8.refs_10_
  21.6 0.0 collective-permute-done.6.refs_8_
  21.6 1.6 %shard_map.80 = (bf16[4,64,1024]{2,1,0:T(8,128)(2,1)S(1)}, bf16[4,64,1024]{2,1,0:T(8,128)(2,1)S(1)}, bf16[4,512,256]{2,1,0:T(8,128)(2,1)S(1)}, f32[4,8,256]{2,1,...) custom-call(s32[3]{0:T(128)S(1)} %pad_add_fusion.index, ...), custom_call_target="tpu_custom_call" | custom-call | tf_op jit(solution)/shard_map/pallas_call | solution.py:373
  23.2 0.7 %collective-permute-start.10 = (bf16[64,896]{1,0:T(8,128)(2,1)S(1)}, bf16[64,896]{1,0:T(8,128)(2,1)S(1)}, u32[]{:S(2)}, u32[]{:S(2)}) collective-permute-start(bf16[64,896]{1,0:T(8,128)(2,1)S(1)} %get-tuple-element.41), channel_id=1, source_target_pairs={{0,3},{1,2},{2,1},{3,0},{4,7},{5,6},{6,5},{7,4},{8,11},{9,10},{10,... | collective-permute-start | bytes 344072 | tf_op jit(solution)/shard_map/ppermute | solution.py:403
  23.9 1.3 %collective-permute-start.11 = (bf16[64,896]{1,0:T(8,128)(2,1)S(1)}, bf16[64,896]{1,0:T(8,128)(2,1)S(1)}, u32[]{:S(2)}, u32[]{:S(2)}) collective-permute-start(bf16[64,896]{1,0:T(8,128)(2,1)S(1)} %get-tuple-element.42), channel_id=1, source_target_pairs={{0,2},{1,3},{2,0},{3,1},{4,6},{5,7},{6,4},{7,5},{8,10},{9,11},{10,... | collective-permute-start | bytes 344072 | tf_op jit(solution)/shard_map/ppermute | solution.py:403
  25.3 0.0 copy-start
  25.3 1.5 %collective-permute-start.12 = (bf16[64,896]{1,0:T(8,128)(2,1)S(1)}, bf16[64,896]{1,0:T(8,128)(2,1)S(1)}, u32[]{:S(2)}, u32[]{:S(2)}) collective-permute-start(bf16[64,896]{1,0:T(8,128)(2,1)S(1)} %get-tuple-element.43), channel_id=1, source_target_pairs={{0,1},{1,0},{2,3},{3,2},{4,5},{5,4},{6,7},{7,6},{8,9},{9,8},{10,11... | collective-permute-start | bytes 344072 | tf_op jit(solution)/shard_map/ppermute | solution.py:403
  26.8 3.4 %collective-permute-done.10.refs_0_ = bf16[64,896]{1,0:T(8,128)(2,1)S(1)} collective-permute-done((bf16[64,896]{1,0:T(8,128)(2,1)S(1)}, bf16[64,896]{1,0:T(8,128)(2,1)S(1)}, u32[]{:S(2)}, u32[]{:S(2)}) %collective-permute-start.10) | collective-permute-done | bytes 114720 | tf_op jit(solution)/shard_map/ppermute | solution.py:403
  30.2 1.3 %collective-permute-done.11.refs_1_ = bf16[64,896]{1,0:T(8,128)(2,1)S(1)} collective-permute-done((bf16[64,896]{1,0:T(8,128)(2,1)S(1)}, bf16[64,896]{1,0:T(8,128)(2,1)S(1)}, u32[]{:S(2)}, u32[]{:S(2)}) %collective-permute-start.11) | collective-permute-done | bytes 114720 | tf_op jit(solution)/shard_map/ppermute | solution.py:403
  31.5 0.0 collective-permute-done.12.refs_2_
  31.5 0.0 copy-done
  31.5 2.7 %shard_map.81.refs_0_ = bf16[64,640]{1,0:T(8,128)(2,1)S(1)} custom-call(s32[3]{0:T(128)S(1)} %pad_add_fusion.index, s32[2,1,2]{2,1,0:T(1,128)S(1)} %copy-done, bf16[64,896]{1,0:T(8,128)(2,1)S(1)} %collective-permute-done.10.refs_0_, bf16[64,896]{1,0:T(8,128)(2,1)S(1)} %collective-permute-done.11.refs_1_, ...), custom_call_target="tpu_custom_call" | custom-call | tf_op jit(solution)/shard_map/pallas_call | solution.py:373
  34.2 1.2 %collective-permute-start.15 = (bf16[64,640]{1,0:T(8,128)(2,1)S(1)}, bf16[64,640]{1,0:T(8,128)(2,1)S(1)}, u32[]{:S(2)}, u32[]{:S(2)}) collective-permute-start(bf16[64,640]{1,0:T(8,128)(2,1)S(1)} %shard_map.81.refs_0_), channel_id=1, source_target_pairs={{0,3},{1,2},{2,1},{3,0},{4,7},{5,6},{6,5},{7,4},{8,11},{9,10},{10,... | collective-permute-start | bytes 245768 | tf_op jit(solution)/shard_map/ppermute | solution.py:403
  35.5 1.3 %collective-permute-start.14 = (bf16[64,640]{1,0:T(8,128)(2,1)S(1)}, bf16[64,640]{1,0:T(8,128)(2,1)S(1)}, u32[]{:S(2)}, u32[]{:S(2)}) collective-permute-start(bf16[64,640]{1,0:T(8,128)(2,1)S(1)} %shard_map.81.refs_0_), channel_id=1, source_target_pairs={{0,2},{1,3},{2,0},{3,1},{4,6},{5,7},{6,4},{7,5},{8,10},{9,11},{10,... | collective-permute-start | bytes 245768 | tf_op jit(solution)/shard_map/ppermute | solution.py:403
  36.8 1.0 %collective-permute-start.13 = (bf16[64,640]{1,0:T(8,128)(2,1)S(1)}, bf16[64,640]{1,0:T(8,128)(2,1)S(1)}, u32[]{:S(2)}, u32[]{:S(2)}) collective-permute-start(bf16[64,640]{1,0:T(8,128)(2,1)S(1)} %shard_map.81.refs_0_), channel_id=1, source_target_pairs={{0,1},{1,0},{2,3},{3,2},{4,5},{5,4},{6,7},{7,6},{8,9},{9,8},{10,11... | collective-permute-start | bytes 245768 | tf_op jit(solution)/shard_map/ppermute | solution.py:403
  37.8 2.5 %collective-permute-done.15.refs_3_ = bf16[64,640]{1,0:T(8,128)(2,1)S(1)} collective-permute-done((bf16[64,640]{1,0:T(8,128)(2,1)S(1)}, bf16[64,640]{1,0:T(8,128)(2,1)S(1)}, u32[]{:S(2)}, u32[]{:S(2)}) %collective-permute-start.15) | collective-permute-done | bytes 81952 | tf_op jit(solution)/shard_map/ppermute | solution.py:403
  40.3 0.5 collective-permute-done.14.refs_2_
  40.8 0.5 collective-permute-done.13.refs_1_
  41.3 1.3 %shard_map.82 = (f32[2,256,256]{2,1,0:T(8,128)S(1)}, bf16[2,256,256]{2,1,0:T(8,128)(2,1)S(1)}, bf16[640,256]{1,0:T(8,128)(2,1)S(1)}, bf16[256,64]{1,0:T(8,128)(2,1)S(1)}, bf16[64,192]{1,0:T(8,128)(2,1)S(1)}) custom-call(s32[3]{0:T(128)S(1)} %pad_add_fusion.index, bf16[64,640]{1,0:T(8,128)(2,1)S(1)} %shard_map.81.refs_0_, ...), custom_call_target="tpu_custom_call" | custom-call | tf_op jit(solution)/shard_map/pallas_call | solution.py:373
  42.5 0.1 collective-permute-start.18
  42.6 1.0 %shard_map.83 = (f32[2,256,256]{2,1,0:T(8,128)S(1)}, bf16[2,256,256]{2,1,0:T(8,128)(2,1)S(1)}) custom-call(s32[3]{0:T(128)S(1)} %pad_add_fusion.index, bf16[640,256]{1,0:T(8,128)(2,1)S(1)} %get-tuple-element.49.turned_ref, bf16[256,64]{1,0:T(8,128)(2,1)S(1)} %get-tuple-element.50.small_ref, bf16[64,192]{1,0:T(8,128)(2,1)S(1)} %get-tuple-element.51.small_t_ref, ...), custom_call_target="tpu_custom_call" | custom-call | tf_op jit(solution)/shard_map/pallas_call | solution.py:373
  43.7 0.6 collective-permute-start.16
  44.2 0.0 collective-permute-done.18.come_ref
  44.2 0.1 shard_map.85
  44.3 1.1 %collective-permute-start.19 = (bf16[256,256]{1,0:T(8,128)(2,1)S(1)}, bf16[256,256]{1,0:T(8,128)(2,1)S(1)}, u32[]{:S(2)}, u32[]{:S(2)}) collective-permute-start(bf16[256,256]{1,0:T(8,128)(2,1)S(1)} %get-tuple-element.59), channel_id=1, source_target_pairs={{0,4},{1,5},{2,6},{3,7},{4,0},{5,1},{6,2},{7,3},{8,12},{9,13},{10,... | collective-permute-start | bytes 393224 | tf_op jit(solution)/shard_map/ppermute | solution.py:396
  45.4 0.0 collective-permute-done.16.come_ref
  45.4 0.1 shard_map.84
  45.4 1.1 %collective-permute-start.17 = (bf16[256,256]{1,0:T(8,128)(2,1)S(1)}, bf16[256,256]{1,0:T(8,128)(2,1)S(1)}, u32[]{:S(2)}, u32[]{:S(2)}) collective-permute-start(bf16[256,256]{1,0:T(8,128)(2,1)S(1)} %get-tuple-element.55), channel_id=1, source_target_pairs={{0,4},{1,5},{2,6},{3,7},{4,0},{5,1},{6,2},{7,3},{8,12},{9,13},{10,... | collective-permute-start | bytes 393224 | tf_op jit(solution)/shard_map/ppermute | solution.py:396
  46.5 4.2 %collective-permute-done.19.b_ref = bf16[256,256]{1,0:T(8,128)(2,1)S(1)} collective-permute-done((bf16[256,256]{1,0:T(8,128)(2,1)S(1)}, bf16[256,256]{1,0:T(8,128)(2,1)S(1)}, u32[]{:S(2)}, u32[]{:S(2)}) %collective-permute-start.19) | collective-permute-done | bytes 131104 | tf_op jit(solution)/shard_map/ppermute | solution.py:396
  50.7 2.7 %collective-permute-start.20 = (bf16[256,256]{1,0:T(8,128)(2,1)S(1)}, bf16[256,256]{1,0:T(8,128)(2,1)S(1)}, u32[]{:S(2)}, u32[]{:S(2)}) collective-permute-start(bf16[256,256]{1,0:T(8,128)(2,1)S(1)} %shard_map.86), channel_id=1, source_target_pairs={{0,8},{1,9},{2,10},{3,11},{4,12},{5,13},{6,14},{7,15},{8,0},{9,1},... | collective-permute-start | bytes 393224 | tf_op jit(solution)/shard_map/ppermute | solution.py:396
  53.5 0.0 collective-permute-done.17.refs_0_
  53.5 5.3 %collective-permute-done.20.refs_1_ = bf16[256,256]{1,0:T(8,128)(2,1)S(1)} collective-permute-done((bf16[256,256]{1,0:T(8,128)(2,1)S(1)}, bf16[256,256]{1,0:T(8,128)(2,1)S(1)}, u32[]{:S(2)}, u32[]{:S(2)}) %collective-permute-start.20) | collective-permute-done | bytes 131104 | tf_op jit(solution)/shard_map/ppermute | solution.py:396
  58.8 0.7 %shard_map.87 = (f32[192,256]{1,0:T(8,128)}, f32[64,256]{1,0:T(8,128)}) custom-call(f32[256,256]{1,0:T(8,128)S(1)} %get-tuple-element.54.keep_ref, bf16[256,256]{1,0:T(8,128)(2,1)S(1)} %collective-permute-done.17.refs_0_, bf16[256,256]{1,0:T(8,128)(2,1)S(1)} %collective-permute-done.20.refs_1_), custom_call_target="tpu_custom_call" | custom-call | tf_op jit(solution)/shard_map/pallas_call | solution.py:373
  (2 shorter events, 0.0 us)
Async XLA Ops:
  2.4 13.4 %collective-permute-start = (bf16[2,64,1024]{2,1,0:T(8,128)(2,1)S(1)}, bf16[2,64,1024]{2,1,0:T(8,128)(2,1)S(1)}, u32[]{:S(2)}, u32[]{:S(2)}) collective-permute-start(bf16[2,64,1024]{2,1,0:T(8,128)(2,1)S(1)} %get-tuple-element.33), channel_id=1, source_target_pairs={{0,3},{1,2},{2,1},{3,0},{4,7},{5,6},{6,5},{7,4},{8,11},{9,10},{10,... | collective-permute-start | bytes 786440 | tf_op jit(solution)/shard_map/ppermute | solution.py:403
  6.4 9.3 %copy-start.1 = (bf16[1,4096]{1,0:T(2,128)(2,1)S(1)}, bf16[1,4096]{1,0:T(2,128)(2,1)}, u32[]{:S(2)}) copy-start(bf16[1,4096]{1,0:T(2,128)(2,1)} %param.9) | copy-start | bytes 24580
  6.4 8.8 %collective-permute-start.4 = (bf16[256,256]{1,0:T(8,128)(2,1)S(1)}, bf16[256,256]{1,0:T(8,128)(2,1)S(1)}, u32[]{:S(2)}, u32[]{:S(2)}) collective-permute-start(bf16[256,256]{1,0:T(8,128)(2,1)S(1)} %get-tuple-element.34.pack_ref), channel_id=1, source_target_pairs={{0,8},{1,9},{2,10},{3,11},{4,12},{5,13},{6,14},{7,15},{8,0},{9,1},... | collective-permute-start | bytes 393224 | tf_op jit(solution)/shard_map/ppermute | solution.py:396
  8.9 6.8 %collective-permute-start.3 = (bf16[256,256]{1,0:T(8,128)(2,1)S(1)}, bf16[256,256]{1,0:T(8,128)(2,1)S(1)}, u32[]{:S(2)}, u32[]{:S(2)}) collective-permute-start(bf16[256,256]{1,0:T(8,128)(2,1)S(1)} %get-tuple-element.34.pack_ref), channel_id=1, source_target_pairs={{0,4},{1,5},{2,6},{3,7},{4,0},{5,1},{6,2},{7,3},{8,12},{9,13},{10,... | collective-permute-start | bytes 393224 | tf_op jit(solution)/shard_map/ppermute | solution.py:396
  12.2 8.4 %collective-permute-start.1 = (bf16[2,64,1024]{2,1,0:T(8,128)(2,1)S(1)}, bf16[2,64,1024]{2,1,0:T(8,128)(2,1)S(1)}, u32[]{:S(2)}, u32[]{:S(2)}) collective-permute-start(bf16[2,64,1024]{2,1,0:T(8,128)(2,1)S(1)} %get-tuple-element.37), channel_id=1, source_target_pairs={{0,2},{1,3},{2,0},{3,1},{4,6},{5,7},{6,4},{7,5},{8,10},{9,11},{10,... | collective-permute-start | bytes 786440 | tf_op jit(solution)/shard_map/ppermute | solution.py:403
  12.8 7.8 %collective-permute-start.2 = (bf16[2,64,1024]{2,1,0:T(8,128)(2,1)S(1)}, bf16[2,64,1024]{2,1,0:T(8,128)(2,1)S(1)}, u32[]{:S(2)}, u32[]{:S(2)}) collective-permute-start(bf16[2,64,1024]{2,1,0:T(8,128)(2,1)S(1)} %get-tuple-element.38), channel_id=1, source_target_pairs={{0,1},{1,0},{2,3},{3,2},{4,5},{5,4},{6,7},{7,6},{8,9},{9,8},{10,11... | collective-permute-start | bytes 786440 | tf_op jit(solution)/shard_map/ppermute | solution.py:403
  15.1 5.0 %collective-permute-start.5 = (bf16[256,256]{1,0:T(8,128)(2,1)S(1)}, bf16[256,256]{1,0:T(8,128)(2,1)S(1)}, u32[]{:S(2)}, u32[]{:S(2)}) collective-permute-start(bf16[256,256]{1,0:T(8,128)(2,1)S(1)} %collective-permute-done.4.refs_6_), channel_id=1, source_target_pairs={{0,4},{1,5},{2,6},{3,7},{4,0},{5,1},{6,2},{7,3},{8,12},{9,13},{10,... | collective-permute-start | bytes 393224 | tf_op jit(solution)/shard_map/ppermute | solution.py:396
  15.7 4.4 %collective-permute-start.7 = (bf16[256,256]{1,0:T(8,128)(2,1)S(1)}, bf16[256,256]{1,0:T(8,128)(2,1)S(1)}, u32[]{:S(2)}, u32[]{:S(2)}) collective-permute-start(bf16[256,256]{1,0:T(8,128)(2,1)S(1)} %collective-permute-done.3.refs_5_), channel_id=1, source_target_pairs={{0,16},{16,0},{1,17},{17,1},{2,18},{18,2},{3,19},{19,3},{4,20},{20... | collective-permute-start | bytes 393224 | tf_op jit(solution)/shard_map/ppermute | solution.py:399
  17.3 4.3 %collective-permute-start.6 = (bf16[272,256]{1,0:T(8,128)(2,1)S(1)}, bf16[272,256]{1,0:T(8,128)(2,1)S(1)}, u32[]{:S(2)}, u32[]{:S(2)}) collective-permute-start(bf16[272,256]{1,0:T(8,128)(2,1)S(1)} %get-tuple-element.39.refs_4_), channel_id=1, source_target_pairs={{0,16},{16,0},{1,17},{17,1},{2,18},{18,2},{3,19},{19,3},{4,20},{20... | collective-permute-start | bytes 417800 | tf_op jit(solution)/shard_map/ppermute | solution.py:399
  20.1 1.3 %collective-permute-start.9 = (bf16[256,256]{1,0:T(8,128)(2,1)S(1)}, bf16[256,256]{1,0:T(8,128)(2,1)S(1)}, u32[]{:S(2)}, u32[]{:S(2)}) collective-permute-start(bf16[256,256]{1,0:T(8,128)(2,1)S(1)} %collective-permute-done.5.refs_7_), channel_id=1, source_target_pairs={{0,16},{16,0},{1,17},{17,1},{2,18},{18,2},{3,19},{19,3},{4,20},{20... | collective-permute-start | bytes 393224 | tf_op jit(solution)/shard_map/ppermute | solution.py:399
  20.1 1.5 %collective-permute-start.8 = (bf16[256,256]{1,0:T(8,128)(2,1)S(1)}, bf16[256,256]{1,0:T(8,128)(2,1)S(1)}, u32[]{:S(2)}, u32[]{:S(2)}) collective-permute-start(bf16[256,256]{1,0:T(8,128)(2,1)S(1)} %collective-permute-done.4.refs_6_), channel_id=1, source_target_pairs={{0,16},{16,0},{1,17},{17,1},{2,18},{18,2},{3,19},{19,3},{4,20},{20... | collective-permute-start | bytes 393224 | tf_op jit(solution)/shard_map/ppermute | solution.py:399
  23.2 7.0 %collective-permute-start.10 = (bf16[64,896]{1,0:T(8,128)(2,1)S(1)}, bf16[64,896]{1,0:T(8,128)(2,1)S(1)}, u32[]{:S(2)}, u32[]{:S(2)}) collective-permute-start(bf16[64,896]{1,0:T(8,128)(2,1)S(1)} %get-tuple-element.41), channel_id=1, source_target_pairs={{0,3},{1,2},{2,1},{3,0},{4,7},{5,6},{6,5},{7,4},{8,11},{9,10},{10,... | collective-permute-start | bytes 344072 | tf_op jit(solution)/shard_map/ppermute | solution.py:403
  23.9 7.6 %collective-permute-start.11 = (bf16[64,896]{1,0:T(8,128)(2,1)S(1)}, bf16[64,896]{1,0:T(8,128)(2,1)S(1)}, u32[]{:S(2)}, u32[]{:S(2)}) collective-permute-start(bf16[64,896]{1,0:T(8,128)(2,1)S(1)} %get-tuple-element.42), channel_id=1, source_target_pairs={{0,2},{1,3},{2,0},{3,1},{4,6},{5,7},{6,4},{7,5},{8,10},{9,11},{10,... | collective-permute-start | bytes 344072 | tf_op jit(solution)/shard_map/ppermute | solution.py:403
  25.3 6.2 %copy-start = (s32[2,1,2]{2,1,0:T(1,128)S(1)}, s32[2,1,2]{2,1,0:T(1,128)}, u32[]{:S(2)}) copy-start(s32[2,1,2]{2,1,0:T(1,128)} %docs.1) | copy-start | bytes 52
  25.3 6.2 %collective-permute-start.12 = (bf16[64,896]{1,0:T(8,128)(2,1)S(1)}, bf16[64,896]{1,0:T(8,128)(2,1)S(1)}, u32[]{:S(2)}, u32[]{:S(2)}) collective-permute-start(bf16[64,896]{1,0:T(8,128)(2,1)S(1)} %get-tuple-element.43), channel_id=1, source_target_pairs={{0,1},{1,0},{2,3},{3,2},{4,5},{5,4},{6,7},{7,6},{8,9},{9,8},{10,11... | collective-permute-start | bytes 344072 | tf_op jit(solution)/shard_map/ppermute | solution.py:403
  34.2 6.0 %collective-permute-start.15 = (bf16[64,640]{1,0:T(8,128)(2,1)S(1)}, bf16[64,640]{1,0:T(8,128)(2,1)S(1)}, u32[]{:S(2)}, u32[]{:S(2)}) collective-permute-start(bf16[64,640]{1,0:T(8,128)(2,1)S(1)} %shard_map.81.refs_0_), channel_id=1, source_target_pairs={{0,3},{1,2},{2,1},{3,0},{4,7},{5,6},{6,5},{7,4},{8,11},{9,10},{10,... | collective-permute-start | bytes 245768 | tf_op jit(solution)/shard_map/ppermute | solution.py:403
  35.5 5.3 %collective-permute-start.14 = (bf16[64,640]{1,0:T(8,128)(2,1)S(1)}, bf16[64,640]{1,0:T(8,128)(2,1)S(1)}, u32[]{:S(2)}, u32[]{:S(2)}) collective-permute-start(bf16[64,640]{1,0:T(8,128)(2,1)S(1)} %shard_map.81.refs_0_), channel_id=1, source_target_pairs={{0,2},{1,3},{2,0},{3,1},{4,6},{5,7},{6,4},{7,5},{8,10},{9,11},{10,... | collective-permute-start | bytes 245768 | tf_op jit(solution)/shard_map/ppermute | solution.py:403
  36.8 4.4 %collective-permute-start.13 = (bf16[64,640]{1,0:T(8,128)(2,1)S(1)}, bf16[64,640]{1,0:T(8,128)(2,1)S(1)}, u32[]{:S(2)}, u32[]{:S(2)}) collective-permute-start(bf16[64,640]{1,0:T(8,128)(2,1)S(1)} %shard_map.81.refs_0_), channel_id=1, source_target_pairs={{0,1},{1,0},{2,3},{3,2},{4,5},{5,4},{6,7},{7,6},{8,9},{9,8},{10,11... | collective-permute-start | bytes 245768 | tf_op jit(solution)/shard_map/ppermute | solution.py:403
  42.5 1.7 %collective-permute-start.18 = (bf16[2,256,256]{2,1,0:T(8,128)(2,1)S(1)}, bf16[2,256,256]{2,1,0:T(8,128)(2,1)S(1)}, u32[]{:S(2)}, u32[]{:S(2)}) collective-permute-start(bf16[2,256,256]{2,1,0:T(8,128)(2,1)S(1)} %get-tuple-element.57), channel_id=1, source_target_pairs={{0,16},{16,0},{1,17},{17,1},{2,18},{18,2},{3,19},{19,3},{4,20},{20... | collective-permute-start | bytes 786440 | tf_op jit(solution)/shard_map/ppermute | solution.py:399
  43.7 1.7 %collective-permute-start.16 = (bf16[2,256,256]{2,1,0:T(8,128)(2,1)S(1)}, bf16[2,256,256]{2,1,0:T(8,128)(2,1)S(1)}, u32[]{:S(2)}, u32[]{:S(2)}) collective-permute-start(bf16[2,256,256]{2,1,0:T(8,128)(2,1)S(1)} %get-tuple-element.53), channel_id=1, source_target_pairs={{0,16},{16,0},{1,17},{17,1},{2,18},{18,2},{3,19},{19,3},{4,20},{20... | collective-permute-start | bytes 786440 | tf_op jit(solution)/shard_map/ppermute | solution.py:399
  44.3 6.4 %collective-permute-start.19 = (bf16[256,256]{1,0:T(8,128)(2,1)S(1)}, bf16[256,256]{1,0:T(8,128)(2,1)S(1)}, u32[]{:S(2)}, u32[]{:S(2)}) collective-permute-start(bf16[256,256]{1,0:T(8,128)(2,1)S(1)} %get-tuple-element.59), channel_id=1, source_target_pairs={{0,4},{1,5},{2,6},{3,7},{4,0},{5,1},{6,2},{7,3},{8,12},{9,13},{10,... | collective-permute-start | bytes 393224 | tf_op jit(solution)/shard_map/ppermute | solution.py:396
  45.4 8.0 %collective-permute-start.17 = (bf16[256,256]{1,0:T(8,128)(2,1)S(1)}, bf16[256,256]{1,0:T(8,128)(2,1)S(1)}, u32[]{:S(2)}, u32[]{:S(2)}) collective-permute-start(bf16[256,256]{1,0:T(8,128)(2,1)S(1)} %get-tuple-element.55), channel_id=1, source_target_pairs={{0,4},{1,5},{2,6},{3,7},{4,0},{5,1},{6,2},{7,3},{8,12},{9,13},{10,... | collective-permute-start | bytes 393224 | tf_op jit(solution)/shard_map/ppermute | solution.py:396
  50.7 8.0 %collective-permute-start.20 = (bf16[256,256]{1,0:T(8,128)(2,1)S(1)}, bf16[256,256]{1,0:T(8,128)(2,1)S(1)}, u32[]{:S(2)}, u32[]{:S(2)}) collective-permute-start(bf16[256,256]{1,0:T(8,128)(2,1)S(1)} %shard_map.86), channel_id=1, source_target_pairs={{0,8},{1,9},{2,10},{3,11},{4,12},{5,13},{6,14},{7,15},{8,0},{9,1},... | collective-permute-start | bytes 393224 | tf_op jit(solution)/shard_map/ppermute | solution.py:396

commit v15 on v14

--- a/solution.py
+++ b/solution.py
@@ -348,6 +348,10 @@
         out_ref[...] = (keep_ref[i] + come_ref[i].astype(F32)).astype(out_ref.dtype)
 
 
+def wide_add_kernel(a_ref, b_ref, out_ref):
+    out_ref[...] = a_ref[...] + b_ref[...].astype(F32)
+
+
 def add_kernel(a_ref, b_ref, out_ref):
     out_ref[...] = (a_ref[...].astype(F32) + b_ref[...].astype(F32)).astype(BF16)
 
@@ -486,15 +490,21 @@
     )
     pieces.update(swap_and_merge(near_order, keep, send))
     kept, parts = pieces[0], []
+    held = []
     for step in [1 << bit for bit in range(planes.bit_length() - 1)]:
-        got = {k ^ step: along_z(pieces.pop(k), step) for k in sorted(pieces, reverse=True) if k & step}
-        parts.append(got.pop(0))
+        got = {k ^ step: along_z(pieces.pop(k), step) for k in sorted(pieces, reverse=True) if k & step and k != step}
+        if step in pieces:
+            held.append((pieces.pop(step), step))
         for k, part in got.items():
             (pieces[k],) = call(add_kernel, [(piece, BF16)], pieces[k], part)
+            held = [(lax.optimization_barrier((value, pieces[k]))[0], at) for value, at in held]
+    parts = [along_z(value, at) for value, at in reversed(held)]
+    for part in parts[:-1]:
+        (kept,) = call(wide_add_kernel, [(piece, F32)], kept, part)
     grad_qkv, grad_out = call(
         functools.partial(last_kernel, qkv_rows),
         [((qkv_rows, width), F32), ((heads, width), F32)],
-        kept, *parts,
+        kept, *parts[-1:],
     )
     return (grad_qkv.T[None], grad_out[None])
 

time: 59.8 us -> 59.7 us (level)
  starting transfers between devices: 23.5 us -> 24.2 us
  waiting for transfers between devices: 22.7 us -> 22 us
    ppermute x6, waiting for transfers between devices: 13.5 us -> 12.8 us  [along_z(): return lax.ppermute(value, 'dp', route)]
    ppermute x6, starting transfers between devices: 9.64 us -> 10.3 us  [along_z(): return lax.ppermute(value, 'dp', route)]
    pallas_call x8 -> x9, Pallas kernels: 7.48 us -> 7.5 us  [call(): pl.pallas_call(kernel, out_shape=[jax.ShapeDtypeStruct(shape, dtype) for...]
  transfers between devices with their start and end apart: 21 -> 21, of which waited for: 11 -> 12; matrix products, arithmetic and copies ran while one was open for 0% -> 0% of each run, Pallas kernels for 7% -> 7%
where the time goes in v15:
time: 59.7 us; the launch traced here: 59.4 us
  starting transfers between devices  24.2 us (41%)
  waiting for transfers between devices  22 us (37%)
  Pallas kernels  12.3 us (21%)
  between operations  0.76 us (1%)
    ppermute x6, waiting for transfers between devices, along_z(): return lax.ppermute(value, 'dp', route)  12.8 us
    ppermute x9, starting transfers between devices, along_plane(): return lax.ppermute(value, 'dp', route)  12.2 us
    ppermute x6, starting transfers between devices, along_z(): return lax.ppermute(value, 'dp', route)  10.3 us
    ppermute x9, waiting for transfers between devices, along_plane(): return lax.ppermute(value, 'dp', route)  8.2 us
    pallas_call x9, Pallas kernels, call(): pl.pallas_call(kernel, out_shape=[jax.ShapeDtypeStruct(shape, dtype) for...  7.5 us
    ppermute x6, starting transfers between devices, to_sibling(): return lax.ppermute(value, 'section', [(0, 1), (1, 0)])  1.71 us
    pallas_call x1, Pallas kernels, planar(): pl.pallas_call(functools.partial(blocks_kernel, planes), out_shape=[one_b...  1.69 us
    pallas_call x1, Pallas kernels, planar(): pl.pallas_call(functools.partial(first_kernel, planes), out_shape=[jax.Sh...  1.66 us
  transfers between devices with their start and end apart: 21, of which 12 were waited for; matrix products, arithmetic and copies ran while one was open for 0% of the time, Pallas kernels for 7%

profile of v15, /device:TPU:0, one launch (start us, length us, event | category | flops | bytes accessed | tf_op | source)
XLA Modules:
  0.0 59.4 jit_solution(15494951298315740501)
XLA Ops:
  0.6 0.1 pad_add_fusion.index
  0.7 1.7 %shard_map.77 = (bf16[256,256]{1,0:T(8,128)(2,1)S(1)}, bf16[2,64,1024]{2,1,0:T(8,128)(2,1)S(1)}) custom-call(s32[3]{0:T(128)S(1)} %pad_add_fusion.index, bf16[192,256]{1,0:T(8,128)(2,1)} %bitcast.11, bf16[64,256]{1,0:T(8,128)(2,1)} %bitcast.12, bf16[2,64,4096]{2,1,0:T(8,128)(2,1)} %x_ref.5, bf16[2,64,4096]{2,1,0:T(8,128)(2,1)} %c_ref.5), custom_call_target="tpu_custom_call" | custom-call | tf_op jit(solution)/shard_map/pallas_call | solution.py:420
  2.4 4.0 %collective-permute-start = (bf16[2,64,1024]{2,1,0:T(8,128)(2,1)S(1)}, bf16[2,64,1024]{2,1,0:T(8,128)(2,1)S(1)}, u32[]{:S(2)}, u32[]{:S(2)}) collective-permute-start(bf16[2,64,1024]{2,1,0:T(8,128)(2,1)S(1)} %get-tuple-element.34), channel_id=1, source_target_pairs={{0,3},{1,2},{2,1},{3,0},{4,7},{5,6},{6,5},{7,4},{8,11},{9,10},{10,... | collective-permute-start | bytes 786440 | tf_op jit(solution)/shard_map/ppermute | solution.py:407
  6.4 0.0 copy-start.1
  6.4 2.6 %collective-permute-start.4 = (bf16[256,256]{1,0:T(8,128)(2,1)S(1)}, bf16[256,256]{1,0:T(8,128)(2,1)S(1)}, u32[]{:S(2)}, u32[]{:S(2)}) collective-permute-start(bf16[256,256]{1,0:T(8,128)(2,1)S(1)} %get-tuple-element.35.pack_ref), channel_id=1, source_target_pairs={{0,8},{1,9},{2,10},{3,11},{4,12},{5,13},{6,14},{7,15},{8,0},{9,1},... | collective-permute-start | bytes 393224 | tf_op jit(solution)/shard_map/ppermute | solution.py:400
  8.9 1.6 %collective-permute-start.3 = (bf16[256,256]{1,0:T(8,128)(2,1)S(1)}, bf16[256,256]{1,0:T(8,128)(2,1)S(1)}, u32[]{:S(2)}, u32[]{:S(2)}) collective-permute-start(bf16[256,256]{1,0:T(8,128)(2,1)S(1)} %get-tuple-element.35.pack_ref), channel_id=1, source_target_pairs={{0,4},{1,5},{2,6},{3,7},{4,0},{5,1},{6,2},{7,3},{8,12},{9,13},{10,... | collective-permute-start | bytes 393224 | tf_op jit(solution)/shard_map/ppermute | solution.py:400
  10.5 1.7 %shard_map.79 = (bf16[2,64,1024]{2,1,0:T(8,128)(2,1)S(1)}, bf16[2,64,1024]{2,1,0:T(8,128)(2,1)S(1)}) custom-call(s32[3]{0:T(128)S(1)} %pad_add_fusion.index, bf16[2,64,4096]{2,1,0:T(8,128)(2,1)} %x_ref.5, bf16[2,64,4096]{2,1,0:T(8,128)(2,1)} %c_ref.5), custom_call_target="tpu_custom_call" | custom-call | tf_op jit(solution)/shard_map/pallas_call | solution.py:428
  12.2 0.6 collective-permute-start.1
  12.8 0.5 collective-permute-start.2
  13.3 1.8 %collective-permute-done.4.refs_6_ = bf16[256,256]{1,0:T(8,128)(2,1)S(1)} collective-permute-done((bf16[256,256]{1,0:T(8,128)(2,1)S(1)}, bf16[256,256]{1,0:T(8,128)(2,1)S(1)}, u32[]{:S(2)}, u32[]{:S(2)}) %collective-permute-start.4) | collective-permute-done | bytes 131104 | tf_op jit(solution)/shard_map/ppermute | solution.py:400
  15.1 0.6 collective-permute-start.5
  15.7 0.0 collective-permute-done.3.refs_5_
  15.7 0.0 collective-permute-start.7
  15.7 0.0 copy-done.1
  15.7 0.1 reduce
  15.8 0.0 collective-permute-done.refs_1_
  15.8 1.5 %shard_map.78 = (bf16[272,256]{1,0:T(8,128)(2,1)S(1)}, bf16[2,64,1024]{2,1,0:T(8,128)(2,1)S(1)}) custom-call(s32[3]{0:T(128)S(1)} %pad_add_fusion.index, bf16[256,256]{1,0:T(8,128)(2,1)S(1)} %get-tuple-element.35.pack_ref, bf16[16,256]{1,0:T(8,128)(2,1)S(1)} %reshape_squeeze.3.gain_ref, bf16[2,64,4096]{2,1,0:T(8,128)(2,1)} %x_ref.5, bf16[2,64,4096]{2,1,0:T(8,128)(2,1)} %c_ref.5), custom_call_target="tpu_custom_call" | custom-call | tf_op jit(solution)/shard_map/pallas_call | solution.py:444
  17.3 0.6 collective-permute-start.6
  17.8 2.2 %collective-permute-done.5.refs_7_ = bf16[256,256]{1,0:T(8,128)(2,1)S(1)} collective-permute-done((bf16[256,256]{1,0:T(8,128)(2,1)S(1)}, bf16[256,256]{1,0:T(8,128)(2,1)S(1)}, u32[]{:S(2)}, u32[]{:S(2)}) %collective-permute-start.5) | collective-permute-done | bytes 131104 | tf_op jit(solution)/shard_map/ppermute | solution.py:400
  20.1 0.0 collective-permute-start.9
  20.1 0.0 collective-permute-done.7.refs_9_
  20.1 0.5 collective-permute-start.8
  20.6 0.0 collective-permute-done.1.refs_2_
  20.6 0.0 collective-permute-done.2.refs_3_
  20.6 0.8 %collective-permute-done.9.refs_11_ = bf16[256,256]{1,0:T(8,128)(2,1)S(1)} collective-permute-done((bf16[256,256]{1,0:T(8,128)(2,1)S(1)}, bf16[256,256]{1,0:T(8,128)(2,1)S(1)}, u32[]{:S(2)}, u32[]{:S(2)}) %collective-permute-start.9) | collective-permute-done | bytes 131104 | tf_op jit(solution)/shard_map/ppermute | solution.py:403
  21.4 0.2 collective-permute-done.8.refs_10_
  21.6 0.0 collective-permute-done.6.refs_8_
  21.6 1.6 %shard_map.80 = (bf16[4,64,1024]{2,1,0:T(8,128)(2,1)S(1)}, bf16[4,64,1024]{2,1,0:T(8,128)(2,1)S(1)}, bf16[4,512,256]{2,1,0:T(8,128)(2,1)S(1)}, f32[4,8,256]{2,1,...) custom-call(s32[3]{0:T(128)S(1)} %pad_add_fusion.index, ...), custom_call_target="tpu_custom_call" | custom-call | tf_op jit(solution)/shard_map/pallas_call | solution.py:377
  23.2 0.7 %collective-permute-start.10 = (bf16[64,896]{1,0:T(8,128)(2,1)S(1)}, bf16[64,896]{1,0:T(8,128)(2,1)S(1)}, u32[]{:S(2)}, u32[]{:S(2)}) collective-permute-start(bf16[64,896]{1,0:T(8,128)(2,1)S(1)} %get-tuple-element.42), channel_id=1, source_target_pairs={{0,3},{1,2},{2,1},{3,0},{4,7},{5,6},{6,5},{7,4},{8,11},{9,10},{10,... | collective-permute-start | bytes 344072 | tf_op jit(solution)/shard_map/ppermute | solution.py:407
  23.9 1.3 %collective-permute-start.11 = (bf16[64,896]{1,0:T(8,128)(2,1)S(1)}, bf16[64,896]{1,0:T(8,128)(2,1)S(1)}, u32[]{:S(2)}, u32[]{:S(2)}) collective-permute-start(bf16[64,896]{1,0:T(8,128)(2,1)S(1)} %get-tuple-element.43), channel_id=1, source_target_pairs={{0,2},{1,3},{2,0},{3,1},{4,6},{5,7},{6,4},{7,5},{8,10},{9,11},{10,... | collective-permute-start | bytes 344072 | tf_op jit(solution)/shard_map/ppermute | solution.py:407
  25.3 0.0 copy-start
  25.3 1.5 %collective-permute-start.12 = (bf16[64,896]{1,0:T(8,128)(2,1)S(1)}, bf16[64,896]{1,0:T(8,128)(2,1)S(1)}, u32[]{:S(2)}, u32[]{:S(2)}) collective-permute-start(bf16[64,896]{1,0:T(8,128)(2,1)S(1)} %get-tuple-element.44), channel_id=1, source_target_pairs={{0,1},{1,0},{2,3},{3,2},{4,5},{5,4},{6,7},{7,6},{8,9},{9,8},{10,11... | collective-permute-start | bytes 344072 | tf_op jit(solution)/shard_map/ppermute | solution.py:407
  26.8 3.4 %collective-permute-done.10.refs_0_ = bf16[64,896]{1,0:T(8,128)(2,1)S(1)} collective-permute-done((bf16[64,896]{1,0:T(8,128)(2,1)S(1)}, bf16[64,896]{1,0:T(8,128)(2,1)S(1)}, u32[]{:S(2)}, u32[]{:S(2)}) %collective-permute-start.10) | collective-permute-done | bytes 114720 | tf_op jit(solution)/shard_map/ppermute | solution.py:407
  30.2 1.3 %collective-permute-done.11.refs_1_ = bf16[64,896]{1,0:T(8,128)(2,1)S(1)} collective-permute-done((bf16[64,896]{1,0:T(8,128)(2,1)S(1)}, bf16[64,896]{1,0:T(8,128)(2,1)S(1)}, u32[]{:S(2)}, u32[]{:S(2)}) %collective-permute-start.11) | collective-permute-done | bytes 114720 | tf_op jit(solution)/shard_map/ppermute | solution.py:407
  31.5 0.0 collective-permute-done.12.refs_2_
  31.5 0.0 copy-done
  31.5 2.7 %shard_map.81.refs_0_ = bf16[64,640]{1,0:T(8,128)(2,1)S(1)} custom-call(s32[3]{0:T(128)S(1)} %pad_add_fusion.index, s32[2,1,2]{2,1,0:T(1,128)S(1)} %copy-done, bf16[64,896]{1,0:T(8,128)(2,1)S(1)} %collective-permute-done.10.refs_0_, bf16[64,896]{1,0:T(8,128)(2,1)S(1)} %collective-permute-done.11.refs_1_, ...), custom_call_target="tpu_custom_call" | custom-call | tf_op jit(solution)/shard_map/pallas_call | solution.py:377
  34.2 1.2 %collective-permute-start.15 = (bf16[64,640]{1,0:T(8,128)(2,1)S(1)}, bf16[64,640]{1,0:T(8,128)(2,1)S(1)}, u32[]{:S(2)}, u32[]{:S(2)}) collective-permute-start(bf16[64,640]{1,0:T(8,128)(2,1)S(1)} %shard_map.81.refs_0_), channel_id=1, source_target_pairs={{0,3},{1,2},{2,1},{3,0},{4,7},{5,6},{6,5},{7,4},{8,11},{9,10},{10,... | collective-permute-start | bytes 245768 | tf_op jit(solution)/shard_map/ppermute | solution.py:407
  35.5 1.3 %collective-permute-start.14 = (bf16[64,640]{1,0:T(8,128)(2,1)S(1)}, bf16[64,640]{1,0:T(8,128)(2,1)S(1)}, u32[]{:S(2)}, u32[]{:S(2)}) collective-permute-start(bf16[64,640]{1,0:T(8,128)(2,1)S(1)} %shard_map.81.refs_0_), channel_id=1, source_target_pairs={{0,2},{1,3},{2,0},{3,1},{4,6},{5,7},{6,4},{7,5},{8,10},{9,11},{10,... | collective-permute-start | bytes 245768 | tf_op jit(solution)/shard_map/ppermute | solution.py:407
  36.8 1.0 %collective-permute-start.13 = (bf16[64,640]{1,0:T(8,128)(2,1)S(1)}, bf16[64,640]{1,0:T(8,128)(2,1)S(1)}, u32[]{:S(2)}, u32[]{:S(2)}) collective-permute-start(bf16[64,640]{1,0:T(8,128)(2,1)S(1)} %shard_map.81.refs_0_), channel_id=1, source_target_pairs={{0,1},{1,0},{2,3},{3,2},{4,5},{5,4},{6,7},{7,6},{8,9},{9,8},{10,11... | collective-permute-start | bytes 245768 | tf_op jit(solution)/shard_map/ppermute | solution.py:407
  37.8 2.5 %collective-permute-done.15.refs_3_ = bf16[64,640]{1,0:T(8,128)(2,1)S(1)} collective-permute-done((bf16[64,640]{1,0:T(8,128)(2,1)S(1)}, bf16[64,640]{1,0:T(8,128)(2,1)S(1)}, u32[]{:S(2)}, u32[]{:S(2)}) %collective-permute-start.15) | collective-permute-done | bytes 81952 | tf_op jit(solution)/shard_map/ppermute | solution.py:407
  40.3 0.5 collective-permute-done.14.refs_2_
  40.8 0.5 collective-permute-done.13.refs_1_
  41.3 1.3 %shard_map.82 = (f32[2,256,256]{2,1,0:T(8,128)S(1)}, bf16[2,256,256]{2,1,0:T(8,128)(2,1)S(1)}, bf16[640,256]{1,0:T(8,128)(2,1)S(1)}, bf16[256,64]{1,0:T(8,128)(2,1)S(1)}, bf16[64,192]{1,0:T(8,128)(2,1)S(1)}) custom-call(s32[3]{0:T(128)S(1)} %pad_add_fusion.index, bf16[64,640]{1,0:T(8,128)(2,1)S(1)} %shard_map.81.refs_0_, ...), custom_call_target="tpu_custom_call" | custom-call | tf_op jit(solution)/shard_map/pallas_call | solution.py:377
  42.5 0.1 collective-permute-start.17
  42.6 1.0 %shard_map.83 = (f32[2,256,256]{2,1,0:T(8,128)S(1)}, bf16[2,256,256]{2,1,0:T(8,128)(2,1)S(1)}) custom-call(s32[3]{0:T(128)S(1)} %pad_add_fusion.index, bf16[640,256]{1,0:T(8,128)(2,1)S(1)} %get-tuple-element.50.turned_ref, bf16[256,64]{1,0:T(8,128)(2,1)S(1)} %get-tuple-element.51.small_ref, bf16[64,192]{1,0:T(8,128)(2,1)S(1)} %get-tuple-element.52.small_t_ref, ...), custom_call_target="tpu_custom_call" | custom-call | tf_op jit(solution)/shard_map/pallas_call | solution.py:377
  43.7 0.6 collective-permute-start.16
  44.2 0.0 collective-permute-done.17.come_ref
  44.2 0.1 shard_map.85
  44.3 1.1 %collective-permute-start.18 = (bf16[256,256]{1,0:T(8,128)(2,1)S(1)}, bf16[256,256]{1,0:T(8,128)(2,1)S(1)}, u32[]{:S(2)}, u32[]{:S(2)}) collective-permute-start(bf16[256,256]{1,0:T(8,128)(2,1)S(1)} %get-tuple-element.59), channel_id=1, source_target_pairs={{0,4},{1,5},{2,6},{3,7},{4,0},{5,1},{6,2},{7,3},{8,12},{9,13},{10,... | collective-permute-start | bytes 393224 | tf_op jit(solution)/shard_map/ppermute | solution.py:400
  45.4 0.0 collective-permute-done.16.come_ref
  45.4 0.1 shard_map.84
  45.4 4.4 %collective-permute-done.18.b_ref = bf16[256,256]{1,0:T(8,128)(2,1)S(1)} collective-permute-done((bf16[256,256]{1,0:T(8,128)(2,1)S(1)}, bf16[256,256]{1,0:T(8,128)(2,1)S(1)}, u32[]{:S(2)}, u32[]{:S(2)}) %collective-permute-start.18) | collective-permute-done | bytes 131104 | tf_op jit(solution)/shard_map/ppermute | solution.py:400
  49.9 2.7 %collective-permute-start.19 = (bf16[256,256]{1,0:T(8,128)(2,1)S(1)}, bf16[256,256]{1,0:T(8,128)(2,1)S(1)}, u32[]{:S(2)}, u32[]{:S(2)}) collective-permute-start(bf16[256,256]{1,0:T(8,128)(2,1)S(1)} %shard_map.86), channel_id=1, source_target_pairs={{0,8},{1,9},{2,10},{3,11},{4,12},{5,13},{6,14},{7,15},{8,0},{9,1},... | collective-permute-start | bytes 393224 | tf_op jit(solution)/shard_map/ppermute | solution.py:400
  52.6 1.7 %collective-permute-start.20 = (bf16[256,256]{1,0:T(8,128)(2,1)S(1)}, bf16[256,256]{1,0:T(8,128)(2,1)S(1)}, u32[]{:S(2)}, u32[]{:S(2)}) collective-permute-start(bf16[256,256]{1,0:T(8,128)(2,1)S(1)} %get-tuple-element.61), channel_id=1, source_target_pairs={{0,4},{1,5},{2,6},{3,7},{4,0},{5,1},{6,2},{7,3},{8,12},{9,13},{10,... | collective-permute-start | bytes 393224 | tf_op jit(solution)/shard_map/ppermute | solution.py:400
  54.3 4.0 %collective-permute-done.19.b_ref = bf16[256,256]{1,0:T(8,128)(2,1)S(1)} collective-permute-done((bf16[256,256]{1,0:T(8,128)(2,1)S(1)}, bf16[256,256]{1,0:T(8,128)(2,1)S(1)}, u32[]{:S(2)}, u32[]{:S(2)}) %collective-permute-start.19) | collective-permute-done | bytes 131104 | tf_op jit(solution)/shard_map/ppermute | solution.py:400
  58.3 0.3 collective-permute-done.20.refs_0_
  58.7 0.7 %shard_map.88 = (f32[192,256]{1,0:T(8,128)}, f32[64,256]{1,0:T(8,128)}) custom-call(f32[256,256]{1,0:T(8,128)S(1)} %shard_map.87.keep_ref, bf16[256,256]{1,0:T(8,128)(2,1)S(1)} %collective-permute-done.20.refs_0_), custom_call_target="tpu_custom_call" | custom-call | tf_op jit(solution)/shard_map/pallas_call | solution.py:377
  (3 shorter events, 0.1 us)
Async XLA Ops:
  2.4 13.4 %collective-permute-start = (bf16[2,64,1024]{2,1,0:T(8,128)(2,1)S(1)}, bf16[2,64,1024]{2,1,0:T(8,128)(2,1)S(1)}, u32[]{:S(2)}, u32[]{:S(2)}) collective-permute-start(bf16[2,64,1024]{2,1,0:T(8,128)(2,1)S(1)} %get-tuple-element.34), channel_id=1, source_target_pairs={{0,3},{1,2},{2,1},{3,0},{4,7},{5,6},{6,5},{7,4},{8,11},{9,10},{10,... | collective-permute-start | bytes 786440 | tf_op jit(solution)/shard_map/ppermute | solution.py:407
  6.4 9.3 %copy-start.1 = (bf16[1,4096]{1,0:T(2,128)(2,1)S(1)}, bf16[1,4096]{1,0:T(2,128)(2,1)}, u32[]{:S(2)}) copy-start(bf16[1,4096]{1,0:T(2,128)(2,1)} %param.9) | copy-start | bytes 24580
  6.4 8.8 %collective-permute-start.4 = (bf16[256,256]{1,0:T(8,128)(2,1)S(1)}, bf16[256,256]{1,0:T(8,128)(2,1)S(1)}, u32[]{:S(2)}, u32[]{:S(2)}) collective-permute-start(bf16[256,256]{1,0:T(8,128)(2,1)S(1)} %get-tuple-element.35.pack_ref), channel_id=1, source_target_pairs={{0,8},{1,9},{2,10},{3,11},{4,12},{5,13},{6,14},{7,15},{8,0},{9,1},... | collective-permute-start | bytes 393224 | tf_op jit(solution)/shard_map/ppermute | solution.py:400
  8.9 6.8 %collective-permute-start.3 = (bf16[256,256]{1,0:T(8,128)(2,1)S(1)}, bf16[256,256]{1,0:T(8,128)(2,1)S(1)}, u32[]{:S(2)}, u32[]{:S(2)}) collective-permute-start(bf16[256,256]{1,0:T(8,128)(2,1)S(1)} %get-tuple-element.35.pack_ref), channel_id=1, source_target_pairs={{0,4},{1,5},{2,6},{3,7},{4,0},{5,1},{6,2},{7,3},{8,12},{9,13},{10,... | collective-permute-start | bytes 393224 | tf_op jit(solution)/shard_map/ppermute | solution.py:400
  12.2 8.4 %collective-permute-start.1 = (bf16[2,64,1024]{2,1,0:T(8,128)(2,1)S(1)}, bf16[2,64,1024]{2,1,0:T(8,128)(2,1)S(1)}, u32[]{:S(2)}, u32[]{:S(2)}) collective-permute-start(bf16[2,64,1024]{2,1,0:T(8,128)(2,1)S(1)} %get-tuple-element.38), channel_id=1, source_target_pairs={{0,2},{1,3},{2,0},{3,1},{4,6},{5,7},{6,4},{7,5},{8,10},{9,11},{10,... | collective-permute-start | bytes 786440 | tf_op jit(solution)/shard_map/ppermute | solution.py:407
  12.8 7.8 %collective-permute-start.2 = (bf16[2,64,1024]{2,1,0:T(8,128)(2,1)S(1)}, bf16[2,64,1024]{2,1,0:T(8,128)(2,1)S(1)}, u32[]{:S(2)}, u32[]{:S(2)}) collective-permute-start(bf16[2,64,1024]{2,1,0:T(8,128)(2,1)S(1)} %get-tuple-element.39), channel_id=1, source_target_pairs={{0,1},{1,0},{2,3},{3,2},{4,5},{5,4},{6,7},{7,6},{8,9},{9,8},{10,11... | collective-permute-start | bytes 786440 | tf_op jit(solution)/shard_map/ppermute | solution.py:407
  15.1 5.0 %collective-permute-start.5 = (bf16[256,256]{1,0:T(8,128)(2,1)S(1)}, bf16[256,256]{1,0:T(8,128)(2,1)S(1)}, u32[]{:S(2)}, u32[]{:S(2)}) collective-permute-start(bf16[256,256]{1,0:T(8,128)(2,1)S(1)} %collective-permute-done.4.refs_6_), channel_id=1, source_target_pairs={{0,4},{1,5},{2,6},{3,7},{4,0},{5,1},{6,2},{7,3},{8,12},{9,13},{10,... | collective-permute-start | bytes 393224 | tf_op jit(solution)/shard_map/ppermute | solution.py:400
  15.7 4.4 %collective-permute-start.7 = (bf16[256,256]{1,0:T(8,128)(2,1)S(1)}, bf16[256,256]{1,0:T(8,128)(2,1)S(1)}, u32[]{:S(2)}, u32[]{:S(2)}) collective-permute-start(bf16[256,256]{1,0:T(8,128)(2,1)S(1)} %collective-permute-done.3.refs_5_), channel_id=1, source_target_pairs={{0,16},{16,0},{1,17},{17,1},{2,18},{18,2},{3,19},{19,3},{4,20},{20... | collective-permute-start | bytes 393224 | tf_op jit(solution)/shard_map/ppermute | solution.py:403
  17.3 4.3 %collective-permute-start.6 = (bf16[272,256]{1,0:T(8,128)(2,1)S(1)}, bf16[272,256]{1,0:T(8,128)(2,1)S(1)}, u32[]{:S(2)}, u32[]{:S(2)}) collective-permute-start(bf16[272,256]{1,0:T(8,128)(2,1)S(1)} %get-tuple-element.40.refs_4_), channel_id=1, source_target_pairs={{0,16},{16,0},{1,17},{17,1},{2,18},{18,2},{3,19},{19,3},{4,20},{20... | collective-permute-start | bytes 417800 | tf_op jit(solution)/shard_map/ppermute | solution.py:403
  20.1 1.3 %collective-permute-start.9 = (bf16[256,256]{1,0:T(8,128)(2,1)S(1)}, bf16[256,256]{1,0:T(8,128)(2,1)S(1)}, u32[]{:S(2)}, u32[]{:S(2)}) collective-permute-start(bf16[256,256]{1,0:T(8,128)(2,1)S(1)} %collective-permute-done.5.refs_7_), channel_id=1, source_target_pairs={{0,16},{16,0},{1,17},{17,1},{2,18},{18,2},{3,19},{19,3},{4,20},{20... | collective-permute-start | bytes 393224 | tf_op jit(solution)/shard_map/ppermute | solution.py:403
  20.1 1.5 %collective-permute-start.8 = (bf16[256,256]{1,0:T(8,128)(2,1)S(1)}, bf16[256,256]{1,0:T(8,128)(2,1)S(1)}, u32[]{:S(2)}, u32[]{:S(2)}) collective-permute-start(bf16[256,256]{1,0:T(8,128)(2,1)S(1)} %collective-permute-done.4.refs_6_), channel_id=1, source_target_pairs={{0,16},{16,0},{1,17},{17,1},{2,18},{18,2},{3,19},{19,3},{4,20},{20... | collective-permute-start | bytes 393224 | tf_op jit(solution)/shard_map/ppermute | solution.py:403
  23.2 7.0 %collective-permute-start.10 = (bf16[64,896]{1,0:T(8,128)(2,1)S(1)}, bf16[64,896]{1,0:T(8,128)(2,1)S(1)}, u32[]{:S(2)}, u32[]{:S(2)}) collective-permute-start(bf16[64,896]{1,0:T(8,128)(2,1)S(1)} %get-tuple-element.42), channel_id=1, source_target_pairs={{0,3},{1,2},{2,1},{3,0},{4,7},{5,6},{6,5},{7,4},{8,11},{9,10},{10,... | collective-permute-start | bytes 344072 | tf_op jit(solution)/shard_map/ppermute | solution.py:407
  23.9 7.6 %collective-permute-start.11 = (bf16[64,896]{1,0:T(8,128)(2,1)S(1)}, bf16[64,896]{1,0:T(8,128)(2,1)S(1)}, u32[]{:S(2)}, u32[]{:S(2)}) collective-permute-start(bf16[64,896]{1,0:T(8,128)(2,1)S(1)} %get-tuple-element.43), channel_id=1, source_target_pairs={{0,2},{1,3},{2,0},{3,1},{4,6},{5,7},{6,4},{7,5},{8,10},{9,11},{10,... | collective-permute-start | bytes 344072 | tf_op jit(solution)/shard_map/ppermute | solution.py:407
  25.3 6.2 %copy-start = (s32[2,1,2]{2,1,0:T(1,128)S(1)}, s32[2,1,2]{2,1,0:T(1,128)}, u32[]{:S(2)}) copy-start(s32[2,1,2]{2,1,0:T(1,128)} %docs.1) | copy-start | bytes 52
  25.3 6.2 %collective-permute-start.12 = (bf16[64,896]{1,0:T(8,128)(2,1)S(1)}, bf16[64,896]{1,0:T(8,128)(2,1)S(1)}, u32[]{:S(2)}, u32[]{:S(2)}) collective-permute-start(bf16[64,896]{1,0:T(8,128)(2,1)S(1)} %get-tuple-element.44), channel_id=1, source_target_pairs={{0,1},{1,0},{2,3},{3,2},{4,5},{5,4},{6,7},{7,6},{8,9},{9,8},{10,11... | collective-permute-start | bytes 344072 | tf_op jit(solution)/shard_map/ppermute | solution.py:407
  34.2 6.0 %collective-permute-start.15 = (bf16[64,640]{1,0:T(8,128)(2,1)S(1)}, bf16[64,640]{1,0:T(8,128)(2,1)S(1)}, u32[]{:S(2)}, u32[]{:S(2)}) collective-permute-start(bf16[64,640]{1,0:T(8,128)(2,1)S(1)} %shard_map.81.refs_0_), channel_id=1, source_target_pairs={{0,3},{1,2},{2,1},{3,0},{4,7},{5,6},{6,5},{7,4},{8,11},{9,10},{10,... | collective-permute-start | bytes 245768 | tf_op jit(solution)/shard_map/ppermute | solution.py:407
  35.5 5.3 %collective-permute-start.14 = (bf16[64,640]{1,0:T(8,128)(2,1)S(1)}, bf16[64,640]{1,0:T(8,128)(2,1)S(1)}, u32[]{:S(2)}, u32[]{:S(2)}) collective-permute-start(bf16[64,640]{1,0:T(8,128)(2,1)S(1)} %shard_map.81.refs_0_), channel_id=1, source_target_pairs={{0,2},{1,3},{2,0},{3,1},{4,6},{5,7},{6,4},{7,5},{8,10},{9,11},{10,... | collective-permute-start | bytes 245768 | tf_op jit(solution)/shard_map/ppermute | solution.py:407
  36.8 4.4 %collective-permute-start.13 = (bf16[64,640]{1,0:T(8,128)(2,1)S(1)}, bf16[64,640]{1,0:T(8,128)(2,1)S(1)}, u32[]{:S(2)}, u32[]{:S(2)}) collective-permute-start(bf16[64,640]{1,0:T(8,128)(2,1)S(1)} %shard_map.81.refs_0_), channel_id=1, source_target_pairs={{0,1},{1,0},{2,3},{3,2},{4,5},{5,4},{6,7},{7,6},{8,9},{9,8},{10,11... | collective-permute-start | bytes 245768 | tf_op jit(solution)/shard_map/ppermute | solution.py:407
  42.5 1.7 %collective-permute-start.17 = (bf16[2,256,256]{2,1,0:T(8,128)(2,1)S(1)}, bf16[2,256,256]{2,1,0:T(8,128)(2,1)S(1)}, u32[]{:S(2)}, u32[]{:S(2)}) collective-permute-start(bf16[2,256,256]{2,1,0:T(8,128)(2,1)S(1)} %get-tuple-element.57), channel_id=1, source_target_pairs={{0,16},{16,0},{1,17},{17,1},{2,18},{18,2},{3,19},{19,3},{4,20},{20... | collective-permute-start | bytes 786440 | tf_op jit(solution)/shard_map/ppermute | solution.py:403
  43.7 1.7 %collective-permute-start.16 = (bf16[2,256,256]{2,1,0:T(8,128)(2,1)S(1)}, bf16[2,256,256]{2,1,0:T(8,128)(2,1)S(1)}, u32[]{:S(2)}, u32[]{:S(2)}) collective-permute-start(bf16[2,256,256]{2,1,0:T(8,128)(2,1)S(1)} %get-tuple-element.54), channel_id=1, source_target_pairs={{0,16},{16,0},{1,17},{17,1},{2,18},{18,2},{3,19},{19,3},{4,20},{20... | collective-permute-start | bytes 786440 | tf_op jit(solution)/shard_map/ppermute | solution.py:403
  44.3 5.5 %collective-permute-start.18 = (bf16[256,256]{1,0:T(8,128)(2,1)S(1)}, bf16[256,256]{1,0:T(8,128)(2,1)S(1)}, u32[]{:S(2)}, u32[]{:S(2)}) collective-permute-start(bf16[256,256]{1,0:T(8,128)(2,1)S(1)} %get-tuple-element.59), channel_id=1, source_target_pairs={{0,4},{1,5},{2,6},{3,7},{4,0},{5,1},{6,2},{7,3},{8,12},{9,13},{10,... | collective-permute-start | bytes 393224 | tf_op jit(solution)/shard_map/ppermute | solution.py:400
  49.9 8.4 %collective-permute-start.19 = (bf16[256,256]{1,0:T(8,128)(2,1)S(1)}, bf16[256,256]{1,0:T(8,128)(2,1)S(1)}, u32[]{:S(2)}, u32[]{:S(2)}) collective-permute-start(bf16[256,256]{1,0:T(8,128)(2,1)S(1)} %shard_map.86), channel_id=1, source_target_pairs={{0,8},{1,9},{2,10},{3,11},{4,12},{5,13},{6,14},{7,15},{8,0},{9,1},... | collective-permute-start | bytes 393224 | tf_op jit(solution)/shard_map/ppermute | solution.py:400
  52.6 6.1 %collective-permute-start.20 = (bf16[256,256]{1,0:T(8,128)(2,1)S(1)}, bf16[256,256]{1,0:T(8,128)(2,1)S(1)}, u32[]{:S(2)}, u32[]{:S(2)}) collective-permute-start(bf16[256,256]{1,0:T(8,128)(2,1)S(1)} %get-tuple-element.61), channel_id=1, source_target_pairs={{0,4},{1,5},{2,6},{3,7},{4,0},{5,1},{6,2},{7,3},{8,12},{9,13},{10,... | collective-permute-start | bytes 393224 | tf_op jit(solution)/shard_map/ppermute | solution.py:400

commit v16 on v15

--- a/solution.py
+++ b/solution.py
@@ -174,52 +174,75 @@
         copy.wait()
 
 
-def project_kernel(planes, heads, index, *refs):
-    blocks, own, other = refs[:PLANE], refs[PLANE : PLANE + planes], refs[PLANE + planes : PLANE + 2 * planes]
-    x_ref, c_ref, vx_ref, gain_ref = refs[PLANE + 2 * planes : PLANE + 2 * planes + 4]
-    out_refs = refs[PLANE + 2 * planes + 4 : -4]
-    vc_ref, sum_ref, *wide_refs = refs[-4:]
+def weights_of(heads, index, at, own, other, gain_refs, vx_ref, vc_ref, gain_ref, i):
     qkv, width = 3 * heads, vx_ref.shape[-1]
-    section, place, p = index[0], index[1], index[2]
-    for ref, wide_ref in zip((own[0], other[0]), wide_refs):
-        wide_ref[...] = ref[qkv + heads :, :].astype(F32)
-    for z in range(planes):
-        mine, theirs = (ref[pl.ds(z * PLANE + p, 1), :] for ref in wide_refs)
-        gain_ref[z, 0:1, :] = jnp.where(section == 0, mine, theirs)
-        gain_ref[z, 1:2, :] = jnp.where(section == 0, theirs, mine)
-    for k in range(planes):
-        at = place ^ k
-        mine, theirs = own[k][: qkv + heads, :], other[k][: qkv + heads, :]
-        zero = jnp.where(section == 0, mine, theirs)
-        one = jnp.where(section == 0, theirs, mine)
-        empty = jnp.zeros((heads, width), BF16)
-        vx_ref[at, :qkv, :] = (zero[:qkv].astype(F32) * gain_ref[at, 0:1, :]).astype(BF16)
-        vx_ref[at, qkv : qkv + heads, :] = zero[qkv : qkv + heads]
-        vx_ref[at, qkv + heads : 2 * qkv + heads, :] = (one[:qkv].astype(F32) * gain_ref[at, 1:2, :]).astype(BF16)
-        vx_ref[at, 2 * qkv + heads :, :] = empty
-        vc_ref[at, :heads, :] = empty
-        vc_ref[at, heads : 2 * heads, :] = one[qkv : qkv + heads]
-        vc_ref[at, 2 * heads : 3 * heads, :] = zero[qkv : qkv + heads]
-        vc_ref[at, 3 * heads :, :] = empty
+    section, p = index[0], index[2]
+    mine, theirs = (ref[pl.ds(at * PLANE + p, 1), :] for ref in gain_refs)
+    gain0, gain1 = jnp.where(section == 0, mine, theirs), jnp.where(section == 0, theirs, mine)
+    gain_ref[i, 0:1, :] = gain0
+    gain_ref[i, 1:2, :] = gain1
+    zero, one = jnp.where(section == 0, own, other), jnp.where(section == 0, other, own)
+    empty = jnp.zeros((heads, width), BF16)
+    vx_ref[i, :qkv, :] = (zero[:qkv].astype(F32) * gain0).astype(BF16)
+    vx_ref[i, qkv : qkv + heads, :] = zero[qkv:]
+    vx_ref[i, qkv + heads : 2 * qkv + heads, :] = (one[:qkv].astype(F32) * gain1).astype(BF16)
+    vx_ref[i, 2 * qkv + heads :, :] = empty
+    vc_ref[i, :heads, :] = empty
+    vc_ref[i, heads : 2 * heads, :] = one[qkv:]
+    vc_ref[i, 2 * heads : 3 * heads, :] = zero[qkv:]
+    vc_ref[i, 3 * heads :, :] = empty
+
+
+def products_of(heads, x, c, vx_ref, vc_ref, i):
+    qkv = 3 * heads
+    wide = x.astype(F32)
+    out = vx_ref[i, qkv : qkv + heads, :]
+    right = jnp.concatenate([vx_ref[i, qkv + heads : 2 * qkv + heads, :], out], axis=0)
+    return nt(x, vx_ref[i]), nt(c, vc_ref[i]), jnp.sum(wide * wide, axis=1, keepdims=True), nt(out, right)
+
+
+def columns(ref, at, width):
+    cols = pl.ds(pl.multiple_of(at * width, width), width)
+    return ref[:, :, cols].reshape(ref.shape[0] * ref.shape[1], width)
+
+
+def early_kernel(planes, heads, index, *refs):
+    count = planes - 1
+    blocks, own, other = refs[:PLANE], refs[PLANE : PLANE + count], refs[PLANE + count : PLANE + 2 * count]
+    x_ref, c_ref, vx_ref, gain_ref, wide_ref, *sum_refs = refs[PLANE + 2 * count : -1]
+    vc_ref = refs[-1]
+    size, width = 4 * heads, vx_ref.shape[-1]
+    place, p = index[1], index[2]
+    rows_of_gain = planes * PLANE
+    for i, ref in enumerate((own[0], other[0])):
+        wide_ref[i * rows_of_gain : (i + 1) * rows_of_gain, :] = ref[size:, :].astype(F32)
+    gain_refs = [wide_ref.at[i * rows_of_gain : (i + 1) * rows_of_gain] for i in range(2)]
     for k in range(PLANE):
         x_ref[p ^ k] = blocks[-k][0]
         c_ref[p ^ k] = blocks[-k][1]
-    rows = x_ref.shape[0] * x_ref.shape[1]
-    with_x = with_c = squares = products = None
-    for z in range(planes):
-        cols = slice(z * width, (z + 1) * width)
-        x = x_ref[:, :, cols].reshape(rows, width)
-        c = c_ref[:, :, cols].reshape(rows, width)
-        wide = x.astype(F32)
-        out = vx_ref[z, qkv : qkv + heads, :]
-        right = jnp.concatenate([vx_ref[z, qkv + heads : 2 * qkv + heads, :], out], axis=0)
-        new = nt(x, vx_ref[z]), nt(c, vc_ref[z]), jnp.sum(wide * wide, axis=1, keepdims=True), nt(out, right)
-        if with_x is None:
-            with_x, with_c, squares, products = new
-        else:
-            with_x, with_c = with_x + new[0], with_c + new[1]
-            squares, products = squares + new[2], products + new[3]
-    half = 2 * heads
+    totals = None
+    for k in range(count):
+        at = place ^ k
+        weights_of(heads, index, at, own[k][:size, :], other[k][:size, :], gain_refs, vx_ref, vc_ref, gain_ref, k)
+        new = products_of(heads, columns(x_ref, at, width), columns(c_ref, at, width), vx_ref, vc_ref, k)
+        totals = new if totals is None else [a + b for a, b in zip(totals, new)]
+    for ref, total in zip(sum_refs, totals):
+        ref[...] = jnp.broadcast_to(total, ref.shape)
+
+
+def project_kernel(planes, heads, index, own, other, x_ref, c_ref, wide_ref, *refs):
+    sums, (vx_ref, gain_ref) = refs[:4], refs[4:6]
+    out_refs, (vc_ref, sum_ref) = refs[6:-2], refs[-2:]
+    width = vx_ref.shape[-1]
+    place, p = index[1], index[2]
+    at = place ^ (planes - 1)
+    rows_of_gain = planes * PLANE
+    gain_refs = [wide_ref.at[i * rows_of_gain : (i + 1) * rows_of_gain] for i in range(2)]
+    weights_of(heads, index, at, own[...], other[...], gain_refs, vx_ref, vc_ref, gain_ref, 0)
+    new = products_of(heads, columns(x_ref, at, width), columns(c_ref, at, width), vx_ref, vc_ref, 0)
+    with_x, with_c, products = (sums[i][...] + new[i] for i in (0, 1, 3))
+    squares = sums[2][:, 0:1] + new[2]
+    rows, half = with_x.shape[0], 2 * heads
     lane = lax.broadcasted_iota(jnp.int32, (rows, half), 1)
     high = squares.astype(BF16).astype(F32)
     last = jnp.where(lane == heads, high, jnp.where(lane == heads + 1, squares - high, with_c[:, half:]))
@@ -298,36 +321,36 @@
     out_ref[...] = jnp.concatenate(factors, axis=1).astype(BF16)
 
 
-def pieces_of(planes, heads, order, index, turned, small, small_t, x_ref, c_ref, vx_ref, gain_ref, keep_ref, send_ref):
-    qkv, half, width = 3 * heads, 2 * heads, vx_ref.shape[-1]
+def pieces_of(heads, order, index, turned, small, small_t, x_ref, c_ref, weights, keep_ref, send_ref):
+    qkv, half = 3 * heads, 2 * heads
     section, place = index[0], index[1]
-    rows = x_ref.shape[0] * x_ref.shape[1]
     att0, att1 = turned[qkv : qkv + heads], turned[4 * half : 4 * half + heads]
+    early_vx, late_vx, early_gain, late_gain = weights
+    count = early_vx.shape[0]
     for i, k in enumerate(order):
-        z = place ^ k
-        cols = pl.ds(pl.multiple_of(z * width, width), width)
-        x = x_ref[:, :, cols].reshape(rows, width)
-        c = c_ref[:, :, cols].reshape(rows, width)
-        out = vx_ref[z, qkv : qkv + heads, :]
+        vx, gain = (early_vx.at[k], early_gain.at[k]) if k < count else (late_vx.at[0], late_gain.at[0])
+        x = columns(x_ref, place ^ k, vx.shape[-1])
+        c = columns(c_ref, place ^ k, vx.shape[-1])
+        out = vx[qkv : qkv + heads, :]
         with_x = nn(turned[: 4 * half], x)
         left = with_x[2 * half :] + nn(small, out)
-        zero = with_x[:qkv] * gain_ref[z, 0:1, :]
-        one = left[:qkv] * gain_ref[z, 1:2, :]
+        zero = with_x[:qkv] * gain[0:1, :]
+        one = left[:qkv] * gain[1:2, :]
         keep_ref[i, :qkv, :] = jnp.where(section == 0, zero, one)
         send_ref[i, :qkv, :] = jnp.where(section == 0, one, zero).astype(BF16)
-        zero = nn(att0, c) + nn(small_t, vx_ref[z, qkv + heads : 2 * qkv + heads, :]) - left[qkv:]
+        zero = nn(att0, c) + nn(small_t, vx[qkv + heads : 2 * qkv + heads, :]) - left[qkv:]
         one = nn(att1, c)
         keep_ref[i, qkv:, :] = jnp.where(section == 0, zero, one)
         send_ref[i, qkv:, :] = jnp.where(section == 0, one, zero).astype(BF16)
 
 
-def far_grads_kernel(planes, heads, order, index, *refs):
-    factors, arrays = refs[:PLANE], refs[PLANE : PLANE + 4]
-    keep_ref, send_ref, turned_ref, small_ref, small_t_ref, all_ref = refs[PLANE + 4 :]
+def far_grads_kernel(heads, order, index, *refs):
+    factors, (x_ref, c_ref, *weights) = refs[:PLANE], refs[PLANE : PLANE + 6]
+    keep_ref, send_ref, turned_ref, small_ref, small_t_ref, all_ref = refs[PLANE + 6 :]
     qkv, half = 3 * heads, 2 * heads
     p = index[2]
     for k in range(PLANE):
-        all_ref[p ^ k] = factors[k][...]
+        all_ref[p ^ k] = factors[-k][...]
     rows = all_ref.shape[0] * all_ref.shape[1]
     turned = jnp.transpose(all_ref[...].astype(F32).reshape(rows, 5 * half)).astype(BF16)
     att0, right = turned[qkv : qkv + heads], turned[2 * half : 4 * half]
@@ -336,11 +359,12 @@
     turned_ref[...] = turned
     small_ref[...] = small
     small_t_ref[...] = small_t
-    pieces_of(planes, heads, order, index, turned, small, small_t, *arrays, keep_ref, send_ref)
-
-
-def near_grads_kernel(planes, heads, order, index, turned_ref, small_ref, small_t_ref, *refs):
-    pieces_of(planes, heads, order, index, turned_ref[...], small_ref[...], small_t_ref[...], *refs)
+    pieces_of(heads, order, index, turned, small, small_t, x_ref, c_ref, weights, keep_ref, send_ref)
+
+
+def near_grads_kernel(heads, order, index, turned_ref, small_ref, small_t_ref, x_ref, c_ref, *refs):
+    factors = turned_ref[...], small_ref[...], small_t_ref[...]
+    pieces_of(heads, order, index, *factors, x_ref, c_ref, refs[:4], *refs[4:])
 
 
 def merge_kernel(keep_ref, come_ref, *out_refs):
@@ -369,6 +393,10 @@
     of = lambda k: value[k] if isinstance(value, (list, tuple)) else value
     got = {k: send(of(k), k) for k in reversed(range(1, count))}
     return [of(0)] + [got[k] for k in range(1, count)]
+
+
+def turned_round(values):
+    return [values[0], *values[:0:-1]]
 
 
 def call(kernel, outs, *args, scalars=0, scratch=()):
@@ -449,19 +477,30 @@
         scratch_shapes=[pltpu.SemaphoreType.DMA((2 * planes,))],
         compiler_params=params,
     )(index, mine, late_gain, x_in, c_in)
-    pieces[planes // 2], _ = lax.optimization_barrier((pieces[planes // 2], blocks[3]))
+    pieces[planes // 2], _ = lax.optimization_barrier((pieces[planes // 2], pieces[1]))
     own = [marked] + [pieces[k] for k in range(1, planes)]
     other = [to_sibling(piece) for piece in own]
 
     split = ((PLANE, block, cols), BF16)
     half = 2 * heads
-    x, c, vx, gains, *sent = call(
+    sums = [((rows, 4 * half), F32), ((rows, 2 * half), F32), ((rows, 2 * heads), F32), ((heads, 2 * half), F32)]
+
+    def weights(count):
+        return [((count, 4 * half, width), BF16), ((count, 8, width), F32)]
+
+    x, c, early_vx, early_gain, wide, *totals = call(
+        functools.partial(early_kernel, planes, heads),
+        [split, split] + weights(planes - 1) + [((2 * shards, width), F32)] + sums,
+        index, blocks[0], *blocks[:0:-1], *own[:-1], *other[:-1], scalars=1,
+        scratch=[((planes - 1, 2 * half, width), BF16)],
+    )
+    late_vx, late_gain, *sent = call(
         functools.partial(project_kernel, planes, heads),
-        [split, split, ((planes, 4 * half, width), BF16), ((planes, 8, width), F32)]
-        + [((block, 7 * half), BF16)] * PLANE,
-        index, blocks[0], *blocks[:0:-1], *own, *other, scalars=1,
-        scratch=[((planes, 2 * half, width), BF16), ((rows, 5 * half), BF16)] + [((shards, width), F32)] * 2,
-    )
+        weights(1) + [((block, 7 * half), BF16)] * PLANE,
+        index, own[-1], other[-1], x, c, wide, *totals, scalars=1,
+        scratch=[((1, 2 * half, width), BF16), ((rows, 5 * half), BF16)],
+    )
+    arrays = x, c, early_vx, late_vx, early_gain, late_gain
     (factors,) = call(
         functools.partial(chain_kernel, features, heads),
         [((block, 5 * half), BF16)],
@@ -476,17 +515,17 @@
         return zip(order, call(merge_kernel, outs, keep, to_sibling(send)))
 
     keep, send, turned, small, small_t = call(
-        functools.partial(far_grads_kernel, planes, heads, far_order),
+        functools.partial(far_grads_kernel, heads, far_order),
         [((len(far_order),) + piece, F32), ((len(far_order),) + piece, BF16)]
         + [((5 * half, rows), BF16), ((2 * half, heads), BF16), ((heads, qkv_rows), BF16)],
-        index, *exchange(factors), x, c, vx, gains, scalars=1,
+        index, *turned_round(exchange(factors)), *arrays, scalars=1,
         scratch=[((PLANE, block, 5 * half), BF16)],
     )
     pieces = dict(swap_and_merge(far_order, keep, send))
     keep, send = call(
-        functools.partial(near_grads_kernel, planes, heads, near_order),
+        functools.partial(near_grads_kernel, heads, near_order),
         [((len(near_order),) + piece, F32), ((len(near_order),) + piece, BF16)],
-        index, turned, small, small_t, x, c, vx, gains, scalars=1,
+        index, turned, small, small_t, *arrays, scalars=1,
     )
     pieces.update(swap_and_merge(near_order, keep, send))
     kept, parts = pieces[0], []

time: 59.7 us -> 59.8 us (level)
  Pallas kernels: 12.3 us -> 12.9 us
    ppermute x6, waiting for transfers between devices: 1.03 us -> 0.11 us  [to_sibling(): return lax.ppermute(value, 'section', [(0, 1), (1, 0)])]
    pallas_call x9 -> x10, Pallas kernels: 7.5 us -> 8.04 us  [call(): pl.pallas_call(kernel, out_shape=[jax.ShapeDtypeStruct(shape, dtype) for...]
  transfers between devices with their start and end apart: 21 -> 21, of which waited for: 12 -> 11; matrix products, arithmetic and copies ran while one was open for 0% -> 0% of each run, Pallas kernels for 7% -> 9%
where the time goes in v16:
time: 59.8 us; the launch traced here: 59.5 us
  starting transfers between devices  24.2 us (40%)
  waiting for transfers between devices  21.5 us (36%)
  Pallas kernels  12.9 us (22%)
  between operations  0.78 us (1%)
    ppermute x6, waiting for transfers between devices, along_z(): return lax.ppermute(value, 'dp', route)  13.1 us
    ppermute x9, starting transfers between devices, along_plane(): return lax.ppermute(value, 'dp', route)  12.2 us
    ppermute x6, starting transfers between devices, along_z(): return lax.ppermute(value, 'dp', route)  10.8 us
    ppermute x9, waiting for transfers between devices, along_plane(): return lax.ppermute(value, 'dp', route)  8.3 us
    pallas_call x10, Pallas kernels, call(): pl.pallas_call(kernel, out_shape=[jax.ShapeDtypeStruct(shape, dtype) for...  8.04 us
    pallas_call x1, Pallas kernels, planar(): pl.pallas_call(functools.partial(blocks_kernel, planes), out_shape=[one_b...  1.69 us
    pallas_call x1, Pallas kernels, planar(): pl.pallas_call(functools.partial(first_kernel, planes), out_shape=[jax.Sh...  1.66 us
    pallas_call x1, Pallas kernels, planar(): pl.pallas_call(functools.partial(mark_kernel, planes), out_shape=[jax.Sha...  1.49 us
  transfers between devices with their start and end apart: 21, of which 11 were waited for; matrix products, arithmetic and copies ran while one was open for 0% of the time, Pallas kernels for 9%

profile of v16, /device:TPU:0, one launch (start us, length us, event | category | flops | bytes accessed | tf_op | source)
XLA Modules:
  0.0 59.5 jit_solution(6030234813197718855)
XLA Ops:
  0.6 0.1 pad_add_fusion.index
  0.7 1.7 %shard_map.77 = (bf16[256,256]{1,0:T(8,128)(2,1)S(1)}, bf16[2,64,1024]{2,1,0:T(8,128)(2,1)S(1)}) custom-call(s32[3]{0:T(128)S(1)} %pad_add_fusion.index, bf16[192,256]{1,0:T(8,128)(2,1)} %bitcast.11, bf16[64,256]{1,0:T(8,128)(2,1)} %bitcast.12, bf16[2,64,4096]{2,1,0:T(8,128)(2,1)} %x_ref.5, bf16[2,64,4096]{2,1,0:T(8,128)(2,1)} %c_ref.5), custom_call_target="tpu_custom_call" | custom-call | tf_op jit(solution)/shard_map/pallas_call | solution.py:448
  2.4 4.0 %collective-permute-start.3 = (bf16[2,64,1024]{2,1,0:T(8,128)(2,1)S(1)}, bf16[2,64,1024]{2,1,0:T(8,128)(2,1)S(1)}, u32[]{:S(2)}, u32[]{:S(2)}) collective-permute-start(bf16[2,64,1024]{2,1,0:T(8,128)(2,1)S(1)} %get-tuple-element.41), channel_id=1, source_target_pairs={{0,3},{1,2},{2,1},{3,0},{4,7},{5,6},{6,5},{7,4},{8,11},{9,10},{10,... | collective-permute-start | bytes 786440 | tf_op jit(solution)/shard_map/ppermute | solution.py:435
  6.4 0.0 copy-start.1
  6.4 2.6 %collective-permute-start = (bf16[256,256]{1,0:T(8,128)(2,1)S(1)}, bf16[256,256]{1,0:T(8,128)(2,1)S(1)}, u32[]{:S(2)}, u32[]{:S(2)}) collective-permute-start(bf16[256,256]{1,0:T(8,128)(2,1)S(1)} %get-tuple-element.42.pack_ref), channel_id=1, source_target_pairs={{0,8},{1,9},{2,10},{3,11},{4,12},{5,13},{6,14},{7,15},{8,0},{9,1},... | collective-permute-start | bytes 393224 | tf_op jit(solution)/shard_map/ppermute | solution.py:428
  8.9 1.6 %collective-permute-start.6 = (bf16[256,256]{1,0:T(8,128)(2,1)S(1)}, bf16[256,256]{1,0:T(8,128)(2,1)S(1)}, u32[]{:S(2)}, u32[]{:S(2)}) collective-permute-start(bf16[256,256]{1,0:T(8,128)(2,1)S(1)} %get-tuple-element.42.pack_ref), channel_id=1, source_target_pairs={{0,4},{1,5},{2,6},{3,7},{4,0},{5,1},{6,2},{7,3},{8,12},{9,13},{10,... | collective-permute-start | bytes 393224 | tf_op jit(solution)/shard_map/ppermute | solution.py:428
  10.5 1.7 %shard_map.79 = (bf16[2,64,1024]{2,1,0:T(8,128)(2,1)S(1)}, bf16[2,64,1024]{2,1,0:T(8,128)(2,1)S(1)}) custom-call(s32[3]{0:T(128)S(1)} %pad_add_fusion.index, bf16[2,64,4096]{2,1,0:T(8,128)(2,1)} %x_ref.5, bf16[2,64,4096]{2,1,0:T(8,128)(2,1)} %c_ref.5), custom_call_target="tpu_custom_call" | custom-call | tf_op jit(solution)/shard_map/pallas_call | solution.py:456
  12.2 0.6 collective-permute-start.4
  12.8 0.5 collective-permute-start.5
  13.3 1.8 %collective-permute-done.refs_6_ = bf16[256,256]{1,0:T(8,128)(2,1)S(1)} collective-permute-done((bf16[256,256]{1,0:T(8,128)(2,1)S(1)}, bf16[256,256]{1,0:T(8,128)(2,1)S(1)}, u32[]{:S(2)}, u32[]{:S(2)}) %collective-permute-start) | collective-permute-done | bytes 131104 | tf_op jit(solution)/shard_map/ppermute | solution.py:428
  15.1 0.2 collective-permute-done.6.refs_5_
  15.3 0.0 collective-permute-start.9
  15.3 1.4 %collective-permute-start.1 = (bf16[256,256]{1,0:T(8,128)(2,1)S(1)}, bf16[256,256]{1,0:T(8,128)(2,1)S(1)}, u32[]{:S(2)}, u32[]{:S(2)}) collective-permute-start(bf16[256,256]{1,0:T(8,128)(2,1)S(1)} %collective-permute-done.refs_6_), channel_id=1, source_target_pairs={{0,4},{1,5},{2,6},{3,7},{4,0},{5,1},{6,2},{7,3},{8,12},{9,13},{10,... | collective-permute-start | bytes 393224 | tf_op jit(solution)/shard_map/ppermute | solution.py:428
  16.7 0.0 copy-done.1
  16.7 0.1 reduce
  16.8 0.0 collective-permute-done.3.refs_1_
  16.8 1.5 %shard_map.78 = (bf16[272,256]{1,0:T(8,128)(2,1)S(1)}, bf16[2,64,1024]{2,1,0:T(8,128)(2,1)S(1)}) custom-call(s32[3]{0:T(128)S(1)} %pad_add_fusion.index, bf16[256,256]{1,0:T(8,128)(2,1)S(1)} %get-tuple-element.42.pack_ref, bf16[16,256]{1,0:T(8,128)(2,1)S(1)} %reshape_squeeze.3.gain_ref, bf16[2,64,4096]{2,1,0:T(8,128)(2,1)} %x_ref.5, bf16[2,64,4096]{2,1,0:T(8,128)(2,1)} %c_ref.5), custom_call_target="tpu_custom_call" | custom-call | tf_op jit(solution)/shard_map/pallas_call | solution.py:472
  18.3 0.3 collective-permute-start.7
  18.6 0.0 collective-permute-done.9.refs_9_
  18.6 0.3 collective-permute-start.8
  18.9 2.4 %collective-permute-done.1.own = bf16[256,256]{1,0:T(8,128)(2,1)S(1)} collective-permute-done((bf16[256,256]{1,0:T(8,128)(2,1)S(1)}, bf16[256,256]{1,0:T(8,128)(2,1)S(1)}, u32[]{:S(2)}, u32[]{:S(2)}) %collective-permute-start.1) | collective-permute-done | bytes 131104 | tf_op jit(solution)/shard_map/ppermute | solution.py:428
  21.2 0.0 collective-permute-start.2
  21.3 0.0 collective-permute-done.4.refs_2_
  21.3 0.0 collective-permute-done.5.refs_3_
  21.3 0.0 collective-permute-done.8.refs_8_
  21.3 0.0 collective-permute-done.7.refs_7_
  21.3 1.2 %shard_map.80 = (bf16[4,64,1024]{2,1,0:T(8,128)(2,1)S(1)}, bf16[4,64,1024]{2,1,0:T(8,128)(2,1)S(1)}, bf16[3,512,256]{2,1,0:T(8,128)(2,1)S(1)}, f32[3,8,256]{2,1,...) custom-call(s32[3]{0:T(128)S(1)} %pad_add_fusion.index, ...), custom_call_target="tpu_custom_call" | custom-call | tf_op jit(solution)/shard_map/pallas_call | solution.py:405
  22.5 0.1 collective-permute-done.2.other
  22.6 0.9 %shard_map.81 = (bf16[1,512,256]{2,1,0:T(8,128)(2,1)S(1)}, f32[1,8,256]{2,1,0:T(8,128)S(1)}, bf16[64,896]{1,0:T(8,128)(2,1)S(1)}, bf16[64,896]{1,0:T(8,128)(2,1)...) custom-call(s32[3]{0:T(128)S(1)} %pad_add_fusion.index, bf16[256,256]{1,0:T(8,128)(2,1)S(1)} %collective-permute-done.1.own, ...), custom_call_target="tpu_custom_call" | custom-call | tf_op jit(solution)/shard_map/pallas_call | solution.py:405
  23.5 0.5 collective-permute-start.10
  24.0 1.6 %collective-permute-start.11 = (bf16[64,896]{1,0:T(8,128)(2,1)S(1)}, bf16[64,896]{1,0:T(8,128)(2,1)S(1)}, u32[]{:S(2)}, u32[]{:S(2)}) collective-permute-start(bf16[64,896]{1,0:T(8,128)(2,1)S(1)} %get-tuple-element.57), channel_id=1, source_target_pairs={{0,2},{1,3},{2,0},{3,1},{4,6},{5,7},{6,4},{7,5},{8,10},{9,11},{10,... | collective-permute-start | bytes 344072 | tf_op jit(solution)/shard_map/ppermute | solution.py:435
  25.6 0.0 copy-start
  25.6 1.5 %collective-permute-start.12 = (bf16[64,896]{1,0:T(8,128)(2,1)S(1)}, bf16[64,896]{1,0:T(8,128)(2,1)S(1)}, u32[]{:S(2)}, u32[]{:S(2)}) collective-permute-start(bf16[64,896]{1,0:T(8,128)(2,1)S(1)} %get-tuple-element.58), channel_id=1, source_target_pairs={{0,1},{1,0},{2,3},{3,2},{4,5},{5,4},{6,7},{7,6},{8,9},{9,8},{10,11... | collective-permute-start | bytes 344072 | tf_op jit(solution)/shard_map/ppermute | solution.py:435
  27.1 3.4 %collective-permute-done.10.refs_0_ = bf16[64,896]{1,0:T(8,128)(2,1)S(1)} collective-permute-done((bf16[64,896]{1,0:T(8,128)(2,1)S(1)}, bf16[64,896]{1,0:T(8,128)(2,1)S(1)}, u32[]{:S(2)}, u32[]{:S(2)}) %collective-permute-start.10) | collective-permute-done | bytes 114720 | tf_op jit(solution)/shard_map/ppermute | solution.py:435
  30.5 1.2 %collective-permute-done.11.refs_1_ = bf16[64,896]{1,0:T(8,128)(2,1)S(1)} collective-permute-done((bf16[64,896]{1,0:T(8,128)(2,1)S(1)}, bf16[64,896]{1,0:T(8,128)(2,1)S(1)}, u32[]{:S(2)}, u32[]{:S(2)}) %collective-permute-start.11) | collective-permute-done | bytes 114720 | tf_op jit(solution)/shard_map/ppermute | solution.py:435
  31.7 0.0 collective-permute-done.12.refs_2_
  31.7 0.0 copy-done
  31.7 2.7 %shard_map.82.refs_0_ = bf16[64,640]{1,0:T(8,128)(2,1)S(1)} custom-call(s32[3]{0:T(128)S(1)} %pad_add_fusion.index, s32[2,1,2]{2,1,0:T(1,128)S(1)} %copy-done, bf16[64,896]{1,0:T(8,128)(2,1)S(1)} %collective-permute-done.10.refs_0_, bf16[64,896]{1,0:T(8,128)(2,1)S(1)} %collective-permute-done.11.refs_1_, ...), custom_call_target="tpu_custom_call" | custom-call | tf_op jit(solution)/shard_map/pallas_call | solution.py:405
  34.5 1.4 %collective-permute-start.13 = (bf16[64,640]{1,0:T(8,128)(2,1)S(1)}, bf16[64,640]{1,0:T(8,128)(2,1)S(1)}, u32[]{:S(2)}, u32[]{:S(2)}) collective-permute-start(bf16[64,640]{1,0:T(8,128)(2,1)S(1)} %shard_map.82.refs_0_), channel_id=1, source_target_pairs={{0,3},{1,2},{2,1},{3,0},{4,7},{5,6},{6,5},{7,4},{8,11},{9,10},{10,... | collective-permute-start | bytes 245768 | tf_op jit(solution)/shard_map/ppermute | solution.py:435
  35.8 1.4 %collective-permute-start.14 = (bf16[64,640]{1,0:T(8,128)(2,1)S(1)}, bf16[64,640]{1,0:T(8,128)(2,1)S(1)}, u32[]{:S(2)}, u32[]{:S(2)}) collective-permute-start(bf16[64,640]{1,0:T(8,128)(2,1)S(1)} %shard_map.82.refs_0_), channel_id=1, source_target_pairs={{0,2},{1,3},{2,0},{3,1},{4,6},{5,7},{6,4},{7,5},{8,10},{9,11},{10,... | collective-permute-start | bytes 245768 | tf_op jit(solution)/shard_map/ppermute | solution.py:435
  37.2 0.8 %collective-permute-start.15 = (bf16[64,640]{1,0:T(8,128)(2,1)S(1)}, bf16[64,640]{1,0:T(8,128)(2,1)S(1)}, u32[]{:S(2)}, u32[]{:S(2)}) collective-permute-start(bf16[64,640]{1,0:T(8,128)(2,1)S(1)} %shard_map.82.refs_0_), channel_id=1, source_target_pairs={{0,1},{1,0},{2,3},{3,2},{4,5},{5,4},{6,7},{7,6},{8,9},{9,8},{10,11... | collective-permute-start | bytes 245768 | tf_op jit(solution)/shard_map/ppermute | solution.py:435
  38.0 2.5 %collective-permute-done.13.refs_1_ = bf16[64,640]{1,0:T(8,128)(2,1)S(1)} collective-permute-done((bf16[64,640]{1,0:T(8,128)(2,1)S(1)}, bf16[64,640]{1,0:T(8,128)(2,1)S(1)}, u32[]{:S(2)}, u32[]{:S(2)}) %collective-permute-start.13) | collective-permute-done | bytes 81952 | tf_op jit(solution)/shard_map/ppermute | solution.py:435
  40.5 0.5 collective-permute-done.14.refs_2_
  41.0 0.7 %collective-permute-done.15.refs_3_ = bf16[64,640]{1,0:T(8,128)(2,1)S(1)} collective-permute-done((bf16[64,640]{1,0:T(8,128)(2,1)S(1)}, bf16[64,640]{1,0:T(8,128)(2,1)S(1)}, u32[]{:S(2)}, u32[]{:S(2)}) %collective-permute-start.15) | collective-permute-done | bytes 81952 | tf_op jit(solution)/shard_map/ppermute | solution.py:435
  41.7 1.3 %shard_map.83 = (f32[2,256,256]{2,1,0:T(8,128)S(1)}, bf16[2,256,256]{2,1,0:T(8,128)(2,1)S(1)}, bf16[640,256]{1,0:T(8,128)(2,1)S(1)}, bf16[256,64]{1,0:T(8,128)(2,1)S(1)}, bf16[64,192]{1,0:T(8,128)(2,1)S(1)}) custom-call(s32[3]{0:T(128)S(1)} %pad_add_fusion.index, bf16[64,640]{1,0:T(8,128)(2,1)S(1)} %shard_map.82.refs_0_, ...), custom_call_target="tpu_custom_call" | custom-call | tf_op jit(solution)/shard_map/pallas_call | solution.py:405
  43.0 0.1 collective-permute-start.17
  43.0 1.0 %shard_map.84 = (f32[2,256,256]{2,1,0:T(8,128)S(1)}, bf16[2,256,256]{2,1,0:T(8,128)(2,1)S(1)}) custom-call(s32[3]{0:T(128)S(1)} %pad_add_fusion.index, bf16[640,256]{1,0:T(8,128)(2,1)S(1)} %get-tuple-element.64.turned_ref, bf16[256,64]{1,0:T(8,128)(2,1)S(1)} %get-tuple-element.65.small_ref, bf16[64,192]{1,0:T(8,128)(2,1)S(1)} %get-tuple-element.66.small_t_ref, ...), custom_call_target="tpu_custom_call" | custom-call | tf_op jit(solution)/shard_map/pallas_call | solution.py:405
  44.1 0.6 collective-permute-start.16
  44.6 0.0 collective-permute-done.17.come_ref
  44.6 0.1 shard_map.86
  44.7 1.5 %collective-permute-start.18 = (bf16[256,256]{1,0:T(8,128)(2,1)S(1)}, bf16[256,256]{1,0:T(8,128)(2,1)S(1)}, u32[]{:S(2)}, u32[]{:S(2)}) collective-permute-start(bf16[256,256]{1,0:T(8,128)(2,1)S(1)} %get-tuple-element.73), channel_id=1, source_target_pairs={{0,4},{1,5},{2,6},{3,7},{4,0},{5,1},{6,2},{7,3},{8,12},{9,13},{10,... | collective-permute-start | bytes 393224 | tf_op jit(solution)/shard_map/ppermute | solution.py:428
  46.1 0.0 collective-permute-done.16.come_ref
  46.1 0.1 shard_map.85
  46.2 4.0 %collective-permute-done.18.b_ref = bf16[256,256]{1,0:T(8,128)(2,1)S(1)} collective-permute-done((bf16[256,256]{1,0:T(8,128)(2,1)S(1)}, bf16[256,256]{1,0:T(8,128)(2,1)S(1)}, u32[]{:S(2)}, u32[]{:S(2)}) %collective-permute-start.18) | collective-permute-done | bytes 131104 | tf_op jit(solution)/shard_map/ppermute | solution.py:428
  50.3 2.1 %collective-permute-start.19 = (bf16[256,256]{1,0:T(8,128)(2,1)S(1)}, bf16[256,256]{1,0:T(8,128)(2,1)S(1)}, u32[]{:S(2)}, u32[]{:S(2)}) collective-permute-start(bf16[256,256]{1,0:T(8,128)(2,1)S(1)} %shard_map.87), channel_id=1, source_target_pairs={{0,8},{1,9},{2,10},{3,11},{4,12},{5,13},{6,14},{7,15},{8,0},{9,1},... | collective-permute-start | bytes 393224 | tf_op jit(solution)/shard_map/ppermute | solution.py:428
  52.3 1.7 %collective-permute-start.20 = (bf16[256,256]{1,0:T(8,128)(2,1)S(1)}, bf16[256,256]{1,0:T(8,128)(2,1)S(1)}, u32[]{:S(2)}, u32[]{:S(2)}) collective-permute-start(bf16[256,256]{1,0:T(8,128)(2,1)S(1)} %get-tuple-element.75), channel_id=1, source_target_pairs={{0,4},{1,5},{2,6},{3,7},{4,0},{5,1},{6,2},{7,3},{8,12},{9,13},{10,... | collective-permute-start | bytes 393224 | tf_op jit(solution)/shard_map/ppermute | solution.py:428
  54.1 4.7 %collective-permute-done.19.b_ref = bf16[256,256]{1,0:T(8,128)(2,1)S(1)} collective-permute-done((bf16[256,256]{1,0:T(8,128)(2,1)S(1)}, bf16[256,256]{1,0:T(8,128)(2,1)S(1)}, u32[]{:S(2)}, u32[]{:S(2)}) %collective-permute-start.19) | collective-permute-done | bytes 131104 | tf_op jit(solution)/shard_map/ppermute | solution.py:428
  58.8 0.0 collective-permute-done.20.refs_0_
  58.8 0.7 %shard_map.89 = (f32[192,256]{1,0:T(8,128)}, f32[64,256]{1,0:T(8,128)}) custom-call(f32[256,256]{1,0:T(8,128)S(1)} %shard_map.88.keep_ref, bf16[256,256]{1,0:T(8,128)(2,1)S(1)} %collective-permute-done.20.refs_0_), custom_call_target="tpu_custom_call" | custom-call | tf_op jit(solution)/shard_map/pallas_call | solution.py:405
  (3 shorter events, 0.1 us)
Async XLA Ops:
  2.4 14.4 %collective-permute-start.3 = (bf16[2,64,1024]{2,1,0:T(8,128)(2,1)S(1)}, bf16[2,64,1024]{2,1,0:T(8,128)(2,1)S(1)}, u32[]{:S(2)}, u32[]{:S(2)}) collective-permute-start(bf16[2,64,1024]{2,1,0:T(8,128)(2,1)S(1)} %get-tuple-element.41), channel_id=1, source_target_pairs={{0,3},{1,2},{2,1},{3,0},{4,7},{5,6},{6,5},{7,4},{8,11},{9,10},{10,... | collective-permute-start | bytes 786440 | tf_op jit(solution)/shard_map/ppermute | solution.py:435
  6.4 10.4 %copy-start.1 = (bf16[1,4096]{1,0:T(2,128)(2,1)S(1)}, bf16[1,4096]{1,0:T(2,128)(2,1)}, u32[]{:S(2)}) copy-start(bf16[1,4096]{1,0:T(2,128)(2,1)} %param.9) | copy-start | bytes 24580
  6.4 8.8 %collective-permute-start = (bf16[256,256]{1,0:T(8,128)(2,1)S(1)}, bf16[256,256]{1,0:T(8,128)(2,1)S(1)}, u32[]{:S(2)}, u32[]{:S(2)}) collective-permute-start(bf16[256,256]{1,0:T(8,128)(2,1)S(1)} %get-tuple-element.42.pack_ref), channel_id=1, source_target_pairs={{0,8},{1,9},{2,10},{3,11},{4,12},{5,13},{6,14},{7,15},{8,0},{9,1},... | collective-permute-start | bytes 393224 | tf_op jit(solution)/shard_map/ppermute | solution.py:428
  8.9 6.4 %collective-permute-start.6 = (bf16[256,256]{1,0:T(8,128)(2,1)S(1)}, bf16[256,256]{1,0:T(8,128)(2,1)S(1)}, u32[]{:S(2)}, u32[]{:S(2)}) collective-permute-start(bf16[256,256]{1,0:T(8,128)(2,1)S(1)} %get-tuple-element.42.pack_ref), channel_id=1, source_target_pairs={{0,4},{1,5},{2,6},{3,7},{4,0},{5,1},{6,2},{7,3},{8,12},{9,13},{10,... | collective-permute-start | bytes 393224 | tf_op jit(solution)/shard_map/ppermute | solution.py:428
  12.2 9.0 %collective-permute-start.4 = (bf16[2,64,1024]{2,1,0:T(8,128)(2,1)S(1)}, bf16[2,64,1024]{2,1,0:T(8,128)(2,1)S(1)}, u32[]{:S(2)}, u32[]{:S(2)}) collective-permute-start(bf16[2,64,1024]{2,1,0:T(8,128)(2,1)S(1)} %get-tuple-element.45), channel_id=1, source_target_pairs={{0,2},{1,3},{2,0},{3,1},{4,6},{5,7},{6,4},{7,5},{8,10},{9,11},{10,... | collective-permute-start | bytes 786440 | tf_op jit(solution)/shard_map/ppermute | solution.py:435
  12.8 8.5 %collective-permute-start.5 = (bf16[2,64,1024]{2,1,0:T(8,128)(2,1)S(1)}, bf16[2,64,1024]{2,1,0:T(8,128)(2,1)S(1)}, u32[]{:S(2)}, u32[]{:S(2)}) collective-permute-start(bf16[2,64,1024]{2,1,0:T(8,128)(2,1)S(1)} %get-tuple-element.46), channel_id=1, source_target_pairs={{0,1},{1,0},{2,3},{3,2},{4,5},{5,4},{6,7},{7,6},{8,9},{9,8},{10,11... | collective-permute-start | bytes 786440 | tf_op jit(solution)/shard_map/ppermute | solution.py:435
  15.3 3.3 %collective-permute-start.9 = (bf16[256,256]{1,0:T(8,128)(2,1)S(1)}, bf16[256,256]{1,0:T(8,128)(2,1)S(1)}, u32[]{:S(2)}, u32[]{:S(2)}) collective-permute-start(bf16[256,256]{1,0:T(8,128)(2,1)S(1)} %collective-permute-done.refs_6_), channel_id=1, source_target_pairs={{0,16},{16,0},{1,17},{17,1},{2,18},{18,2},{3,19},{19,3},{4,20},{20... | collective-permute-start | bytes 393224 | tf_op jit(solution)/shard_map/ppermute | solution.py:431
  15.3 5.9 %collective-permute-start.1 = (bf16[256,256]{1,0:T(8,128)(2,1)S(1)}, bf16[256,256]{1,0:T(8,128)(2,1)S(1)}, u32[]{:S(2)}, u32[]{:S(2)}) collective-permute-start(bf16[256,256]{1,0:T(8,128)(2,1)S(1)} %collective-permute-done.refs_6_), channel_id=1, source_target_pairs={{0,4},{1,5},{2,6},{3,7},{4,0},{5,1},{6,2},{7,3},{8,12},{9,13},{10,... | collective-permute-start | bytes 393224 | tf_op jit(solution)/shard_map/ppermute | solution.py:428
  18.3 3.0 %collective-permute-start.7 = (bf16[272,256]{1,0:T(8,128)(2,1)S(1)}, bf16[272,256]{1,0:T(8,128)(2,1)S(1)}, u32[]{:S(2)}, u32[]{:S(2)}) collective-permute-start(bf16[272,256]{1,0:T(8,128)(2,1)S(1)} %get-tuple-element.47.refs_4_), channel_id=1, source_target_pairs={{0,16},{16,0},{1,17},{17,1},{2,18},{18,2},{3,19},{19,3},{4,20},{20... | collective-permute-start | bytes 417800 | tf_op jit(solution)/shard_map/ppermute | solution.py:431
  18.6 2.7 %collective-permute-start.8 = (bf16[256,256]{1,0:T(8,128)(2,1)S(1)}, bf16[256,256]{1,0:T(8,128)(2,1)S(1)}, u32[]{:S(2)}, u32[]{:S(2)}) collective-permute-start(bf16[256,256]{1,0:T(8,128)(2,1)S(1)} %collective-permute-done.6.refs_5_), channel_id=1, source_target_pairs={{0,16},{16,0},{1,17},{17,1},{2,18},{18,2},{3,19},{19,3},{4,20},{20... | collective-permute-start | bytes 393224 | tf_op jit(solution)/shard_map/ppermute | solution.py:431
  21.2 1.3 %collective-permute-start.2 = (bf16[256,256]{1,0:T(8,128)(2,1)S(1)}, bf16[256,256]{1,0:T(8,128)(2,1)S(1)}, u32[]{:S(2)}, u32[]{:S(2)}) collective-permute-start(bf16[256,256]{1,0:T(8,128)(2,1)S(1)} %collective-permute-done.1.own), channel_id=1, source_target_pairs={{0,16},{16,0},{1,17},{17,1},{2,18},{18,2},{3,19},{19,3},{4,20},{20... | collective-permute-start | bytes 393224 | tf_op jit(solution)/shard_map/ppermute | solution.py:431
  23.5 7.0 %collective-permute-start.10 = (bf16[64,896]{1,0:T(8,128)(2,1)S(1)}, bf16[64,896]{1,0:T(8,128)(2,1)S(1)}, u32[]{:S(2)}, u32[]{:S(2)}) collective-permute-start(bf16[64,896]{1,0:T(8,128)(2,1)S(1)} %get-tuple-element.56), channel_id=1, source_target_pairs={{0,3},{1,2},{2,1},{3,0},{4,7},{5,6},{6,5},{7,4},{8,11},{9,10},{10,... | collective-permute-start | bytes 344072 | tf_op jit(solution)/shard_map/ppermute | solution.py:435
  24.0 7.7 %collective-permute-start.11 = (bf16[64,896]{1,0:T(8,128)(2,1)S(1)}, bf16[64,896]{1,0:T(8,128)(2,1)S(1)}, u32[]{:S(2)}, u32[]{:S(2)}) collective-permute-start(bf16[64,896]{1,0:T(8,128)(2,1)S(1)} %get-tuple-element.57), channel_id=1, source_target_pairs={{0,2},{1,3},{2,0},{3,1},{4,6},{5,7},{6,4},{7,5},{8,10},{9,11},{10,... | collective-permute-start | bytes 344072 | tf_op jit(solution)/shard_map/ppermute | solution.py:435
  25.6 6.1 %copy-start = (s32[2,1,2]{2,1,0:T(1,128)S(1)}, s32[2,1,2]{2,1,0:T(1,128)}, u32[]{:S(2)}) copy-start(s32[2,1,2]{2,1,0:T(1,128)} %docs.1) | copy-start | bytes 52
  25.6 6.1 %collective-permute-start.12 = (bf16[64,896]{1,0:T(8,128)(2,1)S(1)}, bf16[64,896]{1,0:T(8,128)(2,1)S(1)}, u32[]{:S(2)}, u32[]{:S(2)}) collective-permute-start(bf16[64,896]{1,0:T(8,128)(2,1)S(1)} %get-tuple-element.58), channel_id=1, source_target_pairs={{0,1},{1,0},{2,3},{3,2},{4,5},{5,4},{6,7},{7,6},{8,9},{9,8},{10,11... | collective-permute-start | bytes 344072 | tf_op jit(solution)/shard_map/ppermute | solution.py:435
  34.5 6.0 %collective-permute-start.13 = (bf16[64,640]{1,0:T(8,128)(2,1)S(1)}, bf16[64,640]{1,0:T(8,128)(2,1)S(1)}, u32[]{:S(2)}, u32[]{:S(2)}) collective-permute-start(bf16[64,640]{1,0:T(8,128)(2,1)S(1)} %shard_map.82.refs_0_), channel_id=1, source_target_pairs={{0,3},{1,2},{2,1},{3,0},{4,7},{5,6},{6,5},{7,4},{8,11},{9,10},{10,... | collective-permute-start | bytes 245768 | tf_op jit(solution)/shard_map/ppermute | solution.py:435
  35.8 5.1 %collective-permute-start.14 = (bf16[64,640]{1,0:T(8,128)(2,1)S(1)}, bf16[64,640]{1,0:T(8,128)(2,1)S(1)}, u32[]{:S(2)}, u32[]{:S(2)}) collective-permute-start(bf16[64,640]{1,0:T(8,128)(2,1)S(1)} %shard_map.82.refs_0_), channel_id=1, source_target_pairs={{0,2},{1,3},{2,0},{3,1},{4,6},{5,7},{6,4},{7,5},{8,10},{9,11},{10,... | collective-permute-start | bytes 245768 | tf_op jit(solution)/shard_map/ppermute | solution.py:435
  37.2 4.4 %collective-permute-start.15 = (bf16[64,640]{1,0:T(8,128)(2,1)S(1)}, bf16[64,640]{1,0:T(8,128)(2,1)S(1)}, u32[]{:S(2)}, u32[]{:S(2)}) collective-permute-start(bf16[64,640]{1,0:T(8,128)(2,1)S(1)} %shard_map.82.refs_0_), channel_id=1, source_target_pairs={{0,1},{1,0},{2,3},{3,2},{4,5},{5,4},{6,7},{7,6},{8,9},{9,8},{10,11... | collective-permute-start | bytes 245768 | tf_op jit(solution)/shard_map/ppermute | solution.py:435
  43.0 1.7 %collective-permute-start.17 = (bf16[2,256,256]{2,1,0:T(8,128)(2,1)S(1)}, bf16[2,256,256]{2,1,0:T(8,128)(2,1)S(1)}, u32[]{:S(2)}, u32[]{:S(2)}) collective-permute-start(bf16[2,256,256]{2,1,0:T(8,128)(2,1)S(1)} %get-tuple-element.71), channel_id=1, source_target_pairs={{0,16},{16,0},{1,17},{17,1},{2,18},{18,2},{3,19},{19,3},{4,20},{20... | collective-permute-start | bytes 786440 | tf_op jit(solution)/shard_map/ppermute | solution.py:431
  44.1 2.1 %collective-permute-start.16 = (bf16[2,256,256]{2,1,0:T(8,128)(2,1)S(1)}, bf16[2,256,256]{2,1,0:T(8,128)(2,1)S(1)}, u32[]{:S(2)}, u32[]{:S(2)}) collective-permute-start(bf16[2,256,256]{2,1,0:T(8,128)(2,1)S(1)} %get-tuple-element.68), channel_id=1, source_target_pairs={{0,16},{16,0},{1,17},{17,1},{2,18},{18,2},{3,19},{19,3},{4,20},{20... | collective-permute-start | bytes 786440 | tf_op jit(solution)/shard_map/ppermute | solution.py:431
  44.7 5.5 %collective-permute-start.18 = (bf16[256,256]{1,0:T(8,128)(2,1)S(1)}, bf16[256,256]{1,0:T(8,128)(2,1)S(1)}, u32[]{:S(2)}, u32[]{:S(2)}) collective-permute-start(bf16[256,256]{1,0:T(8,128)(2,1)S(1)} %get-tuple-element.73), channel_id=1, source_target_pairs={{0,4},{1,5},{2,6},{3,7},{4,0},{5,1},{6,2},{7,3},{8,12},{9,13},{10,... | collective-permute-start | bytes 393224 | tf_op jit(solution)/shard_map/ppermute | solution.py:428
  50.3 8.5 %collective-permute-start.19 = (bf16[256,256]{1,0:T(8,128)(2,1)S(1)}, bf16[256,256]{1,0:T(8,128)(2,1)S(1)}, u32[]{:S(2)}, u32[]{:S(2)}) collective-permute-start(bf16[256,256]{1,0:T(8,128)(2,1)S(1)} %shard_map.87), channel_id=1, source_target_pairs={{0,8},{1,9},{2,10},{3,11},{4,12},{5,13},{6,14},{7,15},{8,0},{9,1},... | collective-permute-start | bytes 393224 | tf_op jit(solution)/shard_map/ppermute | solution.py:428
  52.3 6.5 %collective-permute-start.20 = (bf16[256,256]{1,0:T(8,128)(2,1)S(1)}, bf16[256,256]{1,0:T(8,128)(2,1)S(1)}, u32[]{:S(2)}, u32[]{:S(2)}) collective-permute-start(bf16[256,256]{1,0:T(8,128)(2,1)S(1)} %get-tuple-element.75), channel_id=1, source_target_pairs={{0,4},{1,5},{2,6},{3,7},{4,0},{5,1},{6,2},{7,3},{8,12},{9,13},{10,... | collective-permute-start | bytes 393224 | tf_op jit(solution)/shard_map/ppermute | solution.py:428

commit v17 on v15

--- a/solution.py
+++ b/solution.py
@@ -197,10 +197,8 @@
         vx_ref[at, qkv : qkv + heads, :] = zero[qkv : qkv + heads]
         vx_ref[at, qkv + heads : 2 * qkv + heads, :] = (one[:qkv].astype(F32) * gain_ref[at, 1:2, :]).astype(BF16)
         vx_ref[at, 2 * qkv + heads :, :] = empty
-        vc_ref[at, :heads, :] = empty
-        vc_ref[at, heads : 2 * heads, :] = one[qkv : qkv + heads]
-        vc_ref[at, 2 * heads : 3 * heads, :] = zero[qkv : qkv + heads]
-        vc_ref[at, 3 * heads :, :] = empty
+        vc_ref[at, :heads, :] = one[qkv : qkv + heads]
+        vc_ref[at, heads:, :] = zero[qkv : qkv + heads]
     for k in range(PLANE):
         x_ref[p ^ k] = blocks[-k][0]
         c_ref[p ^ k] = blocks[-k][1]
@@ -222,10 +220,10 @@
     half = 2 * heads
     lane = lax.broadcasted_iota(jnp.int32, (rows, half), 1)
     high = squares.astype(BF16).astype(F32)
-    last = jnp.where(lane == heads, high, jnp.where(lane == heads + 1, squares - high, with_c[:, half:]))
+    last = jnp.where(lane == heads, high, jnp.where(lane == heads + 1, squares - high, with_x[:, 3 * half :]))
     sum_ref[:, : 3 * half] = with_x[:, : 3 * half].astype(BF16)
-    sum_ref[:, 3 * half : 4 * half] = (with_x[:, 3 * half :] + with_c[:, :half]).astype(BF16)
-    sum_ref[:, 4 * half :] = last.astype(BF16)
+    sum_ref[:, 3 * half : 4 * half] = last.astype(BF16)
+    sum_ref[:, 4 * half :] = with_c.astype(BF16)
     block = rows // PLANE
     for k in range(PLANE):
         start = pl.multiple_of((p ^ k) * block, block)
@@ -273,8 +271,8 @@
         allowed = allowed & ((query_at >= end) == (key_at >= end))
     x_out = total[:, qkv : 2 * half]
     x_one = total[:, 2 * half : 2 * half + qkv]
-    tail = total[:, 4 * half : 5 * half]
-    c_one, c_zero = total[:, 4 * half - heads : 4 * half].astype(BF16), tail[:, :heads]
+    tail = total[:, 3 * half : 4 * half]
+    c_one, c_zero = total[:, 4 * half : 4 * half + heads].astype(BF16), total[:, 4 * half + heads : 5 * half]
     lane = lax.broadcasted_iota(jnp.int32, tail.shape, 1)
     squares = jnp.sum(jnp.where((lane == heads) | (lane == heads + 1), tail, 0.0), axis=1, keepdims=True)
     mixed = total[:, 5 * half : 5 * half + qkv].astype(BF16)
@@ -294,8 +292,11 @@
     e1 = d_qkv1 * scale1
     d_att0 = c_zero + nt(e1.astype(BF16), mixed) - inner * y_out
     e0 = attention_grad(qkv0, probs0, att0, d_att0.astype(BF16), heads) * scale0
-    factors = [e0, wide0, e1, wide0 * inner, att1.astype(F32), jnp.zeros((rows, heads), F32)]
-    out_ref[...] = jnp.concatenate(factors, axis=1).astype(BF16)
+    factors = jnp.concatenate([e0, wide0, e1, wide0 * inner], axis=1).astype(BF16)
+    for g in range(4):
+        out_ref[g * rows : (g + 1) * rows, :] = factors[:, g * half : (g + 1) * half]
+    wide1 = att1.astype(F32)
+    out_ref[4 * rows :, :] = jnp.concatenate([wide1[: rows // 2], wide1[rows // 2 :]], axis=1).astype(BF16)
 
 
 def pieces_of(planes, heads, order, index, turned, small, small_t, x_ref, c_ref, vx_ref, gain_ref, keep_ref, send_ref):
@@ -326,9 +327,14 @@
     keep_ref, send_ref, turned_ref, small_ref, small_t_ref, all_ref = refs[PLANE + 4 :]
     qkv, half = 3 * heads, 2 * heads
     p = index[2]
+    block = all_ref.shape[1]
     for k in range(PLANE):
-        all_ref[p ^ k] = factors[k][...]
-    rows = all_ref.shape[0] * all_ref.shape[1]
+        for g in range(4):
+            all_ref[p ^ k, :, g * half : (g + 1) * half] = factors[k][g * block : (g + 1) * block, :]
+        folded = factors[k][4 * block :, :]
+        last = jnp.concatenate([folded[:, :heads].astype(F32), folded[:, heads:].astype(F32)], axis=0)
+        all_ref[p ^ k, :, 4 * half :] = jnp.concatenate([last, jnp.zeros_like(last)], axis=1).astype(BF16)
+    rows = all_ref.shape[0] * block
     turned = jnp.transpose(all_ref[...].astype(F32).reshape(rows, 5 * half)).astype(BF16)
     att0, right = turned[qkv : qkv + heads], turned[2 * half : 4 * half]
     small = nt(right, att0).astype(BF16)
@@ -460,11 +466,11 @@
         [split, split, ((planes, 4 * half, width), BF16), ((planes, 8, width), F32)]
         + [((block, 7 * half), BF16)] * PLANE,
         index, blocks[0], *blocks[:0:-1], *own, *other, scalars=1,
-        scratch=[((planes, 2 * half, width), BF16), ((rows, 5 * half), BF16)] + [((shards, width), F32)] * 2,
+        scratch=[((planes, half, width), BF16), ((rows, 5 * half), BF16)] + [((shards, width), F32)] * 2,
     )
     (factors,) = call(
         functools.partial(chain_kernel, features, heads),
-        [((block, 5 * half), BF16)],
+        [((9 * block // 2, half), BF16)],
         index, doc_lengths, *exchange(sent)[::-1], scalars=2,
     )
     piece = (qkv_rows + heads, width)

time: 59.7 us -> 59.8 us (level)
  no operation moved by 1% of the time
where the time goes in v17:
time: 59.8 us; the launch traced here: 59.5 us
  starting transfers between devices  24.1 us (40%)
  waiting for transfers between devices  21.9 us (37%)
  Pallas kernels  12.5 us (21%)
  between operations  0.76 us (1%)
    ppermute x6, waiting for transfers between devices, along_z(): return lax.ppermute(value, 'dp', route)  12.7 us
    ppermute x9, starting transfers between devices, along_plane(): return lax.ppermute(value, 'dp', route)  12.2 us
    ppermute x6, starting transfers between devices, along_z(): return lax.ppermute(value, 'dp', route)  10.3 us
    ppermute x9, waiting for transfers between devices, along_plane(): return lax.ppermute(value, 'dp', route)  8.11 us
    pallas_call x9, Pallas kernels, call(): pl.pallas_call(kernel, out_shape=[jax.ShapeDtypeStruct(shape, dtype) for...  7.65 us
    ppermute x6, starting transfers between devices, to_sibling(): return lax.ppermute(value, 'section', [(0, 1), (1, 0)])  1.71 us
    pallas_call x1, Pallas kernels, planar(): pl.pallas_call(functools.partial(blocks_kernel, planes), out_shape=[one_b...  1.69 us
    pallas_call x1, Pallas kernels, planar(): pl.pallas_call(functools.partial(first_kernel, planes), out_shape=[jax.Sh...  1.66 us
  transfers between devices with their start and end apart: 21, of which 12 were waited for; matrix products, arithmetic and copies ran while one was open for 0% of the time, Pallas kernels for 7%

profile of v17, /device:TPU:0, one launch (start us, length us, event | category | flops | bytes accessed | tf_op | source)
XLA Modules:
  0.0 59.5 jit_solution(11862429068203494511)
XLA Ops:
  0.6 0.1 pad_add_fusion.index
  0.7 1.7 %shard_map.77 = (bf16[256,256]{1,0:T(8,128)(2,1)S(1)}, bf16[2,64,1024]{2,1,0:T(8,128)(2,1)S(1)}) custom-call(s32[3]{0:T(128)S(1)} %pad_add_fusion.index, bf16[192,256]{1,0:T(8,128)(2,1)} %bitcast.11, bf16[64,256]{1,0:T(8,128)(2,1)} %bitcast.12, bf16[2,64,4096]{2,1,0:T(8,128)(2,1)} %x_ref.5, bf16[2,64,4096]{2,1,0:T(8,128)(2,1)} %c_ref.5), custom_call_target="tpu_custom_call" | custom-call | tf_op jit(solution)/shard_map/pallas_call | solution.py:426
  2.4 4.0 %collective-permute-start = (bf16[2,64,1024]{2,1,0:T(8,128)(2,1)S(1)}, bf16[2,64,1024]{2,1,0:T(8,128)(2,1)S(1)}, u32[]{:S(2)}, u32[]{:S(2)}) collective-permute-start(bf16[2,64,1024]{2,1,0:T(8,128)(2,1)S(1)} %get-tuple-element.34), channel_id=1, source_target_pairs={{0,3},{1,2},{2,1},{3,0},{4,7},{5,6},{6,5},{7,4},{8,11},{9,10},{10,... | collective-permute-start | bytes 786440 | tf_op jit(solution)/shard_map/ppermute | solution.py:413
  6.4 0.0 copy-start.1
  6.4 2.6 %collective-permute-start.4 = (bf16[256,256]{1,0:T(8,128)(2,1)S(1)}, bf16[256,256]{1,0:T(8,128)(2,1)S(1)}, u32[]{:S(2)}, u32[]{:S(2)}) collective-permute-start(bf16[256,256]{1,0:T(8,128)(2,1)S(1)} %get-tuple-element.35.pack_ref), channel_id=1, source_target_pairs={{0,8},{1,9},{2,10},{3,11},{4,12},{5,13},{6,14},{7,15},{8,0},{9,1},... | collective-permute-start | bytes 393224 | tf_op jit(solution)/shard_map/ppermute | solution.py:406
  8.9 1.6 %collective-permute-start.3 = (bf16[256,256]{1,0:T(8,128)(2,1)S(1)}, bf16[256,256]{1,0:T(8,128)(2,1)S(1)}, u32[]{:S(2)}, u32[]{:S(2)}) collective-permute-start(bf16[256,256]{1,0:T(8,128)(2,1)S(1)} %get-tuple-element.35.pack_ref), channel_id=1, source_target_pairs={{0,4},{1,5},{2,6},{3,7},{4,0},{5,1},{6,2},{7,3},{8,12},{9,13},{10,... | collective-permute-start | bytes 393224 | tf_op jit(solution)/shard_map/ppermute | solution.py:406
  10.5 1.7 %shard_map.79 = (bf16[2,64,1024]{2,1,0:T(8,128)(2,1)S(1)}, bf16[2,64,1024]{2,1,0:T(8,128)(2,1)S(1)}) custom-call(s32[3]{0:T(128)S(1)} %pad_add_fusion.index, bf16[2,64,4096]{2,1,0:T(8,128)(2,1)} %x_ref.5, bf16[2,64,4096]{2,1,0:T(8,128)(2,1)} %c_ref.5), custom_call_target="tpu_custom_call" | custom-call | tf_op jit(solution)/shard_map/pallas_call | solution.py:434
  12.2 0.6 collective-permute-start.1
  12.8 0.5 collective-permute-start.2
  13.3 1.8 %collective-permute-done.4.refs_6_ = bf16[256,256]{1,0:T(8,128)(2,1)S(1)} collective-permute-done((bf16[256,256]{1,0:T(8,128)(2,1)S(1)}, bf16[256,256]{1,0:T(8,128)(2,1)S(1)}, u32[]{:S(2)}, u32[]{:S(2)}) %collective-permute-start.4) | collective-permute-done | bytes 131104 | tf_op jit(solution)/shard_map/ppermute | solution.py:406
  15.1 0.6 collective-permute-start.5
  15.7 0.0 collective-permute-done.3.refs_5_
  15.7 0.0 collective-permute-start.7
  15.7 0.0 copy-done.1
  15.7 0.1 reduce
  15.8 0.0 collective-permute-done.refs_1_
  15.8 1.5 %shard_map.78 = (bf16[272,256]{1,0:T(8,128)(2,1)S(1)}, bf16[2,64,1024]{2,1,0:T(8,128)(2,1)S(1)}) custom-call(s32[3]{0:T(128)S(1)} %pad_add_fusion.index, bf16[256,256]{1,0:T(8,128)(2,1)S(1)} %get-tuple-element.35.pack_ref, bf16[16,256]{1,0:T(8,128)(2,1)S(1)} %reshape_squeeze.3.gain_ref, bf16[2,64,4096]{2,1,0:T(8,128)(2,1)} %x_ref.5, bf16[2,64,4096]{2,1,0:T(8,128)(2,1)} %c_ref.5), custom_call_target="tpu_custom_call" | custom-call | tf_op jit(solution)/shard_map/pallas_call | solution.py:450
  17.3 0.6 collective-permute-start.6
  17.8 2.2 %collective-permute-done.5.refs_7_ = bf16[256,256]{1,0:T(8,128)(2,1)S(1)} collective-permute-done((bf16[256,256]{1,0:T(8,128)(2,1)S(1)}, bf16[256,256]{1,0:T(8,128)(2,1)S(1)}, u32[]{:S(2)}, u32[]{:S(2)}) %collective-permute-start.5) | collective-permute-done | bytes 131104 | tf_op jit(solution)/shard_map/ppermute | solution.py:406
  20.1 0.0 collective-permute-start.9
  20.1 0.0 collective-permute-done.7.refs_9_
  20.1 0.5 collective-permute-start.8
  20.6 0.0 collective-permute-done.1.refs_2_
  20.6 0.0 collective-permute-done.2.refs_3_
  20.6 0.8 %collective-permute-done.9.refs_11_ = bf16[256,256]{1,0:T(8,128)(2,1)S(1)} collective-permute-done((bf16[256,256]{1,0:T(8,128)(2,1)S(1)}, bf16[256,256]{1,0:T(8,128)(2,1)S(1)}, u32[]{:S(2)}, u32[]{:S(2)}) %collective-permute-start.9) | collective-permute-done | bytes 131104 | tf_op jit(solution)/shard_map/ppermute | solution.py:409
  21.4 0.2 collective-permute-done.8.refs_10_
  21.6 0.0 collective-permute-done.6.refs_8_
  21.6 1.6 %shard_map.80 = (bf16[4,64,1024]{2,1,0:T(8,128)(2,1)S(1)}, bf16[4,64,1024]{2,1,0:T(8,128)(2,1)S(1)}, bf16[4,512,256]{2,1,0:T(8,128)(2,1)S(1)}, f32[4,8,256]{2,1,...) custom-call(s32[3]{0:T(128)S(1)} %pad_add_fusion.index, ...), custom_call_target="tpu_custom_call" | custom-call | tf_op jit(solution)/shard_map/pallas_call | solution.py:383
  23.2 0.7 %collective-permute-start.10 = (bf16[64,896]{1,0:T(8,128)(2,1)S(1)}, bf16[64,896]{1,0:T(8,128)(2,1)S(1)}, u32[]{:S(2)}, u32[]{:S(2)}) collective-permute-start(bf16[64,896]{1,0:T(8,128)(2,1)S(1)} %get-tuple-element.42), channel_id=1, source_target_pairs={{0,3},{1,2},{2,1},{3,0},{4,7},{5,6},{6,5},{7,4},{8,11},{9,10},{10,... | collective-permute-start | bytes 344072 | tf_op jit(solution)/shard_map/ppermute | solution.py:413
  23.9 1.3 %collective-permute-start.11 = (bf16[64,896]{1,0:T(8,128)(2,1)S(1)}, bf16[64,896]{1,0:T(8,128)(2,1)S(1)}, u32[]{:S(2)}, u32[]{:S(2)}) collective-permute-start(bf16[64,896]{1,0:T(8,128)(2,1)S(1)} %get-tuple-element.43), channel_id=1, source_target_pairs={{0,2},{1,3},{2,0},{3,1},{4,6},{5,7},{6,4},{7,5},{8,10},{9,11},{10,... | collective-permute-start | bytes 344072 | tf_op jit(solution)/shard_map/ppermute | solution.py:413
  25.3 0.0 copy-start
  25.3 1.5 %collective-permute-start.12 = (bf16[64,896]{1,0:T(8,128)(2,1)S(1)}, bf16[64,896]{1,0:T(8,128)(2,1)S(1)}, u32[]{:S(2)}, u32[]{:S(2)}) collective-permute-start(bf16[64,896]{1,0:T(8,128)(2,1)S(1)} %get-tuple-element.44), channel_id=1, source_target_pairs={{0,1},{1,0},{2,3},{3,2},{4,5},{5,4},{6,7},{7,6},{8,9},{9,8},{10,11... | collective-permute-start | bytes 344072 | tf_op jit(solution)/shard_map/ppermute | solution.py:413
  26.8 3.4 %collective-permute-done.10.refs_0_ = bf16[64,896]{1,0:T(8,128)(2,1)S(1)} collective-permute-done((bf16[64,896]{1,0:T(8,128)(2,1)S(1)}, bf16[64,896]{1,0:T(8,128)(2,1)S(1)}, u32[]{:S(2)}, u32[]{:S(2)}) %collective-permute-start.10) | collective-permute-done | bytes 114720 | tf_op jit(solution)/shard_map/ppermute | solution.py:413
  30.2 1.3 %collective-permute-done.11.refs_1_ = bf16[64,896]{1,0:T(8,128)(2,1)S(1)} collective-permute-done((bf16[64,896]{1,0:T(8,128)(2,1)S(1)}, bf16[64,896]{1,0:T(8,128)(2,1)S(1)}, u32[]{:S(2)}, u32[]{:S(2)}) %collective-permute-start.11) | collective-permute-done | bytes 114720 | tf_op jit(solution)/shard_map/ppermute | solution.py:413
  31.5 0.0 collective-permute-done.12.refs_2_
  31.5 0.0 copy-done
  31.5 2.8 %shard_map.81.refs_0_ = bf16[288,128]{1,0:T(8,128)(2,1)S(1)} custom-call(s32[3]{0:T(128)S(1)} %pad_add_fusion.index, s32[2,1,2]{2,1,0:T(1,128)S(1)} %copy-done, bf16[64,896]{1,0:T(8,128)(2,1)S(1)} %collective-permute-done.10.refs_0_, bf16[64,896]{1,0:T(8,128)(2,1)S(1)} %collective-permute-done.11.refs_1_, ...), custom_call_target="tpu_custom_call" | custom-call | tf_op jit(solution)/shard_map/pallas_call | solution.py:383
  34.3 1.2 %collective-permute-start.15 = (bf16[288,128]{1,0:T(8,128)(2,1)S(1)}, bf16[288,128]{1,0:T(8,128)(2,1)S(1)}, u32[]{:S(2)}, u32[]{:S(2)}) collective-permute-start(bf16[288,128]{1,0:T(8,128)(2,1)S(1)} %shard_map.81.refs_0_), channel_id=1, source_target_pairs={{0,3},{1,2},{2,1},{3,0},{4,7},{5,6},{6,5},{7,4},{8,11},{9,10},{10,... | collective-permute-start | bytes 221192 | tf_op jit(solution)/shard_map/ppermute | solution.py:413
  35.6 1.4 %collective-permute-start.14 = (bf16[288,128]{1,0:T(8,128)(2,1)S(1)}, bf16[288,128]{1,0:T(8,128)(2,1)S(1)}, u32[]{:S(2)}, u32[]{:S(2)}) collective-permute-start(bf16[288,128]{1,0:T(8,128)(2,1)S(1)} %shard_map.81.refs_0_), channel_id=1, source_target_pairs={{0,2},{1,3},{2,0},{3,1},{4,6},{5,7},{6,4},{7,5},{8,10},{9,11},{10,... | collective-permute-start | bytes 221192 | tf_op jit(solution)/shard_map/ppermute | solution.py:413
  36.9 1.0 %collective-permute-start.13 = (bf16[288,128]{1,0:T(8,128)(2,1)S(1)}, bf16[288,128]{1,0:T(8,128)(2,1)S(1)}, u32[]{:S(2)}, u32[]{:S(2)}) collective-permute-start(bf16[288,128]{1,0:T(8,128)(2,1)S(1)} %shard_map.81.refs_0_), channel_id=1, source_target_pairs={{0,1},{1,0},{2,3},{3,2},{4,5},{5,4},{6,7},{7,6},{8,9},{9,8},{10,11... | collective-permute-start | bytes 221192 | tf_op jit(solution)/shard_map/ppermute | solution.py:413
  37.9 2.3 %collective-permute-done.15.refs_3_ = bf16[288,128]{1,0:T(8,128)(2,1)S(1)} collective-permute-done((bf16[288,128]{1,0:T(8,128)(2,1)S(1)}, bf16[288,128]{1,0:T(8,128)(2,1)S(1)}, u32[]{:S(2)}, u32[]{:S(2)}) %collective-permute-start.15) | collective-permute-done | bytes 73760 | tf_op jit(solution)/shard_map/ppermute | solution.py:413
  40.2 0.3 collective-permute-done.14.refs_2_
  40.5 0.7 %collective-permute-done.13.refs_1_ = bf16[288,128]{1,0:T(8,128)(2,1)S(1)} collective-permute-done((bf16[288,128]{1,0:T(8,128)(2,1)S(1)}, bf16[288,128]{1,0:T(8,128)(2,1)S(1)}, u32[]{:S(2)}, u32[]{:S(2)}) %collective-permute-start.13) | collective-permute-done | bytes 73760 | tf_op jit(solution)/shard_map/ppermute | solution.py:413
  41.3 1.3 %shard_map.82 = (f32[2,256,256]{2,1,0:T(8,128)S(1)}, bf16[2,256,256]{2,1,0:T(8,128)(2,1)S(1)}, bf16[640,256]{1,0:T(8,128)(2,1)S(1)}, bf16[256,64]{1,0:T(8,128)(2,1)S(1)}, bf16[64,192]{1,0:T(8,128)(2,1)S(1)}) custom-call(s32[3]{0:T(128)S(1)} %pad_add_fusion.index, bf16[288,128]{1,0:T(8,128)(2,1)S(1)} %shard_map.81.refs_0_, ...), custom_call_target="tpu_custom_call" | custom-call | tf_op jit(solution)/shard_map/pallas_call | solution.py:383
  42.6 0.1 collective-permute-start.17
  42.7 1.0 %shard_map.83 = (f32[2,256,256]{2,1,0:T(8,128)S(1)}, bf16[2,256,256]{2,1,0:T(8,128)(2,1)S(1)}) custom-call(s32[3]{0:T(128)S(1)} %pad_add_fusion.index, bf16[640,256]{1,0:T(8,128)(2,1)S(1)} %get-tuple-element.50.turned_ref, bf16[256,64]{1,0:T(8,128)(2,1)S(1)} %get-tuple-element.51.small_ref, bf16[64,192]{1,0:T(8,128)(2,1)S(1)} %get-tuple-element.52.small_t_ref, ...), custom_call_target="tpu_custom_call" | custom-call | tf_op jit(solution)/shard_map/pallas_call | solution.py:383
  43.7 0.6 collective-permute-start.16
  44.3 0.0 collective-permute-done.17.come_ref
  44.4 1.1 %collective-permute-start.18 = (bf16[256,256]{1,0:T(8,128)(2,1)S(1)}, bf16[256,256]{1,0:T(8,128)(2,1)S(1)}, u32[]{:S(2)}, u32[]{:S(2)}) collective-permute-start(bf16[256,256]{1,0:T(8,128)(2,1)S(1)} %get-tuple-element.59), channel_id=1, source_target_pairs={{0,4},{1,5},{2,6},{3,7},{4,0},{5,1},{6,2},{7,3},{8,12},{9,13},{10,... | collective-permute-start | bytes 393224 | tf_op jit(solution)/shard_map/ppermute | solution.py:406
  45.4 0.0 collective-permute-done.16.come_ref
  45.5 4.4 %collective-permute-done.18.b_ref = bf16[256,256]{1,0:T(8,128)(2,1)S(1)} collective-permute-done((bf16[256,256]{1,0:T(8,128)(2,1)S(1)}, bf16[256,256]{1,0:T(8,128)(2,1)S(1)}, u32[]{:S(2)}, u32[]{:S(2)}) %collective-permute-start.18) | collective-permute-done | bytes 131104 | tf_op jit(solution)/shard_map/ppermute | solution.py:406
  49.9 2.7 %collective-permute-start.19 = (bf16[256,256]{1,0:T(8,128)(2,1)S(1)}, bf16[256,256]{1,0:T(8,128)(2,1)S(1)}, u32[]{:S(2)}, u32[]{:S(2)}) collective-permute-start(bf16[256,256]{1,0:T(8,128)(2,1)S(1)} %shard_map.86), channel_id=1, source_target_pairs={{0,8},{1,9},{2,10},{3,11},{4,12},{5,13},{6,14},{7,15},{8,0},{9,1},... | collective-permute-start | bytes 393224 | tf_op jit(solution)/shard_map/ppermute | solution.py:406
  52.7 1.7 %collective-permute-start.20 = (bf16[256,256]{1,0:T(8,128)(2,1)S(1)}, bf16[256,256]{1,0:T(8,128)(2,1)S(1)}, u32[]{:S(2)}, u32[]{:S(2)}) collective-permute-start(bf16[256,256]{1,0:T(8,128)(2,1)S(1)} %get-tuple-element.61), channel_id=1, source_target_pairs={{0,4},{1,5},{2,6},{3,7},{4,0},{5,1},{6,2},{7,3},{8,12},{9,13},{10,... | collective-permute-start | bytes 393224 | tf_op jit(solution)/shard_map/ppermute | solution.py:406
  54.4 4.0 %collective-permute-done.19.b_ref = bf16[256,256]{1,0:T(8,128)(2,1)S(1)} collective-permute-done((bf16[256,256]{1,0:T(8,128)(2,1)S(1)}, bf16[256,256]{1,0:T(8,128)(2,1)S(1)}, u32[]{:S(2)}, u32[]{:S(2)}) %collective-permute-start.19) | collective-permute-done | bytes 131104 | tf_op jit(solution)/shard_map/ppermute | solution.py:406
  58.4 0.3 collective-permute-done.20.refs_0_
  58.7 0.7 %shard_map.88 = (f32[192,256]{1,0:T(8,128)}, f32[64,256]{1,0:T(8,128)}) custom-call(f32[256,256]{1,0:T(8,128)S(1)} %shard_map.87.keep_ref, bf16[256,256]{1,0:T(8,128)(2,1)S(1)} %collective-permute-done.20.refs_0_), custom_call_target="tpu_custom_call" | custom-call | tf_op jit(solution)/shard_map/pallas_call | solution.py:383
  (5 shorter events, 0.2 us)
Async XLA Ops:
  2.4 13.4 %collective-permute-start = (bf16[2,64,1024]{2,1,0:T(8,128)(2,1)S(1)}, bf16[2,64,1024]{2,1,0:T(8,128)(2,1)S(1)}, u32[]{:S(2)}, u32[]{:S(2)}) collective-permute-start(bf16[2,64,1024]{2,1,0:T(8,128)(2,1)S(1)} %get-tuple-element.34), channel_id=1, source_target_pairs={{0,3},{1,2},{2,1},{3,0},{4,7},{5,6},{6,5},{7,4},{8,11},{9,10},{10,... | collective-permute-start | bytes 786440 | tf_op jit(solution)/shard_map/ppermute | solution.py:413
  6.4 9.3 %copy-start.1 = (bf16[1,4096]{1,0:T(2,128)(2,1)S(1)}, bf16[1,4096]{1,0:T(2,128)(2,1)}, u32[]{:S(2)}) copy-start(bf16[1,4096]{1,0:T(2,128)(2,1)} %param.9) | copy-start | bytes 24580
  6.4 8.8 %collective-permute-start.4 = (bf16[256,256]{1,0:T(8,128)(2,1)S(1)}, bf16[256,256]{1,0:T(8,128)(2,1)S(1)}, u32[]{:S(2)}, u32[]{:S(2)}) collective-permute-start(bf16[256,256]{1,0:T(8,128)(2,1)S(1)} %get-tuple-element.35.pack_ref), channel_id=1, source_target_pairs={{0,8},{1,9},{2,10},{3,11},{4,12},{5,13},{6,14},{7,15},{8,0},{9,1},... | collective-permute-start | bytes 393224 | tf_op jit(solution)/shard_map/ppermute | solution.py:406
  8.9 6.8 %collective-permute-start.3 = (bf16[256,256]{1,0:T(8,128)(2,1)S(1)}, bf16[256,256]{1,0:T(8,128)(2,1)S(1)}, u32[]{:S(2)}, u32[]{:S(2)}) collective-permute-start(bf16[256,256]{1,0:T(8,128)(2,1)S(1)} %get-tuple-element.35.pack_ref), channel_id=1, source_target_pairs={{0,4},{1,5},{2,6},{3,7},{4,0},{5,1},{6,2},{7,3},{8,12},{9,13},{10,... | collective-permute-start | bytes 393224 | tf_op jit(solution)/shard_map/ppermute | solution.py:406
  12.2 8.4 %collective-permute-start.1 = (bf16[2,64,1024]{2,1,0:T(8,128)(2,1)S(1)}, bf16[2,64,1024]{2,1,0:T(8,128)(2,1)S(1)}, u32[]{:S(2)}, u32[]{:S(2)}) collective-permute-start(bf16[2,64,1024]{2,1,0:T(8,128)(2,1)S(1)} %get-tuple-element.38), channel_id=1, source_target_pairs={{0,2},{1,3},{2,0},{3,1},{4,6},{5,7},{6,4},{7,5},{8,10},{9,11},{10,... | collective-permute-start | bytes 786440 | tf_op jit(solution)/shard_map/ppermute | solution.py:413
  12.8 7.8 %collective-permute-start.2 = (bf16[2,64,1024]{2,1,0:T(8,128)(2,1)S(1)}, bf16[2,64,1024]{2,1,0:T(8,128)(2,1)S(1)}, u32[]{:S(2)}, u32[]{:S(2)}) collective-permute-start(bf16[2,64,1024]{2,1,0:T(8,128)(2,1)S(1)} %get-tuple-element.39), channel_id=1, source_target_pairs={{0,1},{1,0},{2,3},{3,2},{4,5},{5,4},{6,7},{7,6},{8,9},{9,8},{10,11... | collective-permute-start | bytes 786440 | tf_op jit(solution)/shard_map/ppermute | solution.py:413
  15.1 5.0 %collective-permute-start.5 = (bf16[256,256]{1,0:T(8,128)(2,1)S(1)}, bf16[256,256]{1,0:T(8,128)(2,1)S(1)}, u32[]{:S(2)}, u32[]{:S(2)}) collective-permute-start(bf16[256,256]{1,0:T(8,128)(2,1)S(1)} %collective-permute-done.4.refs_6_), channel_id=1, source_target_pairs={{0,4},{1,5},{2,6},{3,7},{4,0},{5,1},{6,2},{7,3},{8,12},{9,13},{10,... | collective-permute-start | bytes 393224 | tf_op jit(solution)/shard_map/ppermute | solution.py:406
  15.7 4.4 %collective-permute-start.7 = (bf16[256,256]{1,0:T(8,128)(2,1)S(1)}, bf16[256,256]{1,0:T(8,128)(2,1)S(1)}, u32[]{:S(2)}, u32[]{:S(2)}) collective-permute-start(bf16[256,256]{1,0:T(8,128)(2,1)S(1)} %collective-permute-done.3.refs_5_), channel_id=1, source_target_pairs={{0,16},{16,0},{1,17},{17,1},{2,18},{18,2},{3,19},{19,3},{4,20},{20... | collective-permute-start | bytes 393224 | tf_op jit(solution)/shard_map/ppermute | solution.py:409
  17.3 4.3 %collective-permute-start.6 = (bf16[272,256]{1,0:T(8,128)(2,1)S(1)}, bf16[272,256]{1,0:T(8,128)(2,1)S(1)}, u32[]{:S(2)}, u32[]{:S(2)}) collective-permute-start(bf16[272,256]{1,0:T(8,128)(2,1)S(1)} %get-tuple-element.40.refs_4_), channel_id=1, source_target_pairs={{0,16},{16,0},{1,17},{17,1},{2,18},{18,2},{3,19},{19,3},{4,20},{20... | collective-permute-start | bytes 417800 | tf_op jit(solution)/shard_map/ppermute | solution.py:409
  20.1 1.3 %collective-permute-start.9 = (bf16[256,256]{1,0:T(8,128)(2,1)S(1)}, bf16[256,256]{1,0:T(8,128)(2,1)S(1)}, u32[]{:S(2)}, u32[]{:S(2)}) collective-permute-start(bf16[256,256]{1,0:T(8,128)(2,1)S(1)} %collective-permute-done.5.refs_7_), channel_id=1, source_target_pairs={{0,16},{16,0},{1,17},{17,1},{2,18},{18,2},{3,19},{19,3},{4,20},{20... | collective-permute-start | bytes 393224 | tf_op jit(solution)/shard_map/ppermute | solution.py:409
  20.1 1.5 %collective-permute-start.8 = (bf16[256,256]{1,0:T(8,128)(2,1)S(1)}, bf16[256,256]{1,0:T(8,128)(2,1)S(1)}, u32[]{:S(2)}, u32[]{:S(2)}) collective-permute-start(bf16[256,256]{1,0:T(8,128)(2,1)S(1)} %collective-permute-done.4.refs_6_), channel_id=1, source_target_pairs={{0,16},{16,0},{1,17},{17,1},{2,18},{18,2},{3,19},{19,3},{4,20},{20... | collective-permute-start | bytes 393224 | tf_op jit(solution)/shard_map/ppermute | solution.py:409
  23.2 7.0 %collective-permute-start.10 = (bf16[64,896]{1,0:T(8,128)(2,1)S(1)}, bf16[64,896]{1,0:T(8,128)(2,1)S(1)}, u32[]{:S(2)}, u32[]{:S(2)}) collective-permute-start(bf16[64,896]{1,0:T(8,128)(2,1)S(1)} %get-tuple-element.42), channel_id=1, source_target_pairs={{0,3},{1,2},{2,1},{3,0},{4,7},{5,6},{6,5},{7,4},{8,11},{9,10},{10,... | collective-permute-start | bytes 344072 | tf_op jit(solution)/shard_map/ppermute | solution.py:413
  23.9 7.6 %collective-permute-start.11 = (bf16[64,896]{1,0:T(8,128)(2,1)S(1)}, bf16[64,896]{1,0:T(8,128)(2,1)S(1)}, u32[]{:S(2)}, u32[]{:S(2)}) collective-permute-start(bf16[64,896]{1,0:T(8,128)(2,1)S(1)} %get-tuple-element.43), channel_id=1, source_target_pairs={{0,2},{1,3},{2,0},{3,1},{4,6},{5,7},{6,4},{7,5},{8,10},{9,11},{10,... | collective-permute-start | bytes 344072 | tf_op jit(solution)/shard_map/ppermute | solution.py:413
  25.3 6.2 %copy-start = (s32[2,1,2]{2,1,0:T(1,128)S(1)}, s32[2,1,2]{2,1,0:T(1,128)}, u32[]{:S(2)}) copy-start(s32[2,1,2]{2,1,0:T(1,128)} %docs.1) | copy-start | bytes 52
  25.3 6.2 %collective-permute-start.12 = (bf16[64,896]{1,0:T(8,128)(2,1)S(1)}, bf16[64,896]{1,0:T(8,128)(2,1)S(1)}, u32[]{:S(2)}, u32[]{:S(2)}) collective-permute-start(bf16[64,896]{1,0:T(8,128)(2,1)S(1)} %get-tuple-element.44), channel_id=1, source_target_pairs={{0,1},{1,0},{2,3},{3,2},{4,5},{5,4},{6,7},{7,6},{8,9},{9,8},{10,11... | collective-permute-start | bytes 344072 | tf_op jit(solution)/shard_map/ppermute | solution.py:413
  34.3 5.9 %collective-permute-start.15 = (bf16[288,128]{1,0:T(8,128)(2,1)S(1)}, bf16[288,128]{1,0:T(8,128)(2,1)S(1)}, u32[]{:S(2)}, u32[]{:S(2)}) collective-permute-start(bf16[288,128]{1,0:T(8,128)(2,1)S(1)} %shard_map.81.refs_0_), channel_id=1, source_target_pairs={{0,3},{1,2},{2,1},{3,0},{4,7},{5,6},{6,5},{7,4},{8,11},{9,10},{10,... | collective-permute-start | bytes 221192 | tf_op jit(solution)/shard_map/ppermute | solution.py:413
  35.6 5.0 %collective-permute-start.14 = (bf16[288,128]{1,0:T(8,128)(2,1)S(1)}, bf16[288,128]{1,0:T(8,128)(2,1)S(1)}, u32[]{:S(2)}, u32[]{:S(2)}) collective-permute-start(bf16[288,128]{1,0:T(8,128)(2,1)S(1)} %shard_map.81.refs_0_), channel_id=1, source_target_pairs={{0,2},{1,3},{2,0},{3,1},{4,6},{5,7},{6,4},{7,5},{8,10},{9,11},{10,... | collective-permute-start | bytes 221192 | tf_op jit(solution)/shard_map/ppermute | solution.py:413
  36.9 4.4 %collective-permute-start.13 = (bf16[288,128]{1,0:T(8,128)(2,1)S(1)}, bf16[288,128]{1,0:T(8,128)(2,1)S(1)}, u32[]{:S(2)}, u32[]{:S(2)}) collective-permute-start(bf16[288,128]{1,0:T(8,128)(2,1)S(1)} %shard_map.81.refs_0_), channel_id=1, source_target_pairs={{0,1},{1,0},{2,3},{3,2},{4,5},{5,4},{6,7},{7,6},{8,9},{9,8},{10,11... | collective-permute-start | bytes 221192 | tf_op jit(solution)/shard_map/ppermute | solution.py:413
  42.6 1.7 %collective-permute-start.17 = (bf16[2,256,256]{2,1,0:T(8,128)(2,1)S(1)}, bf16[2,256,256]{2,1,0:T(8,128)(2,1)S(1)}, u32[]{:S(2)}, u32[]{:S(2)}) collective-permute-start(bf16[2,256,256]{2,1,0:T(8,128)(2,1)S(1)} %get-tuple-element.57), channel_id=1, source_target_pairs={{0,16},{16,0},{1,17},{17,1},{2,18},{18,2},{3,19},{19,3},{4,20},{20... | collective-permute-start | bytes 786440 | tf_op jit(solution)/shard_map/ppermute | solution.py:409
  43.7 1.7 %collective-permute-start.16 = (bf16[2,256,256]{2,1,0:T(8,128)(2,1)S(1)}, bf16[2,256,256]{2,1,0:T(8,128)(2,1)S(1)}, u32[]{:S(2)}, u32[]{:S(2)}) collective-permute-start(bf16[2,256,256]{2,1,0:T(8,128)(2,1)S(1)} %get-tuple-element.54), channel_id=1, source_target_pairs={{0,16},{16,0},{1,17},{17,1},{2,18},{18,2},{3,19},{19,3},{4,20},{20... | collective-permute-start | bytes 786440 | tf_op jit(solution)/shard_map/ppermute | solution.py:409
  44.4 5.5 %collective-permute-start.18 = (bf16[256,256]{1,0:T(8,128)(2,1)S(1)}, bf16[256,256]{1,0:T(8,128)(2,1)S(1)}, u32[]{:S(2)}, u32[]{:S(2)}) collective-permute-start(bf16[256,256]{1,0:T(8,128)(2,1)S(1)} %get-tuple-element.59), channel_id=1, source_target_pairs={{0,4},{1,5},{2,6},{3,7},{4,0},{5,1},{6,2},{7,3},{8,12},{9,13},{10,... | collective-permute-start | bytes 393224 | tf_op jit(solution)/shard_map/ppermute | solution.py:406
  49.9 8.4 %collective-permute-start.19 = (bf16[256,256]{1,0:T(8,128)(2,1)S(1)}, bf16[256,256]{1,0:T(8,128)(2,1)S(1)}, u32[]{:S(2)}, u32[]{:S(2)}) collective-permute-start(bf16[256,256]{1,0:T(8,128)(2,1)S(1)} %shard_map.86), channel_id=1, source_target_pairs={{0,8},{1,9},{2,10},{3,11},{4,12},{5,13},{6,14},{7,15},{8,0},{9,1},... | collective-permute-start | bytes 393224 | tf_op jit(solution)/shard_map/ppermute | solution.py:406
  52.7 6.1 %collective-permute-start.20 = (bf16[256,256]{1,0:T(8,128)(2,1)S(1)}, bf16[256,256]{1,0:T(8,128)(2,1)S(1)}, u32[]{:S(2)}, u32[]{:S(2)}) collective-permute-start(bf16[256,256]{1,0:T(8,128)(2,1)S(1)} %get-tuple-element.61), channel_id=1, source_target_pairs={{0,4},{1,5},{2,6},{3,7},{4,0},{5,1},{6,2},{7,3},{8,12},{9,13},{10,... | collective-permute-start | bytes 393224 | tf_op jit(solution)/shard_map/ppermute | solution.py:406

commit v18 on v16

--- a/solution.py
+++ b/solution.py
@@ -468,7 +468,7 @@
     for step in reversed([1 << bit for bit in range(planes.bit_length() - 1)]):
         for k in list(pieces):
             pieces[k ^ step] = along_z(pieces[k], step)
-    mine, late_gain, _ = lax.optimization_barrier((pack, gain, blocks[3]))
+    mine, late_gain, _ = lax.optimization_barrier((pack, gain, pieces[1]))
     marked, blocks[0] = pl.pallas_call(
         functools.partial(mark_kernel, planes),
         out_shape=[jax.ShapeDtypeStruct((qkv_rows + heads + shards, width), BF16), one_block],
@@ -477,7 +477,8 @@
         scratch_shapes=[pltpu.SemaphoreType.DMA((2 * planes,))],
         compiler_params=params,
     )(index, mine, late_gain, x_in, c_in)
-    pieces[planes // 2], _ = lax.optimization_barrier((pieces[planes // 2], pieces[1]))
+    pieces[planes // 2], _ = lax.optimization_barrier((pieces[planes // 2], pieces[3]))
+    pieces[1], _ = lax.optimization_barrier((pieces[1], blocks[3]))
     own = [marked] + [pieces[k] for k in range(1, planes)]
     other = [to_sibling(piece) for piece in own]
 

time: 59.8 us -> 60.5 us (1.012)
  waiting for transfers between devices: 21.5 us -> 22.3 us
    ppermute x9, waiting for transfers between devices: 8.3 us -> 10.6 us  [along_plane(): return lax.ppermute(value, 'dp', route)]
    ppermute x6, waiting for transfers between devices: 13.1 us -> 11.7 us  [along_z(): return lax.ppermute(value, 'dp', route)]
  transfers between devices with their start and end apart: 21 -> 21, of which waited for: 11 -> 12; matrix products, arithmetic and copies ran while one was open for 0% -> 0% of each run, Pallas kernels for 9% -> 9%
where the time goes in v18:
time: 60.5 us; the launch traced here: 60.2 us
  starting transfers between devices  24.1 us (40%)
  waiting for transfers between devices  22.3 us (37%)
  Pallas kernels  12.9 us (21%)
  between operations  0.78 us (1%)
    ppermute x6, waiting for transfers between devices, along_z(): return lax.ppermute(value, 'dp', route)  11.7 us
    ppermute x9, starting transfers between devices, along_plane(): return lax.ppermute(value, 'dp', route)  11.6 us
    ppermute x6, starting transfers between devices, along_z(): return lax.ppermute(value, 'dp', route)  11.2 us
    ppermute x9, waiting for transfers between devices, along_plane(): return lax.ppermute(value, 'dp', route)  10.6 us
    pallas_call x10, Pallas kernels, call(): pl.pallas_call(kernel, out_shape=[jax.ShapeDtypeStruct(shape, dtype) for...  8.04 us
    pallas_call x1, Pallas kernels, planar(): pl.pallas_call(functools.partial(blocks_kernel, planes), out_shape=[one_b...  1.69 us
    pallas_call x1, Pallas kernels, planar(): pl.pallas_call(functools.partial(first_kernel, planes), out_shape=[jax.Sh...  1.66 us
    pallas_call x1, Pallas kernels, planar(): pl.pallas_call(functools.partial(mark_kernel, planes), out_shape=[jax.Sha...  1.49 us
  transfers between devices with their start and end apart: 21, of which 12 were waited for; matrix products, arithmetic and copies ran while one was open for 0% of the time, Pallas kernels for 9%

profile of v18, /device:TPU:0, one launch (start us, length us, event | category | flops | bytes accessed | tf_op | source)
XLA Modules:
  0.0 60.2 jit_solution(4132787608295449090)
XLA Ops:
  0.6 0.1 pad_add_fusion.index
  0.7 1.7 %shard_map.77 = (bf16[256,256]{1,0:T(8,128)(2,1)S(1)}, bf16[2,64,1024]{2,1,0:T(8,128)(2,1)S(1)}) custom-call(s32[3]{0:T(128)S(1)} %pad_add_fusion.index, bf16[192,256]{1,0:T(8,128)(2,1)} %bitcast.11, bf16[64,256]{1,0:T(8,128)(2,1)} %bitcast.12, bf16[2,64,4096]{2,1,0:T(8,128)(2,1)} %x_ref.5, bf16[2,64,4096]{2,1,0:T(8,128)(2,1)} %c_ref.5), custom_call_target="tpu_custom_call" | custom-call | tf_op jit(solution)/shard_map/pallas_call | solution.py:448
  2.4 4.1 %collective-permute-start = (bf16[256,256]{1,0:T(8,128)(2,1)S(1)}, bf16[256,256]{1,0:T(8,128)(2,1)S(1)}, u32[]{:S(2)}, u32[]{:S(2)}) collective-permute-start(bf16[256,256]{1,0:T(8,128)(2,1)S(1)} %get-tuple-element.42.pack_ref), channel_id=1, source_target_pairs={{0,8},{1,9},{2,10},{3,11},{4,12},{5,13},{6,14},{7,15},{8,0},{9,1},... | collective-permute-start | bytes 393224 | tf_op jit(solution)/shard_map/ppermute | solution.py:428
  6.5 0.0 copy-start.1
  6.5 2.4 %collective-permute-start.4 = (bf16[2,64,1024]{2,1,0:T(8,128)(2,1)S(1)}, bf16[2,64,1024]{2,1,0:T(8,128)(2,1)S(1)}, u32[]{:S(2)}, u32[]{:S(2)}) collective-permute-start(bf16[2,64,1024]{2,1,0:T(8,128)(2,1)S(1)} %get-tuple-element.45), channel_id=1, source_target_pairs={{0,3},{1,2},{2,1},{3,0},{4,7},{5,6},{6,5},{7,4},{8,11},{9,10},{10,... | collective-permute-start | bytes 786440 | tf_op jit(solution)/shard_map/ppermute | solution.py:435
  8.9 1.7 %shard_map.79 = (bf16[2,64,1024]{2,1,0:T(8,128)(2,1)S(1)}, bf16[2,64,1024]{2,1,0:T(8,128)(2,1)S(1)}) custom-call(s32[3]{0:T(128)S(1)} %pad_add_fusion.index, bf16[2,64,4096]{2,1,0:T(8,128)(2,1)} %x_ref.5, bf16[2,64,4096]{2,1,0:T(8,128)(2,1)} %c_ref.5), custom_call_target="tpu_custom_call" | custom-call | tf_op jit(solution)/shard_map/pallas_call | solution.py:456
  10.6 0.6 collective-permute-start.5
  11.2 1.6 %collective-permute-start.3 = (bf16[256,256]{1,0:T(8,128)(2,1)S(1)}, bf16[256,256]{1,0:T(8,128)(2,1)S(1)}, u32[]{:S(2)}, u32[]{:S(2)}) collective-permute-start(bf16[256,256]{1,0:T(8,128)(2,1)S(1)} %get-tuple-element.42.pack_ref), channel_id=1, source_target_pairs={{0,4},{1,5},{2,6},{3,7},{4,0},{5,1},{6,2},{7,3},{8,12},{9,13},{10,... | collective-permute-start | bytes 393224 | tf_op jit(solution)/shard_map/ppermute | solution.py:428
  12.8 0.0 collective-permute-done.refs_6_
  12.8 0.8 %collective-permute-start.1 = (bf16[256,256]{1,0:T(8,128)(2,1)S(1)}, bf16[256,256]{1,0:T(8,128)(2,1)S(1)}, u32[]{:S(2)}, u32[]{:S(2)}) collective-permute-start(bf16[256,256]{1,0:T(8,128)(2,1)S(1)} %collective-permute-done.refs_6_), channel_id=1, source_target_pairs={{0,4},{1,5},{2,6},{3,7},{4,0},{5,1},{6,2},{7,3},{8,12},{9,13},{10,... | collective-permute-start | bytes 393224 | tf_op jit(solution)/shard_map/ppermute | solution.py:428
  13.6 1.5 %collective-permute-start.6 = (bf16[2,64,1024]{2,1,0:T(8,128)(2,1)S(1)}, bf16[2,64,1024]{2,1,0:T(8,128)(2,1)S(1)}, u32[]{:S(2)}, u32[]{:S(2)}) collective-permute-start(bf16[2,64,1024]{2,1,0:T(8,128)(2,1)S(1)} %get-tuple-element.47), channel_id=1, source_target_pairs={{0,1},{1,0},{2,3},{3,2},{4,5},{5,4},{6,7},{7,6},{8,9},{9,8},{10,11... | collective-permute-start | bytes 786440 | tf_op jit(solution)/shard_map/ppermute | solution.py:435
  15.1 0.0 copy-done.1
  15.1 0.1 reduce
  15.1 2.4 %collective-permute-done.3.refs_5_ = bf16[256,256]{1,0:T(8,128)(2,1)S(1)} collective-permute-done((bf16[256,256]{1,0:T(8,128)(2,1)S(1)}, bf16[256,256]{1,0:T(8,128)(2,1)S(1)}, u32[]{:S(2)}, u32[]{:S(2)}) %collective-permute-start.3) | collective-permute-done | bytes 131104 | tf_op jit(solution)/shard_map/ppermute | solution.py:428
  17.5 1.5 %shard_map.78 = (bf16[272,256]{1,0:T(8,128)(2,1)S(1)}, bf16[2,64,1024]{2,1,0:T(8,128)(2,1)S(1)}) custom-call(s32[3]{0:T(128)S(1)} %pad_add_fusion.index, bf16[256,256]{1,0:T(8,128)(2,1)S(1)} %get-tuple-element.42.pack_ref, bf16[16,256]{1,0:T(8,128)(2,1)S(1)} %reshape_squeeze.3.gain_ref, bf16[2,64,4096]{2,1,0:T(8,128)(2,1)} %x_ref.5, bf16[2,64,4096]{2,1,0:T(8,128)(2,1)} %c_ref.5), custom_call_target="tpu_custom_call" | custom-call | tf_op jit(solution)/shard_map/pallas_call | solution.py:472
  19.0 0.1 collective-permute-start.7
  19.1 0.0 collective-permute-done.1.own
  19.1 0.5 collective-permute-start.9
  19.6 0.0 collective-permute-done.4.refs_1_
  19.6 0.1 collective-permute-start.8
  19.7 1.1 %collective-permute-done.5.refs_2_ = bf16[2,64,1024]{2,1,0:T(8,128)(2,1)S(1)} collective-permute-done((bf16[2,64,1024]{2,1,0:T(8,128)(2,1)S(1)}, bf16[2,64,1024]{2,1,0:T(8,128)(2,1)S(1)}, u32[]{:S(2)}, u32[]{:S(2)}) %collective-permute-start.5) | collective-permute-done | bytes 262176 | tf_op jit(solution)/shard_map/ppermute | solution.py:435
  20.8 0.0 collective-permute-start.2
  20.8 0.7 %collective-permute-done.6.refs_3_ = bf16[2,64,1024]{2,1,0:T(8,128)(2,1)S(1)} collective-permute-done((bf16[2,64,1024]{2,1,0:T(8,128)(2,1)S(1)}, bf16[2,64,1024]{2,1,0:T(8,128)(2,1)S(1)}, u32[]{:S(2)}, u32[]{:S(2)}) %collective-permute-start.6) | collective-permute-done | bytes 262176 | tf_op jit(solution)/shard_map/ppermute | solution.py:435
  21.5 0.0 collective-permute-done.7.refs_7_
  21.5 0.0 collective-permute-done.9.refs_9_
  21.5 0.0 collective-permute-done.8.refs_8_
  21.6 1.2 %shard_map.80 = (bf16[4,64,1024]{2,1,0:T(8,128)(2,1)S(1)}, bf16[4,64,1024]{2,1,0:T(8,128)(2,1)S(1)}, bf16[3,512,256]{2,1,0:T(8,128)(2,1)S(1)}, f32[3,8,256]{2,1,...) custom-call(s32[3]{0:T(128)S(1)} %pad_add_fusion.index, ...), custom_call_target="tpu_custom_call" | custom-call | tf_op jit(solution)/shard_map/pallas_call | solution.py:405
  22.8 0.0 collective-permute-done.2.other
  22.8 0.9 %shard_map.81 = (bf16[1,512,256]{2,1,0:T(8,128)(2,1)S(1)}, f32[1,8,256]{2,1,0:T(8,128)S(1)}, bf16[64,896]{1,0:T(8,128)(2,1)S(1)}, bf16[64,896]{1,0:T(8,128)(2,1)...) custom-call(s32[3]{0:T(128)S(1)} %pad_add_fusion.index, bf16[256,256]{1,0:T(8,128)(2,1)S(1)} %collective-permute-done.1.own, ...), custom_call_target="tpu_custom_call" | custom-call | tf_op jit(solution)/shard_map/pallas_call | solution.py:405
  23.7 2.5 %collective-permute-start.10 = (bf16[64,896]{1,0:T(8,128)(2,1)S(1)}, bf16[64,896]{1,0:T(8,128)(2,1)S(1)}, u32[]{:S(2)}, u32[]{:S(2)}) collective-permute-start(bf16[64,896]{1,0:T(8,128)(2,1)S(1)} %get-tuple-element.58), channel_id=1, source_target_pairs={{0,3},{1,2},{2,1},{3,0},{4,7},{5,6},{6,5},{7,4},{8,11},{9,10},{10,... | collective-permute-start | bytes 344072 | tf_op jit(solution)/shard_map/ppermute | solution.py:435
  26.2 0.5 collective-permute-start.11
  26.7 0.0 copy-start
  26.7 0.6 collective-permute-start.12
  27.3 2.5 %collective-permute-done.10.refs_0_ = bf16[64,896]{1,0:T(8,128)(2,1)S(1)} collective-permute-done((bf16[64,896]{1,0:T(8,128)(2,1)S(1)}, bf16[64,896]{1,0:T(8,128)(2,1)S(1)}, u32[]{:S(2)}, u32[]{:S(2)}) %collective-permute-start.10) | collective-permute-done | bytes 114720 | tf_op jit(solution)/shard_map/ppermute | solution.py:435
  29.8 2.2 %collective-permute-done.11.refs_1_ = bf16[64,896]{1,0:T(8,128)(2,1)S(1)} collective-permute-done((bf16[64,896]{1,0:T(8,128)(2,1)S(1)}, bf16[64,896]{1,0:T(8,128)(2,1)S(1)}, u32[]{:S(2)}, u32[]{:S(2)}) %collective-permute-start.11) | collective-permute-done | bytes 114720 | tf_op jit(solution)/shard_map/ppermute | solution.py:435
  32.0 0.1 collective-permute-done.12.refs_2_
  32.0 0.0 copy-done
  32.0 2.7 %shard_map.82.refs_0_ = bf16[64,640]{1,0:T(8,128)(2,1)S(1)} custom-call(s32[3]{0:T(128)S(1)} %pad_add_fusion.index, s32[2,1,2]{2,1,0:T(1,128)S(1)} %copy-done, bf16[64,896]{1,0:T(8,128)(2,1)S(1)} %collective-permute-done.10.refs_0_, bf16[64,896]{1,0:T(8,128)(2,1)S(1)} %collective-permute-done.11.refs_1_, ...), custom_call_target="tpu_custom_call" | custom-call | tf_op jit(solution)/shard_map/pallas_call | solution.py:405
  34.8 1.8 %collective-permute-start.13 = (bf16[64,640]{1,0:T(8,128)(2,1)S(1)}, bf16[64,640]{1,0:T(8,128)(2,1)S(1)}, u32[]{:S(2)}, u32[]{:S(2)}) collective-permute-start(bf16[64,640]{1,0:T(8,128)(2,1)S(1)} %shard_map.82.refs_0_), channel_id=1, source_target_pairs={{0,3},{1,2},{2,1},{3,0},{4,7},{5,6},{6,5},{7,4},{8,11},{9,10},{10,... | collective-permute-start | bytes 245768 | tf_op jit(solution)/shard_map/ppermute | solution.py:435
  36.5 1.3 %collective-permute-start.14 = (bf16[64,640]{1,0:T(8,128)(2,1)S(1)}, bf16[64,640]{1,0:T(8,128)(2,1)S(1)}, u32[]{:S(2)}, u32[]{:S(2)}) collective-permute-start(bf16[64,640]{1,0:T(8,128)(2,1)S(1)} %shard_map.82.refs_0_), channel_id=1, source_target_pairs={{0,2},{1,3},{2,0},{3,1},{4,6},{5,7},{6,4},{7,5},{8,10},{9,11},{10,... | collective-permute-start | bytes 245768 | tf_op jit(solution)/shard_map/ppermute | solution.py:435
  37.8 0.5 collective-permute-start.15
  38.3 2.5 %collective-permute-done.13.refs_1_ = bf16[64,640]{1,0:T(8,128)(2,1)S(1)} collective-permute-done((bf16[64,640]{1,0:T(8,128)(2,1)S(1)}, bf16[64,640]{1,0:T(8,128)(2,1)S(1)}, u32[]{:S(2)}, u32[]{:S(2)}) %collective-permute-start.13) | collective-permute-done | bytes 81952 | tf_op jit(solution)/shard_map/ppermute | solution.py:435
  40.8 0.8 %collective-permute-done.14.refs_2_ = bf16[64,640]{1,0:T(8,128)(2,1)S(1)} collective-permute-done((bf16[64,640]{1,0:T(8,128)(2,1)S(1)}, bf16[64,640]{1,0:T(8,128)(2,1)S(1)}, u32[]{:S(2)}, u32[]{:S(2)}) %collective-permute-start.14) | collective-permute-done | bytes 81952 | tf_op jit(solution)/shard_map/ppermute | solution.py:435
  41.6 0.7 %collective-permute-done.15.refs_3_ = bf16[64,640]{1,0:T(8,128)(2,1)S(1)} collective-permute-done((bf16[64,640]{1,0:T(8,128)(2,1)S(1)}, bf16[64,640]{1,0:T(8,128)(2,1)S(1)}, u32[]{:S(2)}, u32[]{:S(2)}) %collective-permute-start.15) | collective-permute-done | bytes 81952 | tf_op jit(solution)/shard_map/ppermute | solution.py:435
  42.3 1.3 %shard_map.83 = (f32[2,256,256]{2,1,0:T(8,128)S(1)}, bf16[2,256,256]{2,1,0:T(8,128)(2,1)S(1)}, bf16[640,256]{1,0:T(8,128)(2,1)S(1)}, bf16[256,64]{1,0:T(8,128)(2,1)S(1)}, bf16[64,192]{1,0:T(8,128)(2,1)S(1)}) custom-call(s32[3]{0:T(128)S(1)} %pad_add_fusion.index, bf16[64,640]{1,0:T(8,128)(2,1)S(1)} %shard_map.82.refs_0_, ...), custom_call_target="tpu_custom_call" | custom-call | tf_op jit(solution)/shard_map/pallas_call | solution.py:405
  43.5 0.1 collective-permute-start.17
  43.6 1.0 %shard_map.84 = (f32[2,256,256]{2,1,0:T(8,128)S(1)}, bf16[2,256,256]{2,1,0:T(8,128)(2,1)S(1)}) custom-call(s32[3]{0:T(128)S(1)} %pad_add_fusion.index, bf16[640,256]{1,0:T(8,128)(2,1)S(1)} %get-tuple-element.66.turned_ref, bf16[256,64]{1,0:T(8,128)(2,1)S(1)} %get-tuple-element.67.small_ref, bf16[64,192]{1,0:T(8,128)(2,1)S(1)} %get-tuple-element.68.small_t_ref, ...), custom_call_target="tpu_custom_call" | custom-call | tf_op jit(solution)/shard_map/pallas_call | solution.py:405
  44.6 0.6 collective-permute-start.16
  45.2 0.0 collective-permute-done.17.come_ref
  45.2 0.1 shard_map.86
  45.3 1.7 %collective-permute-start.18 = (bf16[256,256]{1,0:T(8,128)(2,1)S(1)}, bf16[256,256]{1,0:T(8,128)(2,1)S(1)}, u32[]{:S(2)}, u32[]{:S(2)}) collective-permute-start(bf16[256,256]{1,0:T(8,128)(2,1)S(1)} %get-tuple-element.75), channel_id=1, source_target_pairs={{0,4},{1,5},{2,6},{3,7},{4,0},{5,1},{6,2},{7,3},{8,12},{9,13},{10,... | collective-permute-start | bytes 393224 | tf_op jit(solution)/shard_map/ppermute | solution.py:428
  46.9 0.0 collective-permute-done.16.come_ref
  46.9 0.1 shard_map.85
  47.0 3.8 %collective-permute-done.18.b_ref = bf16[256,256]{1,0:T(8,128)(2,1)S(1)} collective-permute-done((bf16[256,256]{1,0:T(8,128)(2,1)S(1)}, bf16[256,256]{1,0:T(8,128)(2,1)S(1)}, u32[]{:S(2)}, u32[]{:S(2)}) %collective-permute-start.18) | collective-permute-done | bytes 131104 | tf_op jit(solution)/shard_map/ppermute | solution.py:428
  50.8 2.5 %collective-permute-start.19 = (bf16[256,256]{1,0:T(8,128)(2,1)S(1)}, bf16[256,256]{1,0:T(8,128)(2,1)S(1)}, u32[]{:S(2)}, u32[]{:S(2)}) collective-permute-start(bf16[256,256]{1,0:T(8,128)(2,1)S(1)} %shard_map.87), channel_id=1, source_target_pairs={{0,8},{1,9},{2,10},{3,11},{4,12},{5,13},{6,14},{7,15},{8,0},{9,1},... | collective-permute-start | bytes 393224 | tf_op jit(solution)/shard_map/ppermute | solution.py:428
  53.3 0.5 collective-permute-start.20
  53.9 5.4 %collective-permute-done.19.b_ref = bf16[256,256]{1,0:T(8,128)(2,1)S(1)} collective-permute-done((bf16[256,256]{1,0:T(8,128)(2,1)S(1)}, bf16[256,256]{1,0:T(8,128)(2,1)S(1)}, u32[]{:S(2)}, u32[]{:S(2)}) %collective-permute-start.19) | collective-permute-done | bytes 131104 | tf_op jit(solution)/shard_map/ppermute | solution.py:428
  59.3 0.2 collective-permute-done.20.refs_0_
  59.5 0.7 %shard_map.89 = (f32[192,256]{1,0:T(8,128)}, f32[64,256]{1,0:T(8,128)}) custom-call(f32[256,256]{1,0:T(8,128)S(1)} %shard_map.88.keep_ref, bf16[256,256]{1,0:T(8,128)(2,1)S(1)} %collective-permute-done.20.refs_0_), custom_call_target="tpu_custom_call" | custom-call | tf_op jit(solution)/shard_map/pallas_call | solution.py:405
  (3 shorter events, 0.1 us)
Async XLA Ops:
  2.4 10.4 %collective-permute-start = (bf16[256,256]{1,0:T(8,128)(2,1)S(1)}, bf16[256,256]{1,0:T(8,128)(2,1)S(1)}, u32[]{:S(2)}, u32[]{:S(2)}) collective-permute-start(bf16[256,256]{1,0:T(8,128)(2,1)S(1)} %get-tuple-element.42.pack_ref), channel_id=1, source_target_pairs={{0,8},{1,9},{2,10},{3,11},{4,12},{5,13},{6,14},{7,15},{8,0},{9,1},... | collective-permute-start | bytes 393224 | tf_op jit(solution)/shard_map/ppermute | solution.py:428
  6.5 8.6 %copy-start.1 = (bf16[1,4096]{1,0:T(2,128)(2,1)S(1)}, bf16[1,4096]{1,0:T(2,128)(2,1)}, u32[]{:S(2)}) copy-start(bf16[1,4096]{1,0:T(2,128)(2,1)} %param.9) | copy-start | bytes 24580
  6.5 13.1 %collective-permute-start.4 = (bf16[2,64,1024]{2,1,0:T(8,128)(2,1)S(1)}, bf16[2,64,1024]{2,1,0:T(8,128)(2,1)S(1)}, u32[]{:S(2)}, u32[]{:S(2)}) collective-permute-start(bf16[2,64,1024]{2,1,0:T(8,128)(2,1)S(1)} %get-tuple-element.45), channel_id=1, source_target_pairs={{0,3},{1,2},{2,1},{3,0},{4,7},{5,6},{6,5},{7,4},{8,11},{9,10},{10,... | collective-permute-start | bytes 786440 | tf_op jit(solution)/shard_map/ppermute | solution.py:435
  10.6 10.1 %collective-permute-start.5 = (bf16[2,64,1024]{2,1,0:T(8,128)(2,1)S(1)}, bf16[2,64,1024]{2,1,0:T(8,128)(2,1)S(1)}, u32[]{:S(2)}, u32[]{:S(2)}) collective-permute-start(bf16[2,64,1024]{2,1,0:T(8,128)(2,1)S(1)} %get-tuple-element.46), channel_id=1, source_target_pairs={{0,2},{1,3},{2,0},{3,1},{4,6},{5,7},{6,4},{7,5},{8,10},{9,11},{10,... | collective-permute-start | bytes 786440 | tf_op jit(solution)/shard_map/ppermute | solution.py:435
  11.2 6.3 %collective-permute-start.3 = (bf16[256,256]{1,0:T(8,128)(2,1)S(1)}, bf16[256,256]{1,0:T(8,128)(2,1)S(1)}, u32[]{:S(2)}, u32[]{:S(2)}) collective-permute-start(bf16[256,256]{1,0:T(8,128)(2,1)S(1)} %get-tuple-element.42.pack_ref), channel_id=1, source_target_pairs={{0,4},{1,5},{2,6},{3,7},{4,0},{5,1},{6,2},{7,3},{8,12},{9,13},{10,... | collective-permute-start | bytes 393224 | tf_op jit(solution)/shard_map/ppermute | solution.py:428
  12.8 6.3 %collective-permute-start.1 = (bf16[256,256]{1,0:T(8,128)(2,1)S(1)}, bf16[256,256]{1,0:T(8,128)(2,1)S(1)}, u32[]{:S(2)}, u32[]{:S(2)}) collective-permute-start(bf16[256,256]{1,0:T(8,128)(2,1)S(1)} %collective-permute-done.refs_6_), channel_id=1, source_target_pairs={{0,4},{1,5},{2,6},{3,7},{4,0},{5,1},{6,2},{7,3},{8,12},{9,13},{10,... | collective-permute-start | bytes 393224 | tf_op jit(solution)/shard_map/ppermute | solution.py:428
  13.6 8.0 %collective-permute-start.6 = (bf16[2,64,1024]{2,1,0:T(8,128)(2,1)S(1)}, bf16[2,64,1024]{2,1,0:T(8,128)(2,1)S(1)}, u32[]{:S(2)}, u32[]{:S(2)}) collective-permute-start(bf16[2,64,1024]{2,1,0:T(8,128)(2,1)S(1)} %get-tuple-element.47), channel_id=1, source_target_pairs={{0,1},{1,0},{2,3},{3,2},{4,5},{5,4},{6,7},{7,6},{8,9},{9,8},{10,11... | collective-permute-start | bytes 786440 | tf_op jit(solution)/shard_map/ppermute | solution.py:435
  19.0 2.6 %collective-permute-start.7 = (bf16[272,256]{1,0:T(8,128)(2,1)S(1)}, bf16[272,256]{1,0:T(8,128)(2,1)S(1)}, u32[]{:S(2)}, u32[]{:S(2)}) collective-permute-start(bf16[272,256]{1,0:T(8,128)(2,1)S(1)} %get-tuple-element.48.refs_4_), channel_id=1, source_target_pairs={{0,16},{16,0},{1,17},{17,1},{2,18},{18,2},{3,19},{19,3},{4,20},{20... | collective-permute-start | bytes 417800 | tf_op jit(solution)/shard_map/ppermute | solution.py:431
  19.1 2.5 %collective-permute-start.9 = (bf16[256,256]{1,0:T(8,128)(2,1)S(1)}, bf16[256,256]{1,0:T(8,128)(2,1)S(1)}, u32[]{:S(2)}, u32[]{:S(2)}) collective-permute-start(bf16[256,256]{1,0:T(8,128)(2,1)S(1)} %collective-permute-done.refs_6_), channel_id=1, source_target_pairs={{0,16},{16,0},{1,17},{17,1},{2,18},{18,2},{3,19},{19,3},{4,20},{20... | collective-permute-start | bytes 393224 | tf_op jit(solution)/shard_map/ppermute | solution.py:431
  19.6 2.0 %collective-permute-start.8 = (bf16[256,256]{1,0:T(8,128)(2,1)S(1)}, bf16[256,256]{1,0:T(8,128)(2,1)S(1)}, u32[]{:S(2)}, u32[]{:S(2)}) collective-permute-start(bf16[256,256]{1,0:T(8,128)(2,1)S(1)} %collective-permute-done.3.refs_5_), channel_id=1, source_target_pairs={{0,16},{16,0},{1,17},{17,1},{2,18},{18,2},{3,19},{19,3},{4,20},{20... | collective-permute-start | bytes 393224 | tf_op jit(solution)/shard_map/ppermute | solution.py:431
  20.8 2.0 %collective-permute-start.2 = (bf16[256,256]{1,0:T(8,128)(2,1)S(1)}, bf16[256,256]{1,0:T(8,128)(2,1)S(1)}, u32[]{:S(2)}, u32[]{:S(2)}) collective-permute-start(bf16[256,256]{1,0:T(8,128)(2,1)S(1)} %collective-permute-done.1.own), channel_id=1, source_target_pairs={{0,16},{16,0},{1,17},{17,1},{2,18},{18,2},{3,19},{19,3},{4,20},{20... | collective-permute-start | bytes 393224 | tf_op jit(solution)/shard_map/ppermute | solution.py:431
  23.7 6.1 %collective-permute-start.10 = (bf16[64,896]{1,0:T(8,128)(2,1)S(1)}, bf16[64,896]{1,0:T(8,128)(2,1)S(1)}, u32[]{:S(2)}, u32[]{:S(2)}) collective-permute-start(bf16[64,896]{1,0:T(8,128)(2,1)S(1)} %get-tuple-element.58), channel_id=1, source_target_pairs={{0,3},{1,2},{2,1},{3,0},{4,7},{5,6},{6,5},{7,4},{8,11},{9,10},{10,... | collective-permute-start | bytes 344072 | tf_op jit(solution)/shard_map/ppermute | solution.py:435
  26.2 5.7 %collective-permute-start.11 = (bf16[64,896]{1,0:T(8,128)(2,1)S(1)}, bf16[64,896]{1,0:T(8,128)(2,1)S(1)}, u32[]{:S(2)}, u32[]{:S(2)}) collective-permute-start(bf16[64,896]{1,0:T(8,128)(2,1)S(1)} %get-tuple-element.59), channel_id=1, source_target_pairs={{0,2},{1,3},{2,0},{3,1},{4,6},{5,7},{6,4},{7,5},{8,10},{9,11},{10,... | collective-permute-start | bytes 344072 | tf_op jit(solution)/shard_map/ppermute | solution.py:435
  26.7 5.3 %copy-start = (s32[2,1,2]{2,1,0:T(1,128)S(1)}, s32[2,1,2]{2,1,0:T(1,128)}, u32[]{:S(2)}) copy-start(s32[2,1,2]{2,1,0:T(1,128)} %docs.1) | copy-start | bytes 52
  26.7 5.3 %collective-permute-start.12 = (bf16[64,896]{1,0:T(8,128)(2,1)S(1)}, bf16[64,896]{1,0:T(8,128)(2,1)S(1)}, u32[]{:S(2)}, u32[]{:S(2)}) collective-permute-start(bf16[64,896]{1,0:T(8,128)(2,1)S(1)} %get-tuple-element.60), channel_id=1, source_target_pairs={{0,1},{1,0},{2,3},{3,2},{4,5},{5,4},{6,7},{7,6},{8,9},{9,8},{10,11... | collective-permute-start | bytes 344072 | tf_op jit(solution)/shard_map/ppermute | solution.py:435
  34.8 6.1 %collective-permute-start.13 = (bf16[64,640]{1,0:T(8,128)(2,1)S(1)}, bf16[64,640]{1,0:T(8,128)(2,1)S(1)}, u32[]{:S(2)}, u32[]{:S(2)}) collective-permute-start(bf16[64,640]{1,0:T(8,128)(2,1)S(1)} %shard_map.82.refs_0_), channel_id=1, source_target_pairs={{0,3},{1,2},{2,1},{3,0},{4,7},{5,6},{6,5},{7,4},{8,11},{9,10},{10,... | collective-permute-start | bytes 245768 | tf_op jit(solution)/shard_map/ppermute | solution.py:435
  36.5 5.1 %collective-permute-start.14 = (bf16[64,640]{1,0:T(8,128)(2,1)S(1)}, bf16[64,640]{1,0:T(8,128)(2,1)S(1)}, u32[]{:S(2)}, u32[]{:S(2)}) collective-permute-start(bf16[64,640]{1,0:T(8,128)(2,1)S(1)} %shard_map.82.refs_0_), channel_id=1, source_target_pairs={{0,2},{1,3},{2,0},{3,1},{4,6},{5,7},{6,4},{7,5},{8,10},{9,11},{10,... | collective-permute-start | bytes 245768 | tf_op jit(solution)/shard_map/ppermute | solution.py:435
  37.8 4.4 %collective-permute-start.15 = (bf16[64,640]{1,0:T(8,128)(2,1)S(1)}, bf16[64,640]{1,0:T(8,128)(2,1)S(1)}, u32[]{:S(2)}, u32[]{:S(2)}) collective-permute-start(bf16[64,640]{1,0:T(8,128)(2,1)S(1)} %shard_map.82.refs_0_), channel_id=1, source_target_pairs={{0,1},{1,0},{2,3},{3,2},{4,5},{5,4},{6,7},{7,6},{8,9},{9,8},{10,11... | collective-permute-start | bytes 245768 | tf_op jit(solution)/shard_map/ppermute | solution.py:435
  43.5 1.7 %collective-permute-start.17 = (bf16[2,256,256]{2,1,0:T(8,128)(2,1)S(1)}, bf16[2,256,256]{2,1,0:T(8,128)(2,1)S(1)}, u32[]{:S(2)}, u32[]{:S(2)}) collective-permute-start(bf16[2,256,256]{2,1,0:T(8,128)(2,1)S(1)} %get-tuple-element.73), channel_id=1, source_target_pairs={{0,16},{16,0},{1,17},{17,1},{2,18},{18,2},{3,19},{19,3},{4,20},{20... | collective-permute-start | bytes 786440 | tf_op jit(solution)/shard_map/ppermute | solution.py:431
  44.6 2.3 %collective-permute-start.16 = (bf16[2,256,256]{2,1,0:T(8,128)(2,1)S(1)}, bf16[2,256,256]{2,1,0:T(8,128)(2,1)S(1)}, u32[]{:S(2)}, u32[]{:S(2)}) collective-permute-start(bf16[2,256,256]{2,1,0:T(8,128)(2,1)S(1)} %get-tuple-element.70), channel_id=1, source_target_pairs={{0,16},{16,0},{1,17},{17,1},{2,18},{18,2},{3,19},{19,3},{4,20},{20... | collective-permute-start | bytes 786440 | tf_op jit(solution)/shard_map/ppermute | solution.py:431
  45.3 5.5 %collective-permute-start.18 = (bf16[256,256]{1,0:T(8,128)(2,1)S(1)}, bf16[256,256]{1,0:T(8,128)(2,1)S(1)}, u32[]{:S(2)}, u32[]{:S(2)}) collective-permute-start(bf16[256,256]{1,0:T(8,128)(2,1)S(1)} %get-tuple-element.75), channel_id=1, source_target_pairs={{0,4},{1,5},{2,6},{3,7},{4,0},{5,1},{6,2},{7,3},{8,12},{9,13},{10,... | collective-permute-start | bytes 393224 | tf_op jit(solution)/shard_map/ppermute | solution.py:428
  50.8 8.4 %collective-permute-start.19 = (bf16[256,256]{1,0:T(8,128)(2,1)S(1)}, bf16[256,256]{1,0:T(8,128)(2,1)S(1)}, u32[]{:S(2)}, u32[]{:S(2)}) collective-permute-start(bf16[256,256]{1,0:T(8,128)(2,1)S(1)} %shard_map.87), channel_id=1, source_target_pairs={{0,8},{1,9},{2,10},{3,11},{4,12},{5,13},{6,14},{7,15},{8,0},{9,1},... | collective-permute-start | bytes 393224 | tf_op jit(solution)/shard_map/ppermute | solution.py:428
  53.3 6.1 %collective-permute-start.20 = (bf16[256,256]{1,0:T(8,128)(2,1)S(1)}, bf16[256,256]{1,0:T(8,128)(2,1)S(1)}, u32[]{:S(2)}, u32[]{:S(2)}) collective-permute-start(bf16[256,256]{1,0:T(8,128)(2,1)S(1)} %get-tuple-element.77), channel_id=1, source_target_pairs={{0,4},{1,5},{2,6},{3,7},{4,0},{5,1},{6,2},{7,3},{8,12},{9,13},{10,... | collective-permute-start | bytes 393224 | tf_op jit(solution)/shard_map/ppermute | solution.py:428

commit v19 on v17

--- a/solution.py
+++ b/solution.py
@@ -349,13 +349,17 @@
     pieces_of(planes, heads, order, index, turned_ref[...], small_ref[...], small_t_ref[...], *refs)
 
 
-def merge_kernel(keep_ref, come_ref, *out_refs):
-    for i, out_ref in enumerate(out_refs):
-        out_ref[...] = (keep_ref[i] + come_ref[i].astype(F32)).astype(out_ref.dtype)
-
-
-def wide_add_kernel(a_ref, b_ref, out_ref):
-    out_ref[...] = a_ref[...] + b_ref[...].astype(F32)
+def merge_kernel(cuts, keep_ref, come_ref, *out_refs):
+    rows = keep_ref.shape[1] // cuts
+    for j, out_ref in enumerate(out_refs):
+        here = slice(j % cuts * rows, (j % cuts + 1) * rows)
+        out_ref[...] = (keep_ref[j // cuts, here] + come_ref[j // cuts, here].astype(F32)).astype(out_ref.dtype)
+
+
+def wide_add_kernel(at, a_ref, part_ref, out_ref):
+    rows = slice(at, at + part_ref.shape[0])
+    out_ref[...] = a_ref[...]
+    out_ref[rows, :] = a_ref[rows, :] + part_ref[...].astype(F32)
 
 
 def add_kernel(a_ref, b_ref, out_ref):
@@ -477,9 +481,10 @@
     far_order = tuple(reversed(range(planes - planes // 2, planes)))
     near_order = tuple(reversed(range(planes - planes // 2)))
 
-    def swap_and_merge(order, keep, send):
-        outs = [(piece, BF16 if k else F32) for k in order]
-        return zip(order, call(merge_kernel, outs, keep, to_sibling(send)))
+    def swap_and_merge(order, keep, send, cuts):
+        outs = [((piece[0] // cuts, width), BF16 if k else F32) for k in order for _ in range(cuts)]
+        cut = call(functools.partial(merge_kernel, cuts), outs, keep, to_sibling(send))
+        return {k: list(cut[i * cuts : (i + 1) * cuts]) for i, k in enumerate(order)}
 
     keep, send, turned, small, small_t = call(
         functools.partial(far_grads_kernel, planes, heads, far_order),
@@ -488,29 +493,32 @@
         index, *exchange(factors), x, c, vx, gains, scalars=1,
         scratch=[((PLANE, block, 5 * half), BF16)],
     )
-    pieces = dict(swap_and_merge(far_order, keep, send))
+    pieces = swap_and_merge(far_order, keep, send, 2)
     keep, send = call(
         functools.partial(near_grads_kernel, planes, heads, near_order),
         [((len(near_order),) + piece, F32), ((len(near_order),) + piece, BF16)],
         index, turned, small, small_t, x, c, vx, gains, scalars=1,
     )
-    pieces.update(swap_and_merge(near_order, keep, send))
-    kept, parts = pieces[0], []
-    held = []
+    pieces.update(swap_and_merge(near_order, keep, send, 1))
+    (kept,), held = pieces[0], []
     for step in [1 << bit for bit in range(planes.bit_length() - 1)]:
-        got = {k ^ step: along_z(pieces.pop(k), step) for k in sorted(pieces, reverse=True) if k & step and k != step}
+        senders = [k for k in sorted(pieces, reverse=True) if k & step and k != step]
+        got = {k ^ step: [along_z(part, step) for part in pieces.pop(k)] for k in senders}
         if step in pieces:
             held.append((pieces.pop(step), step))
-        for k, part in got.items():
-            (pieces[k],) = call(add_kernel, [(piece, BF16)], pieces[k], part)
-            held = [(lax.optimization_barrier((value, pieces[k]))[0], at) for value, at in held]
-    parts = [along_z(value, at) for value, at in reversed(held)]
-    for part in parts[:-1]:
-        (kept,) = call(wide_add_kernel, [(piece, F32)], kept, part)
+        for k, come in got.items():
+            pieces[k] = [call(add_kernel, [(a.shape, BF16)], a, b)[0] for a, b in zip(pieces[k], come)]
+            held = [
+                (parts, at) for parts, at in held
+            ]
+    parts = [[along_z(part, at) for part in value] for value, at in reversed(held)]
+    for come in parts[:-1]:
+        for i, part in enumerate(come):
+            (kept,) = call(functools.partial(wide_add_kernel, i * part.shape[0]), [(piece, F32)], kept, part)
     grad_qkv, grad_out = call(
         functools.partial(last_kernel, qkv_rows),
         [((qkv_rows, width), F32), ((heads, width), F32)],
-        kept, *parts[-1:],
+        kept, *(parts[-1] if parts else []),
     )
     return (grad_qkv.T[None], grad_out[None])
 

time: 59.8 us -> 58.9 us (0.985)
  waiting for transfers between devices: 21.9 us -> 18.9 us
  starting transfers between devices: 24.1 us -> 26.2 us
    ppermute x6 -> x8, waiting for transfers between devices: 12.7 us -> 9.8 us  [along_z(): return lax.ppermute(value, 'dp', route)]
    ppermute x6 -> x8, starting transfers between devices: 10.3 us -> 12.4 us  [along_z(): return lax.ppermute(value, 'dp', route)]
    pallas_call x9 -> x11, Pallas kernels: 7.65 us -> 7.69 us  [call(): pl.pallas_call(kernel, out_shape=[jax.ShapeDtypeStruct(shape, dtype) for...]
  transfers between devices with their start and end apart: 21 -> 23, of which waited for: 12 -> 12; matrix products, arithmetic and copies ran while one was open for 0% -> 0% of each run, Pallas kernels for 7% -> 7%
where the time goes in v19:
time: 58.9 us; the launch traced here: 58.6 us
  starting transfers between devices  26.2 us (44%)
  waiting for transfers between devices  18.9 us (32%)
  Pallas kernels  12.5 us (21%)
  between operations  0.77 us (1%)
    ppermute x8, starting transfers between devices, along_z(): return lax.ppermute(value, 'dp', route)  12.4 us
    ppermute x9, starting transfers between devices, along_plane(): return lax.ppermute(value, 'dp', route)  12.2 us
    ppermute x8, waiting for transfers between devices, along_z(): return lax.ppermute(value, 'dp', route)  9.8 us
    ppermute x9, waiting for transfers between devices, along_plane(): return lax.ppermute(value, 'dp', route)  8.11 us
    pallas_call x11, Pallas kernels, call(): pl.pallas_call(kernel, out_shape=[jax.ShapeDtypeStruct(shape, dtype) for...  7.69 us
    ppermute x6, starting transfers between devices, to_sibling(): return lax.ppermute(value, 'section', [(0, 1), (1, 0)])  1.71 us
    pallas_call x1, Pallas kernels, planar(): pl.pallas_call(functools.partial(blocks_kernel, planes), out_shape=[one_b...  1.69 us
    pallas_call x1, Pallas kernels, planar(): pl.pallas_call(functools.partial(first_kernel, planes), out_shape=[jax.Sh...  1.66 us
  transfers between devices with their start and end apart: 23, of which 12 were waited for; matrix products, arithmetic and copies ran while one was open for 0% of the time, Pallas kernels for 7%

profile of v19, /device:TPU:0, one launch (start us, length us, event | category | flops | bytes accessed | tf_op | source)
XLA Modules:
  0.0 58.6 jit_solution(14248995384214413428)
XLA Ops:
  0.6 0.1 pad_add_fusion.index
  0.7 1.7 %shard_map.77 = (bf16[256,256]{1,0:T(8,128)(2,1)S(1)}, bf16[2,64,1024]{2,1,0:T(8,128)(2,1)S(1)}) custom-call(s32[3]{0:T(128)S(1)} %pad_add_fusion.index, bf16[192,256]{1,0:T(8,128)(2,1)} %bitcast.11, bf16[64,256]{1,0:T(8,128)(2,1)} %bitcast.12, bf16[2,64,4096]{2,1,0:T(8,128)(2,1)} %x_ref.5, bf16[2,64,4096]{2,1,0:T(8,128)(2,1)} %c_ref.5), custom_call_target="tpu_custom_call" | custom-call | tf_op jit(solution)/shard_map/pallas_call | solution.py:430
  2.4 4.0 %collective-permute-start = (bf16[2,64,1024]{2,1,0:T(8,128)(2,1)S(1)}, bf16[2,64,1024]{2,1,0:T(8,128)(2,1)S(1)}, u32[]{:S(2)}, u32[]{:S(2)}) collective-permute-start(bf16[2,64,1024]{2,1,0:T(8,128)(2,1)S(1)} %get-tuple-element.35), channel_id=1, source_target_pairs={{0,3},{1,2},{2,1},{3,0},{4,7},{5,6},{6,5},{7,4},{8,11},{9,10},{10,... | collective-permute-start | bytes 786440 | tf_op jit(solution)/shard_map/ppermute | solution.py:417
  6.4 0.0 copy-start.1
  6.4 2.6 %collective-permute-start.4 = (bf16[256,256]{1,0:T(8,128)(2,1)S(1)}, bf16[256,256]{1,0:T(8,128)(2,1)S(1)}, u32[]{:S(2)}, u32[]{:S(2)}) collective-permute-start(bf16[256,256]{1,0:T(8,128)(2,1)S(1)} %get-tuple-element.36.pack_ref), channel_id=1, source_target_pairs={{0,8},{1,9},{2,10},{3,11},{4,12},{5,13},{6,14},{7,15},{8,0},{9,1},... | collective-permute-start | bytes 393224 | tf_op jit(solution)/shard_map/ppermute | solution.py:410
  8.9 1.6 %collective-permute-start.3 = (bf16[256,256]{1,0:T(8,128)(2,1)S(1)}, bf16[256,256]{1,0:T(8,128)(2,1)S(1)}, u32[]{:S(2)}, u32[]{:S(2)}) collective-permute-start(bf16[256,256]{1,0:T(8,128)(2,1)S(1)} %get-tuple-element.36.pack_ref), channel_id=1, source_target_pairs={{0,4},{1,5},{2,6},{3,7},{4,0},{5,1},{6,2},{7,3},{8,12},{9,13},{10,... | collective-permute-start | bytes 393224 | tf_op jit(solution)/shard_map/ppermute | solution.py:410
  10.5 1.7 %shard_map.79 = (bf16[2,64,1024]{2,1,0:T(8,128)(2,1)S(1)}, bf16[2,64,1024]{2,1,0:T(8,128)(2,1)S(1)}) custom-call(s32[3]{0:T(128)S(1)} %pad_add_fusion.index, bf16[2,64,4096]{2,1,0:T(8,128)(2,1)} %x_ref.5, bf16[2,64,4096]{2,1,0:T(8,128)(2,1)} %c_ref.5), custom_call_target="tpu_custom_call" | custom-call | tf_op jit(solution)/shard_map/pallas_call | solution.py:438
  12.2 0.6 collective-permute-start.1
  12.8 0.5 collective-permute-start.2
  13.3 1.8 %collective-permute-done.4.refs_6_ = bf16[256,256]{1,0:T(8,128)(2,1)S(1)} collective-permute-done((bf16[256,256]{1,0:T(8,128)(2,1)S(1)}, bf16[256,256]{1,0:T(8,128)(2,1)S(1)}, u32[]{:S(2)}, u32[]{:S(2)}) %collective-permute-start.4) | collective-permute-done | bytes 131104 | tf_op jit(solution)/shard_map/ppermute | solution.py:410
  15.1 0.6 collective-permute-start.5
  15.7 0.0 collective-permute-done.3.refs_5_
  15.7 0.0 collective-permute-start.7
  15.7 0.0 copy-done.1
  15.7 0.1 reduce
  15.8 0.0 collective-permute-done.refs_1_
  15.8 1.5 %shard_map.78 = (bf16[272,256]{1,0:T(8,128)(2,1)S(1)}, bf16[2,64,1024]{2,1,0:T(8,128)(2,1)S(1)}) custom-call(s32[3]{0:T(128)S(1)} %pad_add_fusion.index, bf16[256,256]{1,0:T(8,128)(2,1)S(1)} %get-tuple-element.36.pack_ref, bf16[16,256]{1,0:T(8,128)(2,1)S(1)} %reshape_squeeze.3.gain_ref, bf16[2,64,4096]{2,1,0:T(8,128)(2,1)} %x_ref.5, bf16[2,64,4096]{2,1,0:T(8,128)(2,1)} %c_ref.5), custom_call_target="tpu_custom_call" | custom-call | tf_op jit(solution)/shard_map/pallas_call | solution.py:454
  17.3 0.6 collective-permute-start.6
  17.8 2.2 %collective-permute-done.5.refs_7_ = bf16[256,256]{1,0:T(8,128)(2,1)S(1)} collective-permute-done((bf16[256,256]{1,0:T(8,128)(2,1)S(1)}, bf16[256,256]{1,0:T(8,128)(2,1)S(1)}, u32[]{:S(2)}, u32[]{:S(2)}) %collective-permute-start.5) | collective-permute-done | bytes 131104 | tf_op jit(solution)/shard_map/ppermute | solution.py:410
  20.1 0.0 collective-permute-start.9
  20.1 0.0 collective-permute-done.7.refs_9_
  20.1 0.5 collective-permute-start.8
  20.6 0.0 collective-permute-done.1.refs_2_
  20.6 0.0 collective-permute-done.2.refs_3_
  20.6 0.8 %collective-permute-done.9.refs_11_ = bf16[256,256]{1,0:T(8,128)(2,1)S(1)} collective-permute-done((bf16[256,256]{1,0:T(8,128)(2,1)S(1)}, bf16[256,256]{1,0:T(8,128)(2,1)S(1)}, u32[]{:S(2)}, u32[]{:S(2)}) %collective-permute-start.9) | collective-permute-done | bytes 131104 | tf_op jit(solution)/shard_map/ppermute | solution.py:413
  21.4 0.2 collective-permute-done.8.refs_10_
  21.6 0.0 collective-permute-done.6.refs_8_
  21.6 1.6 %shard_map.80 = (bf16[4,64,1024]{2,1,0:T(8,128)(2,1)S(1)}, bf16[4,64,1024]{2,1,0:T(8,128)(2,1)S(1)}, bf16[4,512,256]{2,1,0:T(8,128)(2,1)S(1)}, f32[4,8,256]{2,1,...) custom-call(s32[3]{0:T(128)S(1)} %pad_add_fusion.index, ...), custom_call_target="tpu_custom_call" | custom-call | tf_op jit(solution)/shard_map/pallas_call | solution.py:387
  23.2 0.7 %collective-permute-start.10 = (bf16[64,896]{1,0:T(8,128)(2,1)S(1)}, bf16[64,896]{1,0:T(8,128)(2,1)S(1)}, u32[]{:S(2)}, u32[]{:S(2)}) collective-permute-start(bf16[64,896]{1,0:T(8,128)(2,1)S(1)} %get-tuple-element.43), channel_id=1, source_target_pairs={{0,3},{1,2},{2,1},{3,0},{4,7},{5,6},{6,5},{7,4},{8,11},{9,10},{10,... | collective-permute-start | bytes 344072 | tf_op jit(solution)/shard_map/ppermute | solution.py:417
  23.9 1.3 %collective-permute-start.11 = (bf16[64,896]{1,0:T(8,128)(2,1)S(1)}, bf16[64,896]{1,0:T(8,128)(2,1)S(1)}, u32[]{:S(2)}, u32[]{:S(2)}) collective-permute-start(bf16[64,896]{1,0:T(8,128)(2,1)S(1)} %get-tuple-element.44), channel_id=1, source_target_pairs={{0,2},{1,3},{2,0},{3,1},{4,6},{5,7},{6,4},{7,5},{8,10},{9,11},{10,... | collective-permute-start | bytes 344072 | tf_op jit(solution)/shard_map/ppermute | solution.py:417
  25.3 0.0 copy-start
  25.3 1.5 %collective-permute-start.12 = (bf16[64,896]{1,0:T(8,128)(2,1)S(1)}, bf16[64,896]{1,0:T(8,128)(2,1)S(1)}, u32[]{:S(2)}, u32[]{:S(2)}) collective-permute-start(bf16[64,896]{1,0:T(8,128)(2,1)S(1)} %get-tuple-element.45), channel_id=1, source_target_pairs={{0,1},{1,0},{2,3},{3,2},{4,5},{5,4},{6,7},{7,6},{8,9},{9,8},{10,11... | collective-permute-start | bytes 344072 | tf_op jit(solution)/shard_map/ppermute | solution.py:417
  26.8 3.4 %collective-permute-done.10.refs_0_ = bf16[64,896]{1,0:T(8,128)(2,1)S(1)} collective-permute-done((bf16[64,896]{1,0:T(8,128)(2,1)S(1)}, bf16[64,896]{1,0:T(8,128)(2,1)S(1)}, u32[]{:S(2)}, u32[]{:S(2)}) %collective-permute-start.10) | collective-permute-done | bytes 114720 | tf_op jit(solution)/shard_map/ppermute | solution.py:417
  30.2 1.3 %collective-permute-done.11.refs_1_ = bf16[64,896]{1,0:T(8,128)(2,1)S(1)} collective-permute-done((bf16[64,896]{1,0:T(8,128)(2,1)S(1)}, bf16[64,896]{1,0:T(8,128)(2,1)S(1)}, u32[]{:S(2)}, u32[]{:S(2)}) %collective-permute-start.11) | collective-permute-done | bytes 114720 | tf_op jit(solution)/shard_map/ppermute | solution.py:417
  31.5 0.0 collective-permute-done.12.refs_2_
  31.5 0.0 copy-done
  31.5 2.8 %shard_map.81.refs_0_ = bf16[288,128]{1,0:T(8,128)(2,1)S(1)} custom-call(s32[3]{0:T(128)S(1)} %pad_add_fusion.index, s32[2,1,2]{2,1,0:T(1,128)S(1)} %copy-done, bf16[64,896]{1,0:T(8,128)(2,1)S(1)} %collective-permute-done.10.refs_0_, bf16[64,896]{1,0:T(8,128)(2,1)S(1)} %collective-permute-done.11.refs_1_, ...), custom_call_target="tpu_custom_call" | custom-call | tf_op jit(solution)/shard_map/pallas_call | solution.py:387
  34.3 1.2 %collective-permute-start.15 = (bf16[288,128]{1,0:T(8,128)(2,1)S(1)}, bf16[288,128]{1,0:T(8,128)(2,1)S(1)}, u32[]{:S(2)}, u32[]{:S(2)}) collective-permute-start(bf16[288,128]{1,0:T(8,128)(2,1)S(1)} %shard_map.81.refs_0_), channel_id=1, source_target_pairs={{0,3},{1,2},{2,1},{3,0},{4,7},{5,6},{6,5},{7,4},{8,11},{9,10},{10,... | collective-permute-start | bytes 221192 | tf_op jit(solution)/shard_map/ppermute | solution.py:417
  35.6 1.4 %collective-permute-start.14 = (bf16[288,128]{1,0:T(8,128)(2,1)S(1)}, bf16[288,128]{1,0:T(8,128)(2,1)S(1)}, u32[]{:S(2)}, u32[]{:S(2)}) collective-permute-start(bf16[288,128]{1,0:T(8,128)(2,1)S(1)} %shard_map.81.refs_0_), channel_id=1, source_target_pairs={{0,2},{1,3},{2,0},{3,1},{4,6},{5,7},{6,4},{7,5},{8,10},{9,11},{10,... | collective-permute-start | bytes 221192 | tf_op jit(solution)/shard_map/ppermute | solution.py:417
  36.9 1.0 %collective-permute-start.13 = (bf16[288,128]{1,0:T(8,128)(2,1)S(1)}, bf16[288,128]{1,0:T(8,128)(2,1)S(1)}, u32[]{:S(2)}, u32[]{:S(2)}) collective-permute-start(bf16[288,128]{1,0:T(8,128)(2,1)S(1)} %shard_map.81.refs_0_), channel_id=1, source_target_pairs={{0,1},{1,0},{2,3},{3,2},{4,5},{5,4},{6,7},{7,6},{8,9},{9,8},{10,11... | collective-permute-start | bytes 221192 | tf_op jit(solution)/shard_map/ppermute | solution.py:417
  37.9 2.3 %collective-permute-done.15.refs_3_ = bf16[288,128]{1,0:T(8,128)(2,1)S(1)} collective-permute-done((bf16[288,128]{1,0:T(8,128)(2,1)S(1)}, bf16[288,128]{1,0:T(8,128)(2,1)S(1)}, u32[]{:S(2)}, u32[]{:S(2)}) %collective-permute-start.15) | collective-permute-done | bytes 73760 | tf_op jit(solution)/shard_map/ppermute | solution.py:417
  40.2 0.3 collective-permute-done.14.refs_2_
  40.5 0.7 %collective-permute-done.13.refs_1_ = bf16[288,128]{1,0:T(8,128)(2,1)S(1)} collective-permute-done((bf16[288,128]{1,0:T(8,128)(2,1)S(1)}, bf16[288,128]{1,0:T(8,128)(2,1)S(1)}, u32[]{:S(2)}, u32[]{:S(2)}) %collective-permute-start.13) | collective-permute-done | bytes 73760 | tf_op jit(solution)/shard_map/ppermute | solution.py:417
  41.3 1.3 %shard_map.82 = (f32[2,256,256]{2,1,0:T(8,128)S(1)}, bf16[2,256,256]{2,1,0:T(8,128)(2,1)S(1)}, bf16[640,256]{1,0:T(8,128)(2,1)S(1)}, bf16[256,64]{1,0:T(8,128)(2,1)S(1)}, bf16[64,192]{1,0:T(8,128)(2,1)S(1)}) custom-call(s32[3]{0:T(128)S(1)} %pad_add_fusion.index, bf16[288,128]{1,0:T(8,128)(2,1)S(1)} %shard_map.81.refs_0_, ...), custom_call_target="tpu_custom_call" | custom-call | tf_op jit(solution)/shard_map/pallas_call | solution.py:387
  42.6 0.1 collective-permute-start.17
  42.7 1.0 %shard_map.83 = (f32[2,256,256]{2,1,0:T(8,128)S(1)}, bf16[2,256,256]{2,1,0:T(8,128)(2,1)S(1)}) custom-call(s32[3]{0:T(128)S(1)} %pad_add_fusion.index, bf16[640,256]{1,0:T(8,128)(2,1)S(1)} %get-tuple-element.51.turned_ref, bf16[256,64]{1,0:T(8,128)(2,1)S(1)} %get-tuple-element.52.small_ref, bf16[64,192]{1,0:T(8,128)(2,1)S(1)} %get-tuple-element.53.small_t_ref, ...), custom_call_target="tpu_custom_call" | custom-call | tf_op jit(solution)/shard_map/pallas_call | solution.py:387
  43.7 0.6 collective-permute-start.16
  44.3 0.0 collective-permute-done.17.come_ref
  44.4 1.1 %collective-permute-start.18 = (bf16[128,256]{1,0:T(8,128)(2,1)S(1)}, bf16[128,256]{1,0:T(8,128)(2,1)S(1)}, u32[]{:S(2)}, u32[]{:S(2)}) collective-permute-start(bf16[128,256]{1,0:T(8,128)(2,1)S(1)} %get-tuple-element.60), channel_id=1, source_target_pairs={{0,4},{1,5},{2,6},{3,7},{4,0},{5,1},{6,2},{7,3},{8,12},{9,13},{10,... | collective-permute-start | bytes 196616 | tf_op jit(solution)/shard_map/ppermute | solution.py:410
  45.4 1.0 %collective-permute-start.20 = (bf16[128,256]{1,0:T(8,128)(2,1)S(1)}, bf16[128,256]{1,0:T(8,128)(2,1)S(1)}, u32[]{:S(2)}, u32[]{:S(2)}) collective-permute-start(bf16[128,256]{1,0:T(8,128)(2,1)S(1)} %get-tuple-element.62), channel_id=1, source_target_pairs={{0,4},{1,5},{2,6},{3,7},{4,0},{5,1},{6,2},{7,3},{8,12},{9,13},{10,... | collective-permute-start | bytes 196616 | tf_op jit(solution)/shard_map/ppermute | solution.py:410
  46.4 0.0 collective-permute-done.16.come_ref
  46.5 0.1 shard_map.84
  46.5 1.1 %collective-permute-start.22 = (bf16[256,256]{1,0:T(8,128)(2,1)S(1)}, bf16[256,256]{1,0:T(8,128)(2,1)S(1)}, u32[]{:S(2)}, u32[]{:S(2)}) collective-permute-start(bf16[256,256]{1,0:T(8,128)(2,1)S(1)} %get-tuple-element.63), channel_id=1, source_target_pairs={{0,4},{1,5},{2,6},{3,7},{4,0},{5,1},{6,2},{7,3},{8,12},{9,13},{10,... | collective-permute-start | bytes 393224 | tf_op jit(solution)/shard_map/ppermute | solution.py:410
  47.6 1.8 %collective-permute-done.18.b_ref = bf16[128,256]{1,0:T(8,128)(2,1)S(1)} collective-permute-done((bf16[128,256]{1,0:T(8,128)(2,1)S(1)}, bf16[128,256]{1,0:T(8,128)(2,1)S(1)}, u32[]{:S(2)}, u32[]{:S(2)}) %collective-permute-start.18) | collective-permute-done | bytes 65568 | tf_op jit(solution)/shard_map/ppermute | solution.py:410
  49.4 2.2 %collective-permute-start.19 = (bf16[128,256]{1,0:T(8,128)(2,1)S(1)}, bf16[128,256]{1,0:T(8,128)(2,1)S(1)}, u32[]{:S(2)}, u32[]{:S(2)}) collective-permute-start(bf16[128,256]{1,0:T(8,128)(2,1)S(1)} %shard_map.86), channel_id=1, source_target_pairs={{0,8},{1,9},{2,10},{3,11},{4,12},{5,13},{6,14},{7,15},{8,0},{9,1},... | collective-permute-start | bytes 196616 | tf_op jit(solution)/shard_map/ppermute | solution.py:410
  51.6 0.0 collective-permute-done.20.b_ref
  51.7 2.2 %collective-permute-start.21 = (bf16[128,256]{1,0:T(8,128)(2,1)S(1)}, bf16[128,256]{1,0:T(8,128)(2,1)S(1)}, u32[]{:S(2)}, u32[]{:S(2)}) collective-permute-start(bf16[128,256]{1,0:T(8,128)(2,1)S(1)} %shard_map.88), channel_id=1, source_target_pairs={{0,8},{1,9},{2,10},{3,11},{4,12},{5,13},{6,14},{7,15},{8,0},{9,1},... | collective-permute-start | bytes 196616 | tf_op jit(solution)/shard_map/ppermute | solution.py:410
  53.9 2.2 %collective-permute-done.19.part_ref = bf16[128,256]{1,0:T(8,128)(2,1)S(1)} collective-permute-done((bf16[128,256]{1,0:T(8,128)(2,1)S(1)}, bf16[128,256]{1,0:T(8,128)(2,1)S(1)}, u32[]{:S(2)}, u32[]{:S(2)}) %collective-permute-start.19) | collective-permute-done | bytes 65568 | tf_op jit(solution)/shard_map/ppermute | solution.py:410
  56.2 1.7 %collective-permute-done.21.part_ref = bf16[128,256]{1,0:T(8,128)(2,1)S(1)} collective-permute-done((bf16[128,256]{1,0:T(8,128)(2,1)S(1)}, bf16[128,256]{1,0:T(8,128)(2,1)S(1)}, u32[]{:S(2)}, u32[]{:S(2)}) %collective-permute-start.21) | collective-permute-done | bytes 65568 | tf_op jit(solution)/shard_map/ppermute | solution.py:410
  57.9 0.0 collective-permute-done.22.refs_0_
  57.9 0.7 %shard_map.90 = (f32[192,256]{1,0:T(8,128)}, f32[64,256]{1,0:T(8,128)}) custom-call(f32[256,256]{1,0:T(8,128)S(1)} %shard_map.89.keep_ref, bf16[256,256]{1,0:T(8,128)(2,1)S(1)} %collective-permute-done.22.refs_0_), custom_call_target="tpu_custom_call" | custom-call | tf_op jit(solution)/shard_map/pallas_call | solution.py:387
  (6 shorter events, 0.1 us)
Async XLA Ops:
  2.4 13.4 %collective-permute-start = (bf16[2,64,1024]{2,1,0:T(8,128)(2,1)S(1)}, bf16[2,64,1024]{2,1,0:T(8,128)(2,1)S(1)}, u32[]{:S(2)}, u32[]{:S(2)}) collective-permute-start(bf16[2,64,1024]{2,1,0:T(8,128)(2,1)S(1)} %get-tuple-element.35), channel_id=1, source_target_pairs={{0,3},{1,2},{2,1},{3,0},{4,7},{5,6},{6,5},{7,4},{8,11},{9,10},{10,... | collective-permute-start | bytes 786440 | tf_op jit(solution)/shard_map/ppermute | solution.py:417
  6.4 9.3 %copy-start.1 = (bf16[1,4096]{1,0:T(2,128)(2,1)S(1)}, bf16[1,4096]{1,0:T(2,128)(2,1)}, u32[]{:S(2)}) copy-start(bf16[1,4096]{1,0:T(2,128)(2,1)} %param.9) | copy-start | bytes 24580
  6.4 8.8 %collective-permute-start.4 = (bf16[256,256]{1,0:T(8,128)(2,1)S(1)}, bf16[256,256]{1,0:T(8,128)(2,1)S(1)}, u32[]{:S(2)}, u32[]{:S(2)}) collective-permute-start(bf16[256,256]{1,0:T(8,128)(2,1)S(1)} %get-tuple-element.36.pack_ref), channel_id=1, source_target_pairs={{0,8},{1,9},{2,10},{3,11},{4,12},{5,13},{6,14},{7,15},{8,0},{9,1},... | collective-permute-start | bytes 393224 | tf_op jit(solution)/shard_map/ppermute | solution.py:410
  8.9 6.8 %collective-permute-start.3 = (bf16[256,256]{1,0:T(8,128)(2,1)S(1)}, bf16[256,256]{1,0:T(8,128)(2,1)S(1)}, u32[]{:S(2)}, u32[]{:S(2)}) collective-permute-start(bf16[256,256]{1,0:T(8,128)(2,1)S(1)} %get-tuple-element.36.pack_ref), channel_id=1, source_target_pairs={{0,4},{1,5},{2,6},{3,7},{4,0},{5,1},{6,2},{7,3},{8,12},{9,13},{10,... | collective-permute-start | bytes 393224 | tf_op jit(solution)/shard_map/ppermute | solution.py:410
  12.2 8.4 %collective-permute-start.1 = (bf16[2,64,1024]{2,1,0:T(8,128)(2,1)S(1)}, bf16[2,64,1024]{2,1,0:T(8,128)(2,1)S(1)}, u32[]{:S(2)}, u32[]{:S(2)}) collective-permute-start(bf16[2,64,1024]{2,1,0:T(8,128)(2,1)S(1)} %get-tuple-element.39), channel_id=1, source_target_pairs={{0,2},{1,3},{2,0},{3,1},{4,6},{5,7},{6,4},{7,5},{8,10},{9,11},{10,... | collective-permute-start | bytes 786440 | tf_op jit(solution)/shard_map/ppermute | solution.py:417
  12.8 7.8 %collective-permute-start.2 = (bf16[2,64,1024]{2,1,0:T(8,128)(2,1)S(1)}, bf16[2,64,1024]{2,1,0:T(8,128)(2,1)S(1)}, u32[]{:S(2)}, u32[]{:S(2)}) collective-permute-start(bf16[2,64,1024]{2,1,0:T(8,128)(2,1)S(1)} %get-tuple-element.40), channel_id=1, source_target_pairs={{0,1},{1,0},{2,3},{3,2},{4,5},{5,4},{6,7},{7,6},{8,9},{9,8},{10,11... | collective-permute-start | bytes 786440 | tf_op jit(solution)/shard_map/ppermute | solution.py:417
  15.1 5.0 %collective-permute-start.5 = (bf16[256,256]{1,0:T(8,128)(2,1)S(1)}, bf16[256,256]{1,0:T(8,128)(2,1)S(1)}, u32[]{:S(2)}, u32[]{:S(2)}) collective-permute-start(bf16[256,256]{1,0:T(8,128)(2,1)S(1)} %collective-permute-done.4.refs_6_), channel_id=1, source_target_pairs={{0,4},{1,5},{2,6},{3,7},{4,0},{5,1},{6,2},{7,3},{8,12},{9,13},{10,... | collective-permute-start | bytes 393224 | tf_op jit(solution)/shard_map/ppermute | solution.py:410
  15.7 4.4 %collective-permute-start.7 = (bf16[256,256]{1,0:T(8,128)(2,1)S(1)}, bf16[256,256]{1,0:T(8,128)(2,1)S(1)}, u32[]{:S(2)}, u32[]{:S(2)}) collective-permute-start(bf16[256,256]{1,0:T(8,128)(2,1)S(1)} %collective-permute-done.3.refs_5_), channel_id=1, source_target_pairs={{0,16},{16,0},{1,17},{17,1},{2,18},{18,2},{3,19},{19,3},{4,20},{20... | collective-permute-start | bytes 393224 | tf_op jit(solution)/shard_map/ppermute | solution.py:413
  17.3 4.3 %collective-permute-start.6 = (bf16[272,256]{1,0:T(8,128)(2,1)S(1)}, bf16[272,256]{1,0:T(8,128)(2,1)S(1)}, u32[]{:S(2)}, u32[]{:S(2)}) collective-permute-start(bf16[272,256]{1,0:T(8,128)(2,1)S(1)} %get-tuple-element.41.refs_4_), channel_id=1, source_target_pairs={{0,16},{16,0},{1,17},{17,1},{2,18},{18,2},{3,19},{19,3},{4,20},{20... | collective-permute-start | bytes 417800 | tf_op jit(solution)/shard_map/ppermute | solution.py:413
  20.1 1.3 %collective-permute-start.9 = (bf16[256,256]{1,0:T(8,128)(2,1)S(1)}, bf16[256,256]{1,0:T(8,128)(2,1)S(1)}, u32[]{:S(2)}, u32[]{:S(2)}) collective-permute-start(bf16[256,256]{1,0:T(8,128)(2,1)S(1)} %collective-permute-done.5.refs_7_), channel_id=1, source_target_pairs={{0,16},{16,0},{1,17},{17,1},{2,18},{18,2},{3,19},{19,3},{4,20},{20... | collective-permute-start | bytes 393224 | tf_op jit(solution)/shard_map/ppermute | solution.py:413
  20.1 1.5 %collective-permute-start.8 = (bf16[256,256]{1,0:T(8,128)(2,1)S(1)}, bf16[256,256]{1,0:T(8,128)(2,1)S(1)}, u32[]{:S(2)}, u32[]{:S(2)}) collective-permute-start(bf16[256,256]{1,0:T(8,128)(2,1)S(1)} %collective-permute-done.4.refs_6_), channel_id=1, source_target_pairs={{0,16},{16,0},{1,17},{17,1},{2,18},{18,2},{3,19},{19,3},{4,20},{20... | collective-permute-start | bytes 393224 | tf_op jit(solution)/shard_map/ppermute | solution.py:413
  23.2 7.0 %collective-permute-start.10 = (bf16[64,896]{1,0:T(8,128)(2,1)S(1)}, bf16[64,896]{1,0:T(8,128)(2,1)S(1)}, u32[]{:S(2)}, u32[]{:S(2)}) collective-permute-start(bf16[64,896]{1,0:T(8,128)(2,1)S(1)} %get-tuple-element.43), channel_id=1, source_target_pairs={{0,3},{1,2},{2,1},{3,0},{4,7},{5,6},{6,5},{7,4},{8,11},{9,10},{10,... | collective-permute-start | bytes 344072 | tf_op jit(solution)/shard_map/ppermute | solution.py:417
  23.9 7.6 %collective-permute-start.11 = (bf16[64,896]{1,0:T(8,128)(2,1)S(1)}, bf16[64,896]{1,0:T(8,128)(2,1)S(1)}, u32[]{:S(2)}, u32[]{:S(2)}) collective-permute-start(bf16[64,896]{1,0:T(8,128)(2,1)S(1)} %get-tuple-element.44), channel_id=1, source_target_pairs={{0,2},{1,3},{2,0},{3,1},{4,6},{5,7},{6,4},{7,5},{8,10},{9,11},{10,... | collective-permute-start | bytes 344072 | tf_op jit(solution)/shard_map/ppermute | solution.py:417
  25.3 6.2 %copy-start = (s32[2,1,2]{2,1,0:T(1,128)S(1)}, s32[2,1,2]{2,1,0:T(1,128)}, u32[]{:S(2)}) copy-start(s32[2,1,2]{2,1,0:T(1,128)} %docs.1) | copy-start | bytes 52
  25.3 6.2 %collective-permute-start.12 = (bf16[64,896]{1,0:T(8,128)(2,1)S(1)}, bf16[64,896]{1,0:T(8,128)(2,1)S(1)}, u32[]{:S(2)}, u32[]{:S(2)}) collective-permute-start(bf16[64,896]{1,0:T(8,128)(2,1)S(1)} %get-tuple-element.45), channel_id=1, source_target_pairs={{0,1},{1,0},{2,3},{3,2},{4,5},{5,4},{6,7},{7,6},{8,9},{9,8},{10,11... | collective-permute-start | bytes 344072 | tf_op jit(solution)/shard_map/ppermute | solution.py:417
  34.3 5.9 %collective-permute-start.15 = (bf16[288,128]{1,0:T(8,128)(2,1)S(1)}, bf16[288,128]{1,0:T(8,128)(2,1)S(1)}, u32[]{:S(2)}, u32[]{:S(2)}) collective-permute-start(bf16[288,128]{1,0:T(8,128)(2,1)S(1)} %shard_map.81.refs_0_), channel_id=1, source_target_pairs={{0,3},{1,2},{2,1},{3,0},{4,7},{5,6},{6,5},{7,4},{8,11},{9,10},{10,... | collective-permute-start | bytes 221192 | tf_op jit(solution)/shard_map/ppermute | solution.py:417
  35.6 5.0 %collective-permute-start.14 = (bf16[288,128]{1,0:T(8,128)(2,1)S(1)}, bf16[288,128]{1,0:T(8,128)(2,1)S(1)}, u32[]{:S(2)}, u32[]{:S(2)}) collective-permute-start(bf16[288,128]{1,0:T(8,128)(2,1)S(1)} %shard_map.81.refs_0_), channel_id=1, source_target_pairs={{0,2},{1,3},{2,0},{3,1},{4,6},{5,7},{6,4},{7,5},{8,10},{9,11},{10,... | collective-permute-start | bytes 221192 | tf_op jit(solution)/shard_map/ppermute | solution.py:417
  36.9 4.4 %collective-permute-start.13 = (bf16[288,128]{1,0:T(8,128)(2,1)S(1)}, bf16[288,128]{1,0:T(8,128)(2,1)S(1)}, u32[]{:S(2)}, u32[]{:S(2)}) collective-permute-start(bf16[288,128]{1,0:T(8,128)(2,1)S(1)} %shard_map.81.refs_0_), channel_id=1, source_target_pairs={{0,1},{1,0},{2,3},{3,2},{4,5},{5,4},{6,7},{7,6},{8,9},{9,8},{10,11... | collective-permute-start | bytes 221192 | tf_op jit(solution)/shard_map/ppermute | solution.py:417
  42.6 1.7 %collective-permute-start.17 = (bf16[2,256,256]{2,1,0:T(8,128)(2,1)S(1)}, bf16[2,256,256]{2,1,0:T(8,128)(2,1)S(1)}, u32[]{:S(2)}, u32[]{:S(2)}) collective-permute-start(bf16[2,256,256]{2,1,0:T(8,128)(2,1)S(1)} %get-tuple-element.58), channel_id=1, source_target_pairs={{0,16},{16,0},{1,17},{17,1},{2,18},{18,2},{3,19},{19,3},{4,20},{20... | collective-permute-start | bytes 786440 | tf_op jit(solution)/shard_map/ppermute | solution.py:413
  43.7 2.7 %collective-permute-start.16 = (bf16[2,256,256]{2,1,0:T(8,128)(2,1)S(1)}, bf16[2,256,256]{2,1,0:T(8,128)(2,1)S(1)}, u32[]{:S(2)}, u32[]{:S(2)}) collective-permute-start(bf16[2,256,256]{2,1,0:T(8,128)(2,1)S(1)} %get-tuple-element.55), channel_id=1, source_target_pairs={{0,16},{16,0},{1,17},{17,1},{2,18},{18,2},{3,19},{19,3},{4,20},{20... | collective-permute-start | bytes 786440 | tf_op jit(solution)/shard_map/ppermute | solution.py:413
  44.4 5.0 %collective-permute-start.18 = (bf16[128,256]{1,0:T(8,128)(2,1)S(1)}, bf16[128,256]{1,0:T(8,128)(2,1)S(1)}, u32[]{:S(2)}, u32[]{:S(2)}) collective-permute-start(bf16[128,256]{1,0:T(8,128)(2,1)S(1)} %get-tuple-element.60), channel_id=1, source_target_pairs={{0,4},{1,5},{2,6},{3,7},{4,0},{5,1},{6,2},{7,3},{8,12},{9,13},{10,... | collective-permute-start | bytes 196616 | tf_op jit(solution)/shard_map/ppermute | solution.py:410
  45.4 6.2 %collective-permute-start.20 = (bf16[128,256]{1,0:T(8,128)(2,1)S(1)}, bf16[128,256]{1,0:T(8,128)(2,1)S(1)}, u32[]{:S(2)}, u32[]{:S(2)}) collective-permute-start(bf16[128,256]{1,0:T(8,128)(2,1)S(1)} %get-tuple-element.62), channel_id=1, source_target_pairs={{0,4},{1,5},{2,6},{3,7},{4,0},{5,1},{6,2},{7,3},{8,12},{9,13},{10,... | collective-permute-start | bytes 196616 | tf_op jit(solution)/shard_map/ppermute | solution.py:410
  46.5 11.4 %collective-permute-start.22 = (bf16[256,256]{1,0:T(8,128)(2,1)S(1)}, bf16[256,256]{1,0:T(8,128)(2,1)S(1)}, u32[]{:S(2)}, u32[]{:S(2)}) collective-permute-start(bf16[256,256]{1,0:T(8,128)(2,1)S(1)} %get-tuple-element.63), channel_id=1, source_target_pairs={{0,4},{1,5},{2,6},{3,7},{4,0},{5,1},{6,2},{7,3},{8,12},{9,13},{10,... | collective-permute-start | bytes 393224 | tf_op jit(solution)/shard_map/ppermute | solution.py:410
  49.4 6.7 %collective-permute-start.19 = (bf16[128,256]{1,0:T(8,128)(2,1)S(1)}, bf16[128,256]{1,0:T(8,128)(2,1)S(1)}, u32[]{:S(2)}, u32[]{:S(2)}) collective-permute-start(bf16[128,256]{1,0:T(8,128)(2,1)S(1)} %shard_map.86), channel_id=1, source_target_pairs={{0,8},{1,9},{2,10},{3,11},{4,12},{5,13},{6,14},{7,15},{8,0},{9,1},... | collective-permute-start | bytes 196616 | tf_op jit(solution)/shard_map/ppermute | solution.py:410
  51.7 6.2 %collective-permute-start.21 = (bf16[128,256]{1,0:T(8,128)(2,1)S(1)}, bf16[128,256]{1,0:T(8,128)(2,1)S(1)}, u32[]{:S(2)}, u32[]{:S(2)}) collective-permute-start(bf16[128,256]{1,0:T(8,128)(2,1)S(1)} %shard_map.88), channel_id=1, source_target_pairs={{0,8},{1,9},{2,10},{3,11},{4,12},{5,13},{6,14},{7,15},{8,0},{9,1},... | collective-permute-start | bytes 196616 | tf_op jit(solution)/shard_map/ppermute | solution.py:410

commit v20 on v19

--- a/solution.py
+++ b/solution.py
@@ -151,12 +151,12 @@
         copy.wait()
 
 
-def first_kernel(planes, index, qkv_ref, wout_ref, x_ref, c_ref, pack_ref, far_ref, pack_sems, sems):
+def first_kernel(planes, index, qkv_ref, wout_ref, x_ref, c_ref, pack_ref, near_ref, pack_sems, sems):
     qkv_rows = qkv_ref.shape[0]
     copies = [
         pltpu.make_async_copy(qkv_ref, pack_ref.at[:qkv_rows], pack_sems.at[0]),
         pltpu.make_async_copy(wout_ref, pack_ref.at[qkv_rows:], pack_sems.at[1]),
-    ] + block_copies(planes, index, PLANE - 1, (x_ref, c_ref), far_ref, sems)
+    ] + block_copies(planes, index, 1, (x_ref, c_ref), near_ref, sems)
     for copy in copies:
         copy.start()
     for copy in copies:
@@ -166,8 +166,8 @@
 def blocks_kernel(planes, index, x_ref, c_ref, *refs):
     out_refs, sems = refs[:-1], refs[-1]
     copies = []
-    for k, out_ref in enumerate(out_refs, 1):
-        copies += block_copies(planes, index, k, (x_ref, c_ref), out_ref, sems.at[k - 1])
+    for k, out_ref in enumerate(out_refs, 2):
+        copies += block_copies(planes, index, k, (x_ref, c_ref), out_ref, sems.at[k - 2])
     for copy in copies:
         copy.start()
     for copy in copies:
@@ -427,7 +427,7 @@
         for value in (w_qkv[0].T, w_out[0], inputs, cotangent)
     ]
     one_block = jax.ShapeDtypeStruct((2, block, cols), BF16)
-    pack, far_block = pl.pallas_call(
+    pack, near_block = pl.pallas_call(
         functools.partial(first_kernel, planes),
         out_shape=[jax.ShapeDtypeStruct((qkv_rows + heads, width), BF16), one_block],
         in_specs=[smem] + [hbm] * 4,
@@ -443,14 +443,14 @@
         scratch_shapes=[pltpu.SemaphoreType.DMA((PLANE - 2, 2 * planes))],
         compiler_params=params,
     )(index, x_in, c_in)
-    blocks = [*blocks, far_block]
+    blocks = [near_block, *blocks]
     gain = norm_gain[0].reshape(shards, width)
     blocks = far_first([None] + blocks, PLANE, along_plane)
     pieces = {0: pack}
     for step in reversed([1 << bit for bit in range(planes.bit_length() - 1)]):
         for k in list(pieces):
             pieces[k ^ step] = along_z(pieces[k], step)
-    mine, late_gain, _ = lax.optimization_barrier((pack, gain, blocks[3]))
+    mine, late_gain, _ = lax.optimization_barrier((pack, gain, blocks[1]))
     marked, blocks[0] = pl.pallas_call(
         functools.partial(mark_kernel, planes),
         out_shape=[jax.ShapeDtypeStruct((qkv_rows + heads + shards, width), BF16), one_block],
@@ -459,7 +459,7 @@
         scratch_shapes=[pltpu.SemaphoreType.DMA((2 * planes,))],
         compiler_params=params,
     )(index, mine, late_gain, x_in, c_in)
-    pieces[planes // 2], _ = lax.optimization_barrier((pieces[planes // 2], blocks[3]))
+    pieces[planes // 2], _ = lax.optimization_barrier((pieces[planes // 2], blocks[1]))
     own = [marked] + [pieces[k] for k in range(1, planes)]
     other = [to_sibling(piece) for piece in own]
 

time: 58.9 us -> 61.4 us (1.042)
  waiting for transfers between devices: 18.9 us -> 24.5 us
  starting transfers between devices: 26.2 us -> 23.1 us
    ppermute x9, waiting for transfers between devices: 8.11 us -> 13.5 us  [along_plane(): return lax.ppermute(value, 'dp', route)]
    ppermute x8, starting transfers between devices: 12.4 us -> 9.23 us  [along_z(): return lax.ppermute(value, 'dp', route)]
    ppermute x8, waiting for transfers between devices: 9.8 us -> 11 us  [along_z(): return lax.ppermute(value, 'dp', route)]
    ppermute x6, waiting for transfers between devices: 1.02 us -> 0.02 us  [to_sibling(): return lax.ppermute(value, 'section', [(0, 1), (1, 0)])]
  transfers between devices with their start and end apart: 23 -> 23, of which waited for: 12 -> 11; matrix products, arithmetic and copies ran while one was open for 0% -> 0% of each run, Pallas kernels for 7% -> 7%
where the time goes in v20:
time: 61.4 us; the launch traced here: 61.1 us
  waiting for transfers between devices  24.5 us (40%)
  starting transfers between devices  23.1 us (38%)
  Pallas kernels  12.5 us (20%)
  between operations  0.79 us (1%)
    ppermute x9, waiting for transfers between devices, along_plane(): return lax.ppermute(value, 'dp', route)  13.5 us
    ppermute x9, starting transfers between devices, along_plane(): return lax.ppermute(value, 'dp', route)  12.2 us
    ppermute x8, waiting for transfers between devices, along_z(): return lax.ppermute(value, 'dp', route)  11 us
    ppermute x8, starting transfers between devices, along_z(): return lax.ppermute(value, 'dp', route)  9.23 us
    pallas_call x11, Pallas kernels, call(): pl.pallas_call(kernel, out_shape=[jax.ShapeDtypeStruct(shape, dtype) for...  7.69 us
    ppermute x6, starting transfers between devices, to_sibling(): return lax.ppermute(value, 'section', [(0, 1), (1, 0)])  1.71 us
    pallas_call x1, Pallas kernels, planar(): pl.pallas_call(functools.partial(blocks_kernel, planes), out_shape=[one_b...  1.69 us
    pallas_call x1, Pallas kernels, planar(): pl.pallas_call(functools.partial(first_kernel, planes), out_shape=[jax.Sh...  1.66 us
  transfers between devices with their start and end apart: 23, of which 11 were waited for; matrix products, arithmetic and copies ran while one was open for 0% of the time, Pallas kernels for 7%

profile of v20, /device:TPU:0, one launch (start us, length us, event | category | flops | bytes accessed | tf_op | source)
XLA Modules:
  0.0 61.1 jit_solution(4173141439926530190)
XLA Ops:
  0.6 0.1 pad_add_fusion.index
  0.7 1.7 %shard_map.77 = (bf16[256,256]{1,0:T(8,128)(2,1)S(1)}, bf16[2,64,1024]{2,1,0:T(8,128)(2,1)S(1)}) custom-call(s32[3]{0:T(128)S(1)} %pad_add_fusion.index, bf16[192,256]{1,0:T(8,128)(2,1)} %bitcast.11, bf16[64,256]{1,0:T(8,128)(2,1)} %bitcast.12, bf16[2,64,4096]{2,1,0:T(8,128)(2,1)} %x_ref.5, bf16[2,64,4096]{2,1,0:T(8,128)(2,1)} %c_ref.5), custom_call_target="tpu_custom_call" | custom-call | tf_op jit(solution)/shard_map/pallas_call | solution.py:430
  2.4 3.0 %collective-permute-start = (bf16[2,64,1024]{2,1,0:T(8,128)(2,1)S(1)}, bf16[2,64,1024]{2,1,0:T(8,128)(2,1)S(1)}, u32[]{:S(2)}, u32[]{:S(2)}) collective-permute-start(bf16[2,64,1024]{2,1,0:T(8,128)(2,1)S(1)} %get-tuple-element.35), channel_id=1, source_target_pairs={{0,1},{1,0},{2,3},{3,2},{4,5},{5,4},{6,7},{7,6},{8,9},{9,8},{10,11... | collective-permute-start | bytes 786440 | tf_op jit(solution)/shard_map/ppermute | solution.py:417
  5.4 0.0 copy-start.1
  5.4 2.6 %collective-permute-start.4 = (bf16[256,256]{1,0:T(8,128)(2,1)S(1)}, bf16[256,256]{1,0:T(8,128)(2,1)S(1)}, u32[]{:S(2)}, u32[]{:S(2)}) collective-permute-start(bf16[256,256]{1,0:T(8,128)(2,1)S(1)} %get-tuple-element.36.pack_ref), channel_id=1, source_target_pairs={{0,8},{1,9},{2,10},{3,11},{4,12},{5,13},{6,14},{7,15},{8,0},{9,1},... | collective-permute-start | bytes 393224 | tf_op jit(solution)/shard_map/ppermute | solution.py:410
  8.0 1.6 %collective-permute-start.3 = (bf16[256,256]{1,0:T(8,128)(2,1)S(1)}, bf16[256,256]{1,0:T(8,128)(2,1)S(1)}, u32[]{:S(2)}, u32[]{:S(2)}) collective-permute-start(bf16[256,256]{1,0:T(8,128)(2,1)S(1)} %get-tuple-element.36.pack_ref), channel_id=1, source_target_pairs={{0,4},{1,5},{2,6},{3,7},{4,0},{5,1},{6,2},{7,3},{8,12},{9,13},{10,... | collective-permute-start | bytes 393224 | tf_op jit(solution)/shard_map/ppermute | solution.py:410
  9.6 1.7 %shard_map.79 = (bf16[2,64,1024]{2,1,0:T(8,128)(2,1)S(1)}, bf16[2,64,1024]{2,1,0:T(8,128)(2,1)S(1)}) custom-call(s32[3]{0:T(128)S(1)} %pad_add_fusion.index, bf16[2,64,4096]{2,1,0:T(8,128)(2,1)} %x_ref.5, bf16[2,64,4096]{2,1,0:T(8,128)(2,1)} %c_ref.5), custom_call_target="tpu_custom_call" | custom-call | tf_op jit(solution)/shard_map/pallas_call | solution.py:438
  11.3 1.6 %collective-permute-start.1 = (bf16[2,64,1024]{2,1,0:T(8,128)(2,1)S(1)}, bf16[2,64,1024]{2,1,0:T(8,128)(2,1)S(1)}, u32[]{:S(2)}, u32[]{:S(2)}) collective-permute-start(bf16[2,64,1024]{2,1,0:T(8,128)(2,1)S(1)} %get-tuple-element.39), channel_id=1, source_target_pairs={{0,3},{1,2},{2,1},{3,0},{4,7},{5,6},{6,5},{7,4},{8,11},{9,10},{10,... | collective-permute-start | bytes 786440 | tf_op jit(solution)/shard_map/ppermute | solution.py:417
  12.8 0.5 collective-permute-start.2
  13.3 0.8 %collective-permute-done.4.refs_6_ = bf16[256,256]{1,0:T(8,128)(2,1)S(1)} collective-permute-done((bf16[256,256]{1,0:T(8,128)(2,1)S(1)}, bf16[256,256]{1,0:T(8,128)(2,1)S(1)}, u32[]{:S(2)}, u32[]{:S(2)}) %collective-permute-start.4) | collective-permute-done | bytes 131104 | tf_op jit(solution)/shard_map/ppermute | solution.py:410
  14.2 0.6 collective-permute-start.5
  14.7 0.0 collective-permute-done.3.refs_5_
  14.7 0.0 collective-permute-start.7
  14.7 0.0 copy-done.1
  14.7 0.1 reduce
  14.8 0.0 collective-permute-done.refs_3_
  14.8 1.5 %shard_map.78 = (bf16[272,256]{1,0:T(8,128)(2,1)S(1)}, bf16[2,64,1024]{2,1,0:T(8,128)(2,1)S(1)}) custom-call(s32[3]{0:T(128)S(1)} %pad_add_fusion.index, bf16[256,256]{1,0:T(8,128)(2,1)S(1)} %get-tuple-element.36.pack_ref, bf16[16,256]{1,0:T(8,128)(2,1)S(1)} %reshape_squeeze.3.gain_ref, bf16[2,64,4096]{2,1,0:T(8,128)(2,1)} %x_ref.5, bf16[2,64,4096]{2,1,0:T(8,128)(2,1)} %c_ref.5), custom_call_target="tpu_custom_call" | custom-call | tf_op jit(solution)/shard_map/pallas_call | solution.py:454
  16.3 0.6 collective-permute-start.6
  16.9 2.2 %collective-permute-done.5.refs_7_ = bf16[256,256]{1,0:T(8,128)(2,1)S(1)} collective-permute-done((bf16[256,256]{1,0:T(8,128)(2,1)S(1)}, bf16[256,256]{1,0:T(8,128)(2,1)S(1)}, u32[]{:S(2)}, u32[]{:S(2)}) %collective-permute-start.5) | collective-permute-done | bytes 131104 | tf_op jit(solution)/shard_map/ppermute | solution.py:410
  19.1 0.0 collective-permute-start.9
  19.1 0.0 collective-permute-done.7.refs_9_
  19.1 0.5 collective-permute-start.8
  19.7 0.0 collective-permute-done.1.refs_1_
  19.7 5.4 %collective-permute-done.2.refs_2_ = bf16[2,64,1024]{2,1,0:T(8,128)(2,1)S(1)} collective-permute-done((bf16[2,64,1024]{2,1,0:T(8,128)(2,1)S(1)}, bf16[2,64,1024]{2,1,0:T(8,128)(2,1)S(1)}, u32[]{:S(2)}, u32[]{:S(2)}) %collective-permute-start.2) | collective-permute-done | bytes 262176 | tf_op jit(solution)/shard_map/ppermute | solution.py:417
  25.1 0.0 collective-permute-done.9.refs_11_
  25.1 0.0 collective-permute-done.8.refs_10_
  25.1 0.0 collective-permute-done.6.refs_8_
  25.1 1.6 %shard_map.80 = (bf16[4,64,1024]{2,1,0:T(8,128)(2,1)S(1)}, bf16[4,64,1024]{2,1,0:T(8,128)(2,1)S(1)}, bf16[4,512,256]{2,1,0:T(8,128)(2,1)S(1)}, f32[4,8,256]{2,1,...) custom-call(s32[3]{0:T(128)S(1)} %pad_add_fusion.index, ...), custom_call_target="tpu_custom_call" | custom-call | tf_op jit(solution)/shard_map/pallas_call | solution.py:387
  26.7 1.6 %collective-permute-start.10 = (bf16[64,896]{1,0:T(8,128)(2,1)S(1)}, bf16[64,896]{1,0:T(8,128)(2,1)S(1)}, u32[]{:S(2)}, u32[]{:S(2)}) collective-permute-start(bf16[64,896]{1,0:T(8,128)(2,1)S(1)} %get-tuple-element.43), channel_id=1, source_target_pairs={{0,3},{1,2},{2,1},{3,0},{4,7},{5,6},{6,5},{7,4},{8,11},{9,10},{10,... | collective-permute-start | bytes 344072 | tf_op jit(solution)/shard_map/ppermute | solution.py:417
  28.2 0.6 collective-permute-start.11
  28.8 0.0 copy-start
  28.8 1.4 %collective-permute-start.12 = (bf16[64,896]{1,0:T(8,128)(2,1)S(1)}, bf16[64,896]{1,0:T(8,128)(2,1)S(1)}, u32[]{:S(2)}, u32[]{:S(2)}) collective-permute-start(bf16[64,896]{1,0:T(8,128)(2,1)S(1)} %get-tuple-element.45), channel_id=1, source_target_pairs={{0,1},{1,0},{2,3},{3,2},{4,5},{5,4},{6,7},{7,6},{8,9},{9,8},{10,11... | collective-permute-start | bytes 344072 | tf_op jit(solution)/shard_map/ppermute | solution.py:417
  30.2 3.4 %collective-permute-done.10.refs_0_ = bf16[64,896]{1,0:T(8,128)(2,1)S(1)} collective-permute-done((bf16[64,896]{1,0:T(8,128)(2,1)S(1)}, bf16[64,896]{1,0:T(8,128)(2,1)S(1)}, u32[]{:S(2)}, u32[]{:S(2)}) %collective-permute-start.10) | collective-permute-done | bytes 114720 | tf_op jit(solution)/shard_map/ppermute | solution.py:417
  33.6 1.5 %collective-permute-done.11.refs_1_ = bf16[64,896]{1,0:T(8,128)(2,1)S(1)} collective-permute-done((bf16[64,896]{1,0:T(8,128)(2,1)S(1)}, bf16[64,896]{1,0:T(8,128)(2,1)S(1)}, u32[]{:S(2)}, u32[]{:S(2)}) %collective-permute-start.11) | collective-permute-done | bytes 114720 | tf_op jit(solution)/shard_map/ppermute | solution.py:417
  35.2 0.0 collective-permute-done.12.refs_2_
  35.2 0.0 copy-done
  35.2 2.8 %shard_map.81.refs_0_ = bf16[288,128]{1,0:T(8,128)(2,1)S(1)} custom-call(s32[3]{0:T(128)S(1)} %pad_add_fusion.index, s32[2,1,2]{2,1,0:T(1,128)S(1)} %copy-done, bf16[64,896]{1,0:T(8,128)(2,1)S(1)} %collective-permute-done.10.refs_0_, bf16[64,896]{1,0:T(8,128)(2,1)S(1)} %collective-permute-done.11.refs_1_, ...), custom_call_target="tpu_custom_call" | custom-call | tf_op jit(solution)/shard_map/pallas_call | solution.py:387
  38.0 1.6 %collective-permute-start.15 = (bf16[288,128]{1,0:T(8,128)(2,1)S(1)}, bf16[288,128]{1,0:T(8,128)(2,1)S(1)}, u32[]{:S(2)}, u32[]{:S(2)}) collective-permute-start(bf16[288,128]{1,0:T(8,128)(2,1)S(1)} %shard_map.81.refs_0_), channel_id=1, source_target_pairs={{0,3},{1,2},{2,1},{3,0},{4,7},{5,6},{6,5},{7,4},{8,11},{9,10},{10,... | collective-permute-start | bytes 221192 | tf_op jit(solution)/shard_map/ppermute | solution.py:417
  39.6 0.6 collective-permute-start.14
  40.1 1.4 %collective-permute-start.13 = (bf16[288,128]{1,0:T(8,128)(2,1)S(1)}, bf16[288,128]{1,0:T(8,128)(2,1)S(1)}, u32[]{:S(2)}, u32[]{:S(2)}) collective-permute-start(bf16[288,128]{1,0:T(8,128)(2,1)S(1)} %shard_map.81.refs_0_), channel_id=1, source_target_pairs={{0,1},{1,0},{2,3},{3,2},{4,5},{5,4},{6,7},{7,6},{8,9},{9,8},{10,11... | collective-permute-start | bytes 221192 | tf_op jit(solution)/shard_map/ppermute | solution.py:417
  41.6 2.1 %collective-permute-done.15.refs_3_ = bf16[288,128]{1,0:T(8,128)(2,1)S(1)} collective-permute-done((bf16[288,128]{1,0:T(8,128)(2,1)S(1)}, bf16[288,128]{1,0:T(8,128)(2,1)S(1)}, u32[]{:S(2)}, u32[]{:S(2)}) %collective-permute-start.15) | collective-permute-done | bytes 73760 | tf_op jit(solution)/shard_map/ppermute | solution.py:417
  43.6 1.1 %collective-permute-done.14.refs_2_ = bf16[288,128]{1,0:T(8,128)(2,1)S(1)} collective-permute-done((bf16[288,128]{1,0:T(8,128)(2,1)S(1)}, bf16[288,128]{1,0:T(8,128)(2,1)S(1)}, u32[]{:S(2)}, u32[]{:S(2)}) %collective-permute-start.14) | collective-permute-done | bytes 73760 | tf_op jit(solution)/shard_map/ppermute | solution.py:417
  44.7 0.0 collective-permute-done.13.refs_1_
  44.7 1.4 %shard_map.82 = (f32[2,256,256]{2,1,0:T(8,128)S(1)}, bf16[2,256,256]{2,1,0:T(8,128)(2,1)S(1)}, bf16[640,256]{1,0:T(8,128)(2,1)S(1)}, bf16[256,64]{1,0:T(8,128)(2,1)S(1)}, bf16[64,192]{1,0:T(8,128)(2,1)S(1)}) custom-call(s32[3]{0:T(128)S(1)} %pad_add_fusion.index, bf16[288,128]{1,0:T(8,128)(2,1)S(1)} %shard_map.81.refs_0_, ...), custom_call_target="tpu_custom_call" | custom-call | tf_op jit(solution)/shard_map/pallas_call | solution.py:387
  46.1 0.1 collective-permute-start.17
  46.2 1.0 %shard_map.83 = (f32[2,256,256]{2,1,0:T(8,128)S(1)}, bf16[2,256,256]{2,1,0:T(8,128)(2,1)S(1)}) custom-call(s32[3]{0:T(128)S(1)} %pad_add_fusion.index, bf16[640,256]{1,0:T(8,128)(2,1)S(1)} %get-tuple-element.51.turned_ref, bf16[256,64]{1,0:T(8,128)(2,1)S(1)} %get-tuple-element.52.small_ref, bf16[64,192]{1,0:T(8,128)(2,1)S(1)} %get-tuple-element.53.small_t_ref, ...), custom_call_target="tpu_custom_call" | custom-call | tf_op jit(solution)/shard_map/pallas_call | solution.py:387
  47.2 0.6 collective-permute-start.16
  47.8 0.0 collective-permute-done.17.come_ref
  47.8 0.7 %collective-permute-start.18 = (bf16[128,256]{1,0:T(8,128)(2,1)S(1)}, bf16[128,256]{1,0:T(8,128)(2,1)S(1)}, u32[]{:S(2)}, u32[]{:S(2)}) collective-permute-start(bf16[128,256]{1,0:T(8,128)(2,1)S(1)} %get-tuple-element.60), channel_id=1, source_target_pairs={{0,4},{1,5},{2,6},{3,7},{4,0},{5,1},{6,2},{7,3},{8,12},{9,13},{10,... | collective-permute-start | bytes 196616 | tf_op jit(solution)/shard_map/ppermute | solution.py:410
  48.5 1.5 %collective-permute-start.20 = (bf16[128,256]{1,0:T(8,128)(2,1)S(1)}, bf16[128,256]{1,0:T(8,128)(2,1)S(1)}, u32[]{:S(2)}, u32[]{:S(2)}) collective-permute-start(bf16[128,256]{1,0:T(8,128)(2,1)S(1)} %get-tuple-element.62), channel_id=1, source_target_pairs={{0,4},{1,5},{2,6},{3,7},{4,0},{5,1},{6,2},{7,3},{8,12},{9,13},{10,... | collective-permute-start | bytes 196616 | tf_op jit(solution)/shard_map/ppermute | solution.py:410
  49.9 0.0 collective-permute-done.16.come_ref
  49.9 0.1 shard_map.84
  50.0 0.6 %collective-permute-start.22 = (bf16[256,256]{1,0:T(8,128)(2,1)S(1)}, bf16[256,256]{1,0:T(8,128)(2,1)S(1)}, u32[]{:S(2)}, u32[]{:S(2)}) collective-permute-start(bf16[256,256]{1,0:T(8,128)(2,1)S(1)} %get-tuple-element.63), channel_id=1, source_target_pairs={{0,4},{1,5},{2,6},{3,7},{4,0},{5,1},{6,2},{7,3},{8,12},{9,13},{10,... | collective-permute-start | bytes 393224 | tf_op jit(solution)/shard_map/ppermute | solution.py:410
  50.6 2.2 %collective-permute-done.18.b_ref = bf16[128,256]{1,0:T(8,128)(2,1)S(1)} collective-permute-done((bf16[128,256]{1,0:T(8,128)(2,1)S(1)}, bf16[128,256]{1,0:T(8,128)(2,1)S(1)}, u32[]{:S(2)}, u32[]{:S(2)}) %collective-permute-start.18) | collective-permute-done | bytes 65568 | tf_op jit(solution)/shard_map/ppermute | solution.py:410
  52.9 0.1 collective-permute-start.19
  53.0 1.3 %collective-permute-done.20.b_ref = bf16[128,256]{1,0:T(8,128)(2,1)S(1)} collective-permute-done((bf16[128,256]{1,0:T(8,128)(2,1)S(1)}, bf16[128,256]{1,0:T(8,128)(2,1)S(1)}, u32[]{:S(2)}, u32[]{:S(2)}) %collective-permute-start.20) | collective-permute-done | bytes 65568 | tf_op jit(solution)/shard_map/ppermute | solution.py:410
  54.3 1.7 %collective-permute-start.21 = (bf16[128,256]{1,0:T(8,128)(2,1)S(1)}, bf16[128,256]{1,0:T(8,128)(2,1)S(1)}, u32[]{:S(2)}, u32[]{:S(2)}) collective-permute-start(bf16[128,256]{1,0:T(8,128)(2,1)S(1)} %shard_map.88), channel_id=1, source_target_pairs={{0,8},{1,9},{2,10},{3,11},{4,12},{5,13},{6,14},{7,15},{8,0},{9,1},... | collective-permute-start | bytes 196616 | tf_op jit(solution)/shard_map/ppermute | solution.py:410
  56.0 3.0 %collective-permute-done.19.part_ref = bf16[128,256]{1,0:T(8,128)(2,1)S(1)} collective-permute-done((bf16[128,256]{1,0:T(8,128)(2,1)S(1)}, bf16[128,256]{1,0:T(8,128)(2,1)S(1)}, u32[]{:S(2)}, u32[]{:S(2)}) %collective-permute-start.19) | collective-permute-done | bytes 65568 | tf_op jit(solution)/shard_map/ppermute | solution.py:410
  59.0 1.4 %collective-permute-done.21.part_ref = bf16[128,256]{1,0:T(8,128)(2,1)S(1)} collective-permute-done((bf16[128,256]{1,0:T(8,128)(2,1)S(1)}, bf16[128,256]{1,0:T(8,128)(2,1)S(1)}, u32[]{:S(2)}, u32[]{:S(2)}) %collective-permute-start.21) | collective-permute-done | bytes 65568 | tf_op jit(solution)/shard_map/ppermute | solution.py:410
  60.4 0.0 collective-permute-done.22.refs_0_
  60.4 0.7 %shard_map.90 = (f32[192,256]{1,0:T(8,128)}, f32[64,256]{1,0:T(8,128)}) custom-call(f32[256,256]{1,0:T(8,128)S(1)} %shard_map.89.keep_ref, bf16[256,256]{1,0:T(8,128)(2,1)S(1)} %collective-permute-done.22.refs_0_), custom_call_target="tpu_custom_call" | custom-call | tf_op jit(solution)/shard_map/pallas_call | solution.py:387
  (6 shorter events, 0.1 us)
Async XLA Ops:
  2.4 12.4 %collective-permute-start = (bf16[2,64,1024]{2,1,0:T(8,128)(2,1)S(1)}, bf16[2,64,1024]{2,1,0:T(8,128)(2,1)S(1)}, u32[]{:S(2)}, u32[]{:S(2)}) collective-permute-start(bf16[2,64,1024]{2,1,0:T(8,128)(2,1)S(1)} %get-tuple-element.35), channel_id=1, source_target_pairs={{0,1},{1,0},{2,3},{3,2},{4,5},{5,4},{6,7},{7,6},{8,9},{9,8},{10,11... | collective-permute-start | bytes 786440 | tf_op jit(solution)/shard_map/ppermute | solution.py:417
  5.4 9.3 %copy-start.1 = (bf16[1,4096]{1,0:T(2,128)(2,1)S(1)}, bf16[1,4096]{1,0:T(2,128)(2,1)}, u32[]{:S(2)}) copy-start(bf16[1,4096]{1,0:T(2,128)(2,1)} %param.9) | copy-start | bytes 24580
  5.4 8.8 %collective-permute-start.4 = (bf16[256,256]{1,0:T(8,128)(2,1)S(1)}, bf16[256,256]{1,0:T(8,128)(2,1)S(1)}, u32[]{:S(2)}, u32[]{:S(2)}) collective-permute-start(bf16[256,256]{1,0:T(8,128)(2,1)S(1)} %get-tuple-element.36.pack_ref), channel_id=1, source_target_pairs={{0,8},{1,9},{2,10},{3,11},{4,12},{5,13},{6,14},{7,15},{8,0},{9,1},... | collective-permute-start | bytes 393224 | tf_op jit(solution)/shard_map/ppermute | solution.py:410
  8.0 6.8 %collective-permute-start.3 = (bf16[256,256]{1,0:T(8,128)(2,1)S(1)}, bf16[256,256]{1,0:T(8,128)(2,1)S(1)}, u32[]{:S(2)}, u32[]{:S(2)}) collective-permute-start(bf16[256,256]{1,0:T(8,128)(2,1)S(1)} %get-tuple-element.36.pack_ref), channel_id=1, source_target_pairs={{0,4},{1,5},{2,6},{3,7},{4,0},{5,1},{6,2},{7,3},{8,12},{9,13},{10,... | collective-permute-start | bytes 393224 | tf_op jit(solution)/shard_map/ppermute | solution.py:410
  11.3 8.4 %collective-permute-start.1 = (bf16[2,64,1024]{2,1,0:T(8,128)(2,1)S(1)}, bf16[2,64,1024]{2,1,0:T(8,128)(2,1)S(1)}, u32[]{:S(2)}, u32[]{:S(2)}) collective-permute-start(bf16[2,64,1024]{2,1,0:T(8,128)(2,1)S(1)} %get-tuple-element.39), channel_id=1, source_target_pairs={{0,3},{1,2},{2,1},{3,0},{4,7},{5,6},{6,5},{7,4},{8,11},{9,10},{10,... | collective-permute-start | bytes 786440 | tf_op jit(solution)/shard_map/ppermute | solution.py:417
  12.8 12.2 %collective-permute-start.2 = (bf16[2,64,1024]{2,1,0:T(8,128)(2,1)S(1)}, bf16[2,64,1024]{2,1,0:T(8,128)(2,1)S(1)}, u32[]{:S(2)}, u32[]{:S(2)}) collective-permute-start(bf16[2,64,1024]{2,1,0:T(8,128)(2,1)S(1)} %get-tuple-element.40), channel_id=1, source_target_pairs={{0,2},{1,3},{2,0},{3,1},{4,6},{5,7},{6,4},{7,5},{8,10},{9,11},{10,... | collective-permute-start | bytes 786440 | tf_op jit(solution)/shard_map/ppermute | solution.py:417
  14.2 5.0 %collective-permute-start.5 = (bf16[256,256]{1,0:T(8,128)(2,1)S(1)}, bf16[256,256]{1,0:T(8,128)(2,1)S(1)}, u32[]{:S(2)}, u32[]{:S(2)}) collective-permute-start(bf16[256,256]{1,0:T(8,128)(2,1)S(1)} %collective-permute-done.4.refs_6_), channel_id=1, source_target_pairs={{0,4},{1,5},{2,6},{3,7},{4,0},{5,1},{6,2},{7,3},{8,12},{9,13},{10,... | collective-permute-start | bytes 393224 | tf_op jit(solution)/shard_map/ppermute | solution.py:410
  14.7 4.4 %collective-permute-start.7 = (bf16[256,256]{1,0:T(8,128)(2,1)S(1)}, bf16[256,256]{1,0:T(8,128)(2,1)S(1)}, u32[]{:S(2)}, u32[]{:S(2)}) collective-permute-start(bf16[256,256]{1,0:T(8,128)(2,1)S(1)} %collective-permute-done.3.refs_5_), channel_id=1, source_target_pairs={{0,16},{16,0},{1,17},{17,1},{2,18},{18,2},{3,19},{19,3},{4,20},{20... | collective-permute-start | bytes 393224 | tf_op jit(solution)/shard_map/ppermute | solution.py:413
  16.3 8.7 %collective-permute-start.6 = (bf16[272,256]{1,0:T(8,128)(2,1)S(1)}, bf16[272,256]{1,0:T(8,128)(2,1)S(1)}, u32[]{:S(2)}, u32[]{:S(2)}) collective-permute-start(bf16[272,256]{1,0:T(8,128)(2,1)S(1)} %get-tuple-element.41.refs_4_), channel_id=1, source_target_pairs={{0,16},{16,0},{1,17},{17,1},{2,18},{18,2},{3,19},{19,3},{4,20},{20... | collective-permute-start | bytes 417800 | tf_op jit(solution)/shard_map/ppermute | solution.py:413
  19.1 5.9 %collective-permute-start.9 = (bf16[256,256]{1,0:T(8,128)(2,1)S(1)}, bf16[256,256]{1,0:T(8,128)(2,1)S(1)}, u32[]{:S(2)}, u32[]{:S(2)}) collective-permute-start(bf16[256,256]{1,0:T(8,128)(2,1)S(1)} %collective-permute-done.5.refs_7_), channel_id=1, source_target_pairs={{0,16},{16,0},{1,17},{17,1},{2,18},{18,2},{3,19},{19,3},{4,20},{20... | collective-permute-start | bytes 393224 | tf_op jit(solution)/shard_map/ppermute | solution.py:413
  19.1 5.9 %collective-permute-start.8 = (bf16[256,256]{1,0:T(8,128)(2,1)S(1)}, bf16[256,256]{1,0:T(8,128)(2,1)S(1)}, u32[]{:S(2)}, u32[]{:S(2)}) collective-permute-start(bf16[256,256]{1,0:T(8,128)(2,1)S(1)} %collective-permute-done.4.refs_6_), channel_id=1, source_target_pairs={{0,16},{16,0},{1,17},{17,1},{2,18},{18,2},{3,19},{19,3},{4,20},{20... | collective-permute-start | bytes 393224 | tf_op jit(solution)/shard_map/ppermute | solution.py:413
  26.7 7.0 %collective-permute-start.10 = (bf16[64,896]{1,0:T(8,128)(2,1)S(1)}, bf16[64,896]{1,0:T(8,128)(2,1)S(1)}, u32[]{:S(2)}, u32[]{:S(2)}) collective-permute-start(bf16[64,896]{1,0:T(8,128)(2,1)S(1)} %get-tuple-element.43), channel_id=1, source_target_pairs={{0,3},{1,2},{2,1},{3,0},{4,7},{5,6},{6,5},{7,4},{8,11},{9,10},{10,... | collective-permute-start | bytes 344072 | tf_op jit(solution)/shard_map/ppermute | solution.py:417
  28.2 6.9 %collective-permute-start.11 = (bf16[64,896]{1,0:T(8,128)(2,1)S(1)}, bf16[64,896]{1,0:T(8,128)(2,1)S(1)}, u32[]{:S(2)}, u32[]{:S(2)}) collective-permute-start(bf16[64,896]{1,0:T(8,128)(2,1)S(1)} %get-tuple-element.44), channel_id=1, source_target_pairs={{0,2},{1,3},{2,0},{3,1},{4,6},{5,7},{6,4},{7,5},{8,10},{9,11},{10,... | collective-permute-start | bytes 344072 | tf_op jit(solution)/shard_map/ppermute | solution.py:417
  28.8 6.4 %copy-start = (s32[2,1,2]{2,1,0:T(1,128)S(1)}, s32[2,1,2]{2,1,0:T(1,128)}, u32[]{:S(2)}) copy-start(s32[2,1,2]{2,1,0:T(1,128)} %docs.1) | copy-start | bytes 52
  28.8 6.4 %collective-permute-start.12 = (bf16[64,896]{1,0:T(8,128)(2,1)S(1)}, bf16[64,896]{1,0:T(8,128)(2,1)S(1)}, u32[]{:S(2)}, u32[]{:S(2)}) collective-permute-start(bf16[64,896]{1,0:T(8,128)(2,1)S(1)} %get-tuple-element.45), channel_id=1, source_target_pairs={{0,1},{1,0},{2,3},{3,2},{4,5},{5,4},{6,7},{7,6},{8,9},{9,8},{10,11... | collective-permute-start | bytes 344072 | tf_op jit(solution)/shard_map/ppermute | solution.py:417
  38.0 5.6 %collective-permute-start.15 = (bf16[288,128]{1,0:T(8,128)(2,1)S(1)}, bf16[288,128]{1,0:T(8,128)(2,1)S(1)}, u32[]{:S(2)}, u32[]{:S(2)}) collective-permute-start(bf16[288,128]{1,0:T(8,128)(2,1)S(1)} %shard_map.81.refs_0_), channel_id=1, source_target_pairs={{0,3},{1,2},{2,1},{3,0},{4,7},{5,6},{6,5},{7,4},{8,11},{9,10},{10,... | collective-permute-start | bytes 221192 | tf_op jit(solution)/shard_map/ppermute | solution.py:417
  39.6 5.2 %collective-permute-start.14 = (bf16[288,128]{1,0:T(8,128)(2,1)S(1)}, bf16[288,128]{1,0:T(8,128)(2,1)S(1)}, u32[]{:S(2)}, u32[]{:S(2)}) collective-permute-start(bf16[288,128]{1,0:T(8,128)(2,1)S(1)} %shard_map.81.refs_0_), channel_id=1, source_target_pairs={{0,2},{1,3},{2,0},{3,1},{4,6},{5,7},{6,4},{7,5},{8,10},{9,11},{10,... | collective-permute-start | bytes 221192 | tf_op jit(solution)/shard_map/ppermute | solution.py:417
  40.1 4.6 %collective-permute-start.13 = (bf16[288,128]{1,0:T(8,128)(2,1)S(1)}, bf16[288,128]{1,0:T(8,128)(2,1)S(1)}, u32[]{:S(2)}, u32[]{:S(2)}) collective-permute-start(bf16[288,128]{1,0:T(8,128)(2,1)S(1)} %shard_map.81.refs_0_), channel_id=1, source_target_pairs={{0,1},{1,0},{2,3},{3,2},{4,5},{5,4},{6,7},{7,6},{8,9},{9,8},{10,11... | collective-permute-start | bytes 221192 | tf_op jit(solution)/shard_map/ppermute | solution.py:417
  46.1 1.7 %collective-permute-start.17 = (bf16[2,256,256]{2,1,0:T(8,128)(2,1)S(1)}, bf16[2,256,256]{2,1,0:T(8,128)(2,1)S(1)}, u32[]{:S(2)}, u32[]{:S(2)}) collective-permute-start(bf16[2,256,256]{2,1,0:T(8,128)(2,1)S(1)} %get-tuple-element.58), channel_id=1, source_target_pairs={{0,16},{16,0},{1,17},{17,1},{2,18},{18,2},{3,19},{19,3},{4,20},{20... | collective-permute-start | bytes 786440 | tf_op jit(solution)/shard_map/ppermute | solution.py:413
  47.2 2.7 %collective-permute-start.16 = (bf16[2,256,256]{2,1,0:T(8,128)(2,1)S(1)}, bf16[2,256,256]{2,1,0:T(8,128)(2,1)S(1)}, u32[]{:S(2)}, u32[]{:S(2)}) collective-permute-start(bf16[2,256,256]{2,1,0:T(8,128)(2,1)S(1)} %get-tuple-element.55), channel_id=1, source_target_pairs={{0,16},{16,0},{1,17},{17,1},{2,18},{18,2},{3,19},{19,3},{4,20},{20... | collective-permute-start | bytes 786440 | tf_op jit(solution)/shard_map/ppermute | solution.py:413
  47.8 5.0 %collective-permute-start.18 = (bf16[128,256]{1,0:T(8,128)(2,1)S(1)}, bf16[128,256]{1,0:T(8,128)(2,1)S(1)}, u32[]{:S(2)}, u32[]{:S(2)}) collective-permute-start(bf16[128,256]{1,0:T(8,128)(2,1)S(1)} %get-tuple-element.60), channel_id=1, source_target_pairs={{0,4},{1,5},{2,6},{3,7},{4,0},{5,1},{6,2},{7,3},{8,12},{9,13},{10,... | collective-permute-start | bytes 196616 | tf_op jit(solution)/shard_map/ppermute | solution.py:410
  48.5 5.8 %collective-permute-start.20 = (bf16[128,256]{1,0:T(8,128)(2,1)S(1)}, bf16[128,256]{1,0:T(8,128)(2,1)S(1)}, u32[]{:S(2)}, u32[]{:S(2)}) collective-permute-start(bf16[128,256]{1,0:T(8,128)(2,1)S(1)} %get-tuple-element.62), channel_id=1, source_target_pairs={{0,4},{1,5},{2,6},{3,7},{4,0},{5,1},{6,2},{7,3},{8,12},{9,13},{10,... | collective-permute-start | bytes 196616 | tf_op jit(solution)/shard_map/ppermute | solution.py:410
  50.0 10.4 %collective-permute-start.22 = (bf16[256,256]{1,0:T(8,128)(2,1)S(1)}, bf16[256,256]{1,0:T(8,128)(2,1)S(1)}, u32[]{:S(2)}, u32[]{:S(2)}) collective-permute-start(bf16[256,256]{1,0:T(8,128)(2,1)S(1)} %get-tuple-element.63), channel_id=1, source_target_pairs={{0,4},{1,5},{2,6},{3,7},{4,0},{5,1},{6,2},{7,3},{8,12},{9,13},{10,... | collective-permute-start | bytes 393224 | tf_op jit(solution)/shard_map/ppermute | solution.py:410
  52.9 6.1 %collective-permute-start.19 = (bf16[128,256]{1,0:T(8,128)(2,1)S(1)}, bf16[128,256]{1,0:T(8,128)(2,1)S(1)}, u32[]{:S(2)}, u32[]{:S(2)}) collective-permute-start(bf16[128,256]{1,0:T(8,128)(2,1)S(1)} %shard_map.86), channel_id=1, source_target_pairs={{0,8},{1,9},{2,10},{3,11},{4,12},{5,13},{6,14},{7,15},{8,0},{9,1},... | collective-permute-start | bytes 196616 | tf_op jit(solution)/shard_map/ppermute | solution.py:410
  54.3 6.1 %collective-permute-start.21 = (bf16[128,256]{1,0:T(8,128)(2,1)S(1)}, bf16[128,256]{1,0:T(8,128)(2,1)S(1)}, u32[]{:S(2)}, u32[]{:S(2)}) collective-permute-start(bf16[128,256]{1,0:T(8,128)(2,1)S(1)} %shard_map.88), channel_id=1, source_target_pairs={{0,8},{1,9},{2,10},{3,11},{4,12},{5,13},{6,14},{7,15},{8,0},{9,1},... | collective-permute-start | bytes 196616 | tf_op jit(solution)/shard_map/ppermute | solution.py:410

commit v21 on v19

--- a/solution.py
+++ b/solution.py
@@ -509,7 +509,7 @@
         for k, come in got.items():
             pieces[k] = [call(add_kernel, [(a.shape, BF16)], a, b)[0] for a, b in zip(pieces[k], come)]
             held = [
-                (parts, at) for parts, at in held
+                ([lax.optimization_barrier((part, pieces[k][0]))[0] for part in parts], at) for parts, at in held
             ]
     parts = [[along_z(part, at) for part in value] for value, at in reversed(held)]
     for come in parts[:-1]:

time: 58.9 us -> 60.3 us (1.024)
  waiting for transfers between devices: 18.9 us -> 21.3 us
  starting transfers between devices: 26.2 us -> 25.2 us
    ppermute x8, waiting for transfers between devices: 9.8 us -> 12.2 us  [along_z(): return lax.ppermute(value, 'dp', route)]
    ppermute x8, starting transfers between devices: 12.4 us -> 11.3 us  [along_z(): return lax.ppermute(value, 'dp', route)]
where the time goes in v21:
time: 60.3 us; the launch traced here: 60 us
  starting transfers between devices  25.2 us (42%)
  waiting for transfers between devices  21.3 us (35%)
  Pallas kernels  12.5 us (21%)
  between operations  0.78 us (1%)
    ppermute x8, waiting for transfers between devices, along_z(): return lax.ppermute(value, 'dp', route)  12.2 us
    ppermute x9, starting transfers between devices, along_plane(): return lax.ppermute(value, 'dp', route)  12.2 us
    ppermute x8, starting transfers between devices, along_z(): return lax.ppermute(value, 'dp', route)  11.3 us
    ppermute x9, waiting for transfers between devices, along_plane(): return lax.ppermute(value, 'dp', route)  8.11 us
    pallas_call x11, Pallas kernels, call(): pl.pallas_call(kernel, out_shape=[jax.ShapeDtypeStruct(shape, dtype) for...  7.69 us
    ppermute x6, starting transfers between devices, to_sibling(): return lax.ppermute(value, 'section', [(0, 1), (1, 0)])  1.71 us
    pallas_call x1, Pallas kernels, planar(): pl.pallas_call(functools.partial(blocks_kernel, planes), out_shape=[one_b...  1.69 us
    pallas_call x1, Pallas kernels, planar(): pl.pallas_call(functools.partial(first_kernel, planes), out_shape=[jax.Sh...  1.66 us
  transfers between devices with their start and end apart: 23, of which 12 were waited for; matrix products, arithmetic and copies ran while one was open for 0% of the time, Pallas kernels for 7%

profile of v21, /device:TPU:0, one launch (start us, length us, event | category | flops | bytes accessed | tf_op | source)
XLA Modules:
  0.0 60.0 jit_solution(11377768538967776521)
XLA Ops:
  0.6 0.1 pad_add_fusion.index
  0.7 1.7 %shard_map.77 = (bf16[256,256]{1,0:T(8,128)(2,1)S(1)}, bf16[2,64,1024]{2,1,0:T(8,128)(2,1)S(1)}) custom-call(s32[3]{0:T(128)S(1)} %pad_add_fusion.index, bf16[192,256]{1,0:T(8,128)(2,1)} %bitcast.11, bf16[64,256]{1,0:T(8,128)(2,1)} %bitcast.12, bf16[2,64,4096]{2,1,0:T(8,128)(2,1)} %x_ref.5, bf16[2,64,4096]{2,1,0:T(8,128)(2,1)} %c_ref.5), custom_call_target="tpu_custom_call" | custom-call | tf_op jit(solution)/shard_map/pallas_call | solution.py:430
  2.4 4.0 %collective-permute-start = (bf16[2,64,1024]{2,1,0:T(8,128)(2,1)S(1)}, bf16[2,64,1024]{2,1,0:T(8,128)(2,1)S(1)}, u32[]{:S(2)}, u32[]{:S(2)}) collective-permute-start(bf16[2,64,1024]{2,1,0:T(8,128)(2,1)S(1)} %get-tuple-element.36), channel_id=1, source_target_pairs={{0,3},{1,2},{2,1},{3,0},{4,7},{5,6},{6,5},{7,4},{8,11},{9,10},{10,... | collective-permute-start | bytes 786440 | tf_op jit(solution)/shard_map/ppermute | solution.py:417
  6.4 0.0 copy-start.1
  6.4 2.6 %collective-permute-start.4 = (bf16[256,256]{1,0:T(8,128)(2,1)S(1)}, bf16[256,256]{1,0:T(8,128)(2,1)S(1)}, u32[]{:S(2)}, u32[]{:S(2)}) collective-permute-start(bf16[256,256]{1,0:T(8,128)(2,1)S(1)} %get-tuple-element.37.pack_ref), channel_id=1, source_target_pairs={{0,8},{1,9},{2,10},{3,11},{4,12},{5,13},{6,14},{7,15},{8,0},{9,1},... | collective-permute-start | bytes 393224 | tf_op jit(solution)/shard_map/ppermute | solution.py:410
  8.9 1.6 %collective-permute-start.3 = (bf16[256,256]{1,0:T(8,128)(2,1)S(1)}, bf16[256,256]{1,0:T(8,128)(2,1)S(1)}, u32[]{:S(2)}, u32[]{:S(2)}) collective-permute-start(bf16[256,256]{1,0:T(8,128)(2,1)S(1)} %get-tuple-element.37.pack_ref), channel_id=1, source_target_pairs={{0,4},{1,5},{2,6},{3,7},{4,0},{5,1},{6,2},{7,3},{8,12},{9,13},{10,... | collective-permute-start | bytes 393224 | tf_op jit(solution)/shard_map/ppermute | solution.py:410
  10.5 1.7 %shard_map.79 = (bf16[2,64,1024]{2,1,0:T(8,128)(2,1)S(1)}, bf16[2,64,1024]{2,1,0:T(8,128)(2,1)S(1)}) custom-call(s32[3]{0:T(128)S(1)} %pad_add_fusion.index, bf16[2,64,4096]{2,1,0:T(8,128)(2,1)} %x_ref.5, bf16[2,64,4096]{2,1,0:T(8,128)(2,1)} %c_ref.5), custom_call_target="tpu_custom_call" | custom-call | tf_op jit(solution)/shard_map/pallas_call | solution.py:438
  12.2 0.6 collective-permute-start.1
  12.8 0.5 collective-permute-start.2
  13.3 1.8 %collective-permute-done.4.refs_6_ = bf16[256,256]{1,0:T(8,128)(2,1)S(1)} collective-permute-done((bf16[256,256]{1,0:T(8,128)(2,1)S(1)}, bf16[256,256]{1,0:T(8,128)(2,1)S(1)}, u32[]{:S(2)}, u32[]{:S(2)}) %collective-permute-start.4) | collective-permute-done | bytes 131104 | tf_op jit(solution)/shard_map/ppermute | solution.py:410
  15.1 0.6 collective-permute-start.5
  15.7 0.0 collective-permute-done.3.refs_5_
  15.7 0.0 collective-permute-start.7
  15.7 0.0 copy-done.1
  15.7 0.1 reduce
  15.8 0.0 collective-permute-done.refs_1_
  15.8 1.5 %shard_map.78 = (bf16[272,256]{1,0:T(8,128)(2,1)S(1)}, bf16[2,64,1024]{2,1,0:T(8,128)(2,1)S(1)}) custom-call(s32[3]{0:T(128)S(1)} %pad_add_fusion.index, bf16[256,256]{1,0:T(8,128)(2,1)S(1)} %get-tuple-element.37.pack_ref, bf16[16,256]{1,0:T(8,128)(2,1)S(1)} %reshape_squeeze.3.gain_ref, bf16[2,64,4096]{2,1,0:T(8,128)(2,1)} %x_ref.5, bf16[2,64,4096]{2,1,0:T(8,128)(2,1)} %c_ref.5), custom_call_target="tpu_custom_call" | custom-call | tf_op jit(solution)/shard_map/pallas_call | solution.py:454
  17.3 0.6 collective-permute-start.6
  17.8 2.2 %collective-permute-done.5.refs_7_ = bf16[256,256]{1,0:T(8,128)(2,1)S(1)} collective-permute-done((bf16[256,256]{1,0:T(8,128)(2,1)S(1)}, bf16[256,256]{1,0:T(8,128)(2,1)S(1)}, u32[]{:S(2)}, u32[]{:S(2)}) %collective-permute-start.5) | collective-permute-done | bytes 131104 | tf_op jit(solution)/shard_map/ppermute | solution.py:410
  20.1 0.0 collective-permute-start.9
  20.1 0.0 collective-permute-done.7.refs_9_
  20.1 0.5 collective-permute-start.8
  20.6 0.0 collective-permute-done.1.refs_2_
  20.6 0.0 collective-permute-done.2.refs_3_
  20.6 0.8 %collective-permute-done.9.refs_11_ = bf16[256,256]{1,0:T(8,128)(2,1)S(1)} collective-permute-done((bf16[256,256]{1,0:T(8,128)(2,1)S(1)}, bf16[256,256]{1,0:T(8,128)(2,1)S(1)}, u32[]{:S(2)}, u32[]{:S(2)}) %collective-permute-start.9) | collective-permute-done | bytes 131104 | tf_op jit(solution)/shard_map/ppermute | solution.py:413
  21.4 0.2 collective-permute-done.8.refs_10_
  21.6 0.0 collective-permute-done.6.refs_8_
  21.6 1.6 %shard_map.80 = (bf16[4,64,1024]{2,1,0:T(8,128)(2,1)S(1)}, bf16[4,64,1024]{2,1,0:T(8,128)(2,1)S(1)}, bf16[4,512,256]{2,1,0:T(8,128)(2,1)S(1)}, f32[4,8,256]{2,1,...) custom-call(s32[3]{0:T(128)S(1)} %pad_add_fusion.index, ...), custom_call_target="tpu_custom_call" | custom-call | tf_op jit(solution)/shard_map/pallas_call | solution.py:387
  23.2 0.7 %collective-permute-start.10 = (bf16[64,896]{1,0:T(8,128)(2,1)S(1)}, bf16[64,896]{1,0:T(8,128)(2,1)S(1)}, u32[]{:S(2)}, u32[]{:S(2)}) collective-permute-start(bf16[64,896]{1,0:T(8,128)(2,1)S(1)} %get-tuple-element.44), channel_id=1, source_target_pairs={{0,3},{1,2},{2,1},{3,0},{4,7},{5,6},{6,5},{7,4},{8,11},{9,10},{10,... | collective-permute-start | bytes 344072 | tf_op jit(solution)/shard_map/ppermute | solution.py:417
  23.9 1.3 %collective-permute-start.11 = (bf16[64,896]{1,0:T(8,128)(2,1)S(1)}, bf16[64,896]{1,0:T(8,128)(2,1)S(1)}, u32[]{:S(2)}, u32[]{:S(2)}) collective-permute-start(bf16[64,896]{1,0:T(8,128)(2,1)S(1)} %get-tuple-element.45), channel_id=1, source_target_pairs={{0,2},{1,3},{2,0},{3,1},{4,6},{5,7},{6,4},{7,5},{8,10},{9,11},{10,... | collective-permute-start | bytes 344072 | tf_op jit(solution)/shard_map/ppermute | solution.py:417
  25.3 0.0 copy-start
  25.3 1.5 %collective-permute-start.12 = (bf16[64,896]{1,0:T(8,128)(2,1)S(1)}, bf16[64,896]{1,0:T(8,128)(2,1)S(1)}, u32[]{:S(2)}, u32[]{:S(2)}) collective-permute-start(bf16[64,896]{1,0:T(8,128)(2,1)S(1)} %get-tuple-element.46), channel_id=1, source_target_pairs={{0,1},{1,0},{2,3},{3,2},{4,5},{5,4},{6,7},{7,6},{8,9},{9,8},{10,11... | collective-permute-start | bytes 344072 | tf_op jit(solution)/shard_map/ppermute | solution.py:417
  26.8 3.4 %collective-permute-done.10.refs_0_ = bf16[64,896]{1,0:T(8,128)(2,1)S(1)} collective-permute-done((bf16[64,896]{1,0:T(8,128)(2,1)S(1)}, bf16[64,896]{1,0:T(8,128)(2,1)S(1)}, u32[]{:S(2)}, u32[]{:S(2)}) %collective-permute-start.10) | collective-permute-done | bytes 114720 | tf_op jit(solution)/shard_map/ppermute | solution.py:417
  30.2 1.3 %collective-permute-done.11.refs_1_ = bf16[64,896]{1,0:T(8,128)(2,1)S(1)} collective-permute-done((bf16[64,896]{1,0:T(8,128)(2,1)S(1)}, bf16[64,896]{1,0:T(8,128)(2,1)S(1)}, u32[]{:S(2)}, u32[]{:S(2)}) %collective-permute-start.11) | collective-permute-done | bytes 114720 | tf_op jit(solution)/shard_map/ppermute | solution.py:417
  31.5 0.0 collective-permute-done.12.refs_2_
  31.5 0.0 copy-done
  31.5 2.8 %shard_map.81.refs_0_ = bf16[288,128]{1,0:T(8,128)(2,1)S(1)} custom-call(s32[3]{0:T(128)S(1)} %pad_add_fusion.index, s32[2,1,2]{2,1,0:T(1,128)S(1)} %copy-done, bf16[64,896]{1,0:T(8,128)(2,1)S(1)} %collective-permute-done.10.refs_0_, bf16[64,896]{1,0:T(8,128)(2,1)S(1)} %collective-permute-done.11.refs_1_, ...), custom_call_target="tpu_custom_call" | custom-call | tf_op jit(solution)/shard_map/pallas_call | solution.py:387
  34.3 1.2 %collective-permute-start.15 = (bf16[288,128]{1,0:T(8,128)(2,1)S(1)}, bf16[288,128]{1,0:T(8,128)(2,1)S(1)}, u32[]{:S(2)}, u32[]{:S(2)}) collective-permute-start(bf16[288,128]{1,0:T(8,128)(2,1)S(1)} %shard_map.81.refs_0_), channel_id=1, source_target_pairs={{0,3},{1,2},{2,1},{3,0},{4,7},{5,6},{6,5},{7,4},{8,11},{9,10},{10,... | collective-permute-start | bytes 221192 | tf_op jit(solution)/shard_map/ppermute | solution.py:417
  35.6 1.4 %collective-permute-start.14 = (bf16[288,128]{1,0:T(8,128)(2,1)S(1)}, bf16[288,128]{1,0:T(8,128)(2,1)S(1)}, u32[]{:S(2)}, u32[]{:S(2)}) collective-permute-start(bf16[288,128]{1,0:T(8,128)(2,1)S(1)} %shard_map.81.refs_0_), channel_id=1, source_target_pairs={{0,2},{1,3},{2,0},{3,1},{4,6},{5,7},{6,4},{7,5},{8,10},{9,11},{10,... | collective-permute-start | bytes 221192 | tf_op jit(solution)/shard_map/ppermute | solution.py:417
  36.9 1.0 %collective-permute-start.13 = (bf16[288,128]{1,0:T(8,128)(2,1)S(1)}, bf16[288,128]{1,0:T(8,128)(2,1)S(1)}, u32[]{:S(2)}, u32[]{:S(2)}) collective-permute-start(bf16[288,128]{1,0:T(8,128)(2,1)S(1)} %shard_map.81.refs_0_), channel_id=1, source_target_pairs={{0,1},{1,0},{2,3},{3,2},{4,5},{5,4},{6,7},{7,6},{8,9},{9,8},{10,11... | collective-permute-start | bytes 221192 | tf_op jit(solution)/shard_map/ppermute | solution.py:417
  37.9 2.3 %collective-permute-done.15.refs_3_ = bf16[288,128]{1,0:T(8,128)(2,1)S(1)} collective-permute-done((bf16[288,128]{1,0:T(8,128)(2,1)S(1)}, bf16[288,128]{1,0:T(8,128)(2,1)S(1)}, u32[]{:S(2)}, u32[]{:S(2)}) %collective-permute-start.15) | collective-permute-done | bytes 73760 | tf_op jit(solution)/shard_map/ppermute | solution.py:417
  40.2 0.3 collective-permute-done.14.refs_2_
  40.5 0.7 %collective-permute-done.13.refs_1_ = bf16[288,128]{1,0:T(8,128)(2,1)S(1)} collective-permute-done((bf16[288,128]{1,0:T(8,128)(2,1)S(1)}, bf16[288,128]{1,0:T(8,128)(2,1)S(1)}, u32[]{:S(2)}, u32[]{:S(2)}) %collective-permute-start.13) | collective-permute-done | bytes 73760 | tf_op jit(solution)/shard_map/ppermute | solution.py:417
  41.3 1.3 %shard_map.82 = (f32[2,256,256]{2,1,0:T(8,128)S(1)}, bf16[2,256,256]{2,1,0:T(8,128)(2,1)S(1)}, bf16[640,256]{1,0:T(8,128)(2,1)S(1)}, bf16[256,64]{1,0:T(8,128)(2,1)S(1)}, bf16[64,192]{1,0:T(8,128)(2,1)S(1)}) custom-call(s32[3]{0:T(128)S(1)} %pad_add_fusion.index, bf16[288,128]{1,0:T(8,128)(2,1)S(1)} %shard_map.81.refs_0_, ...), custom_call_target="tpu_custom_call" | custom-call | tf_op jit(solution)/shard_map/pallas_call | solution.py:387
  42.6 0.1 collective-permute-start.17
  42.7 1.0 %shard_map.83 = (f32[2,256,256]{2,1,0:T(8,128)S(1)}, bf16[2,256,256]{2,1,0:T(8,128)(2,1)S(1)}) custom-call(s32[3]{0:T(128)S(1)} %pad_add_fusion.index, bf16[640,256]{1,0:T(8,128)(2,1)S(1)} %get-tuple-element.52.turned_ref, bf16[256,64]{1,0:T(8,128)(2,1)S(1)} %get-tuple-element.53.small_ref, bf16[64,192]{1,0:T(8,128)(2,1)S(1)} %get-tuple-element.54.small_t_ref, ...), custom_call_target="tpu_custom_call" | custom-call | tf_op jit(solution)/shard_map/pallas_call | solution.py:387
  43.7 0.6 collective-permute-start.16
  44.3 0.0 collective-permute-done.17.come_ref
  44.4 1.1 %collective-permute-start.18 = (bf16[128,256]{1,0:T(8,128)(2,1)S(1)}, bf16[128,256]{1,0:T(8,128)(2,1)S(1)}, u32[]{:S(2)}, u32[]{:S(2)}) collective-permute-start(bf16[128,256]{1,0:T(8,128)(2,1)S(1)} %get-tuple-element.61), channel_id=1, source_target_pairs={{0,4},{1,5},{2,6},{3,7},{4,0},{5,1},{6,2},{7,3},{8,12},{9,13},{10,... | collective-permute-start | bytes 196616 | tf_op jit(solution)/shard_map/ppermute | solution.py:410
  45.4 1.0 %collective-permute-start.20 = (bf16[128,256]{1,0:T(8,128)(2,1)S(1)}, bf16[128,256]{1,0:T(8,128)(2,1)S(1)}, u32[]{:S(2)}, u32[]{:S(2)}) collective-permute-start(bf16[128,256]{1,0:T(8,128)(2,1)S(1)} %get-tuple-element.63), channel_id=1, source_target_pairs={{0,4},{1,5},{2,6},{3,7},{4,0},{5,1},{6,2},{7,3},{8,12},{9,13},{10,... | collective-permute-start | bytes 196616 | tf_op jit(solution)/shard_map/ppermute | solution.py:410
  46.4 0.0 collective-permute-done.16.come_ref
  46.5 0.1 shard_map.84
  46.5 2.7 %collective-permute-done.18.b_ref = bf16[128,256]{1,0:T(8,128)(2,1)S(1)} collective-permute-done((bf16[128,256]{1,0:T(8,128)(2,1)S(1)}, bf16[128,256]{1,0:T(8,128)(2,1)S(1)}, u32[]{:S(2)}, u32[]{:S(2)}) %collective-permute-start.18) | collective-permute-done | bytes 65568 | tf_op jit(solution)/shard_map/ppermute | solution.py:410
  49.2 1.1 %collective-permute-start.22 = (bf16[256,256]{1,0:T(8,128)(2,1)S(1)}, bf16[256,256]{1,0:T(8,128)(2,1)S(1)}, u32[]{:S(2)}, u32[]{:S(2)}) collective-permute-start(bf16[256,256]{1,0:T(8,128)(2,1)S(1)} %get-tuple-element.65), channel_id=1, source_target_pairs={{0,4},{1,5},{2,6},{3,7},{4,0},{5,1},{6,2},{7,3},{8,12},{9,13},{10,... | collective-permute-start | bytes 393224 | tf_op jit(solution)/shard_map/ppermute | solution.py:410
  50.3 3.4 %collective-permute-start.19 = (bf16[128,256]{1,0:T(8,128)(2,1)S(1)}, bf16[128,256]{1,0:T(8,128)(2,1)S(1)}, u32[]{:S(2)}, u32[]{:S(2)}) collective-permute-start(bf16[128,256]{1,0:T(8,128)(2,1)S(1)} %shard_map.86), channel_id=1, source_target_pairs={{0,8},{1,9},{2,10},{3,11},{4,12},{5,13},{6,14},{7,15},{8,0},{9,1},... | collective-permute-start | bytes 196616 | tf_op jit(solution)/shard_map/ppermute | solution.py:410
  53.7 0.0 collective-permute-done.20.b_ref
  53.7 0.1 collective-permute-start.21
  53.8 4.7 %collective-permute-done.19.part_ref = bf16[128,256]{1,0:T(8,128)(2,1)S(1)} collective-permute-done((bf16[128,256]{1,0:T(8,128)(2,1)S(1)}, bf16[128,256]{1,0:T(8,128)(2,1)S(1)}, u32[]{:S(2)}, u32[]{:S(2)}) %collective-permute-start.19) | collective-permute-done | bytes 65568 | tf_op jit(solution)/shard_map/ppermute | solution.py:410
  58.5 0.7 %collective-permute-done.21.part_ref = bf16[128,256]{1,0:T(8,128)(2,1)S(1)} collective-permute-done((bf16[128,256]{1,0:T(8,128)(2,1)S(1)}, bf16[128,256]{1,0:T(8,128)(2,1)S(1)}, u32[]{:S(2)}, u32[]{:S(2)}) %collective-permute-start.21) | collective-permute-done | bytes 65568 | tf_op jit(solution)/shard_map/ppermute | solution.py:410
  59.2 0.0 collective-permute-done.22.refs_0_
  59.3 0.7 %shard_map.90 = (f32[192,256]{1,0:T(8,128)}, f32[64,256]{1,0:T(8,128)}) custom-call(f32[256,256]{1,0:T(8,128)S(1)} %shard_map.89.keep_ref, bf16[256,256]{1,0:T(8,128)(2,1)S(1)} %collective-permute-done.22.refs_0_), custom_call_target="tpu_custom_call" | custom-call | tf_op jit(solution)/shard_map/pallas_call | solution.py:387
  (6 shorter events, 0.1 us)
Async XLA Ops:
  2.4 13.4 %collective-permute-start = (bf16[2,64,1024]{2,1,0:T(8,128)(2,1)S(1)}, bf16[2,64,1024]{2,1,0:T(8,128)(2,1)S(1)}, u32[]{:S(2)}, u32[]{:S(2)}) collective-permute-start(bf16[2,64,1024]{2,1,0:T(8,128)(2,1)S(1)} %get-tuple-element.36), channel_id=1, source_target_pairs={{0,3},{1,2},{2,1},{3,0},{4,7},{5,6},{6,5},{7,4},{8,11},{9,10},{10,... | collective-permute-start | bytes 786440 | tf_op jit(solution)/shard_map/ppermute | solution.py:417
  6.4 9.3 %copy-start.1 = (bf16[1,4096]{1,0:T(2,128)(2,1)S(1)}, bf16[1,4096]{1,0:T(2,128)(2,1)}, u32[]{:S(2)}) copy-start(bf16[1,4096]{1,0:T(2,128)(2,1)} %param.9) | copy-start | bytes 24580
  6.4 8.8 %collective-permute-start.4 = (bf16[256,256]{1,0:T(8,128)(2,1)S(1)}, bf16[256,256]{1,0:T(8,128)(2,1)S(1)}, u32[]{:S(2)}, u32[]{:S(2)}) collective-permute-start(bf16[256,256]{1,0:T(8,128)(2,1)S(1)} %get-tuple-element.37.pack_ref), channel_id=1, source_target_pairs={{0,8},{1,9},{2,10},{3,11},{4,12},{5,13},{6,14},{7,15},{8,0},{9,1},... | collective-permute-start | bytes 393224 | tf_op jit(solution)/shard_map/ppermute | solution.py:410
  8.9 6.8 %collective-permute-start.3 = (bf16[256,256]{1,0:T(8,128)(2,1)S(1)}, bf16[256,256]{1,0:T(8,128)(2,1)S(1)}, u32[]{:S(2)}, u32[]{:S(2)}) collective-permute-start(bf16[256,256]{1,0:T(8,128)(2,1)S(1)} %get-tuple-element.37.pack_ref), channel_id=1, source_target_pairs={{0,4},{1,5},{2,6},{3,7},{4,0},{5,1},{6,2},{7,3},{8,12},{9,13},{10,... | collective-permute-start | bytes 393224 | tf_op jit(solution)/shard_map/ppermute | solution.py:410
  12.2 8.4 %collective-permute-start.1 = (bf16[2,64,1024]{2,1,0:T(8,128)(2,1)S(1)}, bf16[2,64,1024]{2,1,0:T(8,128)(2,1)S(1)}, u32[]{:S(2)}, u32[]{:S(2)}) collective-permute-start(bf16[2,64,1024]{2,1,0:T(8,128)(2,1)S(1)} %get-tuple-element.40), channel_id=1, source_target_pairs={{0,2},{1,3},{2,0},{3,1},{4,6},{5,7},{6,4},{7,5},{8,10},{9,11},{10,... | collective-permute-start | bytes 786440 | tf_op jit(solution)/shard_map/ppermute | solution.py:417
  12.8 7.8 %collective-permute-start.2 = (bf16[2,64,1024]{2,1,0:T(8,128)(2,1)S(1)}, bf16[2,64,1024]{2,1,0:T(8,128)(2,1)S(1)}, u32[]{:S(2)}, u32[]{:S(2)}) collective-permute-start(bf16[2,64,1024]{2,1,0:T(8,128)(2,1)S(1)} %get-tuple-element.41), channel_id=1, source_target_pairs={{0,1},{1,0},{2,3},{3,2},{4,5},{5,4},{6,7},{7,6},{8,9},{9,8},{10,11... | collective-permute-start | bytes 786440 | tf_op jit(solution)/shard_map/ppermute | solution.py:417
  15.1 5.0 %collective-permute-start.5 = (bf16[256,256]{1,0:T(8,128)(2,1)S(1)}, bf16[256,256]{1,0:T(8,128)(2,1)S(1)}, u32[]{:S(2)}, u32[]{:S(2)}) collective-permute-start(bf16[256,256]{1,0:T(8,128)(2,1)S(1)} %collective-permute-done.4.refs_6_), channel_id=1, source_target_pairs={{0,4},{1,5},{2,6},{3,7},{4,0},{5,1},{6,2},{7,3},{8,12},{9,13},{10,... | collective-permute-start | bytes 393224 | tf_op jit(solution)/shard_map/ppermute | solution.py:410
  15.7 4.4 %collective-permute-start.7 = (bf16[256,256]{1,0:T(8,128)(2,1)S(1)}, bf16[256,256]{1,0:T(8,128)(2,1)S(1)}, u32[]{:S(2)}, u32[]{:S(2)}) collective-permute-start(bf16[256,256]{1,0:T(8,128)(2,1)S(1)} %collective-permute-done.3.refs_5_), channel_id=1, source_target_pairs={{0,16},{16,0},{1,17},{17,1},{2,18},{18,2},{3,19},{19,3},{4,20},{20... | collective-permute-start | bytes 393224 | tf_op jit(solution)/shard_map/ppermute | solution.py:413
  17.3 4.3 %collective-permute-start.6 = (bf16[272,256]{1,0:T(8,128)(2,1)S(1)}, bf16[272,256]{1,0:T(8,128)(2,1)S(1)}, u32[]{:S(2)}, u32[]{:S(2)}) collective-permute-start(bf16[272,256]{1,0:T(8,128)(2,1)S(1)} %get-tuple-element.42.refs_4_), channel_id=1, source_target_pairs={{0,16},{16,0},{1,17},{17,1},{2,18},{18,2},{3,19},{19,3},{4,20},{20... | collective-permute-start | bytes 417800 | tf_op jit(solution)/shard_map/ppermute | solution.py:413
  20.1 1.3 %collective-permute-start.9 = (bf16[256,256]{1,0:T(8,128)(2,1)S(1)}, bf16[256,256]{1,0:T(8,128)(2,1)S(1)}, u32[]{:S(2)}, u32[]{:S(2)}) collective-permute-start(bf16[256,256]{1,0:T(8,128)(2,1)S(1)} %collective-permute-done.5.refs_7_), channel_id=1, source_target_pairs={{0,16},{16,0},{1,17},{17,1},{2,18},{18,2},{3,19},{19,3},{4,20},{20... | collective-permute-start | bytes 393224 | tf_op jit(solution)/shard_map/ppermute | solution.py:413
  20.1 1.5 %collective-permute-start.8 = (bf16[256,256]{1,0:T(8,128)(2,1)S(1)}, bf16[256,256]{1,0:T(8,128)(2,1)S(1)}, u32[]{:S(2)}, u32[]{:S(2)}) collective-permute-start(bf16[256,256]{1,0:T(8,128)(2,1)S(1)} %collective-permute-done.4.refs_6_), channel_id=1, source_target_pairs={{0,16},{16,0},{1,17},{17,1},{2,18},{18,2},{3,19},{19,3},{4,20},{20... | collective-permute-start | bytes 393224 | tf_op jit(solution)/shard_map/ppermute | solution.py:413
  23.2 7.0 %collective-permute-start.10 = (bf16[64,896]{1,0:T(8,128)(2,1)S(1)}, bf16[64,896]{1,0:T(8,128)(2,1)S(1)}, u32[]{:S(2)}, u32[]{:S(2)}) collective-permute-start(bf16[64,896]{1,0:T(8,128)(2,1)S(1)} %get-tuple-element.44), channel_id=1, source_target_pairs={{0,3},{1,2},{2,1},{3,0},{4,7},{5,6},{6,5},{7,4},{8,11},{9,10},{10,... | collective-permute-start | bytes 344072 | tf_op jit(solution)/shard_map/ppermute | solution.py:417
  23.9 7.6 %collective-permute-start.11 = (bf16[64,896]{1,0:T(8,128)(2,1)S(1)}, bf16[64,896]{1,0:T(8,128)(2,1)S(1)}, u32[]{:S(2)}, u32[]{:S(2)}) collective-permute-start(bf16[64,896]{1,0:T(8,128)(2,1)S(1)} %get-tuple-element.45), channel_id=1, source_target_pairs={{0,2},{1,3},{2,0},{3,1},{4,6},{5,7},{6,4},{7,5},{8,10},{9,11},{10,... | collective-permute-start | bytes 344072 | tf_op jit(solution)/shard_map/ppermute | solution.py:417
  25.3 6.2 %copy-start = (s32[2,1,2]{2,1,0:T(1,128)S(1)}, s32[2,1,2]{2,1,0:T(1,128)}, u32[]{:S(2)}) copy-start(s32[2,1,2]{2,1,0:T(1,128)} %docs.1) | copy-start | bytes 52
  25.3 6.2 %collective-permute-start.12 = (bf16[64,896]{1,0:T(8,128)(2,1)S(1)}, bf16[64,896]{1,0:T(8,128)(2,1)S(1)}, u32[]{:S(2)}, u32[]{:S(2)}) collective-permute-start(bf16[64,896]{1,0:T(8,128)(2,1)S(1)} %get-tuple-element.46), channel_id=1, source_target_pairs={{0,1},{1,0},{2,3},{3,2},{4,5},{5,4},{6,7},{7,6},{8,9},{9,8},{10,11... | collective-permute-start | bytes 344072 | tf_op jit(solution)/shard_map/ppermute | solution.py:417
  34.3 5.9 %collective-permute-start.15 = (bf16[288,128]{1,0:T(8,128)(2,1)S(1)}, bf16[288,128]{1,0:T(8,128)(2,1)S(1)}, u32[]{:S(2)}, u32[]{:S(2)}) collective-permute-start(bf16[288,128]{1,0:T(8,128)(2,1)S(1)} %shard_map.81.refs_0_), channel_id=1, source_target_pairs={{0,3},{1,2},{2,1},{3,0},{4,7},{5,6},{6,5},{7,4},{8,11},{9,10},{10,... | collective-permute-start | bytes 221192 | tf_op jit(solution)/shard_map/ppermute | solution.py:417
  35.6 5.0 %collective-permute-start.14 = (bf16[288,128]{1,0:T(8,128)(2,1)S(1)}, bf16[288,128]{1,0:T(8,128)(2,1)S(1)}, u32[]{:S(2)}, u32[]{:S(2)}) collective-permute-start(bf16[288,128]{1,0:T(8,128)(2,1)S(1)} %shard_map.81.refs_0_), channel_id=1, source_target_pairs={{0,2},{1,3},{2,0},{3,1},{4,6},{5,7},{6,4},{7,5},{8,10},{9,11},{10,... | collective-permute-start | bytes 221192 | tf_op jit(solution)/shard_map/ppermute | solution.py:417
  36.9 4.4 %collective-permute-start.13 = (bf16[288,128]{1,0:T(8,128)(2,1)S(1)}, bf16[288,128]{1,0:T(8,128)(2,1)S(1)}, u32[]{:S(2)}, u32[]{:S(2)}) collective-permute-start(bf16[288,128]{1,0:T(8,128)(2,1)S(1)} %shard_map.81.refs_0_), channel_id=1, source_target_pairs={{0,1},{1,0},{2,3},{3,2},{4,5},{5,4},{6,7},{7,6},{8,9},{9,8},{10,11... | collective-permute-start | bytes 221192 | tf_op jit(solution)/shard_map/ppermute | solution.py:417
  42.6 1.7 %collective-permute-start.17 = (bf16[2,256,256]{2,1,0:T(8,128)(2,1)S(1)}, bf16[2,256,256]{2,1,0:T(8,128)(2,1)S(1)}, u32[]{:S(2)}, u32[]{:S(2)}) collective-permute-start(bf16[2,256,256]{2,1,0:T(8,128)(2,1)S(1)} %get-tuple-element.59), channel_id=1, source_target_pairs={{0,16},{16,0},{1,17},{17,1},{2,18},{18,2},{3,19},{19,3},{4,20},{20... | collective-permute-start | bytes 786440 | tf_op jit(solution)/shard_map/ppermute | solution.py:413
  43.7 2.7 %collective-permute-start.16 = (bf16[2,256,256]{2,1,0:T(8,128)(2,1)S(1)}, bf16[2,256,256]{2,1,0:T(8,128)(2,1)S(1)}, u32[]{:S(2)}, u32[]{:S(2)}) collective-permute-start(bf16[2,256,256]{2,1,0:T(8,128)(2,1)S(1)} %get-tuple-element.56), channel_id=1, source_target_pairs={{0,16},{16,0},{1,17},{17,1},{2,18},{18,2},{3,19},{19,3},{4,20},{20... | collective-permute-start | bytes 786440 | tf_op jit(solution)/shard_map/ppermute | solution.py:413
  44.4 4.9 %collective-permute-start.18 = (bf16[128,256]{1,0:T(8,128)(2,1)S(1)}, bf16[128,256]{1,0:T(8,128)(2,1)S(1)}, u32[]{:S(2)}, u32[]{:S(2)}) collective-permute-start(bf16[128,256]{1,0:T(8,128)(2,1)S(1)} %get-tuple-element.61), channel_id=1, source_target_pairs={{0,4},{1,5},{2,6},{3,7},{4,0},{5,1},{6,2},{7,3},{8,12},{9,13},{10,... | collective-permute-start | bytes 196616 | tf_op jit(solution)/shard_map/ppermute | solution.py:410
  45.4 8.2 %collective-permute-start.20 = (bf16[128,256]{1,0:T(8,128)(2,1)S(1)}, bf16[128,256]{1,0:T(8,128)(2,1)S(1)}, u32[]{:S(2)}, u32[]{:S(2)}) collective-permute-start(bf16[128,256]{1,0:T(8,128)(2,1)S(1)} %get-tuple-element.63), channel_id=1, source_target_pairs={{0,4},{1,5},{2,6},{3,7},{4,0},{5,1},{6,2},{7,3},{8,12},{9,13},{10,... | collective-permute-start | bytes 196616 | tf_op jit(solution)/shard_map/ppermute | solution.py:410
  49.2 10.0 %collective-permute-start.22 = (bf16[256,256]{1,0:T(8,128)(2,1)S(1)}, bf16[256,256]{1,0:T(8,128)(2,1)S(1)}, u32[]{:S(2)}, u32[]{:S(2)}) collective-permute-start(bf16[256,256]{1,0:T(8,128)(2,1)S(1)} %get-tuple-element.65), channel_id=1, source_target_pairs={{0,4},{1,5},{2,6},{3,7},{4,0},{5,1},{6,2},{7,3},{8,12},{9,13},{10,... | collective-permute-start | bytes 393224 | tf_op jit(solution)/shard_map/ppermute | solution.py:410
  50.3 8.2 %collective-permute-start.19 = (bf16[128,256]{1,0:T(8,128)(2,1)S(1)}, bf16[128,256]{1,0:T(8,128)(2,1)S(1)}, u32[]{:S(2)}, u32[]{:S(2)}) collective-permute-start(bf16[128,256]{1,0:T(8,128)(2,1)S(1)} %shard_map.86), channel_id=1, source_target_pairs={{0,8},{1,9},{2,10},{3,11},{4,12},{5,13},{6,14},{7,15},{8,0},{9,1},... | collective-permute-start | bytes 196616 | tf_op jit(solution)/shard_map/ppermute | solution.py:410
  53.7 5.5 %collective-permute-start.21 = (bf16[128,256]{1,0:T(8,128)(2,1)S(1)}, bf16[128,256]{1,0:T(8,128)(2,1)S(1)}, u32[]{:S(2)}, u32[]{:S(2)}) collective-permute-start(bf16[128,256]{1,0:T(8,128)(2,1)S(1)} %shard_map.88), channel_id=1, source_target_pairs={{0,8},{1,9},{2,10},{3,11},{4,12},{5,13},{6,14},{7,15},{8,0},{9,1},... | collective-permute-start | bytes 196616 | tf_op jit(solution)/shard_map/ppermute | solution.py:410

commit v22 on v19

--- a/solution.py
+++ b/solution.py
@@ -475,7 +475,7 @@
     (factors,) = call(
         functools.partial(chain_kernel, features, heads),
         [((9 * block // 2, half), BF16)],
-        index, doc_lengths, *exchange(sent)[::-1], scalars=2,
+        index, doc_lengths, *exchange(sent), scalars=2,
     )
     piece = (qkv_rows + heads, width)
     far_order = tuple(reversed(range(planes - planes // 2, planes)))

time: 58.9 us -> 59.3 us (level)
  no operation moved by 1% of the time
where the time goes in v22:
time: 59.3 us; the launch traced here: 58.9 us
  starting transfers between devices  26.3 us (44%)
  waiting for transfers between devices  19.2 us (32%)
  Pallas kernels  12.5 us (21%)
  between operations  0.77 us (1%)
    ppermute x8, starting transfers between devices, along_z(): return lax.ppermute(value, 'dp', route)  12.4 us
    ppermute x9, starting transfers between devices, along_plane(): return lax.ppermute(value, 'dp', route)  12.2 us
    ppermute x8, waiting for transfers between devices, along_z(): return lax.ppermute(value, 'dp', route)  9.79 us
    ppermute x9, waiting for transfers between devices, along_plane(): return lax.ppermute(value, 'dp', route)  8.42 us
    pallas_call x11, Pallas kernels, call(): pl.pallas_call(kernel, out_shape=[jax.ShapeDtypeStruct(shape, dtype) for...  7.68 us
    ppermute x6, starting transfers between devices, to_sibling(): return lax.ppermute(value, 'section', [(0, 1), (1, 0)])  1.71 us
    pallas_call x1, Pallas kernels, planar(): pl.pallas_call(functools.partial(blocks_kernel, planes), out_shape=[one_b...  1.69 us
    pallas_call x1, Pallas kernels, planar(): pl.pallas_call(functools.partial(first_kernel, planes), out_shape=[jax.Sh...  1.66 us
  transfers between devices with their start and end apart: 23, of which 12 were waited for; matrix products, arithmetic and copies ran while one was open for 0% of the time, Pallas kernels for 7%

profile of v22, /device:TPU:0, one launch (start us, length us, event | category | flops | bytes accessed | tf_op | source)
XLA Modules:
  0.0 58.9 jit_solution(2907761541991769711)
XLA Ops:
  0.6 0.1 pad_add_fusion.index
  0.7 1.7 %shard_map.77 = (bf16[256,256]{1,0:T(8,128)(2,1)S(1)}, bf16[2,64,1024]{2,1,0:T(8,128)(2,1)S(1)}) custom-call(s32[3]{0:T(128)S(1)} %pad_add_fusion.index, bf16[192,256]{1,0:T(8,128)(2,1)} %bitcast.11, bf16[64,256]{1,0:T(8,128)(2,1)} %bitcast.12, bf16[2,64,4096]{2,1,0:T(8,128)(2,1)} %x_ref.5, bf16[2,64,4096]{2,1,0:T(8,128)(2,1)} %c_ref.5), custom_call_target="tpu_custom_call" | custom-call | tf_op jit(solution)/shard_map/pallas_call | solution.py:430
  2.4 4.0 %collective-permute-start = (bf16[2,64,1024]{2,1,0:T(8,128)(2,1)S(1)}, bf16[2,64,1024]{2,1,0:T(8,128)(2,1)S(1)}, u32[]{:S(2)}, u32[]{:S(2)}) collective-permute-start(bf16[2,64,1024]{2,1,0:T(8,128)(2,1)S(1)} %get-tuple-element.35), channel_id=1, source_target_pairs={{0,3},{1,2},{2,1},{3,0},{4,7},{5,6},{6,5},{7,4},{8,11},{9,10},{10,... | collective-permute-start | bytes 786440 | tf_op jit(solution)/shard_map/ppermute | solution.py:417
  6.4 0.0 copy-start.1
  6.4 2.6 %collective-permute-start.4 = (bf16[256,256]{1,0:T(8,128)(2,1)S(1)}, bf16[256,256]{1,0:T(8,128)(2,1)S(1)}, u32[]{:S(2)}, u32[]{:S(2)}) collective-permute-start(bf16[256,256]{1,0:T(8,128)(2,1)S(1)} %get-tuple-element.36.pack_ref), channel_id=1, source_target_pairs={{0,8},{1,9},{2,10},{3,11},{4,12},{5,13},{6,14},{7,15},{8,0},{9,1},... | collective-permute-start | bytes 393224 | tf_op jit(solution)/shard_map/ppermute | solution.py:410
  8.9 1.6 %collective-permute-start.3 = (bf16[256,256]{1,0:T(8,128)(2,1)S(1)}, bf16[256,256]{1,0:T(8,128)(2,1)S(1)}, u32[]{:S(2)}, u32[]{:S(2)}) collective-permute-start(bf16[256,256]{1,0:T(8,128)(2,1)S(1)} %get-tuple-element.36.pack_ref), channel_id=1, source_target_pairs={{0,4},{1,5},{2,6},{3,7},{4,0},{5,1},{6,2},{7,3},{8,12},{9,13},{10,... | collective-permute-start | bytes 393224 | tf_op jit(solution)/shard_map/ppermute | solution.py:410
  10.5 1.7 %shard_map.79 = (bf16[2,64,1024]{2,1,0:T(8,128)(2,1)S(1)}, bf16[2,64,1024]{2,1,0:T(8,128)(2,1)S(1)}) custom-call(s32[3]{0:T(128)S(1)} %pad_add_fusion.index, bf16[2,64,4096]{2,1,0:T(8,128)(2,1)} %x_ref.5, bf16[2,64,4096]{2,1,0:T(8,128)(2,1)} %c_ref.5), custom_call_target="tpu_custom_call" | custom-call | tf_op jit(solution)/shard_map/pallas_call | solution.py:438
  12.2 0.6 collective-permute-start.1
  12.8 0.5 collective-permute-start.2
  13.3 1.8 %collective-permute-done.4.refs_6_ = bf16[256,256]{1,0:T(8,128)(2,1)S(1)} collective-permute-done((bf16[256,256]{1,0:T(8,128)(2,1)S(1)}, bf16[256,256]{1,0:T(8,128)(2,1)S(1)}, u32[]{:S(2)}, u32[]{:S(2)}) %collective-permute-start.4) | collective-permute-done | bytes 131104 | tf_op jit(solution)/shard_map/ppermute | solution.py:410
  15.1 0.6 collective-permute-start.5
  15.7 0.0 collective-permute-done.3.refs_5_
  15.7 0.0 collective-permute-start.7
  15.7 0.0 copy-done.1
  15.7 0.1 reduce
  15.8 0.0 collective-permute-done.refs_1_
  15.8 1.5 %shard_map.78 = (bf16[272,256]{1,0:T(8,128)(2,1)S(1)}, bf16[2,64,1024]{2,1,0:T(8,128)(2,1)S(1)}) custom-call(s32[3]{0:T(128)S(1)} %pad_add_fusion.index, bf16[256,256]{1,0:T(8,128)(2,1)S(1)} %get-tuple-element.36.pack_ref, bf16[16,256]{1,0:T(8,128)(2,1)S(1)} %reshape_squeeze.3.gain_ref, bf16[2,64,4096]{2,1,0:T(8,128)(2,1)} %x_ref.5, bf16[2,64,4096]{2,1,0:T(8,128)(2,1)} %c_ref.5), custom_call_target="tpu_custom_call" | custom-call | tf_op jit(solution)/shard_map/pallas_call | solution.py:454
  17.3 0.6 collective-permute-start.6
  17.8 2.2 %collective-permute-done.5.refs_7_ = bf16[256,256]{1,0:T(8,128)(2,1)S(1)} collective-permute-done((bf16[256,256]{1,0:T(8,128)(2,1)S(1)}, bf16[256,256]{1,0:T(8,128)(2,1)S(1)}, u32[]{:S(2)}, u32[]{:S(2)}) %collective-permute-start.5) | collective-permute-done | bytes 131104 | tf_op jit(solution)/shard_map/ppermute | solution.py:410
  20.1 0.0 collective-permute-start.9
  20.1 0.0 collective-permute-done.7.refs_9_
  20.1 0.5 collective-permute-start.8
  20.6 0.0 collective-permute-done.1.refs_2_
  20.6 0.0 collective-permute-done.2.refs_3_
  20.6 0.8 %collective-permute-done.9.refs_11_ = bf16[256,256]{1,0:T(8,128)(2,1)S(1)} collective-permute-done((bf16[256,256]{1,0:T(8,128)(2,1)S(1)}, bf16[256,256]{1,0:T(8,128)(2,1)S(1)}, u32[]{:S(2)}, u32[]{:S(2)}) %collective-permute-start.9) | collective-permute-done | bytes 131104 | tf_op jit(solution)/shard_map/ppermute | solution.py:413
  21.4 0.2 collective-permute-done.8.refs_10_
  21.6 0.0 collective-permute-done.6.refs_8_
  21.6 1.6 %shard_map.80 = (bf16[4,64,1024]{2,1,0:T(8,128)(2,1)S(1)}, bf16[4,64,1024]{2,1,0:T(8,128)(2,1)S(1)}, bf16[4,512,256]{2,1,0:T(8,128)(2,1)S(1)}, f32[4,8,256]{2,1,...) custom-call(s32[3]{0:T(128)S(1)} %pad_add_fusion.index, ...), custom_call_target="tpu_custom_call" | custom-call | tf_op jit(solution)/shard_map/pallas_call | solution.py:387
  23.2 0.6 %collective-permute-start.10 = (bf16[64,896]{1,0:T(8,128)(2,1)S(1)}, bf16[64,896]{1,0:T(8,128)(2,1)S(1)}, u32[]{:S(2)}, u32[]{:S(2)}) collective-permute-start(bf16[64,896]{1,0:T(8,128)(2,1)S(1)} %get-tuple-element.44), channel_id=1, source_target_pairs={{0,1},{1,0},{2,3},{3,2},{4,5},{5,4},{6,7},{7,6},{8,9},{9,8},{10,11... | collective-permute-start | bytes 344072 | tf_op jit(solution)/shard_map/ppermute | solution.py:417
  23.8 0.7 %collective-permute-start.11 = (bf16[64,896]{1,0:T(8,128)(2,1)S(1)}, bf16[64,896]{1,0:T(8,128)(2,1)S(1)}, u32[]{:S(2)}, u32[]{:S(2)}) collective-permute-start(bf16[64,896]{1,0:T(8,128)(2,1)S(1)} %get-tuple-element.45), channel_id=1, source_target_pairs={{0,2},{1,3},{2,0},{3,1},{4,6},{5,7},{6,4},{7,5},{8,10},{9,11},{10,... | collective-permute-start | bytes 344072 | tf_op jit(solution)/shard_map/ppermute | solution.py:417
  24.5 0.0 copy-start
  24.5 2.3 %collective-permute-start.12 = (bf16[64,896]{1,0:T(8,128)(2,1)S(1)}, bf16[64,896]{1,0:T(8,128)(2,1)S(1)}, u32[]{:S(2)}, u32[]{:S(2)}) collective-permute-start(bf16[64,896]{1,0:T(8,128)(2,1)S(1)} %get-tuple-element.46), channel_id=1, source_target_pairs={{0,3},{1,2},{2,1},{3,0},{4,7},{5,6},{6,5},{7,4},{8,11},{9,10},{10,... | collective-permute-start | bytes 344072 | tf_op jit(solution)/shard_map/ppermute | solution.py:417
  26.8 2.5 %collective-permute-done.10.refs_1_ = bf16[64,896]{1,0:T(8,128)(2,1)S(1)} collective-permute-done((bf16[64,896]{1,0:T(8,128)(2,1)S(1)}, bf16[64,896]{1,0:T(8,128)(2,1)S(1)}, u32[]{:S(2)}, u32[]{:S(2)}) %collective-permute-start.10) | collective-permute-done | bytes 114720 | tf_op jit(solution)/shard_map/ppermute | solution.py:417
  29.3 2.1 %collective-permute-done.11.refs_2_ = bf16[64,896]{1,0:T(8,128)(2,1)S(1)} collective-permute-done((bf16[64,896]{1,0:T(8,128)(2,1)S(1)}, bf16[64,896]{1,0:T(8,128)(2,1)S(1)}, u32[]{:S(2)}, u32[]{:S(2)}) %collective-permute-start.11) | collective-permute-done | bytes 114720 | tf_op jit(solution)/shard_map/ppermute | solution.py:417
  31.4 0.0 collective-permute-done.12.refs_3_
  31.4 0.0 copy-done
  31.4 2.8 %shard_map.81.refs_0_ = bf16[288,128]{1,0:T(8,128)(2,1)S(1)} custom-call(s32[3]{0:T(128)S(1)} %pad_add_fusion.index, s32[2,1,2]{2,1,0:T(1,128)S(1)} %copy-done, bf16[64,896]{1,0:T(8,128)(2,1)S(1)} %get-tuple-element.43.refs_0_, bf16[64,896]{1,0:T(8,128)(2,1)S(1)} %collective-permute-done.10.refs_1_, bf16[64,896]{1,0:T(8,128)(2,1)S(1)} %collective-permute-done.11.refs_2_, ...), custom_call_target="tpu_custom_call" | custom-call | tf_op jit(solution)/shard_map/pallas_call | solution.py:387
  34.2 1.5 %collective-permute-start.15 = (bf16[288,128]{1,0:T(8,128)(2,1)S(1)}, bf16[288,128]{1,0:T(8,128)(2,1)S(1)}, u32[]{:S(2)}, u32[]{:S(2)}) collective-permute-start(bf16[288,128]{1,0:T(8,128)(2,1)S(1)} %shard_map.81.refs_0_), channel_id=1, source_target_pairs={{0,3},{1,2},{2,1},{3,0},{4,7},{5,6},{6,5},{7,4},{8,11},{9,10},{10,... | collective-permute-start | bytes 221192 | tf_op jit(solution)/shard_map/ppermute | solution.py:417
  35.7 1.5 %collective-permute-start.14 = (bf16[288,128]{1,0:T(8,128)(2,1)S(1)}, bf16[288,128]{1,0:T(8,128)(2,1)S(1)}, u32[]{:S(2)}, u32[]{:S(2)}) collective-permute-start(bf16[288,128]{1,0:T(8,128)(2,1)S(1)} %shard_map.81.refs_0_), channel_id=1, source_target_pairs={{0,2},{1,3},{2,0},{3,1},{4,6},{5,7},{6,4},{7,5},{8,10},{9,11},{10,... | collective-permute-start | bytes 221192 | tf_op jit(solution)/shard_map/ppermute | solution.py:417
  37.2 0.5 collective-permute-start.13
  37.8 2.1 %collective-permute-done.15.refs_3_ = bf16[288,128]{1,0:T(8,128)(2,1)S(1)} collective-permute-done((bf16[288,128]{1,0:T(8,128)(2,1)S(1)}, bf16[288,128]{1,0:T(8,128)(2,1)S(1)}, u32[]{:S(2)}, u32[]{:S(2)}) %collective-permute-start.15) | collective-permute-done | bytes 73760 | tf_op jit(solution)/shard_map/ppermute | solution.py:417
  39.9 0.7 %collective-permute-done.14.refs_2_ = bf16[288,128]{1,0:T(8,128)(2,1)S(1)} collective-permute-done((bf16[288,128]{1,0:T(8,128)(2,1)S(1)}, bf16[288,128]{1,0:T(8,128)(2,1)S(1)}, u32[]{:S(2)}, u32[]{:S(2)}) %collective-permute-start.14) | collective-permute-done | bytes 73760 | tf_op jit(solution)/shard_map/ppermute | solution.py:417
  40.6 1.0 %collective-permute-done.13.refs_1_ = bf16[288,128]{1,0:T(8,128)(2,1)S(1)} collective-permute-done((bf16[288,128]{1,0:T(8,128)(2,1)S(1)}, bf16[288,128]{1,0:T(8,128)(2,1)S(1)}, u32[]{:S(2)}, u32[]{:S(2)}) %collective-permute-start.13) | collective-permute-done | bytes 73760 | tf_op jit(solution)/shard_map/ppermute | solution.py:417
  41.6 1.3 %shard_map.82 = (f32[2,256,256]{2,1,0:T(8,128)S(1)}, bf16[2,256,256]{2,1,0:T(8,128)(2,1)S(1)}, bf16[640,256]{1,0:T(8,128)(2,1)S(1)}, bf16[256,64]{1,0:T(8,128)(2,1)S(1)}, bf16[64,192]{1,0:T(8,128)(2,1)S(1)}) custom-call(s32[3]{0:T(128)S(1)} %pad_add_fusion.index, bf16[288,128]{1,0:T(8,128)(2,1)S(1)} %shard_map.81.refs_0_, ...), custom_call_target="tpu_custom_call" | custom-call | tf_op jit(solution)/shard_map/pallas_call | solution.py:387
  42.9 0.1 collective-permute-start.17
  43.0 1.0 %shard_map.83 = (f32[2,256,256]{2,1,0:T(8,128)S(1)}, bf16[2,256,256]{2,1,0:T(8,128)(2,1)S(1)}) custom-call(s32[3]{0:T(128)S(1)} %pad_add_fusion.index, bf16[640,256]{1,0:T(8,128)(2,1)S(1)} %get-tuple-element.51.turned_ref, bf16[256,64]{1,0:T(8,128)(2,1)S(1)} %get-tuple-element.52.small_ref, bf16[64,192]{1,0:T(8,128)(2,1)S(1)} %get-tuple-element.53.small_t_ref, ...), custom_call_target="tpu_custom_call" | custom-call | tf_op jit(solution)/shard_map/pallas_call | solution.py:387
  44.1 0.6 collective-permute-start.16
  44.6 0.0 collective-permute-done.17.come_ref
  44.7 1.1 %collective-permute-start.18 = (bf16[128,256]{1,0:T(8,128)(2,1)S(1)}, bf16[128,256]{1,0:T(8,128)(2,1)S(1)}, u32[]{:S(2)}, u32[]{:S(2)}) collective-permute-start(bf16[128,256]{1,0:T(8,128)(2,1)S(1)} %get-tuple-element.60), channel_id=1, source_target_pairs={{0,4},{1,5},{2,6},{3,7},{4,0},{5,1},{6,2},{7,3},{8,12},{9,13},{10,... | collective-permute-start | bytes 196616 | tf_op jit(solution)/shard_map/ppermute | solution.py:410
  45.8 1.0 %collective-permute-start.20 = (bf16[128,256]{1,0:T(8,128)(2,1)S(1)}, bf16[128,256]{1,0:T(8,128)(2,1)S(1)}, u32[]{:S(2)}, u32[]{:S(2)}) collective-permute-start(bf16[128,256]{1,0:T(8,128)(2,1)S(1)} %get-tuple-element.62), channel_id=1, source_target_pairs={{0,4},{1,5},{2,6},{3,7},{4,0},{5,1},{6,2},{7,3},{8,12},{9,13},{10,... | collective-permute-start | bytes 196616 | tf_op jit(solution)/shard_map/ppermute | solution.py:410
  46.8 0.0 collective-permute-done.16.come_ref
  46.8 0.1 shard_map.84
  46.8 1.1 %collective-permute-start.22 = (bf16[256,256]{1,0:T(8,128)(2,1)S(1)}, bf16[256,256]{1,0:T(8,128)(2,1)S(1)}, u32[]{:S(2)}, u32[]{:S(2)}) collective-permute-start(bf16[256,256]{1,0:T(8,128)(2,1)S(1)} %get-tuple-element.63), channel_id=1, source_target_pairs={{0,4},{1,5},{2,6},{3,7},{4,0},{5,1},{6,2},{7,3},{8,12},{9,13},{10,... | collective-permute-start | bytes 393224 | tf_op jit(solution)/shard_map/ppermute | solution.py:410
  47.9 1.8 %collective-permute-done.18.b_ref = bf16[128,256]{1,0:T(8,128)(2,1)S(1)} collective-permute-done((bf16[128,256]{1,0:T(8,128)(2,1)S(1)}, bf16[128,256]{1,0:T(8,128)(2,1)S(1)}, u32[]{:S(2)}, u32[]{:S(2)}) %collective-permute-start.18) | collective-permute-done | bytes 65568 | tf_op jit(solution)/shard_map/ppermute | solution.py:410
  49.7 2.2 %collective-permute-start.19 = (bf16[128,256]{1,0:T(8,128)(2,1)S(1)}, bf16[128,256]{1,0:T(8,128)(2,1)S(1)}, u32[]{:S(2)}, u32[]{:S(2)}) collective-permute-start(bf16[128,256]{1,0:T(8,128)(2,1)S(1)} %shard_map.86), channel_id=1, source_target_pairs={{0,8},{1,9},{2,10},{3,11},{4,12},{5,13},{6,14},{7,15},{8,0},{9,1},... | collective-permute-start | bytes 196616 | tf_op jit(solution)/shard_map/ppermute | solution.py:410
  52.0 0.0 collective-permute-done.20.b_ref
  52.0 2.2 %collective-permute-start.21 = (bf16[128,256]{1,0:T(8,128)(2,1)S(1)}, bf16[128,256]{1,0:T(8,128)(2,1)S(1)}, u32[]{:S(2)}, u32[]{:S(2)}) collective-permute-start(bf16[128,256]{1,0:T(8,128)(2,1)S(1)} %shard_map.88), channel_id=1, source_target_pairs={{0,8},{1,9},{2,10},{3,11},{4,12},{5,13},{6,14},{7,15},{8,0},{9,1},... | collective-permute-start | bytes 196616 | tf_op jit(solution)/shard_map/ppermute | solution.py:410
  54.2 2.2 %collective-permute-done.19.part_ref = bf16[128,256]{1,0:T(8,128)(2,1)S(1)} collective-permute-done((bf16[128,256]{1,0:T(8,128)(2,1)S(1)}, bf16[128,256]{1,0:T(8,128)(2,1)S(1)}, u32[]{:S(2)}, u32[]{:S(2)}) %collective-permute-start.19) | collective-permute-done | bytes 65568 | tf_op jit(solution)/shard_map/ppermute | solution.py:410
  56.5 1.7 %collective-permute-done.21.part_ref = bf16[128,256]{1,0:T(8,128)(2,1)S(1)} collective-permute-done((bf16[128,256]{1,0:T(8,128)(2,1)S(1)}, bf16[128,256]{1,0:T(8,128)(2,1)S(1)}, u32[]{:S(2)}, u32[]{:S(2)}) %collective-permute-start.21) | collective-permute-done | bytes 65568 | tf_op jit(solution)/shard_map/ppermute | solution.py:410
  58.2 0.0 collective-permute-done.22.refs_0_
  58.2 0.7 %shard_map.90 = (f32[192,256]{1,0:T(8,128)}, f32[64,256]{1,0:T(8,128)}) custom-call(f32[256,256]{1,0:T(8,128)S(1)} %shard_map.89.keep_ref, bf16[256,256]{1,0:T(8,128)(2,1)S(1)} %collective-permute-done.22.refs_0_), custom_call_target="tpu_custom_call" | custom-call | tf_op jit(solution)/shard_map/pallas_call | solution.py:387
  (6 shorter events, 0.1 us)
Async XLA Ops:
  2.4 13.4 %collective-permute-start = (bf16[2,64,1024]{2,1,0:T(8,128)(2,1)S(1)}, bf16[2,64,1024]{2,1,0:T(8,128)(2,1)S(1)}, u32[]{:S(2)}, u32[]{:S(2)}) collective-permute-start(bf16[2,64,1024]{2,1,0:T(8,128)(2,1)S(1)} %get-tuple-element.35), channel_id=1, source_target_pairs={{0,3},{1,2},{2,1},{3,0},{4,7},{5,6},{6,5},{7,4},{8,11},{9,10},{10,... | collective-permute-start | bytes 786440 | tf_op jit(solution)/shard_map/ppermute | solution.py:417
  6.4 9.3 %copy-start.1 = (bf16[1,4096]{1,0:T(2,128)(2,1)S(1)}, bf16[1,4096]{1,0:T(2,128)(2,1)}, u32[]{:S(2)}) copy-start(bf16[1,4096]{1,0:T(2,128)(2,1)} %param.9) | copy-start | bytes 24580
  6.4 8.8 %collective-permute-start.4 = (bf16[256,256]{1,0:T(8,128)(2,1)S(1)}, bf16[256,256]{1,0:T(8,128)(2,1)S(1)}, u32[]{:S(2)}, u32[]{:S(2)}) collective-permute-start(bf16[256,256]{1,0:T(8,128)(2,1)S(1)} %get-tuple-element.36.pack_ref), channel_id=1, source_target_pairs={{0,8},{1,9},{2,10},{3,11},{4,12},{5,13},{6,14},{7,15},{8,0},{9,1},... | collective-permute-start | bytes 393224 | tf_op jit(solution)/shard_map/ppermute | solution.py:410
  8.9 6.8 %collective-permute-start.3 = (bf16[256,256]{1,0:T(8,128)(2,1)S(1)}, bf16[256,256]{1,0:T(8,128)(2,1)S(1)}, u32[]{:S(2)}, u32[]{:S(2)}) collective-permute-start(bf16[256,256]{1,0:T(8,128)(2,1)S(1)} %get-tuple-element.36.pack_ref), channel_id=1, source_target_pairs={{0,4},{1,5},{2,6},{3,7},{4,0},{5,1},{6,2},{7,3},{8,12},{9,13},{10,... | collective-permute-start | bytes 393224 | tf_op jit(solution)/shard_map/ppermute | solution.py:410
  12.2 8.4 %collective-permute-start.1 = (bf16[2,64,1024]{2,1,0:T(8,128)(2,1)S(1)}, bf16[2,64,1024]{2,1,0:T(8,128)(2,1)S(1)}, u32[]{:S(2)}, u32[]{:S(2)}) collective-permute-start(bf16[2,64,1024]{2,1,0:T(8,128)(2,1)S(1)} %get-tuple-element.39), channel_id=1, source_target_pairs={{0,2},{1,3},{2,0},{3,1},{4,6},{5,7},{6,4},{7,5},{8,10},{9,11},{10,... | collective-permute-start | bytes 786440 | tf_op jit(solution)/shard_map/ppermute | solution.py:417
  12.8 7.8 %collective-permute-start.2 = (bf16[2,64,1024]{2,1,0:T(8,128)(2,1)S(1)}, bf16[2,64,1024]{2,1,0:T(8,128)(2,1)S(1)}, u32[]{:S(2)}, u32[]{:S(2)}) collective-permute-start(bf16[2,64,1024]{2,1,0:T(8,128)(2,1)S(1)} %get-tuple-element.40), channel_id=1, source_target_pairs={{0,1},{1,0},{2,3},{3,2},{4,5},{5,4},{6,7},{7,6},{8,9},{9,8},{10,11... | collective-permute-start | bytes 786440 | tf_op jit(solution)/shard_map/ppermute | solution.py:417
  15.1 5.0 %collective-permute-start.5 = (bf16[256,256]{1,0:T(8,128)(2,1)S(1)}, bf16[256,256]{1,0:T(8,128)(2,1)S(1)}, u32[]{:S(2)}, u32[]{:S(2)}) collective-permute-start(bf16[256,256]{1,0:T(8,128)(2,1)S(1)} %collective-permute-done.4.refs_6_), channel_id=1, source_target_pairs={{0,4},{1,5},{2,6},{3,7},{4,0},{5,1},{6,2},{7,3},{8,12},{9,13},{10,... | collective-permute-start | bytes 393224 | tf_op jit(solution)/shard_map/ppermute | solution.py:410
  15.7 4.4 %collective-permute-start.7 = (bf16[256,256]{1,0:T(8,128)(2,1)S(1)}, bf16[256,256]{1,0:T(8,128)(2,1)S(1)}, u32[]{:S(2)}, u32[]{:S(2)}) collective-permute-start(bf16[256,256]{1,0:T(8,128)(2,1)S(1)} %collective-permute-done.3.refs_5_), channel_id=1, source_target_pairs={{0,16},{16,0},{1,17},{17,1},{2,18},{18,2},{3,19},{19,3},{4,20},{20... | collective-permute-start | bytes 393224 | tf_op jit(solution)/shard_map/ppermute | solution.py:413
  17.3 4.3 %collective-permute-start.6 = (bf16[272,256]{1,0:T(8,128)(2,1)S(1)}, bf16[272,256]{1,0:T(8,128)(2,1)S(1)}, u32[]{:S(2)}, u32[]{:S(2)}) collective-permute-start(bf16[272,256]{1,0:T(8,128)(2,1)S(1)} %get-tuple-element.41.refs_4_), channel_id=1, source_target_pairs={{0,16},{16,0},{1,17},{17,1},{2,18},{18,2},{3,19},{19,3},{4,20},{20... | collective-permute-start | bytes 417800 | tf_op jit(solution)/shard_map/ppermute | solution.py:413
  20.1 1.3 %collective-permute-start.9 = (bf16[256,256]{1,0:T(8,128)(2,1)S(1)}, bf16[256,256]{1,0:T(8,128)(2,1)S(1)}, u32[]{:S(2)}, u32[]{:S(2)}) collective-permute-start(bf16[256,256]{1,0:T(8,128)(2,1)S(1)} %collective-permute-done.5.refs_7_), channel_id=1, source_target_pairs={{0,16},{16,0},{1,17},{17,1},{2,18},{18,2},{3,19},{19,3},{4,20},{20... | collective-permute-start | bytes 393224 | tf_op jit(solution)/shard_map/ppermute | solution.py:413
  20.1 1.5 %collective-permute-start.8 = (bf16[256,256]{1,0:T(8,128)(2,1)S(1)}, bf16[256,256]{1,0:T(8,128)(2,1)S(1)}, u32[]{:S(2)}, u32[]{:S(2)}) collective-permute-start(bf16[256,256]{1,0:T(8,128)(2,1)S(1)} %collective-permute-done.4.refs_6_), channel_id=1, source_target_pairs={{0,16},{16,0},{1,17},{17,1},{2,18},{18,2},{3,19},{19,3},{4,20},{20... | collective-permute-start | bytes 393224 | tf_op jit(solution)/shard_map/ppermute | solution.py:413
  23.2 6.0 %collective-permute-start.10 = (bf16[64,896]{1,0:T(8,128)(2,1)S(1)}, bf16[64,896]{1,0:T(8,128)(2,1)S(1)}, u32[]{:S(2)}, u32[]{:S(2)}) collective-permute-start(bf16[64,896]{1,0:T(8,128)(2,1)S(1)} %get-tuple-element.44), channel_id=1, source_target_pairs={{0,1},{1,0},{2,3},{3,2},{4,5},{5,4},{6,7},{7,6},{8,9},{9,8},{10,11... | collective-permute-start | bytes 344072 | tf_op jit(solution)/shard_map/ppermute | solution.py:417
  23.8 7.6 %collective-permute-start.11 = (bf16[64,896]{1,0:T(8,128)(2,1)S(1)}, bf16[64,896]{1,0:T(8,128)(2,1)S(1)}, u32[]{:S(2)}, u32[]{:S(2)}) collective-permute-start(bf16[64,896]{1,0:T(8,128)(2,1)S(1)} %get-tuple-element.45), channel_id=1, source_target_pairs={{0,2},{1,3},{2,0},{3,1},{4,6},{5,7},{6,4},{7,5},{8,10},{9,11},{10,... | collective-permute-start | bytes 344072 | tf_op jit(solution)/shard_map/ppermute | solution.py:417
  24.5 6.9 %copy-start = (s32[2,1,2]{2,1,0:T(1,128)S(1)}, s32[2,1,2]{2,1,0:T(1,128)}, u32[]{:S(2)}) copy-start(s32[2,1,2]{2,1,0:T(1,128)} %docs.1) | copy-start | bytes 52
  24.5 6.9 %collective-permute-start.12 = (bf16[64,896]{1,0:T(8,128)(2,1)S(1)}, bf16[64,896]{1,0:T(8,128)(2,1)S(1)}, u32[]{:S(2)}, u32[]{:S(2)}) collective-permute-start(bf16[64,896]{1,0:T(8,128)(2,1)S(1)} %get-tuple-element.46), channel_id=1, source_target_pairs={{0,3},{1,2},{2,1},{3,0},{4,7},{5,6},{6,5},{7,4},{8,11},{9,10},{10,... | collective-permute-start | bytes 344072 | tf_op jit(solution)/shard_map/ppermute | solution.py:417
  34.2 5.7 %collective-permute-start.15 = (bf16[288,128]{1,0:T(8,128)(2,1)S(1)}, bf16[288,128]{1,0:T(8,128)(2,1)S(1)}, u32[]{:S(2)}, u32[]{:S(2)}) collective-permute-start(bf16[288,128]{1,0:T(8,128)(2,1)S(1)} %shard_map.81.refs_0_), channel_id=1, source_target_pairs={{0,3},{1,2},{2,1},{3,0},{4,7},{5,6},{6,5},{7,4},{8,11},{9,10},{10,... | collective-permute-start | bytes 221192 | tf_op jit(solution)/shard_map/ppermute | solution.py:417
  35.7 4.8 %collective-permute-start.14 = (bf16[288,128]{1,0:T(8,128)(2,1)S(1)}, bf16[288,128]{1,0:T(8,128)(2,1)S(1)}, u32[]{:S(2)}, u32[]{:S(2)}) collective-permute-start(bf16[288,128]{1,0:T(8,128)(2,1)S(1)} %shard_map.81.refs_0_), channel_id=1, source_target_pairs={{0,2},{1,3},{2,0},{3,1},{4,6},{5,7},{6,4},{7,5},{8,10},{9,11},{10,... | collective-permute-start | bytes 221192 | tf_op jit(solution)/shard_map/ppermute | solution.py:417
  37.2 4.4 %collective-permute-start.13 = (bf16[288,128]{1,0:T(8,128)(2,1)S(1)}, bf16[288,128]{1,0:T(8,128)(2,1)S(1)}, u32[]{:S(2)}, u32[]{:S(2)}) collective-permute-start(bf16[288,128]{1,0:T(8,128)(2,1)S(1)} %shard_map.81.refs_0_), channel_id=1, source_target_pairs={{0,1},{1,0},{2,3},{3,2},{4,5},{5,4},{6,7},{7,6},{8,9},{9,8},{10,11... | collective-permute-start | bytes 221192 | tf_op jit(solution)/shard_map/ppermute | solution.py:417
  42.9 1.7 %collective-permute-start.17 = (bf16[2,256,256]{2,1,0:T(8,128)(2,1)S(1)}, bf16[2,256,256]{2,1,0:T(8,128)(2,1)S(1)}, u32[]{:S(2)}, u32[]{:S(2)}) collective-permute-start(bf16[2,256,256]{2,1,0:T(8,128)(2,1)S(1)} %get-tuple-element.58), channel_id=1, source_target_pairs={{0,16},{16,0},{1,17},{17,1},{2,18},{18,2},{3,19},{19,3},{4,20},{20... | collective-permute-start | bytes 786440 | tf_op jit(solution)/shard_map/ppermute | solution.py:413
  44.1 2.7 %collective-permute-start.16 = (bf16[2,256,256]{2,1,0:T(8,128)(2,1)S(1)}, bf16[2,256,256]{2,1,0:T(8,128)(2,1)S(1)}, u32[]{:S(2)}, u32[]{:S(2)}) collective-permute-start(bf16[2,256,256]{2,1,0:T(8,128)(2,1)S(1)} %get-tuple-element.55), channel_id=1, source_target_pairs={{0,16},{16,0},{1,17},{17,1},{2,18},{18,2},{3,19},{19,3},{4,20},{20... | collective-permute-start | bytes 786440 | tf_op jit(solution)/shard_map/ppermute | solution.py:413
  44.7 5.0 %collective-permute-start.18 = (bf16[128,256]{1,0:T(8,128)(2,1)S(1)}, bf16[128,256]{1,0:T(8,128)(2,1)S(1)}, u32[]{:S(2)}, u32[]{:S(2)}) collective-permute-start(bf16[128,256]{1,0:T(8,128)(2,1)S(1)} %get-tuple-element.60), channel_id=1, source_target_pairs={{0,4},{1,5},{2,6},{3,7},{4,0},{5,1},{6,2},{7,3},{8,12},{9,13},{10,... | collective-permute-start | bytes 196616 | tf_op jit(solution)/shard_map/ppermute | solution.py:410
  45.8 6.2 %collective-permute-start.20 = (bf16[128,256]{1,0:T(8,128)(2,1)S(1)}, bf16[128,256]{1,0:T(8,128)(2,1)S(1)}, u32[]{:S(2)}, u32[]{:S(2)}) collective-permute-start(bf16[128,256]{1,0:T(8,128)(2,1)S(1)} %get-tuple-element.62), channel_id=1, source_target_pairs={{0,4},{1,5},{2,6},{3,7},{4,0},{5,1},{6,2},{7,3},{8,12},{9,13},{10,... | collective-permute-start | bytes 196616 | tf_op jit(solution)/shard_map/ppermute | solution.py:410
  46.8 11.4 %collective-permute-start.22 = (bf16[256,256]{1,0:T(8,128)(2,1)S(1)}, bf16[256,256]{1,0:T(8,128)(2,1)S(1)}, u32[]{:S(2)}, u32[]{:S(2)}) collective-permute-start(bf16[256,256]{1,0:T(8,128)(2,1)S(1)} %get-tuple-element.63), channel_id=1, source_target_pairs={{0,4},{1,5},{2,6},{3,7},{4,0},{5,1},{6,2},{7,3},{8,12},{9,13},{10,... | collective-permute-start | bytes 393224 | tf_op jit(solution)/shard_map/ppermute | solution.py:410
  49.7 6.7 %collective-permute-start.19 = (bf16[128,256]{1,0:T(8,128)(2,1)S(1)}, bf16[128,256]{1,0:T(8,128)(2,1)S(1)}, u32[]{:S(2)}, u32[]{:S(2)}) collective-permute-start(bf16[128,256]{1,0:T(8,128)(2,1)S(1)} %shard_map.86), channel_id=1, source_target_pairs={{0,8},{1,9},{2,10},{3,11},{4,12},{5,13},{6,14},{7,15},{8,0},{9,1},... | collective-permute-start | bytes 196616 | tf_op jit(solution)/shard_map/ppermute | solution.py:410
  52.0 6.2 %collective-permute-start.21 = (bf16[128,256]{1,0:T(8,128)(2,1)S(1)}, bf16[128,256]{1,0:T(8,128)(2,1)S(1)}, u32[]{:S(2)}, u32[]{:S(2)}) collective-permute-start(bf16[128,256]{1,0:T(8,128)(2,1)S(1)} %shard_map.88), channel_id=1, source_target_pairs={{0,8},{1,9},{2,10},{3,11},{4,12},{5,13},{6,14},{7,15},{8,0},{9,1},... | collective-permute-start | bytes 196616 | tf_op jit(solution)/shard_map/ppermute | solution.py:410
